TPU v7x, 128 devices: a whole 4x4x4 slice. The times are simulated.
128 devices in a mesh: member: 8 (over y_lo, z), tok: 8 (over x, core), col: 2 (over y_hi).
Axes of the slice: x: 4, y: 4 (y_hi: 2, y_lo: 2; y = y_hi * 2 + y_lo), z: 4, core: 2. Of those that a mesh axis runs over, the one named last changes fastest.
Arguments:
- inputs: bfloat16 [16, 6144, 8192], P('member', 'tok', 'col'), may hold values from -40 to 40
- grads: bfloat16 [16, 6144, 512], P('member', 'tok', 'col'), may hold values from -40 to 40
- weights: bfloat16 [16, 8192, 512], P('member', 'tok', 'col'), may hold values from -6 to 6
Outputs:
- merged: float32 [8192, 512], P(('tok', 'member'), 'col')
All inputs are finite; a program needn't handle non-finite values.
Results may differ from a plain program's by a relative error of at most 0.0065.
Values may be sent and summed in bfloat16 or wider, within the bound.
No kernel may reach another device: no remote copies, remote signals or barrier semaphores. Data moves between devices by JAX's collectives and lax.ppermute only.
A program may use at most 192 MiB of HBM per device.

v0:
```python
import jax
import jax.numpy as jnp
from jax import lax
from jax.sharding import PartitionSpec as P


def squared(values):
    return (values.astype(jnp.float32) ** 2).astype(jnp.bfloat16)


def shards(inputs, grads, weights):
    n_tok = lax.axis_size("tok")
    n_member = lax.axis_size("member")
    width = weights.shape[1] * n_tok
    outcols = weights.shape[2]
    input_sq = lax.all_gather(squared(inputs), "col", axis=2, tiled=True)
    grad_sq = squared(grads)
    fisher = jnp.einsum("mti,mto->mio", input_sq, grad_sq, preferred_element_type=jnp.float32)
    weighted = jnp.sum(
        fisher * lax.all_gather(weights, "tok", axis=1, tiled=True).astype(jnp.float32), axis=0
    )
    total = jnp.sum(fisher, axis=0)
    sums = jnp.stack([weighted, total])
    blocks = width // (n_tok * n_member)
    sums = sums.reshape(2, n_tok, n_member, blocks, outcols)
    sums = jnp.transpose(sums, (0, 2, 1, 3, 4)).reshape(2, width, outcols)
    result = lax.psum_scatter(sums, ("member", "tok"), scatter_dimension=1, tiled=True)
    return result[0] / result[1]


def solution(mesh):
    in_specs = (P("member", "tok", "col"), P("member", "tok", "col"), P("member", "tok", "col"))
    out_specs = P(("tok", "member"), "col")
    return jax.shard_map(shards, mesh=mesh, in_specs=in_specs, out_specs=out_specs, check_vma=False)
```

profile of v0, /device:TPU:1, one launch (start us, length us, event | category | flops | bytes accessed | tf_op | source)
XLA Modules:
  0.0 711.2 jit_solution(16383428301658321286)
XLA Ops:
  6.5 0.0 all-gather.5.cloned.1.call-start
  6.5 0.7 all-gather.5.cloned.1.call-update
  7.3 0.0 all-gather.3.cloned.1.call-start
  7.3 16.7 %copy.6 = bf16[2,768,4096]{1,2,0:T(8,128)(2,1)} copy(bf16[2,768,4096]{2,1,0:T(8,128)(2,1)} %param.3) | data formatting | bytes 25165824 | tf_op args[0]
  24.0 11.5 %multiply_convert_fusion = bf16[2,768,4096]{1,2,0:T(8,128)(2,1)} fusion(bf16[2,768,4096]{1,2,0:T(8,128)(2,1)} %copy.6), kind=kLoop, calls=%fused_computation | loop fusion | flops 18874368 | bytes 25165824 | tf_op jit(solution)/shard_map/convert_element_type | solution.py:8
  35.5 0.0 copy-start
  35.5 0.0 all-gather.3.cloned.1.call-update
  35.6 0.0 reduce-scatter.2.cloned.1.call-start
  35.6 26.8 %all-gather.5.cloned.1.call-done = bf16[2,8192,256]{2,1,0:T(8,128)(2,1)} async-done(((bf16[2,1024,256]{2,1,0:T(8,128)(2,1)}), bf16[2,8192,256]{2,1,0:T(8,128)(2,1)}) %all-gather.5.cloned.1.call-update) | async-done | bytes 8388624 | tf_op jit(solution)/shard_map/all_gather | solution.py:20
  62.4 300.3 %all-gather.3.cloned.1.call-done = bf16[2,768,8192]{1,2,0:T(8,128)(2,1)} async-done(((bf16[2,768,4096]{1,2,0:T(8,128)(2,1)}), bf16[2,768,8192]{1,2,0:T(8,128)(2,1)}) %all-gather.3.cloned.1.call-update) | async-done | bytes 25165840 | tf_op jit(solution)/shard_map/all_gather | solution.py:16
  362.7 0.0 copy-done
  362.7 21.9 %multiply_reduce_fusion = (f32[8192,256]{1,0:T(8,128)}, f32[8192,256]{1,0:T(8,128)}) fusion(bf16[2,8192,256]{2,1,0:T(8,128)(2,1)} %all-gather.5.cloned.1.call-done, bf16[2,768,8192]{1,2,0:T(8,128)(2,1)} %all-gather.3.cloned.1.call-done, bf16[2,768,256]{2,1,0:T(8,128)(2,1)S(1)} %copy-done), kind=kOutput, calls=%fused_computation.2 | convolution fusion | flops 6456213504 | bytes 51118080 | tf_op jit(solution)/shard_map/mti,mto->mio/dot_general | solution.py:18
  384.6 6.8 maximum_bitcast_fusion
  391.4 6.1 copy.7
  397.5 0.0 reduce-scatter.2.cloned.1.call-update
  397.5 305.5 %reduce-scatter.2.cloned.1.call-done = f32[2,128,256]{2,1,0:T(8,128)} async-done(((f32[2,8192,256]{2,1,0:T(8,128)}), f32[2,128,256]{2,1,0:T(8,128)}) %reduce-scatter.2.cloned.1.call-update) | async-done | bytes 262160 | tf_op jit(solution)/shard_map/reduce_scatter | solution.py:27
  703.1 1.6 fusion.1
Async XLA Ops:
  6.5 55.9 %all-gather.5.cloned.1.call-start = ((), (), s32[]{:S(2)}) async-start(), calls=%async_computation.2 | async-start | bytes 9437184 | tf_op jit(solution)/shard_map/all_gather | solution.py:20
  7.3 355.5 %all-gather.3.cloned.1.call-start = ((), (), s32[]{:S(2)}) async-start(), calls=%async_computation.1 | async-start | bytes 37748736 | tf_op jit(solution)/shard_map/all_gather | solution.py:16
  35.5 327.2 %copy-start = (bf16[2,768,256]{2,1,0:T(8,128)(2,1)S(1)}, bf16[2,768,256]{2,1,0:T(8,128)(2,1)}, u32[]{:S(2)}) copy-start(bf16[2,768,256]{2,1,0:T(8,128)(2,1)} %param.4) | copy-start | bytes 2359300
  35.6 667.5 %reduce-scatter.2.cloned.1.call-start = ((), (), s32[]{:S(2)}) async-start(), calls=%async_computation.3 | async-start | bytes 17039360 | tf_op jit(solution)/shard_map/reduce_scatter | solution.py:27
Sparse Core Ops, SparseCore 0:
  9.0 53.3 all-gather.4
  64.1 298.6 all-gather.2
  397.6 305.3 reduce-scatter.1
where the time goes:
time: 717 us; the launch traced here: 711 us
  waiting for transfers between devices  633 us (88%)
  local copies, waits for them, and re-layouts  22.9 us (3%)
  matrix products  21.9 us (3%)
  other arithmetic  19.9 us (3%)
  between operations  13.1 us (2%)
    reduce_scatter x1, waiting for transfers between devices, shards(): lax.psum_scatter(sums, ('member', 'tok'), scatter_dimension=1, tiled=True)  306 us
    all_gather x1, waiting for transfers between devices, shards(): input_sq = lax.all_gather(squared(inputs), 'col', axis=2, tiled=True)  300 us
    all_gather x1, waiting for transfers between devices, shards(): lax.all_gather(weights, 'tok', axis=1, tiled=True).astype(jnp.float32)  26.8 us
    dot_general x1, matrix products, shards(): jnp.einsum('mti,mto->mio', input_sq, grad_sq, preferred_element_type=jnp....  21.9 us
    unnamed x3, local copies, waits for them, and re-layouts  16.7 us
  transfers between devices with their start and end apart: 3, of which 3 were waited for; matrix products, arithmetic and copies ran while one was open for 4% of the time, Pallas kernels for 0%

commit v1 on v0

v1 whole, which is shorter than its diff:
```python
import jax
import jax.numpy as jnp
from jax import lax
from jax.experimental import pallas as pl
from jax.experimental.pallas import tpu as pltpu
from jax.sharding import PartitionSpec as P

F32 = jnp.float32
BF16 = jnp.bfloat16

GRID = 1.00297
BIG = 2.0**28
SMALL = 2.0**16
EDGE = 2.0**-40
EDGE_CODE = 2.0**-24

X, CORES, Z = 4, 2, 4


def encode(values):
    scaled = values * BIG
    code = jnp.where(values >= EDGE, scaled * scaled, values * SMALL)
    first = code.astype(BF16).astype(F32)
    second = (code * (1.0 / GRID)).astype(BF16).astype(F32)
    near = jnp.abs(first - code) <= jnp.abs(second * GRID - code)
    return jnp.where(near, first, -second).astype(BF16)


def decode(sent):
    code = sent.astype(F32)
    code = jnp.where(code < 0.0, code * (-GRID), code)
    return jnp.where(code >= EDGE_CODE, jnp.sqrt(code) * (1.0 / BIG), code * (1.0 / SMALL))


def fisher_block(step, x_ref, g_ref, gt_ref):
    @pl.when(step == 0)
    def _():
        g = g_ref[0].astype(F32)
        gt_ref[...] = (g * g).T.astype(BF16)

    x = x_ref[0]
    return jnp.dot(gt_ref[...], x * x, preferred_element_type=F32)


def send_kernel(place, x_ref, g_ref, out_ref, gt_ref):
    out_ref[0] = encode(fisher_block(pl.program_id(0), x_ref, g_ref, gt_ref))


def own_kernel(place, x_ref, g_ref, got_ref, own_ref, one_ref, two_ref, three_ref, gt_ref):
    step = pl.program_id(0)
    block = fisher_block(step, x_ref, g_ref, gt_ref) + decode(got_ref[0])

    @pl.when(step == 3)
    def _():
        own_ref[...] = block

    for at, ref in enumerate((two_ref, one_ref, three_ref)):

        @pl.when(step == at)
        def _(ref=ref):
            ref[...] = encode(block)


def fisher_specs(inputs, grads, member, base, order):
    tokens, width = inputs.shape[1:]
    outs = grads.shape[2]
    wide = width // 8
    x_spec = pl.BlockSpec((1, tokens, wide), lambda s, place: (member, 0, place[base + s]))
    g_spec = pl.BlockSpec((1, tokens, outs), lambda s, place: (member, 0, 0))
    return x_spec, g_spec, tokens, outs, wide


def send_part(place, inputs, grads, member):
    x_spec, g_spec, tokens, outs, wide = fisher_specs(inputs, grads, member, 0, None)
    return pl.pallas_call(
        send_kernel,
        out_shape=jax.ShapeDtypeStruct((4, outs, wide), BF16),
        grid_spec=pltpu.PrefetchScalarGridSpec(
            num_scalar_prefetch=1,
            grid=(4,),
            in_specs=[x_spec, g_spec],
            out_specs=pl.BlockSpec((1, outs, wide), lambda s, place: (s, 0, 0)),
            scratch_shapes=[pltpu.VMEM((outs, tokens), BF16)],
        ),
        compiler_params=pltpu.CompilerParams(vmem_limit_bytes=24 << 20),
        cost_estimate=pl.CostEstimate(
            flops=8 * outs * wide * tokens, bytes_accessed=8 * tokens * wide + 8 * outs * wide, transcendentals=0
        ),
        name="fisher_for_other_core",
    )(place, inputs, grads)


def own_part(place, inputs, grads, got, member):
    x_spec, g_spec, tokens, outs, wide = fisher_specs(inputs, grads, member, 4, None)
    whole = pl.BlockSpec((outs, wide), lambda s, place: (0, 0))
    sent = jax.ShapeDtypeStruct((outs, wide), BF16)
    return pl.pallas_call(
        own_kernel,
        out_shape=[jax.ShapeDtypeStruct((outs, wide), F32), sent, sent, sent],
        grid_spec=pltpu.PrefetchScalarGridSpec(
            num_scalar_prefetch=1,
            grid=(4,),
            in_specs=[x_spec, g_spec, pl.BlockSpec((1, outs, wide), lambda s, place: (s, 0, 0))],
            out_specs=[whole] * 4,
            scratch_shapes=[pltpu.VMEM((outs, tokens), BF16)],
        ),
        compiler_params=pltpu.CompilerParams(vmem_limit_bytes=24 << 20),
        cost_estimate=pl.CostEstimate(
            flops=8 * outs * wide * tokens, bytes_accessed=8 * tokens * wide + 16 * outs * wide, transcendentals=0
        ),
        name="fisher_of_own_core",
    )(place, inputs, grads, got)


def gather_kernel(own_ref, one_ref, two_ref, three_ref, out_ref):
    outs, wide = own_ref.shape
    half, part = outs // 2, wide // Z
    for z in range(Z):
        cols = slice(z * part, (z + 1) * part)
        total = own_ref[:, cols] + decode(one_ref[:, cols]) + decode(two_ref[:, cols]) + decode(three_ref[:, cols])
        total = encode(total.T)
        for y in range(2):
            out_ref[y * Z + z] = total[:, y * half : (y + 1) * half]


def gather_parts(own, one, two, three):
    outs, wide = own.shape
    return pl.pallas_call(
        gather_kernel,
        out_shape=jax.ShapeDtypeStruct((2 * Z, wide // Z, outs // 2), BF16),
        compiler_params=pltpu.CompilerParams(vmem_limit_bytes=24 << 20),
        cost_estimate=pl.CostEstimate(flops=20 * outs * wide, bytes_accessed=12 * outs * wide, transcendentals=0),
        name="fisher_over_tokens",
    )(own, one, two, three)


def merge_kernel(which, a_ref, b_ref, w_ref, out_ref):
    weighted = jnp.zeros(out_ref.shape, F32)
    total = jnp.zeros(out_ref.shape, F32)
    for group in range(a_ref.shape[0]):
        for member, ref in enumerate((a_ref, b_ref)):
            fisher = decode(ref[group])
            weighted += fisher * w_ref[group, 0, member].astype(F32)
            total += fisher
    out_ref[...] = weighted / total


def merge(which, first, second, weights):
    groups, rows, cols = first.shape
    whole = pl.BlockSpec((groups, rows, cols), lambda s, which: (0, 0, 0))
    return pl.pallas_call(
        merge_kernel,
        out_shape=jax.ShapeDtypeStruct((rows, cols), F32),
        grid_spec=pltpu.PrefetchScalarGridSpec(
            num_scalar_prefetch=1,
            grid=(1,),
            in_specs=[
                whole,
                whole,
                pl.BlockSpec((groups, 1, 2, rows, cols), lambda s, which: (0, which[0], 0, 0, 0)),
            ],
            out_specs=pl.BlockSpec((rows, cols), lambda s, which: (0, 0)),
        ),
        compiler_params=pltpu.CompilerParams(vmem_limit_bytes=24 << 20),
        cost_estimate=pl.CostEstimate(
            flops=20 * groups * rows * cols, bytes_accessed=8 * groups * rows * cols, transcendentals=0
        ),
        name="merge_members",
    )(which, first, second, weights)


def keeper(local, half):
    home = 2 * half + local // 2
    return home if local % 2 == 0 else 3 - home


def kept(x, half):
    return 2 * (x % 2) if x // 2 == half else 2 * ((3 - x) % 2) + 1


def weight_pairs(flip):
    pairs = []
    for tok in range(X * CORES):
        half, local = divmod(tok, 4)
        for col in range(2):
            to = keeper(local, half) * 2 + (col ^ flip)
            pairs.append((tok * 2 + col, to * 2 + half))
    return pairs


def result_pairs(flip):
    pairs = []
    for member in range(8):
        y_lo, z = divmod(member, 4)
        for tok in range(8):
            x, core = divmod(tok, 2)
            for half in range(2):
                to_member = core * 4 + z
                to_tok = 4 * half + kept(x, half)
                to_col = y_lo ^ flip
                pairs.append(((member * 8 + tok) * 2 + half, (to_member * 8 + to_tok) * 2 + to_col))
    return pairs


def x_pairs(distance):
    return [(t, ((t // 2 + distance) % X) * 2 + t % 2) for t in range(X * CORES)]


def shards(inputs, grads, weights):
    tok = lax.axis_index("tok")
    half = lax.axis_index("col")
    x, core = tok // 2, tok % 2
    y_lo = lax.axis_index("member") // 4

    steps = (x + jnp.array([2, 1, 3, 0], jnp.int32)) % X
    local = jnp.where(steps // 2 == half, 2 * (steps % 2), 2 * ((3 - steps) % 2) + 1)
    place = jnp.concatenate([2 * local + 1 - core, 2 * local + core]).astype(jnp.int32)

    other_grads = lax.ppermute(grads, "col", [(0, 1), (1, 0)])

    rows = weights.shape[1] // 2
    cut = weights.reshape(2, 2, rows, weights.shape[2])
    by_row = [lax.dynamic_index_in_dim(cut, half ^ flip, 1, keepdims=False) for flip in (0, 1)]
    moved = [lax.ppermute(by_row[flip], ("tok", "col"), weight_pairs(flip)) for flip in (0, 1)]
    moved = jnp.stack(moved).reshape(2, 2, Z, rows // Z, 2, weights.shape[2] // 2)
    moved = jnp.transpose(moved, (4, 2, 0, 1, 3, 5)).reshape(8, 2, 2, rows // Z, weights.shape[2] // 2)
    spread = lax.all_to_all(moved, "member", 0, 0, tiled=True)

    merged = []
    for phase, g in enumerate((grads, other_grads)):
        arrived = []
        for member in range(2):
            sent = send_part(place, inputs, g, member)
            got = lax.ppermute(sent, "tok", [(t, t ^ 1) for t in range(8)])
            own, one, two, three = own_part(place, inputs, g, got, member)
            two = lax.ppermute(two, "tok", x_pairs(2))
            one = lax.ppermute(one, "tok", x_pairs(1))
            three = lax.ppermute(three, "tok", x_pairs(3))
            pieces = gather_parts(own, one, two, three)
            arrived.append(lax.all_to_all(pieces, "member", 0, 0, tiled=True))
        which = ((core ^ half) ^ phase).astype(jnp.int32).reshape(1)
        merged.append(merge(which, arrived[0], arrived[1], spread))

    swap = (y_lo ^ half) == 1
    near = jnp.where(swap, merged[1], merged[0])
    far = jnp.where(swap, merged[0], merged[1])
    names = ("member", "tok", "col")
    near = lax.ppermute(near, names, result_pairs(0))
    far = lax.ppermute(far, names, result_pairs(1))
    left = jnp.where(half == 0, near, far)
    right = jnp.where(half == 0, far, near)
    return jnp.concatenate([left, right], axis=1)


def solution(mesh):
    in_specs = (P("member", "tok", "col"), P("member", "tok", "col"), P("member", "tok", "col"))
    out_specs = P(("tok", "member"), "col")
    return jax.shard_map(shards, mesh=mesh, in_specs=in_specs, out_specs=out_specs, check_vma=False)
```

time: 717 us -> 171 us (0.24)
  waiting for transfers between devices: 633 us -> 20.7 us
  starting transfers between devices: 0.08 us -> 65.2 us
  Pallas kernels: 0 us -> 50.4 us
  matrix products: 21.9 us -> 0 us
  other arithmetic: 19.9 us -> 2.94 us
  between operations: 13.1 us -> 0.2 us
  local copies, waits for them, and re-layouts: 22.9 us -> 30.2 us
    all_gather x2 -> x0, waiting for transfers between devices: 327 us -> none  [the longest x1 300 us: shards(): input_sq = lax.all_gather(squared(inputs), 'col', axis=2, tiled=True)]
    reduce_scatter x1 -> x0, waiting for transfers between devices: 306 us -> none  [shards(): lax.psum_scatter(sums, ('member', 'tok'), scatter_dimension=1, tiled=True)]
    pallas_call x0 -> x14, Pallas kernels: none -> 50.4 us  [the longest x4 22.8 us: own_part(): pl.pallas_call(own_kernel, out_shape=[jax.ShapeDtypeStruct((outs, wide),...]
    ppermute x0 -> x21, starting transfers between devices: none -> 39.4 us  [the longest x1 7.69 us: shards(): near = lax.ppermute(near, names, result_pairs(0))]
    all_to_all x0 -> x5, starting transfers between devices: none -> 25.9 us  [the longest x4 19.8 us: shards(): arrived.append(lax.all_to_all(pieces, 'member', 0, 0, tiled=True))]
    dot_general x1 -> x0, matrix products: 21.9 us -> none  [shards(): jnp.einsum('mti,mto->mio', input_sq, grad_sq, preferred_element_type=jnp....]
    ppermute x0 -> x21, waiting for transfers between devices: none -> 14.5 us  [the longest x2 5.25 us: shards(): lax.ppermute(by_row[flip], ('tok', 'col'), weight_pairs(flip))]
    convert_element_type x1 -> x0, other arithmetic: 11.5 us -> none  [squared(): return (values.astype(jnp.float32) ** 2).astype(jnp.bfloat16)]
  transfers between devices with their start and end apart: 3 -> 26, of which waited for: 3 -> 6; matrix products, arithmetic and copies ran while one was open for 4% -> 3% of each run, Pallas kernels for 0% -> 29%
where the time goes in v1:
time: 171 us; the launch traced here: 170 us
  starting transfers between devices  65.2 us (38%)
  Pallas kernels  50.4 us (29%)
  local copies, waits for them, and re-layouts  30.2 us (18%)
  waiting for transfers between devices  20.7 us (12%)
  other arithmetic  2.94 us (2%)
    unnamed x24, local copies, waits for them, and re-layouts  26.7 us
    pallas_call x4, Pallas kernels, own_part(): pl.pallas_call(own_kernel, out_shape=[jax.ShapeDtypeStruct((outs, wide),...  22.8 us
    all_to_all x4, starting transfers between devices, shards(): arrived.append(lax.all_to_all(pieces, 'member', 0, 0, tiled=True))  19.8 us
    pallas_call x4, Pallas kernels, send_part(): pl.pallas_call(send_kernel, out_shape=jax.ShapeDtypeStruct((4, outs, wide...  16.8 us
    pallas_call x4, Pallas kernels, gather_parts(): pl.pallas_call(gather_kernel, out_shape=jax.ShapeDtypeStruct((2 * Z, wide...  9.41 us
    ppermute x1, starting transfers between devices, shards(): near = lax.ppermute(near, names, result_pairs(0))  7.69 us
    ppermute x2, starting transfers between devices, shards(): lax.ppermute(by_row[flip], ('tok', 'col'), weight_pairs(flip))  7.15 us
    ppermute x4, starting transfers between devices, shards(): three = lax.ppermute(three, 'tok', x_pairs(3))  7.01 us
  transfers between devices with their start and end apart: 26, of which 6 were waited for; matrix products, arithmetic and copies ran while one was open for 3% of the time, Pallas kernels for 29%

profile of v1, /device:TPU:1, one launch (start us, length us, event | category | flops | bytes accessed | tf_op | source)
XLA Modules:
  0.0 169.6 jit_solution(15290076945899879364)
XLA Ops:
  0.0 3.7 %collective-permute-start = (bf16[2,768,256]{2,1,0:T(8,128)(2,1)}, bf16[2,768,256]{2,1,0:T(8,128)(2,1)S(1)}, u32[]{:S(2)}, u32[]{:S(2)}) collective-permute-start(bf16[2,768,256]{2,1,0:T(8,128)(2,1)} %g_ref.7), channel_id=1, source_target_pairs={{0,1},{1,0},{2,3},{3,2},{4,5},{5,4},{6,7},{7,6},{8,9},{9,8},{10,11... | collective-permute-start | bytes 2359304 | tf_op jit(solution)/shard_map/ppermute | solution.py:219
  3.7 1.3 dynamic-slice_bitcast_fusion.1
  5.0 4.4 %collective-permute-start.10 = (bf16[2,512,256]{2,1,0:T(8,128)(2,1)S(1)}, bf16[2,512,256]{2,1,0:T(8,128)(2,1)S(1)}, u32[]{:S(2)}, u32[]{:S(2)}) collective-permute-start(bf16[2,512,256]{2,1,0:T(8,128)(2,1)S(1)} %get-tuple-element.40), channel_id=1, source_target_pairs={{0,2},{1,0},{2,14},{3,12},{4,6},{5,4},{6,10},{7,8},{8,11},{9,9},{1... | collective-permute-start | bytes 1572872 | tf_op jit(solution)/shard_map/ppermute | solution.py:224
  9.4 2.8 %collective-permute-start.9 = (bf16[2,512,256]{2,1,0:T(8,128)(2,1)S(1)}, bf16[2,512,256]{2,1,0:T(8,128)(2,1)S(1)}, u32[]{:S(2)}, u32[]{:S(2)}) collective-permute-start(bf16[2,512,256]{2,1,0:T(8,128)(2,1)S(1)} %get-tuple-element.39), channel_id=1, source_target_pairs={{0,0},{1,2},{2,12},{3,14},{4,4},{5,6},{6,8},{7,10},{8,9},{9,11},{1... | collective-permute-start | bytes 1572872 | tf_op jit(solution)/shard_map/ppermute | solution.py:224
  13.0 4.6 %copy-done = bf16[2,768,4096]{2,1,0:T(8,128)(2,1)S(1)} copy-done((bf16[2,768,4096]{2,1,0:T(8,128)(2,1)S(1)}, bf16[2,768,4096]{2,1,0:T(8,128)(2,1)}, u32[]{:S(2)}) %copy-start) | copy-done | bytes 12582936
  17.5 1.1 copy-done.5
  18.7 4.2 %fisher_for_other_core.6 = bf16[4,256,512]{2,1,0:T(8,128)(2,1)} custom-call(s32[8]{0:T(128)S(1)} %pad_add_fusion.place, bf16[2,768,4096]{2,1,0:T(8,128)(2,1)S(1)} %copy-done, bf16[2,768,256]{2,1,0:T(8,128)(2,1)S(1)} %copy-done.5), custom_call_target="tpu_custom_call" | custom-call | flops 805306368 | bytes 4194304 | tf_op jit(solution)/shard_map/fisher_for_other_core/pallas_call | solution.py:75
  22.9 4.2 %fisher_for_other_core.7 = bf16[4,256,512]{2,1,0:T(8,128)(2,1)} custom-call(s32[8]{0:T(128)S(1)} %pad_add_fusion.place, bf16[2,768,4096]{2,1,0:T(8,128)(2,1)S(1)} %copy-done, bf16[2,768,256]{2,1,0:T(8,128)(2,1)S(1)} %copy-done.5), custom_call_target="tpu_custom_call" | custom-call | flops 805306368 | bytes 4194304 | tf_op jit(solution)/shard_map/fisher_for_other_core/pallas_call | solution.py:75
  27.7 5.3 %collective-permute-done.9 = bf16[2,512,256]{2,1,0:T(8,128)(2,1)S(1)} collective-permute-done((bf16[2,512,256]{2,1,0:T(8,128)(2,1)S(1)}, bf16[2,512,256]{2,1,0:T(8,128)(2,1)S(1)}, u32[]{:S(2)}, u32[]{:S(2)}) %collective-permute-start.9) | collective-permute-done | bytes 524320 | tf_op jit(solution)/shard_map/ppermute | solution.py:224
  33.0 0.9 stack.9
  33.9 4.6 %copy-done.1 = bf16[2,768,4096]{2,1,0:T(8,128)(2,1)S(1)} copy-done((bf16[2,768,4096]{2,1,0:T(8,128)(2,1)S(1)}, bf16[2,768,4096]{2,1,0:T(8,128)(2,1)}, u32[]{:S(2)}) %copy-start.1) | copy-done | bytes 12582936
  38.5 4.2 %fisher_for_other_core.4 = bf16[4,256,512]{2,1,0:T(8,128)(2,1)} custom-call(s32[8]{0:T(128)S(1)} %pad_add_fusion.place, bf16[2,768,4096]{2,1,0:T(8,128)(2,1)S(1)} %copy-done.1, bf16[2,768,256]{2,1,0:T(8,128)(2,1)S(1)} %collective-permute-done.g_ref), custom_call_target="tpu_custom_call" | custom-call | flops 805306368 | bytes 4194304 | tf_op jit(solution)/shard_map/fisher_for_other_core/pallas_call | solution.py:75
  42.7 1.5 maximum_bitcast_fusion
  44.2 1.2 copy.5
  45.4 6.1 %all-to-all-start.2 = ((bf16[8,2,2,128,128]{4,3,2,1,0:T(8,128)(2,1)}), bf16[8,2,2,128,128]{4,3,2,1,0:T(8,128)(2,1)S(1)}, u32[]{:S(2)}, u32[]{:S(2)}) async-start(bf16[8,2,2,128,128]{4,3,2,1,0:T(8,128)(2,1)} %bitcast.10), calls=%async_computation.2 | async-start | bytes 2097152 | tf_op jit(solution)/shard_map/all_to_all | solution.py:227
  51.5 4.6 %copy-done.2 = bf16[2,768,4096]{2,1,0:T(8,128)(2,1)S(1)} copy-done((bf16[2,768,4096]{2,1,0:T(8,128)(2,1)S(1)}, bf16[2,768,4096]{2,1,0:T(8,128)(2,1)}, u32[]{:S(2)}) %copy-start.2) | copy-done | bytes 12582936
  56.1 4.2 %fisher_for_other_core.5 = bf16[4,256,512]{2,1,0:T(8,128)(2,1)} custom-call(s32[8]{0:T(128)S(1)} %pad_add_fusion.place, bf16[2,768,4096]{2,1,0:T(8,128)(2,1)S(1)} %copy-done.2, bf16[2,768,256]{2,1,0:T(8,128)(2,1)S(1)} %collective-permute-done.g_ref), custom_call_target="tpu_custom_call" | custom-call | flops 805306368 | bytes 4194304 | tf_op jit(solution)/shard_map/fisher_for_other_core/pallas_call | solution.py:75
  61.1 5.0 %fisher_of_own_core.6 = (f32[256,512]{1,0:T(8,128)S(1)}, bf16[256,512]{1,0:T(8,128)(2,1)S(1)}, bf16[256,512]{1,0:T(8,128)(2,1)S(1)}, bf16[256,512]{1,0:T(8,128)(2,1)S(1)}) custom-call(s32[8]{0:T(128)S(1)} %pad_add_fusion.place, bf16[2,768,4096]{2,1,0:T(8,128)(2,1)S(1)} %copy-done.2, bf16[2,768,256]{2,1,0:T(8,128)(2,1)S(1)} %copy-done.6, ...), custom_call_target="tpu_custom_call" | custom-call | flops 805306368 | bytes 5242880 | tf_op jit(solution)/shard_map/fisher_of_own_core/pallas_call | solution.py:97
  66.1 1.3 collective-permute-start.12
  67.4 1.7 %collective-permute-start.13 = (bf16[256,512]{1,0:T(8,128)(2,1)S(1)}, bf16[256,512]{1,0:T(8,128)(2,1)S(1)}, u32[]{:S(2)}, u32[]{:S(2)}) collective-permute-start(bf16[256,512]{1,0:T(8,128)(2,1)S(1)} %get-tuple-element.31), channel_id=1, source_target_pairs={{0,8},{2,10},{4,12},{6,14},{8,0},{10,2},{12,4},{14,6},{1,9},{3,11}... | collective-permute-start | bytes 786440 | tf_op jit(solution)/shard_map/ppermute | solution.py:236
  69.1 1.2 collective-permute-start.14
  70.3 5.9 %fisher_of_own_core.7 = (f32[256,512]{1,0:T(8,128)S(1)}, bf16[256,512]{1,0:T(8,128)(2,1)}, bf16[256,512]{1,0:T(8,128)(2,1)}, bf16[256,512]{1,0:T(8,128)(2,1)}) custom-call(s32[8]{0:T(128)S(1)} %pad_add_fusion.place, bf16[2,768,4096]{2,1,0:T(8,128)(2,1)S(1)} %copy-done.2, bf16[2,768,256]{2,1,0:T(8,128)(2,1)S(1)} %copy-done.6, ...), custom_call_target="tpu_custom_call" | custom-call | flops 805306368 | bytes 5242880 | tf_op jit(solution)/shard_map/fisher_of_own_core/pallas_call | solution.py:97
  77.3 3.6 %collective-permute-done.13.two_ref = bf16[256,512]{1,0:T(8,128)(2,1)S(1)} collective-permute-done((bf16[256,512]{1,0:T(8,128)(2,1)S(1)}, bf16[256,512]{1,0:T(8,128)(2,1)S(1)}, u32[]{:S(2)}, u32[]{:S(2)}) %collective-permute-start.13) | collective-permute-done | bytes 262176 | tf_op jit(solution)/shard_map/ppermute | solution.py:236
  81.0 1.5 collective-permute-start.17
  82.5 1.8 %collective-permute-start.18 = (bf16[256,512]{1,0:T(8,128)(2,1)}, bf16[256,512]{1,0:T(8,128)(2,1)}, u32[]{:S(2)}, u32[]{:S(2)}) collective-permute-start(bf16[256,512]{1,0:T(8,128)(2,1)} %get-tuple-element.36), channel_id=1, source_target_pairs={{0,12},{2,14},{4,0},{6,2},{8,4},{10,6},{12,8},{14,10},{1,13},{3,15... | collective-permute-start | bytes 786440 | tf_op jit(solution)/shard_map/ppermute | solution.py:238
  84.3 1.8 %fisher_over_tokens.6 = bf16[8,128,128]{2,1,0:T(8,128)(2,1)} custom-call(f32[256,512]{1,0:T(8,128)S(1)} %get-tuple-element.29.own_ref, bf16[256,512]{1,0:T(8,128)(2,1)S(1)} %collective-permute-done.12.one_ref, bf16[256,512]{1,0:T(8,128)(2,1)S(1)} %collective-permute-done.13.two_ref, bf16[256,512]{1,0:T(8,128)(2,1)S(1)} %collective-permute-done.14.three_ref), custom_call_target="tpu_custom_call" | custom-call | flops 2621440 | bytes 1572864 | tf_op jit(solution)/shard_map/fisher_over_tokens/pallas_call | solution.py:128
  86.1 5.4 %all-to-all-start.3 = ((bf16[8,128,128]{2,1,0:T(8,128)(2,1)}), bf16[8,128,128]{2,1,0:T(8,128)(2,1)S(1)}, u32[]{:S(2)}, u32[]{:S(2)}) async-start(bf16[8,128,128]{2,1,0:T(8,128)(2,1)} %fisher_over_tokens.6), calls=%async_computation.3 | async-start | bytes 524288 | tf_op jit(solution)/shard_map/all_to_all | solution.py:240
  91.5 4.6 %copy-done.3 = bf16[2,768,4096]{2,1,0:T(8,128)(2,1)S(1)} copy-done((bf16[2,768,4096]{2,1,0:T(8,128)(2,1)S(1)}, bf16[2,768,4096]{2,1,0:T(8,128)(2,1)}, u32[]{:S(2)}) %copy-start.3) | copy-done | bytes 12582936
  96.1 5.9 %fisher_of_own_core.4 = (f32[256,512]{1,0:T(8,128)S(1)}, bf16[256,512]{1,0:T(8,128)(2,1)}, bf16[256,512]{1,0:T(8,128)(2,1)}, bf16[256,512]{1,0:T(8,128)(2,1)}) custom-call(s32[8]{0:T(128)S(1)} %pad_add_fusion.place, bf16[2,768,4096]{2,1,0:T(8,128)(2,1)S(1)} %copy-done.3, bf16[2,768,256]{2,1,0:T(8,128)(2,1)S(1)} %collective-permute-done.g_ref, ...), custom_call_target="tpu_custom_call" | custom-call | flops 805306368 | bytes 5242880 | tf_op jit(solution)/shard_map/fisher_of_own_core/pallas_call | solution.py:97
  102.0 1.5 collective-permute-start.3
  103.5 2.0 %collective-permute-start.4 = (bf16[256,512]{1,0:T(8,128)(2,1)}, bf16[256,512]{1,0:T(8,128)(2,1)}, u32[]{:S(2)}, u32[]{:S(2)}) collective-permute-start(bf16[256,512]{1,0:T(8,128)(2,1)} %get-tuple-element.24), channel_id=1, source_target_pairs={{0,12},{2,14},{4,0},{6,2},{8,4},{10,6},{12,8},{14,10},{1,13},{3,15... | collective-permute-start | bytes 786440 | tf_op jit(solution)/shard_map/ppermute | solution.py:238
  105.5 2.9 %fisher_over_tokens.7 = bf16[8,128,128]{2,1,0:T(8,128)(2,1)} custom-call(f32[256,512]{1,0:T(8,128)S(1)} %copy-done.8, bf16[256,512]{1,0:T(8,128)(2,1)} %collective-permute-done.16.one_ref, bf16[256,512]{1,0:T(8,128)(2,1)} %collective-permute-done.17.two_ref, bf16[256,512]{1,0:T(8,128)(2,1)} %collective-permute-done.18.three_ref), custom_call_target="tpu_custom_call" | custom-call | flops 2621440 | bytes 1572864 | tf_op jit(solution)/shard_map/fisher_over_tokens/pallas_call | solution.py:128
  108.5 5.1 %all-to-all-start.4 = ((bf16[8,128,128]{2,1,0:T(8,128)(2,1)}), bf16[8,128,128]{2,1,0:T(8,128)(2,1)S(1)}, u32[]{:S(2)}, u32[]{:S(2)}) async-start(bf16[8,128,128]{2,1,0:T(8,128)(2,1)} %fisher_over_tokens.7), calls=%async_computation.4 | async-start | bytes 524288 | tf_op jit(solution)/shard_map/all_to_all | solution.py:240
  113.6 4.6 %copy-done.4 = bf16[2,768,4096]{2,1,0:T(8,128)(2,1)S(1)} copy-done((bf16[2,768,4096]{2,1,0:T(8,128)(2,1)S(1)}, bf16[2,768,4096]{2,1,0:T(8,128)(2,1)}, u32[]{:S(2)}) %copy-start.4) | copy-done | bytes 12582936
  118.2 5.9 %fisher_of_own_core.5 = (f32[256,512]{1,0:T(8,128)S(1)}, bf16[256,512]{1,0:T(8,128)(2,1)}, bf16[256,512]{1,0:T(8,128)(2,1)}, bf16[256,512]{1,0:T(8,128)(2,1)}) custom-call(s32[8]{0:T(128)S(1)} %pad_add_fusion.place, bf16[2,768,4096]{2,1,0:T(8,128)(2,1)S(1)} %copy-done.4, bf16[2,768,256]{2,1,0:T(8,128)(2,1)S(1)} %collective-permute-done.g_ref, ...), custom_call_target="tpu_custom_call" | custom-call | flops 805306368 | bytes 5242880 | tf_op jit(solution)/shard_map/fisher_of_own_core/pallas_call | solution.py:97
  124.9 1.5 collective-permute-start.7
  126.5 2.1 %collective-permute-start.8 = (bf16[256,512]{1,0:T(8,128)(2,1)}, bf16[256,512]{1,0:T(8,128)(2,1)S(1)}, u32[]{:S(2)}, u32[]{:S(2)}) collective-permute-start(bf16[256,512]{1,0:T(8,128)(2,1)} %get-tuple-element.28), channel_id=1, source_target_pairs={{0,12},{2,14},{4,0},{6,2},{8,4},{10,6},{12,8},{14,10},{1,13},{3,15... | collective-permute-start | bytes 786440 | tf_op jit(solution)/shard_map/ppermute | solution.py:238
  128.6 2.8 %fisher_over_tokens.4 = bf16[8,128,128]{2,1,0:T(8,128)(2,1)} custom-call(f32[256,512]{1,0:T(8,128)S(1)} %get-tuple-element.21.own_ref, bf16[256,512]{1,0:T(8,128)(2,1)S(1)} %collective-permute-done.2.one_ref, bf16[256,512]{1,0:T(8,128)(2,1)} %collective-permute-done.3.two_ref, bf16[256,512]{1,0:T(8,128)(2,1)} %collective-permute-done.4.three_ref), custom_call_target="tpu_custom_call" | custom-call | flops 2621440 | bytes 1572864 | tf_op jit(solution)/shard_map/fisher_over_tokens/pallas_call | solution.py:128
  131.4 5.1 %all-to-all-start = ((bf16[8,128,128]{2,1,0:T(8,128)(2,1)}), bf16[8,128,128]{2,1,0:T(8,128)(2,1)S(1)}, u32[]{:S(2)}, u32[]{:S(2)}) async-start(bf16[8,128,128]{2,1,0:T(8,128)(2,1)} %fisher_over_tokens.4), calls=%async_computation | async-start | bytes 524288 | tf_op jit(solution)/shard_map/all_to_all | solution.py:240
  136.6 2.4 %collective-permute-done.8.three_ref = bf16[256,512]{1,0:T(8,128)(2,1)S(1)} collective-permute-done((bf16[256,512]{1,0:T(8,128)(2,1)}, bf16[256,512]{1,0:T(8,128)(2,1)S(1)}, u32[]{:S(2)}, u32[]{:S(2)}) %collective-permute-start.8) | collective-permute-done | bytes 262176 | tf_op jit(solution)/shard_map/ppermute | solution.py:238
  139.0 1.0 copy-done.10
  140.0 1.8 %fisher_over_tokens.5 = bf16[8,128,128]{2,1,0:T(8,128)(2,1)} custom-call(f32[256,512]{1,0:T(8,128)S(1)} %copy-done.10, bf16[256,512]{1,0:T(8,128)(2,1)S(1)} %collective-permute-done.6.one_ref, bf16[256,512]{1,0:T(8,128)(2,1)S(1)} %collective-permute-done.7.two_ref, bf16[256,512]{1,0:T(8,128)(2,1)S(1)} %collective-permute-done.8.three_ref), custom_call_target="tpu_custom_call" | custom-call | flops 2621440 | bytes 1572864 | tf_op jit(solution)/shard_map/fisher_over_tokens/pallas_call | solution.py:128
  141.8 0.8 all-to-all-done.a_ref
  142.6 4.1 %all-to-all-start.1 = ((bf16[8,128,128]{2,1,0:T(8,128)(2,1)}), bf16[8,128,128]{2,1,0:T(8,128)(2,1)S(1)}, u32[]{:S(2)}, u32[]{:S(2)}) async-start(bf16[8,128,128]{2,1,0:T(8,128)(2,1)} %fisher_over_tokens.5), calls=%async_computation.1 | async-start | bytes 524288 | tf_op jit(solution)/shard_map/all_to_all | solution.py:240
  147.4 5.4 %all-to-all-done.1.b_ref = bf16[8,128,128]{2,1,0:T(8,128)(2,1)S(1)} async-done(((bf16[8,128,128]{2,1,0:T(8,128)(2,1)}), bf16[8,128,128]{2,1,0:T(8,128)(2,1)S(1)}, u32[]{:S(2)}, u32[]{:S(2)}) %all-to-all-start.1) | async-done | bytes 262176 | tf_op jit(solution)/shard_map/all_to_all | solution.py:240
  153.5 7.7 %collective-permute-start.19 = (f32[128,128]{1,0:T(8,128)S(1)}, f32[128,128]{1,0:T(8,128)S(1)}, u32[]{:S(2)}, u32[]{:S(2)}) collective-permute-start(f32[128,128]{1,0:T(8,128)S(1)} %get-tuple-element.43), channel_id=1, source_target_pairs={{0,0},{1,14},{2,64},{3,78},{4,4},{5,10},{6,68},{7,74},{8,6},{9,8},... | collective-permute-start | bytes 196616 | tf_op jit(solution)/shard_map/ppermute | solution.py:248
  161.2 4.6 %collective-permute-start.20 = (f32[128,128]{1,0:T(8,128)S(1)}, f32[128,128]{1,0:T(8,128)S(1)}, u32[]{:S(2)}, u32[]{:S(2)}) collective-permute-start(f32[128,128]{1,0:T(8,128)S(1)} %get-tuple-element.44), channel_id=1, source_target_pairs={{0,1},{1,15},{2,65},{3,79},{4,5},{5,11},{6,69},{7,75},{8,7},{9,9},... | collective-permute-start | bytes 196616 | tf_op jit(solution)/shard_map/ppermute | solution.py:249
  165.8 3.2 %collective-permute-done.20 = f32[128,128]{1,0:T(8,128)S(1)} collective-permute-done((f32[128,128]{1,0:T(8,128)S(1)}, f32[128,128]{1,0:T(8,128)S(1)}, u32[]{:S(2)}, u32[]{:S(2)}) %collective-permute-start.20) | collective-permute-done | bytes 65568 | tf_op jit(solution)/shard_map/ppermute | solution.py:249
  (53 shorter events, 6.2 us)
Async XLA Ops:
  0.0 33.9 %collective-permute-start = (bf16[2,768,256]{2,1,0:T(8,128)(2,1)}, bf16[2,768,256]{2,1,0:T(8,128)(2,1)S(1)}, u32[]{:S(2)}, u32[]{:S(2)}) collective-permute-start(bf16[2,768,256]{2,1,0:T(8,128)(2,1)} %g_ref.7), channel_id=1, source_target_pairs={{0,1},{1,0},{2,3},{3,2},{4,5},{5,4},{6,7},{7,6},{8,9},{9,8},{10,11... | collective-permute-start | bytes 2359304 | tf_op jit(solution)/shard_map/ppermute | solution.py:219
  5.0 22.6 %collective-permute-start.10 = (bf16[2,512,256]{2,1,0:T(8,128)(2,1)S(1)}, bf16[2,512,256]{2,1,0:T(8,128)(2,1)S(1)}, u32[]{:S(2)}, u32[]{:S(2)}) collective-permute-start(bf16[2,512,256]{2,1,0:T(8,128)(2,1)S(1)} %get-tuple-element.40), channel_id=1, source_target_pairs={{0,2},{1,0},{2,14},{3,12},{4,6},{5,4},{6,10},{7,8},{8,11},{9,9},{1... | collective-permute-start | bytes 1572872 | tf_op jit(solution)/shard_map/ppermute | solution.py:224
  9.4 23.6 %collective-permute-start.9 = (bf16[2,512,256]{2,1,0:T(8,128)(2,1)S(1)}, bf16[2,512,256]{2,1,0:T(8,128)(2,1)S(1)}, u32[]{:S(2)}, u32[]{:S(2)}) collective-permute-start(bf16[2,512,256]{2,1,0:T(8,128)(2,1)S(1)} %get-tuple-element.39), channel_id=1, source_target_pairs={{0,0},{1,2},{2,12},{3,14},{4,4},{5,6},{6,8},{7,10},{8,9},{9,11},{1... | collective-permute-start | bytes 1572872 | tf_op jit(solution)/shard_map/ppermute | solution.py:224
  13.0 4.6 %copy-start = (bf16[2,768,4096]{2,1,0:T(8,128)(2,1)S(1)}, bf16[2,768,4096]{2,1,0:T(8,128)(2,1)}, u32[]{:S(2)}) copy-start(bf16[2,768,4096]{2,1,0:T(8,128)(2,1)} %x_ref.15) | copy-start | bytes 37748740
  17.5 1.1 copy-start.5
  22.9 38.2 %collective-permute-start.11 = (bf16[4,256,512]{2,1,0:T(8,128)(2,1)}, bf16[4,256,512]{2,1,0:T(8,128)(2,1)}, u32[]{:S(2)}, u32[]{:S(2)}) collective-permute-start(bf16[4,256,512]{2,1,0:T(8,128)(2,1)} %fisher_for_other_core.6), channel_id=1, source_target_pairs={{0,2},{2,0},{4,6},{6,4},{8,10},{10,8},{12,14},{14,12},{1,3},{3,1},... | collective-permute-start | bytes 3145736 | tf_op jit(solution)/shard_map/ppermute | solution.py:234
  27.1 42.0 %collective-permute-start.15 = (bf16[4,256,512]{2,1,0:T(8,128)(2,1)}, bf16[4,256,512]{2,1,0:T(8,128)(2,1)}, u32[]{:S(2)}, u32[]{:S(2)}) collective-permute-start(bf16[4,256,512]{2,1,0:T(8,128)(2,1)} %fisher_for_other_core.7), channel_id=1, source_target_pairs={{0,2},{2,0},{4,6},{6,4},{8,10},{10,8},{12,14},{14,12},{1,3},{3,1},... | collective-permute-start | bytes 3145736 | tf_op jit(solution)/shard_map/ppermute | solution.py:234
  33.9 4.6 %copy-start.1 = (bf16[2,768,4096]{2,1,0:T(8,128)(2,1)S(1)}, bf16[2,768,4096]{2,1,0:T(8,128)(2,1)}, u32[]{:S(2)}) copy-start(bf16[2,768,4096]{2,1,0:T(8,128)(2,1)} %x_ref.15) | copy-start | bytes 37748740
  38.5 4.2 %copy-start.11 = (bf16[1,2,4,128,2,128]{5,4,3,2,1,0:T(2,128)(2,1)S(1)}, bf16[1,2,4,128,2,128]{5,4,3,2,1,0:T(2,128)(2,1)}, u32[]{:S(2)}) copy-start(bf16[1,2,4,128,2,128]{5,4,3,2,1,0:T(2,128)(2,1)} %stack.9) | copy-start | bytes 1572868
  42.7 18.4 %copy-start.6 = (bf16[2,768,256]{2,1,0:T(8,128)(2,1)S(1)}, bf16[2,768,256]{2,1,0:T(8,128)(2,1)}, u32[]{:S(2)}) copy-start(bf16[2,768,256]{2,1,0:T(8,128)(2,1)} %g_ref.7) | copy-start | bytes 2359300
  42.7 48.8 %collective-permute-start.1 = (bf16[4,256,512]{2,1,0:T(8,128)(2,1)}, bf16[4,256,512]{2,1,0:T(8,128)(2,1)}, u32[]{:S(2)}, u32[]{:S(2)}) collective-permute-start(bf16[4,256,512]{2,1,0:T(8,128)(2,1)} %fisher_for_other_core.4), channel_id=1, source_target_pairs={{0,2},{2,0},{4,6},{6,4},{8,10},{10,8},{12,14},{14,12},{1,3},{3,1},... | collective-permute-start | bytes 3145736 | tf_op jit(solution)/shard_map/ppermute | solution.py:234
  45.4 40.7 %all-to-all-start.2 = ((bf16[8,2,2,128,128]{4,3,2,1,0:T(8,128)(2,1)}), bf16[8,2,2,128,128]{4,3,2,1,0:T(8,128)(2,1)S(1)}, u32[]{:S(2)}, u32[]{:S(2)}) async-start(bf16[8,2,2,128,128]{4,3,2,1,0:T(8,128)(2,1)} %bitcast.10), calls=%async_computation.2 | async-start | bytes 2097152 | tf_op jit(solution)/shard_map/all_to_all | solution.py:227
  51.5 4.6 %copy-start.2 = (bf16[2,768,4096]{2,1,0:T(8,128)(2,1)S(1)}, bf16[2,768,4096]{2,1,0:T(8,128)(2,1)}, u32[]{:S(2)}) copy-start(bf16[2,768,4096]{2,1,0:T(8,128)(2,1)} %x_ref.15) | copy-start | bytes 37748740
  60.3 53.3 %collective-permute-start.5 = (bf16[4,256,512]{2,1,0:T(8,128)(2,1)}, bf16[4,256,512]{2,1,0:T(8,128)(2,1)}, u32[]{:S(2)}, u32[]{:S(2)}) collective-permute-start(bf16[4,256,512]{2,1,0:T(8,128)(2,1)} %fisher_for_other_core.5), channel_id=1, source_target_pairs={{0,2},{2,0},{4,6},{6,4},{8,10},{10,8},{12,14},{14,12},{1,3},{3,1},... | collective-permute-start | bytes 3145736 | tf_op jit(solution)/shard_map/ppermute | solution.py:234
  66.1 10.9 %collective-permute-start.12 = (bf16[256,512]{1,0:T(8,128)(2,1)S(1)}, bf16[256,512]{1,0:T(8,128)(2,1)S(1)}, u32[]{:S(2)}, u32[]{:S(2)}) collective-permute-start(bf16[256,512]{1,0:T(8,128)(2,1)S(1)} %get-tuple-element.30), channel_id=1, source_target_pairs={{0,4},{2,6},{4,8},{6,10},{8,12},{10,14},{12,0},{14,2},{1,5},{3,7},... | collective-permute-start | bytes 786440 | tf_op jit(solution)/shard_map/ppermute | solution.py:237
  67.4 13.6 %collective-permute-start.13 = (bf16[256,512]{1,0:T(8,128)(2,1)S(1)}, bf16[256,512]{1,0:T(8,128)(2,1)S(1)}, u32[]{:S(2)}, u32[]{:S(2)}) collective-permute-start(bf16[256,512]{1,0:T(8,128)(2,1)S(1)} %get-tuple-element.31), channel_id=1, source_target_pairs={{0,8},{2,10},{4,12},{6,14},{8,0},{10,2},{12,4},{14,6},{1,9},{3,11}... | collective-permute-start | bytes 786440 | tf_op jit(solution)/shard_map/ppermute | solution.py:236
  69.1 13.3 %collective-permute-start.14 = (bf16[256,512]{1,0:T(8,128)(2,1)S(1)}, bf16[256,512]{1,0:T(8,128)(2,1)S(1)}, u32[]{:S(2)}, u32[]{:S(2)}) collective-permute-start(bf16[256,512]{1,0:T(8,128)(2,1)S(1)} %get-tuple-element.32), channel_id=1, source_target_pairs={{0,12},{2,14},{4,0},{6,2},{8,4},{10,6},{12,8},{14,10},{1,13},{3,15... | collective-permute-start | bytes 786440 | tf_op jit(solution)/shard_map/ppermute | solution.py:238
  76.2 0.8 copy-start.7
  77.0 28.5 %copy-start.8 = (f32[256,512]{1,0:T(8,128)S(1)}, f32[256,512]{1,0:T(8,128)}, u32[]{:S(2)}) copy-start(f32[256,512]{1,0:T(8,128)} %copy-done.7) | copy-start | bytes 1572868
  77.0 25.0 %collective-permute-start.16 = (bf16[256,512]{1,0:T(8,128)(2,1)}, bf16[256,512]{1,0:T(8,128)(2,1)}, u32[]{:S(2)}, u32[]{:S(2)}) collective-permute-start(bf16[256,512]{1,0:T(8,128)(2,1)} %get-tuple-element.34), channel_id=1, source_target_pairs={{0,4},{2,6},{4,8},{6,10},{8,12},{10,14},{12,0},{14,2},{1,5},{3,7},... | collective-permute-start | bytes 786440 | tf_op jit(solution)/shard_map/ppermute | solution.py:237
  81.0 22.6 %collective-permute-start.17 = (bf16[256,512]{1,0:T(8,128)(2,1)}, bf16[256,512]{1,0:T(8,128)(2,1)}, u32[]{:S(2)}, u32[]{:S(2)}) collective-permute-start(bf16[256,512]{1,0:T(8,128)(2,1)} %get-tuple-element.35), channel_id=1, source_target_pairs={{0,8},{2,10},{4,12},{6,14},{8,0},{10,2},{12,4},{14,6},{1,9},{3,11}... | collective-permute-start | bytes 786440 | tf_op jit(solution)/shard_map/ppermute | solution.py:236
  82.5 23.1 %collective-permute-start.18 = (bf16[256,512]{1,0:T(8,128)(2,1)}, bf16[256,512]{1,0:T(8,128)(2,1)}, u32[]{:S(2)}, u32[]{:S(2)}) collective-permute-start(bf16[256,512]{1,0:T(8,128)(2,1)} %get-tuple-element.36), channel_id=1, source_target_pairs={{0,12},{2,14},{4,0},{6,2},{8,4},{10,6},{12,8},{14,10},{1,13},{3,15... | collective-permute-start | bytes 786440 | tf_op jit(solution)/shard_map/ppermute | solution.py:238
  86.1 22.4 %all-to-all-start.3 = ((bf16[8,128,128]{2,1,0:T(8,128)(2,1)}), bf16[8,128,128]{2,1,0:T(8,128)(2,1)S(1)}, u32[]{:S(2)}, u32[]{:S(2)}) async-start(bf16[8,128,128]{2,1,0:T(8,128)(2,1)} %fisher_over_tokens.6), calls=%async_computation.3 | async-start | bytes 524288 | tf_op jit(solution)/shard_map/all_to_all | solution.py:240
  91.5 4.6 %copy-start.3 = (bf16[2,768,4096]{2,1,0:T(8,128)(2,1)S(1)}, bf16[2,768,4096]{2,1,0:T(8,128)(2,1)}, u32[]{:S(2)}) copy-start(bf16[2,768,4096]{2,1,0:T(8,128)(2,1)} %x_ref.15) | copy-start | bytes 37748740
  102.0 24.4 %collective-permute-start.2 = (bf16[256,512]{1,0:T(8,128)(2,1)}, bf16[256,512]{1,0:T(8,128)(2,1)S(1)}, u32[]{:S(2)}, u32[]{:S(2)}) collective-permute-start(bf16[256,512]{1,0:T(8,128)(2,1)} %get-tuple-element.22), channel_id=1, source_target_pairs={{0,4},{2,6},{4,8},{6,10},{8,12},{10,14},{12,0},{14,2},{1,5},{3,7},... | collective-permute-start | bytes 786440 | tf_op jit(solution)/shard_map/ppermute | solution.py:237
  102.0 26.5 %collective-permute-start.3 = (bf16[256,512]{1,0:T(8,128)(2,1)}, bf16[256,512]{1,0:T(8,128)(2,1)}, u32[]{:S(2)}, u32[]{:S(2)}) collective-permute-start(bf16[256,512]{1,0:T(8,128)(2,1)} %get-tuple-element.23), channel_id=1, source_target_pairs={{0,8},{2,10},{4,12},{6,14},{8,0},{10,2},{12,4},{14,6},{1,9},{3,11}... | collective-permute-start | bytes 786440 | tf_op jit(solution)/shard_map/ppermute | solution.py:236
  103.5 25.0 %collective-permute-start.4 = (bf16[256,512]{1,0:T(8,128)(2,1)}, bf16[256,512]{1,0:T(8,128)(2,1)}, u32[]{:S(2)}, u32[]{:S(2)}) collective-permute-start(bf16[256,512]{1,0:T(8,128)(2,1)} %get-tuple-element.24), channel_id=1, source_target_pairs={{0,12},{2,14},{4,0},{6,2},{8,4},{10,6},{12,8},{14,10},{1,13},{3,15... | collective-permute-start | bytes 786440 | tf_op jit(solution)/shard_map/ppermute | solution.py:238
  108.5 22.9 %all-to-all-start.4 = ((bf16[8,128,128]{2,1,0:T(8,128)(2,1)}), bf16[8,128,128]{2,1,0:T(8,128)(2,1)S(1)}, u32[]{:S(2)}, u32[]{:S(2)}) async-start(bf16[8,128,128]{2,1,0:T(8,128)(2,1)} %fisher_over_tokens.7), calls=%async_computation.4 | async-start | bytes 524288 | tf_op jit(solution)/shard_map/all_to_all | solution.py:240
  113.6 4.6 %copy-start.4 = (bf16[2,768,4096]{2,1,0:T(8,128)(2,1)S(1)}, bf16[2,768,4096]{2,1,0:T(8,128)(2,1)}, u32[]{:S(2)}) copy-start(bf16[2,768,4096]{2,1,0:T(8,128)(2,1)} %x_ref.15) | copy-start | bytes 37748740
  124.1 0.8 copy-start.9
  124.9 11.6 %collective-permute-start.6 = (bf16[256,512]{1,0:T(8,128)(2,1)}, bf16[256,512]{1,0:T(8,128)(2,1)S(1)}, u32[]{:S(2)}, u32[]{:S(2)}) collective-permute-start(bf16[256,512]{1,0:T(8,128)(2,1)} %get-tuple-element.26), channel_id=1, source_target_pairs={{0,4},{2,6},{4,8},{6,10},{8,12},{10,14},{12,0},{14,2},{1,5},{3,7},... | collective-permute-start | bytes 786440 | tf_op jit(solution)/shard_map/ppermute | solution.py:237
  124.9 11.6 %collective-permute-start.7 = (bf16[256,512]{1,0:T(8,128)(2,1)}, bf16[256,512]{1,0:T(8,128)(2,1)S(1)}, u32[]{:S(2)}, u32[]{:S(2)}) collective-permute-start(bf16[256,512]{1,0:T(8,128)(2,1)} %get-tuple-element.27), channel_id=1, source_target_pairs={{0,8},{2,10},{4,12},{6,14},{8,0},{10,2},{12,4},{14,6},{1,9},{3,11}... | collective-permute-start | bytes 786440 | tf_op jit(solution)/shard_map/ppermute | solution.py:236
  126.5 12.5 %collective-permute-start.8 = (bf16[256,512]{1,0:T(8,128)(2,1)}, bf16[256,512]{1,0:T(8,128)(2,1)S(1)}, u32[]{:S(2)}, u32[]{:S(2)}) collective-permute-start(bf16[256,512]{1,0:T(8,128)(2,1)} %get-tuple-element.28), channel_id=1, source_target_pairs={{0,12},{2,14},{4,0},{6,2},{8,4},{10,6},{12,8},{14,10},{1,13},{3,15... | collective-permute-start | bytes 786440 | tf_op jit(solution)/shard_map/ppermute | solution.py:238
  131.4 11.2 %all-to-all-start = ((bf16[8,128,128]{2,1,0:T(8,128)(2,1)}), bf16[8,128,128]{2,1,0:T(8,128)(2,1)S(1)}, u32[]{:S(2)}, u32[]{:S(2)}) async-start(bf16[8,128,128]{2,1,0:T(8,128)(2,1)} %fisher_over_tokens.4), calls=%async_computation | async-start | bytes 524288 | tf_op jit(solution)/shard_map/all_to_all | solution.py:240
  139.0 1.0 copy-start.10
  142.6 10.1 %all-to-all-start.1 = ((bf16[8,128,128]{2,1,0:T(8,128)(2,1)}), bf16[8,128,128]{2,1,0:T(8,128)(2,1)S(1)}, u32[]{:S(2)}, u32[]{:S(2)}) async-start(bf16[8,128,128]{2,1,0:T(8,128)(2,1)} %fisher_over_tokens.5), calls=%async_computation.1 | async-start | bytes 524288 | tf_op jit(solution)/shard_map/all_to_all | solution.py:240
  153.5 12.3 %collective-permute-start.19 = (f32[128,128]{1,0:T(8,128)S(1)}, f32[128,128]{1,0:T(8,128)S(1)}, u32[]{:S(2)}, u32[]{:S(2)}) collective-permute-start(f32[128,128]{1,0:T(8,128)S(1)} %get-tuple-element.43), channel_id=1, source_target_pairs={{0,0},{1,14},{2,64},{3,78},{4,4},{5,10},{6,68},{7,74},{8,6},{9,8},... | collective-permute-start | bytes 196616 | tf_op jit(solution)/shard_map/ppermute | solution.py:248
  161.2 7.8 %collective-permute-start.20 = (f32[128,128]{1,0:T(8,128)S(1)}, f32[128,128]{1,0:T(8,128)S(1)}, u32[]{:S(2)}, u32[]{:S(2)}) collective-permute-start(f32[128,128]{1,0:T(8,128)S(1)} %get-tuple-element.44), channel_id=1, source_target_pairs={{0,1},{1,15},{2,65},{3,79},{4,5},{5,11},{6,69},{7,75},{8,7},{9,9},... | collective-permute-start | bytes 196616 | tf_op jit(solution)/shard_map/ppermute | solution.py:249

commit v2 on v0

v2 whole, which is shorter than its diff:
```python
import jax
import jax.numpy as jnp
from jax import lax
from jax.experimental import pallas as pl
from jax.experimental.pallas import tpu as pltpu
from jax.sharding import PartitionSpec as P

F32 = jnp.float32
BF16 = jnp.bfloat16
ANY = pl.BlockSpec(memory_space=pltpu.HBM)
SMEM = pl.BlockSpec(memory_space=pltpu.SMEM)
VMEM_LIMIT = 56 << 20

GRID = 1.00297
BIG = 2.0**28
SMALL = 2.0**16
EDGE = 2.0**-40
EDGE_CODE = 2.0**-24

X, CORES, Z = 4, 2, 4


def code_of(values):
    scaled = values * BIG
    return jnp.where(values >= EDGE, scaled * scaled, values * SMALL)


def value_of(code):
    return jnp.where(code >= EDGE_CODE, jnp.sqrt(code) * (1.0 / BIG), code * (1.0 / SMALL))


def encode(values):
    return code_of(values).astype(BF16)


def decode(sent):
    return value_of(sent.astype(F32))


def encode_fine(values):
    code = code_of(values)
    first = code.astype(BF16).astype(F32)
    second = (code * (1.0 / GRID)).astype(BF16).astype(F32)
    near = jnp.abs(first - code) <= jnp.abs(second * GRID - code)
    return jnp.where(near, first, -second).astype(BF16)


def decode_fine(sent):
    code = sent.astype(F32)
    return value_of(jnp.where(code < 0.0, code * (-GRID), code))


def load_all(place, base, member, x_ref, g_ref, x_buf, g_buf, x_sem, g_sem):
    wide = x_buf.shape[2]
    g_copy = pltpu.make_async_copy(g_ref, g_buf, g_sem)
    g_copy.start()
    copies = []
    for s in range(4):
        at = pl.multiple_of(place[base + s] * wide, wide)
        copies.append(pltpu.make_async_copy(x_ref.at[member, :, pl.ds(at, wide)], x_buf.at[s], x_sem.at[s]))
        copies[s].start()
    return g_copy, copies


def squared_grads(g_copy, g_buf, gt_buf):
    g_copy.wait()
    g = g_buf[...].astype(F32)
    gt_buf[...] = (g * g).T.astype(BF16)


def send_kernel(member, place, x_ref, g_ref, after, out_ref, x_buf, g_buf, gt_buf, out_buf, x_sem, g_sem, out_sem):
    g_copy, copies = load_all(place, 0, member, x_ref, g_ref, x_buf, g_buf, x_sem, g_sem)
    squared_grads(g_copy, g_buf, gt_buf)
    outs = []
    for s in range(4):
        copies[s].wait()
        x = x_buf[s]
        out_buf[s] = jnp.dot(gt_buf[...], x * x, preferred_element_type=F32).astype(BF16)
        outs.append(pltpu.make_async_copy(out_buf.at[s], out_ref.at[s], out_sem.at[s]))
        outs[s].start()
    for copy in outs:
        copy.wait()


def own_kernel(
    member, place, x_ref, g_ref, got_ref, after, two_ref, one_ref, three_ref, own_ref,
    x_buf, g_buf, gt_buf, got_buf, out_buf, own_buf, x_sem, g_sem, got_sem, out_sem,
):
    g_copy, copies = load_all(place, 4, member, x_ref, g_ref, x_buf, g_buf, x_sem, g_sem)
    gots = []
    for s in range(4):
        gots.append(pltpu.make_async_copy(got_ref.at[s], got_buf.at[s], got_sem.at[s]))
        gots[s].start()
    squared_grads(g_copy, g_buf, gt_buf)
    outs = []
    for s, ref in enumerate((two_ref, one_ref, three_ref, own_ref)):
        copies[s].wait()
        gots[s].wait()
        x = x_buf[s]
        block = jnp.dot(gt_buf[...], x * x, preferred_element_type=F32) + got_buf[s].astype(F32)
        if s < 3:
            out_buf[s] = encode(block)
            outs.append(pltpu.make_async_copy(out_buf.at[s], ref, out_sem.at[s]))
        else:
            own_buf[...] = block
            outs.append(pltpu.make_async_copy(own_buf, ref, out_sem.at[s]))
        outs[s].start()
    for copy in outs:
        copy.wait()


def kernel_sizes(inputs, grads):
    tokens, width = inputs.shape[1:]
    return tokens, grads.shape[1], width // 8


def fisher_cost(tokens, outs, wide):
    return pl.CostEstimate(
        flops=8 * outs * wide * tokens, bytes_accessed=8 * tokens * wide + 16 * outs * wide, transcendentals=0
    )


def send_part(place, inputs, grads, member, after):
    tokens, outs, wide = kernel_sizes(inputs, grads)
    return pl.pallas_call(
        lambda *refs: send_kernel(member, *refs),
        out_shape=jax.ShapeDtypeStruct((4, outs, wide), BF16),
        in_specs=[SMEM, ANY, ANY, ANY],
        out_specs=ANY,
        scratch_shapes=[
            pltpu.VMEM((4, tokens, wide), BF16),
            pltpu.VMEM((tokens, outs), BF16),
            pltpu.VMEM((outs, tokens), BF16),
            pltpu.VMEM((4, outs, wide), BF16),
            pltpu.SemaphoreType.DMA((4,)),
            pltpu.SemaphoreType.DMA,
            pltpu.SemaphoreType.DMA((4,)),
        ],
        compiler_params=pltpu.CompilerParams(vmem_limit_bytes=VMEM_LIMIT),
        cost_estimate=fisher_cost(tokens, outs, wide),
        name="fisher_for_other_core",
    )(place, inputs, grads, after)


def own_part(place, inputs, grads, got, member, after):
    tokens, outs, wide = kernel_sizes(inputs, grads)
    sent = jax.ShapeDtypeStruct((outs, wide), BF16)
    return pl.pallas_call(
        lambda *refs: own_kernel(member, *refs),
        out_shape=[sent, sent, sent, jax.ShapeDtypeStruct((outs, wide), F32)],
        in_specs=[SMEM, ANY, ANY, ANY, ANY],
        out_specs=[ANY] * 4,
        scratch_shapes=[
            pltpu.VMEM((4, tokens, wide), BF16),
            pltpu.VMEM((tokens, outs), BF16),
            pltpu.VMEM((outs, tokens), BF16),
            pltpu.VMEM((4, outs, wide), BF16),
            pltpu.VMEM((3, outs, wide), BF16),
            pltpu.VMEM((outs, wide), F32),
            pltpu.SemaphoreType.DMA((4,)),
            pltpu.SemaphoreType.DMA,
            pltpu.SemaphoreType.DMA((4,)),
            pltpu.SemaphoreType.DMA((4,)),
        ],
        compiler_params=pltpu.CompilerParams(vmem_limit_bytes=VMEM_LIMIT),
        cost_estimate=fisher_cost(tokens, outs, wide),
        name="fisher_of_own_core",
    )(place, inputs, grads, got, after)


def pick_kernel(half, w_ref, after, a_ref, b_ref, sem):
    rows = a_ref.shape[1]
    copies = []
    for flip, ref in enumerate((a_ref, b_ref)):
        at = pl.multiple_of((half[0] ^ flip) * rows, rows)
        copies.append(pltpu.make_async_copy(w_ref.at[:, pl.ds(at, rows), :], ref, sem.at[flip]))
        copies[flip].start()
    for copy in copies:
        copy.wait()


def pick_weights(half, weights, after):
    members, rows, outs = weights.shape
    part = jax.ShapeDtypeStruct((members, rows // 2, outs), BF16)
    return pl.pallas_call(
        pick_kernel,
        out_shape=[part, part],
        in_specs=[SMEM, ANY, ANY],
        out_specs=[ANY, ANY],
        scratch_shapes=[pltpu.SemaphoreType.DMA((2,))],
        compiler_params=pltpu.CompilerParams(vmem_limit_bytes=VMEM_LIMIT),
        cost_estimate=pl.CostEstimate(flops=0, bytes_accessed=4 * members * rows * outs, transcendentals=0),
        name="pick_weights",
    )(half, weights, after)


def weigh_kernel(which, *refs):
    parts, (w_a, w_b, after, out_ref), (buf, own_buf, w_buf, out_buf, sem, w_sem, out_sem) = refs[:8], refs[8:12], refs[12:]
    copies = []
    for m in range(2):
        for j in range(3):
            copies.append(pltpu.make_async_copy(parts[4 * m + j], buf.at[m, j], sem.at[m, j]))
        copies.append(pltpu.make_async_copy(parts[4 * m + 3], own_buf.at[m], sem.at[m, 3]))
    for copy in copies:
        copy.start()

    @pl.when(which[0] == 0)
    def _():
        pltpu.make_async_copy(w_a, w_buf, w_sem).start()

    @pl.when(which[0] != 0)
    def _():
        pltpu.make_async_copy(w_b, w_buf, w_sem).start()

    for copy in copies:
        copy.wait()
    pltpu.make_async_copy(w_a, w_buf, w_sem).wait()
    outs, wide = own_buf.shape[1:]
    half, part = outs // 2, wide // Z
    done = []
    for z in range(Z):
        cols = slice(z * part, (z + 1) * part)
        weighted = total = None
        for m in range(2):
            fisher = own_buf[m, :, cols]
            for j in range(3):
                fisher += decode(buf[m, j, :, cols])
            fisher = fisher.T
            product = fisher * w_buf[m, cols, :].astype(F32)
            weighted = product if m == 0 else weighted + product
            total = fisher if m == 0 else total + fisher
        high = weighted.astype(BF16)
        low = (weighted - high.astype(F32)).astype(BF16)
        code = encode_fine(total)
        for y in range(2):
            outcols = slice(y * half, (y + 1) * half)
            for word, values in enumerate((high, low, code)):
                out_buf[y * Z + z, word] = values[:, outcols]
            done.append(pltpu.make_async_copy(out_buf.at[y * Z + z], out_ref.at[y * Z + z], out_sem.at[y * Z + z]))
            done[-1].start()
    for copy in done:
        copy.wait()


def weigh(which, parts, w_a, w_b, after):
    outs, wide = parts[3].shape
    members = w_a.shape[0]
    shape = (2 * Z, 3, wide // Z, outs // 2)
    return pl.pallas_call(
        weigh_kernel,
        out_shape=jax.ShapeDtypeStruct(shape, BF16),
        in_specs=[SMEM] + [ANY] * 11,
        out_specs=ANY,
        scratch_shapes=[
            pltpu.VMEM((members, 3, outs, wide), BF16),
            pltpu.VMEM((members, outs, wide), F32),
            pltpu.VMEM(w_a.shape, BF16),
            pltpu.VMEM(shape, BF16),
            pltpu.SemaphoreType.DMA((members, 4)),
            pltpu.SemaphoreType.DMA,
            pltpu.SemaphoreType.DMA((2 * Z,)),
        ],
        compiler_params=pltpu.CompilerParams(vmem_limit_bytes=VMEM_LIMIT),
        cost_estimate=pl.CostEstimate(flops=40 * outs * wide, bytes_accessed=30 * outs * wide, transcendentals=0),
        name="weigh_members",
    )(which, *parts, w_a, w_b, after)


def merge_kernel(got_ref, out_ref):
    weighted = total = 0.0
    for group in range(got_ref.shape[0]):
        weighted += got_ref[group, 0].astype(F32) + got_ref[group, 1].astype(F32)
        total += decode_fine(got_ref[group, 2])
    out_ref[...] = weighted / total


def merge(got):
    groups, words, rows, cols = got.shape
    return pl.pallas_call(
        merge_kernel,
        out_shape=jax.ShapeDtypeStruct((rows, cols), F32),
        compiler_params=pltpu.CompilerParams(vmem_limit_bytes=VMEM_LIMIT),
        cost_estimate=pl.CostEstimate(
            flops=20 * groups * rows * cols, bytes_accessed=6 * groups * rows * cols, transcendentals=0
        ),
        name="merge_members",
    )(got)


def keeper(local, half):
    home = 2 * half + local // 2
    return home if local % 2 == 0 else 3 - home


def kept(x, half):
    return 2 * (x % 2) if x // 2 == half else 2 * ((3 - x) % 2) + 1


def weight_pairs(flip):
    pairs = []
    for tok in range(X * CORES):
        half, local = divmod(tok, 4)
        for col in range(2):
            to = keeper(local, half) * 2 + (col ^ flip)
            pairs.append((tok * 2 + col, to * 2 + half))
    return pairs


def result_pairs(flip):
    pairs = []
    for member in range(8):
        y_lo, z = divmod(member, 4)
        for tok in range(8):
            x, core = divmod(tok, 2)
            for half in range(2):
                to_member = core * 4 + z
                to_tok = 4 * half + kept(x, half)
                to_col = y_lo ^ flip
                pairs.append(((member * 8 + tok) * 2 + half, (to_member * 8 + to_tok) * 2 + to_col))
    return pairs


def x_pairs(distance):
    return [(t, ((t // 2 + distance) % X) * 2 + t % 2) for t in range(X * CORES)]


def shards(inputs, grads, weights):
    tok = lax.axis_index("tok")
    half = lax.axis_index("col")
    x, core = tok // 2, tok % 2
    y_lo = lax.axis_index("member") // 4

    steps = (x + jnp.array([2, 1, 3, 0], jnp.int32)) % X
    local = jnp.where(steps // 2 == half, 2 * (steps % 2), 2 * ((3 - steps) % 2) + 1)
    place = jnp.concatenate([2 * local + 1 - core, 2 * local + core]).astype(jnp.int32)

    own_grads = [grads[0], grads[1]]
    other_grads = [lax.ppermute(g, "col", [(0, 1), (1, 0)]) for g in own_grads]

    after = place
    words = []
    moved = None
    for phase, gs in enumerate((own_grads, other_grads)):
        got = []
        for member in range(2):
            after = send_part(place, inputs, gs[member], member, after)
            got.append(lax.ppermute(after, "tok", [(t, t ^ 1) for t in range(8)]))
        parts = []
        for member in range(2):
            two, one, three, own = own_part(place, inputs, gs[member], got[member], member, after)
            after = own
            two = lax.ppermute(two, "tok", x_pairs(2))
            one = lax.ppermute(one, "tok", x_pairs(1))
            three = lax.ppermute(three, "tok", x_pairs(3))
            parts += [two, one, three, own]
            if moved is None:
                picked = pick_weights(half.reshape(1), weights, after)
                moved = [lax.ppermute(w, ("tok", "col"), weight_pairs(flip)) for flip, w in enumerate(picked)]
        words.append(parts)

    merged = []
    for phase in range(2):
        which = ((core ^ half) ^ phase).astype(jnp.int32).reshape(1)
        after = weigh(which, words[phase], moved[0], moved[1], after)
        merged.append(merge(lax.all_to_all(after, "member", 0, 0, tiled=True)))

    swap = (y_lo ^ half) == 1
    near = jnp.where(swap, merged[1], merged[0])
    far = jnp.where(swap, merged[0], merged[1])
    names = ("member", "tok", "col")
    near = lax.ppermute(near, names, result_pairs(0))
    far = lax.ppermute(far, names, result_pairs(1))
    left = jnp.where(half == 0, near, far)
    right = jnp.where(half == 0, far, near)
    return jnp.concatenate([left, right], axis=1)


def solution(mesh):
    in_specs = (P("member", "tok", "col"), P("member", "tok", "col"), P("member", "tok", "col"))
    out_specs = P(("tok", "member"), "col")
    return jax.shard_map(shards, mesh=mesh, in_specs=in_specs, out_specs=out_specs, check_vma=False)
```

time: 717 us -> 187 us (0.26)
  waiting for transfers between devices: 633 us -> 41.1 us
  Pallas kernels: 0 us -> 87.4 us
  starting transfers between devices: 0.08 us -> 46.5 us
  matrix products: 21.9 us -> 0 us
  other arithmetic: 19.9 us -> 2.91 us
  local copies, waits for them, and re-layouts: 22.9 us -> 8.22 us
  between operations: 13.1 us -> 0.47 us
    all_gather x2 -> x0, waiting for transfers between devices: 327 us -> none  [the longest x1 300 us: shards(): input_sq = lax.all_gather(squared(inputs), 'col', axis=2, tiled=True)]
    reduce_scatter x1 -> x0, waiting for transfers between devices: 306 us -> none  [shards(): lax.psum_scatter(sums, ('member', 'tok'), scatter_dimension=1, tiled=True)]
    pallas_call x0 -> x13, Pallas kernels: none -> 87.4 us  [the longest x1 32.9 us: pick_weights(): pl.pallas_call(pick_kernel, out_shape=[part, part], in_specs=[SMEM, ANY,...]
    ppermute x0 -> x22, starting transfers between devices: none -> 36.5 us  [the longest x2 10 us: shards(): lax.ppermute(w, ('tok', 'col'), weight_pairs(flip))]
    ppermute x0 -> x22, waiting for transfers between devices: none -> 31.6 us  [the longest x4 25.6 us: shards(): one = lax.ppermute(one, 'tok', x_pairs(1))]
    dot_general x1 -> x0, matrix products: 21.9 us -> none  [shards(): jnp.einsum('mti,mto->mio', input_sq, grad_sq, preferred_element_type=jnp....]
    convert_element_type x1 -> x0, other arithmetic: 11.5 us -> none  [squared(): return (values.astype(jnp.float32) ** 2).astype(jnp.bfloat16)]
    unnamed x3 -> x54, local copies, waits for them, and re-layouts: 16.7 us -> 6.16 us
  transfers between devices with their start and end apart: 3 -> 24, of which waited for: 3 -> 7; matrix products, arithmetic and copies ran while one was open for 4% -> 0% of each run, Pallas kernels for 0% -> 41%
where the time goes in v2:
time: 187 us
  Pallas kernels  87.4 us (47%)
  starting transfers between devices  46.5 us (25%)
  waiting for transfers between devices  41.1 us (22%)
  local copies, waits for them, and re-layouts  8.22 us (4%)
  other arithmetic  2.91 us (2%)
    pallas_call x1, Pallas kernels, pick_weights(): pl.pallas_call(pick_kernel, out_shape=[part, part], in_specs=[SMEM, ANY,...  32.9 us
    ppermute x4, waiting for transfers between devices, shards(): one = lax.ppermute(one, 'tok', x_pairs(1))  25.6 us
    pallas_call x4, Pallas kernels, own_part(): pl.pallas_call(lambda *refs: own_kernel(member, *refs), out_shape=[sent,...  21.7 us
    pallas_call x4, Pallas kernels, send_part(): pl.pallas_call(lambda *refs: send_kernel(member, *refs), out_shape=jax.Sh...  19.8 us
    ppermute x2, starting transfers between devices, shards(): lax.ppermute(w, ('tok', 'col'), weight_pairs(flip))  10 us
    all_to_all x2, starting transfers between devices, shards(): merged.append(merge(lax.all_to_all(after, 'member', 0, 0, tiled=True)))  9.92 us
    all_to_all x2, waiting for transfers between devices, shards(): merged.append(merge(lax.all_to_all(after, 'member', 0, 0, tiled=True)))  9.52 us
    pallas_call x2, Pallas kernels, weigh(): pl.pallas_call(weigh_kernel, out_shape=jax.ShapeDtypeStruct(shape, BF16),...  8.89 us
  transfers between devices with their start and end apart: 24, of which 7 were waited for; matrix products, arithmetic and copies ran while one was open for 0% of the time, Pallas kernels for 41%

profile of v2, /device:TPU:1, one launch (start us, length us, event | category | flops | bytes accessed | tf_op | source)
XLA Modules:
  0.0 186.6 jit_solution(9732724418561320138)
XLA Ops:
  0.0 0.7 add_subtract_fusion
  0.7 2.1 %slice_bitcast_fusion = (bf16[768,256]{1,0:T(8,128)(2,1)}, bf16[768,256]{1,0:T(8,128)(2,1)}) fusion(bf16[2,768,256]{2,1,0:T(8,128)(2,1)} %param.5), kind=kLoop, calls=%fused_computation | loop fusion | bytes 1572864 | tf_op jit(solution)/shard_map/squeeze | solution.py:337
  2.7 0.7 pad_add_fusion.refs_0_.refs_3_
  3.4 5.1 %fisher_for_other_core.4.refs_3_ = bf16[4,256,512]{2,1,0:T(8,128)(2,1)} custom-call(s32[8]{0:T(128)} %pad_add_fusion.refs_0_.refs_3_, bf16[2,768,4096]{2,1,0:T(8,128)(2,1)} %refs_1_.15, bf16[768,256]{1,0:T(8,128)(2,1)} %get-tuple-element.44.refs_2_, s32[8]{0:T(128)} %pad_add_fusion.refs_0_.refs_3_), custom_call_target="tpu_custom_call" | custom-call | flops 805306368 | bytes 5242880 | tf_op jit(solution)/shard_map/fisher_for_other_core/pallas_call | solution.py:125
  8.5 1.5 collective-permute-start.2
  10.0 4.8 %fisher_for_other_core.5.refs_4_ = bf16[4,256,512]{2,1,0:T(8,128)(2,1)} custom-call(s32[8]{0:T(128)} %pad_add_fusion.refs_0_.refs_3_, bf16[2,768,4096]{2,1,0:T(8,128)(2,1)} %refs_1_.15, bf16[768,256]{1,0:T(8,128)(2,1)} %get-tuple-element.43.refs_2_, bf16[4,256,512]{2,1,0:T(8,128)(2,1)} %fisher_for_other_core.4.refs_3_), custom_call_target="tpu_custom_call" | custom-call | flops 805306368 | bytes 5242880 | tf_op jit(solution)/shard_map/fisher_for_other_core/pallas_call | solution.py:125
  15.0 3.2 %collective-permute-start = (bf16[768,256]{1,0:T(8,128)(2,1)S(1)}, bf16[768,256]{1,0:T(8,128)(2,1)S(1)}, u32[]{:S(2)}, u32[]{:S(2)}) collective-permute-start(bf16[768,256]{1,0:T(8,128)(2,1)S(1)} %copy-done), channel_id=1, source_target_pairs={{0,1},{1,0},{2,3},{3,2},{4,5},{5,4},{6,7},{7,6},{8,9},{9,8},{10,11... | collective-permute-start | bytes 1179656 | tf_op jit(solution)/shard_map/ppermute | solution.py:338
  18.3 1.0 copy-done.10
  19.3 5.4 %fisher_of_own_core.4 = (bf16[256,512]{1,0:T(8,128)(2,1)}, bf16[256,512]{1,0:T(8,128)(2,1)}, bf16[256,512]{1,0:T(8,128)(2,1)}, f32[256,512]{1,0:T(8,128)}) custom-call(s32[8]{0:T(128)} %pad_add_fusion.refs_0_.refs_3_, bf16[2,768,4096]{2,1,0:T(8,128)(2,1)} %refs_1_.15, bf16[768,256]{1,0:T(8,128)(2,1)} %get-tuple-element.44.refs_2_, ...), custom_call_target="tpu_custom_call" | custom-call | flops 805306368 | bytes 5242880 | tf_op jit(solution)/shard_map/fisher_of_own_core/pallas_call | solution.py:148
  24.6 1.0 copy-done.9
  25.7 5.4 %fisher_of_own_core.5 = (bf16[256,512]{1,0:T(8,128)(2,1)}, bf16[256,512]{1,0:T(8,128)(2,1)}, bf16[256,512]{1,0:T(8,128)(2,1)}, f32[256,512]{1,0:T(8,128)}) custom-call(s32[8]{0:T(128)} %pad_add_fusion.refs_0_.refs_3_, bf16[2,768,4096]{2,1,0:T(8,128)(2,1)} %refs_1_.15, bf16[768,256]{1,0:T(8,128)(2,1)} %get-tuple-element.43.refs_2_, ...), custom_call_target="tpu_custom_call" | custom-call | flops 805306368 | bytes 5242880 | tf_op jit(solution)/shard_map/fisher_of_own_core/pallas_call | solution.py:148
  31.1 0.7 copy-done.7
  31.8 5.0 %fisher_for_other_core.6.refs_3_ = bf16[4,256,512]{2,1,0:T(8,128)(2,1)} custom-call(s32[8]{0:T(128)} %pad_add_fusion.refs_0_.refs_3_, bf16[2,768,4096]{2,1,0:T(8,128)(2,1)} %refs_1_.15, bf16[768,256]{1,0:T(8,128)(2,1)} %copy-done.7, f32[256,512]{1,0:T(8,128)} %get-tuple-element.24.refs_3_.refs_7_), custom_call_target="tpu_custom_call" | custom-call | flops 805306368 | bytes 5242880 | tf_op jit(solution)/shard_map/fisher_for_other_core/pallas_call | solution.py:125
  36.8 0.8 collective-permute-start.3
  37.6 0.7 copy-done.6
  38.4 4.8 %fisher_for_other_core.7.refs_4_ = bf16[4,256,512]{2,1,0:T(8,128)(2,1)} custom-call(s32[8]{0:T(128)} %pad_add_fusion.refs_0_.refs_3_, bf16[2,768,4096]{2,1,0:T(8,128)(2,1)} %refs_1_.15, bf16[768,256]{1,0:T(8,128)(2,1)} %copy-done.6, bf16[4,256,512]{2,1,0:T(8,128)(2,1)} %fisher_for_other_core.6.refs_3_), custom_call_target="tpu_custom_call" | custom-call | flops 805306368 | bytes 5242880 | tf_op jit(solution)/shard_map/fisher_for_other_core/pallas_call | solution.py:125
  43.3 3.2 %collective-permute-start.17 = (bf16[256,512]{1,0:T(8,128)(2,1)S(1)}, bf16[256,512]{1,0:T(8,128)(2,1)S(1)}, u32[]{:S(2)}, u32[]{:S(2)}) collective-permute-start(bf16[256,512]{1,0:T(8,128)(2,1)S(1)} %copy-done.26), channel_id=1, source_target_pairs={{0,8},{2,10},{4,12},{6,14},{8,0},{10,2},{12,4},{14,6},{1,9},{3,11}... | collective-permute-start | bytes 786440 | tf_op jit(solution)/shard_map/ppermute | solution.py:352
  46.6 2.5 %collective-permute-start.19 = (bf16[256,512]{1,0:T(8,128)(2,1)S(1)}, bf16[256,512]{1,0:T(8,128)(2,1)S(1)}, u32[]{:S(2)}, u32[]{:S(2)}) collective-permute-start(bf16[256,512]{1,0:T(8,128)(2,1)S(1)} %copy-done.24), channel_id=1, source_target_pairs={{0,12},{2,14},{4,0},{6,2},{8,4},{10,6},{12,8},{14,10},{1,13},{3,15... | collective-permute-start | bytes 786440 | tf_op jit(solution)/shard_map/ppermute | solution.py:354
  49.2 32.9 %pick_weights.1 = (bf16[2,512,256]{2,1,0:T(8,128)(2,1)}, bf16[2,512,256]{2,1,0:T(8,128)(2,1)}) custom-call(s32[1]{0:T(128)} %bitcast.3.half, bf16[2,1024,256]{2,1,0:T(8,128)(2,1)} %w_ref.1, f32[256,512]{1,0:T(8,128)} %get-tuple-element.23.refs_4_.after.refs_3_), custom_call_target="tpu_custom_call" | custom-call | bytes 2097152 | tf_op jit(solution)/shard_map/pick_weights/pallas_call | solution.py:185
  82.1 2.8 %collective-permute-start.12 = (bf16[2,512,256]{2,1,0:T(8,128)(2,1)}, bf16[2,512,256]{2,1,0:T(8,128)(2,1)S(1)}, u32[]{:S(2)}, u32[]{:S(2)}) collective-permute-start(bf16[2,512,256]{2,1,0:T(8,128)(2,1)} %get-tuple-element.33), channel_id=1, source_target_pairs={{0,0},{1,2},{2,12},{3,14},{4,4},{5,6},{6,8},{7,10},{8,9},{9,11},{1... | collective-permute-start | bytes 1572872 | tf_op jit(solution)/shard_map/ppermute | solution.py:358
  84.9 7.2 %collective-permute-start.13 = (bf16[2,512,256]{2,1,0:T(8,128)(2,1)}, bf16[2,512,256]{2,1,0:T(8,128)(2,1)S(1)}, u32[]{:S(2)}, u32[]{:S(2)}) collective-permute-start(bf16[2,512,256]{2,1,0:T(8,128)(2,1)} %get-tuple-element.34), channel_id=1, source_target_pairs={{0,2},{1,0},{2,14},{3,12},{4,6},{5,4},{6,10},{7,8},{8,11},{9,9},{1... | collective-permute-start | bytes 1572872 | tf_op jit(solution)/shard_map/ppermute | solution.py:358
  92.2 0.6 collective-permute-start.15
  92.8 2.2 %collective-permute-start.16 = (bf16[256,512]{1,0:T(8,128)(2,1)}, bf16[256,512]{1,0:T(8,128)(2,1)}, u32[]{:S(2)}, u32[]{:S(2)}) collective-permute-start(bf16[256,512]{1,0:T(8,128)(2,1)} %get-tuple-element.37), channel_id=1, source_target_pairs={{0,12},{2,14},{4,0},{6,2},{8,4},{10,6},{12,8},{14,10},{1,13},{3,15... | collective-permute-start | bytes 786440 | tf_op jit(solution)/shard_map/ppermute | solution.py:354
  95.0 5.4 %fisher_of_own_core.6 = (bf16[256,512]{1,0:T(8,128)(2,1)}, bf16[256,512]{1,0:T(8,128)(2,1)}, bf16[256,512]{1,0:T(8,128)(2,1)}, f32[256,512]{1,0:T(8,128)}) custom-call(s32[8]{0:T(128)} %pad_add_fusion.refs_0_.refs_3_, bf16[2,768,4096]{2,1,0:T(8,128)(2,1)} %refs_1_.15, bf16[768,256]{1,0:T(8,128)(2,1)} %copy-done.7, bf16[4,256,512]{2,1,0:T(8,128)(2,1)} %copy-done.8, ...), custom_call_target="tpu_custom_call" | custom-call | flops 805306368 | bytes 5242880 | tf_op jit(solution)/shard_map/fisher_of_own_core/pallas_call | solution.py:148
  100.4 5.6 %fisher_of_own_core.7 = (bf16[256,512]{1,0:T(8,128)(2,1)}, bf16[256,512]{1,0:T(8,128)(2,1)}, bf16[256,512]{1,0:T(8,128)(2,1)}, f32[256,512]{1,0:T(8,128)}) custom-call(s32[8]{0:T(128)} %pad_add_fusion.refs_0_.refs_3_, bf16[2,768,4096]{2,1,0:T(8,128)(2,1)} %refs_1_.15, bf16[768,256]{1,0:T(8,128)(2,1)} %copy-done.6, ...), custom_call_target="tpu_custom_call" | custom-call | flops 805306368 | bytes 5242880 | tf_op jit(solution)/shard_map/fisher_of_own_core/pallas_call | solution.py:148
  106.0 7.8 %collective-permute-done.15.refs_1_ = bf16[256,512]{1,0:T(8,128)(2,1)S(1)} collective-permute-done((bf16[256,512]{1,0:T(8,128)(2,1)}, bf16[256,512]{1,0:T(8,128)(2,1)S(1)}, u32[]{:S(2)}, u32[]{:S(2)}) %collective-permute-start.15) | collective-permute-done | bytes 262176 | tf_op jit(solution)/shard_map/ppermute | solution.py:353
  113.9 0.6 copy-done.15
  114.5 0.2 copy-done.4
  114.9 4.4 %weigh_members.2.refs_10_ = bf16[8,3,128,128]{3,2,1,0:T(8,128)(2,1)} custom-call(s32[1]{0:T(128)} %bitcast.4.which, bf16[256,512]{1,0:T(8,128)(2,1)} %copy-done.14, bf16[256,512]{1,0:T(8,128)(2,1)} %copy-done.15, bf16[256,512]{1,0:T(8,128)(2,1)} %collective-permute-done.16.refs_2_, f32[256,512]{1,0:T(8,128)} %get-tuple-element.23.refs_4_.after.refs_3_, ...), custom_call_target="tpu_custom_call" | custom-call | flops 5242880 | bytes 3932160 | tf_op jit(solution)/shard_map/weigh_members/pallas_call | solution.py:249
  119.3 5.2 %all-to-all-start.1 = ((bf16[8,3,128,128]{3,2,1,0:T(8,128)(2,1)}), bf16[8,3,128,128]{3,2,1,0:T(8,128)(2,1)S(1)}, u32[]{:S(2)}, u32[]{:S(2)}) async-start(bf16[8,3,128,128]{3,2,1,0:T(8,128)(2,1)} %weigh_members.2.refs_10_), calls=%async_computation.1 | async-start | bytes 1572864 | tf_op jit(solution)/shard_map/all_to_all | solution.py:365
  124.5 2.7 %collective-permute-start.11 = (bf16[256,512]{1,0:T(8,128)(2,1)}, bf16[256,512]{1,0:T(8,128)(2,1)S(1)}, u32[]{:S(2)}, u32[]{:S(2)}) collective-permute-start(bf16[256,512]{1,0:T(8,128)(2,1)} %get-tuple-element.31), channel_id=1, source_target_pairs={{0,12},{2,14},{4,0},{6,2},{8,4},{10,6},{12,8},{14,10},{1,13},{3,15... | collective-permute-start | bytes 786440 | tf_op jit(solution)/shard_map/ppermute | solution.py:354
  127.2 3.0 %collective-permute-start.5 = (bf16[256,512]{1,0:T(8,128)(2,1)}, bf16[256,512]{1,0:T(8,128)(2,1)S(1)}, u32[]{:S(2)}, u32[]{:S(2)}) collective-permute-start(bf16[256,512]{1,0:T(8,128)(2,1)} %get-tuple-element.25), channel_id=1, source_target_pairs={{0,8},{2,10},{4,12},{6,14},{8,0},{10,2},{12,4},{14,6},{1,9},{3,11}... | collective-permute-start | bytes 786440 | tf_op jit(solution)/shard_map/ppermute | solution.py:352
  130.1 14.0 %collective-permute-done.10.refs_5_ = bf16[256,512]{1,0:T(8,128)(2,1)S(1)} collective-permute-done((bf16[256,512]{1,0:T(8,128)(2,1)}, bf16[256,512]{1,0:T(8,128)(2,1)S(1)}, u32[]{:S(2)}, u32[]{:S(2)}) %collective-permute-start.10) | collective-permute-done | bytes 262176 | tf_op jit(solution)/shard_map/ppermute | solution.py:353
  144.3 3.7 %collective-permute-done.6.refs_1_ = bf16[256,512]{1,0:T(8,128)(2,1)S(1)} collective-permute-done((bf16[256,512]{1,0:T(8,128)(2,1)S(1)}, bf16[256,512]{1,0:T(8,128)(2,1)S(1)}, u32[]{:S(2)}, u32[]{:S(2)}) %collective-permute-start.6) | collective-permute-done | bytes 262176 | tf_op jit(solution)/shard_map/ppermute | solution.py:353
  148.0 1.4 collective-permute-done.7.refs_2_
  149.4 0.7 copy-done.21
  150.1 4.4 %weigh_members.3 = bf16[8,3,128,128]{3,2,1,0:T(8,128)(2,1)} custom-call(s32[1]{0:T(128)} %bitcast.which, bf16[256,512]{1,0:T(8,128)(2,1)} %copy-done.19, bf16[256,512]{1,0:T(8,128)(2,1)} %copy-done.20, bf16[256,512]{1,0:T(8,128)(2,1)} %copy-done.21, f32[256,512]{1,0:T(8,128)} %get-tuple-element.28.refs_4_.refs_3_, bf16[256,512]{1,0:T(8,128)(2,1)} %copy-done.18, ...), custom_call_target="tpu_custom_call" | custom-call | flops 5242880 | bytes 3932160 | tf_op jit(solution)/shard_map/weigh_members/pallas_call | solution.py:249
  154.6 4.8 %all-to-all-start = ((bf16[8,3,128,128]{3,2,1,0:T(8,128)(2,1)}), bf16[8,3,128,128]{3,2,1,0:T(8,128)(2,1)S(1)}, u32[]{:S(2)}, u32[]{:S(2)}) async-start(bf16[8,3,128,128]{3,2,1,0:T(8,128)(2,1)} %weigh_members.3), calls=%async_computation | async-start | bytes 1572864 | tf_op jit(solution)/shard_map/all_to_all | solution.py:365
  159.3 2.1 %merge_members.3 = f32[128,128]{1,0:T(8,128)} custom-call(bf16[8,3,128,128]{3,2,1,0:T(8,128)(2,1)} %copy-done.2), custom_call_target="tpu_custom_call" | custom-call | flops 2621440 | bytes 786432 | tf_op jit(solution)/shard_map/merge_members/pallas_call | solution.py:279
  161.4 9.5 %all-to-all-done.got_ref = bf16[8,3,128,128]{3,2,1,0:T(8,128)(2,1)S(1)} async-done(((bf16[8,3,128,128]{3,2,1,0:T(8,128)(2,1)}), bf16[8,3,128,128]{3,2,1,0:T(8,128)(2,1)S(1)}, u32[]{:S(2)}, u32[]{:S(2)}) %all-to-all-start) | async-done | bytes 786464 | tf_op jit(solution)/shard_map/all_to_all | solution.py:365
  171.0 0.9 copy-done.3
  171.9 2.1 %merge_members.2 = f32[128,128]{1,0:T(8,128)} custom-call(bf16[8,3,128,128]{3,2,1,0:T(8,128)(2,1)} %copy-done.3), custom_call_target="tpu_custom_call" | custom-call | flops 2621440 | bytes 786432 | tf_op jit(solution)/shard_map/merge_members/pallas_call | solution.py:279
  174.0 0.9 broadcast_select_fusion.1
  174.9 3.3 %collective-permute-start.20 = (f32[128,128]{1,0:T(8,128)S(1)}, f32[128,128]{1,0:T(8,128)S(1)}, u32[]{:S(2)}, u32[]{:S(2)}) collective-permute-start(f32[128,128]{1,0:T(8,128)S(1)} %get-tuple-element.47), channel_id=1, source_target_pairs={{0,0},{1,14},{2,64},{3,78},{4,4},{5,10},{6,68},{7,74},{8,6},{9,8},... | collective-permute-start | bytes 196616 | tf_op jit(solution)/shard_map/ppermute | solution.py:371
  178.2 3.1 %collective-permute-start.21 = (f32[128,128]{1,0:T(8,128)S(1)}, f32[128,128]{1,0:T(8,128)S(1)}, u32[]{:S(2)}, u32[]{:S(2)}) collective-permute-start(f32[128,128]{1,0:T(8,128)S(1)} %get-tuple-element.48), channel_id=1, source_target_pairs={{0,1},{1,15},{2,65},{3,79},{4,5},{5,11},{6,69},{7,75},{8,7},{9,9},... | collective-permute-start | bytes 196616 | tf_op jit(solution)/shard_map/ppermute | solution.py:372
  181.4 0.7 collective-permute-done.20
  182.0 3.9 %collective-permute-done.21 = f32[128,128]{1,0:T(8,128)S(1)} collective-permute-done((f32[128,128]{1,0:T(8,128)S(1)}, f32[128,128]{1,0:T(8,128)S(1)}, u32[]{:S(2)}, u32[]{:S(2)}) %collective-permute-start.21) | collective-permute-done | bytes 65568 | tf_op jit(solution)/shard_map/ppermute | solution.py:372
  185.9 0.7 pad_maximum_fusion
  (74 shorter events, 0.9 us)
Async XLA Ops:
  3.4 11.5 %copy-start = (bf16[768,256]{1,0:T(8,128)(2,1)S(1)}, bf16[768,256]{1,0:T(8,128)(2,1)}, u32[]{:S(2)}) copy-start(bf16[768,256]{1,0:T(8,128)(2,1)} %get-tuple-element.44.refs_2_) | copy-start | bytes 1179652
  3.4 14.7 %copy-start.1 = (bf16[768,256]{1,0:T(8,128)(2,1)S(1)}, bf16[768,256]{1,0:T(8,128)(2,1)}, u32[]{:S(2)}) copy-start(bf16[768,256]{1,0:T(8,128)(2,1)} %get-tuple-element.43.refs_2_) | copy-start | bytes 1179652
  8.5 9.7 %collective-permute-start.2 = (bf16[4,256,512]{2,1,0:T(8,128)(2,1)}, bf16[4,256,512]{2,1,0:T(8,128)(2,1)S(1)}, u32[]{:S(2)}, u32[]{:S(2)}) collective-permute-start(bf16[4,256,512]{2,1,0:T(8,128)(2,1)} %fisher_for_other_core.4.refs_3_), channel_id=1, source_target_pairs={{0,2},{2,0},{4,6},{6,4},{8,10},{10,8},{12,14},{14,12},{1,3},{3,1},... | collective-permute-start | bytes 3145736 | tf_op jit(solution)/shard_map/ppermute | solution.py:347
  14.9 9.8 %collective-permute-start.1 = (bf16[4,256,512]{2,1,0:T(8,128)(2,1)}, bf16[4,256,512]{2,1,0:T(8,128)(2,1)S(1)}, u32[]{:S(2)}, u32[]{:S(2)}) collective-permute-start(bf16[4,256,512]{2,1,0:T(8,128)(2,1)} %fisher_for_other_core.5.refs_4_), channel_id=1, source_target_pairs={{0,2},{2,0},{4,6},{6,4},{8,10},{10,8},{12,14},{14,12},{1,3},{3,1},... | collective-permute-start | bytes 3145736 | tf_op jit(solution)/shard_map/ppermute | solution.py:347
  15.0 16.1 %collective-permute-start = (bf16[768,256]{1,0:T(8,128)(2,1)S(1)}, bf16[768,256]{1,0:T(8,128)(2,1)S(1)}, u32[]{:S(2)}, u32[]{:S(2)}) collective-permute-start(bf16[768,256]{1,0:T(8,128)(2,1)S(1)} %copy-done), channel_id=1, source_target_pairs={{0,1},{1,0},{2,3},{3,2},{4,5},{5,4},{6,7},{7,6},{8,9},{9,8},{10,11... | collective-permute-start | bytes 1179656 | tf_op jit(solution)/shard_map/ppermute | solution.py:338
  18.2 19.5 %collective-permute-start.4 = (bf16[768,256]{1,0:T(8,128)(2,1)S(1)}, bf16[768,256]{1,0:T(8,128)(2,1)S(1)}, u32[]{:S(2)}, u32[]{:S(2)}) collective-permute-start(bf16[768,256]{1,0:T(8,128)(2,1)S(1)} %copy-done.1), channel_id=1, source_target_pairs={{0,1},{1,0},{2,3},{3,2},{4,5},{5,4},{6,7},{7,6},{8,9},{9,8},{10,11... | collective-permute-start | bytes 1179656 | tf_op jit(solution)/shard_map/ppermute | solution.py:338
  18.3 1.0 copy-start.10
  24.6 1.0 copy-start.9
  31.8 11.5 %copy-start.26 = (bf16[256,512]{1,0:T(8,128)(2,1)S(1)}, bf16[256,512]{1,0:T(8,128)(2,1)}, u32[]{:S(2)}) copy-start(bf16[256,512]{1,0:T(8,128)(2,1)} %get-tuple-element.38) | copy-start | bytes 786436
  31.8 14.7 %copy-start.25 = (bf16[256,512]{1,0:T(8,128)(2,1)S(1)}, bf16[256,512]{1,0:T(8,128)(2,1)}, u32[]{:S(2)}) copy-start(bf16[256,512]{1,0:T(8,128)(2,1)} %get-tuple-element.39) | copy-start | bytes 786436
  31.8 14.8 %copy-start.24 = (bf16[256,512]{1,0:T(8,128)(2,1)S(1)}, bf16[256,512]{1,0:T(8,128)(2,1)}, u32[]{:S(2)}) copy-start(bf16[256,512]{1,0:T(8,128)(2,1)} %get-tuple-element.40) | copy-start | bytes 786436
  36.8 55.4 %collective-permute-start.3 = (bf16[4,256,512]{2,1,0:T(8,128)(2,1)}, bf16[4,256,512]{2,1,0:T(8,128)(2,1)S(1)}, u32[]{:S(2)}, u32[]{:S(2)}) collective-permute-start(bf16[4,256,512]{2,1,0:T(8,128)(2,1)} %fisher_for_other_core.6.refs_3_), channel_id=1, source_target_pairs={{0,2},{2,0},{4,6},{6,4},{8,10},{10,8},{12,14},{14,12},{1,3},{3,1},... | collective-permute-start | bytes 3145736 | tf_op jit(solution)/shard_map/ppermute | solution.py:347
  37.6 0.7 copy-start.6
  43.2 49.6 %collective-permute-start.8 = (bf16[4,256,512]{2,1,0:T(8,128)(2,1)}, bf16[4,256,512]{2,1,0:T(8,128)(2,1)}, u32[]{:S(2)}, u32[]{:S(2)}) collective-permute-start(bf16[4,256,512]{2,1,0:T(8,128)(2,1)} %fisher_for_other_core.7.refs_4_), channel_id=1, source_target_pairs={{0,2},{2,0},{4,6},{6,4},{8,10},{10,8},{12,14},{14,12},{1,3},{3,1},... | collective-permute-start | bytes 3145736 | tf_op jit(solution)/shard_map/ppermute | solution.py:347
  43.3 38.7 %collective-permute-start.17 = (bf16[256,512]{1,0:T(8,128)(2,1)S(1)}, bf16[256,512]{1,0:T(8,128)(2,1)S(1)}, u32[]{:S(2)}, u32[]{:S(2)}) collective-permute-start(bf16[256,512]{1,0:T(8,128)(2,1)S(1)} %copy-done.26), channel_id=1, source_target_pairs={{0,8},{2,10},{4,12},{6,14},{8,0},{10,2},{12,4},{14,6},{1,9},{3,11}... | collective-permute-start | bytes 786440 | tf_op jit(solution)/shard_map/ppermute | solution.py:352
  46.5 38.4 %collective-permute-start.18 = (bf16[256,512]{1,0:T(8,128)(2,1)S(1)}, bf16[256,512]{1,0:T(8,128)(2,1)S(1)}, u32[]{:S(2)}, u32[]{:S(2)}) collective-permute-start(bf16[256,512]{1,0:T(8,128)(2,1)S(1)} %copy-done.25), channel_id=1, source_target_pairs={{0,4},{2,6},{4,8},{6,10},{8,12},{10,14},{12,0},{14,2},{1,5},{3,7},... | collective-permute-start | bytes 786440 | tf_op jit(solution)/shard_map/ppermute | solution.py:353
  46.6 45.5 %collective-permute-start.19 = (bf16[256,512]{1,0:T(8,128)(2,1)S(1)}, bf16[256,512]{1,0:T(8,128)(2,1)S(1)}, u32[]{:S(2)}, u32[]{:S(2)}) collective-permute-start(bf16[256,512]{1,0:T(8,128)(2,1)S(1)} %copy-done.24), channel_id=1, source_target_pairs={{0,12},{2,14},{4,0},{6,2},{8,4},{10,6},{12,8},{14,10},{1,13},{3,15... | collective-permute-start | bytes 786440 | tf_op jit(solution)/shard_map/ppermute | solution.py:354
  82.1 31.8 %copy-start.11 = (bf16[256,512]{1,0:T(8,128)(2,1)}, bf16[256,512]{1,0:T(8,128)(2,1)S(1)}, u32[]{:S(2)}) copy-start(bf16[256,512]{1,0:T(8,128)(2,1)S(1)} %collective-permute-done.17.refs_4_) | copy-start | bytes 786436
  82.1 31.7 %collective-permute-start.12 = (bf16[2,512,256]{2,1,0:T(8,128)(2,1)}, bf16[2,512,256]{2,1,0:T(8,128)(2,1)S(1)}, u32[]{:S(2)}, u32[]{:S(2)}) collective-permute-start(bf16[2,512,256]{2,1,0:T(8,128)(2,1)} %get-tuple-element.33), channel_id=1, source_target_pairs={{0,0},{1,2},{2,12},{3,14},{4,4},{5,6},{6,8},{7,10},{8,9},{9,11},{1... | collective-permute-start | bytes 1572872 | tf_op jit(solution)/shard_map/ppermute | solution.py:358
  84.8 29.0 %copy-start.12 = (bf16[256,512]{1,0:T(8,128)(2,1)}, bf16[256,512]{1,0:T(8,128)(2,1)S(1)}, u32[]{:S(2)}) copy-start(bf16[256,512]{1,0:T(8,128)(2,1)S(1)} %collective-permute-done.18.refs_5_) | copy-start | bytes 786436
  84.9 28.9 %collective-permute-start.13 = (bf16[2,512,256]{2,1,0:T(8,128)(2,1)}, bf16[2,512,256]{2,1,0:T(8,128)(2,1)S(1)}, u32[]{:S(2)}, u32[]{:S(2)}) collective-permute-start(bf16[2,512,256]{2,1,0:T(8,128)(2,1)} %get-tuple-element.34), channel_id=1, source_target_pairs={{0,2},{1,0},{2,14},{3,12},{4,6},{5,4},{6,10},{7,8},{8,11},{9,9},{1... | collective-permute-start | bytes 1572872 | tf_op jit(solution)/shard_map/ppermute | solution.py:358
  92.1 21.7 %copy-start.13 = (bf16[256,512]{1,0:T(8,128)(2,1)}, bf16[256,512]{1,0:T(8,128)(2,1)S(1)}, u32[]{:S(2)}) copy-start(bf16[256,512]{1,0:T(8,128)(2,1)S(1)} %collective-permute-done.19.refs_6_) | copy-start | bytes 786436
  92.1 13.8 %collective-permute-start.14 = (bf16[256,512]{1,0:T(8,128)(2,1)}, bf16[256,512]{1,0:T(8,128)(2,1)S(1)}, u32[]{:S(2)}, u32[]{:S(2)}) collective-permute-start(bf16[256,512]{1,0:T(8,128)(2,1)} %get-tuple-element.35), channel_id=1, source_target_pairs={{0,8},{2,10},{4,12},{6,14},{8,0},{10,2},{12,4},{14,6},{1,9},{3,11}... | collective-permute-start | bytes 786440 | tf_op jit(solution)/shard_map/ppermute | solution.py:352
  92.2 2.8 %copy-start.8 = (bf16[4,256,512]{2,1,0:T(8,128)(2,1)}, bf16[4,256,512]{2,1,0:T(8,128)(2,1)S(1)}, u32[]{:S(2)}) copy-start(bf16[4,256,512]{2,1,0:T(8,128)(2,1)S(1)} %collective-permute-done.3.refs_3_) | copy-start | bytes 3145732
  92.2 21.5 %collective-permute-start.15 = (bf16[256,512]{1,0:T(8,128)(2,1)}, bf16[256,512]{1,0:T(8,128)(2,1)S(1)}, u32[]{:S(2)}, u32[]{:S(2)}) collective-permute-start(bf16[256,512]{1,0:T(8,128)(2,1)} %get-tuple-element.36), channel_id=1, source_target_pairs={{0,4},{2,6},{4,8},{6,10},{8,12},{10,14},{12,0},{14,2},{1,5},{3,7},... | collective-permute-start | bytes 786440 | tf_op jit(solution)/shard_map/ppermute | solution.py:353
  92.8 21.0 %collective-permute-start.16 = (bf16[256,512]{1,0:T(8,128)(2,1)}, bf16[256,512]{1,0:T(8,128)(2,1)}, u32[]{:S(2)}, u32[]{:S(2)}) collective-permute-start(bf16[256,512]{1,0:T(8,128)(2,1)} %get-tuple-element.37), channel_id=1, source_target_pairs={{0,12},{2,14},{4,0},{6,2},{8,4},{10,6},{12,8},{14,10},{1,13},{3,15... | collective-permute-start | bytes 786440 | tf_op jit(solution)/shard_map/ppermute | solution.py:354
  100.4 29.8 %copy-start.23 = (bf16[256,512]{1,0:T(8,128)(2,1)S(1)}, bf16[256,512]{1,0:T(8,128)(2,1)}, u32[]{:S(2)}) copy-start(bf16[256,512]{1,0:T(8,128)(2,1)} %get-tuple-element.26) | copy-start | bytes 786436
  100.4 43.8 %copy-start.22 = (bf16[256,512]{1,0:T(8,128)(2,1)S(1)}, bf16[256,512]{1,0:T(8,128)(2,1)}, u32[]{:S(2)}) copy-start(bf16[256,512]{1,0:T(8,128)(2,1)} %get-tuple-element.27) | copy-start | bytes 786436
  106.0 7.9 %copy-start.14 = (bf16[256,512]{1,0:T(8,128)(2,1)}, bf16[256,512]{1,0:T(8,128)(2,1)S(1)}, u32[]{:S(2)}) copy-start(bf16[256,512]{1,0:T(8,128)(2,1)S(1)} %collective-permute-done.14.refs_0_) | copy-start | bytes 786436
  113.8 0.9 copy-start.4
  113.8 1.1 copy-start.5
  119.3 35.2 %all-to-all-start.1 = ((bf16[8,3,128,128]{3,2,1,0:T(8,128)(2,1)}), bf16[8,3,128,128]{3,2,1,0:T(8,128)(2,1)S(1)}, u32[]{:S(2)}, u32[]{:S(2)}) async-start(bf16[8,3,128,128]{3,2,1,0:T(8,128)(2,1)} %weigh_members.2.refs_10_), calls=%async_computation.1 | async-start | bytes 1572864 | tf_op jit(solution)/shard_map/all_to_all | solution.py:365
  124.5 19.7 %collective-permute-start.10 = (bf16[256,512]{1,0:T(8,128)(2,1)}, bf16[256,512]{1,0:T(8,128)(2,1)S(1)}, u32[]{:S(2)}, u32[]{:S(2)}) collective-permute-start(bf16[256,512]{1,0:T(8,128)(2,1)} %get-tuple-element.30), channel_id=1, source_target_pairs={{0,4},{2,6},{4,8},{6,10},{8,12},{10,14},{12,0},{14,2},{1,5},{3,7},... | collective-permute-start | bytes 786440 | tf_op jit(solution)/shard_map/ppermute | solution.py:353
  124.5 19.7 %collective-permute-start.11 = (bf16[256,512]{1,0:T(8,128)(2,1)}, bf16[256,512]{1,0:T(8,128)(2,1)S(1)}, u32[]{:S(2)}, u32[]{:S(2)}) collective-permute-start(bf16[256,512]{1,0:T(8,128)(2,1)} %get-tuple-element.31), channel_id=1, source_target_pairs={{0,12},{2,14},{4,0},{6,2},{8,4},{10,6},{12,8},{14,10},{1,13},{3,15... | collective-permute-start | bytes 786440 | tf_op jit(solution)/shard_map/ppermute | solution.py:354
  127.2 17.1 %collective-permute-start.9 = (bf16[256,512]{1,0:T(8,128)(2,1)}, bf16[256,512]{1,0:T(8,128)(2,1)S(1)}, u32[]{:S(2)}, u32[]{:S(2)}) collective-permute-start(bf16[256,512]{1,0:T(8,128)(2,1)} %get-tuple-element.29), channel_id=1, source_target_pairs={{0,8},{2,10},{4,12},{6,14},{8,0},{10,2},{12,4},{14,6},{1,9},{3,11}... | collective-permute-start | bytes 786440 | tf_op jit(solution)/shard_map/ppermute | solution.py:352
  127.2 17.1 %collective-permute-start.5 = (bf16[256,512]{1,0:T(8,128)(2,1)}, bf16[256,512]{1,0:T(8,128)(2,1)S(1)}, u32[]{:S(2)}, u32[]{:S(2)}) collective-permute-start(bf16[256,512]{1,0:T(8,128)(2,1)} %get-tuple-element.25), channel_id=1, source_target_pairs={{0,8},{2,10},{4,12},{6,14},{8,0},{10,2},{12,4},{14,6},{1,9},{3,11}... | collective-permute-start | bytes 786440 | tf_op jit(solution)/shard_map/ppermute | solution.py:352
  130.1 17.8 %collective-permute-start.6 = (bf16[256,512]{1,0:T(8,128)(2,1)S(1)}, bf16[256,512]{1,0:T(8,128)(2,1)S(1)}, u32[]{:S(2)}, u32[]{:S(2)}) collective-permute-start(bf16[256,512]{1,0:T(8,128)(2,1)S(1)} %copy-done.23), channel_id=1, source_target_pairs={{0,4},{2,6},{4,8},{6,10},{8,12},{10,14},{12,0},{14,2},{1,5},{3,7},... | collective-permute-start | bytes 786440 | tf_op jit(solution)/shard_map/ppermute | solution.py:353
  144.2 5.2 %copy-start.16 = (bf16[256,512]{1,0:T(8,128)(2,1)}, bf16[256,512]{1,0:T(8,128)(2,1)S(1)}, u32[]{:S(2)}) copy-start(bf16[256,512]{1,0:T(8,128)(2,1)S(1)} %collective-permute-done.10.refs_5_) | copy-start | bytes 786436
  144.2 5.2 %collective-permute-start.7 = (bf16[256,512]{1,0:T(8,128)(2,1)S(1)}, bf16[256,512]{1,0:T(8,128)(2,1)S(1)}, u32[]{:S(2)}, u32[]{:S(2)}) collective-permute-start(bf16[256,512]{1,0:T(8,128)(2,1)S(1)} %copy-done.22), channel_id=1, source_target_pairs={{0,12},{2,14},{4,0},{6,2},{8,4},{10,6},{12,8},{14,10},{1,13},{3,15... | collective-permute-start | bytes 786440 | tf_op jit(solution)/shard_map/ppermute | solution.py:354
  144.2 5.2 %copy-start.17 = (bf16[256,512]{1,0:T(8,128)(2,1)}, bf16[256,512]{1,0:T(8,128)(2,1)S(1)}, u32[]{:S(2)}) copy-start(bf16[256,512]{1,0:T(8,128)(2,1)S(1)} %collective-permute-done.11.refs_6_) | copy-start | bytes 786436
  144.2 5.2 %copy-start.18 = (bf16[256,512]{1,0:T(8,128)(2,1)}, bf16[256,512]{1,0:T(8,128)(2,1)S(1)}, u32[]{:S(2)}) copy-start(bf16[256,512]{1,0:T(8,128)(2,1)S(1)} %collective-permute-done.9.refs_4_) | copy-start | bytes 786436
  144.2 5.2 %copy-start.19 = (bf16[256,512]{1,0:T(8,128)(2,1)}, bf16[256,512]{1,0:T(8,128)(2,1)S(1)}, u32[]{:S(2)}) copy-start(bf16[256,512]{1,0:T(8,128)(2,1)S(1)} %collective-permute-done.5.refs_0_) | copy-start | bytes 786436
  148.0 1.5 copy-start.20
  154.6 4.8 %copy-start.2 = (bf16[8,3,128,128]{3,2,1,0:T(8,128)(2,1)}, bf16[8,3,128,128]{3,2,1,0:T(8,128)(2,1)S(1)}, u32[]{:S(2)}) copy-start(bf16[8,3,128,128]{3,2,1,0:T(8,128)(2,1)S(1)} %all-to-all-done.1.got_ref) | copy-start | bytes 2359300
  154.6 16.4 %all-to-all-start = ((bf16[8,3,128,128]{3,2,1,0:T(8,128)(2,1)}), bf16[8,3,128,128]{3,2,1,0:T(8,128)(2,1)S(1)}, u32[]{:S(2)}, u32[]{:S(2)}) async-start(bf16[8,3,128,128]{3,2,1,0:T(8,128)(2,1)} %weigh_members.3), calls=%async_computation | async-start | bytes 1572864 | tf_op jit(solution)/shard_map/all_to_all | solution.py:365
  171.0 0.9 copy-start.3
  174.9 7.2 %collective-permute-start.20 = (f32[128,128]{1,0:T(8,128)S(1)}, f32[128,128]{1,0:T(8,128)S(1)}, u32[]{:S(2)}, u32[]{:S(2)}) collective-permute-start(f32[128,128]{1,0:T(8,128)S(1)} %get-tuple-element.47), channel_id=1, source_target_pairs={{0,0},{1,14},{2,64},{3,78},{4,4},{5,10},{6,68},{7,74},{8,6},{9,8},... | collective-permute-start | bytes 196616 | tf_op jit(solution)/shard_map/ppermute | solution.py:371
  178.2 7.7 %collective-permute-start.21 = (f32[128,128]{1,0:T(8,128)S(1)}, f32[128,128]{1,0:T(8,128)S(1)}, u32[]{:S(2)}, u32[]{:S(2)}) collective-permute-start(f32[128,128]{1,0:T(8,128)S(1)} %get-tuple-element.48), channel_id=1, source_target_pairs={{0,1},{1,15},{2,65},{3,79},{4,5},{5,11},{6,69},{7,75},{8,7},{9,9},... | collective-permute-start | bytes 196616 | tf_op jit(solution)/shard_map/ppermute | solution.py:372
  (3 other events, 2.2 us)

commit v3 on v0

v3 whole, which is shorter than its diff:
```python
import jax
import jax.numpy as jnp
from jax import lax
from jax.experimental import pallas as pl
from jax.experimental.pallas import tpu as pltpu
from jax.sharding import PartitionSpec as P

F32 = jnp.float32
BF16 = jnp.bfloat16
HBM = pl.BlockSpec(memory_space=pltpu.HBM)
SMEM = pl.BlockSpec(memory_space=pltpu.SMEM)
VMEM = pl.BlockSpec(memory_space=pltpu.VMEM)
VMEM_LIMIT = 16 << 20

GRID = 1.00297
BIG = 2.0**28
SMALL = 2.0**16
EDGE = 2.0**-40
EDGE_CODE = 2.0**-24

X, CORES, Z = 4, 2, 4


def code_of(values):
    scaled = values * BIG
    return jnp.where(values >= EDGE, scaled * scaled, values * SMALL)


def value_of(code):
    return jnp.where(code >= EDGE_CODE, jnp.sqrt(code) * (1.0 / BIG), code * (1.0 / SMALL))


def encode(values):
    return code_of(values).astype(BF16)


def decode(sent):
    return value_of(sent.astype(F32))


def encode_fine(values):
    code = code_of(values)
    first = code.astype(BF16).astype(F32)
    second = (code * (1.0 / GRID)).astype(BF16).astype(F32)
    near = jnp.abs(first - code) <= jnp.abs(second * GRID - code)
    return jnp.where(near, first, -second).astype(BF16)


def decode_fine(sent):
    code = sent.astype(F32)
    return value_of(jnp.where(code < 0.0, code * (-GRID), code))


def in_vmem(array):
    return pltpu.with_memory_space_constraint(array, pltpu.VMEM)


def in_hbm(array):
    return pltpu.with_memory_space_constraint(array, pltpu.HBM)


def call(kernel, name, outs, scalars, hbm, vmem, scratch=(), flops=0):
    single = not isinstance(outs, list)
    shapes = [pltpu.VMEM(shape, kind) for shape, kind in ([outs] if single else outs)]
    moved = sum(a.size * 2 for a in vmem) + sum(a.size * 2 for a in hbm)
    result = pl.pallas_call(
        kernel,
        out_shape=shapes,
        in_specs=[SMEM] * len(scalars) + [HBM] * len(hbm) + [VMEM] * len(vmem),
        out_specs=[VMEM] * len(shapes),
        scratch_shapes=list(scratch),
        compiler_params=pltpu.CompilerParams(vmem_limit_bytes=VMEM_LIMIT),
        cost_estimate=pl.CostEstimate(flops=flops, bytes_accessed=moved, transcendentals=0),
        name=name,
    )(*scalars, *[in_hbm(a) for a in hbm], *[in_vmem(a) for a in vmem])
    return result[0] if single else result


def squared_transposed(g):
    g = g.astype(F32)
    return (g * g).T.astype(BF16)


def fisher_block(x, gt_ref):
    return jnp.dot(gt_ref[...], x * x, preferred_element_type=F32)


def load_inputs(member, place, x_ref, x_out, sem):
    wide = x_out.shape[2]
    copies = []
    for s in range(8):
        at = pl.multiple_of(place[s] * wide, wide)
        copies.append(pltpu.make_async_copy(x_ref.at[member, :, pl.ds(at, wide)], x_out.at[s], sem.at[s]))
        copies[s].start()
    return copies


def send_blocks(copies, x_out, gt_out, send_out):
    for s in range(8):
        copies[s].wait()
        if s < 4:
            send_out[s] = fisher_block(x_out[s], gt_out).astype(BF16)


def load_kernel(member, place, x_ref, g_ref, *refs):
    send_out, x_out, gt_out, g_buf, sem, g_sem = refs[-6:]
    load = pltpu.make_async_copy(g_ref.at[member], g_buf, g_sem)
    load.start()
    copies = load_inputs(member, place, x_ref, x_out, sem)
    load.wait()
    gt_out[...] = squared_transposed(g_buf[...])
    send_blocks(copies, x_out, gt_out, send_out)


def send_kernel(member, x_ref, g_ref, after, send_out, gt_out):
    gt_out[...] = squared_transposed(g_ref[member])
    for s in range(4):
        send_out[s] = fisher_block(x_ref[s], gt_out).astype(BF16)


def own_kernel(x_ref, gt_ref, got_ref, after, sent_out, kept_out):
    for s in range(4):
        block = fisher_block(x_ref[4 + s], gt_ref) + got_ref[s].astype(F32)
        if s < 2:
            sent_out[s] = encode(block)
        else:
            kept_out[s - 2] = block


def middle_kernel(kept_ref, got_ref, after, sent_out, own_out):
    sent_out[...] = encode_fine(kept_ref[1] + decode(got_ref[1]))
    own_out[...] = kept_ref[0] + decode(got_ref[0])


def split_kernel(core, w_ref, after, own_out, send_out):
    rows = own_out.shape[1]
    own_out[...] = w_ref[:, pl.ds(pl.multiple_of(core[0] * rows, rows), rows), :]
    send_out[...] = w_ref[:, pl.ds(pl.multiple_of((1 - core[0]) * rows, rows), rows), :]


def over_tokens(own, got, cols):
    return (own[:, cols] + decode_fine(got[:, cols])).T


def begin_kernel(which, own, got, w_a, w_b, after, weighted_out, total_out):
    part = own.shape[1] // Z
    for z in range(Z):
        cols = slice(z * part, (z + 1) * part)
        fisher = over_tokens(own, got, cols)
        weight = jnp.where(which[0] == 0, w_a[0, cols, :].astype(F32), w_b[0, cols, :].astype(F32))
        weighted_out[cols, :] = fisher * weight
        total_out[cols, :] = fisher


def finish_kernel(which, own, got, w_a, w_b, weighted_ref, total_ref, out):
    outs, wide = own.shape
    half, part = outs // 2, wide // Z
    for z in range(Z):
        cols = slice(z * part, (z + 1) * part)
        fisher = over_tokens(own, got, cols)
        weight = jnp.where(which[0] == 0, w_a[1, cols, :].astype(F32), w_b[1, cols, :].astype(F32))
        weighted = weighted_ref[cols, :] + fisher * weight
        high = weighted.astype(BF16)
        low = (weighted - high.astype(F32)).astype(BF16)
        code = encode_fine(total_ref[cols, :] + fisher)
        for y in range(2):
            for word, values in enumerate((high, low, code)):
                out[y * Z + z, word] = values[:, y * half : (y + 1) * half]


def merged_of(got_ref):
    weighted = total = 0.0
    for group in range(got_ref.shape[0]):
        weighted += got_ref[group, 0].astype(F32) + got_ref[group, 1].astype(F32)
        total += decode_fine(got_ref[group, 2])
    return weighted / total


def merge_kernel(got_ref, out):
    out[...] = merged_of(got_ref)


def merge_last_kernel(swap, got_ref, first_ref, near_out, far_out):
    first, second = first_ref[...], merged_of(got_ref)
    near_out[...] = jnp.where(swap[0] == 1, second, first)
    far_out[...] = jnp.where(swap[0] == 1, first, second)


def keeper(local, half):
    home = 2 * half + local // 2
    return home if local % 2 == 0 else 3 - home


def kept(x, half):
    return 2 * (x % 2) if x // 2 == half else 2 * ((3 - x) % 2) + 1


def weight_pairs():
    pairs = []
    for tok in range(X * CORES):
        half, local = divmod(tok, 4)
        for col in range(2):
            pairs.append((tok * 2 + col, (keeper(local, half) * 2 + col) * 2 + half))
    return pairs


def result_pairs(flip):
    pairs = []
    for member in range(8):
        y_lo, z = divmod(member, 4)
        for tok in range(8):
            x, core = divmod(tok, 2)
            for half in range(2):
                to_member = core * 4 + z
                to_tok = 4 * half + kept(x, half)
                to_col = y_lo ^ flip
                pairs.append(((member * 8 + tok) * 2 + half, (to_member * 8 + to_tok) * 2 + to_col))
    return pairs


def x_pairs(flip):
    return [(t, ((t // 2) ^ flip) * 2 + t % 2) for t in range(X * CORES)]


def shards(inputs, grads, weights):
    tok = lax.axis_index("tok")
    half = lax.axis_index("col")
    x, core = tok // 2, tok % 2
    y_lo = lax.axis_index("member") // 4

    flips = ((1, 3), (3, 1))
    places = []
    for first, second in flips:
        steps = x ^ jnp.array([first, 2, 0, second], jnp.int32)
        local = jnp.where(steps // 2 == half, 2 * (steps % 2), 2 * ((3 - steps) % 2) + 1)
        places.append(jnp.concatenate([2 * local + 1 - core, 2 * local + core]).astype(jnp.int32))

    tokens, outs = grads.shape[1:]
    wide = inputs.shape[2] // 8
    send_shape, x_shape, gt_shape = ((4, outs, wide), BF16), ((8, tokens, wide), BF16), ((outs, tokens), BF16)
    pair, kept_shape = ((2, outs, wide), BF16), ((2, outs, wide), F32)
    block, own_shape, sums = ((outs, wide), BF16), ((outs, wide), F32), ((wide, outs), F32)
    dma = pltpu.SemaphoreType.DMA
    flops = 8 * outs * wide * tokens

    def swap_cores(send):
        return lax.ppermute(send, "tok", [(t, t ^ 1) for t in range(8)])

    def load(member, after):
        return call(
            lambda *refs: load_kernel(member, *refs), "load_and_fisher_for_other_core",
            [send_shape, x_shape, gt_shape], [places[member]], [inputs, grads], after,
            [pltpu.VMEM((tokens, outs), BF16), dma((8,)), dma], flops,
        )

    def own_part(member, x_blocks, gt, got, after):
        sent, kept_blocks = call(
            own_kernel, "fisher_of_own_core", [pair, kept_shape], [], [], [x_blocks, gt, got, after], flops=flops
        )
        return lax.ppermute(sent, "tok", x_pairs(flips[member][0])), kept_blocks

    def middle(member, got, kept_blocks, after):
        sent, own = call(
            middle_kernel, "fisher_over_first_swap", [block, own_shape], [], [], [kept_blocks, got, after], flops=30 * outs * wide
        )
        return own, lax.ppermute(sent, "tok", x_pairs(flips[member][1]))

    def other_part(member, after):
        return call(
            lambda *refs: send_kernel(member, *refs), "fisher_for_other_core", [send_shape, gt_shape], [], [],
            [xs[member], other, after], flops=flops,
        )

    def weigh(phase, one, two, after):
        which = ((core ^ half) ^ phase).astype(jnp.int32).reshape(1)
        words = ((2 * Z, 3, wide // Z, outs // 2), BF16)
        begun = call(begin_kernel, "weigh_first", [sums, sums], [which], [], [*one, *moved, after], flops=20 * outs * wide)
        return call(finish_kernel, "weigh_second", words, [which], [], [*two, *moved, *begun], flops=40 * outs * wide)

    other = lax.ppermute(grads, "col", [(0, 1), (1, 0)])
    arrived = lax.ppermute(weights, ("tok", "col"), weight_pairs())

    send0, x0, gt0 = load(0, [])
    got0 = swap_cores(send0)
    send1, x1, gt1 = load(1, [gt0])
    got1 = swap_cores(send1)
    xs = (x0, x1)
    swap00, kept00 = own_part(0, x0, gt0, got0, gt1)
    swap01, kept01 = own_part(1, x1, gt1, got1, kept00)
    part00 = middle(0, swap00, kept00, kept01)
    part01 = middle(1, swap01, kept01, part00[0])
    rows = weights.shape[1] // 2
    w_own, w_send = call(
        split_kernel, "split_weights", [((2, rows, outs), BF16)] * 2, [core.astype(jnp.int32).reshape(1)], [],
        [arrived, part01[0]],
    )
    moved = (w_own, swap_cores(w_send))

    send0, gt0 = other_part(0, w_own)
    got0 = swap_cores(send0)
    send1, gt1 = other_part(1, gt0)
    got1 = swap_cores(send1)
    swap10, kept10 = own_part(0, x0, gt0, got0, gt1)
    swap11, kept11 = own_part(1, x1, gt1, got1, kept10)

    out = ((wide // Z, outs // 2), F32)
    words = weigh(0, part00, part01, kept11)
    merged = call(merge_kernel, "merge_members", out, [], [], [lax.all_to_all(words, "member", 0, 0, tiled=True)])
    part10 = middle(0, swap10, kept10, words)
    part11 = middle(1, swap11, kept11, part10[0])
    words = weigh(1, part10, part11, part11[0])
    got = lax.all_to_all(words, "member", 0, 0, tiled=True)
    swap = (y_lo ^ half).astype(jnp.int32).reshape(1)
    near, far = call(merge_last_kernel, "merge_members", [out, out], [swap], [], [got, merged])

    names = ("member", "tok", "col")
    near = lax.ppermute(near, names, result_pairs(0))
    far = lax.ppermute(far, names, result_pairs(1))
    left = jnp.where(half == 0, near, far)
    right = jnp.where(half == 0, far, near)
    return jnp.concatenate([left, right], axis=1)


def solution(mesh):
    in_specs = (P("member", "tok", "col"), P("member", "tok", "col"), P("member", "tok", "col"))
    out_specs = P(("tok", "member"), "col")
    return jax.shard_map(shards, mesh=mesh, in_specs=in_specs, out_specs=out_specs, check_vma=False)
```

time: 717 us -> 119 us (0.17)
  waiting for transfers between devices: 633 us -> 40.6 us
  starting transfers between devices: 0.08 us -> 39.5 us
  Pallas kernels: 0 us -> 32.4 us
  matrix products: 21.9 us -> 0 us
  local copies, waits for them, and re-layouts: 22.9 us -> 3.14 us
  other arithmetic: 19.9 us -> 1.53 us
  between operations: 13.1 us -> 0.19 us
    all_gather x2 -> x0, waiting for transfers between devices: 327 us -> none  [the longest x1 300 us: shards(): input_sq = lax.all_gather(squared(inputs), 'col', axis=2, tiled=True)]
    reduce_scatter x1 -> x0, waiting for transfers between devices: 306 us -> none  [shards(): lax.psum_scatter(sums, ('member', 'tok'), scatter_dimension=1, tiled=True)]
    ppermute x0 -> x17, waiting for transfers between devices: none -> 33.7 us  [the longest x4 20.5 us: own_part(): return (lax.ppermute(sent, 'tok', x_pairs(flips[member][0])), kept_blocks)]
    pallas_call x0 -> x19, Pallas kernels: none -> 32.4 us  [call(): pl.pallas_call(kernel, out_shape=shapes, in_specs=[SMEM] * len(scalars) +...]
    ppermute x0 -> x17, starting transfers between devices: none -> 27.9 us  [the longest x1 7.59 us: shards(): near = lax.ppermute(near, names, result_pairs(0))]
    dot_general x1 -> x0, matrix products: 21.9 us -> none  [shards(): jnp.einsum('mti,mto->mio', input_sq, grad_sq, preferred_element_type=jnp....]
    unnamed x3 -> x16, local copies, waits for them, and re-layouts: 16.7 us -> 3.14 us
    all_to_all x0 -> x2, starting transfers between devices: none -> 11.7 us  [the longest x1 6.05 us: shards(): lax.all_to_all(words, 'member', 0, 0, tiled=True)]
  transfers between devices with their start and end apart: 3 -> 19, of which waited for: 3 -> 10; matrix products, arithmetic and copies ran while one was open for 4% -> 0% of each run, Pallas kernels for 0% -> 22%
where the time goes in v3:
time: 119 us; the launch traced here: 117 us
  waiting for transfers between devices  40.6 us (34%)
  starting transfers between devices  39.5 us (33%)
  Pallas kernels  32.4 us (27%)
  local copies, waits for them, and re-layouts  3.14 us (3%)
  other arithmetic  1.53 us (1%)
    pallas_call x19, Pallas kernels, call(): pl.pallas_call(kernel, out_shape=shapes, in_specs=[SMEM] * len(scalars) +...  32.4 us
    ppermute x4, waiting for transfers between devices, own_part(): return (lax.ppermute(sent, 'tok', x_pairs(flips[member][0])), kept_blocks)  20.5 us
    ppermute x1, starting transfers between devices, shards(): near = lax.ppermute(near, names, result_pairs(0))  7.59 us
    all_to_all x1, waiting for transfers between devices, shards(): got = lax.all_to_all(words, 'member', 0, 0, tiled=True)  6.86 us
    ppermute x4, waiting for transfers between devices, middle(): return (own, lax.ppermute(sent, 'tok', x_pairs(flips[member][1])))  6.48 us
    all_to_all x1, starting transfers between devices, shards(): lax.all_to_all(words, 'member', 0, 0, tiled=True)  6.05 us
    all_to_all x1, starting transfers between devices, shards(): got = lax.all_to_all(words, 'member', 0, 0, tiled=True)  5.63 us
    ppermute x4, starting transfers between devices, middle(): return (own, lax.ppermute(sent, 'tok', x_pairs(flips[member][1])))  5.37 us
  transfers between devices with their start and end apart: 19, of which 10 were waited for; matrix products, arithmetic and copies ran while one was open for 0% of the time, Pallas kernels for 22%

profile of v3, /device:TPU:1, one launch (start us, length us, event | category | flops | bytes accessed | tf_op | source)
XLA Modules:
  0.0 117.4 jit_solution(3567473887238298102)
XLA Ops:
  0.0 0.7 add_subtract_fusion
  0.8 5.0 %load_and_fisher_for_other_core.2 = (bf16[4,256,512]{2,1,0:T(8,128)(2,1)S(1)}, bf16[8,768,512]{2,1,0:T(8,128)(2,1)S(1)}, bf16[256,768]{1,0:T(8,128)(2,1)S(1)}) custom-call(s32[8]{0:T(128)S(1)} %pad_add_fusion.1.refs_0_, bf16[2,768,4096]{2,1,0:T(8,128)(2,1)} %refs_1_.3, bf16[2,768,256]{2,1,0:T(8,128)(2,1)} %refs_2_.3), custom_call_target="tpu_custom_call" | custom-call | flops 805306368 | bytes 13369344 | tf_op jit(solution)/shard_map/load_and_fisher_for_other_core/pallas_call | solution.py:66
  5.8 1.5 %collective-permute-start.3 = (bf16[4,256,512]{2,1,0:T(8,128)(2,1)S(1)}, bf16[4,256,512]{2,1,0:T(8,128)(2,1)S(1)}, u32[]{:S(2)}, u32[]{:S(2)}) collective-permute-start(bf16[4,256,512]{2,1,0:T(8,128)(2,1)S(1)} %get-tuple-element.44), channel_id=1, source_target_pairs={{0,2},{2,0},{4,6},{6,4},{8,10},{10,8},{12,14},{14,12},{1,3},{3,1},... | collective-permute-start | bytes 3145736 | tf_op jit(solution)/shard_map/ppermute | solution.py:247
  7.4 5.0 %load_and_fisher_for_other_core.3 = (bf16[4,256,512]{2,1,0:T(8,128)(2,1)S(1)}, bf16[8,768,512]{2,1,0:T(8,128)(2,1)S(1)}, bf16[256,768]{1,0:T(8,128)(2,1)S(1)}) custom-call(s32[8]{0:T(128)S(1)} %pad_add_fusion.refs_0_, bf16[2,768,4096]{2,1,0:T(8,128)(2,1)} %refs_1_.3, bf16[2,768,256]{2,1,0:T(8,128)(2,1)} %refs_2_.3, ...), custom_call_target="tpu_custom_call" | custom-call | flops 805306368 | bytes 13762560 | tf_op jit(solution)/shard_map/load_and_fisher_for_other_core/pallas_call | solution.py:66
  12.4 0.1 collective-permute-start.2
  12.5 4.8 %collective-permute-start.1 = (bf16[2,1024,256]{2,1,0:T(8,128)(2,1)S(1)}, bf16[2,1024,256]{2,1,0:T(8,128)(2,1)S(1)}, u32[]{:S(2)}, u32[]{:S(2)}) collective-permute-start(bf16[2,1024,256]{2,1,0:T(8,128)(2,1)S(1)} %copy-done.7), channel_id=1, source_target_pairs={{0,0},{1,2},{2,12},{3,14},{4,4},{5,6},{6,8},{7,10},{8,9},{9,11},{1... | collective-permute-start | bytes 3145736 | tf_op jit(solution)/shard_map/ppermute | solution.py:281
  17.4 2.4 %collective-permute-start = (bf16[2,768,256]{2,1,0:T(8,128)(2,1)S(1)}, bf16[2,768,256]{2,1,0:T(8,128)(2,1)S(1)}, u32[]{:S(2)}, u32[]{:S(2)}) collective-permute-start(bf16[2,768,256]{2,1,0:T(8,128)(2,1)S(1)} %copy-done.6), channel_id=1, source_target_pairs={{0,1},{1,0},{2,3},{3,2},{4,5},{5,4},{6,7},{7,6},{8,9},{9,8},{10,11... | collective-permute-start | bytes 2359304 | tf_op jit(solution)/shard_map/ppermute | solution.py:280
  19.8 1.2 fisher_of_own_core.4
  21.0 1.1 fisher_of_own_core.5
  22.2 1.2 %collective-permute-start.4 = (bf16[2,256,512]{2,1,0:T(8,128)(2,1)S(1)}, bf16[2,256,512]{2,1,0:T(8,128)(2,1)S(1)}, u32[]{:S(2)}, u32[]{:S(2)}) collective-permute-start(bf16[2,256,512]{2,1,0:T(8,128)(2,1)S(1)} %get-tuple-element.47), channel_id=1, source_target_pairs={{0,12},{2,14},{4,8},{6,10},{8,4},{10,6},{12,0},{14,2},{1,13},{3,15... | collective-permute-start | bytes 1572872 | tf_op jit(solution)/shard_map/ppermute | solution.py:260
  23.4 10.6 %collective-permute-done.5.got_ref = bf16[2,256,512]{2,1,0:T(8,128)(2,1)S(1)} collective-permute-done((bf16[2,256,512]{2,1,0:T(8,128)(2,1)S(1)}, bf16[2,256,512]{2,1,0:T(8,128)(2,1)S(1)}, u32[]{:S(2)}, u32[]{:S(2)}) %collective-permute-start.5) | collective-permute-done | bytes 524320 | tf_op jit(solution)/shard_map/ppermute | solution.py:260
  33.9 1.2 %fisher_over_first_swap.4 = (bf16[256,512]{1,0:T(8,128)(2,1)}, f32[256,512]{1,0:T(8,128)S(1)}) custom-call(f32[2,256,512]{2,1,0:T(8,128)S(1)} %get-tuple-element.45.after.kept_ref, bf16[2,256,512]{2,1,0:T(8,128)(2,1)S(1)} %collective-permute-done.5.got_ref, f32[2,256,512]{2,1,0:T(8,128)S(1)} %get-tuple-element.46.after.kept_ref), custom_call_target="tpu_custom_call" | custom-call | flops 3932160 | bytes 1572864 | tf_op jit(solution)/shard_map/fisher_over_first_swap/pallas_call | solution.py:66
  35.2 8.7 %collective-permute-done.4.got_ref = bf16[2,256,512]{2,1,0:T(8,128)(2,1)S(1)} collective-permute-done((bf16[2,256,512]{2,1,0:T(8,128)(2,1)S(1)}, bf16[2,256,512]{2,1,0:T(8,128)(2,1)S(1)}, u32[]{:S(2)}, u32[]{:S(2)}) %collective-permute-start.4) | collective-permute-done | bytes 524320 | tf_op jit(solution)/shard_map/ppermute | solution.py:260
  43.9 1.2 %fisher_over_first_swap.5 = (bf16[256,512]{1,0:T(8,128)(2,1)}, f32[256,512]{1,0:T(8,128)S(1)}) custom-call(f32[2,256,512]{2,1,0:T(8,128)S(1)} %get-tuple-element.46.after.kept_ref, bf16[2,256,512]{2,1,0:T(8,128)(2,1)S(1)} %collective-permute-done.4.got_ref, f32[256,512]{1,0:T(8,128)S(1)} %get-tuple-element.49.after.own), custom_call_target="tpu_custom_call" | custom-call | flops 3932160 | bytes 1310720 | tf_op jit(solution)/shard_map/fisher_over_first_swap/pallas_call | solution.py:66
  45.2 0.9 split_weights.1
  46.1 1.0 collective-permute-done.refs_1_
  47.1 1.0 fisher_for_other_core.2
  48.1 0.8 collective-permute-start.7
  48.9 1.0 fisher_for_other_core.3
  50.1 0.5 collective-permute-start.11
  50.6 4.0 %collective-permute-start.12 = (bf16[256,512]{1,0:T(8,128)(2,1)}, bf16[256,512]{1,0:T(8,128)(2,1)S(1)}, u32[]{:S(2)}, u32[]{:S(2)}) collective-permute-start(bf16[256,512]{1,0:T(8,128)(2,1)} %get-tuple-element.62), channel_id=1, source_target_pairs={{0,12},{2,14},{4,8},{6,10},{8,4},{10,6},{12,0},{14,2},{1,13},{3,15... | collective-permute-start | bytes 786440 | tf_op jit(solution)/shard_map/ppermute | solution.py:266
  54.6 1.8 %fisher_of_own_core.6 = (bf16[2,256,512]{2,1,0:T(8,128)(2,1)}, f32[2,256,512]{2,1,0:T(8,128)S(1)}) custom-call(bf16[8,768,512]{2,1,0:T(8,128)(2,1)S(1)} %get-tuple-element.41.x_ref.refs_0_, bf16[256,768]{1,0:T(8,128)(2,1)S(1)} %get-tuple-element.52.refs_2_.gt_ref, bf16[4,256,512]{2,1,0:T(8,128)(2,1)S(1)} %collective-permute-done.7.got_ref, ...), custom_call_target="tpu_custom_call" | custom-call | flops 805306368 | bytes 8126464 | tf_op jit(solution)/shard_map/fisher_of_own_core/pallas_call | solution.py:66
  56.3 1.5 %collective-permute-start.9 = (bf16[2,256,512]{2,1,0:T(8,128)(2,1)}, bf16[2,256,512]{2,1,0:T(8,128)(2,1)}, u32[]{:S(2)}, u32[]{:S(2)}) collective-permute-start(bf16[2,256,512]{2,1,0:T(8,128)(2,1)} %get-tuple-element.59), channel_id=1, source_target_pairs={{0,4},{2,6},{4,0},{6,2},{8,12},{10,14},{12,8},{14,10},{1,5},{3,7},... | collective-permute-start | bytes 1572872 | tf_op jit(solution)/shard_map/ppermute | solution.py:260
  57.8 1.7 %fisher_of_own_core.7 = (bf16[2,256,512]{2,1,0:T(8,128)(2,1)}, f32[2,256,512]{2,1,0:T(8,128)S(1)}) custom-call(bf16[8,768,512]{2,1,0:T(8,128)(2,1)S(1)} %get-tuple-element.40.x_ref.refs_0_, bf16[256,768]{1,0:T(8,128)(2,1)S(1)} %get-tuple-element.53.after.gt_ref, bf16[4,256,512]{2,1,0:T(8,128)(2,1)S(1)} %collective-permute-done.6.got_ref, ...), custom_call_target="tpu_custom_call" | custom-call | flops 805306368 | bytes 8257536 | tf_op jit(solution)/shard_map/fisher_of_own_core/pallas_call | solution.py:66
  59.5 1.8 %collective-permute-done.12.got = bf16[256,512]{1,0:T(8,128)(2,1)S(1)} collective-permute-done((bf16[256,512]{1,0:T(8,128)(2,1)}, bf16[256,512]{1,0:T(8,128)(2,1)S(1)}, u32[]{:S(2)}, u32[]{:S(2)}) %collective-permute-start.12) | collective-permute-done | bytes 262176 | tf_op jit(solution)/shard_map/ppermute | solution.py:266
  61.3 1.0 copy-done.5
  62.4 0.4 weigh_first.2
  62.8 1.0 copy-done.3
  63.8 2.6 %weigh_second.2.after = bf16[8,3,128,128]{3,2,1,0:T(8,128)(2,1)} custom-call(s32[1]{0:T(128)} %bitcast.3.which, f32[256,512]{1,0:T(8,128)S(1)} %copy-done.3, bf16[256,512]{1,0:T(8,128)(2,1)} %collective-permute-done.10.got, bf16[2,512,256]{2,1,0:T(8,128)(2,1)S(1)} %get-tuple-element.51.refs_2_.w_a, bf16[2,512,256]{2,1,0:T(8,128)(2,1)S(1)} %collective-permute-done.11.w_b, ...), custom_call_target="tpu_custom_call" | custom-call | flops 5242880 | bytes 2097152 | tf_op jit(solution)/shard_map/weigh_second/pallas_call | solution.py:66
  66.4 6.0 %all-to-all-start.1 = ((bf16[8,3,128,128]{3,2,1,0:T(8,128)(2,1)}), bf16[8,3,128,128]{3,2,1,0:T(8,128)(2,1)}, u32[]{:S(2)}, u32[]{:S(2)}) async-start(bf16[8,3,128,128]{3,2,1,0:T(8,128)(2,1)} %weigh_second.2.after), calls=%async_computation.1 | async-start | bytes 1572864 | tf_op jit(solution)/shard_map/all_to_all | solution.py:308
  72.4 1.2 %collective-permute-done.9.got_ref = bf16[2,256,512]{2,1,0:T(8,128)(2,1)} collective-permute-done((bf16[2,256,512]{2,1,0:T(8,128)(2,1)}, bf16[2,256,512]{2,1,0:T(8,128)(2,1)}, u32[]{:S(2)}, u32[]{:S(2)}) %collective-permute-start.9) | collective-permute-done | bytes 524320 | tf_op jit(solution)/shard_map/ppermute | solution.py:260
  73.6 2.0 %fisher_over_first_swap.6 = (bf16[256,512]{1,0:T(8,128)(2,1)S(1)}, f32[256,512]{1,0:T(8,128)S(1)}) custom-call(f32[2,256,512]{2,1,0:T(8,128)S(1)} %get-tuple-element.56.after.kept_ref, bf16[2,256,512]{2,1,0:T(8,128)(2,1)} %collective-permute-done.9.got_ref, bf16[8,3,128,128]{3,2,1,0:T(8,128)(2,1)} %weigh_second.2.after), custom_call_target="tpu_custom_call" | custom-call | flops 3932160 | bytes 1835008 | tf_op jit(solution)/shard_map/fisher_over_first_swap/pallas_call | solution.py:66
  75.7 1.4 %collective-permute-start.14 = (bf16[256,512]{1,0:T(8,128)(2,1)S(1)}, bf16[256,512]{1,0:T(8,128)(2,1)S(1)}, u32[]{:S(2)}, u32[]{:S(2)}) collective-permute-start(bf16[256,512]{1,0:T(8,128)(2,1)S(1)} %get-tuple-element.68), channel_id=1, source_target_pairs={{0,12},{2,14},{4,8},{6,10},{8,4},{10,6},{12,0},{14,2},{1,13},{3,15... | collective-permute-start | bytes 786440 | tf_op jit(solution)/shard_map/ppermute | solution.py:266
  77.1 2.3 %fisher_over_first_swap.7 = (bf16[256,512]{1,0:T(8,128)(2,1)}, f32[256,512]{1,0:T(8,128)S(1)}) custom-call(f32[2,256,512]{2,1,0:T(8,128)S(1)} %get-tuple-element.57.after.kept_ref, bf16[2,256,512]{2,1,0:T(8,128)(2,1)} %collective-permute-done.8.got_ref, f32[256,512]{1,0:T(8,128)S(1)} %get-tuple-element.65.after.own), custom_call_target="tpu_custom_call" | custom-call | flops 3932160 | bytes 1310720 | tf_op jit(solution)/shard_map/fisher_over_first_swap/pallas_call | solution.py:66
  79.3 4.4 %collective-permute-done.14.got = bf16[256,512]{1,0:T(8,128)(2,1)S(1)} collective-permute-done((bf16[256,512]{1,0:T(8,128)(2,1)S(1)}, bf16[256,512]{1,0:T(8,128)(2,1)S(1)}, u32[]{:S(2)}, u32[]{:S(2)}) %collective-permute-start.14) | collective-permute-done | bytes 262176 | tf_op jit(solution)/shard_map/ppermute | solution.py:266
  83.7 1.0 copy-done.1
  84.7 0.4 weigh_first.3
  85.1 0.3 collective-permute-done.13.got
  85.4 1.6 %weigh_second.3 = bf16[8,3,128,128]{3,2,1,0:T(8,128)(2,1)} custom-call(s32[1]{0:T(128)} %bitcast.1.which, f32[256,512]{1,0:T(8,128)S(1)} %get-tuple-element.66.after.own, bf16[256,512]{1,0:T(8,128)(2,1)S(1)} %collective-permute-done.13.got, bf16[2,512,256]{2,1,0:T(8,128)(2,1)S(1)} %get-tuple-element.51.refs_2_.w_a, ...), custom_call_target="tpu_custom_call" | custom-call | flops 5242880 | bytes 2097152 | tf_op jit(solution)/shard_map/weigh_second/pallas_call | solution.py:66
  87.1 5.6 %all-to-all-start = ((bf16[8,3,128,128]{3,2,1,0:T(8,128)(2,1)}), bf16[8,3,128,128]{3,2,1,0:T(8,128)(2,1)S(1)}, u32[]{:S(2)}, u32[]{:S(2)}) async-start(bf16[8,3,128,128]{3,2,1,0:T(8,128)(2,1)} %weigh_second.3), calls=%async_computation | async-start | bytes 1572864 | tf_op jit(solution)/shard_map/all_to_all | solution.py:312
  92.7 1.5 %merge_members.2.first_ref = f32[128,128]{1,0:T(8,128)S(1)} custom-call(bf16[8,3,128,128]{3,2,1,0:T(8,128)(2,1)} %all-to-all-done.1.got_ref), custom_call_target="tpu_custom_call" | custom-call | bytes 786432 | tf_op jit(solution)/shard_map/merge_members/pallas_call | solution.py:66
  94.2 6.9 %all-to-all-done.got_ref = bf16[8,3,128,128]{3,2,1,0:T(8,128)(2,1)S(1)} async-done(((bf16[8,3,128,128]{3,2,1,0:T(8,128)(2,1)}), bf16[8,3,128,128]{3,2,1,0:T(8,128)(2,1)S(1)}, u32[]{:S(2)}, u32[]{:S(2)}) %all-to-all-start) | async-done | bytes 786464 | tf_op jit(solution)/shard_map/all_to_all | solution.py:312
  101.0 0.3 merge_members.3
  101.4 7.6 %collective-permute-start.15 = (f32[128,128]{1,0:T(8,128)S(1)}, f32[128,128]{1,0:T(8,128)S(1)}, u32[]{:S(2)}, u32[]{:S(2)}) collective-permute-start(f32[128,128]{1,0:T(8,128)S(1)} %get-tuple-element.71), channel_id=1, source_target_pairs={{0,0},{1,14},{2,64},{3,78},{4,4},{5,10},{6,68},{7,74},{8,6},{9,8},... | collective-permute-start | bytes 196616 | tf_op jit(solution)/shard_map/ppermute | solution.py:317
  109.0 1.9 %collective-permute-start.16 = (f32[128,128]{1,0:T(8,128)S(1)}, f32[128,128]{1,0:T(8,128)S(1)}, u32[]{:S(2)}, u32[]{:S(2)}) collective-permute-start(f32[128,128]{1,0:T(8,128)S(1)} %get-tuple-element.72), channel_id=1, source_target_pairs={{0,1},{1,15},{2,65},{3,79},{4,5},{5,11},{6,69},{7,75},{8,7},{9,9},... | collective-permute-start | bytes 196616 | tf_op jit(solution)/shard_map/ppermute | solution.py:318
  110.9 2.0 %collective-permute-done.15 = f32[128,128]{1,0:T(8,128)S(1)} collective-permute-done((f32[128,128]{1,0:T(8,128)S(1)}, f32[128,128]{1,0:T(8,128)S(1)}, u32[]{:S(2)}, u32[]{:S(2)}) %collective-permute-start.15) | collective-permute-done | bytes 65568 | tf_op jit(solution)/shard_map/ppermute | solution.py:317
  112.9 3.8 %collective-permute-done.16 = f32[128,128]{1,0:T(8,128)S(1)} collective-permute-done((f32[128,128]{1,0:T(8,128)S(1)}, f32[128,128]{1,0:T(8,128)S(1)}, u32[]{:S(2)}, u32[]{:S(2)}) %collective-permute-start.16) | collective-permute-done | bytes 65568 | tf_op jit(solution)/shard_map/ppermute | solution.py:318
  116.7 0.7 pad_maximum_fusion
  (32 shorter events, 0.4 us)
Async XLA Ops:
  5.8 14.0 %collective-permute-start.3 = (bf16[4,256,512]{2,1,0:T(8,128)(2,1)S(1)}, bf16[4,256,512]{2,1,0:T(8,128)(2,1)S(1)}, u32[]{:S(2)}, u32[]{:S(2)}) collective-permute-start(bf16[4,256,512]{2,1,0:T(8,128)(2,1)S(1)} %get-tuple-element.44), channel_id=1, source_target_pairs={{0,2},{2,0},{4,6},{6,4},{8,10},{10,8},{12,14},{14,12},{1,3},{3,1},... | collective-permute-start | bytes 3145736 | tf_op jit(solution)/shard_map/ppermute | solution.py:247
  7.4 5.1 %copy-start.7 = (bf16[2,1024,256]{2,1,0:T(8,128)(2,1)S(1)}, bf16[2,1024,256]{2,1,0:T(8,128)(2,1)}, u32[]{:S(2)}) copy-start(bf16[2,1024,256]{2,1,0:T(8,128)(2,1)} %param.7) | copy-start | bytes 3145732
  7.4 10.0 %copy-start.6 = (bf16[2,768,256]{2,1,0:T(8,128)(2,1)S(1)}, bf16[2,768,256]{2,1,0:T(8,128)(2,1)}, u32[]{:S(2)}) copy-start(bf16[2,768,256]{2,1,0:T(8,128)(2,1)} %refs_2_.3) | copy-start | bytes 2359300
  12.4 8.6 %collective-permute-start.2 = (bf16[4,256,512]{2,1,0:T(8,128)(2,1)S(1)}, bf16[4,256,512]{2,1,0:T(8,128)(2,1)S(1)}, u32[]{:S(2)}, u32[]{:S(2)}) collective-permute-start(bf16[4,256,512]{2,1,0:T(8,128)(2,1)S(1)} %get-tuple-element.43), channel_id=1, source_target_pairs={{0,2},{2,0},{4,6},{6,4},{8,10},{10,8},{12,14},{14,12},{1,3},{3,1},... | collective-permute-start | bytes 3145736 | tf_op jit(solution)/shard_map/ppermute | solution.py:247
  12.5 32.6 %collective-permute-start.1 = (bf16[2,1024,256]{2,1,0:T(8,128)(2,1)S(1)}, bf16[2,1024,256]{2,1,0:T(8,128)(2,1)S(1)}, u32[]{:S(2)}, u32[]{:S(2)}) collective-permute-start(bf16[2,1024,256]{2,1,0:T(8,128)(2,1)S(1)} %copy-done.7), channel_id=1, source_target_pairs={{0,0},{1,2},{2,12},{3,14},{4,4},{5,6},{6,8},{7,10},{8,9},{9,11},{1... | collective-permute-start | bytes 3145736 | tf_op jit(solution)/shard_map/ppermute | solution.py:281
  17.4 29.7 %collective-permute-start = (bf16[2,768,256]{2,1,0:T(8,128)(2,1)S(1)}, bf16[2,768,256]{2,1,0:T(8,128)(2,1)S(1)}, u32[]{:S(2)}, u32[]{:S(2)}) collective-permute-start(bf16[2,768,256]{2,1,0:T(8,128)(2,1)S(1)} %copy-done.6), channel_id=1, source_target_pairs={{0,1},{1,0},{2,3},{3,2},{4,5},{5,4},{6,7},{7,6},{8,9},{9,8},{10,11... | collective-permute-start | bytes 2359304 | tf_op jit(solution)/shard_map/ppermute | solution.py:280
  20.9 13.0 %collective-permute-start.5 = (bf16[2,256,512]{2,1,0:T(8,128)(2,1)S(1)}, bf16[2,256,512]{2,1,0:T(8,128)(2,1)S(1)}, u32[]{:S(2)}, u32[]{:S(2)}) collective-permute-start(bf16[2,256,512]{2,1,0:T(8,128)(2,1)S(1)} %get-tuple-element.48), channel_id=1, source_target_pairs={{0,4},{2,6},{4,0},{6,2},{8,12},{10,14},{12,8},{14,10},{1,5},{3,7},... | collective-permute-start | bytes 1572872 | tf_op jit(solution)/shard_map/ppermute | solution.py:260
  22.2 21.7 %collective-permute-start.4 = (bf16[2,256,512]{2,1,0:T(8,128)(2,1)S(1)}, bf16[2,256,512]{2,1,0:T(8,128)(2,1)S(1)}, u32[]{:S(2)}, u32[]{:S(2)}) collective-permute-start(bf16[2,256,512]{2,1,0:T(8,128)(2,1)S(1)} %get-tuple-element.47), channel_id=1, source_target_pairs={{0,12},{2,14},{4,8},{6,10},{8,4},{10,6},{12,0},{14,2},{1,13},{3,15... | collective-permute-start | bytes 1572872 | tf_op jit(solution)/shard_map/ppermute | solution.py:260
  35.2 14.8 %copy-start.4 = (f32[256,512]{1,0:T(8,128)}, f32[256,512]{1,0:T(8,128)S(1)}, u32[]{:S(2)}) copy-start(f32[256,512]{1,0:T(8,128)S(1)} %get-tuple-element.49.after.own) | copy-start | bytes 1572868
  45.2 4.8 %copy-start.2 = (f32[256,512]{1,0:T(8,128)}, f32[256,512]{1,0:T(8,128)S(1)}, u32[]{:S(2)}) copy-start(f32[256,512]{1,0:T(8,128)S(1)} %get-tuple-element.50.after.own) | copy-start | bytes 1572868
  48.1 6.5 %collective-permute-start.7 = (bf16[4,256,512]{2,1,0:T(8,128)(2,1)S(1)}, bf16[4,256,512]{2,1,0:T(8,128)(2,1)S(1)}, u32[]{:S(2)}, u32[]{:S(2)}) collective-permute-start(bf16[4,256,512]{2,1,0:T(8,128)(2,1)S(1)} %get-tuple-element.55), channel_id=1, source_target_pairs={{0,2},{2,0},{4,6},{6,4},{8,10},{10,8},{12,14},{14,12},{1,3},{3,1},... | collective-permute-start | bytes 3145736 | tf_op jit(solution)/shard_map/ppermute | solution.py:247
  50.0 7.8 %collective-permute-start.6 = (bf16[4,256,512]{2,1,0:T(8,128)(2,1)S(1)}, bf16[4,256,512]{2,1,0:T(8,128)(2,1)S(1)}, u32[]{:S(2)}, u32[]{:S(2)}) collective-permute-start(bf16[4,256,512]{2,1,0:T(8,128)(2,1)S(1)} %get-tuple-element.54), channel_id=1, source_target_pairs={{0,2},{2,0},{4,6},{6,4},{8,10},{10,8},{12,14},{14,12},{1,3},{3,1},... | collective-permute-start | bytes 3145736 | tf_op jit(solution)/shard_map/ppermute | solution.py:247
  50.1 11.3 %collective-permute-start.11 = (bf16[2,512,256]{2,1,0:T(8,128)(2,1)}, bf16[2,512,256]{2,1,0:T(8,128)(2,1)S(1)}, u32[]{:S(2)}, u32[]{:S(2)}) collective-permute-start(bf16[2,512,256]{2,1,0:T(8,128)(2,1)} %get-tuple-element.61), channel_id=1, source_target_pairs={{0,2},{2,0},{4,6},{6,4},{8,10},{10,8},{12,14},{14,12},{1,3},{3,1},... | collective-permute-start | bytes 1572872 | tf_op jit(solution)/shard_map/ppermute | solution.py:247
  50.6 10.8 %collective-permute-start.12 = (bf16[256,512]{1,0:T(8,128)(2,1)}, bf16[256,512]{1,0:T(8,128)(2,1)S(1)}, u32[]{:S(2)}, u32[]{:S(2)}) collective-permute-start(bf16[256,512]{1,0:T(8,128)(2,1)} %get-tuple-element.62), channel_id=1, source_target_pairs={{0,12},{2,14},{4,8},{6,10},{8,4},{10,6},{12,0},{14,2},{1,13},{3,15... | collective-permute-start | bytes 786440 | tf_op jit(solution)/shard_map/ppermute | solution.py:266
  54.5 8.2 %collective-permute-start.10 = (bf16[256,512]{1,0:T(8,128)(2,1)}, bf16[256,512]{1,0:T(8,128)(2,1)}, u32[]{:S(2)}, u32[]{:S(2)}) collective-permute-start(bf16[256,512]{1,0:T(8,128)(2,1)} %get-tuple-element.60), channel_id=1, source_target_pairs={{0,4},{2,6},{4,0},{6,2},{8,12},{10,14},{12,8},{14,10},{1,5},{3,7},... | collective-permute-start | bytes 786440 | tf_op jit(solution)/shard_map/ppermute | solution.py:266
  56.3 17.3 %collective-permute-start.9 = (bf16[2,256,512]{2,1,0:T(8,128)(2,1)}, bf16[2,256,512]{2,1,0:T(8,128)(2,1)}, u32[]{:S(2)}, u32[]{:S(2)}) collective-permute-start(bf16[2,256,512]{2,1,0:T(8,128)(2,1)} %get-tuple-element.59), channel_id=1, source_target_pairs={{0,4},{2,6},{4,0},{6,2},{8,12},{10,14},{12,8},{14,10},{1,5},{3,7},... | collective-permute-start | bytes 1572872 | tf_op jit(solution)/shard_map/ppermute | solution.py:260
  59.5 17.5 %collective-permute-start.8 = (bf16[2,256,512]{2,1,0:T(8,128)(2,1)}, bf16[2,256,512]{2,1,0:T(8,128)(2,1)}, u32[]{:S(2)}, u32[]{:S(2)}) collective-permute-start(bf16[2,256,512]{2,1,0:T(8,128)(2,1)} %get-tuple-element.58), channel_id=1, source_target_pairs={{0,12},{2,14},{4,8},{6,10},{8,4},{10,6},{12,0},{14,2},{1,13},{3,15... | collective-permute-start | bytes 1572872 | tf_op jit(solution)/shard_map/ppermute | solution.py:260
  61.3 1.0 copy-start.5
  62.8 1.0 copy-start.3
  66.4 20.7 %all-to-all-start.1 = ((bf16[8,3,128,128]{3,2,1,0:T(8,128)(2,1)}), bf16[8,3,128,128]{3,2,1,0:T(8,128)(2,1)}, u32[]{:S(2)}, u32[]{:S(2)}) async-start(bf16[8,3,128,128]{3,2,1,0:T(8,128)(2,1)} %weigh_second.2.after), calls=%async_computation.1 | async-start | bytes 1572864 | tf_op jit(solution)/shard_map/all_to_all | solution.py:308
  75.7 3.7 %copy-start = (f32[256,512]{1,0:T(8,128)}, f32[256,512]{1,0:T(8,128)S(1)}, u32[]{:S(2)}) copy-start(f32[256,512]{1,0:T(8,128)S(1)} %get-tuple-element.65.after.own) | copy-start | bytes 1572868
  75.7 8.0 %collective-permute-start.14 = (bf16[256,512]{1,0:T(8,128)(2,1)S(1)}, bf16[256,512]{1,0:T(8,128)(2,1)S(1)}, u32[]{:S(2)}, u32[]{:S(2)}) collective-permute-start(bf16[256,512]{1,0:T(8,128)(2,1)S(1)} %get-tuple-element.68), channel_id=1, source_target_pairs={{0,12},{2,14},{4,8},{6,10},{8,4},{10,6},{12,0},{14,2},{1,13},{3,15... | collective-permute-start | bytes 786440 | tf_op jit(solution)/shard_map/ppermute | solution.py:266
  79.3 6.1 %collective-permute-start.13 = (bf16[256,512]{1,0:T(8,128)(2,1)}, bf16[256,512]{1,0:T(8,128)(2,1)S(1)}, u32[]{:S(2)}, u32[]{:S(2)}) collective-permute-start(bf16[256,512]{1,0:T(8,128)(2,1)} %get-tuple-element.67), channel_id=1, source_target_pairs={{0,4},{2,6},{4,0},{6,2},{8,12},{10,14},{12,8},{14,10},{1,5},{3,7},... | collective-permute-start | bytes 786440 | tf_op jit(solution)/shard_map/ppermute | solution.py:266
  83.7 1.0 copy-start.1
  87.1 14.0 %all-to-all-start = ((bf16[8,3,128,128]{3,2,1,0:T(8,128)(2,1)}), bf16[8,3,128,128]{3,2,1,0:T(8,128)(2,1)S(1)}, u32[]{:S(2)}, u32[]{:S(2)}) async-start(bf16[8,3,128,128]{3,2,1,0:T(8,128)(2,1)} %weigh_second.3), calls=%async_computation | async-start | bytes 1572864 | tf_op jit(solution)/shard_map/all_to_all | solution.py:312
  101.4 11.5 %collective-permute-start.15 = (f32[128,128]{1,0:T(8,128)S(1)}, f32[128,128]{1,0:T(8,128)S(1)}, u32[]{:S(2)}, u32[]{:S(2)}) collective-permute-start(f32[128,128]{1,0:T(8,128)S(1)} %get-tuple-element.71), channel_id=1, source_target_pairs={{0,0},{1,14},{2,64},{3,78},{4,4},{5,10},{6,68},{7,74},{8,6},{9,8},... | collective-permute-start | bytes 196616 | tf_op jit(solution)/shard_map/ppermute | solution.py:317
  109.0 7.7 %collective-permute-start.16 = (f32[128,128]{1,0:T(8,128)S(1)}, f32[128,128]{1,0:T(8,128)S(1)}, u32[]{:S(2)}, u32[]{:S(2)}) collective-permute-start(f32[128,128]{1,0:T(8,128)S(1)} %get-tuple-element.72), channel_id=1, source_target_pairs={{0,1},{1,15},{2,65},{3,79},{4,5},{5,11},{6,69},{7,75},{8,7},{9,9},... | collective-permute-start | bytes 196616 | tf_op jit(solution)/shard_map/ppermute | solution.py:318

commit v4 on v0

v4 whole, which is shorter than its diff:
```python
import jax
import jax.numpy as jnp
from jax import lax
from jax.experimental import pallas as pl
from jax.experimental.pallas import tpu as pltpu
from jax.sharding import PartitionSpec as P

F32 = jnp.float32
BF16 = jnp.bfloat16
HBM = pl.BlockSpec(memory_space=pltpu.HBM)
VMEM = pl.BlockSpec(memory_space=pltpu.VMEM)
VMEM_LIMIT = 16 << 20

GRID = 1.00297
BIG = 2.0**28
SMALL = 2.0**16
EDGE = 2.0**-40
EDGE_CODE = 2.0**-24

X, CORES, Z = 4, 2, 4

ORDERS = ((1, 2, 0, 3), (3, 2, 0, 1))


def code_of(values):
    scaled = values * BIG
    return jnp.where(values >= EDGE, scaled * scaled, values * SMALL)


def value_of(code):
    return jnp.where(code >= EDGE_CODE, jnp.sqrt(code) * (1.0 / BIG), code * (1.0 / SMALL))


def encode(values):
    return code_of(values).astype(BF16)


def decode(sent):
    return value_of(sent.astype(F32))


def encode_fine(values):
    code = code_of(values)
    first = code.astype(BF16).astype(F32)
    second = (code * (1.0 / GRID)).astype(BF16).astype(F32)
    near = jnp.abs(first - code) <= jnp.abs(second * GRID - code)
    return jnp.where(near, first, -second).astype(BF16)


def decode_fine(sent):
    code = sent.astype(F32)
    return value_of(jnp.where(code < 0.0, code * (-GRID), code))


def in_vmem(array):
    return pltpu.with_memory_space_constraint(array, pltpu.VMEM)


def in_hbm(array):
    return pltpu.with_memory_space_constraint(array, pltpu.HBM)


def call(kernel, name, outs, hbm, vmem, scratch=(), flops=0):
    single = not isinstance(outs, list)
    shapes = [pltpu.VMEM(shape, kind) for shape, kind in ([outs] if single else outs)]
    moved = sum(a.size * 2 for a in vmem) + sum(a.size * 2 for a in hbm)
    result = pl.pallas_call(
        kernel,
        out_shape=shapes,
        in_specs=[HBM] * len(hbm) + [VMEM] * len(vmem),
        out_specs=[VMEM] * len(shapes),
        scratch_shapes=list(scratch),
        compiler_params=pltpu.CompilerParams(vmem_limit_bytes=VMEM_LIMIT),
        cost_estimate=pl.CostEstimate(flops=flops, bytes_accessed=moved, transcendentals=0),
        name=name,
    )(*[in_hbm(a) for a in hbm], *[in_vmem(a) for a in vmem])
    return result[0] if single else result


def squared_transposed(g):
    g = g.astype(F32)
    return (g * g).T.astype(BF16)


def fisher_block(x, gt_ref):
    return jnp.dot(gt_ref[...], x * x, preferred_element_type=F32)


def where_am_i():
    tok, half, member = lax.axis_index("tok"), lax.axis_index("col"), lax.axis_index("member")
    return tok // 2, tok % 2, half, member // Z, member % Z


def column_block(flip, part):
    x, _, half, _, _ = where_am_i()
    owner = x ^ flip
    local = jnp.where(owner // 2 == half, 2 * (owner % 2), 2 * ((3 - owner) % 2) + 1)
    return 2 * local + part


def load_inputs(member, part, x_ref, x_out, sem):
    wide = x_out.shape[2]
    copies = []
    for s, flip in enumerate(ORDERS[part]):
        at = pl.multiple_of(column_block(flip, part) * wide, wide)
        copies.append(pltpu.make_async_copy(x_ref.at[member, :, pl.ds(at, wide)], x_out.at[s], sem.at[s]))
        copies[s].start()
    return copies


def load_first_kernel(x_ref, g_ref, x_out, g_out, g_own_out, sem, g_sem):
    core = where_am_i()[1]
    loads = [
        pltpu.make_async_copy(g_ref.at[1 - core], g_out, g_sem.at[0]),
        pltpu.make_async_copy(g_ref.at[core], g_own_out, g_sem.at[1]),
    ]
    for copy in loads:
        copy.start()
    for copy in load_inputs(1 - core, 0, x_ref, x_out, sem) + loads:
        copy.wait()


def load_second_kernel(x_ref, after, x_out, sem):
    for copy in load_inputs(1 - where_am_i()[1], 1, x_ref, x_out, sem):
        copy.wait()


def pair_kernel(own, got, after, out):
    out[0], out[1] = own[...], got[...]


def own_tokens(copies, x_out, gt_ref, part_out):
    for s in range(4):
        copies[s].wait()
        part_out[s] = fisher_block(x_out[s], gt_ref)


def own_first_kernel(x_ref, g_ref, after, x_out, gt_out, part_out, sem):
    copies = load_inputs(where_am_i()[1], 0, x_ref, x_out, sem)
    gt_out[...] = squared_transposed(g_ref[...])
    own_tokens(copies, x_out, gt_out, part_out)


def own_second_kernel(x_ref, gt_ref, after, x_out, part_out, sem):
    copies = load_inputs(where_am_i()[1], 1, x_ref, x_out, sem)
    own_tokens(copies, x_out, gt_ref, part_out)


def put(s, block, sent_out, kept_out):
    if s < 2:
        sent_out[s] = encode(block)
    else:
        kept_out[s - 2] = block


def add_first_kernel(x_ref, g_ref, part_ref, sent_out, kept_out, gt_out):
    gt_out[...] = squared_transposed(g_ref[...])
    for s in range(4):
        put(s, part_ref[s] + fisher_block(x_ref[s], gt_out), sent_out, kept_out)


def add_second_kernel(x_ref, gt_ref, part_ref, after, sent_out, kept_out):
    for s in range(4):
        put(s, part_ref[s] + fisher_block(x_ref[s], gt_ref), sent_out, kept_out)


def both_first_kernel(xa_ref, xb_ref, g_ref, after, sent_out, kept_out, gta_out, gtb_out):
    gta_out[...] = squared_transposed(g_ref[0])
    gtb_out[...] = squared_transposed(g_ref[1])
    for s in range(4):
        put(s, fisher_block(xa_ref[s], gta_out) + fisher_block(xb_ref[s], gtb_out), sent_out, kept_out)


def both_second_kernel(xa_ref, xb_ref, gta_ref, gtb_ref, after, sent_out, kept_out):
    for s in range(4):
        put(s, fisher_block(xa_ref[s], gta_ref) + fisher_block(xb_ref[s], gtb_ref), sent_out, kept_out)


def middle_kernel(kept_ref, got_ref, after, sent_out, own_out):
    sent_out[...] = encode_fine(kept_ref[1] + decode(got_ref[1]))
    own_out[...] = kept_ref[0] + decode(got_ref[0])


def join_kernel(own_a, got_a, own_b, got_b, after, kept_out, sent_out):
    first = own_a[...] + decode_fine(got_a[...])
    second = own_b[...] + decode_fine(got_b[...])
    core = where_am_i()[1]
    kept_out[...] = jnp.where(core == 0, first, second)
    sent_out[...] = jnp.where(core == 0, second, first)


def split_kernel(w_ref, after, own_out, send_out):
    rows, core = own_out.shape[1], where_am_i()[1]
    own_out[...] = w_ref[:, pl.ds(pl.multiple_of(core * rows, rows), rows), :]
    send_out[...] = w_ref[:, pl.ds(pl.multiple_of((1 - core) * rows, rows), rows), :]


def to_words(weighted, total, out):
    high = weighted.astype(BF16)
    out[0] = high
    out[1] = (weighted - high.astype(F32)).astype(BF16)
    out[2] = encode_fine(total)


def from_words(words):
    return words[0].astype(F32) + words[1].astype(F32), decode_fine(words[2])


def weigh_kernel(phase, own, other, w_a, w_b, after, one_out, two_out, three_out, sums_out):
    _, core, half, _, z = where_am_i()
    part = own.shape[1] // Z
    first = (core ^ half ^ phase) == 0
    for d, out in ((2, two_out), (1, one_out), (3, three_out), (0, sums_out)):
        cols = pl.ds(pl.multiple_of((z + d) % Z * part, part), part)
        weighted = total = 0.0
        for values, m in ((own, core), (other, 1 - core)):
            fisher = values[:, cols].T
            weight = jnp.where(first, w_a[m, cols, :].astype(F32), w_b[m, cols, :].astype(F32))
            weighted += fisher * weight
            total += fisher
        if d == 0:
            out[0], out[1] = weighted, total
        else:
            to_words(weighted, total, out)


def over_z(sums, words):
    weighted, total = sums[0], sums[1]
    for ref in words:
        more, added = from_words(ref)
        weighted += more
        total += added
    return weighted, total


def sum_kernel(one, two, three, sums, out):
    to_words(*over_z(sums, (one, two, three)), out)


def sum_last_kernel(one, two, three, sums, first, near_out, far_out):
    y_lo = where_am_i()[3]

    @pl.when(y_lo == 0)
    def _():
        to_words(*over_z(sums, (one, two, three)), far_out)
        near_out[...] = first[...]

    @pl.when(y_lo != 0)
    def _():
        to_words(*over_z(sums, (one, two, three)), near_out)
        far_out[...] = first[...]


def merge_kernel(near, far, out):
    weighted, total = from_words(near)
    more, added = from_words(far)
    out[...] = (weighted + more) / (total + added)


def keeper(local, half):
    home = 2 * half + local // 2
    return home if local % 2 == 0 else 3 - home


def kept(x, half):
    return 2 * (x % 2) if x // 2 == half else 2 * ((3 - x) % 2) + 1


def weight_pairs():
    pairs = []
    for tok in range(X * CORES):
        half, local = divmod(tok, 4)
        for col in range(2):
            pairs.append((tok * 2 + col, (keeper(local, half) * 2 + col) * 2 + half))
    return pairs


def result_pairs(flip):
    pairs = []
    for member in range(8):
        y_lo, z = divmod(member, 4)
        for tok in range(8):
            x, core = divmod(tok, 2)
            for half in range(2):
                to_member = core * 4 + z
                to_tok = 4 * half + kept(x, half)
                to_col = half ^ y_lo ^ flip
                pairs.append(((member * 8 + tok) * 2 + half, (to_member * 8 + to_tok) * 2 + to_col))
    return pairs


def x_pairs(flip):
    return [(t, ((t // 2) ^ flip) * 2 + t % 2) for t in range(X * CORES)]


def z_pairs(distance):
    return [(m, m // Z * Z + (m + distance) % Z) for m in range(2 * Z)]


def shards(inputs, grads, weights):
    tokens, outs = grads.shape[1:]
    wide = inputs.shape[2] // 8
    x_shape, g_shape, gt_shape = ((4, tokens, wide), BF16), ((tokens, outs), BF16), ((outs, tokens), BF16)
    part_shape, sent_shape, kept_shape = ((4, outs, wide), F32), ((2, outs, wide), BF16), ((2, outs, wide), F32)
    code_shape, own_shape = ((outs, wide), BF16), ((outs, wide), F32)
    words, sums = ((3, wide // Z, outs), BF16), ((2, wide // Z, outs), F32)
    dma = pltpu.SemaphoreType.DMA
    flops = 8 * outs * wide * tokens

    def swap_cores(send):
        return lax.ppermute(send, "tok", [(t, t ^ 1) for t in range(8)])

    def swap_cols(send):
        return lax.ppermute(send, "col", [(0, 1), (1, 0)])

    def first_swap(part, sent):
        return lax.ppermute(sent, "tok", x_pairs(ORDERS[part][0]))

    def middle(part, got, kept_blocks, after):
        sent, own = call(middle_kernel, "fisher_over_first_swap", [code_shape, own_shape], [], [kept_blocks, got, after])
        return own, lax.ppermute(sent, "tok", x_pairs(ORDERS[part][3]))

    def join(one, two, after):
        kept_block, sent = call(join_kernel, "fisher_over_tokens", [own_shape, own_shape], [], [*one, *two, after])
        return kept_block, swap_cores(sent)

    def weigh(phase, own, other, after):
        one, two, three, own_sums = call(
            lambda *refs: weigh_kernel(phase, *refs), "weigh_members", [words] * 3 + [sums], [], [own, other, *moved, after]
        )
        send = ((1, one), (2, two), (3, three))
        return [lax.ppermute(v, "member", z_pairs(d)) for d, v in send] + [own_sums]

    x_send0, g_send, g_own = call(
        load_first_kernel, "load_to_swap", [x_shape, g_shape, g_shape], [inputs, grads], [], [dma((4,)), dma((2,))]
    )
    x_got0 = swap_cores(x_send0)
    g_got = swap_cores(g_send)
    x_send1 = call(load_second_kernel, "load_to_swap", x_shape, [inputs], [g_own], [dma((4,))])
    x_got1 = swap_cores(x_send1)
    g_pair = call(pair_kernel, "pair_grads", ((2, tokens, outs), BF16), [], [g_own, g_got, x_send1])
    g_other = swap_cols(g_pair)

    x_own0, gt_own, part0 = call(
        own_first_kernel, "fisher_of_own_tokens", [x_shape, gt_shape, part_shape], [inputs], [g_own, g_pair],
        [dma((4,))], flops,
    )
    sent, kept00, gt_got = call(
        add_first_kernel, "fisher_of_both_cores", [sent_shape, kept_shape, gt_shape], [], [x_got0, g_got, part0], flops=flops
    )
    swap00 = first_swap(0, sent)
    x_own1, part1 = call(
        own_second_kernel, "fisher_of_own_tokens", [x_shape, part_shape], [inputs], [gt_own, kept00], [dma((4,))], flops
    )
    sent, kept01 = call(
        add_second_kernel, "fisher_of_both_cores", [sent_shape, kept_shape], [], [x_got1, gt_got, part1, x_own1], flops=flops
    )
    swap01 = first_swap(1, sent)
    part00 = middle(0, swap00, kept00, kept01)
    part01 = middle(1, swap01, kept01, part00[0])

    sent, kept10, gt_own, gt_got = call(
        both_first_kernel, "fisher_of_other_grads", [sent_shape, kept_shape, gt_shape, gt_shape], [],
        [x_own0, x_got0, g_other, part01[0]], flops=2 * flops,
    )
    swap10 = first_swap(0, sent)
    sent, kept11 = call(
        both_second_kernel, "fisher_of_other_grads", [sent_shape, kept_shape], [],
        [x_own1, x_got1, gt_own, gt_got, kept10], flops=2 * flops,
    )
    swap11 = first_swap(1, sent)
    own0, other0 = join(part00, part01, kept11)
    part10 = middle(0, swap10, kept10, own0)
    part11 = middle(1, swap11, kept11, part10[0])

    arrived = lax.ppermute(weights, ("tok", "col"), weight_pairs())
    rows = weights.shape[1] // 2
    w_own, w_send = call(split_kernel, "split_weights", [((2, rows, outs), BF16)] * 2, [], [arrived, part11[0]])
    moved = (w_own, swap_cores(w_send))
    words0 = weigh(0, own0, other0, w_own)
    own1, other1 = join(part10, part11, words0[3])
    words1 = weigh(1, own1, other1, own1)
    first = call(sum_kernel, "sum_over_z", words, [], words0)
    near, far = call(sum_last_kernel, "sum_over_z", [words, words], [], [*words1, first])

    names = ("member", "tok", "col")
    near = lax.ppermute(near, names, result_pairs(0))
    far = lax.ppermute(far, names, result_pairs(1))
    return pl.pallas_call(
        merge_kernel,
        out_shape=jax.ShapeDtypeStruct((wide // Z, outs), F32),
        in_specs=[VMEM, VMEM],
        out_specs=VMEM,
        compiler_params=pltpu.CompilerParams(vmem_limit_bytes=VMEM_LIMIT),
        name="merge_members",
    )(in_vmem(near), in_vmem(far))


def solution(mesh):
    in_specs = (P("member", "tok", "col"), P("member", "tok", "col"), P("member", "tok", "col"))
    out_specs = P(("tok", "member"), "col")
    return jax.shard_map(shards, mesh=mesh, in_specs=in_specs, out_specs=out_specs, check_vma=False)
```

time: 717 us -> 121 us (0.17)
  waiting for transfers between devices: 633 us -> 64.5 us
  starting transfers between devices: 0.08 us -> 33.5 us
  local copies, waits for them, and re-layouts: 22.9 us -> 0.01 us
  Pallas kernels: 0 us -> 22.5 us
  matrix products: 21.9 us -> 0 us
  other arithmetic: 19.9 us -> 0 us
  between operations: 13.1 us -> 0.22 us
    all_gather x2 -> x0, waiting for transfers between devices: 327 us -> none  [the longest x1 300 us: shards(): input_sq = lax.all_gather(squared(inputs), 'col', axis=2, tiled=True)]
    reduce_scatter x1 -> x0, waiting for transfers between devices: 306 us -> none  [shards(): lax.psum_scatter(sums, ('member', 'tok'), scatter_dimension=1, tiled=True)]
    ppermute x0 -> x24, waiting for transfers between devices: none -> 64.5 us  [the longest x4 28.2 us: middle(): return (own, lax.ppermute(sent, 'tok', x_pairs(ORDERS[part][3])))]
    ppermute x0 -> x24, starting transfers between devices: none -> 33.5 us  [the longest x6 8.22 us: weigh(): return [lax.ppermute(v, 'member', z_pairs(d)) for d, v in send] + [own_sums]]
    pallas_call x0 -> x21, Pallas kernels: none -> 22.5 us  [the longest x20 21.6 us: call(): pl.pallas_call(kernel, out_shape=shapes, in_specs=[HBM] * len(hbm) + [VME...]
    dot_general x1 -> x0, matrix products: 21.9 us -> none  [shards(): jnp.einsum('mti,mto->mio', input_sq, grad_sq, preferred_element_type=jnp....]
    unnamed x3 -> x2, local copies, waits for them, and re-layouts: 16.7 us -> 0.01 us
    convert_element_type x1 -> x0, other arithmetic: 11.5 us -> none  [squared(): return (values.astype(jnp.float32) ** 2).astype(jnp.bfloat16)]
  transfers between devices with their start and end apart: 3 -> 24, of which waited for: 3 -> 12; matrix products, arithmetic and copies ran while one was open for 4% -> 0% of each run, Pallas kernels for 0% -> 15%
where the time goes in v4:
time: 121 us
  waiting for transfers between devices  64.5 us (53%)
  starting transfers between devices  33.5 us (28%)
  Pallas kernels  22.5 us (19%)
    ppermute x4, waiting for transfers between devices, middle(): return (own, lax.ppermute(sent, 'tok', x_pairs(ORDERS[part][3])))  28.2 us
    pallas_call x20, Pallas kernels, call(): pl.pallas_call(kernel, out_shape=shapes, in_specs=[HBM] * len(hbm) + [VME...  21.6 us
    ppermute x6, waiting for transfers between devices, weigh(): return [lax.ppermute(v, 'member', z_pairs(d)) for d, v in send] + [own_sums]  13.5 us
    ppermute x6, starting transfers between devices, weigh(): return [lax.ppermute(v, 'member', z_pairs(d)) for d, v in send] + [own_sums]  8.22 us
    ppermute x6, waiting for transfers between devices, swap_cores(): return lax.ppermute(send, 'tok', [(t, t ^ 1) for t in range(8)])  7.87 us
    ppermute x4, waiting for transfers between devices, first_swap(): return lax.ppermute(sent, 'tok', x_pairs(ORDERS[part][0]))  7.32 us
    ppermute x4, starting transfers between devices, first_swap(): return lax.ppermute(sent, 'tok', x_pairs(ORDERS[part][0]))  5.13 us
    ppermute x6, starting transfers between devices, swap_cores(): return lax.ppermute(send, 'tok', [(t, t ^ 1) for t in range(8)])  4.39 us
  transfers between devices with their start and end apart: 24, of which 12 were waited for; matrix products, arithmetic and copies ran while one was open for 0% of the time, Pallas kernels for 15%

profile of v4, /device:TPU:1, one launch (start us, length us, event | category | flops | bytes accessed | tf_op | source)
XLA Modules:
  0.0 120.7 jit_solution(7685447410424629127)
XLA Ops:
  0.0 2.2 %load_to_swap.2 = (bf16[4,768,512]{2,1,0:T(8,128)(2,1)S(1)}, bf16[768,256]{1,0:T(8,128)(2,1)S(1)}, bf16[768,256]{1,0:T(8,128)(2,1)S(1)}) custom-call(bf16[2,768,4096]{2,1,0:T(8,128)(2,1)} %x_ref.7, bf16[2,768,256]{2,1,0:T(8,128)(2,1)} %g_ref.1), custom_call_target="tpu_custom_call" | custom-call | bytes 13369344 | tf_op jit(solution)/shard_map/load_to_swap/pallas_call | solution.py:67
  2.2 1.5 %collective-permute-start.1 = (bf16[4,768,512]{2,1,0:T(8,128)(2,1)S(1)}, bf16[4,768,512]{2,1,0:T(8,128)(2,1)S(1)}, u32[]{:S(2)}, u32[]{:S(2)}) collective-permute-start(bf16[4,768,512]{2,1,0:T(8,128)(2,1)S(1)} %get-tuple-element.51), channel_id=1, source_target_pairs={{0,2},{2,0},{4,6},{6,4},{8,10},{10,8},{12,14},{14,12},{1,3},{3,1},... | collective-permute-start | bytes 9437192 | tf_op jit(solution)/shard_map/ppermute | solution.py:311
  3.7 1.9 %load_to_swap.3.after = bf16[4,768,512]{2,1,0:T(8,128)(2,1)S(1)} custom-call(bf16[2,768,4096]{2,1,0:T(8,128)(2,1)} %x_ref.7, bf16[768,256]{1,0:T(8,128)(2,1)S(1)} %get-tuple-element.48.after.own.g_ref), custom_call_target="tpu_custom_call" | custom-call | bytes 12976128 | tf_op jit(solution)/shard_map/load_to_swap/pallas_call | solution.py:67
  5.7 0.5 collective-permute-start
  6.2 7.9 %collective-permute-done.got.g_ref = bf16[768,256]{1,0:T(8,128)(2,1)S(1)} collective-permute-done((bf16[768,256]{1,0:T(8,128)(2,1)S(1)}, bf16[768,256]{1,0:T(8,128)(2,1)S(1)}, u32[]{:S(2)}, u32[]{:S(2)}) %collective-permute-start) | collective-permute-done | bytes 393248 | tf_op jit(solution)/shard_map/ppermute | solution.py:311
  14.1 3.1 %collective-permute-start.2 = (bf16[2,768,256]{2,1,0:T(8,128)(2,1)S(1)}, bf16[2,768,256]{2,1,0:T(8,128)(2,1)S(1)}, u32[]{:S(2)}, u32[]{:S(2)}) collective-permute-start(bf16[2,768,256]{2,1,0:T(8,128)(2,1)S(1)} %pair_grads.1.after), channel_id=1, source_target_pairs={{0,1},{1,0},{2,3},{3,2},{4,5},{5,4},{6,7},{7,6},{8,9},{9,8},{10,11... | collective-permute-start | bytes 2359304 | tf_op jit(solution)/shard_map/ppermute | solution.py:314
  17.1 2.8 %fisher_of_own_tokens.2 = (bf16[4,768,512]{2,1,0:T(8,128)(2,1)S(1)}, bf16[256,768]{1,0:T(8,128)(2,1)S(1)}, f32[4,256,512]{2,1,0:T(8,128)S(1)}) custom-call(bf16[2,768,4096]{2,1,0:T(8,128)(2,1)} %x_ref.7, bf16[768,256]{1,0:T(8,128)(2,1)S(1)} %get-tuple-element.48.after.own.g_ref, bf16[2,768,256]{2,1,0:T(8,128)(2,1)S(1)} %pair_grads.1.after), custom_call_target="tpu_custom_call" | custom-call | flops 805306368 | bytes 13762560 | tf_op jit(solution)/shard_map/fisher_of_own_tokens/pallas_call | solution.py:67
  19.9 1.2 fisher_of_both_cores.2
  21.1 1.3 %collective-permute-start.5 = (bf16[2,256,512]{2,1,0:T(8,128)(2,1)S(1)}, bf16[2,256,512]{2,1,0:T(8,128)(2,1)S(1)}, u32[]{:S(2)}, u32[]{:S(2)}) collective-permute-start(bf16[2,256,512]{2,1,0:T(8,128)(2,1)S(1)} %get-tuple-element.60), channel_id=1, source_target_pairs={{0,4},{2,6},{4,0},{6,2},{8,12},{10,14},{12,8},{14,10},{1,5},{3,7},... | collective-permute-start | bytes 1572872 | tf_op jit(solution)/shard_map/ppermute | solution.py:317
  22.4 2.7 %fisher_of_own_tokens.3 = (bf16[4,768,512]{2,1,0:T(8,128)(2,1)S(1)}, f32[4,256,512]{2,1,0:T(8,128)S(1)}) custom-call(bf16[2,768,4096]{2,1,0:T(8,128)(2,1)} %x_ref.7, bf16[256,768]{1,0:T(8,128)(2,1)S(1)} %get-tuple-element.54.gt_ref, f32[2,256,512]{2,1,0:T(8,128)S(1)} %get-tuple-element.55.after.kept_ref), custom_call_target="tpu_custom_call" | custom-call | flops 805306368 | bytes 13500416 | tf_op jit(solution)/shard_map/fisher_of_own_tokens/pallas_call | solution.py:67
  25.1 1.1 fisher_of_both_cores.3
  26.2 1.9 %collective-permute-start.4 = (bf16[2,256,512]{2,1,0:T(8,128)(2,1)S(1)}, bf16[2,256,512]{2,1,0:T(8,128)(2,1)S(1)}, u32[]{:S(2)}, u32[]{:S(2)}) collective-permute-start(bf16[2,256,512]{2,1,0:T(8,128)(2,1)S(1)} %get-tuple-element.59), channel_id=1, source_target_pairs={{0,12},{2,14},{4,8},{6,10},{8,4},{10,6},{12,0},{14,2},{1,13},{3,15... | collective-permute-start | bytes 1572872 | tf_op jit(solution)/shard_map/ppermute | solution.py:317
  28.1 3.9 %collective-permute-start.13 = (bf16[2,1024,256]{2,1,0:T(8,128)(2,1)S(1)}, bf16[2,1024,256]{2,1,0:T(8,128)(2,1)S(1)}, u32[]{:S(2)}, u32[]{:S(2)}) collective-permute-start(bf16[2,1024,256]{2,1,0:T(8,128)(2,1)S(1)} %copy-done), channel_id=1, source_target_pairs={{0,0},{1,2},{2,12},{3,14},{4,4},{5,6},{6,8},{7,10},{8,9},{9,11},{1... | collective-permute-start | bytes 3145736 | tf_op jit(solution)/shard_map/ppermute | solution.py:376
  32.0 2.0 %collective-permute-done.5.got_ref = bf16[2,256,512]{2,1,0:T(8,128)(2,1)S(1)} collective-permute-done((bf16[2,256,512]{2,1,0:T(8,128)(2,1)S(1)}, bf16[2,256,512]{2,1,0:T(8,128)(2,1)S(1)}, u32[]{:S(2)}, u32[]{:S(2)}) %collective-permute-start.5) | collective-permute-done | bytes 524320 | tf_op jit(solution)/shard_map/ppermute | solution.py:317
  34.0 0.7 fisher_over_first_swap.4
  34.8 5.3 %collective-permute-done.4.got_ref = bf16[2,256,512]{2,1,0:T(8,128)(2,1)S(1)} collective-permute-done((bf16[2,256,512]{2,1,0:T(8,128)(2,1)S(1)}, bf16[2,256,512]{2,1,0:T(8,128)(2,1)S(1)}, u32[]{:S(2)}, u32[]{:S(2)}) %collective-permute-start.4) | collective-permute-done | bytes 524320 | tf_op jit(solution)/shard_map/ppermute | solution.py:317
  40.0 0.7 fisher_over_first_swap.5
  40.8 1.9 %fisher_of_other_grads.2 = (bf16[2,256,512]{2,1,0:T(8,128)(2,1)S(1)}, f32[2,256,512]{2,1,0:T(8,128)S(1)}, bf16[256,768]{1,0:T(8,128)(2,1)S(1)}, bf16[256,768]{1,0:T(8,128)(2,1)S(1)}) custom-call(bf16[4,768,512]{2,1,0:T(8,128)(2,1)S(1)} %get-tuple-element.50.xa_ref, bf16[4,768,512]{2,1,0:T(8,128)(2,1)S(1)} %collective-permute-done.1.x_ref.xb_ref, ...), custom_call_target="tpu_custom_call" | custom-call | flops 1610612736 | bytes 7340032 | tf_op jit(solution)/shard_map/fisher_of_other_grads/pallas_call | solution.py:67
  42.8 1.9 %fisher_of_other_grads.3 = (bf16[2,256,512]{2,1,0:T(8,128)(2,1)S(1)}, f32[2,256,512]{2,1,0:T(8,128)S(1)}) custom-call(bf16[4,768,512]{2,1,0:T(8,128)(2,1)S(1)} %get-tuple-element.57.after.xa_ref, bf16[4,768,512]{2,1,0:T(8,128)(2,1)S(1)} %collective-permute-done.3.x_ref.xb_ref, bf16[256,768]{1,0:T(8,128)(2,1)S(1)} %get-tuple-element.67.gta_ref, ...), custom_call_target="tpu_custom_call" | custom-call | flops 1610612736 | bytes 7602176 | tf_op jit(solution)/shard_map/fisher_of_other_grads/pallas_call | solution.py:67
  44.7 1.9 %collective-permute-start.10 = (bf16[2,256,512]{2,1,0:T(8,128)(2,1)S(1)}, bf16[2,256,512]{2,1,0:T(8,128)(2,1)S(1)}, u32[]{:S(2)}, u32[]{:S(2)}) collective-permute-start(bf16[2,256,512]{2,1,0:T(8,128)(2,1)S(1)} %get-tuple-element.73), channel_id=1, source_target_pairs={{0,12},{2,14},{4,8},{6,10},{8,4},{10,6},{12,0},{14,2},{1,13},{3,15... | collective-permute-start | bytes 1572872 | tf_op jit(solution)/shard_map/ppermute | solution.py:317
  46.5 0.9 collective-permute-start.7
  47.7 21.6 %collective-permute-done.7.got_a = bf16[256,512]{1,0:T(8,128)(2,1)S(1)} collective-permute-done((bf16[256,512]{1,0:T(8,128)(2,1)S(1)}, bf16[256,512]{1,0:T(8,128)(2,1)S(1)}, u32[]{:S(2)}, u32[]{:S(2)}) %collective-permute-start.7) | collective-permute-done | bytes 262176 | tf_op jit(solution)/shard_map/ppermute | solution.py:321
  69.3 0.6 fisher_over_tokens.2
  69.9 0.5 collective-permute-start.12
  70.4 0.7 fisher_over_first_swap.6
  71.1 0.7 fisher_over_first_swap.7
  72.2 1.8 %collective-permute-start.9 = (bf16[256,512]{1,0:T(8,128)(2,1)S(1)}, bf16[256,512]{1,0:T(8,128)(2,1)S(1)}, u32[]{:S(2)}, u32[]{:S(2)}) collective-permute-start(bf16[256,512]{1,0:T(8,128)(2,1)S(1)} %get-tuple-element.72), channel_id=1, source_target_pairs={{0,12},{2,14},{4,8},{6,10},{8,4},{10,6},{12,0},{14,2},{1,13},{3,15... | collective-permute-start | bytes 786440 | tf_op jit(solution)/shard_map/ppermute | solution.py:321
  74.0 0.6 weigh_members.2
  74.6 6.3 %collective-permute-done.9.got_a = bf16[256,512]{1,0:T(8,128)(2,1)S(1)} collective-permute-done((bf16[256,512]{1,0:T(8,128)(2,1)S(1)}, bf16[256,512]{1,0:T(8,128)(2,1)S(1)}, u32[]{:S(2)}, u32[]{:S(2)}) %collective-permute-start.9) | collective-permute-done | bytes 262176 | tf_op jit(solution)/shard_map/ppermute | solution.py:321
  81.2 0.6 fisher_over_tokens.3
  81.8 1.6 %collective-permute-start.15 = (f32[256,512]{1,0:T(8,128)S(1)}, f32[256,512]{1,0:T(8,128)S(1)}, u32[]{:S(2)}, u32[]{:S(2)}) collective-permute-start(f32[256,512]{1,0:T(8,128)S(1)} %get-tuple-element.81), channel_id=1, source_target_pairs={{0,2},{2,0},{4,6},{6,4},{8,10},{10,8},{12,14},{14,12},{1,3},{3,1},... | collective-permute-start | bytes 1572872 | tf_op jit(solution)/shard_map/ppermute | solution.py:311
  83.4 1.6 %collective-permute-start.19 = (bf16[3,128,256]{2,1,0:T(8,128)(2,1)S(1)}, bf16[3,128,256]{2,1,0:T(8,128)(2,1)S(1)}, u32[]{:S(2)}, u32[]{:S(2)}) collective-permute-start(bf16[3,128,256]{2,1,0:T(8,128)(2,1)S(1)} %get-tuple-element.86), channel_id=1, source_target_pairs={{0,16},{16,32},{32,48},{48,0},{64,80},{80,96},{96,112},{112,64},{1... | collective-permute-start | bytes 589832 | tf_op jit(solution)/shard_map/ppermute | solution.py:332
  85.1 3.3 %collective-permute-start.20 = (bf16[3,128,256]{2,1,0:T(8,128)(2,1)S(1)}, bf16[3,128,256]{2,1,0:T(8,128)(2,1)S(1)}, u32[]{:S(2)}, u32[]{:S(2)}) collective-permute-start(bf16[3,128,256]{2,1,0:T(8,128)(2,1)S(1)} %get-tuple-element.87), channel_id=1, source_target_pairs={{0,32},{16,48},{32,0},{48,16},{64,96},{80,112},{96,64},{112,80},{1... | collective-permute-start | bytes 589832 | tf_op jit(solution)/shard_map/ppermute | solution.py:332
  88.4 0.7 collective-permute-start.21
  89.1 0.5 weigh_members.3
  89.7 0.8 collective-permute-start.16
  90.5 0.5 collective-permute-start.17
  90.9 1.5 %collective-permute-done.19.one = bf16[3,128,256]{2,1,0:T(8,128)(2,1)S(1)} collective-permute-done((bf16[3,128,256]{2,1,0:T(8,128)(2,1)S(1)}, bf16[3,128,256]{2,1,0:T(8,128)(2,1)S(1)}, u32[]{:S(2)}, u32[]{:S(2)}) %collective-permute-start.19) | collective-permute-done | bytes 196640 | tf_op jit(solution)/shard_map/ppermute | solution.py:332
  92.4 1.3 %collective-permute-start.18 = (bf16[3,128,256]{2,1,0:T(8,128)(2,1)S(1)}, bf16[3,128,256]{2,1,0:T(8,128)(2,1)S(1)}, u32[]{:S(2)}, u32[]{:S(2)}) collective-permute-start(bf16[3,128,256]{2,1,0:T(8,128)(2,1)S(1)} %get-tuple-element.84), channel_id=1, source_target_pairs={{0,48},{16,0},{32,16},{48,32},{64,112},{80,64},{96,80},{112,96},{1... | collective-permute-start | bytes 589832 | tf_op jit(solution)/shard_map/ppermute | solution.py:332
  93.7 4.0 %collective-permute-done.20.two = bf16[3,128,256]{2,1,0:T(8,128)(2,1)S(1)} collective-permute-done((bf16[3,128,256]{2,1,0:T(8,128)(2,1)S(1)}, bf16[3,128,256]{2,1,0:T(8,128)(2,1)S(1)}, u32[]{:S(2)}, u32[]{:S(2)}) %collective-permute-start.20) | collective-permute-done | bytes 196640 | tf_op jit(solution)/shard_map/ppermute | solution.py:332
  98.0 3.5 %collective-permute-done.16.one = bf16[3,128,256]{2,1,0:T(8,128)(2,1)S(1)} collective-permute-done((bf16[3,128,256]{2,1,0:T(8,128)(2,1)S(1)}, bf16[3,128,256]{2,1,0:T(8,128)(2,1)S(1)}, u32[]{:S(2)}, u32[]{:S(2)}) %collective-permute-start.16) | collective-permute-done | bytes 196640 | tf_op jit(solution)/shard_map/ppermute | solution.py:332
  101.5 4.6 %collective-permute-done.17.two = bf16[3,128,256]{2,1,0:T(8,128)(2,1)S(1)} collective-permute-done((bf16[3,128,256]{2,1,0:T(8,128)(2,1)S(1)}, bf16[3,128,256]{2,1,0:T(8,128)(2,1)S(1)}, u32[]{:S(2)}, u32[]{:S(2)}) %collective-permute-start.17) | collective-permute-done | bytes 196640 | tf_op jit(solution)/shard_map/ppermute | solution.py:332
  106.1 0.3 sum_over_z.3
  106.4 3.0 %collective-permute-start.22 = (bf16[3,128,256]{2,1,0:T(8,128)(2,1)S(1)}, bf16[3,128,256]{2,1,0:T(8,128)(2,1)S(1)}, u32[]{:S(2)}, u32[]{:S(2)}) collective-permute-start(bf16[3,128,256]{2,1,0:T(8,128)(2,1)S(1)} %get-tuple-element.89), channel_id=1, source_target_pairs={{0,0},{1,15},{2,64},{3,79},{4,4},{5,11},{6,68},{7,75},{8,6},{9,9},... | collective-permute-start | bytes 589832 | tf_op jit(solution)/shard_map/ppermute | solution.py:387
  109.5 2.8 %collective-permute-start.23 = (bf16[3,128,256]{2,1,0:T(8,128)(2,1)S(1)}, bf16[3,128,256]{2,1,0:T(8,128)(2,1)S(1)}, u32[]{:S(2)}, u32[]{:S(2)}) collective-permute-start(bf16[3,128,256]{2,1,0:T(8,128)(2,1)S(1)} %get-tuple-element.90), channel_id=1, source_target_pairs={{0,1},{1,14},{2,65},{3,78},{4,5},{5,10},{6,69},{7,74},{8,7},{9,8},... | collective-permute-start | bytes 589832 | tf_op jit(solution)/shard_map/ppermute | solution.py:388
  112.3 4.3 %collective-permute-done.22.near = bf16[3,128,256]{2,1,0:T(8,128)(2,1)S(1)} collective-permute-done((bf16[3,128,256]{2,1,0:T(8,128)(2,1)S(1)}, bf16[3,128,256]{2,1,0:T(8,128)(2,1)S(1)}, u32[]{:S(2)}, u32[]{:S(2)}) %collective-permute-start.22) | collective-permute-done | bytes 196640 | tf_op jit(solution)/shard_map/ppermute | solution.py:387
  116.6 3.2 %collective-permute-done.23.far = bf16[3,128,256]{2,1,0:T(8,128)(2,1)S(1)} collective-permute-done((bf16[3,128,256]{2,1,0:T(8,128)(2,1)S(1)}, bf16[3,128,256]{2,1,0:T(8,128)(2,1)S(1)}, u32[]{:S(2)}, u32[]{:S(2)}) %collective-permute-start.23) | collective-permute-done | bytes 196640 | tf_op jit(solution)/shard_map/ppermute | solution.py:388
  119.9 0.8 merge_members.1
  (23 shorter events, 1.5 us)
Async XLA Ops:
  2.2 17.8 %collective-permute-start.1 = (bf16[4,768,512]{2,1,0:T(8,128)(2,1)S(1)}, bf16[4,768,512]{2,1,0:T(8,128)(2,1)S(1)}, u32[]{:S(2)}, u32[]{:S(2)}) collective-permute-start(bf16[4,768,512]{2,1,0:T(8,128)(2,1)S(1)} %get-tuple-element.51), channel_id=1, source_target_pairs={{0,2},{2,0},{4,6},{6,4},{8,10},{10,8},{12,14},{14,12},{1,3},{3,1},... | collective-permute-start | bytes 9437192 | tf_op jit(solution)/shard_map/ppermute | solution.py:311
  5.6 19.5 %collective-permute-start.3 = (bf16[4,768,512]{2,1,0:T(8,128)(2,1)S(1)}, bf16[4,768,512]{2,1,0:T(8,128)(2,1)S(1)}, u32[]{:S(2)}, u32[]{:S(2)}) collective-permute-start(bf16[4,768,512]{2,1,0:T(8,128)(2,1)S(1)} %load_to_swap.3.after), channel_id=1, source_target_pairs={{0,2},{2,0},{4,6},{6,4},{8,10},{10,8},{12,14},{14,12},{1,3},{3,1},... | collective-permute-start | bytes 9437192 | tf_op jit(solution)/shard_map/ppermute | solution.py:311
  5.7 8.3 %collective-permute-start = (bf16[768,256]{1,0:T(8,128)(2,1)S(1)}, bf16[768,256]{1,0:T(8,128)(2,1)S(1)}, u32[]{:S(2)}, u32[]{:S(2)}) collective-permute-start(bf16[768,256]{1,0:T(8,128)(2,1)S(1)} %get-tuple-element.49), channel_id=1, source_target_pairs={{0,2},{2,0},{4,6},{6,4},{8,10},{10,8},{12,14},{14,12},{1,3},{3,1},... | collective-permute-start | bytes 1179656 | tf_op jit(solution)/shard_map/ppermute | solution.py:311
  14.1 26.7 %collective-permute-start.2 = (bf16[2,768,256]{2,1,0:T(8,128)(2,1)S(1)}, bf16[2,768,256]{2,1,0:T(8,128)(2,1)S(1)}, u32[]{:S(2)}, u32[]{:S(2)}) collective-permute-start(bf16[2,768,256]{2,1,0:T(8,128)(2,1)S(1)} %pair_grads.1.after), channel_id=1, source_target_pairs={{0,1},{1,0},{2,3},{3,2},{4,5},{5,4},{6,7},{7,6},{8,9},{9,8},{10,11... | collective-permute-start | bytes 2359304 | tf_op jit(solution)/shard_map/ppermute | solution.py:314
  21.1 12.9 %collective-permute-start.5 = (bf16[2,256,512]{2,1,0:T(8,128)(2,1)S(1)}, bf16[2,256,512]{2,1,0:T(8,128)(2,1)S(1)}, u32[]{:S(2)}, u32[]{:S(2)}) collective-permute-start(bf16[2,256,512]{2,1,0:T(8,128)(2,1)S(1)} %get-tuple-element.60), channel_id=1, source_target_pairs={{0,4},{2,6},{4,0},{6,2},{8,12},{10,14},{12,8},{14,10},{1,5},{3,7},... | collective-permute-start | bytes 1572872 | tf_op jit(solution)/shard_map/ppermute | solution.py:317
  25.1 3.0 %copy-start = (bf16[2,1024,256]{2,1,0:T(8,128)(2,1)S(1)}, bf16[2,1024,256]{2,1,0:T(8,128)(2,1)}, u32[]{:S(2)}) copy-start(bf16[2,1024,256]{2,1,0:T(8,128)(2,1)} %param.5) | copy-start | bytes 3145732
  26.2 13.8 %collective-permute-start.4 = (bf16[2,256,512]{2,1,0:T(8,128)(2,1)S(1)}, bf16[2,256,512]{2,1,0:T(8,128)(2,1)S(1)}, u32[]{:S(2)}, u32[]{:S(2)}) collective-permute-start(bf16[2,256,512]{2,1,0:T(8,128)(2,1)S(1)} %get-tuple-element.59), channel_id=1, source_target_pairs={{0,12},{2,14},{4,8},{6,10},{8,4},{10,6},{12,0},{14,2},{1,13},{3,15... | collective-permute-start | bytes 1572872 | tf_op jit(solution)/shard_map/ppermute | solution.py:317
  28.1 43.8 %collective-permute-start.13 = (bf16[2,1024,256]{2,1,0:T(8,128)(2,1)S(1)}, bf16[2,1024,256]{2,1,0:T(8,128)(2,1)S(1)}, u32[]{:S(2)}, u32[]{:S(2)}) collective-permute-start(bf16[2,1024,256]{2,1,0:T(8,128)(2,1)S(1)} %copy-done), channel_id=1, source_target_pairs={{0,0},{1,2},{2,12},{3,14},{4,4},{5,6},{6,8},{7,10},{8,9},{9,11},{1... | collective-permute-start | bytes 3145736 | tf_op jit(solution)/shard_map/ppermute | solution.py:376
  42.7 27.7 %collective-permute-start.6 = (bf16[2,256,512]{2,1,0:T(8,128)(2,1)S(1)}, bf16[2,256,512]{2,1,0:T(8,128)(2,1)S(1)}, u32[]{:S(2)}, u32[]{:S(2)}) collective-permute-start(bf16[2,256,512]{2,1,0:T(8,128)(2,1)S(1)} %get-tuple-element.64), channel_id=1, source_target_pairs={{0,4},{2,6},{4,0},{6,2},{8,12},{10,14},{12,8},{14,10},{1,5},{3,7},... | collective-permute-start | bytes 1572872 | tf_op jit(solution)/shard_map/ppermute | solution.py:317
  44.7 26.5 %collective-permute-start.10 = (bf16[2,256,512]{2,1,0:T(8,128)(2,1)S(1)}, bf16[2,256,512]{2,1,0:T(8,128)(2,1)S(1)}, u32[]{:S(2)}, u32[]{:S(2)}) collective-permute-start(bf16[2,256,512]{2,1,0:T(8,128)(2,1)S(1)} %get-tuple-element.73), channel_id=1, source_target_pairs={{0,12},{2,14},{4,8},{6,10},{8,4},{10,6},{12,0},{14,2},{1,13},{3,15... | collective-permute-start | bytes 1572872 | tf_op jit(solution)/shard_map/ppermute | solution.py:317
  46.5 22.8 %collective-permute-start.7 = (bf16[256,512]{1,0:T(8,128)(2,1)S(1)}, bf16[256,512]{1,0:T(8,128)(2,1)S(1)}, u32[]{:S(2)}, u32[]{:S(2)}) collective-permute-start(bf16[256,512]{1,0:T(8,128)(2,1)S(1)} %get-tuple-element.65), channel_id=1, source_target_pairs={{0,12},{2,14},{4,8},{6,10},{8,4},{10,6},{12,0},{14,2},{1,13},{3,15... | collective-permute-start | bytes 786440 | tf_op jit(solution)/shard_map/ppermute | solution.py:321
  47.4 21.9 %collective-permute-start.8 = (bf16[256,512]{1,0:T(8,128)(2,1)S(1)}, bf16[256,512]{1,0:T(8,128)(2,1)S(1)}, u32[]{:S(2)}, u32[]{:S(2)}) collective-permute-start(bf16[256,512]{1,0:T(8,128)(2,1)S(1)} %get-tuple-element.66), channel_id=1, source_target_pairs={{0,4},{2,6},{4,0},{6,2},{8,12},{10,14},{12,8},{14,10},{1,5},{3,7},... | collective-permute-start | bytes 786440 | tf_op jit(solution)/shard_map/ppermute | solution.py:321
  69.9 4.1 %collective-permute-start.12 = (f32[256,512]{1,0:T(8,128)S(1)}, f32[256,512]{1,0:T(8,128)S(1)}, u32[]{:S(2)}, u32[]{:S(2)}) collective-permute-start(f32[256,512]{1,0:T(8,128)S(1)} %get-tuple-element.76), channel_id=1, source_target_pairs={{0,2},{2,0},{4,6},{6,4},{8,10},{10,8},{12,14},{14,12},{1,3},{3,1},... | collective-permute-start | bytes 1572872 | tf_op jit(solution)/shard_map/ppermute | solution.py:311
  72.0 2.0 %collective-permute-start.14 = (bf16[2,512,256]{2,1,0:T(8,128)(2,1)S(1)}, bf16[2,512,256]{2,1,0:T(8,128)(2,1)S(1)}, u32[]{:S(2)}, u32[]{:S(2)}) collective-permute-start(bf16[2,512,256]{2,1,0:T(8,128)(2,1)S(1)} %get-tuple-element.78), channel_id=1, source_target_pairs={{0,2},{2,0},{4,6},{6,4},{8,10},{10,8},{12,14},{14,12},{1,3},{3,1},... | collective-permute-start | bytes 1572872 | tf_op jit(solution)/shard_map/ppermute | solution.py:311
  72.2 8.7 %collective-permute-start.9 = (bf16[256,512]{1,0:T(8,128)(2,1)S(1)}, bf16[256,512]{1,0:T(8,128)(2,1)S(1)}, u32[]{:S(2)}, u32[]{:S(2)}) collective-permute-start(bf16[256,512]{1,0:T(8,128)(2,1)S(1)} %get-tuple-element.72), channel_id=1, source_target_pairs={{0,12},{2,14},{4,8},{6,10},{8,4},{10,6},{12,0},{14,2},{1,13},{3,15... | collective-permute-start | bytes 786440 | tf_op jit(solution)/shard_map/ppermute | solution.py:321
  74.0 7.2 %collective-permute-start.11 = (bf16[256,512]{1,0:T(8,128)(2,1)S(1)}, bf16[256,512]{1,0:T(8,128)(2,1)S(1)}, u32[]{:S(2)}, u32[]{:S(2)}) collective-permute-start(bf16[256,512]{1,0:T(8,128)(2,1)S(1)} %get-tuple-element.75), channel_id=1, source_target_pairs={{0,4},{2,6},{4,0},{6,2},{8,12},{10,14},{12,8},{14,10},{1,5},{3,7},... | collective-permute-start | bytes 786440 | tf_op jit(solution)/shard_map/ppermute | solution.py:321
  81.8 7.3 %collective-permute-start.15 = (f32[256,512]{1,0:T(8,128)S(1)}, f32[256,512]{1,0:T(8,128)S(1)}, u32[]{:S(2)}, u32[]{:S(2)}) collective-permute-start(f32[256,512]{1,0:T(8,128)S(1)} %get-tuple-element.81), channel_id=1, source_target_pairs={{0,2},{2,0},{4,6},{6,4},{8,10},{10,8},{12,14},{14,12},{1,3},{3,1},... | collective-permute-start | bytes 1572872 | tf_op jit(solution)/shard_map/ppermute | solution.py:311
  83.4 8.9 %collective-permute-start.19 = (bf16[3,128,256]{2,1,0:T(8,128)(2,1)S(1)}, bf16[3,128,256]{2,1,0:T(8,128)(2,1)S(1)}, u32[]{:S(2)}, u32[]{:S(2)}) collective-permute-start(bf16[3,128,256]{2,1,0:T(8,128)(2,1)S(1)} %get-tuple-element.86), channel_id=1, source_target_pairs={{0,16},{16,32},{32,48},{48,0},{64,80},{80,96},{96,112},{112,64},{1... | collective-permute-start | bytes 589832 | tf_op jit(solution)/shard_map/ppermute | solution.py:332
  85.1 12.6 %collective-permute-start.20 = (bf16[3,128,256]{2,1,0:T(8,128)(2,1)S(1)}, bf16[3,128,256]{2,1,0:T(8,128)(2,1)S(1)}, u32[]{:S(2)}, u32[]{:S(2)}) collective-permute-start(bf16[3,128,256]{2,1,0:T(8,128)(2,1)S(1)} %get-tuple-element.87), channel_id=1, source_target_pairs={{0,32},{16,48},{32,0},{48,16},{64,96},{80,112},{96,64},{112,80},{1... | collective-permute-start | bytes 589832 | tf_op jit(solution)/shard_map/ppermute | solution.py:332
  88.4 9.3 %collective-permute-start.21 = (bf16[3,128,256]{2,1,0:T(8,128)(2,1)S(1)}, bf16[3,128,256]{2,1,0:T(8,128)(2,1)S(1)}, u32[]{:S(2)}, u32[]{:S(2)}) collective-permute-start(bf16[3,128,256]{2,1,0:T(8,128)(2,1)S(1)} %get-tuple-element.88), channel_id=1, source_target_pairs={{0,48},{16,0},{32,16},{48,32},{64,112},{80,64},{96,80},{112,96},{1... | collective-permute-start | bytes 589832 | tf_op jit(solution)/shard_map/ppermute | solution.py:332
  89.7 11.8 %collective-permute-start.16 = (bf16[3,128,256]{2,1,0:T(8,128)(2,1)S(1)}, bf16[3,128,256]{2,1,0:T(8,128)(2,1)S(1)}, u32[]{:S(2)}, u32[]{:S(2)}) collective-permute-start(bf16[3,128,256]{2,1,0:T(8,128)(2,1)S(1)} %get-tuple-element.82), channel_id=1, source_target_pairs={{0,16},{16,32},{32,48},{48,0},{64,80},{80,96},{96,112},{112,64},{1... | collective-permute-start | bytes 589832 | tf_op jit(solution)/shard_map/ppermute | solution.py:332
  90.5 15.6 %collective-permute-start.17 = (bf16[3,128,256]{2,1,0:T(8,128)(2,1)S(1)}, bf16[3,128,256]{2,1,0:T(8,128)(2,1)S(1)}, u32[]{:S(2)}, u32[]{:S(2)}) collective-permute-start(bf16[3,128,256]{2,1,0:T(8,128)(2,1)S(1)} %get-tuple-element.83), channel_id=1, source_target_pairs={{0,32},{16,48},{32,0},{48,16},{64,96},{80,112},{96,64},{112,80},{1... | collective-permute-start | bytes 589832 | tf_op jit(solution)/shard_map/ppermute | solution.py:332
  92.4 13.7 %collective-permute-start.18 = (bf16[3,128,256]{2,1,0:T(8,128)(2,1)S(1)}, bf16[3,128,256]{2,1,0:T(8,128)(2,1)S(1)}, u32[]{:S(2)}, u32[]{:S(2)}) collective-permute-start(bf16[3,128,256]{2,1,0:T(8,128)(2,1)S(1)} %get-tuple-element.84), channel_id=1, source_target_pairs={{0,48},{16,0},{32,16},{48,32},{64,112},{80,64},{96,80},{112,96},{1... | collective-permute-start | bytes 589832 | tf_op jit(solution)/shard_map/ppermute | solution.py:332
  106.4 10.2 %collective-permute-start.22 = (bf16[3,128,256]{2,1,0:T(8,128)(2,1)S(1)}, bf16[3,128,256]{2,1,0:T(8,128)(2,1)S(1)}, u32[]{:S(2)}, u32[]{:S(2)}) collective-permute-start(bf16[3,128,256]{2,1,0:T(8,128)(2,1)S(1)} %get-tuple-element.89), channel_id=1, source_target_pairs={{0,0},{1,15},{2,64},{3,79},{4,4},{5,11},{6,68},{7,75},{8,6},{9,9},... | collective-permute-start | bytes 589832 | tf_op jit(solution)/shard_map/ppermute | solution.py:387
  109.5 10.4 %collective-permute-start.23 = (bf16[3,128,256]{2,1,0:T(8,128)(2,1)S(1)}, bf16[3,128,256]{2,1,0:T(8,128)(2,1)S(1)}, u32[]{:S(2)}, u32[]{:S(2)}) collective-permute-start(bf16[3,128,256]{2,1,0:T(8,128)(2,1)S(1)} %get-tuple-element.90), channel_id=1, source_target_pairs={{0,1},{1,14},{2,65},{3,78},{4,5},{5,10},{6,69},{7,74},{8,7},{9,8},... | collective-permute-start | bytes 589832 | tf_op jit(solution)/shard_map/ppermute | solution.py:388

commit v5 on v4

--- a/solution.py
+++ b/solution.py
@@ -19,7 +19,8 @@
 
 X, CORES, Z = 4, 2, 4
 
-ORDERS = ((1, 2, 0, 3), (3, 2, 0, 1))
+ORDER = (1, 2, 0, 3)
+BACK = (3, 1, 2, 0)
 
 
 def code_of(values):
@@ -63,7 +64,6 @@
 def call(kernel, name, outs, hbm, vmem, scratch=(), flops=0):
     single = not isinstance(outs, list)
     shapes = [pltpu.VMEM(shape, kind) for shape, kind in ([outs] if single else outs)]
-    moved = sum(a.size * 2 for a in vmem) + sum(a.size * 2 for a in hbm)
     result = pl.pallas_call(
         kernel,
         out_shape=shapes,
@@ -71,7 +71,7 @@
         out_specs=[VMEM] * len(shapes),
         scratch_shapes=list(scratch),
         compiler_params=pltpu.CompilerParams(vmem_limit_bytes=VMEM_LIMIT),
-        cost_estimate=pl.CostEstimate(flops=flops, bytes_accessed=moved, transcendentals=0),
+        cost_estimate=pl.CostEstimate(flops=1, bytes_accessed=1, transcendentals=0),
         name=name,
     )(*[in_hbm(a) for a in hbm], *[in_vmem(a) for a in vmem])
     return result[0] if single else result
@@ -101,22 +101,37 @@
 def load_inputs(member, part, x_ref, x_out, sem):
     wide = x_out.shape[2]
     copies = []
-    for s, flip in enumerate(ORDERS[part]):
+    for s, flip in enumerate(ORDER):
         at = pl.multiple_of(column_block(flip, part) * wide, wide)
         copies.append(pltpu.make_async_copy(x_ref.at[member, :, pl.ds(at, wide)], x_out.at[s], sem.at[s]))
         copies[s].start()
     return copies
 
 
-def load_first_kernel(x_ref, g_ref, x_out, g_out, g_own_out, sem, g_sem):
+def load_grads_kernel(g_ref, g_out, g_own_out, sem):
     core = where_am_i()[1]
     loads = [
-        pltpu.make_async_copy(g_ref.at[1 - core], g_out, g_sem.at[0]),
-        pltpu.make_async_copy(g_ref.at[core], g_own_out, g_sem.at[1]),
+        pltpu.make_async_copy(g_ref, g_out.at[:, pl.ds(0, g_ref.shape[1])], sem.at[0]),
+        pltpu.make_async_copy(g_ref.at[core], g_own_out, sem.at[1]),
     ]
     for copy in loads:
         copy.start()
-    for copy in load_inputs(1 - core, 0, x_ref, x_out, sem) + loads:
+    for copy in loads:
+        copy.wait()
+
+
+def load_first_kernel(x_ref, g_ref, after, out, sem, g_sem):
+    core = where_am_i()[1]
+    wide = x_ref.shape[2] // 8
+    copies = [pltpu.make_async_copy(g_ref.at[1 - core], out.at[:, pl.ds(4 * wide, g_ref.shape[2])], g_sem)]
+    for s, flip in enumerate(ORDER):
+        at = pl.multiple_of(column_block(flip, 0) * wide, wide)
+        copies.append(
+            pltpu.make_async_copy(x_ref.at[1 - core, :, pl.ds(at, wide)], out.at[:, pl.ds(s * wide, wide)], sem.at[s])
+        )
+    for copy in copies:
+        copy.start()
+    for copy in copies:
         copy.wait()
 
 
@@ -125,8 +140,11 @@
         copy.wait()
 
 
-def pair_kernel(own, got, after, out):
-    out[0], out[1] = own[...], got[...]
+def pick_grads_kernel(g_ref, after, kept_out, sent_out):
+    core = where_am_i()[1]
+    rows = kept_out.shape[0]
+    kept_out[...] = g_ref[core, :rows]
+    sent_out[...] = g_ref[1 - core, :rows]
 
 
 def own_tokens(copies, x_out, gt_ref, part_out):
@@ -153,10 +171,12 @@
         kept_out[s - 2] = block
 
 
-def add_first_kernel(x_ref, g_ref, part_ref, sent_out, kept_out, gt_out):
-    gt_out[...] = squared_transposed(g_ref[...])
+def add_first_kernel(x_ref, part_ref, sent_out, kept_out, gt_out):
+    wide = part_ref.shape[2]
+    gt_out[...] = squared_transposed(x_ref[:, 4 * wide :])
     for s in range(4):
-        put(s, part_ref[s] + fisher_block(x_ref[s], gt_out), sent_out, kept_out)
+        block = fisher_block(x_ref[:, s * wide : (s + 1) * wide], gt_out)
+        put(s, part_ref[s] + block, sent_out, kept_out)
 
 
 def add_second_kernel(x_ref, gt_ref, part_ref, after, sent_out, kept_out):
@@ -164,16 +184,18 @@
         put(s, part_ref[s] + fisher_block(x_ref[s], gt_ref), sent_out, kept_out)
 
 
-def both_first_kernel(xa_ref, xb_ref, g_ref, after, sent_out, kept_out, gta_out, gtb_out):
-    gta_out[...] = squared_transposed(g_ref[0])
-    gtb_out[...] = squared_transposed(g_ref[1])
+def both_first_kernel(xa_ref, xb_ref, ga_ref, gb_ref, after, sent_out, kept_out, gta_out, gtb_out):
+    wide = kept_out.shape[2]
+    gta_out[...] = squared_transposed(ga_ref[...])
+    gtb_out[...] = squared_transposed(gb_ref[...])
     for s in range(4):
-        put(s, fisher_block(xa_ref[s], gta_out) + fisher_block(xb_ref[s], gtb_out), sent_out, kept_out)
+        block = fisher_block(xb_ref[:, s * wide : (s + 1) * wide], gtb_out)
+        put(s, fisher_block(xa_ref[s], gta_out) + block, sent_out, kept_out)
 
 
 def both_second_kernel(xa_ref, xb_ref, gta_ref, gtb_ref, after, sent_out, kept_out):
-    for s in range(4):
-        put(s, fisher_block(xa_ref[s], gta_ref) + fisher_block(xb_ref[s], gtb_ref), sent_out, kept_out)
+    for s, block in enumerate(BACK):
+        put(s, fisher_block(xa_ref[block], gta_ref) + fisher_block(xb_ref[block], gtb_ref), sent_out, kept_out)
 
 
 def middle_kernel(kept_ref, got_ref, after, sent_out, own_out):
@@ -181,9 +203,13 @@
     own_out[...] = kept_ref[0] + decode(got_ref[0])
 
 
-def join_kernel(own_a, got_a, own_b, got_b, after, kept_out, sent_out):
-    first = own_a[...] + decode_fine(got_a[...])
-    second = own_b[...] + decode_fine(got_b[...])
+def settle_kernel(own, got, out):
+    out[...] = own[...] + decode_fine(got[...])
+
+
+def join_kernel(first_ref, own, got, after, kept_out, sent_out):
+    first = first_ref[...]
+    second = own[...] + decode_fine(got[...])
     core = where_am_i()[1]
     kept_out[...] = jnp.where(core == 0, first, second)
     sent_out[...] = jnp.where(core == 0, second, first)
@@ -237,24 +263,14 @@
     to_words(*over_z(sums, (one, two, three)), out)
 
 
-def sum_last_kernel(one, two, three, sums, first, near_out, far_out):
-    y_lo = where_am_i()[3]
-
-    @pl.when(y_lo == 0)
-    def _():
-        to_words(*over_z(sums, (one, two, three)), far_out)
-        near_out[...] = first[...]
-
-    @pl.when(y_lo != 0)
-    def _():
-        to_words(*over_z(sums, (one, two, three)), near_out)
-        far_out[...] = first[...]
-
-
-def merge_kernel(near, far, out):
-    weighted, total = from_words(near)
-    more, added = from_words(far)
-    out[...] = (weighted + more) / (total + added)
+def meet_kernel(near, far, after, out):
+    (weighted, total), (more, added) = from_words(near), from_words(far)
+    out[0], out[1] = weighted + more, total + added
+
+
+def merge_kernel(near, far, sums, out):
+    (weighted, total), (more, added) = from_words(near), from_words(far)
+    out[...] = (weighted + more + sums[0]) / (total + added + sums[1])
 
 
 def keeper(local, half):
@@ -275,17 +291,15 @@
     return pairs
 
 
-def result_pairs(flip):
+def result_pairs(phase, sender):
     pairs = []
-    for member in range(8):
-        y_lo, z = divmod(member, 4)
-        for tok in range(8):
+    for z in range(Z):
+        for tok in range(X * CORES):
             x, core = divmod(tok, 2)
             for half in range(2):
-                to_member = core * 4 + z
                 to_tok = 4 * half + kept(x, half)
-                to_col = half ^ y_lo ^ flip
-                pairs.append(((member * 8 + tok) * 2 + half, (to_member * 8 + to_tok) * 2 + to_col))
+                to = ((core * Z + z) * 8 + to_tok) * 2 + (half ^ phase)
+                pairs.append((((sender * Z + z) * 8 + tok) * 2 + half, to))
     return pairs
 
 
@@ -313,16 +327,22 @@
     def swap_cols(send):
         return lax.ppermute(send, "col", [(0, 1), (1, 0)])
 
-    def first_swap(part, sent):
-        return lax.ppermute(sent, "tok", x_pairs(ORDERS[part][0]))
-
-    def middle(part, got, kept_blocks, after):
+    def swap_x(flip, sent):
+        return lax.ppermute(sent, "tok", x_pairs(flip))
+
+    def middle(flip, got, kept_blocks, after):
         sent, own = call(middle_kernel, "fisher_over_first_swap", [code_shape, own_shape], [], [kept_blocks, got, after])
-        return own, lax.ppermute(sent, "tok", x_pairs(ORDERS[part][3]))
-
-    def join(one, two, after):
-        kept_block, sent = call(join_kernel, "fisher_over_tokens", [own_shape, own_shape], [], [*one, *two, after])
+        return own, swap_x(flip, sent)
+
+    def settle(one):
+        return call(settle_kernel, "fisher_over_tokens", own_shape, [], [*one])
+
+    def join(first, two, after):
+        kept_block, sent = call(join_kernel, "fisher_over_tokens", [own_shape, own_shape], [], [first, *two, after])
         return kept_block, swap_cores(sent)
+
+    def results(phase, sums):
+        return [lax.ppermute(sums, ("member", "tok", "col"), result_pairs(phase, y_lo)) for y_lo in range(2)]
 
     def weigh(phase, own, other, after):
         one, two, three, own_sums = call(
@@ -331,69 +351,70 @@
         send = ((1, one), (2, two), (3, three))
         return [lax.ppermute(v, "member", z_pairs(d)) for d, v in send] + [own_sums]
 
-    x_send0, g_send, g_own = call(
-        load_first_kernel, "load_to_swap", [x_shape, g_shape, g_shape], [inputs, grads], [], [dma((4,)), dma((2,))]
+    g_pair, g_own = call(
+        load_grads_kernel, "load_grads", [((2, tokens + 64, outs), BF16), g_shape], [grads], [], [dma((2,))]
+    )
+    g_other = swap_cols(g_pair)
+    x_send0 = call(
+        load_first_kernel, "load_to_swap", ((tokens, 4 * wide + outs), BF16), [inputs, grads], [g_own], [dma((4,)), dma]
     )
     x_got0 = swap_cores(x_send0)
-    g_got = swap_cores(g_send)
-    x_send1 = call(load_second_kernel, "load_to_swap", x_shape, [inputs], [g_own], [dma((4,))])
+    x_send1 = call(load_second_kernel, "load_to_swap", x_shape, [inputs], [x_send0], [dma((4,))])
     x_got1 = swap_cores(x_send1)
-    g_pair = call(pair_kernel, "pair_grads", ((2, tokens, outs), BF16), [], [g_own, g_got, x_send1])
-    g_other = swap_cols(g_pair)
 
     x_own0, gt_own, part0 = call(
-        own_first_kernel, "fisher_of_own_tokens", [x_shape, gt_shape, part_shape], [inputs], [g_own, g_pair],
+        own_first_kernel, "fisher_of_own_tokens", [x_shape, gt_shape, part_shape], [inputs], [g_own, x_send1],
         [dma((4,))], flops,
     )
     sent, kept00, gt_got = call(
-        add_first_kernel, "fisher_of_both_cores", [sent_shape, kept_shape, gt_shape], [], [x_got0, g_got, part0], flops=flops
-    )
-    swap00 = first_swap(0, sent)
+        add_first_kernel, "fisher_of_both_cores", [sent_shape, kept_shape, gt_shape], [], [x_got0, part0], flops=flops
+    )
+    swap00 = swap_x(1, sent)
     x_own1, part1 = call(
         own_second_kernel, "fisher_of_own_tokens", [x_shape, part_shape], [inputs], [gt_own, kept00], [dma((4,))], flops
     )
     sent, kept01 = call(
         add_second_kernel, "fisher_of_both_cores", [sent_shape, kept_shape], [], [x_got1, gt_got, part1, x_own1], flops=flops
     )
-    swap01 = first_swap(1, sent)
-    part00 = middle(0, swap00, kept00, kept01)
-    part01 = middle(1, swap01, kept01, part00[0])
-
+    swap01 = swap_x(1, sent)
+    settled0 = settle(middle(3, swap00, kept00, kept01))
+    part01 = middle(3, swap01, kept01, settled0)
+
+    arrived = lax.ppermute(weights, ("tok", "col"), weight_pairs())
+    rows = weights.shape[1] // 2
+    w_own, w_send = call(split_kernel, "split_weights", [((2, rows, outs), BF16)] * 2, [], [arrived, part01[0]])
+    moved = (w_own, swap_cores(w_send))
+
+    g_kept, g_sent = call(pick_grads_kernel, "pick_grads", [g_shape, g_shape], [], [g_other, part01[0]])
     sent, kept10, gt_own, gt_got = call(
         both_first_kernel, "fisher_of_other_grads", [sent_shape, kept_shape, gt_shape, gt_shape], [],
-        [x_own0, x_got0, g_other, part01[0]], flops=2 * flops,
-    )
-    swap10 = first_swap(0, sent)
+        [x_own0, x_got0, g_kept, swap_cores(g_sent), w_own], flops=2 * flops,
+    )
+    swap10 = swap_x(1, sent)
     sent, kept11 = call(
         both_second_kernel, "fisher_of_other_grads", [sent_shape, kept_shape], [],
         [x_own1, x_got1, gt_own, gt_got, kept10], flops=2 * flops,
     )
-    swap11 = first_swap(1, sent)
-    own0, other0 = join(part00, part01, kept11)
-    part10 = middle(0, swap10, kept10, own0)
+    swap11 = swap_x(3, sent)
+    own0, other0 = join(settled0, part01, kept11)
+    part10 = middle(3, swap10, kept10, own0)
     part11 = middle(1, swap11, kept11, part10[0])
 
-    arrived = lax.ppermute(weights, ("tok", "col"), weight_pairs())
-    rows = weights.shape[1] // 2
-    w_own, w_send = call(split_kernel, "split_weights", [((2, rows, outs), BF16)] * 2, [], [arrived, part11[0]])
-    moved = (w_own, swap_cores(w_send))
-    words0 = weigh(0, own0, other0, w_own)
-    own1, other1 = join(part10, part11, words0[3])
+    words0 = weigh(0, own0, other0, part11[0])
+    first = call(sum_kernel, "sum_over_z", words, [], words0)
+    own1, other1 = join(settle(part10), part11, first)
     words1 = weigh(1, own1, other1, own1)
-    first = call(sum_kernel, "sum_over_z", words, [], words0)
-    near, far = call(sum_last_kernel, "sum_over_z", [words, words], [], [*words1, first])
-
-    names = ("member", "tok", "col")
-    near = lax.ppermute(near, names, result_pairs(0))
-    far = lax.ppermute(far, names, result_pairs(1))
+    met = call(meet_kernel, "meet_over_y", sums, [], [*results(0, first), own1])
+    second = call(sum_kernel, "sum_over_z", words, [], [*words1])
+    near, far = results(1, second)
     return pl.pallas_call(
         merge_kernel,
         out_shape=jax.ShapeDtypeStruct((wide // Z, outs), F32),
-        in_specs=[VMEM, VMEM],
+        in_specs=[VMEM] * 3,
         out_specs=VMEM,
         compiler_params=pltpu.CompilerParams(vmem_limit_bytes=VMEM_LIMIT),
         name="merge_members",
-    )(in_vmem(near), in_vmem(far))
+    )(in_vmem(near), in_vmem(far), in_vmem(met))
 
 
 def solution(mesh):

time: 121 us -> 111 us (0.917)
  waiting for transfers between devices: 64.5 us -> 36.9 us
  starting transfers between devices: 33.5 us -> 48.7 us
  Pallas kernels: 22.5 us -> 23.8 us
    ppermute x10 -> x12, waiting for transfers between devices: 43.2 us -> 27.4 us  [the longest x8 19.3 us: swap_x(): return lax.ppermute(sent, 'tok', x_pairs(flip))]
    ppermute x10 -> x12, starting transfers between devices: 14 us -> 22.8 us  [the longest x4 12 us: results(): lax.ppermute(sums, ('member', 'tok', 'col'), result_pairs(phase, y_lo))]
    ppermute x6, waiting for transfers between devices: 7.87 us -> 1.55 us  [swap_cores(): return lax.ppermute(send, 'tok', [(t, t ^ 1) for t in range(8)])]
    ppermute x6, waiting for transfers between devices: 13.5 us -> 7.78 us  [weigh(): return [lax.ppermute(v, 'member', z_pairs(d)) for d, v in send] + [own_sums]]
    ppermute x6, starting transfers between devices: 4.39 us -> 8.33 us  [swap_cores(): return lax.ppermute(send, 'tok', [(t, t ^ 1) for t in range(8)])]
    ppermute x6, starting transfers between devices: 8.22 us -> 9.94 us  [weigh(): return [lax.ppermute(v, 'member', z_pairs(d)) for d, v in send] + [own_sums]]
    pallas_call x20 -> x24, Pallas kernels: 21.6 us -> 23 us  [call(): pl.pallas_call(kernel, out_shape=shapes, in_specs=[HBM] * len(hbm) + [VME...]
  transfers between devices with their start and end apart: 24 -> 26, of which waited for: 12 -> 10; matrix products, arithmetic and copies ran while one was open for 0% -> 0% of each run, Pallas kernels for 15% -> 17%
where the time goes in v5:
time: 111 us; the launch traced here: 110 us
  starting transfers between devices  48.7 us (44%)
  waiting for transfers between devices  36.9 us (33%)
  Pallas kernels  23.8 us (21%)
    pallas_call x24, Pallas kernels, call(): pl.pallas_call(kernel, out_shape=shapes, in_specs=[HBM] * len(hbm) + [VME...  23 us
    ppermute x8, waiting for transfers between devices, swap_x(): return lax.ppermute(sent, 'tok', x_pairs(flip))  19.3 us
    ppermute x4, starting transfers between devices, results(): lax.ppermute(sums, ('member', 'tok', 'col'), result_pairs(phase, y_lo))  12 us
    ppermute x8, starting transfers between devices, swap_x(): return lax.ppermute(sent, 'tok', x_pairs(flip))  10.9 us
    ppermute x6, starting transfers between devices, weigh(): return [lax.ppermute(v, 'member', z_pairs(d)) for d, v in send] + [own_sums]  9.94 us
    ppermute x6, starting transfers between devices, swap_cores(): return lax.ppermute(send, 'tok', [(t, t ^ 1) for t in range(8)])  8.33 us
    ppermute x4, waiting for transfers between devices, results(): lax.ppermute(sums, ('member', 'tok', 'col'), result_pairs(phase, y_lo))  8.04 us
    ppermute x6, waiting for transfers between devices, weigh(): return [lax.ppermute(v, 'member', z_pairs(d)) for d, v in send] + [own_sums]  7.78 us
  transfers between devices with their start and end apart: 26, of which 10 were waited for; matrix products, arithmetic and copies ran while one was open for 0% of the time, Pallas kernels for 17%

profile of v5, /device:TPU:1, one launch (start us, length us, event | category | flops | bytes accessed | tf_op | source)
XLA Modules:
  0.0 109.7 jit_solution(2524110403214437898)
XLA Ops:
  0.0 1.2 %load_grads.1 = (bf16[2,832,256]{2,1,0:T(8,128)(2,1)S(1)}, bf16[768,256]{1,0:T(8,128)(2,1)S(1)}) custom-call(bf16[2,768,256]{2,1,0:T(8,128)(2,1)} %g_ref.3), custom_call_target="tpu_custom_call" | custom-call | flops 1 | bytes 1 | tf_op jit(solution)/shard_map/load_grads/pallas_call | solution.py:67
  1.3 2.1 %load_to_swap.2.after = bf16[768,2304]{1,0:T(8,128)(2,1)S(1)} custom-call(bf16[2,768,4096]{2,1,0:T(8,128)(2,1)} %x_ref.7, bf16[2,768,256]{2,1,0:T(8,128)(2,1)} %g_ref.3, bf16[768,256]{1,0:T(8,128)(2,1)S(1)} %get-tuple-element.47.after.g_ref), custom_call_target="tpu_custom_call" | custom-call | flops 1 | bytes 1 | tf_op jit(solution)/shard_map/load_to_swap/pallas_call | solution.py:67
  3.3 1.5 %collective-permute-start = (bf16[768,2304]{1,0:T(8,128)(2,1)S(1)}, bf16[768,2304]{1,0:T(8,128)(2,1)S(1)}, u32[]{:S(2)}, u32[]{:S(2)}) collective-permute-start(bf16[768,2304]{1,0:T(8,128)(2,1)S(1)} %load_to_swap.2.after), channel_id=1, source_target_pairs={{0,2},{2,0},{4,6},{6,4},{8,10},{10,8},{12,14},{14,12},{1,3},{3,1},... | collective-permute-start | bytes 10616840 | tf_op jit(solution)/shard_map/ppermute | solution.py:325
  4.8 1.9 %load_to_swap.3.after = bf16[4,768,512]{2,1,0:T(8,128)(2,1)S(1)} custom-call(bf16[2,768,4096]{2,1,0:T(8,128)(2,1)} %x_ref.7, bf16[768,2304]{1,0:T(8,128)(2,1)S(1)} %load_to_swap.2.after), custom_call_target="tpu_custom_call" | custom-call | flops 1 | bytes 1 | tf_op jit(solution)/shard_map/load_to_swap/pallas_call | solution.py:67
  6.9 3.0 %collective-permute-start.1 = (bf16[2,832,256]{2,1,0:T(8,128)(2,1)S(1)}, bf16[2,832,256]{2,1,0:T(8,128)(2,1)S(1)}, u32[]{:S(2)}, u32[]{:S(2)}) collective-permute-start(bf16[2,832,256]{2,1,0:T(8,128)(2,1)S(1)} %get-tuple-element.49), channel_id=1, source_target_pairs={{0,1},{1,0},{2,3},{3,2},{4,5},{5,4},{6,7},{7,6},{8,9},{9,8},{10,11... | collective-permute-start | bytes 2555912 | tf_op jit(solution)/shard_map/ppermute | solution.py:328
  9.9 2.8 %fisher_of_own_tokens.2 = (bf16[4,768,512]{2,1,0:T(8,128)(2,1)S(1)}, bf16[256,768]{1,0:T(8,128)(2,1)S(1)}, f32[4,256,512]{2,1,0:T(8,128)S(1)}) custom-call(bf16[2,768,4096]{2,1,0:T(8,128)(2,1)} %x_ref.7, bf16[768,256]{1,0:T(8,128)(2,1)S(1)} %get-tuple-element.47.after.g_ref, bf16[4,768,512]{2,1,0:T(8,128)(2,1)S(1)} %load_to_swap.3.after), custom_call_target="tpu_custom_call" | custom-call | flops 1 | bytes 1 | tf_op jit(solution)/shard_map/fisher_of_own_tokens/pallas_call | solution.py:67
  12.7 1.2 %fisher_of_both_cores.2 = (bf16[2,256,512]{2,1,0:T(8,128)(2,1)S(1)}, f32[2,256,512]{2,1,0:T(8,128)S(1)}, bf16[256,768]{1,0:T(8,128)(2,1)S(1)}) custom-call(bf16[768,2304]{1,0:T(8,128)(2,1)S(1)} %collective-permute-done.x_ref.xb_ref, f32[4,256,512]{2,1,0:T(8,128)S(1)} %get-tuple-element.50.part_ref), custom_call_target="tpu_custom_call" | custom-call | flops 1 | bytes 1 | tf_op jit(solution)/shard_map/fisher_of_both_cores/pallas_call | solution.py:67
  13.9 1.3 %collective-permute-start.4 = (bf16[2,256,512]{2,1,0:T(8,128)(2,1)S(1)}, bf16[2,256,512]{2,1,0:T(8,128)(2,1)S(1)}, u32[]{:S(2)}, u32[]{:S(2)}) collective-permute-start(bf16[2,256,512]{2,1,0:T(8,128)(2,1)S(1)} %get-tuple-element.58), channel_id=1, source_target_pairs={{0,4},{2,6},{4,0},{6,2},{8,12},{10,14},{12,8},{14,10},{1,5},{3,7},... | collective-permute-start | bytes 1572872 | tf_op jit(solution)/shard_map/ppermute | solution.py:331
  15.2 4.6 %collective-permute-start.7 = (bf16[2,1024,256]{2,1,0:T(8,128)(2,1)S(1)}, bf16[2,1024,256]{2,1,0:T(8,128)(2,1)S(1)}, u32[]{:S(2)}, u32[]{:S(2)}) collective-permute-start(bf16[2,1024,256]{2,1,0:T(8,128)(2,1)S(1)} %copy-done), channel_id=1, source_target_pairs={{0,0},{1,2},{2,12},{3,14},{4,4},{5,6},{6,8},{7,10},{8,9},{9,11},{1... | collective-permute-start | bytes 3145736 | tf_op jit(solution)/shard_map/ppermute | solution.py:383
  19.7 2.7 %fisher_of_own_tokens.3 = (bf16[4,768,512]{2,1,0:T(8,128)(2,1)S(1)}, f32[4,256,512]{2,1,0:T(8,128)S(1)}) custom-call(bf16[2,768,4096]{2,1,0:T(8,128)(2,1)} %x_ref.7, bf16[256,768]{1,0:T(8,128)(2,1)S(1)} %get-tuple-element.52.gt_ref, f32[2,256,512]{2,1,0:T(8,128)S(1)} %get-tuple-element.53.after.kept_ref), custom_call_target="tpu_custom_call" | custom-call | flops 1 | bytes 1 | tf_op jit(solution)/shard_map/fisher_of_own_tokens/pallas_call | solution.py:67
  22.5 1.1 %fisher_of_both_cores.3 = (bf16[2,256,512]{2,1,0:T(8,128)(2,1)S(1)}, f32[2,256,512]{2,1,0:T(8,128)S(1)}) custom-call(bf16[4,768,512]{2,1,0:T(8,128)(2,1)S(1)} %collective-permute-done.2.x_ref.xb_ref, bf16[256,768]{1,0:T(8,128)(2,1)S(1)} %get-tuple-element.51.gt_ref, f32[4,256,512]{2,1,0:T(8,128)S(1)} %get-tuple-element.54.part_ref, ...), custom_call_target="tpu_custom_call" | custom-call | flops 1 | bytes 1 | tf_op jit(solution)/shard_map/fisher_of_both_cores/pallas_call | solution.py:67
  23.6 0.4 collective-permute-start.3
  24.0 2.7 %collective-permute-done.4.got_ref = bf16[2,256,512]{2,1,0:T(8,128)(2,1)S(1)} collective-permute-done((bf16[2,256,512]{2,1,0:T(8,128)(2,1)S(1)}, bf16[2,256,512]{2,1,0:T(8,128)(2,1)S(1)}, u32[]{:S(2)}, u32[]{:S(2)}) %collective-permute-start.4) | collective-permute-done | bytes 524320 | tf_op jit(solution)/shard_map/ppermute | solution.py:331
  26.7 0.7 fisher_over_first_swap.4
  27.4 2.6 %collective-permute-start.5 = (bf16[256,512]{1,0:T(8,128)(2,1)S(1)}, bf16[256,512]{1,0:T(8,128)(2,1)S(1)}, u32[]{:S(2)}, u32[]{:S(2)}) collective-permute-start(bf16[256,512]{1,0:T(8,128)(2,1)S(1)} %get-tuple-element.60), channel_id=1, source_target_pairs={{0,12},{2,14},{4,8},{6,10},{8,4},{10,6},{12,0},{14,2},{1,13},{3,15... | collective-permute-start | bytes 786440 | tf_op jit(solution)/shard_map/ppermute | solution.py:331
  30.0 7.8 %collective-permute-done.5.got = bf16[256,512]{1,0:T(8,128)(2,1)S(1)} collective-permute-done((bf16[256,512]{1,0:T(8,128)(2,1)S(1)}, bf16[256,512]{1,0:T(8,128)(2,1)S(1)}, u32[]{:S(2)}, u32[]{:S(2)}) %collective-permute-start.5) | collective-permute-done | bytes 262176 | tf_op jit(solution)/shard_map/ppermute | solution.py:331
  38.1 0.7 fisher_over_first_swap.5
  39.1 1.6 %collective-permute-start.6 = (bf16[768,256]{1,0:T(8,128)(2,1)S(1)}, bf16[768,256]{1,0:T(8,128)(2,1)S(1)}, u32[]{:S(2)}, u32[]{:S(2)}) collective-permute-start(bf16[768,256]{1,0:T(8,128)(2,1)S(1)} %get-tuple-element.63), channel_id=1, source_target_pairs={{0,2},{2,0},{4,6},{6,4},{8,10},{10,8},{12,14},{14,12},{1,3},{3,1},... | collective-permute-start | bytes 1179656 | tf_op jit(solution)/shard_map/ppermute | solution.py:325
  40.7 3.0 %collective-permute-start.9 = (bf16[256,512]{1,0:T(8,128)(2,1)S(1)}, bf16[256,512]{1,0:T(8,128)(2,1)S(1)}, u32[]{:S(2)}, u32[]{:S(2)}) collective-permute-start(bf16[256,512]{1,0:T(8,128)(2,1)S(1)} %get-tuple-element.67), channel_id=1, source_target_pairs={{0,12},{2,14},{4,8},{6,10},{8,4},{10,6},{12,0},{14,2},{1,13},{3,15... | collective-permute-start | bytes 786440 | tf_op jit(solution)/shard_map/ppermute | solution.py:331
  43.8 2.0 %fisher_of_other_grads.2 = (bf16[2,256,512]{2,1,0:T(8,128)(2,1)S(1)}, f32[2,256,512]{2,1,0:T(8,128)S(1)}, bf16[256,768]{1,0:T(8,128)(2,1)S(1)}, bf16[256,768]{1,0:T(8,128)(2,1)S(1)}) custom-call(bf16[4,768,512]{2,1,0:T(8,128)(2,1)S(1)} %get-tuple-element.48.xa_ref, bf16[768,2304]{1,0:T(8,128)(2,1)S(1)} %collective-permute-done.x_ref.xb_ref, ...), custom_call_target="tpu_custom_call" | custom-call | flops 1 | bytes 1 | tf_op jit(solution)/shard_map/fisher_of_other_grads/pallas_call | solution.py:67
  45.9 1.9 %fisher_of_other_grads.3 = (bf16[2,256,512]{2,1,0:T(8,128)(2,1)S(1)}, f32[2,256,512]{2,1,0:T(8,128)S(1)}) custom-call(bf16[4,768,512]{2,1,0:T(8,128)(2,1)S(1)} %get-tuple-element.55.after.xa_ref, bf16[4,768,512]{2,1,0:T(8,128)(2,1)S(1)} %collective-permute-done.2.x_ref.xb_ref, bf16[256,768]{1,0:T(8,128)(2,1)S(1)} %get-tuple-element.68.gta_ref, ...), custom_call_target="tpu_custom_call" | custom-call | flops 1 | bytes 1 | tf_op jit(solution)/shard_map/fisher_of_other_grads/pallas_call | solution.py:67
  47.7 2.0 %collective-permute-start.11 = (bf16[2,256,512]{2,1,0:T(8,128)(2,1)S(1)}, bf16[2,256,512]{2,1,0:T(8,128)(2,1)S(1)}, u32[]{:S(2)}, u32[]{:S(2)}) collective-permute-start(bf16[2,256,512]{2,1,0:T(8,128)(2,1)S(1)} %get-tuple-element.74), channel_id=1, source_target_pairs={{0,12},{2,14},{4,8},{6,10},{8,4},{10,6},{12,0},{14,2},{1,13},{3,15... | collective-permute-start | bytes 1572872 | tf_op jit(solution)/shard_map/ppermute | solution.py:331
  49.7 0.9 collective-permute-start.14
  51.0 0.4 collective-permute-start.13
  51.4 7.7 %collective-permute-done.8.got_ref = bf16[2,256,512]{2,1,0:T(8,128)(2,1)S(1)} collective-permute-done((bf16[2,256,512]{2,1,0:T(8,128)(2,1)S(1)}, bf16[2,256,512]{2,1,0:T(8,128)(2,1)S(1)}, u32[]{:S(2)}, u32[]{:S(2)}) %collective-permute-start.8) | collective-permute-done | bytes 524320 | tf_op jit(solution)/shard_map/ppermute | solution.py:331
  59.0 0.7 fisher_over_first_swap.6
  59.8 1.2 %collective-permute-start.10 = (bf16[256,512]{1,0:T(8,128)(2,1)S(1)}, bf16[256,512]{1,0:T(8,128)(2,1)S(1)}, u32[]{:S(2)}, u32[]{:S(2)}) collective-permute-start(bf16[256,512]{1,0:T(8,128)(2,1)S(1)} %get-tuple-element.73), channel_id=1, source_target_pairs={{0,12},{2,14},{4,8},{6,10},{8,4},{10,6},{12,0},{14,2},{1,13},{3,15... | collective-permute-start | bytes 786440 | tf_op jit(solution)/shard_map/ppermute | solution.py:331
  61.0 1.1 %collective-permute-done.11.got_ref = bf16[2,256,512]{2,1,0:T(8,128)(2,1)S(1)} collective-permute-done((bf16[2,256,512]{2,1,0:T(8,128)(2,1)S(1)}, bf16[2,256,512]{2,1,0:T(8,128)(2,1)S(1)}, u32[]{:S(2)}, u32[]{:S(2)}) %collective-permute-start.11) | collective-permute-done | bytes 524320 | tf_op jit(solution)/shard_map/ppermute | solution.py:331
  62.1 0.7 fisher_over_first_swap.7
  63.1 0.5 weigh_members.2
  63.7 1.6 %collective-permute-start.15 = (bf16[3,128,256]{2,1,0:T(8,128)(2,1)S(1)}, bf16[3,128,256]{2,1,0:T(8,128)(2,1)S(1)}, u32[]{:S(2)}, u32[]{:S(2)}) collective-permute-start(bf16[3,128,256]{2,1,0:T(8,128)(2,1)S(1)} %get-tuple-element.79), channel_id=1, source_target_pairs={{0,16},{16,32},{32,48},{48,0},{64,80},{80,96},{96,112},{112,64},{1... | collective-permute-start | bytes 589832 | tf_op jit(solution)/shard_map/ppermute | solution.py:352
  65.3 3.3 %collective-permute-start.16 = (bf16[3,128,256]{2,1,0:T(8,128)(2,1)S(1)}, bf16[3,128,256]{2,1,0:T(8,128)(2,1)S(1)}, u32[]{:S(2)}, u32[]{:S(2)}) collective-permute-start(bf16[3,128,256]{2,1,0:T(8,128)(2,1)S(1)} %get-tuple-element.80), channel_id=1, source_target_pairs={{0,32},{16,48},{32,0},{48,16},{64,96},{80,112},{96,64},{112,80},{1... | collective-permute-start | bytes 589832 | tf_op jit(solution)/shard_map/ppermute | solution.py:352
  68.6 0.8 collective-permute-start.17
  69.4 1.1 collective-permute-done.15.one
  70.5 4.5 %collective-permute-done.16.two = bf16[3,128,256]{2,1,0:T(8,128)(2,1)S(1)} collective-permute-done((bf16[3,128,256]{2,1,0:T(8,128)(2,1)S(1)}, bf16[3,128,256]{2,1,0:T(8,128)(2,1)S(1)}, u32[]{:S(2)}, u32[]{:S(2)}) %collective-permute-start.16) | collective-permute-done | bytes 196640 | tf_op jit(solution)/shard_map/ppermute | solution.py:352
  76.0 3.8 %collective-permute-start.18 = (f32[256,512]{1,0:T(8,128)S(1)}, f32[256,512]{1,0:T(8,128)S(1)}, u32[]{:S(2)}, u32[]{:S(2)}) collective-permute-start(f32[256,512]{1,0:T(8,128)S(1)} %get-tuple-element.84), channel_id=1, source_target_pairs={{0,2},{2,0},{4,6},{6,4},{8,10},{10,8},{12,14},{14,12},{1,3},{3,1},... | collective-permute-start | bytes 1572872 | tf_op jit(solution)/shard_map/ppermute | solution.py:325
  79.8 1.5 %collective-permute-done.18.refs_1_ = f32[256,512]{1,0:T(8,128)S(1)} collective-permute-done((f32[256,512]{1,0:T(8,128)S(1)}, f32[256,512]{1,0:T(8,128)S(1)}, u32[]{:S(2)}, u32[]{:S(2)}) %collective-permute-start.18) | collective-permute-done | bytes 524320 | tf_op jit(solution)/shard_map/ppermute | solution.py:325
  81.3 0.5 weigh_members.3
  81.8 1.0 collective-permute-start.19
  82.8 2.1 %collective-permute-start.20 = (bf16[3,128,256]{2,1,0:T(8,128)(2,1)S(1)}, bf16[3,128,256]{2,1,0:T(8,128)(2,1)S(1)}, u32[]{:S(2)}, u32[]{:S(2)}) collective-permute-start(bf16[3,128,256]{2,1,0:T(8,128)(2,1)S(1)} %get-tuple-element.86), channel_id=1, source_target_pairs={{0,32},{16,48},{32,0},{48,16},{64,96},{80,112},{96,64},{112,80},{1... | collective-permute-start | bytes 589832 | tf_op jit(solution)/shard_map/ppermute | solution.py:352
  85.0 1.1 collective-permute-start.21
  86.0 4.2 %collective-permute-start.24 = (bf16[3,128,256]{2,1,0:T(8,128)(2,1)S(1)}, bf16[3,128,256]{2,1,0:T(8,128)(2,1)S(1)}, u32[]{:S(2)}, u32[]{:S(2)}) collective-permute-start(bf16[3,128,256]{2,1,0:T(8,128)(2,1)S(1)} %sum_over_z.2.after), channel_id=1, source_target_pairs={{0,0},{1,15},{2,64},{3,79},{4,4},{5,11},{6,68},{7,75},{8,6},{9,9},... | collective-permute-start | bytes 589832 | tf_op jit(solution)/shard_map/ppermute | solution.py:345
  90.3 1.3 %collective-permute-start.25 = (bf16[3,128,256]{2,1,0:T(8,128)(2,1)S(1)}, bf16[3,128,256]{2,1,0:T(8,128)(2,1)S(1)}, u32[]{:S(2)}, u32[]{:S(2)}) collective-permute-start(bf16[3,128,256]{2,1,0:T(8,128)(2,1)S(1)} %sum_over_z.2.after), channel_id=1, source_target_pairs={{64,0},{65,15},{66,64},{67,79},{68,4},{69,11},{70,68},{71,75},{72,... | collective-permute-start | bytes 589832 | tf_op jit(solution)/shard_map/ppermute | solution.py:345
  91.6 2.2 %collective-permute-done.20.two = bf16[3,128,256]{2,1,0:T(8,128)(2,1)S(1)} collective-permute-done((bf16[3,128,256]{2,1,0:T(8,128)(2,1)S(1)}, bf16[3,128,256]{2,1,0:T(8,128)(2,1)S(1)}, u32[]{:S(2)}, u32[]{:S(2)}) %collective-permute-start.20) | collective-permute-done | bytes 196640 | tf_op jit(solution)/shard_map/ppermute | solution.py:352
  94.2 5.7 %collective-permute-start.22 = (bf16[3,128,256]{2,1,0:T(8,128)(2,1)S(1)}, bf16[3,128,256]{2,1,0:T(8,128)(2,1)S(1)}, u32[]{:S(2)}, u32[]{:S(2)}) collective-permute-start(bf16[3,128,256]{2,1,0:T(8,128)(2,1)S(1)} %sum_over_z.3), channel_id=1, source_target_pairs={{0,1},{1,14},{2,65},{3,78},{4,5},{5,10},{6,69},{7,74},{8,7},{9,8},... | collective-permute-start | bytes 589832 | tf_op jit(solution)/shard_map/ppermute | solution.py:345
  99.9 0.7 collective-permute-start.23
  100.8 8.0 %collective-permute-done.22.near = bf16[3,128,256]{2,1,0:T(8,128)(2,1)S(1)} collective-permute-done((bf16[3,128,256]{2,1,0:T(8,128)(2,1)S(1)}, bf16[3,128,256]{2,1,0:T(8,128)(2,1)S(1)}, u32[]{:S(2)}, u32[]{:S(2)}) %collective-permute-start.22) | collective-permute-done | bytes 196640 | tf_op jit(solution)/shard_map/ppermute | solution.py:345
  108.8 0.8 merge_members.1
  (31 shorter events, 2.9 us)
Async XLA Ops:
  3.3 9.4 %collective-permute-start = (bf16[768,2304]{1,0:T(8,128)(2,1)S(1)}, bf16[768,2304]{1,0:T(8,128)(2,1)S(1)}, u32[]{:S(2)}, u32[]{:S(2)}) collective-permute-start(bf16[768,2304]{1,0:T(8,128)(2,1)S(1)} %load_to_swap.2.after), channel_id=1, source_target_pairs={{0,2},{2,0},{4,6},{6,4},{8,10},{10,8},{12,14},{14,12},{1,3},{3,1},... | collective-permute-start | bytes 10616840 | tf_op jit(solution)/shard_map/ppermute | solution.py:325
  6.7 15.7 %collective-permute-start.2 = (bf16[4,768,512]{2,1,0:T(8,128)(2,1)S(1)}, bf16[4,768,512]{2,1,0:T(8,128)(2,1)S(1)}, u32[]{:S(2)}, u32[]{:S(2)}) collective-permute-start(bf16[4,768,512]{2,1,0:T(8,128)(2,1)S(1)} %load_to_swap.3.after), channel_id=1, source_target_pairs={{0,2},{2,0},{4,6},{6,4},{8,10},{10,8},{12,14},{14,12},{1,3},{3,1},... | collective-permute-start | bytes 9437192 | tf_op jit(solution)/shard_map/ppermute | solution.py:325
  6.9 32.2 %collective-permute-start.1 = (bf16[2,832,256]{2,1,0:T(8,128)(2,1)S(1)}, bf16[2,832,256]{2,1,0:T(8,128)(2,1)S(1)}, u32[]{:S(2)}, u32[]{:S(2)}) collective-permute-start(bf16[2,832,256]{2,1,0:T(8,128)(2,1)S(1)} %get-tuple-element.49), channel_id=1, source_target_pairs={{0,1},{1,0},{2,3},{3,2},{4,5},{5,4},{6,7},{7,6},{8,9},{9,8},{10,11... | collective-permute-start | bytes 2555912 | tf_op jit(solution)/shard_map/ppermute | solution.py:328
  12.7 2.5 %copy-start = (bf16[2,1024,256]{2,1,0:T(8,128)(2,1)S(1)}, bf16[2,1024,256]{2,1,0:T(8,128)(2,1)}, u32[]{:S(2)}) copy-start(bf16[2,1024,256]{2,1,0:T(8,128)(2,1)} %param.5) | copy-start | bytes 3145732
  13.9 12.8 %collective-permute-start.4 = (bf16[2,256,512]{2,1,0:T(8,128)(2,1)S(1)}, bf16[2,256,512]{2,1,0:T(8,128)(2,1)S(1)}, u32[]{:S(2)}, u32[]{:S(2)}) collective-permute-start(bf16[2,256,512]{2,1,0:T(8,128)(2,1)S(1)} %get-tuple-element.58), channel_id=1, source_target_pairs={{0,4},{2,6},{4,0},{6,2},{8,12},{10,14},{12,8},{14,10},{1,5},{3,7},... | collective-permute-start | bytes 1572872 | tf_op jit(solution)/shard_map/ppermute | solution.py:331
  15.2 28.6 %collective-permute-start.7 = (bf16[2,1024,256]{2,1,0:T(8,128)(2,1)S(1)}, bf16[2,1024,256]{2,1,0:T(8,128)(2,1)S(1)}, u32[]{:S(2)}, u32[]{:S(2)}) collective-permute-start(bf16[2,1024,256]{2,1,0:T(8,128)(2,1)S(1)} %copy-done), channel_id=1, source_target_pairs={{0,0},{1,2},{2,12},{3,14},{4,4},{5,6},{6,8},{7,10},{8,9},{9,11},{1... | collective-permute-start | bytes 3145736 | tf_op jit(solution)/shard_map/ppermute | solution.py:383
  23.6 14.5 %collective-permute-start.3 = (bf16[2,256,512]{2,1,0:T(8,128)(2,1)S(1)}, bf16[2,256,512]{2,1,0:T(8,128)(2,1)S(1)}, u32[]{:S(2)}, u32[]{:S(2)}) collective-permute-start(bf16[2,256,512]{2,1,0:T(8,128)(2,1)S(1)} %get-tuple-element.57), channel_id=1, source_target_pairs={{0,4},{2,6},{4,0},{6,2},{8,12},{10,14},{12,8},{14,10},{1,5},{3,7},... | collective-permute-start | bytes 1572872 | tf_op jit(solution)/shard_map/ppermute | solution.py:331
  27.4 10.4 %collective-permute-start.5 = (bf16[256,512]{1,0:T(8,128)(2,1)S(1)}, bf16[256,512]{1,0:T(8,128)(2,1)S(1)}, u32[]{:S(2)}, u32[]{:S(2)}) collective-permute-start(bf16[256,512]{1,0:T(8,128)(2,1)S(1)} %get-tuple-element.60), channel_id=1, source_target_pairs={{0,12},{2,14},{4,8},{6,10},{8,4},{10,6},{12,0},{14,2},{1,13},{3,15... | collective-permute-start | bytes 786440 | tf_op jit(solution)/shard_map/ppermute | solution.py:331
  39.1 4.7 %collective-permute-start.6 = (bf16[768,256]{1,0:T(8,128)(2,1)S(1)}, bf16[768,256]{1,0:T(8,128)(2,1)S(1)}, u32[]{:S(2)}, u32[]{:S(2)}) collective-permute-start(bf16[768,256]{1,0:T(8,128)(2,1)S(1)} %get-tuple-element.63), channel_id=1, source_target_pairs={{0,2},{2,0},{4,6},{6,4},{8,10},{10,8},{12,14},{14,12},{1,3},{3,1},... | collective-permute-start | bytes 1179656 | tf_op jit(solution)/shard_map/ppermute | solution.py:325
  40.7 10.0 %collective-permute-start.9 = (bf16[256,512]{1,0:T(8,128)(2,1)S(1)}, bf16[256,512]{1,0:T(8,128)(2,1)S(1)}, u32[]{:S(2)}, u32[]{:S(2)}) collective-permute-start(bf16[256,512]{1,0:T(8,128)(2,1)S(1)} %get-tuple-element.67), channel_id=1, source_target_pairs={{0,12},{2,14},{4,8},{6,10},{8,4},{10,6},{12,0},{14,2},{1,13},{3,15... | collective-permute-start | bytes 786440 | tf_op jit(solution)/shard_map/ppermute | solution.py:331
  45.8 13.3 %collective-permute-start.8 = (bf16[2,256,512]{2,1,0:T(8,128)(2,1)S(1)}, bf16[2,256,512]{2,1,0:T(8,128)(2,1)S(1)}, u32[]{:S(2)}, u32[]{:S(2)}) collective-permute-start(bf16[2,256,512]{2,1,0:T(8,128)(2,1)S(1)} %get-tuple-element.66), channel_id=1, source_target_pairs={{0,4},{2,6},{4,0},{6,2},{8,12},{10,14},{12,8},{14,10},{1,5},{3,7},... | collective-permute-start | bytes 1572872 | tf_op jit(solution)/shard_map/ppermute | solution.py:331
  47.7 14.4 %collective-permute-start.11 = (bf16[2,256,512]{2,1,0:T(8,128)(2,1)S(1)}, bf16[2,256,512]{2,1,0:T(8,128)(2,1)S(1)}, u32[]{:S(2)}, u32[]{:S(2)}) collective-permute-start(bf16[2,256,512]{2,1,0:T(8,128)(2,1)S(1)} %get-tuple-element.74), channel_id=1, source_target_pairs={{0,12},{2,14},{4,8},{6,10},{8,4},{10,6},{12,0},{14,2},{1,13},{3,15... | collective-permute-start | bytes 1572872 | tf_op jit(solution)/shard_map/ppermute | solution.py:331
  49.7 13.4 %collective-permute-start.14 = (bf16[2,512,256]{2,1,0:T(8,128)(2,1)S(1)}, bf16[2,512,256]{2,1,0:T(8,128)(2,1)S(1)}, u32[]{:S(2)}, u32[]{:S(2)}) collective-permute-start(bf16[2,512,256]{2,1,0:T(8,128)(2,1)S(1)} %get-tuple-element.78), channel_id=1, source_target_pairs={{0,2},{2,0},{4,6},{6,4},{8,10},{10,8},{12,14},{14,12},{1,3},{3,1},... | collective-permute-start | bytes 1572872 | tf_op jit(solution)/shard_map/ppermute | solution.py:325
  51.0 12.1 %collective-permute-start.13 = (f32[256,512]{1,0:T(8,128)S(1)}, f32[256,512]{1,0:T(8,128)S(1)}, u32[]{:S(2)}, u32[]{:S(2)}) collective-permute-start(f32[256,512]{1,0:T(8,128)S(1)} %get-tuple-element.77), channel_id=1, source_target_pairs={{0,2},{2,0},{4,6},{6,4},{8,10},{10,8},{12,14},{14,12},{1,3},{3,1},... | collective-permute-start | bytes 1572872 | tf_op jit(solution)/shard_map/ppermute | solution.py:325
  59.8 15.5 %collective-permute-start.10 = (bf16[256,512]{1,0:T(8,128)(2,1)S(1)}, bf16[256,512]{1,0:T(8,128)(2,1)S(1)}, u32[]{:S(2)}, u32[]{:S(2)}) collective-permute-start(bf16[256,512]{1,0:T(8,128)(2,1)S(1)} %get-tuple-element.73), channel_id=1, source_target_pairs={{0,12},{2,14},{4,8},{6,10},{8,4},{10,6},{12,0},{14,2},{1,13},{3,15... | collective-permute-start | bytes 786440 | tf_op jit(solution)/shard_map/ppermute | solution.py:331
  62.9 12.7 %collective-permute-start.12 = (bf16[256,512]{1,0:T(8,128)(2,1)S(1)}, bf16[256,512]{1,0:T(8,128)(2,1)S(1)}, u32[]{:S(2)}, u32[]{:S(2)}) collective-permute-start(bf16[256,512]{1,0:T(8,128)(2,1)S(1)} %get-tuple-element.76), channel_id=1, source_target_pairs={{0,4},{2,6},{4,0},{6,2},{8,12},{10,14},{12,8},{14,10},{1,5},{3,7},... | collective-permute-start | bytes 786440 | tf_op jit(solution)/shard_map/ppermute | solution.py:331
  63.7 6.8 %collective-permute-start.15 = (bf16[3,128,256]{2,1,0:T(8,128)(2,1)S(1)}, bf16[3,128,256]{2,1,0:T(8,128)(2,1)S(1)}, u32[]{:S(2)}, u32[]{:S(2)}) collective-permute-start(bf16[3,128,256]{2,1,0:T(8,128)(2,1)S(1)} %get-tuple-element.79), channel_id=1, source_target_pairs={{0,16},{16,32},{32,48},{48,0},{64,80},{80,96},{96,112},{112,64},{1... | collective-permute-start | bytes 589832 | tf_op jit(solution)/shard_map/ppermute | solution.py:352
  65.3 9.7 %collective-permute-start.16 = (bf16[3,128,256]{2,1,0:T(8,128)(2,1)S(1)}, bf16[3,128,256]{2,1,0:T(8,128)(2,1)S(1)}, u32[]{:S(2)}, u32[]{:S(2)}) collective-permute-start(bf16[3,128,256]{2,1,0:T(8,128)(2,1)S(1)} %get-tuple-element.80), channel_id=1, source_target_pairs={{0,32},{16,48},{32,0},{48,16},{64,96},{80,112},{96,64},{112,80},{1... | collective-permute-start | bytes 589832 | tf_op jit(solution)/shard_map/ppermute | solution.py:352
  68.6 6.3 %collective-permute-start.17 = (bf16[3,128,256]{2,1,0:T(8,128)(2,1)S(1)}, bf16[3,128,256]{2,1,0:T(8,128)(2,1)S(1)}, u32[]{:S(2)}, u32[]{:S(2)}) collective-permute-start(bf16[3,128,256]{2,1,0:T(8,128)(2,1)S(1)} %get-tuple-element.81), channel_id=1, source_target_pairs={{0,48},{16,0},{32,16},{48,32},{64,112},{80,64},{96,80},{112,96},{1... | collective-permute-start | bytes 589832 | tf_op jit(solution)/shard_map/ppermute | solution.py:352
  76.0 5.3 %collective-permute-start.18 = (f32[256,512]{1,0:T(8,128)S(1)}, f32[256,512]{1,0:T(8,128)S(1)}, u32[]{:S(2)}, u32[]{:S(2)}) collective-permute-start(f32[256,512]{1,0:T(8,128)S(1)} %get-tuple-element.84), channel_id=1, source_target_pairs={{0,2},{2,0},{4,6},{6,4},{8,10},{10,8},{12,14},{14,12},{1,3},{3,1},... | collective-permute-start | bytes 1572872 | tf_op jit(solution)/shard_map/ppermute | solution.py:325
  81.8 9.8 %collective-permute-start.19 = (bf16[3,128,256]{2,1,0:T(8,128)(2,1)S(1)}, bf16[3,128,256]{2,1,0:T(8,128)(2,1)S(1)}, u32[]{:S(2)}, u32[]{:S(2)}) collective-permute-start(bf16[3,128,256]{2,1,0:T(8,128)(2,1)S(1)} %get-tuple-element.85), channel_id=1, source_target_pairs={{0,16},{16,32},{32,48},{48,0},{64,80},{80,96},{96,112},{112,64},{1... | collective-permute-start | bytes 589832 | tf_op jit(solution)/shard_map/ppermute | solution.py:352
  82.8 11.0 %collective-permute-start.20 = (bf16[3,128,256]{2,1,0:T(8,128)(2,1)S(1)}, bf16[3,128,256]{2,1,0:T(8,128)(2,1)S(1)}, u32[]{:S(2)}, u32[]{:S(2)}) collective-permute-start(bf16[3,128,256]{2,1,0:T(8,128)(2,1)S(1)} %get-tuple-element.86), channel_id=1, source_target_pairs={{0,32},{16,48},{32,0},{48,16},{64,96},{80,112},{96,64},{112,80},{1... | collective-permute-start | bytes 589832 | tf_op jit(solution)/shard_map/ppermute | solution.py:352
  85.0 8.9 %collective-permute-start.21 = (bf16[3,128,256]{2,1,0:T(8,128)(2,1)S(1)}, bf16[3,128,256]{2,1,0:T(8,128)(2,1)S(1)}, u32[]{:S(2)}, u32[]{:S(2)}) collective-permute-start(bf16[3,128,256]{2,1,0:T(8,128)(2,1)S(1)} %get-tuple-element.87), channel_id=1, source_target_pairs={{0,48},{16,0},{32,16},{48,32},{64,112},{80,64},{96,80},{112,96},{1... | collective-permute-start | bytes 589832 | tf_op jit(solution)/shard_map/ppermute | solution.py:352
  86.0 14.6 %collective-permute-start.24 = (bf16[3,128,256]{2,1,0:T(8,128)(2,1)S(1)}, bf16[3,128,256]{2,1,0:T(8,128)(2,1)S(1)}, u32[]{:S(2)}, u32[]{:S(2)}) collective-permute-start(bf16[3,128,256]{2,1,0:T(8,128)(2,1)S(1)} %sum_over_z.2.after), channel_id=1, source_target_pairs={{0,0},{1,15},{2,64},{3,79},{4,4},{5,11},{6,68},{7,75},{8,6},{9,9},... | collective-permute-start | bytes 589832 | tf_op jit(solution)/shard_map/ppermute | solution.py:345
  90.3 10.3 %collective-permute-start.25 = (bf16[3,128,256]{2,1,0:T(8,128)(2,1)S(1)}, bf16[3,128,256]{2,1,0:T(8,128)(2,1)S(1)}, u32[]{:S(2)}, u32[]{:S(2)}) collective-permute-start(bf16[3,128,256]{2,1,0:T(8,128)(2,1)S(1)} %sum_over_z.2.after), channel_id=1, source_target_pairs={{64,0},{65,15},{66,64},{67,79},{68,4},{69,11},{70,68},{71,75},{72,... | collective-permute-start | bytes 589832 | tf_op jit(solution)/shard_map/ppermute | solution.py:345
  94.2 14.7 %collective-permute-start.22 = (bf16[3,128,256]{2,1,0:T(8,128)(2,1)S(1)}, bf16[3,128,256]{2,1,0:T(8,128)(2,1)S(1)}, u32[]{:S(2)}, u32[]{:S(2)}) collective-permute-start(bf16[3,128,256]{2,1,0:T(8,128)(2,1)S(1)} %sum_over_z.3), channel_id=1, source_target_pairs={{0,1},{1,14},{2,65},{3,78},{4,5},{5,10},{6,69},{7,74},{8,7},{9,8},... | collective-permute-start | bytes 589832 | tf_op jit(solution)/shard_map/ppermute | solution.py:345
  99.9 8.9 %collective-permute-start.23 = (bf16[3,128,256]{2,1,0:T(8,128)(2,1)S(1)}, bf16[3,128,256]{2,1,0:T(8,128)(2,1)S(1)}, u32[]{:S(2)}, u32[]{:S(2)}) collective-permute-start(bf16[3,128,256]{2,1,0:T(8,128)(2,1)S(1)} %sum_over_z.3), channel_id=1, source_target_pairs={{64,1},{65,14},{66,65},{67,78},{68,5},{69,10},{70,69},{71,74},{72,... | collective-permute-start | bytes 589832 | tf_op jit(solution)/shard_map/ppermute | solution.py:345

commit v6 on v5

--- a/solution.py
+++ b/solution.py
@@ -61,7 +61,7 @@
     return pltpu.with_memory_space_constraint(array, pltpu.HBM)
 
 
-def call(kernel, name, outs, hbm, vmem, scratch=(), flops=0):
+def call(kernel, name, outs, hbm, vmem, scratch=()):
     single = not isinstance(outs, list)
     shapes = [pltpu.VMEM(shape, kind) for shape, kind in ([outs] if single else outs)]
     result = pl.pallas_call(
@@ -171,7 +171,7 @@
         kept_out[s - 2] = block
 
 
-def add_first_kernel(x_ref, part_ref, sent_out, kept_out, gt_out):
+def add_first_kernel(x_ref, part_ref, after, sent_out, kept_out, gt_out):
     wide = part_ref.shape[2]
     gt_out[...] = squared_transposed(x_ref[:, 4 * wide :])
     for s in range(4):
@@ -203,7 +203,7 @@
     own_out[...] = kept_ref[0] + decode(got_ref[0])
 
 
-def settle_kernel(own, got, out):
+def settle_kernel(own, got, after, out):
     out[...] = own[...] + decode_fine(got[...])
 
 
@@ -212,7 +212,7 @@
     second = own[...] + decode_fine(got[...])
     core = where_am_i()[1]
     kept_out[...] = jnp.where(core == 0, first, second)
-    sent_out[...] = jnp.where(core == 0, second, first)
+    sent_out[...] = encode_fine(jnp.where(core == 0, second, first))
 
 
 def split_kernel(w_ref, after, own_out, send_out):
@@ -239,8 +239,8 @@
     for d, out in ((2, two_out), (1, one_out), (3, three_out), (0, sums_out)):
         cols = pl.ds(pl.multiple_of((z + d) % Z * part, part), part)
         weighted = total = 0.0
-        for values, m in ((own, core), (other, 1 - core)):
-            fisher = values[:, cols].T
+        for values, m in ((own[:, cols], core), (decode_fine(other[:, cols]), 1 - core)):
+            fisher = values.T
             weight = jnp.where(first, w_a[m, cols, :].astype(F32), w_b[m, cols, :].astype(F32))
             weighted += fisher * weight
             total += fisher
@@ -259,7 +259,7 @@
     return weighted, total
 
 
-def sum_kernel(one, two, three, sums, out):
+def sum_kernel(one, two, three, sums, after, out):
     to_words(*over_z(sums, (one, two, three)), out)
 
 
@@ -319,7 +319,6 @@
     code_shape, own_shape = ((outs, wide), BF16), ((outs, wide), F32)
     words, sums = ((3, wide // Z, outs), BF16), ((2, wide // Z, outs), F32)
     dma = pltpu.SemaphoreType.DMA
-    flops = 8 * outs * wide * tokens
 
     def swap_cores(send):
         return lax.ppermute(send, "tok", [(t, t ^ 1) for t in range(8)])
@@ -334,11 +333,11 @@
         sent, own = call(middle_kernel, "fisher_over_first_swap", [code_shape, own_shape], [], [kept_blocks, got, after])
         return own, swap_x(flip, sent)
 
-    def settle(one):
-        return call(settle_kernel, "fisher_over_tokens", own_shape, [], [*one])
+    def settle(one, after):
+        return call(settle_kernel, "fisher_over_tokens", own_shape, [], [*one, after])
 
     def join(first, two, after):
-        kept_block, sent = call(join_kernel, "fisher_over_tokens", [own_shape, own_shape], [], [first, *two, after])
+        kept_block, sent = call(join_kernel, "fisher_over_tokens", [own_shape, code_shape], [], [first, *two, after])
         return kept_block, swap_cores(sent)
 
     def results(phase, sums):
@@ -359,53 +358,52 @@
         load_first_kernel, "load_to_swap", ((tokens, 4 * wide + outs), BF16), [inputs, grads], [g_own], [dma((4,)), dma]
     )
     x_got0 = swap_cores(x_send0)
-    x_send1 = call(load_second_kernel, "load_to_swap", x_shape, [inputs], [x_send0], [dma((4,))])
+    x_own0, gt_own, part0 = call(
+        own_first_kernel, "fisher_of_own_tokens", [x_shape, gt_shape, part_shape], [inputs], [g_own, x_send0], [dma((4,))]
+    )
+    x_send1 = call(load_second_kernel, "load_to_swap", x_shape, [inputs], [gt_own], [dma((4,))])
     x_got1 = swap_cores(x_send1)
-
-    x_own0, gt_own, part0 = call(
-        own_first_kernel, "fisher_of_own_tokens", [x_shape, gt_shape, part_shape], [inputs], [g_own, x_send1],
-        [dma((4,))], flops,
-    )
     sent, kept00, gt_got = call(
-        add_first_kernel, "fisher_of_both_cores", [sent_shape, kept_shape, gt_shape], [], [x_got0, part0], flops=flops
+        add_first_kernel, "fisher_of_both_cores", [sent_shape, kept_shape, gt_shape], [], [x_got0, part0, x_send1]
     )
     swap00 = swap_x(1, sent)
     x_own1, part1 = call(
-        own_second_kernel, "fisher_of_own_tokens", [x_shape, part_shape], [inputs], [gt_own, kept00], [dma((4,))], flops
+        own_second_kernel, "fisher_of_own_tokens", [x_shape, part_shape], [inputs], [gt_own, kept00], [dma((4,))]
     )
     sent, kept01 = call(
-        add_second_kernel, "fisher_of_both_cores", [sent_shape, kept_shape], [], [x_got1, gt_got, part1, x_own1], flops=flops
+        add_second_kernel, "fisher_of_both_cores", [sent_shape, kept_shape], [], [x_got1, gt_got, part1, x_own1]
     )
     swap01 = swap_x(1, sent)
-    settled0 = settle(middle(3, swap00, kept00, kept01))
-    part01 = middle(3, swap01, kept01, settled0)
+    part00 = middle(3, swap00, kept00, kept01)
+    part01 = middle(3, swap01, kept01, part00[0])
+    settled0 = settle(part00, part01[0])
 
     arrived = lax.ppermute(weights, ("tok", "col"), weight_pairs())
     rows = weights.shape[1] // 2
-    w_own, w_send = call(split_kernel, "split_weights", [((2, rows, outs), BF16)] * 2, [], [arrived, part01[0]])
+    w_own, w_send = call(split_kernel, "split_weights", [((2, rows, outs), BF16)] * 2, [], [arrived, settled0])
     moved = (w_own, swap_cores(w_send))
 
-    g_kept, g_sent = call(pick_grads_kernel, "pick_grads", [g_shape, g_shape], [], [g_other, part01[0]])
+    g_kept, g_sent = call(pick_grads_kernel, "pick_grads", [g_shape, g_shape], [], [g_other, settled0])
     sent, kept10, gt_own, gt_got = call(
         both_first_kernel, "fisher_of_other_grads", [sent_shape, kept_shape, gt_shape, gt_shape], [],
-        [x_own0, x_got0, g_kept, swap_cores(g_sent), w_own], flops=2 * flops,
+        [x_own0, x_got0, g_kept, swap_cores(g_sent), w_own],
     )
     swap10 = swap_x(1, sent)
     sent, kept11 = call(
         both_second_kernel, "fisher_of_other_grads", [sent_shape, kept_shape], [],
-        [x_own1, x_got1, gt_own, gt_got, kept10], flops=2 * flops,
+        [x_own1, x_got1, gt_own, gt_got, kept10],
     )
     swap11 = swap_x(3, sent)
     own0, other0 = join(settled0, part01, kept11)
-    part10 = middle(3, swap10, kept10, own0)
-    part11 = middle(1, swap11, kept11, part10[0])
-
-    words0 = weigh(0, own0, other0, part11[0])
-    first = call(sum_kernel, "sum_over_z", words, [], words0)
-    own1, other1 = join(settle(part10), part11, first)
+    words0 = weigh(0, own0, other0, kept11)
+    part10 = middle(3, swap10, kept10, words0[3])
+    first = call(sum_kernel, "sum_over_z", words, [], [*words0, part10[0]])
+    part11 = middle(1, swap11, kept11, first)
+
+    own1, other1 = join(settle(part10, part11[0]), part11, first)
     words1 = weigh(1, own1, other1, own1)
     met = call(meet_kernel, "meet_over_y", sums, [], [*results(0, first), own1])
-    second = call(sum_kernel, "sum_over_z", words, [], [*words1])
+    second = call(sum_kernel, "sum_over_z", words, [], [*words1, own1])
     near, far = results(1, second)
     return pl.pallas_call(
         merge_kernel,

time: 111 us -> 112 us (level)
  waiting for transfers between devices: 36.9 us -> 41.5 us
  starting transfers between devices: 48.7 us -> 44.9 us
    ppermute x8, waiting for transfers between devices: 19.3 us -> 23.2 us  [swap_x(): return lax.ppermute(sent, 'tok', x_pairs(flip))]
    ppermute x6, starting transfers between devices: 8.33 us -> 6.1 us  [swap_cores(): return lax.ppermute(send, 'tok', [(t, t ^ 1) for t in range(8)])]
    ppermute x8, starting transfers between devices: 10.9 us -> 9.03 us  [swap_x(): return lax.ppermute(sent, 'tok', x_pairs(flip))]
  transfers between devices with their start and end apart: 26 -> 26, of which waited for: 10 -> 11; matrix products, arithmetic and copies ran while one was open for 0% -> 0% of each run, Pallas kernels for 17% -> 17%
where the time goes in v6:
time: 112 us
  starting transfers between devices  44.9 us (40%)
  waiting for transfers between devices  41.5 us (37%)
  Pallas kernels  24.9 us (22%)
    pallas_call x24, Pallas kernels, call(): pl.pallas_call(kernel, out_shape=shapes, in_specs=[HBM] * len(hbm) + [VME...  24 us
    ppermute x8, waiting for transfers between devices, swap_x(): return lax.ppermute(sent, 'tok', x_pairs(flip))  23.2 us
    ppermute x4, starting transfers between devices, results(): lax.ppermute(sums, ('member', 'tok', 'col'), result_pairs(phase, y_lo))  12.2 us
    ppermute x6, starting transfers between devices, weigh(): return [lax.ppermute(v, 'member', z_pairs(d)) for d, v in send] + [own_sums]  9.58 us
    ppermute x8, starting transfers between devices, swap_x(): return lax.ppermute(sent, 'tok', x_pairs(flip))  9.03 us
    ppermute x4, waiting for transfers between devices, results(): lax.ppermute(sums, ('member', 'tok', 'col'), result_pairs(phase, y_lo))  8.04 us
    ppermute x6, waiting for transfers between devices, weigh(): return [lax.ppermute(v, 'member', z_pairs(d)) for d, v in send] + [own_sums]  7.89 us
    ppermute x6, starting transfers between devices, swap_cores(): return lax.ppermute(send, 'tok', [(t, t ^ 1) for t in range(8)])  6.1 us
  transfers between devices with their start and end apart: 26, of which 11 were waited for; matrix products, arithmetic and copies ran while one was open for 0% of the time, Pallas kernels for 17%

profile of v6, /device:TPU:1, one launch (start us, length us, event | category | flops | bytes accessed | tf_op | source)
XLA Modules:
  0.0 111.6 jit_solution(15410131505151086459)
XLA Ops:
  0.0 1.2 %load_grads.1 = (bf16[2,832,256]{2,1,0:T(8,128)(2,1)S(1)}, bf16[768,256]{1,0:T(8,128)(2,1)S(1)}) custom-call(bf16[2,768,256]{2,1,0:T(8,128)(2,1)} %g_ref.3), custom_call_target="tpu_custom_call" | custom-call | flops 1 | bytes 1 | tf_op jit(solution)/shard_map/load_grads/pallas_call | solution.py:67
  1.3 2.1 %load_to_swap.2.after = bf16[768,2304]{1,0:T(8,128)(2,1)S(1)} custom-call(bf16[2,768,4096]{2,1,0:T(8,128)(2,1)} %x_ref.7, bf16[2,768,256]{2,1,0:T(8,128)(2,1)} %g_ref.3, bf16[768,256]{1,0:T(8,128)(2,1)S(1)} %get-tuple-element.47.after.g_ref), custom_call_target="tpu_custom_call" | custom-call | flops 1 | bytes 1 | tf_op jit(solution)/shard_map/load_to_swap/pallas_call | solution.py:67
  3.3 1.5 %collective-permute-start = (bf16[768,2304]{1,0:T(8,128)(2,1)S(1)}, bf16[768,2304]{1,0:T(8,128)(2,1)S(1)}, u32[]{:S(2)}, u32[]{:S(2)}) collective-permute-start(bf16[768,2304]{1,0:T(8,128)(2,1)S(1)} %load_to_swap.2.after), channel_id=1, source_target_pairs={{0,2},{2,0},{4,6},{6,4},{8,10},{10,8},{12,14},{14,12},{1,3},{3,1},... | collective-permute-start | bytes 10616840 | tf_op jit(solution)/shard_map/ppermute | solution.py:324
  4.8 2.8 %fisher_of_own_tokens.2 = (bf16[4,768,512]{2,1,0:T(8,128)(2,1)S(1)}, bf16[256,768]{1,0:T(8,128)(2,1)S(1)}, f32[4,256,512]{2,1,0:T(8,128)S(1)}) custom-call(bf16[2,768,4096]{2,1,0:T(8,128)(2,1)} %x_ref.7, bf16[768,256]{1,0:T(8,128)(2,1)S(1)} %get-tuple-element.47.after.g_ref, bf16[768,2304]{1,0:T(8,128)(2,1)S(1)} %load_to_swap.2.after), custom_call_target="tpu_custom_call" | custom-call | flops 1 | bytes 1 | tf_op jit(solution)/shard_map/fisher_of_own_tokens/pallas_call | solution.py:67
  7.6 2.0 %load_to_swap.3.after = bf16[4,768,512]{2,1,0:T(8,128)(2,1)S(1)} custom-call(bf16[2,768,4096]{2,1,0:T(8,128)(2,1)} %x_ref.7, bf16[256,768]{1,0:T(8,128)(2,1)S(1)} %get-tuple-element.51.after.gt_ref), custom_call_target="tpu_custom_call" | custom-call | flops 1 | bytes 1 | tf_op jit(solution)/shard_map/load_to_swap/pallas_call | solution.py:67
  9.7 3.1 %collective-permute-start.1 = (bf16[2,832,256]{2,1,0:T(8,128)(2,1)S(1)}, bf16[2,832,256]{2,1,0:T(8,128)(2,1)S(1)}, u32[]{:S(2)}, u32[]{:S(2)}) collective-permute-start(bf16[2,832,256]{2,1,0:T(8,128)(2,1)S(1)} %get-tuple-element.49), channel_id=1, source_target_pairs={{0,1},{1,0},{2,3},{3,2},{4,5},{5,4},{6,7},{7,6},{8,9},{9,8},{10,11... | collective-permute-start | bytes 2555912 | tf_op jit(solution)/shard_map/ppermute | solution.py:327
  12.8 5.0 %collective-permute-start.7 = (bf16[2,1024,256]{2,1,0:T(8,128)(2,1)S(1)}, bf16[2,1024,256]{2,1,0:T(8,128)(2,1)S(1)}, u32[]{:S(2)}, u32[]{:S(2)}) collective-permute-start(bf16[2,1024,256]{2,1,0:T(8,128)(2,1)S(1)} %copy-done), channel_id=1, source_target_pairs={{0,0},{1,2},{2,12},{3,14},{4,4},{5,6},{6,8},{7,10},{8,9},{9,11},{1... | collective-permute-start | bytes 3145736 | tf_op jit(solution)/shard_map/ppermute | solution.py:381
  17.8 1.2 %fisher_of_both_cores.2 = (bf16[2,256,512]{2,1,0:T(8,128)(2,1)S(1)}, f32[2,256,512]{2,1,0:T(8,128)S(1)}, bf16[256,768]{1,0:T(8,128)(2,1)S(1)}) custom-call(bf16[768,2304]{1,0:T(8,128)(2,1)S(1)} %collective-permute-done.x_ref.xb_ref, f32[4,256,512]{2,1,0:T(8,128)S(1)} %get-tuple-element.50.part_ref, bf16[4,768,512]{2,1,0:T(8,128)(2,1)S(1)} %load_to_swap.3.after), custom_call_target="tpu_custom_call" | custom-call | flops 1 | bytes 1 | tf_op jit(solution)/shard_map/fisher_of_both_cores/pallas_call | solution.py:67
  19.1 2.7 %fisher_of_own_tokens.3 = (bf16[4,768,512]{2,1,0:T(8,128)(2,1)S(1)}, f32[4,256,512]{2,1,0:T(8,128)S(1)}) custom-call(bf16[2,768,4096]{2,1,0:T(8,128)(2,1)} %x_ref.7, bf16[256,768]{1,0:T(8,128)(2,1)S(1)} %get-tuple-element.51.after.gt_ref, f32[2,256,512]{2,1,0:T(8,128)S(1)} %get-tuple-element.52.after.kept_ref), custom_call_target="tpu_custom_call" | custom-call | flops 1 | bytes 1 | tf_op jit(solution)/shard_map/fisher_of_own_tokens/pallas_call | solution.py:67
  21.8 1.1 fisher_of_both_cores.3
  22.9 1.5 %collective-permute-start.5 = (bf16[2,256,512]{2,1,0:T(8,128)(2,1)S(1)}, bf16[2,256,512]{2,1,0:T(8,128)(2,1)S(1)}, u32[]{:S(2)}, u32[]{:S(2)}) collective-permute-start(bf16[2,256,512]{2,1,0:T(8,128)(2,1)S(1)} %get-tuple-element.60), channel_id=1, source_target_pairs={{0,4},{2,6},{4,0},{6,2},{8,12},{10,14},{12,8},{14,10},{1,5},{3,7},... | collective-permute-start | bytes 1572872 | tf_op jit(solution)/shard_map/ppermute | solution.py:330
  24.4 8.7 %collective-permute-done.2.got_ref = bf16[2,256,512]{2,1,0:T(8,128)(2,1)S(1)} collective-permute-done((bf16[2,256,512]{2,1,0:T(8,128)(2,1)S(1)}, bf16[2,256,512]{2,1,0:T(8,128)(2,1)S(1)}, u32[]{:S(2)}, u32[]{:S(2)}) %collective-permute-start.2) | collective-permute-done | bytes 524320 | tf_op jit(solution)/shard_map/ppermute | solution.py:330
  33.1 0.7 fisher_over_first_swap.4
  33.9 7.0 %collective-permute-done.5.got_ref = bf16[2,256,512]{2,1,0:T(8,128)(2,1)S(1)} collective-permute-done((bf16[2,256,512]{2,1,0:T(8,128)(2,1)S(1)}, bf16[2,256,512]{2,1,0:T(8,128)(2,1)S(1)}, u32[]{:S(2)}, u32[]{:S(2)}) %collective-permute-start.5) | collective-permute-done | bytes 524320 | tf_op jit(solution)/shard_map/ppermute | solution.py:330
  40.9 0.7 fisher_over_first_swap.5
  42.2 1.1 collective-permute-start.6
  43.3 3.3 %collective-permute-start.9 = (bf16[256,512]{1,0:T(8,128)(2,1)S(1)}, bf16[256,512]{1,0:T(8,128)(2,1)S(1)}, u32[]{:S(2)}, u32[]{:S(2)}) collective-permute-start(bf16[256,512]{1,0:T(8,128)(2,1)S(1)} %get-tuple-element.67), channel_id=1, source_target_pairs={{0,12},{2,14},{4,8},{6,10},{8,4},{10,6},{12,0},{14,2},{1,13},{3,15... | collective-permute-start | bytes 786440 | tf_op jit(solution)/shard_map/ppermute | solution.py:330
  46.7 0.4 collective-permute-start.11
  47.1 1.9 %fisher_of_other_grads.2 = (bf16[2,256,512]{2,1,0:T(8,128)(2,1)S(1)}, f32[2,256,512]{2,1,0:T(8,128)S(1)}, bf16[256,768]{1,0:T(8,128)(2,1)S(1)}, bf16[256,768]{1,0:T(8,128)(2,1)S(1)}) custom-call(bf16[4,768,512]{2,1,0:T(8,128)(2,1)S(1)} %get-tuple-element.48.xa_ref, bf16[768,2304]{1,0:T(8,128)(2,1)S(1)} %collective-permute-done.x_ref.xb_ref, ...), custom_call_target="tpu_custom_call" | custom-call | flops 1 | bytes 1 | tf_op jit(solution)/shard_map/fisher_of_other_grads/pallas_call | solution.py:67
  49.3 1.9 %fisher_of_other_grads.3 = (bf16[2,256,512]{2,1,0:T(8,128)(2,1)S(1)}, f32[2,256,512]{2,1,0:T(8,128)S(1)}) custom-call(bf16[4,768,512]{2,1,0:T(8,128)(2,1)S(1)} %get-tuple-element.56.after.xa_ref, bf16[4,768,512]{2,1,0:T(8,128)(2,1)S(1)} %collective-permute-done.3.x_ref.xb_ref, bf16[256,768]{1,0:T(8,128)(2,1)S(1)} %get-tuple-element.68.gta_ref, ...), custom_call_target="tpu_custom_call" | custom-call | flops 1 | bytes 1 | tf_op jit(solution)/shard_map/fisher_of_other_grads/pallas_call | solution.py:67
  51.2 1.4 %collective-permute-start.13 = (bf16[2,256,512]{2,1,0:T(8,128)(2,1)S(1)}, bf16[2,256,512]{2,1,0:T(8,128)(2,1)S(1)}, u32[]{:S(2)}, u32[]{:S(2)}) collective-permute-start(bf16[2,256,512]{2,1,0:T(8,128)(2,1)S(1)} %get-tuple-element.77), channel_id=1, source_target_pairs={{0,12},{2,14},{4,8},{6,10},{8,4},{10,6},{12,0},{14,2},{1,13},{3,15... | collective-permute-start | bytes 1572872 | tf_op jit(solution)/shard_map/ppermute | solution.py:330
  52.6 0.5 collective-permute-done.9.got
  53.2 0.6 fisher_over_tokens.5
  53.8 0.8 collective-permute-start.10
  54.6 1.2 %collective-permute-done.10.refs_1_ = bf16[256,512]{1,0:T(8,128)(2,1)S(1)} collective-permute-done((bf16[256,512]{1,0:T(8,128)(2,1)S(1)}, bf16[256,512]{1,0:T(8,128)(2,1)S(1)}, u32[]{:S(2)}, u32[]{:S(2)}) %collective-permute-start.10) | collective-permute-done | bytes 262176 | tf_op jit(solution)/shard_map/ppermute | solution.py:324
  55.7 0.7 weigh_members.2
  56.4 1.7 %collective-permute-start.14 = (bf16[3,128,256]{2,1,0:T(8,128)(2,1)S(1)}, bf16[3,128,256]{2,1,0:T(8,128)(2,1)S(1)}, u32[]{:S(2)}, u32[]{:S(2)}) collective-permute-start(bf16[3,128,256]{2,1,0:T(8,128)(2,1)S(1)} %get-tuple-element.78), channel_id=1, source_target_pairs={{0,16},{16,32},{32,48},{48,0},{64,80},{80,96},{96,112},{112,64},{1... | collective-permute-start | bytes 589832 | tf_op jit(solution)/shard_map/ppermute | solution.py:351
  58.1 3.3 %collective-permute-start.15 = (bf16[3,128,256]{2,1,0:T(8,128)(2,1)S(1)}, bf16[3,128,256]{2,1,0:T(8,128)(2,1)S(1)}, u32[]{:S(2)}, u32[]{:S(2)}) collective-permute-start(bf16[3,128,256]{2,1,0:T(8,128)(2,1)S(1)} %get-tuple-element.79), channel_id=1, source_target_pairs={{0,32},{16,48},{32,0},{48,16},{64,96},{80,112},{96,64},{112,80},{1... | collective-permute-start | bytes 589832 | tf_op jit(solution)/shard_map/ppermute | solution.py:351
  61.5 0.7 collective-permute-start.16
  62.2 0.5 collective-permute-done.8.got_ref
  62.7 0.7 fisher_over_first_swap.6
  63.4 2.3 %collective-permute-start.12 = (bf16[256,512]{1,0:T(8,128)(2,1)S(1)}, bf16[256,512]{1,0:T(8,128)(2,1)S(1)}, u32[]{:S(2)}, u32[]{:S(2)}) collective-permute-start(bf16[256,512]{1,0:T(8,128)(2,1)S(1)} %get-tuple-element.76), channel_id=1, source_target_pairs={{0,12},{2,14},{4,8},{6,10},{8,4},{10,6},{12,0},{14,2},{1,13},{3,15... | collective-permute-start | bytes 786440 | tf_op jit(solution)/shard_map/ppermute | solution.py:330
  65.7 4.6 %collective-permute-done.15.two = bf16[3,128,256]{2,1,0:T(8,128)(2,1)S(1)} collective-permute-done((bf16[3,128,256]{2,1,0:T(8,128)(2,1)S(1)}, bf16[3,128,256]{2,1,0:T(8,128)(2,1)S(1)}, u32[]{:S(2)}, u32[]{:S(2)}) %collective-permute-start.15) | collective-permute-done | bytes 196640 | tf_op jit(solution)/shard_map/ppermute | solution.py:351
  70.7 0.7 fisher_over_first_swap.7
  71.8 6.3 %collective-permute-done.17.got = bf16[256,512]{1,0:T(8,128)(2,1)S(1)} collective-permute-done((bf16[256,512]{1,0:T(8,128)(2,1)S(1)}, bf16[256,512]{1,0:T(8,128)(2,1)S(1)}, u32[]{:S(2)}, u32[]{:S(2)}) %collective-permute-start.17) | collective-permute-done | bytes 262176 | tf_op jit(solution)/shard_map/ppermute | solution.py:330
  78.1 0.6 fisher_over_tokens.7
  78.7 2.2 %collective-permute-start.18 = (bf16[256,512]{1,0:T(8,128)(2,1)S(1)}, bf16[256,512]{1,0:T(8,128)(2,1)S(1)}, u32[]{:S(2)}, u32[]{:S(2)}) collective-permute-start(bf16[256,512]{1,0:T(8,128)(2,1)S(1)} %get-tuple-element.84), channel_id=1, source_target_pairs={{0,2},{2,0},{4,6},{6,4},{8,10},{10,8},{12,14},{14,12},{1,3},{3,1},... | collective-permute-start | bytes 786440 | tf_op jit(solution)/shard_map/ppermute | solution.py:324
  80.9 1.2 %collective-permute-done.18.refs_1_ = bf16[256,512]{1,0:T(8,128)(2,1)S(1)} collective-permute-done((bf16[256,512]{1,0:T(8,128)(2,1)S(1)}, bf16[256,512]{1,0:T(8,128)(2,1)S(1)}, u32[]{:S(2)}, u32[]{:S(2)}) %collective-permute-start.18) | collective-permute-done | bytes 262176 | tf_op jit(solution)/shard_map/ppermute | solution.py:324
  82.1 0.7 weigh_members.3
  82.8 1.4 %collective-permute-start.19 = (bf16[3,128,256]{2,1,0:T(8,128)(2,1)S(1)}, bf16[3,128,256]{2,1,0:T(8,128)(2,1)S(1)}, u32[]{:S(2)}, u32[]{:S(2)}) collective-permute-start(bf16[3,128,256]{2,1,0:T(8,128)(2,1)S(1)} %get-tuple-element.85), channel_id=1, source_target_pairs={{0,16},{16,32},{32,48},{48,0},{64,80},{80,96},{96,112},{112,64},{1... | collective-permute-start | bytes 589832 | tf_op jit(solution)/shard_map/ppermute | solution.py:351
  84.2 2.5 %collective-permute-start.20 = (bf16[3,128,256]{2,1,0:T(8,128)(2,1)S(1)}, bf16[3,128,256]{2,1,0:T(8,128)(2,1)S(1)}, u32[]{:S(2)}, u32[]{:S(2)}) collective-permute-start(bf16[3,128,256]{2,1,0:T(8,128)(2,1)S(1)} %get-tuple-element.86), channel_id=1, source_target_pairs={{0,32},{16,48},{32,0},{48,16},{64,96},{80,112},{96,64},{112,80},{1... | collective-permute-start | bytes 589832 | tf_op jit(solution)/shard_map/ppermute | solution.py:351
  86.7 4.3 %collective-permute-start.24 = (bf16[3,128,256]{2,1,0:T(8,128)(2,1)S(1)}, bf16[3,128,256]{2,1,0:T(8,128)(2,1)S(1)}, u32[]{:S(2)}, u32[]{:S(2)}) collective-permute-start(bf16[3,128,256]{2,1,0:T(8,128)(2,1)S(1)} %sum_over_z.2.after), channel_id=1, source_target_pairs={{0,0},{1,15},{2,64},{3,79},{4,4},{5,11},{6,68},{7,75},{8,6},{9,9},... | collective-permute-start | bytes 589832 | tf_op jit(solution)/shard_map/ppermute | solution.py:344
  90.9 1.3 %collective-permute-start.25 = (bf16[3,128,256]{2,1,0:T(8,128)(2,1)S(1)}, bf16[3,128,256]{2,1,0:T(8,128)(2,1)S(1)}, u32[]{:S(2)}, u32[]{:S(2)}) collective-permute-start(bf16[3,128,256]{2,1,0:T(8,128)(2,1)S(1)} %sum_over_z.2.after), channel_id=1, source_target_pairs={{64,0},{65,15},{66,64},{67,79},{68,4},{69,11},{70,68},{71,75},{72,... | collective-permute-start | bytes 589832 | tf_op jit(solution)/shard_map/ppermute | solution.py:344
  92.3 3.3 %collective-permute-done.20.two = bf16[3,128,256]{2,1,0:T(8,128)(2,1)S(1)} collective-permute-done((bf16[3,128,256]{2,1,0:T(8,128)(2,1)S(1)}, bf16[3,128,256]{2,1,0:T(8,128)(2,1)S(1)}, u32[]{:S(2)}, u32[]{:S(2)}) %collective-permute-start.20) | collective-permute-done | bytes 196640 | tf_op jit(solution)/shard_map/ppermute | solution.py:351
  95.9 5.9 %collective-permute-start.22 = (bf16[3,128,256]{2,1,0:T(8,128)(2,1)S(1)}, bf16[3,128,256]{2,1,0:T(8,128)(2,1)S(1)}, u32[]{:S(2)}, u32[]{:S(2)}) collective-permute-start(bf16[3,128,256]{2,1,0:T(8,128)(2,1)S(1)} %sum_over_z.3), channel_id=1, source_target_pairs={{0,1},{1,14},{2,65},{3,78},{4,5},{5,10},{6,69},{7,74},{8,7},{9,8},... | collective-permute-start | bytes 589832 | tf_op jit(solution)/shard_map/ppermute | solution.py:344
  101.8 0.7 collective-permute-start.23
  102.7 8.0 %collective-permute-done.22.near = bf16[3,128,256]{2,1,0:T(8,128)(2,1)S(1)} collective-permute-done((bf16[3,128,256]{2,1,0:T(8,128)(2,1)S(1)}, bf16[3,128,256]{2,1,0:T(8,128)(2,1)S(1)}, u32[]{:S(2)}, u32[]{:S(2)}) %collective-permute-start.22) | collective-permute-done | bytes 196640 | tf_op jit(solution)/shard_map/ppermute | solution.py:344
  110.7 0.8 merge_members.1
  (31 shorter events, 2.5 us)
Async XLA Ops:
  3.3 14.5 %collective-permute-start = (bf16[768,2304]{1,0:T(8,128)(2,1)S(1)}, bf16[768,2304]{1,0:T(8,128)(2,1)S(1)}, u32[]{:S(2)}, u32[]{:S(2)}) collective-permute-start(bf16[768,2304]{1,0:T(8,128)(2,1)S(1)} %load_to_swap.2.after), channel_id=1, source_target_pairs={{0,2},{2,0},{4,6},{6,4},{8,10},{10,8},{12,14},{14,12},{1,3},{3,1},... | collective-permute-start | bytes 10616840 | tf_op jit(solution)/shard_map/ppermute | solution.py:324
  7.6 5.2 %copy-start = (bf16[2,1024,256]{2,1,0:T(8,128)(2,1)S(1)}, bf16[2,1024,256]{2,1,0:T(8,128)(2,1)}, u32[]{:S(2)}) copy-start(bf16[2,1024,256]{2,1,0:T(8,128)(2,1)} %param.5) | copy-start | bytes 3145732
  9.6 12.1 %collective-permute-start.3 = (bf16[4,768,512]{2,1,0:T(8,128)(2,1)S(1)}, bf16[4,768,512]{2,1,0:T(8,128)(2,1)S(1)}, u32[]{:S(2)}, u32[]{:S(2)}) collective-permute-start(bf16[4,768,512]{2,1,0:T(8,128)(2,1)S(1)} %load_to_swap.3.after), channel_id=1, source_target_pairs={{0,2},{2,0},{4,6},{6,4},{8,10},{10,8},{12,14},{14,12},{1,3},{3,1},... | collective-permute-start | bytes 9437192 | tf_op jit(solution)/shard_map/ppermute | solution.py:324
  9.7 32.4 %collective-permute-start.1 = (bf16[2,832,256]{2,1,0:T(8,128)(2,1)S(1)}, bf16[2,832,256]{2,1,0:T(8,128)(2,1)S(1)}, u32[]{:S(2)}, u32[]{:S(2)}) collective-permute-start(bf16[2,832,256]{2,1,0:T(8,128)(2,1)S(1)} %get-tuple-element.49), channel_id=1, source_target_pairs={{0,1},{1,0},{2,3},{3,2},{4,5},{5,4},{6,7},{7,6},{8,9},{9,8},{10,11... | collective-permute-start | bytes 2555912 | tf_op jit(solution)/shard_map/ppermute | solution.py:327
  12.8 33.8 %collective-permute-start.7 = (bf16[2,1024,256]{2,1,0:T(8,128)(2,1)S(1)}, bf16[2,1024,256]{2,1,0:T(8,128)(2,1)S(1)}, u32[]{:S(2)}, u32[]{:S(2)}) collective-permute-start(bf16[2,1024,256]{2,1,0:T(8,128)(2,1)S(1)} %copy-done), channel_id=1, source_target_pairs={{0,0},{1,2},{2,12},{3,14},{4,4},{5,6},{6,8},{7,10},{8,9},{9,11},{1... | collective-permute-start | bytes 3145736 | tf_op jit(solution)/shard_map/ppermute | solution.py:381
  19.0 14.1 %collective-permute-start.2 = (bf16[2,256,512]{2,1,0:T(8,128)(2,1)S(1)}, bf16[2,256,512]{2,1,0:T(8,128)(2,1)S(1)}, u32[]{:S(2)}, u32[]{:S(2)}) collective-permute-start(bf16[2,256,512]{2,1,0:T(8,128)(2,1)S(1)} %get-tuple-element.53), channel_id=1, source_target_pairs={{0,4},{2,6},{4,0},{6,2},{8,12},{10,14},{12,8},{14,10},{1,5},{3,7},... | collective-permute-start | bytes 1572872 | tf_op jit(solution)/shard_map/ppermute | solution.py:330
  22.9 18.0 %collective-permute-start.5 = (bf16[2,256,512]{2,1,0:T(8,128)(2,1)S(1)}, bf16[2,256,512]{2,1,0:T(8,128)(2,1)S(1)}, u32[]{:S(2)}, u32[]{:S(2)}) collective-permute-start(bf16[2,256,512]{2,1,0:T(8,128)(2,1)S(1)} %get-tuple-element.60), channel_id=1, source_target_pairs={{0,4},{2,6},{4,0},{6,2},{8,12},{10,14},{12,8},{14,10},{1,5},{3,7},... | collective-permute-start | bytes 1572872 | tf_op jit(solution)/shard_map/ppermute | solution.py:330
  33.8 8.1 %collective-permute-start.4 = (bf16[256,512]{1,0:T(8,128)(2,1)S(1)}, bf16[256,512]{1,0:T(8,128)(2,1)S(1)}, u32[]{:S(2)}, u32[]{:S(2)}) collective-permute-start(bf16[256,512]{1,0:T(8,128)(2,1)S(1)} %get-tuple-element.59), channel_id=1, source_target_pairs={{0,12},{2,14},{4,8},{6,10},{8,4},{10,6},{12,0},{14,2},{1,13},{3,15... | collective-permute-start | bytes 786440 | tf_op jit(solution)/shard_map/ppermute | solution.py:330
  42.2 4.9 %collective-permute-start.6 = (bf16[768,256]{1,0:T(8,128)(2,1)S(1)}, bf16[768,256]{1,0:T(8,128)(2,1)S(1)}, u32[]{:S(2)}, u32[]{:S(2)}) collective-permute-start(bf16[768,256]{1,0:T(8,128)(2,1)S(1)} %get-tuple-element.63), channel_id=1, source_target_pairs={{0,2},{2,0},{4,6},{6,4},{8,10},{10,8},{12,14},{14,12},{1,3},{3,1},... | collective-permute-start | bytes 1179656 | tf_op jit(solution)/shard_map/ppermute | solution.py:324
  43.3 9.9 %collective-permute-start.9 = (bf16[256,512]{1,0:T(8,128)(2,1)S(1)}, bf16[256,512]{1,0:T(8,128)(2,1)S(1)}, u32[]{:S(2)}, u32[]{:S(2)}) collective-permute-start(bf16[256,512]{1,0:T(8,128)(2,1)S(1)} %get-tuple-element.67), channel_id=1, source_target_pairs={{0,12},{2,14},{4,8},{6,10},{8,4},{10,6},{12,0},{14,2},{1,13},{3,15... | collective-permute-start | bytes 786440 | tf_op jit(solution)/shard_map/ppermute | solution.py:330
  46.7 7.9 %collective-permute-start.11 = (bf16[2,512,256]{2,1,0:T(8,128)(2,1)S(1)}, bf16[2,512,256]{2,1,0:T(8,128)(2,1)S(1)}, u32[]{:S(2)}, u32[]{:S(2)}) collective-permute-start(bf16[2,512,256]{2,1,0:T(8,128)(2,1)S(1)} %get-tuple-element.73), channel_id=1, source_target_pairs={{0,2},{2,0},{4,6},{6,4},{8,10},{10,8},{12,14},{14,12},{1,3},{3,1},... | collective-permute-start | bytes 1572872 | tf_op jit(solution)/shard_map/ppermute | solution.py:324
  49.1 13.6 %collective-permute-start.8 = (bf16[2,256,512]{2,1,0:T(8,128)(2,1)S(1)}, bf16[2,256,512]{2,1,0:T(8,128)(2,1)S(1)}, u32[]{:S(2)}, u32[]{:S(2)}) collective-permute-start(bf16[2,256,512]{2,1,0:T(8,128)(2,1)S(1)} %get-tuple-element.66), channel_id=1, source_target_pairs={{0,4},{2,6},{4,0},{6,2},{8,12},{10,14},{12,8},{14,10},{1,5},{3,7},... | collective-permute-start | bytes 1572872 | tf_op jit(solution)/shard_map/ppermute | solution.py:330
  51.2 19.5 %collective-permute-start.13 = (bf16[2,256,512]{2,1,0:T(8,128)(2,1)S(1)}, bf16[2,256,512]{2,1,0:T(8,128)(2,1)S(1)}, u32[]{:S(2)}, u32[]{:S(2)}) collective-permute-start(bf16[2,256,512]{2,1,0:T(8,128)(2,1)S(1)} %get-tuple-element.77), channel_id=1, source_target_pairs={{0,12},{2,14},{4,8},{6,10},{8,4},{10,6},{12,0},{14,2},{1,13},{3,15... | collective-permute-start | bytes 1572872 | tf_op jit(solution)/shard_map/ppermute | solution.py:330
  53.8 1.9 %collective-permute-start.10 = (bf16[256,512]{1,0:T(8,128)(2,1)S(1)}, bf16[256,512]{1,0:T(8,128)(2,1)S(1)}, u32[]{:S(2)}, u32[]{:S(2)}) collective-permute-start(bf16[256,512]{1,0:T(8,128)(2,1)S(1)} %get-tuple-element.72), channel_id=1, source_target_pairs={{0,2},{2,0},{4,6},{6,4},{8,10},{10,8},{12,14},{14,12},{1,3},{3,1},... | collective-permute-start | bytes 786440 | tf_op jit(solution)/shard_map/ppermute | solution.py:324
  56.4 9.3 %collective-permute-start.14 = (bf16[3,128,256]{2,1,0:T(8,128)(2,1)S(1)}, bf16[3,128,256]{2,1,0:T(8,128)(2,1)S(1)}, u32[]{:S(2)}, u32[]{:S(2)}) collective-permute-start(bf16[3,128,256]{2,1,0:T(8,128)(2,1)S(1)} %get-tuple-element.78), channel_id=1, source_target_pairs={{0,16},{16,32},{32,48},{48,0},{64,80},{80,96},{96,112},{112,64},{1... | collective-permute-start | bytes 589832 | tf_op jit(solution)/shard_map/ppermute | solution.py:351
  58.1 12.2 %collective-permute-start.15 = (bf16[3,128,256]{2,1,0:T(8,128)(2,1)S(1)}, bf16[3,128,256]{2,1,0:T(8,128)(2,1)S(1)}, u32[]{:S(2)}, u32[]{:S(2)}) collective-permute-start(bf16[3,128,256]{2,1,0:T(8,128)(2,1)S(1)} %get-tuple-element.79), channel_id=1, source_target_pairs={{0,32},{16,48},{32,0},{48,16},{64,96},{80,112},{96,64},{112,80},{1... | collective-permute-start | bytes 589832 | tf_op jit(solution)/shard_map/ppermute | solution.py:351
  61.5 8.9 %collective-permute-start.16 = (bf16[3,128,256]{2,1,0:T(8,128)(2,1)S(1)}, bf16[3,128,256]{2,1,0:T(8,128)(2,1)S(1)}, u32[]{:S(2)}, u32[]{:S(2)}) collective-permute-start(bf16[3,128,256]{2,1,0:T(8,128)(2,1)S(1)} %get-tuple-element.80), channel_id=1, source_target_pairs={{0,48},{16,0},{32,16},{48,32},{64,112},{80,64},{96,80},{112,96},{1... | collective-permute-start | bytes 589832 | tf_op jit(solution)/shard_map/ppermute | solution.py:351
  63.4 8.1 %collective-permute-start.12 = (bf16[256,512]{1,0:T(8,128)(2,1)S(1)}, bf16[256,512]{1,0:T(8,128)(2,1)S(1)}, u32[]{:S(2)}, u32[]{:S(2)}) collective-permute-start(bf16[256,512]{1,0:T(8,128)(2,1)S(1)} %get-tuple-element.76), channel_id=1, source_target_pairs={{0,12},{2,14},{4,8},{6,10},{8,4},{10,6},{12,0},{14,2},{1,13},{3,15... | collective-permute-start | bytes 786440 | tf_op jit(solution)/shard_map/ppermute | solution.py:330
  71.4 6.7 %collective-permute-start.17 = (bf16[256,512]{1,0:T(8,128)(2,1)S(1)}, bf16[256,512]{1,0:T(8,128)(2,1)S(1)}, u32[]{:S(2)}, u32[]{:S(2)}) collective-permute-start(bf16[256,512]{1,0:T(8,128)(2,1)S(1)} %get-tuple-element.82), channel_id=1, source_target_pairs={{0,4},{2,6},{4,0},{6,2},{8,12},{10,14},{12,8},{14,10},{1,5},{3,7},... | collective-permute-start | bytes 786440 | tf_op jit(solution)/shard_map/ppermute | solution.py:330
  78.7 3.4 %collective-permute-start.18 = (bf16[256,512]{1,0:T(8,128)(2,1)S(1)}, bf16[256,512]{1,0:T(8,128)(2,1)S(1)}, u32[]{:S(2)}, u32[]{:S(2)}) collective-permute-start(bf16[256,512]{1,0:T(8,128)(2,1)S(1)} %get-tuple-element.84), channel_id=1, source_target_pairs={{0,2},{2,0},{4,6},{6,4},{8,10},{10,8},{12,14},{14,12},{1,3},{3,1},... | collective-permute-start | bytes 786440 | tf_op jit(solution)/shard_map/ppermute | solution.py:324
  82.8 9.4 %collective-permute-start.19 = (bf16[3,128,256]{2,1,0:T(8,128)(2,1)S(1)}, bf16[3,128,256]{2,1,0:T(8,128)(2,1)S(1)}, u32[]{:S(2)}, u32[]{:S(2)}) collective-permute-start(bf16[3,128,256]{2,1,0:T(8,128)(2,1)S(1)} %get-tuple-element.85), channel_id=1, source_target_pairs={{0,16},{16,32},{32,48},{48,0},{64,80},{80,96},{96,112},{112,64},{1... | collective-permute-start | bytes 589832 | tf_op jit(solution)/shard_map/ppermute | solution.py:351
  84.2 11.3 %collective-permute-start.20 = (bf16[3,128,256]{2,1,0:T(8,128)(2,1)S(1)}, bf16[3,128,256]{2,1,0:T(8,128)(2,1)S(1)}, u32[]{:S(2)}, u32[]{:S(2)}) collective-permute-start(bf16[3,128,256]{2,1,0:T(8,128)(2,1)S(1)} %get-tuple-element.86), channel_id=1, source_target_pairs={{0,32},{16,48},{32,0},{48,16},{64,96},{80,112},{96,64},{112,80},{1... | collective-permute-start | bytes 589832 | tf_op jit(solution)/shard_map/ppermute | solution.py:351
  86.7 8.9 %collective-permute-start.21 = (bf16[3,128,256]{2,1,0:T(8,128)(2,1)S(1)}, bf16[3,128,256]{2,1,0:T(8,128)(2,1)S(1)}, u32[]{:S(2)}, u32[]{:S(2)}) collective-permute-start(bf16[3,128,256]{2,1,0:T(8,128)(2,1)S(1)} %get-tuple-element.87), channel_id=1, source_target_pairs={{0,48},{16,0},{32,16},{48,32},{64,112},{80,64},{96,80},{112,96},{1... | collective-permute-start | bytes 589832 | tf_op jit(solution)/shard_map/ppermute | solution.py:351
  86.7 15.8 %collective-permute-start.24 = (bf16[3,128,256]{2,1,0:T(8,128)(2,1)S(1)}, bf16[3,128,256]{2,1,0:T(8,128)(2,1)S(1)}, u32[]{:S(2)}, u32[]{:S(2)}) collective-permute-start(bf16[3,128,256]{2,1,0:T(8,128)(2,1)S(1)} %sum_over_z.2.after), channel_id=1, source_target_pairs={{0,0},{1,15},{2,64},{3,79},{4,4},{5,11},{6,68},{7,75},{8,6},{9,9},... | collective-permute-start | bytes 589832 | tf_op jit(solution)/shard_map/ppermute | solution.py:344
  90.9 11.6 %collective-permute-start.25 = (bf16[3,128,256]{2,1,0:T(8,128)(2,1)S(1)}, bf16[3,128,256]{2,1,0:T(8,128)(2,1)S(1)}, u32[]{:S(2)}, u32[]{:S(2)}) collective-permute-start(bf16[3,128,256]{2,1,0:T(8,128)(2,1)S(1)} %sum_over_z.2.after), channel_id=1, source_target_pairs={{64,0},{65,15},{66,64},{67,79},{68,4},{69,11},{70,68},{71,75},{72,... | collective-permute-start | bytes 589832 | tf_op jit(solution)/shard_map/ppermute | solution.py:344
  95.9 14.9 %collective-permute-start.22 = (bf16[3,128,256]{2,1,0:T(8,128)(2,1)S(1)}, bf16[3,128,256]{2,1,0:T(8,128)(2,1)S(1)}, u32[]{:S(2)}, u32[]{:S(2)}) collective-permute-start(bf16[3,128,256]{2,1,0:T(8,128)(2,1)S(1)} %sum_over_z.3), channel_id=1, source_target_pairs={{0,1},{1,14},{2,65},{3,78},{4,5},{5,10},{6,69},{7,74},{8,7},{9,8},... | collective-permute-start | bytes 589832 | tf_op jit(solution)/shard_map/ppermute | solution.py:344
  101.8 8.9 %collective-permute-start.23 = (bf16[3,128,256]{2,1,0:T(8,128)(2,1)S(1)}, bf16[3,128,256]{2,1,0:T(8,128)(2,1)S(1)}, u32[]{:S(2)}, u32[]{:S(2)}) collective-permute-start(bf16[3,128,256]{2,1,0:T(8,128)(2,1)S(1)} %sum_over_z.3), channel_id=1, source_target_pairs={{64,1},{65,14},{66,65},{67,78},{68,5},{69,10},{70,69},{71,74},{72,... | collective-permute-start | bytes 589832 | tf_op jit(solution)/shard_map/ppermute | solution.py:344

commit v7 on v6

--- a/solution.py
+++ b/solution.py
@@ -108,19 +108,7 @@
     return copies
 
 
-def load_grads_kernel(g_ref, g_out, g_own_out, sem):
-    core = where_am_i()[1]
-    loads = [
-        pltpu.make_async_copy(g_ref, g_out.at[:, pl.ds(0, g_ref.shape[1])], sem.at[0]),
-        pltpu.make_async_copy(g_ref.at[core], g_own_out, sem.at[1]),
-    ]
-    for copy in loads:
-        copy.start()
-    for copy in loads:
-        copy.wait()
-
-
-def load_first_kernel(x_ref, g_ref, after, out, sem, g_sem):
+def load_first_kernel(x_ref, g_ref, out, sem, g_sem):
     core = where_am_i()[1]
     wide = x_ref.shape[2] // 8
     copies = [pltpu.make_async_copy(g_ref.at[1 - core], out.at[:, pl.ds(4 * wide, g_ref.shape[2])], g_sem)]
@@ -140,11 +128,9 @@
         copy.wait()
 
 
-def pick_grads_kernel(g_ref, after, kept_out, sent_out):
-    core = where_am_i()[1]
-    rows = kept_out.shape[0]
-    kept_out[...] = g_ref[core, :rows]
-    sent_out[...] = g_ref[1 - core, :rows]
+def pair_kernel(own, got, after, out):
+    outs = own.shape[1]
+    out[0], out[1] = own[...], got[:, got.shape[1] - outs :]
 
 
 def own_tokens(copies, x_out, gt_ref, part_out):
@@ -153,9 +139,13 @@
         part_out[s] = fisher_block(x_out[s], gt_ref)
 
 
-def own_first_kernel(x_ref, g_ref, after, x_out, gt_out, part_out, sem):
-    copies = load_inputs(where_am_i()[1], 0, x_ref, x_out, sem)
-    gt_out[...] = squared_transposed(g_ref[...])
+def own_first_kernel(x_ref, g_ref, after, x_out, g_out, gt_out, part_out, sem, g_sem):
+    core = where_am_i()[1]
+    load = pltpu.make_async_copy(g_ref.at[core], g_out, g_sem)
+    load.start()
+    copies = load_inputs(core, 0, x_ref, x_out, sem)
+    load.wait()
+    gt_out[...] = squared_transposed(g_out[...])
     own_tokens(copies, x_out, gt_out, part_out)
 
 
@@ -184,10 +174,10 @@
         put(s, part_ref[s] + fisher_block(x_ref[s], gt_ref), sent_out, kept_out)
 
 
-def both_first_kernel(xa_ref, xb_ref, ga_ref, gb_ref, after, sent_out, kept_out, gta_out, gtb_out):
+def both_first_kernel(xa_ref, xb_ref, g_ref, after, sent_out, kept_out, gta_out, gtb_out):
     wide = kept_out.shape[2]
-    gta_out[...] = squared_transposed(ga_ref[...])
-    gtb_out[...] = squared_transposed(gb_ref[...])
+    gta_out[...] = squared_transposed(g_ref[0])
+    gtb_out[...] = squared_transposed(g_ref[1])
     for s in range(4):
         block = fisher_block(xb_ref[:, s * wide : (s + 1) * wide], gtb_out)
         put(s, fisher_block(xa_ref[s], gta_out) + block, sent_out, kept_out)
@@ -232,16 +222,16 @@
     return words[0].astype(F32) + words[1].astype(F32), decode_fine(words[2])
 
 
-def weigh_kernel(phase, own, other, w_a, w_b, after, one_out, two_out, three_out, sums_out):
+def weigh_kernel(phase, own, other, w_own, w_other, after, one_out, two_out, three_out, sums_out):
     _, core, half, _, z = where_am_i()
     part = own.shape[1] // Z
-    first = (core ^ half ^ phase) == 0
+    mine = (core ^ half ^ phase) == 0
     for d, out in ((2, two_out), (1, one_out), (3, three_out), (0, sums_out)):
         cols = pl.ds(pl.multiple_of((z + d) % Z * part, part), part)
         weighted = total = 0.0
         for values, m in ((own[:, cols], core), (decode_fine(other[:, cols]), 1 - core)):
             fisher = values.T
-            weight = jnp.where(first, w_a[m, cols, :].astype(F32), w_b[m, cols, :].astype(F32))
+            weight = jnp.where(mine, w_own[m, cols, :].astype(F32), w_other[m, cols, :].astype(F32))
             weighted += fisher * weight
             total += fisher
         if d == 0:
@@ -282,12 +272,12 @@
     return 2 * (x % 2) if x // 2 == half else 2 * ((3 - x) % 2) + 1
 
 
-def weight_pairs():
+def weight_pairs(phase):
     pairs = []
     for tok in range(X * CORES):
         half, local = divmod(tok, 4)
-        for col in range(2):
-            pairs.append((tok * 2 + col, (keeper(local, half) * 2 + col) * 2 + half))
+        col = half ^ phase
+        pairs.append((tok * 2 + col, (keeper(local, half) * 2 + col) * 2 + half))
     return pairs
 
 
@@ -343,28 +333,33 @@
     def results(phase, sums):
         return [lax.ppermute(sums, ("member", "tok", "col"), result_pairs(phase, y_lo)) for y_lo in range(2)]
 
-    def weigh(phase, own, other, after):
+    def bring_weights(phase, after):
+        arrived = lax.ppermute(weights, ("tok", "col"), weight_pairs(phase))
+        half_shape = ((2, weights.shape[1] // 2, outs), BF16)
+        own, send = call(split_kernel, "split_weights", [half_shape, half_shape], [], [arrived, after])
+        return own, swap_cores(send)
+
+    def weigh(phase, own, other, moved, after):
         one, two, three, own_sums = call(
             lambda *refs: weigh_kernel(phase, *refs), "weigh_members", [words] * 3 + [sums], [], [own, other, *moved, after]
         )
         send = ((1, one), (2, two), (3, three))
         return [lax.ppermute(v, "member", z_pairs(d)) for d, v in send] + [own_sums]
 
-    g_pair, g_own = call(
-        load_grads_kernel, "load_grads", [((2, tokens + 64, outs), BF16), g_shape], [grads], [], [dma((2,))]
-    )
-    g_other = swap_cols(g_pair)
     x_send0 = call(
-        load_first_kernel, "load_to_swap", ((tokens, 4 * wide + outs), BF16), [inputs, grads], [g_own], [dma((4,)), dma]
+        load_first_kernel, "load_to_swap", ((tokens, 4 * wide + outs), BF16), [inputs, grads], [], [dma((4,)), dma]
     )
     x_got0 = swap_cores(x_send0)
-    x_own0, gt_own, part0 = call(
-        own_first_kernel, "fisher_of_own_tokens", [x_shape, gt_shape, part_shape], [inputs], [g_own, x_send0], [dma((4,))]
+    x_own0, g_own, gt_own, part0 = call(
+        own_first_kernel, "fisher_of_own_tokens", [x_shape, g_shape, gt_shape, part_shape], [inputs, grads], [x_send0],
+        [dma((4,)), dma],
     )
     x_send1 = call(load_second_kernel, "load_to_swap", x_shape, [inputs], [gt_own], [dma((4,))])
     x_got1 = swap_cores(x_send1)
+    g_pair = call(pair_kernel, "pair_grads", ((2, tokens, outs), BF16), [], [g_own, x_got0, x_send1])
+    g_other = swap_cols(g_pair)
     sent, kept00, gt_got = call(
-        add_first_kernel, "fisher_of_both_cores", [sent_shape, kept_shape, gt_shape], [], [x_got0, part0, x_send1]
+        add_first_kernel, "fisher_of_both_cores", [sent_shape, kept_shape, gt_shape], [], [x_got0, part0, g_pair]
     )
     swap00 = swap_x(1, sent)
     x_own1, part1 = call(
@@ -375,33 +370,29 @@
     )
     swap01 = swap_x(1, sent)
     part00 = middle(3, swap00, kept00, kept01)
-    part01 = middle(3, swap01, kept01, part00[0])
-    settled0 = settle(part00, part01[0])
-
-    arrived = lax.ppermute(weights, ("tok", "col"), weight_pairs())
-    rows = weights.shape[1] // 2
-    w_own, w_send = call(split_kernel, "split_weights", [((2, rows, outs), BF16)] * 2, [], [arrived, settled0])
-    moved = (w_own, swap_cores(w_send))
-
-    g_kept, g_sent = call(pick_grads_kernel, "pick_grads", [g_shape, g_shape], [], [g_other, settled0])
+    w0 = bring_weights(0, part00[0])
+
     sent, kept10, gt_own, gt_got = call(
         both_first_kernel, "fisher_of_other_grads", [sent_shape, kept_shape, gt_shape, gt_shape], [],
-        [x_own0, x_got0, g_kept, swap_cores(g_sent), w_own],
+        [x_own0, x_got0, g_other, w0[0]],
     )
     swap10 = swap_x(1, sent)
+    part01 = middle(3, swap01, kept01, kept10)
     sent, kept11 = call(
         both_second_kernel, "fisher_of_other_grads", [sent_shape, kept_shape], [],
-        [x_own1, x_got1, gt_own, gt_got, kept10],
+        [x_own1, x_got1, gt_own, gt_got, part01[0]],
     )
     swap11 = swap_x(3, sent)
+
+    settled0 = settle(part00, kept11)
     own0, other0 = join(settled0, part01, kept11)
-    words0 = weigh(0, own0, other0, kept11)
+    words0 = weigh(0, own0, other0, w0, own0)
     part10 = middle(3, swap10, kept10, words0[3])
     first = call(sum_kernel, "sum_over_z", words, [], [*words0, part10[0]])
     part11 = middle(1, swap11, kept11, first)
-
     own1, other1 = join(settle(part10, part11[0]), part11, first)
-    words1 = weigh(1, own1, other1, own1)
+    w1 = bring_weights(1, own1)
+    words1 = weigh(1, own1, other1, w1, w1[0])
     met = call(meet_kernel, "meet_over_y", sums, [], [*results(0, first), own1])
     second = call(sum_kernel, "sum_over_z", words, [], [*words1, own1])
     near, far = results(1, second)

time: 112 us -> 119 us (1.062)
  waiting for transfers between devices: 41.5 us -> 55.9 us
  starting transfers between devices: 44.9 us -> 38 us
    ppermute x8, waiting for transfers between devices: 23.2 us -> 34.4 us  [swap_x(): return lax.ppermute(sent, 'tok', x_pairs(flip))]
    ppermute x8, starting transfers between devices: 9.03 us -> 5.75 us  [swap_x(): return lax.ppermute(sent, 'tok', x_pairs(flip))]
    ppermute x1, starting transfers between devices: 3.07 us -> 0.09 us  [swap_cols(): return lax.ppermute(send, 'col', [(0, 1), (1, 0)])]
    ppermute x6, waiting for transfers between devices: 7.89 us -> 10.1 us  [weigh(): return [lax.ppermute(v, 'member', z_pairs(d)) for d, v in send] + [own_sums]]
    ppermute x4, starting transfers between devices: 12.2 us -> 10.9 us  [results(): lax.ppermute(sums, ('member', 'tok', 'col'), result_pairs(phase, y_lo))]
    ppermute x1 -> x2, starting transfers between devices: 4.96 us -> 6.11 us  [bring_weights(): arrived = lax.ppermute(weights, ('tok', 'col'), weight_pairs(phase))]
  transfers between devices with their start and end apart: 26 -> 27, of which waited for: 11 -> 12; matrix products, arithmetic and copies ran while one was open for 0% -> 0% of each run, Pallas kernels for 17% -> 17%
where the time goes in v7:
time: 119 us; the launch traced here: 118 us
  waiting for transfers between devices  55.9 us (47%)
  starting transfers between devices  38 us (32%)
  Pallas kernels  24.1 us (20%)
    ppermute x8, waiting for transfers between devices, swap_x(): return lax.ppermute(sent, 'tok', x_pairs(flip))  34.4 us
    pallas_call x24, Pallas kernels, call(): pl.pallas_call(kernel, out_shape=shapes, in_specs=[HBM] * len(hbm) + [VME...  23.2 us
    ppermute x4, starting transfers between devices, results(): lax.ppermute(sums, ('member', 'tok', 'col'), result_pairs(phase, y_lo))  10.9 us
    ppermute x6, waiting for transfers between devices, weigh(): return [lax.ppermute(v, 'member', z_pairs(d)) for d, v in send] + [own_sums]  10.1 us
    ppermute x6, starting transfers between devices, weigh(): return [lax.ppermute(v, 'member', z_pairs(d)) for d, v in send] + [own_sums]  9.58 us
    ppermute x4, waiting for transfers between devices, results(): lax.ppermute(sums, ('member', 'tok', 'col'), result_pairs(phase, y_lo))  8.05 us
    ppermute x2, starting transfers between devices, bring_weights(): arrived = lax.ppermute(weights, ('tok', 'col'), weight_pairs(phase))  6.11 us
    ppermute x8, starting transfers between devices, swap_x(): return lax.ppermute(sent, 'tok', x_pairs(flip))  5.75 us
  transfers between devices with their start and end apart: 27, of which 12 were waited for; matrix products, arithmetic and copies ran while one was open for 0% of the time, Pallas kernels for 17%

profile of v7, /device:TPU:1, one launch (start us, length us, event | category | flops | bytes accessed | tf_op | source)
XLA Modules:
  0.0 118.3 jit_solution(285861709390293254)
XLA Ops:
  0.0 2.0 %load_to_swap.2.after = bf16[768,2304]{1,0:T(8,128)(2,1)S(1)} custom-call(bf16[2,768,4096]{2,1,0:T(8,128)(2,1)} %x_ref.7, bf16[2,768,256]{2,1,0:T(8,128)(2,1)} %g_ref.3), custom_call_target="tpu_custom_call" | custom-call | flops 1 | bytes 1 | tf_op jit(solution)/shard_map/load_to_swap/pallas_call | solution.py:67
  2.0 1.5 %collective-permute-start = (bf16[768,2304]{1,0:T(8,128)(2,1)S(1)}, bf16[768,2304]{1,0:T(8,128)(2,1)S(1)}, u32[]{:S(2)}, u32[]{:S(2)}) collective-permute-start(bf16[768,2304]{1,0:T(8,128)(2,1)S(1)} %load_to_swap.2.after), channel_id=1, source_target_pairs={{0,2},{2,0},{4,6},{6,4},{8,10},{10,8},{12,14},{14,12},{1,3},{3,1},... | collective-permute-start | bytes 10616840 | tf_op jit(solution)/shard_map/ppermute | solution.py:314
  3.5 3.2 %fisher_of_own_tokens.2 = (bf16[4,768,512]{2,1,0:T(8,128)(2,1)S(1)}, bf16[768,256]{1,0:T(8,128)(2,1)S(1)}, bf16[256,768]{1,0:T(8,128)(2,1)S(1)}, f32[4,256,512]{2,1,0:T(8,128)S(1)}) custom-call(bf16[2,768,4096]{2,1,0:T(8,128)(2,1)} %x_ref.7, bf16[2,768,256]{2,1,0:T(8,128)(2,1)} %g_ref.3, bf16[768,2304]{1,0:T(8,128)(2,1)S(1)} %load_to_swap.2.after), custom_call_target="tpu_custom_call" | custom-call | flops 1 | bytes 1 | tf_op jit(solution)/shard_map/fisher_of_own_tokens/pallas_call | solution.py:67
  6.8 2.0 %load_to_swap.3.after = bf16[4,768,512]{2,1,0:T(8,128)(2,1)S(1)} custom-call(bf16[2,768,4096]{2,1,0:T(8,128)(2,1)} %x_ref.7, bf16[256,768]{1,0:T(8,128)(2,1)S(1)} %get-tuple-element.48.after.gt_ref), custom_call_target="tpu_custom_call" | custom-call | flops 1 | bytes 1 | tf_op jit(solution)/shard_map/load_to_swap/pallas_call | solution.py:67
  8.9 4.8 %collective-permute-start.2 = (bf16[2,1024,256]{2,1,0:T(8,128)(2,1)S(1)}, bf16[2,1024,256]{2,1,0:T(8,128)(2,1)S(1)}, u32[]{:S(2)}, u32[]{:S(2)}) collective-permute-start(bf16[2,1024,256]{2,1,0:T(8,128)(2,1)S(1)} %copy-done), channel_id=1, source_target_pairs={{0,0},{2,12},{4,4},{6,8},{9,11},{11,7},{13,15},{15,3},{16,16},{18,... | collective-permute-start | bytes 3145736 | tf_op jit(solution)/shard_map/ppermute | solution.py:337
  13.9 1.2 fisher_of_both_cores.2
  15.1 0.7 collective-permute-start.3
  15.8 2.7 %fisher_of_own_tokens.3 = (bf16[4,768,512]{2,1,0:T(8,128)(2,1)S(1)}, f32[4,256,512]{2,1,0:T(8,128)S(1)}) custom-call(bf16[2,768,4096]{2,1,0:T(8,128)(2,1)} %x_ref.7, bf16[256,768]{1,0:T(8,128)(2,1)S(1)} %get-tuple-element.48.after.gt_ref, f32[2,256,512]{2,1,0:T(8,128)S(1)} %get-tuple-element.50.after.kept_ref), custom_call_target="tpu_custom_call" | custom-call | flops 1 | bytes 1 | tf_op jit(solution)/shard_map/fisher_of_own_tokens/pallas_call | solution.py:67
  18.5 1.1 fisher_of_both_cores.3
  19.6 0.9 collective-permute-start.7
  20.6 8.6 %collective-permute-done.3.got_ref = bf16[2,256,512]{2,1,0:T(8,128)(2,1)S(1)} collective-permute-done((bf16[2,256,512]{2,1,0:T(8,128)(2,1)S(1)}, bf16[2,256,512]{2,1,0:T(8,128)(2,1)S(1)}, u32[]{:S(2)}, u32[]{:S(2)}) %collective-permute-start.3) | collective-permute-done | bytes 524320 | tf_op jit(solution)/shard_map/ppermute | solution.py:320
  29.1 0.7 fisher_over_first_swap.4
  29.9 1.7 %collective-permute-start.6 = (bf16[256,512]{1,0:T(8,128)(2,1)S(1)}, bf16[256,512]{1,0:T(8,128)(2,1)S(1)}, u32[]{:S(2)}, u32[]{:S(2)}) collective-permute-start(bf16[256,512]{1,0:T(8,128)(2,1)S(1)} %get-tuple-element.60), channel_id=1, source_target_pairs={{0,12},{2,14},{4,8},{6,10},{8,4},{10,6},{12,0},{14,2},{1,13},{3,15... | collective-permute-start | bytes 786440 | tf_op jit(solution)/shard_map/ppermute | solution.py:320
  31.5 1.3 %collective-permute-start.18 = (bf16[2,1024,256]{2,1,0:T(8,128)(2,1)S(1)}, bf16[2,1024,256]{2,1,0:T(8,128)(2,1)S(1)}, u32[]{:S(2)}, u32[]{:S(2)}) collective-permute-start(bf16[2,1024,256]{2,1,0:T(8,128)(2,1)S(1)} %copy-done), channel_id=1, source_target_pairs={{1,2},{3,14},{5,6},{7,10},{8,9},{10,5},{12,13},{14,1},{17,18},{19,... | collective-permute-start | bytes 3145736 | tf_op jit(solution)/shard_map/ppermute | solution.py:337
  32.9 1.9 %fisher_of_other_grads.2 = (bf16[2,256,512]{2,1,0:T(8,128)(2,1)S(1)}, f32[2,256,512]{2,1,0:T(8,128)S(1)}, bf16[256,768]{1,0:T(8,128)(2,1)S(1)}, bf16[256,768]{1,0:T(8,128)(2,1)S(1)}) custom-call(bf16[4,768,512]{2,1,0:T(8,128)(2,1)S(1)} %get-tuple-element.46.xa_ref, bf16[768,2304]{1,0:T(8,128)(2,1)S(1)} %collective-permute-done.got.x_ref.xb_ref, ...), custom_call_target="tpu_custom_call" | custom-call | flops 1 | bytes 1 | tf_op jit(solution)/shard_map/fisher_of_other_grads/pallas_call | solution.py:67
  34.9 5.5 %collective-permute-done.7.got_ref = bf16[2,256,512]{2,1,0:T(8,128)(2,1)S(1)} collective-permute-done((bf16[2,256,512]{2,1,0:T(8,128)(2,1)S(1)}, bf16[2,256,512]{2,1,0:T(8,128)(2,1)S(1)}, u32[]{:S(2)}, u32[]{:S(2)}) %collective-permute-start.7) | collective-permute-done | bytes 524320 | tf_op jit(solution)/shard_map/ppermute | solution.py:320
  40.4 0.7 fisher_over_first_swap.5
  41.1 1.7 %collective-permute-start.8 = (bf16[256,512]{1,0:T(8,128)(2,1)S(1)}, bf16[256,512]{1,0:T(8,128)(2,1)S(1)}, u32[]{:S(2)}, u32[]{:S(2)}) collective-permute-start(bf16[256,512]{1,0:T(8,128)(2,1)S(1)} %get-tuple-element.66), channel_id=1, source_target_pairs={{0,12},{2,14},{4,8},{6,10},{8,4},{10,6},{12,0},{14,2},{1,13},{3,15... | collective-permute-start | bytes 786440 | tf_op jit(solution)/shard_map/ppermute | solution.py:320
  42.8 1.8 %collective-permute-start.10 = (bf16[2,512,256]{2,1,0:T(8,128)(2,1)S(1)}, bf16[2,512,256]{2,1,0:T(8,128)(2,1)S(1)}, u32[]{:S(2)}, u32[]{:S(2)}) collective-permute-start(bf16[2,512,256]{2,1,0:T(8,128)(2,1)S(1)} %get-tuple-element.69), channel_id=1, source_target_pairs={{0,2},{2,0},{4,6},{6,4},{8,10},{10,8},{12,14},{14,12},{1,3},{3,1},... | collective-permute-start | bytes 1572872 | tf_op jit(solution)/shard_map/ppermute | solution.py:314
  44.6 1.9 %fisher_of_other_grads.3 = (bf16[2,256,512]{2,1,0:T(8,128)(2,1)S(1)}, f32[2,256,512]{2,1,0:T(8,128)S(1)}) custom-call(bf16[4,768,512]{2,1,0:T(8,128)(2,1)S(1)} %get-tuple-element.54.after.xa_ref, bf16[4,768,512]{2,1,0:T(8,128)(2,1)S(1)} %collective-permute-done.4.x_ref.xb_ref, bf16[256,768]{1,0:T(8,128)(2,1)S(1)} %get-tuple-element.61.gta_ref, ...), custom_call_target="tpu_custom_call" | custom-call | flops 1 | bytes 1 | tf_op jit(solution)/shard_map/fisher_of_other_grads/pallas_call | solution.py:67
  46.5 0.7 collective-permute-start.12
  47.4 13.8 %collective-permute-done.8.got = bf16[256,512]{1,0:T(8,128)(2,1)S(1)} collective-permute-done((bf16[256,512]{1,0:T(8,128)(2,1)S(1)}, bf16[256,512]{1,0:T(8,128)(2,1)S(1)}, u32[]{:S(2)}, u32[]{:S(2)}) %collective-permute-start.8) | collective-permute-done | bytes 262176 | tf_op jit(solution)/shard_map/ppermute | solution.py:320
  61.2 0.6 fisher_over_tokens.5
  61.9 1.5 %collective-permute-done.9.refs_1_ = bf16[256,512]{1,0:T(8,128)(2,1)S(1)} collective-permute-done((bf16[256,512]{1,0:T(8,128)(2,1)S(1)}, bf16[256,512]{1,0:T(8,128)(2,1)S(1)}, u32[]{:S(2)}, u32[]{:S(2)}) %collective-permute-start.9) | collective-permute-done | bytes 262176 | tf_op jit(solution)/shard_map/ppermute | solution.py:314
  63.4 0.7 weigh_members.2
  64.2 1.7 %collective-permute-start.13 = (bf16[3,128,256]{2,1,0:T(8,128)(2,1)S(1)}, bf16[3,128,256]{2,1,0:T(8,128)(2,1)S(1)}, u32[]{:S(2)}, u32[]{:S(2)}) collective-permute-start(bf16[3,128,256]{2,1,0:T(8,128)(2,1)S(1)} %get-tuple-element.74), channel_id=1, source_target_pairs={{0,16},{16,32},{32,48},{48,0},{64,80},{80,96},{96,112},{112,64},{1... | collective-permute-start | bytes 589832 | tf_op jit(solution)/shard_map/ppermute | solution.py:347
  65.9 3.3 %collective-permute-start.14 = (bf16[3,128,256]{2,1,0:T(8,128)(2,1)S(1)}, bf16[3,128,256]{2,1,0:T(8,128)(2,1)S(1)}, u32[]{:S(2)}, u32[]{:S(2)}) collective-permute-start(bf16[3,128,256]{2,1,0:T(8,128)(2,1)S(1)} %get-tuple-element.75), channel_id=1, source_target_pairs={{0,32},{16,48},{32,0},{48,16},{64,96},{80,112},{96,64},{112,80},{1... | collective-permute-start | bytes 589832 | tf_op jit(solution)/shard_map/ppermute | solution.py:347
  69.2 0.8 collective-permute-start.15
  69.9 0.7 fisher_over_first_swap.6
  70.7 2.5 %collective-permute-done.13.one = bf16[3,128,256]{2,1,0:T(8,128)(2,1)S(1)} collective-permute-done((bf16[3,128,256]{2,1,0:T(8,128)(2,1)S(1)}, bf16[3,128,256]{2,1,0:T(8,128)(2,1)S(1)}, u32[]{:S(2)}, u32[]{:S(2)}) %collective-permute-start.13) | collective-permute-done | bytes 196640 | tf_op jit(solution)/shard_map/ppermute | solution.py:347
  73.1 5.1 %collective-permute-done.14.two = bf16[3,128,256]{2,1,0:T(8,128)(2,1)S(1)} collective-permute-done((bf16[3,128,256]{2,1,0:T(8,128)(2,1)S(1)}, bf16[3,128,256]{2,1,0:T(8,128)(2,1)S(1)}, u32[]{:S(2)}, u32[]{:S(2)}) %collective-permute-start.14) | collective-permute-done | bytes 196640 | tf_op jit(solution)/shard_map/ppermute | solution.py:347
  78.7 0.7 fisher_over_first_swap.7
  79.5 2.0 %collective-permute-done.11.got = bf16[256,512]{1,0:T(8,128)(2,1)S(1)} collective-permute-done((bf16[256,512]{1,0:T(8,128)(2,1)S(1)}, bf16[256,512]{1,0:T(8,128)(2,1)S(1)}, u32[]{:S(2)}, u32[]{:S(2)}) %collective-permute-start.11) | collective-permute-done | bytes 262176 | tf_op jit(solution)/shard_map/ppermute | solution.py:320
  81.8 4.6 %collective-permute-done.16.got = bf16[256,512]{1,0:T(8,128)(2,1)S(1)} collective-permute-done((bf16[256,512]{1,0:T(8,128)(2,1)S(1)}, bf16[256,512]{1,0:T(8,128)(2,1)S(1)}, u32[]{:S(2)}, u32[]{:S(2)}) %collective-permute-start.16) | collective-permute-done | bytes 262176 | tf_op jit(solution)/shard_map/ppermute | solution.py:320
  86.3 0.6 fisher_over_tokens.7
  87.0 1.9 %collective-permute-start.19 = (bf16[2,512,256]{2,1,0:T(8,128)(2,1)S(1)}, bf16[2,512,256]{2,1,0:T(8,128)(2,1)S(1)}, u32[]{:S(2)}, u32[]{:S(2)}) collective-permute-start(bf16[2,512,256]{2,1,0:T(8,128)(2,1)S(1)} %get-tuple-element.82), channel_id=1, source_target_pairs={{0,2},{2,0},{4,6},{6,4},{8,10},{10,8},{12,14},{14,12},{1,3},{3,1},... | collective-permute-start | bytes 1572872 | tf_op jit(solution)/shard_map/ppermute | solution.py:314
  89.1 1.8 %collective-permute-done.17.refs_1_ = bf16[256,512]{1,0:T(8,128)(2,1)S(1)} collective-permute-done((bf16[256,512]{1,0:T(8,128)(2,1)S(1)}, bf16[256,512]{1,0:T(8,128)(2,1)S(1)}, u32[]{:S(2)}, u32[]{:S(2)}) %collective-permute-start.17) | collective-permute-done | bytes 262176 | tf_op jit(solution)/shard_map/ppermute | solution.py:314
  90.9 0.7 weigh_members.3
  91.6 1.1 collective-permute-start.20
  92.8 2.5 %collective-permute-start.21 = (bf16[3,128,256]{2,1,0:T(8,128)(2,1)S(1)}, bf16[3,128,256]{2,1,0:T(8,128)(2,1)S(1)}, u32[]{:S(2)}, u32[]{:S(2)}) collective-permute-start(bf16[3,128,256]{2,1,0:T(8,128)(2,1)S(1)} %get-tuple-element.84), channel_id=1, source_target_pairs={{0,32},{16,48},{32,0},{48,16},{64,96},{80,112},{96,64},{112,80},{1... | collective-permute-start | bytes 589832 | tf_op jit(solution)/shard_map/ppermute | solution.py:347
  95.5 4.8 %collective-permute-start.25 = (bf16[3,128,256]{2,1,0:T(8,128)(2,1)S(1)}, bf16[3,128,256]{2,1,0:T(8,128)(2,1)S(1)}, u32[]{:S(2)}, u32[]{:S(2)}) collective-permute-start(bf16[3,128,256]{2,1,0:T(8,128)(2,1)S(1)} %sum_over_z.2.after), channel_id=1, source_target_pairs={{0,0},{1,15},{2,64},{3,79},{4,4},{5,11},{6,68},{7,75},{8,6},{9,9},... | collective-permute-start | bytes 589832 | tf_op jit(solution)/shard_map/ppermute | solution.py:334
  100.3 1.3 %collective-permute-start.26 = (bf16[3,128,256]{2,1,0:T(8,128)(2,1)S(1)}, bf16[3,128,256]{2,1,0:T(8,128)(2,1)S(1)}, u32[]{:S(2)}, u32[]{:S(2)}) collective-permute-start(bf16[3,128,256]{2,1,0:T(8,128)(2,1)S(1)} %sum_over_z.2.after), channel_id=1, source_target_pairs={{64,0},{65,15},{66,64},{67,79},{68,4},{69,11},{70,68},{71,75},{72,... | collective-permute-start | bytes 589832 | tf_op jit(solution)/shard_map/ppermute | solution.py:334
  101.6 2.5 %collective-permute-done.21.two = bf16[3,128,256]{2,1,0:T(8,128)(2,1)S(1)} collective-permute-done((bf16[3,128,256]{2,1,0:T(8,128)(2,1)S(1)}, bf16[3,128,256]{2,1,0:T(8,128)(2,1)S(1)}, u32[]{:S(2)}, u32[]{:S(2)}) %collective-permute-start.21) | collective-permute-done | bytes 196640 | tf_op jit(solution)/shard_map/ppermute | solution.py:347
  104.1 0.3 sum_over_z.3
  104.5 4.1 %collective-permute-start.23 = (bf16[3,128,256]{2,1,0:T(8,128)(2,1)S(1)}, bf16[3,128,256]{2,1,0:T(8,128)(2,1)S(1)}, u32[]{:S(2)}, u32[]{:S(2)}) collective-permute-start(bf16[3,128,256]{2,1,0:T(8,128)(2,1)S(1)} %sum_over_z.3), channel_id=1, source_target_pairs={{0,1},{1,14},{2,65},{3,78},{4,5},{5,10},{6,69},{7,74},{8,7},{9,8},... | collective-permute-start | bytes 589832 | tf_op jit(solution)/shard_map/ppermute | solution.py:334
  108.5 0.7 collective-permute-start.24
  109.6 7.9 %collective-permute-done.23.near = bf16[3,128,256]{2,1,0:T(8,128)(2,1)S(1)} collective-permute-done((bf16[3,128,256]{2,1,0:T(8,128)(2,1)S(1)}, bf16[3,128,256]{2,1,0:T(8,128)(2,1)S(1)}, u32[]{:S(2)}, u32[]{:S(2)}) %collective-permute-start.23) | collective-permute-done | bytes 196640 | tf_op jit(solution)/shard_map/ppermute | solution.py:334
  117.5 0.8 merge_members.1
  (33 shorter events, 2.2 us)
Async XLA Ops:
  2.0 11.7 %collective-permute-start = (bf16[768,2304]{1,0:T(8,128)(2,1)S(1)}, bf16[768,2304]{1,0:T(8,128)(2,1)S(1)}, u32[]{:S(2)}, u32[]{:S(2)}) collective-permute-start(bf16[768,2304]{1,0:T(8,128)(2,1)S(1)} %load_to_swap.2.after), channel_id=1, source_target_pairs={{0,2},{2,0},{4,6},{6,4},{8,10},{10,8},{12,14},{14,12},{1,3},{3,1},... | collective-permute-start | bytes 10616840 | tf_op jit(solution)/shard_map/ppermute | solution.py:314
  6.7 2.2 %copy-start = (bf16[2,1024,256]{2,1,0:T(8,128)(2,1)S(1)}, bf16[2,1024,256]{2,1,0:T(8,128)(2,1)}, u32[]{:S(2)}) copy-start(bf16[2,1024,256]{2,1,0:T(8,128)(2,1)} %param.5) | copy-start | bytes 3145732
  8.8 9.7 %collective-permute-start.4 = (bf16[4,768,512]{2,1,0:T(8,128)(2,1)S(1)}, bf16[4,768,512]{2,1,0:T(8,128)(2,1)S(1)}, u32[]{:S(2)}, u32[]{:S(2)}) collective-permute-start(bf16[4,768,512]{2,1,0:T(8,128)(2,1)S(1)} %load_to_swap.3.after), channel_id=1, source_target_pairs={{0,2},{2,0},{4,6},{6,4},{8,10},{10,8},{12,14},{14,12},{1,3},{3,1},... | collective-permute-start | bytes 9437192 | tf_op jit(solution)/shard_map/ppermute | solution.py:314
  8.9 23.9 %collective-permute-start.2 = (bf16[2,1024,256]{2,1,0:T(8,128)(2,1)S(1)}, bf16[2,1024,256]{2,1,0:T(8,128)(2,1)S(1)}, u32[]{:S(2)}, u32[]{:S(2)}) collective-permute-start(bf16[2,1024,256]{2,1,0:T(8,128)(2,1)S(1)} %copy-done), channel_id=1, source_target_pairs={{0,0},{2,12},{4,4},{6,8},{9,11},{11,7},{13,15},{15,3},{16,16},{18,... | collective-permute-start | bytes 3145736 | tf_op jit(solution)/shard_map/ppermute | solution.py:337
  13.8 19.1 %collective-permute-start.1 = (bf16[2,768,256]{2,1,0:T(8,128)(2,1)S(1)}, bf16[2,768,256]{2,1,0:T(8,128)(2,1)S(1)}, u32[]{:S(2)}, u32[]{:S(2)}) collective-permute-start(bf16[2,768,256]{2,1,0:T(8,128)(2,1)S(1)} %pair_grads.1.after), channel_id=1, source_target_pairs={{0,1},{1,0},{2,3},{3,2},{4,5},{5,4},{6,7},{7,6},{8,9},{9,8},{10,11... | collective-permute-start | bytes 2359304 | tf_op jit(solution)/shard_map/ppermute | solution.py:317
  15.1 14.0 %collective-permute-start.3 = (bf16[2,256,512]{2,1,0:T(8,128)(2,1)S(1)}, bf16[2,256,512]{2,1,0:T(8,128)(2,1)S(1)}, u32[]{:S(2)}, u32[]{:S(2)}) collective-permute-start(bf16[2,256,512]{2,1,0:T(8,128)(2,1)S(1)} %get-tuple-element.51), channel_id=1, source_target_pairs={{0,4},{2,6},{4,0},{6,2},{8,12},{10,14},{12,8},{14,10},{1,5},{3,7},... | collective-permute-start | bytes 1572872 | tf_op jit(solution)/shard_map/ppermute | solution.py:320
  19.6 20.7 %collective-permute-start.7 = (bf16[2,256,512]{2,1,0:T(8,128)(2,1)S(1)}, bf16[2,256,512]{2,1,0:T(8,128)(2,1)S(1)}, u32[]{:S(2)}, u32[]{:S(2)}) collective-permute-start(bf16[2,256,512]{2,1,0:T(8,128)(2,1)S(1)} %get-tuple-element.63), channel_id=1, source_target_pairs={{0,4},{2,6},{4,0},{6,2},{8,12},{10,14},{12,8},{14,10},{1,5},{3,7},... | collective-permute-start | bytes 1572872 | tf_op jit(solution)/shard_map/ppermute | solution.py:320
  29.9 16.6 %collective-permute-start.6 = (bf16[256,512]{1,0:T(8,128)(2,1)S(1)}, bf16[256,512]{1,0:T(8,128)(2,1)S(1)}, u32[]{:S(2)}, u32[]{:S(2)}) collective-permute-start(bf16[256,512]{1,0:T(8,128)(2,1)S(1)} %get-tuple-element.60), channel_id=1, source_target_pairs={{0,12},{2,14},{4,8},{6,10},{8,4},{10,6},{12,0},{14,2},{1,13},{3,15... | collective-permute-start | bytes 786440 | tf_op jit(solution)/shard_map/ppermute | solution.py:320
  31.5 55.4 %collective-permute-start.18 = (bf16[2,1024,256]{2,1,0:T(8,128)(2,1)S(1)}, bf16[2,1024,256]{2,1,0:T(8,128)(2,1)S(1)}, u32[]{:S(2)}, u32[]{:S(2)}) collective-permute-start(bf16[2,1024,256]{2,1,0:T(8,128)(2,1)S(1)} %copy-done), channel_id=1, source_target_pairs={{1,2},{3,14},{5,6},{7,10},{8,9},{10,5},{12,13},{14,1},{17,18},{19,... | collective-permute-start | bytes 3145736 | tf_op jit(solution)/shard_map/ppermute | solution.py:337
  41.1 20.1 %collective-permute-start.8 = (bf16[256,512]{1,0:T(8,128)(2,1)S(1)}, bf16[256,512]{1,0:T(8,128)(2,1)S(1)}, u32[]{:S(2)}, u32[]{:S(2)}) collective-permute-start(bf16[256,512]{1,0:T(8,128)(2,1)S(1)} %get-tuple-element.66), channel_id=1, source_target_pairs={{0,12},{2,14},{4,8},{6,10},{8,4},{10,6},{12,0},{14,2},{1,13},{3,15... | collective-permute-start | bytes 786440 | tf_op jit(solution)/shard_map/ppermute | solution.py:320
  42.8 19.1 %collective-permute-start.10 = (bf16[2,512,256]{2,1,0:T(8,128)(2,1)S(1)}, bf16[2,512,256]{2,1,0:T(8,128)(2,1)S(1)}, u32[]{:S(2)}, u32[]{:S(2)}) collective-permute-start(bf16[2,512,256]{2,1,0:T(8,128)(2,1)S(1)} %get-tuple-element.69), channel_id=1, source_target_pairs={{0,2},{2,0},{4,6},{6,4},{8,10},{10,8},{12,14},{14,12},{1,3},{3,1},... | collective-permute-start | bytes 1572872 | tf_op jit(solution)/shard_map/ppermute | solution.py:314
  44.6 24.6 %collective-permute-start.5 = (bf16[2,256,512]{2,1,0:T(8,128)(2,1)S(1)}, bf16[2,256,512]{2,1,0:T(8,128)(2,1)S(1)}, u32[]{:S(2)}, u32[]{:S(2)}) collective-permute-start(bf16[2,256,512]{2,1,0:T(8,128)(2,1)S(1)} %get-tuple-element.59), channel_id=1, source_target_pairs={{0,4},{2,6},{4,0},{6,2},{8,12},{10,14},{12,8},{14,10},{1,5},{3,7},... | collective-permute-start | bytes 1572872 | tf_op jit(solution)/shard_map/ppermute | solution.py:320
  46.5 32.2 %collective-permute-start.12 = (bf16[2,256,512]{2,1,0:T(8,128)(2,1)S(1)}, bf16[2,256,512]{2,1,0:T(8,128)(2,1)S(1)}, u32[]{:S(2)}, u32[]{:S(2)}) collective-permute-start(bf16[2,256,512]{2,1,0:T(8,128)(2,1)S(1)} %get-tuple-element.73), channel_id=1, source_target_pairs={{0,12},{2,14},{4,8},{6,10},{8,4},{10,6},{12,0},{14,2},{1,13},{3,15... | collective-permute-start | bytes 1572872 | tf_op jit(solution)/shard_map/ppermute | solution.py:320
  61.8 1.6 %collective-permute-start.9 = (bf16[256,512]{1,0:T(8,128)(2,1)S(1)}, bf16[256,512]{1,0:T(8,128)(2,1)S(1)}, u32[]{:S(2)}, u32[]{:S(2)}) collective-permute-start(bf16[256,512]{1,0:T(8,128)(2,1)S(1)} %get-tuple-element.68), channel_id=1, source_target_pairs={{0,2},{2,0},{4,6},{6,4},{8,10},{10,8},{12,14},{14,12},{1,3},{3,1},... | collective-permute-start | bytes 786440 | tf_op jit(solution)/shard_map/ppermute | solution.py:314
  64.2 9.0 %collective-permute-start.13 = (bf16[3,128,256]{2,1,0:T(8,128)(2,1)S(1)}, bf16[3,128,256]{2,1,0:T(8,128)(2,1)S(1)}, u32[]{:S(2)}, u32[]{:S(2)}) collective-permute-start(bf16[3,128,256]{2,1,0:T(8,128)(2,1)S(1)} %get-tuple-element.74), channel_id=1, source_target_pairs={{0,16},{16,32},{32,48},{48,0},{64,80},{80,96},{96,112},{112,64},{1... | collective-permute-start | bytes 589832 | tf_op jit(solution)/shard_map/ppermute | solution.py:347
  65.9 12.4 %collective-permute-start.14 = (bf16[3,128,256]{2,1,0:T(8,128)(2,1)S(1)}, bf16[3,128,256]{2,1,0:T(8,128)(2,1)S(1)}, u32[]{:S(2)}, u32[]{:S(2)}) collective-permute-start(bf16[3,128,256]{2,1,0:T(8,128)(2,1)S(1)} %get-tuple-element.75), channel_id=1, source_target_pairs={{0,32},{16,48},{32,0},{48,16},{64,96},{80,112},{96,64},{112,80},{1... | collective-permute-start | bytes 589832 | tf_op jit(solution)/shard_map/ppermute | solution.py:347
  69.2 9.1 %collective-permute-start.15 = (bf16[3,128,256]{2,1,0:T(8,128)(2,1)S(1)}, bf16[3,128,256]{2,1,0:T(8,128)(2,1)S(1)}, u32[]{:S(2)}, u32[]{:S(2)}) collective-permute-start(bf16[3,128,256]{2,1,0:T(8,128)(2,1)S(1)} %get-tuple-element.76), channel_id=1, source_target_pairs={{0,48},{16,0},{32,16},{48,32},{64,112},{80,64},{96,80},{112,96},{1... | collective-permute-start | bytes 589832 | tf_op jit(solution)/shard_map/ppermute | solution.py:347
  73.1 8.3 %collective-permute-start.11 = (bf16[256,512]{1,0:T(8,128)(2,1)S(1)}, bf16[256,512]{1,0:T(8,128)(2,1)S(1)}, u32[]{:S(2)}, u32[]{:S(2)}) collective-permute-start(bf16[256,512]{1,0:T(8,128)(2,1)S(1)} %get-tuple-element.72), channel_id=1, source_target_pairs={{0,12},{2,14},{4,8},{6,10},{8,4},{10,6},{12,0},{14,2},{1,13},{3,15... | collective-permute-start | bytes 786440 | tf_op jit(solution)/shard_map/ppermute | solution.py:320
  79.4 6.9 %collective-permute-start.16 = (bf16[256,512]{1,0:T(8,128)(2,1)S(1)}, bf16[256,512]{1,0:T(8,128)(2,1)S(1)}, u32[]{:S(2)}, u32[]{:S(2)}) collective-permute-start(bf16[256,512]{1,0:T(8,128)(2,1)S(1)} %get-tuple-element.78), channel_id=1, source_target_pairs={{0,4},{2,6},{4,0},{6,2},{8,12},{10,14},{12,8},{14,10},{1,5},{3,7},... | collective-permute-start | bytes 786440 | tf_op jit(solution)/shard_map/ppermute | solution.py:320
  87.0 3.9 %collective-permute-start.19 = (bf16[2,512,256]{2,1,0:T(8,128)(2,1)S(1)}, bf16[2,512,256]{2,1,0:T(8,128)(2,1)S(1)}, u32[]{:S(2)}, u32[]{:S(2)}) collective-permute-start(bf16[2,512,256]{2,1,0:T(8,128)(2,1)S(1)} %get-tuple-element.82), channel_id=1, source_target_pairs={{0,2},{2,0},{4,6},{6,4},{8,10},{10,8},{12,14},{14,12},{1,3},{3,1},... | collective-permute-start | bytes 1572872 | tf_op jit(solution)/shard_map/ppermute | solution.py:314
  89.0 1.9 %collective-permute-start.17 = (bf16[256,512]{1,0:T(8,128)(2,1)S(1)}, bf16[256,512]{1,0:T(8,128)(2,1)S(1)}, u32[]{:S(2)}, u32[]{:S(2)}) collective-permute-start(bf16[256,512]{1,0:T(8,128)(2,1)S(1)} %get-tuple-element.80), channel_id=1, source_target_pairs={{0,2},{2,0},{4,6},{6,4},{8,10},{10,8},{12,14},{14,12},{1,3},{3,1},... | collective-permute-start | bytes 786440 | tf_op jit(solution)/shard_map/ppermute | solution.py:314
  91.6 9.9 %collective-permute-start.20 = (bf16[3,128,256]{2,1,0:T(8,128)(2,1)S(1)}, bf16[3,128,256]{2,1,0:T(8,128)(2,1)S(1)}, u32[]{:S(2)}, u32[]{:S(2)}) collective-permute-start(bf16[3,128,256]{2,1,0:T(8,128)(2,1)S(1)} %get-tuple-element.83), channel_id=1, source_target_pairs={{0,16},{16,32},{32,48},{48,0},{64,80},{80,96},{96,112},{112,64},{1... | collective-permute-start | bytes 589832 | tf_op jit(solution)/shard_map/ppermute | solution.py:347
  92.8 11.3 %collective-permute-start.21 = (bf16[3,128,256]{2,1,0:T(8,128)(2,1)S(1)}, bf16[3,128,256]{2,1,0:T(8,128)(2,1)S(1)}, u32[]{:S(2)}, u32[]{:S(2)}) collective-permute-start(bf16[3,128,256]{2,1,0:T(8,128)(2,1)S(1)} %get-tuple-element.84), channel_id=1, source_target_pairs={{0,32},{16,48},{32,0},{48,16},{64,96},{80,112},{96,64},{112,80},{1... | collective-permute-start | bytes 589832 | tf_op jit(solution)/shard_map/ppermute | solution.py:347
  95.2 8.9 %collective-permute-start.22 = (bf16[3,128,256]{2,1,0:T(8,128)(2,1)S(1)}, bf16[3,128,256]{2,1,0:T(8,128)(2,1)S(1)}, u32[]{:S(2)}, u32[]{:S(2)}) collective-permute-start(bf16[3,128,256]{2,1,0:T(8,128)(2,1)S(1)} %get-tuple-element.85), channel_id=1, source_target_pairs={{0,48},{16,0},{32,16},{48,32},{64,112},{80,64},{96,80},{112,96},{1... | collective-permute-start | bytes 589832 | tf_op jit(solution)/shard_map/ppermute | solution.py:347
  95.5 13.8 %collective-permute-start.25 = (bf16[3,128,256]{2,1,0:T(8,128)(2,1)S(1)}, bf16[3,128,256]{2,1,0:T(8,128)(2,1)S(1)}, u32[]{:S(2)}, u32[]{:S(2)}) collective-permute-start(bf16[3,128,256]{2,1,0:T(8,128)(2,1)S(1)} %sum_over_z.2.after), channel_id=1, source_target_pairs={{0,0},{1,15},{2,64},{3,79},{4,4},{5,11},{6,68},{7,75},{8,6},{9,9},... | collective-permute-start | bytes 589832 | tf_op jit(solution)/shard_map/ppermute | solution.py:334
  100.3 9.1 %collective-permute-start.26 = (bf16[3,128,256]{2,1,0:T(8,128)(2,1)S(1)}, bf16[3,128,256]{2,1,0:T(8,128)(2,1)S(1)}, u32[]{:S(2)}, u32[]{:S(2)}) collective-permute-start(bf16[3,128,256]{2,1,0:T(8,128)(2,1)S(1)} %sum_over_z.2.after), channel_id=1, source_target_pairs={{64,0},{65,15},{66,64},{67,79},{68,4},{69,11},{70,68},{71,75},{72,... | collective-permute-start | bytes 589832 | tf_op jit(solution)/shard_map/ppermute | solution.py:334
  104.5 13.0 %collective-permute-start.23 = (bf16[3,128,256]{2,1,0:T(8,128)(2,1)S(1)}, bf16[3,128,256]{2,1,0:T(8,128)(2,1)S(1)}, u32[]{:S(2)}, u32[]{:S(2)}) collective-permute-start(bf16[3,128,256]{2,1,0:T(8,128)(2,1)S(1)} %sum_over_z.3), channel_id=1, source_target_pairs={{0,1},{1,14},{2,65},{3,78},{4,5},{5,10},{6,69},{7,74},{8,7},{9,8},... | collective-permute-start | bytes 589832 | tf_op jit(solution)/shard_map/ppermute | solution.py:334
  108.5 8.9 %collective-permute-start.24 = (bf16[3,128,256]{2,1,0:T(8,128)(2,1)S(1)}, bf16[3,128,256]{2,1,0:T(8,128)(2,1)S(1)}, u32[]{:S(2)}, u32[]{:S(2)}) collective-permute-start(bf16[3,128,256]{2,1,0:T(8,128)(2,1)S(1)} %sum_over_z.3), channel_id=1, source_target_pairs={{64,1},{65,14},{66,65},{67,78},{68,5},{69,10},{70,69},{71,74},{72,... | collective-permute-start | bytes 589832 | tf_op jit(solution)/shard_map/ppermute | solution.py:334

commit v8 on v7

--- a/solution.py
+++ b/solution.py
@@ -19,8 +19,7 @@
 
 X, CORES, Z = 4, 2, 4
 
-ORDER = (1, 2, 0, 3)
-BACK = (3, 1, 2, 0)
+ORDER = ((2, 1), (3, 0))
 
 
 def code_of(values):
@@ -91,35 +90,26 @@
     return tok // 2, tok % 2, half, member // Z, member % Z
 
 
-def column_block(flip, part):
+def load_inputs(member, pair, x_ref, x_out, sem):
     x, _, half, _, _ = where_am_i()
-    owner = x ^ flip
-    local = jnp.where(owner // 2 == half, 2 * (owner % 2), 2 * ((3 - owner) % 2) + 1)
-    return 2 * local + part
-
-
-def load_inputs(member, part, x_ref, x_out, sem):
-    wide = x_out.shape[2]
+    wide = x_ref.shape[2] // 4
     copies = []
-    for s, flip in enumerate(ORDER):
-        at = pl.multiple_of(column_block(flip, part) * wide, wide)
-        copies.append(pltpu.make_async_copy(x_ref.at[member, :, pl.ds(at, wide)], x_out.at[s], sem.at[s]))
+    for s, distance in enumerate(ORDER[pair]):
+        owner = (x + distance) % X
+        local = jnp.where(owner // 2 == half, 2 * (owner % 2), 2 * ((3 - owner) % 2) + 1)
+        at = pl.multiple_of(local * wide, wide)
+        source = x_ref.at[member, :, pl.ds(at, wide)]
+        copies.append(pltpu.make_async_copy(source, x_out.at[:, pl.ds(s * wide, wide)], sem.at[s]))
         copies[s].start()
     return copies
 
 
 def load_first_kernel(x_ref, g_ref, out, sem, g_sem):
     core = where_am_i()[1]
-    wide = x_ref.shape[2] // 8
-    copies = [pltpu.make_async_copy(g_ref.at[1 - core], out.at[:, pl.ds(4 * wide, g_ref.shape[2])], g_sem)]
-    for s, flip in enumerate(ORDER):
-        at = pl.multiple_of(column_block(flip, 0) * wide, wide)
-        copies.append(
-            pltpu.make_async_copy(x_ref.at[1 - core, :, pl.ds(at, wide)], out.at[:, pl.ds(s * wide, wide)], sem.at[s])
-        )
-    for copy in copies:
-        copy.start()
-    for copy in copies:
+    outs = g_ref.shape[2]
+    load = pltpu.make_async_copy(g_ref.at[1 - core], out.at[:, pl.ds(out.shape[1] - outs, outs)], g_sem)
+    load.start()
+    for copy in load_inputs(1 - core, 0, x_ref, out, sem) + [load]:
         copy.wait()
 
 
@@ -133,10 +123,14 @@
     out[0], out[1] = own[...], got[:, got.shape[1] - outs :]
 
 
+def columns(s, x_ref, wide):
+    return x_ref[:, s * wide : (s + 1) * wide]
+
+
 def own_tokens(copies, x_out, gt_ref, part_out):
-    for s in range(4):
+    for s in range(2):
         copies[s].wait()
-        part_out[s] = fisher_block(x_out[s], gt_ref)
+        part_out[s] = fisher_block(columns(s, x_out, part_out.shape[2]), gt_ref)
 
 
 def own_first_kernel(x_ref, g_ref, after, x_out, g_out, gt_out, part_out, sem, g_sem):
@@ -154,55 +148,45 @@
     own_tokens(copies, x_out, gt_ref, part_out)
 
 
-def put(s, block, sent_out, kept_out):
-    if s < 2:
-        sent_out[s] = encode(block)
-    else:
-        kept_out[s - 2] = block
-
-
-def add_first_kernel(x_ref, part_ref, after, sent_out, kept_out, gt_out):
+def add_first_kernel(x_ref, part_ref, after, two_out, one_out, gt_out):
+    wide, outs = part_ref.shape[2], part_ref.shape[1]
+    gt_out[...] = squared_transposed(x_ref[:, 2 * wide :])
+    for s, out in enumerate((two_out, one_out)):
+        out[...] = encode(part_ref[s] + fisher_block(columns(s, x_ref, wide), gt_out))
+
+
+def add_second_kernel(x_ref, gt_ref, part_ref, after, three_out, own_out):
     wide = part_ref.shape[2]
-    gt_out[...] = squared_transposed(x_ref[:, 4 * wide :])
-    for s in range(4):
-        block = fisher_block(x_ref[:, s * wide : (s + 1) * wide], gt_out)
-        put(s, part_ref[s] + block, sent_out, kept_out)
-
-
-def add_second_kernel(x_ref, gt_ref, part_ref, after, sent_out, kept_out):
-    for s in range(4):
-        put(s, part_ref[s] + fisher_block(x_ref[s], gt_ref), sent_out, kept_out)
-
-
-def both_first_kernel(xa_ref, xb_ref, g_ref, after, sent_out, kept_out, gta_out, gtb_out):
-    wide = kept_out.shape[2]
+    three_out[...] = encode(part_ref[0] + fisher_block(columns(0, x_ref, wide), gt_ref))
+    own_out[...] = part_ref[1] + fisher_block(columns(1, x_ref, wide), gt_ref)
+
+
+def both(s, xa_ref, xb_ref, gta_ref, gtb_ref, wide):
+    return fisher_block(columns(s, xa_ref, wide), gta_ref) + fisher_block(columns(s, xb_ref, wide), gtb_ref)
+
+
+def both_first_kernel(xa_ref, xb_ref, g_ref, after, two_out, one_out, gta_out, gtb_out):
     gta_out[...] = squared_transposed(g_ref[0])
     gtb_out[...] = squared_transposed(g_ref[1])
-    for s in range(4):
-        block = fisher_block(xb_ref[:, s * wide : (s + 1) * wide], gtb_out)
-        put(s, fisher_block(xa_ref[s], gta_out) + block, sent_out, kept_out)
-
-
-def both_second_kernel(xa_ref, xb_ref, gta_ref, gtb_ref, after, sent_out, kept_out):
-    for s, block in enumerate(BACK):
-        put(s, fisher_block(xa_ref[block], gta_ref) + fisher_block(xb_ref[block], gtb_ref), sent_out, kept_out)
-
-
-def middle_kernel(kept_ref, got_ref, after, sent_out, own_out):
-    sent_out[...] = encode_fine(kept_ref[1] + decode(got_ref[1]))
-    own_out[...] = kept_ref[0] + decode(got_ref[0])
-
-
-def settle_kernel(own, got, after, out):
-    out[...] = own[...] + decode_fine(got[...])
-
-
-def join_kernel(first_ref, own, got, after, kept_out, sent_out):
-    first = first_ref[...]
-    second = own[...] + decode_fine(got[...])
+    for s, out in enumerate((two_out, one_out)):
+        out[...] = encode(both(s, xa_ref, xb_ref, gta_out, gtb_out, out.shape[1]))
+
+
+def both_second_kernel(xa_ref, xb_ref, gta_ref, gtb_ref, after, three_out, own_out):
+    wide = own_out.shape[1]
+    three_out[...] = encode(both(0, xa_ref, xb_ref, gta_ref, gtb_ref, wide))
+    own_out[...] = both(1, xa_ref, xb_ref, gta_ref, gtb_ref, wide)
+
+
+def join_kernel(own, one, two, three, after, kept_out, sent_out):
+    wide = kept_out.shape[1]
+    halves = []
+    for s in range(2):
+        got = [decode(columns(s, ref, wide)) for ref in (one, two, three)]
+        halves.append(columns(s, own, wide) + got[0] + got[1] + got[2])
     core = where_am_i()[1]
-    kept_out[...] = jnp.where(core == 0, first, second)
-    sent_out[...] = encode_fine(jnp.where(core == 0, second, first))
+    kept_out[...] = jnp.where(core == 0, halves[0], halves[1])
+    sent_out[...] = encode_fine(jnp.where(core == 0, halves[1], halves[0]))
 
 
 def split_kernel(w_ref, after, own_out, send_out):
@@ -240,6 +224,30 @@
             to_words(weighted, total, out)
 
 
+def weigh_all_kernel(phase, own, other, w_own, w_other, after, out):
+    _, core, half, _, _ = where_am_i()
+    part = own.shape[1] // Z
+    mine = (core ^ half ^ phase) == 0
+    for z in range(Z):
+        cols = slice(z * part, (z + 1) * part)
+        weighted = total = 0.0
+        for values, m in ((own[:, cols], core), (decode_fine(other[:, cols]), 1 - core)):
+            fisher = values.T
+            weight = jnp.where(mine, w_own[m, cols, :].astype(F32), w_other[m, cols, :].astype(F32))
+            weighted += fisher * weight
+            total += fisher
+        to_words(weighted, total, out.at[z])
+
+
+def sum_all_kernel(got, after, out):
+    weighted = total = 0.0
+    for z in range(Z):
+        more, added = from_words(got.at[z])
+        weighted += more
+        total += added
+    to_words(weighted, total, out)
+
+
 def over_z(sums, words):
     weighted, total = sums[0], sums[1]
     for ref in words:
@@ -293,8 +301,8 @@
     return pairs
 
 
-def x_pairs(flip):
-    return [(t, ((t // 2) ^ flip) * 2 + t % 2) for t in range(X * CORES)]
+def x_pairs(distance):
+    return [(t, ((t // 2 + distance) % X) * 2 + t % 2) for t in range(X * CORES)]
 
 
 def z_pairs(distance):
@@ -304,8 +312,8 @@
 def shards(inputs, grads, weights):
     tokens, outs = grads.shape[1:]
     wide = inputs.shape[2] // 8
-    x_shape, g_shape, gt_shape = ((4, tokens, wide), BF16), ((tokens, outs), BF16), ((outs, tokens), BF16)
-    part_shape, sent_shape, kept_shape = ((4, outs, wide), F32), ((2, outs, wide), BF16), ((2, outs, wide), F32)
+    x_shape, g_shape, gt_shape = ((tokens, 4 * wide), BF16), ((tokens, outs), BF16), ((outs, tokens), BF16)
+    part_shape, sent_shape, sum_shape = ((2, outs, 2 * wide), F32), ((outs, 2 * wide), BF16), ((outs, 2 * wide), F32)
     code_shape, own_shape = ((outs, wide), BF16), ((outs, wide), F32)
     words, sums = ((3, wide // Z, outs), BF16), ((2, wide // Z, outs), F32)
     dma = pltpu.SemaphoreType.DMA
@@ -316,18 +324,13 @@
     def swap_cols(send):
         return lax.ppermute(send, "col", [(0, 1), (1, 0)])
 
-    def swap_x(flip, sent):
-        return lax.ppermute(sent, "tok", x_pairs(flip))
-
-    def middle(flip, got, kept_blocks, after):
-        sent, own = call(middle_kernel, "fisher_over_first_swap", [code_shape, own_shape], [], [kept_blocks, got, after])
-        return own, swap_x(flip, sent)
-
-    def settle(one, after):
-        return call(settle_kernel, "fisher_over_tokens", own_shape, [], [*one, after])
-
-    def join(first, two, after):
-        kept_block, sent = call(join_kernel, "fisher_over_tokens", [own_shape, code_shape], [], [first, *two, after])
+    def send_x(distance, sent):
+        return lax.ppermute(sent, "tok", x_pairs(distance))
+
+    def join(own, got, after):
+        kept_block, sent = call(
+            join_kernel, "fisher_over_tokens", [own_shape, code_shape], [], [own, got[1], got[2], got[3], after]
+        )
         return kept_block, swap_cores(sent)
 
     def results(phase, sums):
@@ -347,50 +350,49 @@
         return [lax.ppermute(v, "member", z_pairs(d)) for d, v in send] + [own_sums]
 
     x_send0 = call(
-        load_first_kernel, "load_to_swap", ((tokens, 4 * wide + outs), BF16), [inputs, grads], [], [dma((4,)), dma]
+        load_first_kernel, "load_to_swap", ((tokens, 4 * wide + outs), BF16), [inputs, grads], [], [dma((2,)), dma]
     )
     x_got0 = swap_cores(x_send0)
     x_own0, g_own, gt_own, part0 = call(
         own_first_kernel, "fisher_of_own_tokens", [x_shape, g_shape, gt_shape, part_shape], [inputs, grads], [x_send0],
-        [dma((4,)), dma],
-    )
-    x_send1 = call(load_second_kernel, "load_to_swap", x_shape, [inputs], [gt_own], [dma((4,))])
+        [dma((2,)), dma],
+    )
+    x_send1 = call(load_second_kernel, "load_to_swap", x_shape, [inputs], [gt_own], [dma((2,))])
     x_got1 = swap_cores(x_send1)
     g_pair = call(pair_kernel, "pair_grads", ((2, tokens, outs), BF16), [], [g_own, x_got0, x_send1])
     g_other = swap_cols(g_pair)
-    sent, kept00, gt_got = call(
-        add_first_kernel, "fisher_of_both_cores", [sent_shape, kept_shape, gt_shape], [], [x_got0, part0, g_pair]
-    )
-    swap00 = swap_x(1, sent)
+    two, one, gt_got = call(
+        add_first_kernel, "fisher_of_both_cores", [sent_shape, sent_shape, gt_shape], [], [x_got0, part0, g_pair]
+    )
+    got0 = {2: send_x(2, two), 1: send_x(1, one)}
     x_own1, part1 = call(
-        own_second_kernel, "fisher_of_own_tokens", [x_shape, part_shape], [inputs], [gt_own, kept00], [dma((4,))]
-    )
-    sent, kept01 = call(
-        add_second_kernel, "fisher_of_both_cores", [sent_shape, kept_shape], [], [x_got1, gt_got, part1, x_own1]
-    )
-    swap01 = swap_x(1, sent)
-    part00 = middle(3, swap00, kept00, kept01)
-    w0 = bring_weights(0, part00[0])
-
-    sent, kept10, gt_own, gt_got = call(
-        both_first_kernel, "fisher_of_other_grads", [sent_shape, kept_shape, gt_shape, gt_shape], [],
+        own_second_kernel, "fisher_of_own_tokens", [x_shape, part_shape], [inputs], [gt_own, two], [dma((2,))]
+    )
+    three, sum0 = call(
+        add_second_kernel, "fisher_of_both_cores", [sent_shape, sum_shape], [], [x_got1, gt_got, part1, x_own1]
+    )
+    got0[3] = send_x(3, three)
+    w0 = bring_weights(0, three)
+
+    two, one, gt_own, gt_got = call(
+        both_first_kernel, "fisher_of_other_grads", [sent_shape, sent_shape, gt_shape, gt_shape], [],
         [x_own0, x_got0, g_other, w0[0]],
     )
-    swap10 = swap_x(1, sent)
-    part01 = middle(3, swap01, kept01, kept10)
-    sent, kept11 = call(
-        both_second_kernel, "fisher_of_other_grads", [sent_shape, kept_shape], [],
-        [x_own1, x_got1, gt_own, gt_got, part01[0]],
-    )
-    swap11 = swap_x(3, sent)
-
-    settled0 = settle(part00, kept11)
-    own0, other0 = join(settled0, part01, kept11)
-    words0 = weigh(0, own0, other0, w0, own0)
-    part10 = middle(3, swap10, kept10, words0[3])
-    first = call(sum_kernel, "sum_over_z", words, [], [*words0, part10[0]])
-    part11 = middle(1, swap11, kept11, first)
-    own1, other1 = join(settle(part10, part11[0]), part11, first)
+    got1 = {2: send_x(2, two), 1: send_x(1, one)}
+    three, sum1 = call(
+        both_second_kernel, "fisher_of_other_grads", [sent_shape, sum_shape], [], [x_own1, x_got1, gt_own, gt_got, two]
+    )
+    got1[3] = send_x(3, three)
+
+    own0, other0 = join(sum0, got0, three)
+    words0 = call(
+        lambda *refs: weigh_all_kernel(0, *refs), "weigh_members", ((Z, 3, wide // Z, outs), BF16), [],
+        [own0, other0, *w0, own0],
+    )
+    groups = [[y * Z + z for z in range(Z)] for y in range(2)]
+    words0 = lax.all_to_all(words0, "member", 0, 0, axis_index_groups=groups, tiled=True)
+    first = call(sum_all_kernel, "sum_over_z", words, [], [words0, own0])
+    own1, other1 = join(sum1, got1, first)
     w1 = bring_weights(1, own1)
     words1 = weigh(1, own1, other1, w1, w1[0])
     met = call(meet_kernel, "meet_over_y", sums, [], [*results(0, first), own1])

time: 119 us -> 124 us (1.042)
  starting transfers between devices: 38 us -> 40.4 us
  waiting for transfers between devices: 55.9 us -> 58.3 us
    ppermute x2, waiting for transfers between devices: 0.01 us -> 17.4 us  [bring_weights(): arrived = lax.ppermute(weights, ('tok', 'col'), weight_pairs(phase))]
    ppermute x8 -> x6, waiting for transfers between devices: 34.4 us -> 21.5 us  [send_x(): return lax.ppermute(sent, 'tok', x_pairs(distance))]
    ppermute x8 -> x6, starting transfers between devices: 5.75 us -> 12.5 us  [send_x(): return lax.ppermute(sent, 'tok', x_pairs(distance))]
    ppermute x6 -> x3, waiting for transfers between devices: 10.1 us -> 3.87 us  [weigh(): return [lax.ppermute(v, 'member', z_pairs(d)) for d, v in send] + [own_sums]]
    all_to_all x0 -> x1, starting transfers between devices: none -> 5.03 us  [shards(): lax.all_to_all(words0, 'member', 0, 0, axis_index_groups=groups, tiled=True)]
    ppermute x6 -> x3, starting transfers between devices: 9.58 us -> 5.11 us  [weigh(): return [lax.ppermute(v, 'member', z_pairs(d)) for d, v in send] + [own_sums]]
    all_to_all x0 -> x1, waiting for transfers between devices: none -> 4.1 us  [shards(): lax.all_to_all(words0, 'member', 0, 0, axis_index_groups=groups, tiled=True)]
    ppermute x4, starting transfers between devices: 10.9 us -> 7.82 us  [results(): lax.ppermute(sums, ('member', 'tok', 'col'), result_pairs(phase, y_lo))]
  transfers between devices with their start and end apart: 27 -> 23, of which waited for: 12 -> 9; matrix products, arithmetic and copies ran while one was open for 0% -> 0% of each run, Pallas kernels for 17% -> 17%
where the time goes in v8:
time: 124 us
  waiting for transfers between devices  58.3 us (47%)
  starting transfers between devices  40.4 us (33%)
  Pallas kernels  24.8 us (20%)
    pallas_call x18, Pallas kernels, call(): pl.pallas_call(kernel, out_shape=shapes, in_specs=[HBM] * len(hbm) + [VME...  23.9 us
    ppermute x6, waiting for transfers between devices, send_x(): return lax.ppermute(sent, 'tok', x_pairs(distance))  21.5 us
    ppermute x2, waiting for transfers between devices, bring_weights(): arrived = lax.ppermute(weights, ('tok', 'col'), weight_pairs(phase))  17.4 us
    ppermute x6, starting transfers between devices, send_x(): return lax.ppermute(sent, 'tok', x_pairs(distance))  12.5 us
    ppermute x4, waiting for transfers between devices, results(): lax.ppermute(sums, ('member', 'tok', 'col'), result_pairs(phase, y_lo))  8.04 us
    ppermute x4, starting transfers between devices, results(): lax.ppermute(sums, ('member', 'tok', 'col'), result_pairs(phase, y_lo))  7.82 us
    ppermute x2, starting transfers between devices, bring_weights(): arrived = lax.ppermute(weights, ('tok', 'col'), weight_pairs(phase))  6.16 us
    ppermute x3, starting transfers between devices, weigh(): return [lax.ppermute(v, 'member', z_pairs(d)) for d, v in send] + [own_sums]  5.11 us
  transfers between devices with their start and end apart: 23, of which 9 were waited for; matrix products, arithmetic and copies ran while one was open for 0% of the time, Pallas kernels for 17%

profile of v8, /device:TPU:1, one launch (start us, length us, event | category | flops | bytes accessed | tf_op | source)
XLA Modules:
  0.0 123.8 jit_solution(4046388411851243652)
XLA Ops:
  0.0 2.0 %load_to_swap.2.after = bf16[768,2304]{1,0:T(8,128)(2,1)S(1)} custom-call(bf16[2,768,4096]{2,1,0:T(8,128)(2,1)} %x_ref.7, bf16[2,768,256]{2,1,0:T(8,128)(2,1)} %g_ref.3), custom_call_target="tpu_custom_call" | custom-call | flops 1 | bytes 1 | tf_op jit(solution)/shard_map/load_to_swap/pallas_call | solution.py:66
  2.1 1.5 %collective-permute-start = (bf16[768,2304]{1,0:T(8,128)(2,1)S(1)}, bf16[768,2304]{1,0:T(8,128)(2,1)S(1)}, u32[]{:S(2)}, u32[]{:S(2)}) collective-permute-start(bf16[768,2304]{1,0:T(8,128)(2,1)S(1)} %load_to_swap.2.after), channel_id=1, source_target_pairs={{0,2},{2,0},{4,6},{6,4},{8,10},{10,8},{12,14},{14,12},{1,3},{3,1},... | collective-permute-start | bytes 10616840 | tf_op jit(solution)/shard_map/ppermute | solution.py:322
  3.6 2.8 %fisher_of_own_tokens.2 = (bf16[768,2048]{1,0:T(8,128)(2,1)S(1)}, bf16[768,256]{1,0:T(8,128)(2,1)S(1)}, bf16[256,768]{1,0:T(8,128)(2,1)S(1)}, f32[2,256,1024]{2,1,0:T(8,128)S(1)}) custom-call(bf16[2,768,4096]{2,1,0:T(8,128)(2,1)} %x_ref.7, bf16[2,768,256]{2,1,0:T(8,128)(2,1)} %g_ref.3, bf16[768,2304]{1,0:T(8,128)(2,1)S(1)} %load_to_swap.2.after), custom_call_target="tpu_custom_call" | custom-call | flops 1 | bytes 1 | tf_op jit(solution)/shard_map/fisher_of_own_tokens/pallas_call | solution.py:66
  6.4 2.0 %load_to_swap.3.after = bf16[768,2048]{1,0:T(8,128)(2,1)S(1)} custom-call(bf16[2,768,4096]{2,1,0:T(8,128)(2,1)} %x_ref.7, bf16[256,768]{1,0:T(8,128)(2,1)S(1)} %get-tuple-element.34.after.gt_ref), custom_call_target="tpu_custom_call" | custom-call | flops 1 | bytes 1 | tf_op jit(solution)/shard_map/load_to_swap/pallas_call | solution.py:66
  8.4 0.1 collective-permute-start.1
  8.5 4.9 %collective-permute-start.3 = (bf16[2,1024,256]{2,1,0:T(8,128)(2,1)}, bf16[2,1024,256]{2,1,0:T(8,128)(2,1)S(1)}, u32[]{:S(2)}, u32[]{:S(2)}) collective-permute-start(bf16[2,1024,256]{2,1,0:T(8,128)(2,1)} %param.5), channel_id=1, source_target_pairs={{0,0},{2,12},{4,4},{6,8},{9,11},{11,7},{13,15},{15,3},{16,16},{18,... | collective-permute-start | bytes 3145736 | tf_op jit(solution)/shard_map/ppermute | solution.py:340
  13.4 0.1 collective-permute-start.2
  13.5 1.3 %fisher_of_both_cores.2 = (bf16[256,1024]{1,0:T(8,128)(2,1)S(1)}, bf16[256,1024]{1,0:T(8,128)(2,1)S(1)}, bf16[256,768]{1,0:T(8,128)(2,1)S(1)}) custom-call(bf16[768,2304]{1,0:T(8,128)(2,1)S(1)} %collective-permute-done.got.x_ref.xb_ref, f32[2,256,1024]{2,1,0:T(8,128)S(1)} %get-tuple-element.35.part_ref, bf16[2,768,256]{2,1,0:T(8,128)(2,1)S(1)} %pair_grads.1.after), custom_call_target="tpu_custom_call" | custom-call | flops 1 | bytes 1 | tf_op jit(solution)/shard_map/fisher_of_both_cores/pallas_call | solution.py:66
  14.8 2.6 %fisher_of_own_tokens.3 = (bf16[768,2048]{1,0:T(8,128)(2,1)S(1)}, f32[2,256,1024]{2,1,0:T(8,128)S(1)}) custom-call(bf16[2,768,4096]{2,1,0:T(8,128)(2,1)} %x_ref.7, bf16[256,768]{1,0:T(8,128)(2,1)S(1)} %get-tuple-element.34.after.gt_ref, bf16[256,1024]{1,0:T(8,128)(2,1)S(1)} %get-tuple-element.37.after), custom_call_target="tpu_custom_call" | custom-call | flops 1 | bytes 1 | tf_op jit(solution)/shard_map/fisher_of_own_tokens/pallas_call | solution.py:66
  17.4 3.1 %collective-permute-start.8 = (bf16[256,1024]{1,0:T(8,128)(2,1)S(1)}, bf16[256,1024]{1,0:T(8,128)(2,1)S(1)}, u32[]{:S(2)}, u32[]{:S(2)}) collective-permute-start(bf16[256,1024]{1,0:T(8,128)(2,1)S(1)} %get-tuple-element.37.after), channel_id=1, source_target_pairs={{0,8},{2,10},{4,12},{6,14},{8,0},{10,2},{12,4},{14,6},{1,9},{3,11}... | collective-permute-start | bytes 1572872 | tf_op jit(solution)/shard_map/ppermute | solution.py:328
  20.5 1.1 fisher_of_both_cores.3
  21.6 0.1 collective-permute-start.9
  21.7 1.5 %collective-permute-start.7 = (bf16[256,1024]{1,0:T(8,128)(2,1)S(1)}, bf16[256,1024]{1,0:T(8,128)(2,1)S(1)}, u32[]{:S(2)}, u32[]{:S(2)}) collective-permute-start(bf16[256,1024]{1,0:T(8,128)(2,1)S(1)} %get-tuple-element.51), channel_id=1, source_target_pairs={{0,4},{2,6},{4,8},{6,10},{8,12},{10,14},{12,0},{14,2},{1,5},{3,7},... | collective-permute-start | bytes 1572872 | tf_op jit(solution)/shard_map/ppermute | solution.py:328
  23.2 17.4 %collective-permute-done.3.w_ref = bf16[2,1024,256]{2,1,0:T(8,128)(2,1)S(1)} collective-permute-done((bf16[2,1024,256]{2,1,0:T(8,128)(2,1)}, bf16[2,1024,256]{2,1,0:T(8,128)(2,1)S(1)}, u32[]{:S(2)}, u32[]{:S(2)}) %collective-permute-start.3) | collective-permute-done | bytes 1048608 | tf_op jit(solution)/shard_map/ppermute | solution.py:340
  40.7 0.1 collective-permute-start.11
  40.8 1.3 %collective-permute-start.13 = (bf16[2,1024,256]{2,1,0:T(8,128)(2,1)}, bf16[2,1024,256]{2,1,0:T(8,128)(2,1)S(1)}, u32[]{:S(2)}, u32[]{:S(2)}) collective-permute-start(bf16[2,1024,256]{2,1,0:T(8,128)(2,1)} %param.5), channel_id=1, source_target_pairs={{1,2},{3,14},{5,6},{7,10},{8,9},{10,5},{12,13},{14,1},{17,18},{19,... | collective-permute-start | bytes 3145736 | tf_op jit(solution)/shard_map/ppermute | solution.py:340
  42.1 2.0 %fisher_of_other_grads.2 = (bf16[256,1024]{1,0:T(8,128)(2,1)S(1)}, bf16[256,1024]{1,0:T(8,128)(2,1)S(1)}, bf16[256,768]{1,0:T(8,128)(2,1)S(1)}, bf16[256,768]{1,0:T(8,128)(2,1)S(1)}) custom-call(bf16[768,2048]{1,0:T(8,128)(2,1)S(1)} %get-tuple-element.39.xa_ref, bf16[768,2304]{1,0:T(8,128)(2,1)S(1)} %collective-permute-done.got.x_ref.xb_ref, ...), custom_call_target="tpu_custom_call" | custom-call | flops 1 | bytes 1 | tf_op jit(solution)/shard_map/fisher_of_other_grads/pallas_call | solution.py:66
  44.1 1.9 %fisher_of_other_grads.3 = (bf16[256,1024]{1,0:T(8,128)(2,1)S(1)}, f32[256,1024]{1,0:T(8,128)S(1)}) custom-call(bf16[768,2048]{1,0:T(8,128)(2,1)S(1)} %get-tuple-element.38.after.xa_ref, bf16[768,2048]{1,0:T(8,128)(2,1)S(1)} %collective-permute-done.1.x_ref.xb_ref, bf16[256,768]{1,0:T(8,128)(2,1)S(1)} %get-tuple-element.44.gta_ref, ...), custom_call_target="tpu_custom_call" | custom-call | flops 1 | bytes 1 | tf_op jit(solution)/shard_map/fisher_of_other_grads/pallas_call | solution.py:66
  46.0 1.7 %collective-permute-done.9.three = bf16[256,1024]{1,0:T(8,128)(2,1)S(1)} collective-permute-done((bf16[256,1024]{1,0:T(8,128)(2,1)S(1)}, bf16[256,1024]{1,0:T(8,128)(2,1)S(1)}, u32[]{:S(2)}, u32[]{:S(2)}) %collective-permute-start.9) | collective-permute-done | bytes 524320 | tf_op jit(solution)/shard_map/ppermute | solution.py:328
  47.7 1.6 %fisher_over_tokens.2 = (f32[256,512]{1,0:T(8,128)S(1)}, bf16[256,512]{1,0:T(8,128)(2,1)S(1)}) custom-call(f32[256,1024]{1,0:T(8,128)S(1)} %get-tuple-element.50.own, bf16[256,1024]{1,0:T(8,128)(2,1)S(1)} %collective-permute-done.7.one, bf16[256,1024]{1,0:T(8,128)(2,1)S(1)} %collective-permute-done.8.two, ...), custom_call_target="tpu_custom_call" | custom-call | flops 1 | bytes 1 | tf_op jit(solution)/shard_map/fisher_over_tokens/pallas_call | solution.py:66
  49.4 0.3 collective-permute-start.10
  49.6 1.5 %collective-permute-done.10.refs_1_ = bf16[256,512]{1,0:T(8,128)(2,1)S(1)} collective-permute-done((bf16[256,512]{1,0:T(8,128)(2,1)S(1)}, bf16[256,512]{1,0:T(8,128)(2,1)S(1)}, u32[]{:S(2)}, u32[]{:S(2)}) %collective-permute-start.10) | collective-permute-done | bytes 262176 | tf_op jit(solution)/shard_map/ppermute | solution.py:322
  51.2 1.7 %weigh_members.2 = bf16[4,3,128,256]{3,2,1,0:T(8,128)(2,1)} custom-call(f32[256,512]{1,0:T(8,128)S(1)} %get-tuple-element.52.refs_0_.refs_4_.after, bf16[256,512]{1,0:T(8,128)(2,1)S(1)} %collective-permute-done.10.refs_1_, bf16[2,512,256]{2,1,0:T(8,128)(2,1)S(1)} %get-tuple-element.43.after.refs_2_, ...), custom_call_target="tpu_custom_call" | custom-call | flops 1 | bytes 1 | tf_op jit(solution)/shard_map/weigh_members/pallas_call | solution.py:66
  52.8 5.0 %all-to-all-start = ((bf16[4,3,128,256]{3,2,1,0:T(8,128)(2,1)}), bf16[4,3,128,256]{3,2,1,0:T(8,128)(2,1)S(1)}, u32[]{:S(2)}, u32[]{:S(2)}) async-start(bf16[4,3,128,256]{3,2,1,0:T(8,128)(2,1)} %weigh_members.2), calls=%async_computation | async-start | bytes 1572864 | tf_op jit(solution)/shard_map/all_to_all | solution.py:393
  57.9 6.7 %collective-permute-start.6 = (bf16[256,1024]{1,0:T(8,128)(2,1)}, bf16[256,1024]{1,0:T(8,128)(2,1)}, u32[]{:S(2)}, u32[]{:S(2)}) collective-permute-start(bf16[256,1024]{1,0:T(8,128)(2,1)} %copy-done), channel_id=1, source_target_pairs={{0,12},{2,14},{4,0},{6,2},{8,4},{10,6},{12,8},{14,10},{1,13},{3,15... | collective-permute-start | bytes 1572872 | tf_op jit(solution)/shard_map/ppermute | solution.py:328
  64.6 1.2 collective-permute-start.5
  65.7 4.1 %all-to-all-done.got = bf16[4,3,128,256]{3,2,1,0:T(8,128)(2,1)S(1)} async-done(((bf16[4,3,128,256]{3,2,1,0:T(8,128)(2,1)}), bf16[4,3,128,256]{3,2,1,0:T(8,128)(2,1)S(1)}, u32[]{:S(2)}, u32[]{:S(2)}) %all-to-all-start) | async-done | bytes 786464 | tf_op jit(solution)/shard_map/all_to_all | solution.py:393
  69.8 0.4 sum_over_z.2.after
  70.3 16.7 %collective-permute-done.6.three = bf16[256,1024]{1,0:T(8,128)(2,1)} collective-permute-done((bf16[256,1024]{1,0:T(8,128)(2,1)}, bf16[256,1024]{1,0:T(8,128)(2,1)}, u32[]{:S(2)}, u32[]{:S(2)}) %collective-permute-start.6) | collective-permute-done | bytes 524320 | tf_op jit(solution)/shard_map/ppermute | solution.py:328
  87.0 3.1 %collective-permute-done.4.one = bf16[256,1024]{1,0:T(8,128)(2,1)} collective-permute-done((bf16[256,1024]{1,0:T(8,128)(2,1)}, bf16[256,1024]{1,0:T(8,128)(2,1)}, u32[]{:S(2)}, u32[]{:S(2)}) %collective-permute-start.4) | collective-permute-done | bytes 524320 | tf_op jit(solution)/shard_map/ppermute | solution.py:328
  90.1 3.0 %fisher_over_tokens.3 = (f32[256,512]{1,0:T(8,128)S(1)}, bf16[256,512]{1,0:T(8,128)(2,1)S(1)}) custom-call(f32[256,1024]{1,0:T(8,128)S(1)} %get-tuple-element.47.own, bf16[256,1024]{1,0:T(8,128)(2,1)} %collective-permute-done.4.one, bf16[256,1024]{1,0:T(8,128)(2,1)} %collective-permute-done.5.two, bf16[256,1024]{1,0:T(8,128)(2,1)} %collective-permute-done.6.three, ...), custom_call_target="tpu_custom_call" | custom-call | flops 1 | bytes 1 | tf_op jit(solution)/shard_map/fisher_over_tokens/pallas_call | solution.py:66
  93.1 0.1 split_weights.3
  93.2 1.7 %collective-permute-start.14 = (bf16[2,512,256]{2,1,0:T(8,128)(2,1)S(1)}, bf16[2,512,256]{2,1,0:T(8,128)(2,1)S(1)}, u32[]{:S(2)}, u32[]{:S(2)}) collective-permute-start(bf16[2,512,256]{2,1,0:T(8,128)(2,1)S(1)} %get-tuple-element.58), channel_id=1, source_target_pairs={{0,2},{2,0},{4,6},{6,4},{8,10},{10,8},{12,14},{14,12},{1,3},{3,1},... | collective-permute-start | bytes 1572872 | tf_op jit(solution)/shard_map/ppermute | solution.py:322
  94.8 0.1 collective-permute-start.12
  94.9 1.8 %collective-permute-done.12.refs_1_ = bf16[256,512]{1,0:T(8,128)(2,1)S(1)} collective-permute-done((bf16[256,512]{1,0:T(8,128)(2,1)S(1)}, bf16[256,512]{1,0:T(8,128)(2,1)S(1)}, u32[]{:S(2)}, u32[]{:S(2)}) %collective-permute-start.12) | collective-permute-done | bytes 262176 | tf_op jit(solution)/shard_map/ppermute | solution.py:322
  96.8 0.7 weigh_members.3
  97.5 1.5 %collective-permute-start.15 = (bf16[3,128,256]{2,1,0:T(8,128)(2,1)S(1)}, bf16[3,128,256]{2,1,0:T(8,128)(2,1)S(1)}, u32[]{:S(2)}, u32[]{:S(2)}) collective-permute-start(bf16[3,128,256]{2,1,0:T(8,128)(2,1)S(1)} %get-tuple-element.59), channel_id=1, source_target_pairs={{0,16},{16,32},{32,48},{48,0},{64,80},{80,96},{96,112},{112,64},{1... | collective-permute-start | bytes 589832 | tf_op jit(solution)/shard_map/ppermute | solution.py:350
  99.0 2.4 %collective-permute-start.16 = (bf16[3,128,256]{2,1,0:T(8,128)(2,1)S(1)}, bf16[3,128,256]{2,1,0:T(8,128)(2,1)S(1)}, u32[]{:S(2)}, u32[]{:S(2)}) collective-permute-start(bf16[3,128,256]{2,1,0:T(8,128)(2,1)S(1)} %get-tuple-element.60), channel_id=1, source_target_pairs={{0,32},{16,48},{32,0},{48,16},{64,96},{80,112},{96,64},{112,80},{1... | collective-permute-start | bytes 589832 | tf_op jit(solution)/shard_map/ppermute | solution.py:350
  101.4 1.2 collective-permute-start.17
  102.6 2.5 %collective-permute-start.20 = (bf16[3,128,256]{2,1,0:T(8,128)(2,1)S(1)}, bf16[3,128,256]{2,1,0:T(8,128)(2,1)S(1)}, u32[]{:S(2)}, u32[]{:S(2)}) collective-permute-start(bf16[3,128,256]{2,1,0:T(8,128)(2,1)S(1)} %sum_over_z.2.after), channel_id=1, source_target_pairs={{0,0},{1,15},{2,64},{3,79},{4,4},{5,11},{6,68},{7,75},{8,6},{9,9},... | collective-permute-start | bytes 589832 | tf_op jit(solution)/shard_map/ppermute | solution.py:337
  105.1 1.3 %collective-permute-start.21 = (bf16[3,128,256]{2,1,0:T(8,128)(2,1)S(1)}, bf16[3,128,256]{2,1,0:T(8,128)(2,1)S(1)}, u32[]{:S(2)}, u32[]{:S(2)}) collective-permute-start(bf16[3,128,256]{2,1,0:T(8,128)(2,1)S(1)} %sum_over_z.2.after), channel_id=1, source_target_pairs={{64,0},{65,15},{66,64},{67,79},{68,4},{69,11},{70,68},{71,75},{72,... | collective-permute-start | bytes 589832 | tf_op jit(solution)/shard_map/ppermute | solution.py:337
  106.4 3.9 %collective-permute-done.16.two = bf16[3,128,256]{2,1,0:T(8,128)(2,1)S(1)} collective-permute-done((bf16[3,128,256]{2,1,0:T(8,128)(2,1)S(1)}, bf16[3,128,256]{2,1,0:T(8,128)(2,1)S(1)}, u32[]{:S(2)}, u32[]{:S(2)}) %collective-permute-start.16) | collective-permute-done | bytes 196640 | tf_op jit(solution)/shard_map/ppermute | solution.py:350
  110.3 0.3 sum_over_z.3
  110.6 3.4 %collective-permute-start.18 = (bf16[3,128,256]{2,1,0:T(8,128)(2,1)S(1)}, bf16[3,128,256]{2,1,0:T(8,128)(2,1)S(1)}, u32[]{:S(2)}, u32[]{:S(2)}) collective-permute-start(bf16[3,128,256]{2,1,0:T(8,128)(2,1)S(1)} %sum_over_z.3), channel_id=1, source_target_pairs={{0,1},{1,14},{2,65},{3,78},{4,5},{5,10},{6,69},{7,74},{8,7},{9,8},... | collective-permute-start | bytes 589832 | tf_op jit(solution)/shard_map/ppermute | solution.py:337
  114.0 0.7 collective-permute-start.19
  114.7 0.2 meet_over_y.1.sums
  114.9 8.0 %collective-permute-done.18.near = bf16[3,128,256]{2,1,0:T(8,128)(2,1)S(1)} collective-permute-done((bf16[3,128,256]{2,1,0:T(8,128)(2,1)S(1)}, bf16[3,128,256]{2,1,0:T(8,128)(2,1)S(1)}, u32[]{:S(2)}, u32[]{:S(2)}) %collective-permute-start.18) | collective-permute-done | bytes 196640 | tf_op jit(solution)/shard_map/ppermute | solution.py:337
  122.9 0.8 merge_members.1
  (23 shorter events, 0.2 us)
Async XLA Ops:
  2.1 11.3 %collective-permute-start = (bf16[768,2304]{1,0:T(8,128)(2,1)S(1)}, bf16[768,2304]{1,0:T(8,128)(2,1)S(1)}, u32[]{:S(2)}, u32[]{:S(2)}) collective-permute-start(bf16[768,2304]{1,0:T(8,128)(2,1)S(1)} %load_to_swap.2.after), channel_id=1, source_target_pairs={{0,2},{2,0},{4,6},{6,4},{8,10},{10,8},{12,14},{14,12},{1,3},{3,1},... | collective-permute-start | bytes 10616840 | tf_op jit(solution)/shard_map/ppermute | solution.py:322
  8.4 12.1 %collective-permute-start.1 = (bf16[768,2048]{1,0:T(8,128)(2,1)S(1)}, bf16[768,2048]{1,0:T(8,128)(2,1)S(1)}, u32[]{:S(2)}, u32[]{:S(2)}) collective-permute-start(bf16[768,2048]{1,0:T(8,128)(2,1)S(1)} %load_to_swap.3.after), channel_id=1, source_target_pairs={{0,2},{2,0},{4,6},{6,4},{8,10},{10,8},{12,14},{14,12},{1,3},{3,1},... | collective-permute-start | bytes 9437192 | tf_op jit(solution)/shard_map/ppermute | solution.py:322
  8.5 32.1 %collective-permute-start.3 = (bf16[2,1024,256]{2,1,0:T(8,128)(2,1)}, bf16[2,1024,256]{2,1,0:T(8,128)(2,1)S(1)}, u32[]{:S(2)}, u32[]{:S(2)}) collective-permute-start(bf16[2,1024,256]{2,1,0:T(8,128)(2,1)} %param.5), channel_id=1, source_target_pairs={{0,0},{2,12},{4,4},{6,8},{9,11},{11,7},{13,15},{15,3},{16,16},{18,... | collective-permute-start | bytes 3145736 | tf_op jit(solution)/shard_map/ppermute | solution.py:340
  13.4 27.4 %collective-permute-start.2 = (bf16[2,768,256]{2,1,0:T(8,128)(2,1)S(1)}, bf16[2,768,256]{2,1,0:T(8,128)(2,1)S(1)}, u32[]{:S(2)}, u32[]{:S(2)}) collective-permute-start(bf16[2,768,256]{2,1,0:T(8,128)(2,1)S(1)} %pair_grads.1.after), channel_id=1, source_target_pairs={{0,1},{1,0},{2,3},{3,2},{4,5},{5,4},{6,7},{7,6},{8,9},{9,8},{10,11... | collective-permute-start | bytes 2359304 | tf_op jit(solution)/shard_map/ppermute | solution.py:325
  17.4 30.3 %collective-permute-start.8 = (bf16[256,1024]{1,0:T(8,128)(2,1)S(1)}, bf16[256,1024]{1,0:T(8,128)(2,1)S(1)}, u32[]{:S(2)}, u32[]{:S(2)}) collective-permute-start(bf16[256,1024]{1,0:T(8,128)(2,1)S(1)} %get-tuple-element.37.after), channel_id=1, source_target_pairs={{0,8},{2,10},{4,12},{6,14},{8,0},{10,2},{12,4},{14,6},{1,9},{3,11}... | collective-permute-start | bytes 1572872 | tf_op jit(solution)/shard_map/ppermute | solution.py:328
  21.6 26.1 %collective-permute-start.9 = (bf16[256,1024]{1,0:T(8,128)(2,1)S(1)}, bf16[256,1024]{1,0:T(8,128)(2,1)S(1)}, u32[]{:S(2)}, u32[]{:S(2)}) collective-permute-start(bf16[256,1024]{1,0:T(8,128)(2,1)S(1)} %get-tuple-element.42.after), channel_id=1, source_target_pairs={{0,12},{2,14},{4,0},{6,2},{8,4},{10,6},{12,8},{14,10},{1,13},{3,15... | collective-permute-start | bytes 1572872 | tf_op jit(solution)/shard_map/ppermute | solution.py:328
  21.7 26.0 %collective-permute-start.7 = (bf16[256,1024]{1,0:T(8,128)(2,1)S(1)}, bf16[256,1024]{1,0:T(8,128)(2,1)S(1)}, u32[]{:S(2)}, u32[]{:S(2)}) collective-permute-start(bf16[256,1024]{1,0:T(8,128)(2,1)S(1)} %get-tuple-element.51), channel_id=1, source_target_pairs={{0,4},{2,6},{4,8},{6,10},{8,12},{10,14},{12,0},{14,2},{1,5},{3,7},... | collective-permute-start | bytes 1572872 | tf_op jit(solution)/shard_map/ppermute | solution.py:328
  40.7 8.9 %collective-permute-start.11 = (bf16[2,512,256]{2,1,0:T(8,128)(2,1)S(1)}, bf16[2,512,256]{2,1,0:T(8,128)(2,1)S(1)}, u32[]{:S(2)}, u32[]{:S(2)}) collective-permute-start(bf16[2,512,256]{2,1,0:T(8,128)(2,1)S(1)} %get-tuple-element.54), channel_id=1, source_target_pairs={{0,2},{2,0},{4,6},{6,4},{8,10},{10,8},{12,14},{14,12},{1,3},{3,1},... | collective-permute-start | bytes 1572872 | tf_op jit(solution)/shard_map/ppermute | solution.py:322
  40.8 52.3 %collective-permute-start.13 = (bf16[2,1024,256]{2,1,0:T(8,128)(2,1)}, bf16[2,1024,256]{2,1,0:T(8,128)(2,1)S(1)}, u32[]{:S(2)}, u32[]{:S(2)}) collective-permute-start(bf16[2,1024,256]{2,1,0:T(8,128)(2,1)} %param.5), channel_id=1, source_target_pairs={{1,2},{3,14},{5,6},{7,10},{8,9},{10,5},{12,13},{14,1},{17,18},{19,... | collective-permute-start | bytes 3145736 | tf_op jit(solution)/shard_map/ppermute | solution.py:340
  44.1 1.9 %copy-start.1 = (bf16[256,1024]{1,0:T(8,128)(2,1)}, bf16[256,1024]{1,0:T(8,128)(2,1)S(1)}, u32[]{:S(2)}) copy-start(bf16[256,1024]{1,0:T(8,128)(2,1)S(1)} %get-tuple-element.46.after) | copy-start | bytes 1572868
  44.1 1.9 %copy-start.2 = (bf16[256,1024]{1,0:T(8,128)(2,1)}, bf16[256,1024]{1,0:T(8,128)(2,1)S(1)}, u32[]{:S(2)}) copy-start(bf16[256,1024]{1,0:T(8,128)(2,1)S(1)} %get-tuple-element.48) | copy-start | bytes 1572868
  46.0 3.4 %copy-start = (bf16[256,1024]{1,0:T(8,128)(2,1)}, bf16[256,1024]{1,0:T(8,128)(2,1)S(1)}, u32[]{:S(2)}) copy-start(bf16[256,1024]{1,0:T(8,128)(2,1)S(1)} %get-tuple-element.49.after) | copy-start | bytes 1572868
  49.4 1.8 %collective-permute-start.10 = (bf16[256,512]{1,0:T(8,128)(2,1)S(1)}, bf16[256,512]{1,0:T(8,128)(2,1)S(1)}, u32[]{:S(2)}, u32[]{:S(2)}) collective-permute-start(bf16[256,512]{1,0:T(8,128)(2,1)S(1)} %get-tuple-element.53), channel_id=1, source_target_pairs={{0,2},{2,0},{4,6},{6,4},{8,10},{10,8},{12,14},{14,12},{1,3},{3,1},... | collective-permute-start | bytes 786440 | tf_op jit(solution)/shard_map/ppermute | solution.py:322
  52.8 17.0 %all-to-all-start = ((bf16[4,3,128,256]{3,2,1,0:T(8,128)(2,1)}), bf16[4,3,128,256]{3,2,1,0:T(8,128)(2,1)S(1)}, u32[]{:S(2)}, u32[]{:S(2)}) async-start(bf16[4,3,128,256]{3,2,1,0:T(8,128)(2,1)} %weigh_members.2), calls=%async_computation | async-start | bytes 1572864 | tf_op jit(solution)/shard_map/all_to_all | solution.py:393
  57.9 29.1 %collective-permute-start.6 = (bf16[256,1024]{1,0:T(8,128)(2,1)}, bf16[256,1024]{1,0:T(8,128)(2,1)}, u32[]{:S(2)}, u32[]{:S(2)}) collective-permute-start(bf16[256,1024]{1,0:T(8,128)(2,1)} %copy-done), channel_id=1, source_target_pairs={{0,12},{2,14},{4,0},{6,2},{8,4},{10,6},{12,8},{14,10},{1,13},{3,15... | collective-permute-start | bytes 1572872 | tf_op jit(solution)/shard_map/ppermute | solution.py:328
  64.5 25.5 %collective-permute-start.4 = (bf16[256,1024]{1,0:T(8,128)(2,1)}, bf16[256,1024]{1,0:T(8,128)(2,1)}, u32[]{:S(2)}, u32[]{:S(2)}) collective-permute-start(bf16[256,1024]{1,0:T(8,128)(2,1)} %copy-done.2), channel_id=1, source_target_pairs={{0,4},{2,6},{4,8},{6,10},{8,12},{10,14},{12,0},{14,2},{1,5},{3,7},... | collective-permute-start | bytes 1572872 | tf_op jit(solution)/shard_map/ppermute | solution.py:328
  64.6 25.5 %collective-permute-start.5 = (bf16[256,1024]{1,0:T(8,128)(2,1)}, bf16[256,1024]{1,0:T(8,128)(2,1)}, u32[]{:S(2)}, u32[]{:S(2)}) collective-permute-start(bf16[256,1024]{1,0:T(8,128)(2,1)} %copy-done.1), channel_id=1, source_target_pairs={{0,8},{2,10},{4,12},{6,14},{8,0},{10,2},{12,4},{14,6},{1,9},{3,11}... | collective-permute-start | bytes 1572872 | tf_op jit(solution)/shard_map/ppermute | solution.py:328
  93.2 3.6 %collective-permute-start.14 = (bf16[2,512,256]{2,1,0:T(8,128)(2,1)S(1)}, bf16[2,512,256]{2,1,0:T(8,128)(2,1)S(1)}, u32[]{:S(2)}, u32[]{:S(2)}) collective-permute-start(bf16[2,512,256]{2,1,0:T(8,128)(2,1)S(1)} %get-tuple-element.58), channel_id=1, source_target_pairs={{0,2},{2,0},{4,6},{6,4},{8,10},{10,8},{12,14},{14,12},{1,3},{3,1},... | collective-permute-start | bytes 1572872 | tf_op jit(solution)/shard_map/ppermute | solution.py:322
  94.8 1.9 %collective-permute-start.12 = (bf16[256,512]{1,0:T(8,128)(2,1)S(1)}, bf16[256,512]{1,0:T(8,128)(2,1)S(1)}, u32[]{:S(2)}, u32[]{:S(2)}) collective-permute-start(bf16[256,512]{1,0:T(8,128)(2,1)S(1)} %get-tuple-element.56), channel_id=1, source_target_pairs={{0,2},{2,0},{4,6},{6,4},{8,10},{10,8},{12,14},{14,12},{1,3},{3,1},... | collective-permute-start | bytes 786440 | tf_op jit(solution)/shard_map/ppermute | solution.py:322
  97.5 8.9 %collective-permute-start.15 = (bf16[3,128,256]{2,1,0:T(8,128)(2,1)S(1)}, bf16[3,128,256]{2,1,0:T(8,128)(2,1)S(1)}, u32[]{:S(2)}, u32[]{:S(2)}) collective-permute-start(bf16[3,128,256]{2,1,0:T(8,128)(2,1)S(1)} %get-tuple-element.59), channel_id=1, source_target_pairs={{0,16},{16,32},{32,48},{48,0},{64,80},{80,96},{96,112},{112,64},{1... | collective-permute-start | bytes 589832 | tf_op jit(solution)/shard_map/ppermute | solution.py:350
  99.0 11.3 %collective-permute-start.16 = (bf16[3,128,256]{2,1,0:T(8,128)(2,1)S(1)}, bf16[3,128,256]{2,1,0:T(8,128)(2,1)S(1)}, u32[]{:S(2)}, u32[]{:S(2)}) collective-permute-start(bf16[3,128,256]{2,1,0:T(8,128)(2,1)S(1)} %get-tuple-element.60), channel_id=1, source_target_pairs={{0,32},{16,48},{32,0},{48,16},{64,96},{80,112},{96,64},{112,80},{1... | collective-permute-start | bytes 589832 | tf_op jit(solution)/shard_map/ppermute | solution.py:350
  101.4 8.9 %collective-permute-start.17 = (bf16[3,128,256]{2,1,0:T(8,128)(2,1)S(1)}, bf16[3,128,256]{2,1,0:T(8,128)(2,1)S(1)}, u32[]{:S(2)}, u32[]{:S(2)}) collective-permute-start(bf16[3,128,256]{2,1,0:T(8,128)(2,1)S(1)} %get-tuple-element.61), channel_id=1, source_target_pairs={{0,48},{16,0},{32,16},{48,32},{64,112},{80,64},{96,80},{112,96},{1... | collective-permute-start | bytes 589832 | tf_op jit(solution)/shard_map/ppermute | solution.py:350
  102.6 12.1 %collective-permute-start.20 = (bf16[3,128,256]{2,1,0:T(8,128)(2,1)S(1)}, bf16[3,128,256]{2,1,0:T(8,128)(2,1)S(1)}, u32[]{:S(2)}, u32[]{:S(2)}) collective-permute-start(bf16[3,128,256]{2,1,0:T(8,128)(2,1)S(1)} %sum_over_z.2.after), channel_id=1, source_target_pairs={{0,0},{1,15},{2,64},{3,79},{4,4},{5,11},{6,68},{7,75},{8,6},{9,9},... | collective-permute-start | bytes 589832 | tf_op jit(solution)/shard_map/ppermute | solution.py:337
  105.1 9.6 %collective-permute-start.21 = (bf16[3,128,256]{2,1,0:T(8,128)(2,1)S(1)}, bf16[3,128,256]{2,1,0:T(8,128)(2,1)S(1)}, u32[]{:S(2)}, u32[]{:S(2)}) collective-permute-start(bf16[3,128,256]{2,1,0:T(8,128)(2,1)S(1)} %sum_over_z.2.after), channel_id=1, source_target_pairs={{64,0},{65,15},{66,64},{67,79},{68,4},{69,11},{70,68},{71,75},{72,... | collective-permute-start | bytes 589832 | tf_op jit(solution)/shard_map/ppermute | solution.py:337
  110.6 12.3 %collective-permute-start.18 = (bf16[3,128,256]{2,1,0:T(8,128)(2,1)S(1)}, bf16[3,128,256]{2,1,0:T(8,128)(2,1)S(1)}, u32[]{:S(2)}, u32[]{:S(2)}) collective-permute-start(bf16[3,128,256]{2,1,0:T(8,128)(2,1)S(1)} %sum_over_z.3), channel_id=1, source_target_pairs={{0,1},{1,14},{2,65},{3,78},{4,5},{5,10},{6,69},{7,74},{8,7},{9,8},... | collective-permute-start | bytes 589832 | tf_op jit(solution)/shard_map/ppermute | solution.py:337
  114.0 8.9 %collective-permute-start.19 = (bf16[3,128,256]{2,1,0:T(8,128)(2,1)S(1)}, bf16[3,128,256]{2,1,0:T(8,128)(2,1)S(1)}, u32[]{:S(2)}, u32[]{:S(2)}) collective-permute-start(bf16[3,128,256]{2,1,0:T(8,128)(2,1)S(1)} %sum_over_z.3), channel_id=1, source_target_pairs={{64,1},{65,14},{66,65},{67,78},{68,5},{69,10},{70,69},{71,74},{72,... | collective-permute-start | bytes 589832 | tf_op jit(solution)/shard_map/ppermute | solution.py:337

commit v9 on v7

--- a/solution.py
+++ b/solution.py
@@ -272,12 +272,12 @@
     return 2 * (x % 2) if x // 2 == half else 2 * ((3 - x) % 2) + 1
 
 
-def weight_pairs(phase):
+def weight_pairs():
     pairs = []
     for tok in range(X * CORES):
         half, local = divmod(tok, 4)
-        col = half ^ phase
-        pairs.append((tok * 2 + col, (keeper(local, half) * 2 + col) * 2 + half))
+        for col in range(2):
+            pairs.append((tok * 2 + col, (keeper(local, half) * 2 + col) * 2 + half))
     return pairs
 
 
@@ -333,8 +333,8 @@
     def results(phase, sums):
         return [lax.ppermute(sums, ("member", "tok", "col"), result_pairs(phase, y_lo)) for y_lo in range(2)]
 
-    def bring_weights(phase, after):
-        arrived = lax.ppermute(weights, ("tok", "col"), weight_pairs(phase))
+    def bring_weights(after):
+        arrived = lax.ppermute(weights, ("tok", "col"), weight_pairs())
         half_shape = ((2, weights.shape[1] // 2, outs), BF16)
         own, send = call(split_kernel, "split_weights", [half_shape, half_shape], [], [arrived, after])
         return own, swap_cores(send)
@@ -350,13 +350,13 @@
         load_first_kernel, "load_to_swap", ((tokens, 4 * wide + outs), BF16), [inputs, grads], [], [dma((4,)), dma]
     )
     x_got0 = swap_cores(x_send0)
+    x_send1 = call(load_second_kernel, "load_to_swap", x_shape, [inputs], [x_send0], [dma((4,))])
+    x_got1 = swap_cores(x_send1)
     x_own0, g_own, gt_own, part0 = call(
-        own_first_kernel, "fisher_of_own_tokens", [x_shape, g_shape, gt_shape, part_shape], [inputs, grads], [x_send0],
+        own_first_kernel, "fisher_of_own_tokens", [x_shape, g_shape, gt_shape, part_shape], [inputs, grads], [x_send1],
         [dma((4,)), dma],
     )
-    x_send1 = call(load_second_kernel, "load_to_swap", x_shape, [inputs], [gt_own], [dma((4,))])
-    x_got1 = swap_cores(x_send1)
-    g_pair = call(pair_kernel, "pair_grads", ((2, tokens, outs), BF16), [], [g_own, x_got0, x_send1])
+    g_pair = call(pair_kernel, "pair_grads", ((2, tokens, outs), BF16), [], [g_own, x_got0, gt_own])
     g_other = swap_cols(g_pair)
     sent, kept00, gt_got = call(
         add_first_kernel, "fisher_of_both_cores", [sent_shape, kept_shape, gt_shape], [], [x_got0, part0, g_pair]
@@ -370,14 +370,14 @@
     )
     swap01 = swap_x(1, sent)
     part00 = middle(3, swap00, kept00, kept01)
-    w0 = bring_weights(0, part00[0])
 
     sent, kept10, gt_own, gt_got = call(
         both_first_kernel, "fisher_of_other_grads", [sent_shape, kept_shape, gt_shape, gt_shape], [],
-        [x_own0, x_got0, g_other, w0[0]],
+        [x_own0, x_got0, g_other, part00[0]],
     )
     swap10 = swap_x(1, sent)
-    part01 = middle(3, swap01, kept01, kept10)
+    moved = bring_weights(kept10)
+    part01 = middle(3, swap01, kept01, moved[0])
     sent, kept11 = call(
         both_second_kernel, "fisher_of_other_grads", [sent_shape, kept_shape], [],
         [x_own1, x_got1, gt_own, gt_got, part01[0]],
@@ -386,13 +386,12 @@
 
     settled0 = settle(part00, kept11)
     own0, other0 = join(settled0, part01, kept11)
-    words0 = weigh(0, own0, other0, w0, own0)
+    words0 = weigh(0, own0, other0, moved, own0)
     part10 = middle(3, swap10, kept10, words0[3])
     first = call(sum_kernel, "sum_over_z", words, [], [*words0, part10[0]])
     part11 = middle(1, swap11, kept11, first)
     own1, other1 = join(settle(part10, part11[0]), part11, first)
-    w1 = bring_weights(1, own1)
-    words1 = weigh(1, own1, other1, w1, w1[0])
+    words1 = weigh(1, own1, other1, moved, own1)
     met = call(meet_kernel, "meet_over_y", sums, [], [*results(0, first), own1])
     second = call(sum_kernel, "sum_over_z", words, [], [*words1, own1])
     near, far = results(1, second)

time: 119 us -> 114 us (0.958)
  waiting for transfers between devices: 55.9 us -> 44.8 us
  starting transfers between devices: 38 us -> 44.2 us
    ppermute x8, waiting for transfers between devices: 34.4 us -> 18 us  [swap_x(): return lax.ppermute(sent, 'tok', x_pairs(flip))]
    ppermute x1, waiting for transfers between devices: 0.01 us -> 9.36 us  [swap_cols(): return lax.ppermute(send, 'col', [(0, 1), (1, 0)])]
    ppermute x6, waiting for transfers between devices: 10.1 us -> 7.16 us  [weigh(): return [lax.ppermute(v, 'member', z_pairs(d)) for d, v in send] + [own_sums]]
    ppermute x8, starting transfers between devices: 5.75 us -> 8.43 us  [swap_x(): return lax.ppermute(sent, 'tok', x_pairs(flip))]
    ppermute x1, starting transfers between devices: 0.09 us -> 2.49 us  [swap_cols(): return lax.ppermute(send, 'col', [(0, 1), (1, 0)])]
    ppermute x4, starting transfers between devices: 10.9 us -> 13.1 us  [results(): lax.ppermute(sums, ('member', 'tok', 'col'), result_pairs(phase, y_lo))]
    ppermute x2 -> x1, starting transfers between devices: 6.11 us -> 4.73 us  [bring_weights(): arrived = lax.ppermute(weights, ('tok', 'col'), weight_pairs())]
    ppermute x6 -> x5, waiting for transfers between devices: 3.34 us -> 2.33 us  [swap_cores(): return lax.ppermute(send, 'tok', [(t, t ^ 1) for t in range(8)])]
  transfers between devices with their start and end apart: 27 -> 25, of which waited for: 12 -> 10; matrix products, arithmetic and copies ran while one was open for 0% -> 0% of each run, Pallas kernels for 17% -> 17%
where the time goes in v9:
time: 114 us; the launch traced here: 113 us
  waiting for transfers between devices  44.8 us (39%)
  starting transfers between devices  44.2 us (39%)
  Pallas kernels  24 us (21%)
    pallas_call x23, Pallas kernels, call(): pl.pallas_call(kernel, out_shape=shapes, in_specs=[HBM] * len(hbm) + [VME...  23.1 us
    ppermute x8, waiting for transfers between devices, swap_x(): return lax.ppermute(sent, 'tok', x_pairs(flip))  18 us
    ppermute x4, starting transfers between devices, results(): lax.ppermute(sums, ('member', 'tok', 'col'), result_pairs(phase, y_lo))  13.1 us
    ppermute x6, starting transfers between devices, weigh(): return [lax.ppermute(v, 'member', z_pairs(d)) for d, v in send] + [own_sums]  9.56 us
    ppermute x1, waiting for transfers between devices, swap_cols(): return lax.ppermute(send, 'col', [(0, 1), (1, 0)])  9.36 us
    ppermute x8, starting transfers between devices, swap_x(): return lax.ppermute(sent, 'tok', x_pairs(flip))  8.43 us
    ppermute x4, waiting for transfers between devices, results(): lax.ppermute(sums, ('member', 'tok', 'col'), result_pairs(phase, y_lo))  8.04 us
    ppermute x6, waiting for transfers between devices, weigh(): return [lax.ppermute(v, 'member', z_pairs(d)) for d, v in send] + [own_sums]  7.16 us
  transfers between devices with their start and end apart: 25, of which 10 were waited for; matrix products, arithmetic and copies ran while one was open for 0% of the time, Pallas kernels for 17%

profile of v9, /device:TPU:1, one launch (start us, length us, event | category | flops | bytes accessed | tf_op | source)
XLA Modules:
  0.0 113.3 jit_solution(15711249252020955284)
XLA Ops:
  0.0 2.0 %load_to_swap.2.after = bf16[768,2304]{1,0:T(8,128)(2,1)S(1)} custom-call(bf16[2,768,4096]{2,1,0:T(8,128)(2,1)} %x_ref.7, bf16[2,768,256]{2,1,0:T(8,128)(2,1)} %g_ref.3), custom_call_target="tpu_custom_call" | custom-call | flops 1 | bytes 1 | tf_op jit(solution)/shard_map/load_to_swap/pallas_call | solution.py:67
  2.0 1.5 %collective-permute-start = (bf16[768,2304]{1,0:T(8,128)(2,1)S(1)}, bf16[768,2304]{1,0:T(8,128)(2,1)S(1)}, u32[]{:S(2)}, u32[]{:S(2)}) collective-permute-start(bf16[768,2304]{1,0:T(8,128)(2,1)S(1)} %load_to_swap.2.after), channel_id=1, source_target_pairs={{0,2},{2,0},{4,6},{6,4},{8,10},{10,8},{12,14},{14,12},{1,3},{3,1},... | collective-permute-start | bytes 10616840 | tf_op jit(solution)/shard_map/ppermute | solution.py:314
  3.5 1.9 %load_to_swap.3.after = bf16[4,768,512]{2,1,0:T(8,128)(2,1)S(1)} custom-call(bf16[2,768,4096]{2,1,0:T(8,128)(2,1)} %x_ref.7, bf16[768,2304]{1,0:T(8,128)(2,1)S(1)} %load_to_swap.2.after), custom_call_target="tpu_custom_call" | custom-call | flops 1 | bytes 1 | tf_op jit(solution)/shard_map/load_to_swap/pallas_call | solution.py:67
  5.7 4.7 %collective-permute-start.7 = (bf16[2,1024,256]{2,1,0:T(8,128)(2,1)S(1)}, bf16[2,1024,256]{2,1,0:T(8,128)(2,1)S(1)}, u32[]{:S(2)}, u32[]{:S(2)}) collective-permute-start(bf16[2,1024,256]{2,1,0:T(8,128)(2,1)S(1)} %copy-done), channel_id=1, source_target_pairs={{0,0},{1,2},{2,12},{3,14},{4,4},{5,6},{6,8},{7,10},{8,9},{9,11},{1... | collective-permute-start | bytes 3145736 | tf_op jit(solution)/shard_map/ppermute | solution.py:337
  10.4 3.2 %fisher_of_own_tokens.2 = (bf16[4,768,512]{2,1,0:T(8,128)(2,1)S(1)}, bf16[768,256]{1,0:T(8,128)(2,1)S(1)}, bf16[256,768]{1,0:T(8,128)(2,1)S(1)}, f32[4,256,512]{2,1,0:T(8,128)S(1)}) custom-call(bf16[2,768,4096]{2,1,0:T(8,128)(2,1)} %x_ref.7, bf16[2,768,256]{2,1,0:T(8,128)(2,1)} %g_ref.3, bf16[4,768,512]{2,1,0:T(8,128)(2,1)S(1)} %load_to_swap.3.after), custom_call_target="tpu_custom_call" | custom-call | flops 1 | bytes 1 | tf_op jit(solution)/shard_map/fisher_of_own_tokens/pallas_call | solution.py:67
  13.7 2.5 %collective-permute-start.1 = (bf16[2,768,256]{2,1,0:T(8,128)(2,1)S(1)}, bf16[2,768,256]{2,1,0:T(8,128)(2,1)S(1)}, u32[]{:S(2)}, u32[]{:S(2)}) collective-permute-start(bf16[2,768,256]{2,1,0:T(8,128)(2,1)S(1)} %pair_grads.1.after), channel_id=1, source_target_pairs={{0,1},{1,0},{2,3},{3,2},{4,5},{5,4},{6,7},{7,6},{8,9},{9,8},{10,11... | collective-permute-start | bytes 2359304 | tf_op jit(solution)/shard_map/ppermute | solution.py:317
  16.2 1.2 %fisher_of_both_cores.2 = (bf16[2,256,512]{2,1,0:T(8,128)(2,1)S(1)}, f32[2,256,512]{2,1,0:T(8,128)S(1)}, bf16[256,768]{1,0:T(8,128)(2,1)S(1)}) custom-call(bf16[768,2304]{1,0:T(8,128)(2,1)S(1)} %collective-permute-done.got.x_ref.xb_ref, f32[4,256,512]{2,1,0:T(8,128)S(1)} %get-tuple-element.47.part_ref, bf16[2,768,256]{2,1,0:T(8,128)(2,1)S(1)} %pair_grads.1.after), custom_call_target="tpu_custom_call" | custom-call | flops 1 | bytes 1 | tf_op jit(solution)/shard_map/fisher_of_both_cores/pallas_call | solution.py:67
  17.5 2.7 %fisher_of_own_tokens.3 = (bf16[4,768,512]{2,1,0:T(8,128)(2,1)S(1)}, f32[4,256,512]{2,1,0:T(8,128)S(1)}) custom-call(bf16[2,768,4096]{2,1,0:T(8,128)(2,1)} %x_ref.7, bf16[256,768]{1,0:T(8,128)(2,1)S(1)} %get-tuple-element.46.after.gt_ref, f32[2,256,512]{2,1,0:T(8,128)S(1)} %get-tuple-element.48.after.kept_ref), custom_call_target="tpu_custom_call" | custom-call | flops 1 | bytes 1 | tf_op jit(solution)/shard_map/fisher_of_own_tokens/pallas_call | solution.py:67
  20.2 1.1 fisher_of_both_cores.3
  21.3 1.5 %collective-permute-start.6 = (bf16[2,256,512]{2,1,0:T(8,128)(2,1)S(1)}, bf16[2,256,512]{2,1,0:T(8,128)(2,1)S(1)}, u32[]{:S(2)}, u32[]{:S(2)}) collective-permute-start(bf16[2,256,512]{2,1,0:T(8,128)(2,1)S(1)} %get-tuple-element.60), channel_id=1, source_target_pairs={{0,4},{2,6},{4,0},{6,2},{8,12},{10,14},{12,8},{14,10},{1,5},{3,7},... | collective-permute-start | bytes 1572872 | tf_op jit(solution)/shard_map/ppermute | solution.py:320
  22.8 8.6 %collective-permute-done.2.got_ref = bf16[2,256,512]{2,1,0:T(8,128)(2,1)S(1)} collective-permute-done((bf16[2,256,512]{2,1,0:T(8,128)(2,1)S(1)}, bf16[2,256,512]{2,1,0:T(8,128)(2,1)S(1)}, u32[]{:S(2)}, u32[]{:S(2)}) %collective-permute-start.2) | collective-permute-done | bytes 524320 | tf_op jit(solution)/shard_map/ppermute | solution.py:320
  31.4 0.7 fisher_over_first_swap.4
  32.2 9.4 %collective-permute-done.1.g_ref = bf16[2,768,256]{2,1,0:T(8,128)(2,1)S(1)} collective-permute-done((bf16[2,768,256]{2,1,0:T(8,128)(2,1)S(1)}, bf16[2,768,256]{2,1,0:T(8,128)(2,1)S(1)}, u32[]{:S(2)}, u32[]{:S(2)}) %collective-permute-start.1) | collective-permute-done | bytes 786464 | tf_op jit(solution)/shard_map/ppermute | solution.py:317
  41.6 1.9 %fisher_of_other_grads.2 = (bf16[2,256,512]{2,1,0:T(8,128)(2,1)S(1)}, f32[2,256,512]{2,1,0:T(8,128)S(1)}, bf16[256,768]{1,0:T(8,128)(2,1)S(1)}, bf16[256,768]{1,0:T(8,128)(2,1)S(1)}) custom-call(bf16[4,768,512]{2,1,0:T(8,128)(2,1)S(1)} %get-tuple-element.44.xa_ref, bf16[768,2304]{1,0:T(8,128)(2,1)S(1)} %collective-permute-done.got.x_ref.xb_ref, ...), custom_call_target="tpu_custom_call" | custom-call | flops 1 | bytes 1 | tf_op jit(solution)/shard_map/fisher_of_other_grads/pallas_call | solution.py:67
  43.7 0.7 fisher_over_first_swap.5
  44.4 2.9 %collective-permute-start.8 = (bf16[256,512]{1,0:T(8,128)(2,1)S(1)}, bf16[256,512]{1,0:T(8,128)(2,1)S(1)}, u32[]{:S(2)}, u32[]{:S(2)}) collective-permute-start(bf16[256,512]{1,0:T(8,128)(2,1)S(1)} %get-tuple-element.64), channel_id=1, source_target_pairs={{0,12},{2,14},{4,8},{6,10},{8,4},{10,6},{12,0},{14,2},{1,13},{3,15... | collective-permute-start | bytes 786440 | tf_op jit(solution)/shard_map/ppermute | solution.py:320
  47.3 0.8 collective-permute-start.10
  48.1 1.9 %fisher_of_other_grads.3 = (bf16[2,256,512]{2,1,0:T(8,128)(2,1)S(1)}, f32[2,256,512]{2,1,0:T(8,128)S(1)}) custom-call(bf16[4,768,512]{2,1,0:T(8,128)(2,1)S(1)} %get-tuple-element.52.after.xa_ref, bf16[4,768,512]{2,1,0:T(8,128)(2,1)S(1)} %collective-permute-done.3.x_ref.xb_ref, bf16[256,768]{1,0:T(8,128)(2,1)S(1)} %get-tuple-element.58.gta_ref, ...), custom_call_target="tpu_custom_call" | custom-call | flops 1 | bytes 1 | tf_op jit(solution)/shard_map/fisher_of_other_grads/pallas_call | solution.py:67
  50.2 0.3 fisher_over_tokens.4.first_ref
  50.5 3.0 %collective-permute-done.8.got = bf16[256,512]{1,0:T(8,128)(2,1)S(1)} collective-permute-done((bf16[256,512]{1,0:T(8,128)(2,1)S(1)}, bf16[256,512]{1,0:T(8,128)(2,1)S(1)}, u32[]{:S(2)}, u32[]{:S(2)}) %collective-permute-start.8) | collective-permute-done | bytes 262176 | tf_op jit(solution)/shard_map/ppermute | solution.py:320
  53.6 0.6 fisher_over_tokens.5
  54.2 1.3 %collective-permute-start.9 = (bf16[256,512]{1,0:T(8,128)(2,1)S(1)}, bf16[256,512]{1,0:T(8,128)(2,1)S(1)}, u32[]{:S(2)}, u32[]{:S(2)}) collective-permute-start(bf16[256,512]{1,0:T(8,128)(2,1)S(1)} %get-tuple-element.66), channel_id=1, source_target_pairs={{0,2},{2,0},{4,6},{6,4},{8,10},{10,8},{12,14},{14,12},{1,3},{3,1},... | collective-permute-start | bytes 786440 | tf_op jit(solution)/shard_map/ppermute | solution.py:314
  55.5 1.2 %collective-permute-done.9.refs_1_ = bf16[256,512]{1,0:T(8,128)(2,1)S(1)} collective-permute-done((bf16[256,512]{1,0:T(8,128)(2,1)S(1)}, bf16[256,512]{1,0:T(8,128)(2,1)S(1)}, u32[]{:S(2)}, u32[]{:S(2)}) %collective-permute-start.9) | collective-permute-done | bytes 262176 | tf_op jit(solution)/shard_map/ppermute | solution.py:314
  56.6 0.7 weigh_members.2
  57.3 1.7 %collective-permute-start.13 = (bf16[3,128,256]{2,1,0:T(8,128)(2,1)S(1)}, bf16[3,128,256]{2,1,0:T(8,128)(2,1)S(1)}, u32[]{:S(2)}, u32[]{:S(2)}) collective-permute-start(bf16[3,128,256]{2,1,0:T(8,128)(2,1)S(1)} %get-tuple-element.72), channel_id=1, source_target_pairs={{0,16},{16,32},{32,48},{48,0},{64,80},{80,96},{96,112},{112,64},{1... | collective-permute-start | bytes 589832 | tf_op jit(solution)/shard_map/ppermute | solution.py:347
  59.0 3.3 %collective-permute-start.14 = (bf16[3,128,256]{2,1,0:T(8,128)(2,1)S(1)}, bf16[3,128,256]{2,1,0:T(8,128)(2,1)S(1)}, u32[]{:S(2)}, u32[]{:S(2)}) collective-permute-start(bf16[3,128,256]{2,1,0:T(8,128)(2,1)S(1)} %get-tuple-element.73), channel_id=1, source_target_pairs={{0,32},{16,48},{32,0},{48,16},{64,96},{80,112},{96,64},{112,80},{1... | collective-permute-start | bytes 589832 | tf_op jit(solution)/shard_map/ppermute | solution.py:347
  62.3 0.7 collective-permute-start.15
  63.1 0.7 fisher_over_first_swap.6
  63.8 3.5 %collective-permute-start.11 = (bf16[256,512]{1,0:T(8,128)(2,1)S(1)}, bf16[256,512]{1,0:T(8,128)(2,1)S(1)}, u32[]{:S(2)}, u32[]{:S(2)}) collective-permute-start(bf16[256,512]{1,0:T(8,128)(2,1)S(1)} %get-tuple-element.70), channel_id=1, source_target_pairs={{0,12},{2,14},{4,8},{6,10},{8,4},{10,6},{12,0},{14,2},{1,13},{3,15... | collective-permute-start | bytes 786440 | tf_op jit(solution)/shard_map/ppermute | solution.py:320
  67.3 3.9 %collective-permute-done.14.two = bf16[3,128,256]{2,1,0:T(8,128)(2,1)S(1)} collective-permute-done((bf16[3,128,256]{2,1,0:T(8,128)(2,1)S(1)}, bf16[3,128,256]{2,1,0:T(8,128)(2,1)S(1)}, u32[]{:S(2)}, u32[]{:S(2)}) %collective-permute-start.14) | collective-permute-done | bytes 196640 | tf_op jit(solution)/shard_map/ppermute | solution.py:347
  71.2 0.3 sum_over_z.2.after
  71.6 0.7 fisher_over_first_swap.7
  72.4 0.3 collective-permute-done.11.got
  73.0 6.0 %collective-permute-done.16.got = bf16[256,512]{1,0:T(8,128)(2,1)S(1)} collective-permute-done((bf16[256,512]{1,0:T(8,128)(2,1)S(1)}, bf16[256,512]{1,0:T(8,128)(2,1)S(1)}, u32[]{:S(2)}, u32[]{:S(2)}) %collective-permute-start.16) | collective-permute-done | bytes 262176 | tf_op jit(solution)/shard_map/ppermute | solution.py:320
  79.0 0.6 fisher_over_tokens.7
  79.6 2.2 %collective-permute-start.17 = (bf16[256,512]{1,0:T(8,128)(2,1)S(1)}, bf16[256,512]{1,0:T(8,128)(2,1)S(1)}, u32[]{:S(2)}, u32[]{:S(2)}) collective-permute-start(bf16[256,512]{1,0:T(8,128)(2,1)S(1)} %get-tuple-element.78), channel_id=1, source_target_pairs={{0,2},{2,0},{4,6},{6,4},{8,10},{10,8},{12,14},{14,12},{1,3},{3,1},... | collective-permute-start | bytes 786440 | tf_op jit(solution)/shard_map/ppermute | solution.py:314
  81.8 1.2 %collective-permute-done.17.refs_1_ = bf16[256,512]{1,0:T(8,128)(2,1)S(1)} collective-permute-done((bf16[256,512]{1,0:T(8,128)(2,1)S(1)}, bf16[256,512]{1,0:T(8,128)(2,1)S(1)}, u32[]{:S(2)}, u32[]{:S(2)}) %collective-permute-start.17) | collective-permute-done | bytes 262176 | tf_op jit(solution)/shard_map/ppermute | solution.py:314
  83.0 0.7 weigh_members.3
  83.7 1.4 %collective-permute-start.18 = (bf16[3,128,256]{2,1,0:T(8,128)(2,1)S(1)}, bf16[3,128,256]{2,1,0:T(8,128)(2,1)S(1)}, u32[]{:S(2)}, u32[]{:S(2)}) collective-permute-start(bf16[3,128,256]{2,1,0:T(8,128)(2,1)S(1)} %get-tuple-element.79), channel_id=1, source_target_pairs={{0,16},{16,32},{32,48},{48,0},{64,80},{80,96},{96,112},{112,64},{1... | collective-permute-start | bytes 589832 | tf_op jit(solution)/shard_map/ppermute | solution.py:347
  85.0 2.5 %collective-permute-start.19 = (bf16[3,128,256]{2,1,0:T(8,128)(2,1)S(1)}, bf16[3,128,256]{2,1,0:T(8,128)(2,1)S(1)}, u32[]{:S(2)}, u32[]{:S(2)}) collective-permute-start(bf16[3,128,256]{2,1,0:T(8,128)(2,1)S(1)} %get-tuple-element.80), channel_id=1, source_target_pairs={{0,32},{16,48},{32,0},{48,16},{64,96},{80,112},{96,64},{112,80},{1... | collective-permute-start | bytes 589832 | tf_op jit(solution)/shard_map/ppermute | solution.py:347
  87.5 4.3 %collective-permute-start.23 = (bf16[3,128,256]{2,1,0:T(8,128)(2,1)S(1)}, bf16[3,128,256]{2,1,0:T(8,128)(2,1)S(1)}, u32[]{:S(2)}, u32[]{:S(2)}) collective-permute-start(bf16[3,128,256]{2,1,0:T(8,128)(2,1)S(1)} %sum_over_z.2.after), channel_id=1, source_target_pairs={{0,0},{1,15},{2,64},{3,79},{4,4},{5,11},{6,68},{7,75},{8,6},{9,9},... | collective-permute-start | bytes 589832 | tf_op jit(solution)/shard_map/ppermute | solution.py:334
  91.8 1.3 %collective-permute-start.24 = (bf16[3,128,256]{2,1,0:T(8,128)(2,1)S(1)}, bf16[3,128,256]{2,1,0:T(8,128)(2,1)S(1)}, u32[]{:S(2)}, u32[]{:S(2)}) collective-permute-start(bf16[3,128,256]{2,1,0:T(8,128)(2,1)S(1)} %sum_over_z.2.after), channel_id=1, source_target_pairs={{64,0},{65,15},{66,64},{67,79},{68,4},{69,11},{70,68},{71,75},{72,... | collective-permute-start | bytes 589832 | tf_op jit(solution)/shard_map/ppermute | solution.py:334
  93.1 3.3 %collective-permute-done.19.two = bf16[3,128,256]{2,1,0:T(8,128)(2,1)S(1)} collective-permute-done((bf16[3,128,256]{2,1,0:T(8,128)(2,1)S(1)}, bf16[3,128,256]{2,1,0:T(8,128)(2,1)S(1)}, u32[]{:S(2)}, u32[]{:S(2)}) %collective-permute-start.19) | collective-permute-done | bytes 196640 | tf_op jit(solution)/shard_map/ppermute | solution.py:347
  96.4 0.3 sum_over_z.3
  96.7 6.8 %collective-permute-start.21 = (bf16[3,128,256]{2,1,0:T(8,128)(2,1)S(1)}, bf16[3,128,256]{2,1,0:T(8,128)(2,1)S(1)}, u32[]{:S(2)}, u32[]{:S(2)}) collective-permute-start(bf16[3,128,256]{2,1,0:T(8,128)(2,1)S(1)} %sum_over_z.3), channel_id=1, source_target_pairs={{0,1},{1,14},{2,65},{3,78},{4,5},{5,10},{6,69},{7,74},{8,7},{9,8},... | collective-permute-start | bytes 589832 | tf_op jit(solution)/shard_map/ppermute | solution.py:334
  103.6 0.7 collective-permute-start.22
  104.5 8.0 %collective-permute-done.21.near = bf16[3,128,256]{2,1,0:T(8,128)(2,1)S(1)} collective-permute-done((bf16[3,128,256]{2,1,0:T(8,128)(2,1)S(1)}, bf16[3,128,256]{2,1,0:T(8,128)(2,1)S(1)}, u32[]{:S(2)}, u32[]{:S(2)}) %collective-permute-start.21) | collective-permute-done | bytes 196640 | tf_op jit(solution)/shard_map/ppermute | solution.py:334
  112.5 0.8 merge_members.1
  (28 shorter events, 1.4 us)
Async XLA Ops:
  2.0 3.6 %copy-start = (bf16[2,1024,256]{2,1,0:T(8,128)(2,1)S(1)}, bf16[2,1024,256]{2,1,0:T(8,128)(2,1)}, u32[]{:S(2)}) copy-start(bf16[2,1024,256]{2,1,0:T(8,128)(2,1)} %param.5) | copy-start | bytes 3145732
  2.0 11.6 %collective-permute-start = (bf16[768,2304]{1,0:T(8,128)(2,1)S(1)}, bf16[768,2304]{1,0:T(8,128)(2,1)S(1)}, u32[]{:S(2)}, u32[]{:S(2)}) collective-permute-start(bf16[768,2304]{1,0:T(8,128)(2,1)S(1)} %load_to_swap.2.after), channel_id=1, source_target_pairs={{0,2},{2,0},{4,6},{6,4},{8,10},{10,8},{12,14},{14,12},{1,3},{3,1},... | collective-permute-start | bytes 10616840 | tf_op jit(solution)/shard_map/ppermute | solution.py:314
  5.5 14.7 %collective-permute-start.3 = (bf16[4,768,512]{2,1,0:T(8,128)(2,1)S(1)}, bf16[4,768,512]{2,1,0:T(8,128)(2,1)S(1)}, u32[]{:S(2)}, u32[]{:S(2)}) collective-permute-start(bf16[4,768,512]{2,1,0:T(8,128)(2,1)S(1)} %load_to_swap.3.after), channel_id=1, source_target_pairs={{0,2},{2,0},{4,6},{6,4},{8,10},{10,8},{12,14},{14,12},{1,3},{3,1},... | collective-permute-start | bytes 9437192 | tf_op jit(solution)/shard_map/ppermute | solution.py:314
  5.7 37.9 %collective-permute-start.7 = (bf16[2,1024,256]{2,1,0:T(8,128)(2,1)S(1)}, bf16[2,1024,256]{2,1,0:T(8,128)(2,1)S(1)}, u32[]{:S(2)}, u32[]{:S(2)}) collective-permute-start(bf16[2,1024,256]{2,1,0:T(8,128)(2,1)S(1)} %copy-done), channel_id=1, source_target_pairs={{0,0},{1,2},{2,12},{3,14},{4,4},{5,6},{6,8},{7,10},{8,9},{9,11},{1... | collective-permute-start | bytes 3145736 | tf_op jit(solution)/shard_map/ppermute | solution.py:337
  13.7 27.9 %collective-permute-start.1 = (bf16[2,768,256]{2,1,0:T(8,128)(2,1)S(1)}, bf16[2,768,256]{2,1,0:T(8,128)(2,1)S(1)}, u32[]{:S(2)}, u32[]{:S(2)}) collective-permute-start(bf16[2,768,256]{2,1,0:T(8,128)(2,1)S(1)} %pair_grads.1.after), channel_id=1, source_target_pairs={{0,1},{1,0},{2,3},{3,2},{4,5},{5,4},{6,7},{7,6},{8,9},{9,8},{10,11... | collective-permute-start | bytes 2359304 | tf_op jit(solution)/shard_map/ppermute | solution.py:317
  17.4 14.0 %collective-permute-start.2 = (bf16[2,256,512]{2,1,0:T(8,128)(2,1)S(1)}, bf16[2,256,512]{2,1,0:T(8,128)(2,1)S(1)}, u32[]{:S(2)}, u32[]{:S(2)}) collective-permute-start(bf16[2,256,512]{2,1,0:T(8,128)(2,1)S(1)} %get-tuple-element.49), channel_id=1, source_target_pairs={{0,4},{2,6},{4,0},{6,2},{8,12},{10,14},{12,8},{14,10},{1,5},{3,7},... | collective-permute-start | bytes 1572872 | tf_op jit(solution)/shard_map/ppermute | solution.py:320
  21.3 22.3 %collective-permute-start.6 = (bf16[2,256,512]{2,1,0:T(8,128)(2,1)S(1)}, bf16[2,256,512]{2,1,0:T(8,128)(2,1)S(1)}, u32[]{:S(2)}, u32[]{:S(2)}) collective-permute-start(bf16[2,256,512]{2,1,0:T(8,128)(2,1)S(1)} %get-tuple-element.60), channel_id=1, source_target_pairs={{0,4},{2,6},{4,0},{6,2},{8,12},{10,14},{12,8},{14,10},{1,5},{3,7},... | collective-permute-start | bytes 1572872 | tf_op jit(solution)/shard_map/ppermute | solution.py:320
  32.2 18.1 %collective-permute-start.5 = (bf16[256,512]{1,0:T(8,128)(2,1)S(1)}, bf16[256,512]{1,0:T(8,128)(2,1)S(1)}, u32[]{:S(2)}, u32[]{:S(2)}) collective-permute-start(bf16[256,512]{1,0:T(8,128)(2,1)S(1)} %get-tuple-element.57), channel_id=1, source_target_pairs={{0,12},{2,14},{4,8},{6,10},{8,4},{10,6},{12,0},{14,2},{1,13},{3,15... | collective-permute-start | bytes 786440 | tf_op jit(solution)/shard_map/ppermute | solution.py:320
  44.4 9.2 %collective-permute-start.8 = (bf16[256,512]{1,0:T(8,128)(2,1)S(1)}, bf16[256,512]{1,0:T(8,128)(2,1)S(1)}, u32[]{:S(2)}, u32[]{:S(2)}) collective-permute-start(bf16[256,512]{1,0:T(8,128)(2,1)S(1)} %get-tuple-element.64), channel_id=1, source_target_pairs={{0,12},{2,14},{4,8},{6,10},{8,4},{10,6},{12,0},{14,2},{1,13},{3,15... | collective-permute-start | bytes 786440 | tf_op jit(solution)/shard_map/ppermute | solution.py:320
  47.3 8.1 %collective-permute-start.10 = (bf16[2,512,256]{2,1,0:T(8,128)(2,1)S(1)}, bf16[2,512,256]{2,1,0:T(8,128)(2,1)S(1)}, u32[]{:S(2)}, u32[]{:S(2)}) collective-permute-start(bf16[2,512,256]{2,1,0:T(8,128)(2,1)S(1)} %get-tuple-element.67), channel_id=1, source_target_pairs={{0,2},{2,0},{4,6},{6,4},{8,10},{10,8},{12,14},{14,12},{1,3},{3,1},... | collective-permute-start | bytes 1572872 | tf_op jit(solution)/shard_map/ppermute | solution.py:314
  48.1 15.0 %collective-permute-start.4 = (bf16[2,256,512]{2,1,0:T(8,128)(2,1)S(1)}, bf16[2,256,512]{2,1,0:T(8,128)(2,1)S(1)}, u32[]{:S(2)}, u32[]{:S(2)}) collective-permute-start(bf16[2,256,512]{2,1,0:T(8,128)(2,1)S(1)} %get-tuple-element.56), channel_id=1, source_target_pairs={{0,4},{2,6},{4,0},{6,2},{8,12},{10,14},{12,8},{14,10},{1,5},{3,7},... | collective-permute-start | bytes 1572872 | tf_op jit(solution)/shard_map/ppermute | solution.py:320
  50.0 21.6 %collective-permute-start.12 = (bf16[2,256,512]{2,1,0:T(8,128)(2,1)S(1)}, bf16[2,256,512]{2,1,0:T(8,128)(2,1)S(1)}, u32[]{:S(2)}, u32[]{:S(2)}) collective-permute-start(bf16[2,256,512]{2,1,0:T(8,128)(2,1)S(1)} %get-tuple-element.71), channel_id=1, source_target_pairs={{0,12},{2,14},{4,8},{6,10},{8,4},{10,6},{12,0},{14,2},{1,13},{3,15... | collective-permute-start | bytes 1572872 | tf_op jit(solution)/shard_map/ppermute | solution.py:320
  54.2 2.4 %collective-permute-start.9 = (bf16[256,512]{1,0:T(8,128)(2,1)S(1)}, bf16[256,512]{1,0:T(8,128)(2,1)S(1)}, u32[]{:S(2)}, u32[]{:S(2)}) collective-permute-start(bf16[256,512]{1,0:T(8,128)(2,1)S(1)} %get-tuple-element.66), channel_id=1, source_target_pairs={{0,2},{2,0},{4,6},{6,4},{8,10},{10,8},{12,14},{14,12},{1,3},{3,1},... | collective-permute-start | bytes 786440 | tf_op jit(solution)/shard_map/ppermute | solution.py:314
  57.3 10.0 %collective-permute-start.13 = (bf16[3,128,256]{2,1,0:T(8,128)(2,1)S(1)}, bf16[3,128,256]{2,1,0:T(8,128)(2,1)S(1)}, u32[]{:S(2)}, u32[]{:S(2)}) collective-permute-start(bf16[3,128,256]{2,1,0:T(8,128)(2,1)S(1)} %get-tuple-element.72), channel_id=1, source_target_pairs={{0,16},{16,32},{32,48},{48,0},{64,80},{80,96},{96,112},{112,64},{1... | collective-permute-start | bytes 589832 | tf_op jit(solution)/shard_map/ppermute | solution.py:347
  59.0 12.2 %collective-permute-start.14 = (bf16[3,128,256]{2,1,0:T(8,128)(2,1)S(1)}, bf16[3,128,256]{2,1,0:T(8,128)(2,1)S(1)}, u32[]{:S(2)}, u32[]{:S(2)}) collective-permute-start(bf16[3,128,256]{2,1,0:T(8,128)(2,1)S(1)} %get-tuple-element.73), channel_id=1, source_target_pairs={{0,32},{16,48},{32,0},{48,16},{64,96},{80,112},{96,64},{112,80},{1... | collective-permute-start | bytes 589832 | tf_op jit(solution)/shard_map/ppermute | solution.py:347
  62.3 8.9 %collective-permute-start.15 = (bf16[3,128,256]{2,1,0:T(8,128)(2,1)S(1)}, bf16[3,128,256]{2,1,0:T(8,128)(2,1)S(1)}, u32[]{:S(2)}, u32[]{:S(2)}) collective-permute-start(bf16[3,128,256]{2,1,0:T(8,128)(2,1)S(1)} %get-tuple-element.74), channel_id=1, source_target_pairs={{0,48},{16,0},{32,16},{48,32},{64,112},{80,64},{96,80},{112,96},{1... | collective-permute-start | bytes 589832 | tf_op jit(solution)/shard_map/ppermute | solution.py:347
  63.8 8.9 %collective-permute-start.11 = (bf16[256,512]{1,0:T(8,128)(2,1)S(1)}, bf16[256,512]{1,0:T(8,128)(2,1)S(1)}, u32[]{:S(2)}, u32[]{:S(2)}) collective-permute-start(bf16[256,512]{1,0:T(8,128)(2,1)S(1)} %get-tuple-element.70), channel_id=1, source_target_pairs={{0,12},{2,14},{4,8},{6,10},{8,4},{10,6},{12,0},{14,2},{1,13},{3,15... | collective-permute-start | bytes 786440 | tf_op jit(solution)/shard_map/ppermute | solution.py:320
  72.3 6.7 %collective-permute-start.16 = (bf16[256,512]{1,0:T(8,128)(2,1)S(1)}, bf16[256,512]{1,0:T(8,128)(2,1)S(1)}, u32[]{:S(2)}, u32[]{:S(2)}) collective-permute-start(bf16[256,512]{1,0:T(8,128)(2,1)S(1)} %get-tuple-element.76), channel_id=1, source_target_pairs={{0,4},{2,6},{4,0},{6,2},{8,12},{10,14},{12,8},{14,10},{1,5},{3,7},... | collective-permute-start | bytes 786440 | tf_op jit(solution)/shard_map/ppermute | solution.py:320
  79.6 3.4 %collective-permute-start.17 = (bf16[256,512]{1,0:T(8,128)(2,1)S(1)}, bf16[256,512]{1,0:T(8,128)(2,1)S(1)}, u32[]{:S(2)}, u32[]{:S(2)}) collective-permute-start(bf16[256,512]{1,0:T(8,128)(2,1)S(1)} %get-tuple-element.78), channel_id=1, source_target_pairs={{0,2},{2,0},{4,6},{6,4},{8,10},{10,8},{12,14},{14,12},{1,3},{3,1},... | collective-permute-start | bytes 786440 | tf_op jit(solution)/shard_map/ppermute | solution.py:314
  83.7 9.4 %collective-permute-start.18 = (bf16[3,128,256]{2,1,0:T(8,128)(2,1)S(1)}, bf16[3,128,256]{2,1,0:T(8,128)(2,1)S(1)}, u32[]{:S(2)}, u32[]{:S(2)}) collective-permute-start(bf16[3,128,256]{2,1,0:T(8,128)(2,1)S(1)} %get-tuple-element.79), channel_id=1, source_target_pairs={{0,16},{16,32},{32,48},{48,0},{64,80},{80,96},{96,112},{112,64},{1... | collective-permute-start | bytes 589832 | tf_op jit(solution)/shard_map/ppermute | solution.py:347
  85.0 11.3 %collective-permute-start.19 = (bf16[3,128,256]{2,1,0:T(8,128)(2,1)S(1)}, bf16[3,128,256]{2,1,0:T(8,128)(2,1)S(1)}, u32[]{:S(2)}, u32[]{:S(2)}) collective-permute-start(bf16[3,128,256]{2,1,0:T(8,128)(2,1)S(1)} %get-tuple-element.80), channel_id=1, source_target_pairs={{0,32},{16,48},{32,0},{48,16},{64,96},{80,112},{96,64},{112,80},{1... | collective-permute-start | bytes 589832 | tf_op jit(solution)/shard_map/ppermute | solution.py:347
  87.5 8.9 %collective-permute-start.20 = (bf16[3,128,256]{2,1,0:T(8,128)(2,1)S(1)}, bf16[3,128,256]{2,1,0:T(8,128)(2,1)S(1)}, u32[]{:S(2)}, u32[]{:S(2)}) collective-permute-start(bf16[3,128,256]{2,1,0:T(8,128)(2,1)S(1)} %get-tuple-element.81), channel_id=1, source_target_pairs={{0,48},{16,0},{32,16},{48,32},{64,112},{80,64},{96,80},{112,96},{1... | collective-permute-start | bytes 589832 | tf_op jit(solution)/shard_map/ppermute | solution.py:347
  87.5 16.7 %collective-permute-start.23 = (bf16[3,128,256]{2,1,0:T(8,128)(2,1)S(1)}, bf16[3,128,256]{2,1,0:T(8,128)(2,1)S(1)}, u32[]{:S(2)}, u32[]{:S(2)}) collective-permute-start(bf16[3,128,256]{2,1,0:T(8,128)(2,1)S(1)} %sum_over_z.2.after), channel_id=1, source_target_pairs={{0,0},{1,15},{2,64},{3,79},{4,4},{5,11},{6,68},{7,75},{8,6},{9,9},... | collective-permute-start | bytes 589832 | tf_op jit(solution)/shard_map/ppermute | solution.py:334
  91.8 12.5 %collective-permute-start.24 = (bf16[3,128,256]{2,1,0:T(8,128)(2,1)S(1)}, bf16[3,128,256]{2,1,0:T(8,128)(2,1)S(1)}, u32[]{:S(2)}, u32[]{:S(2)}) collective-permute-start(bf16[3,128,256]{2,1,0:T(8,128)(2,1)S(1)} %sum_over_z.2.after), channel_id=1, source_target_pairs={{64,0},{65,15},{66,64},{67,79},{68,4},{69,11},{70,68},{71,75},{72,... | collective-permute-start | bytes 589832 | tf_op jit(solution)/shard_map/ppermute | solution.py:334
  96.7 15.7 %collective-permute-start.21 = (bf16[3,128,256]{2,1,0:T(8,128)(2,1)S(1)}, bf16[3,128,256]{2,1,0:T(8,128)(2,1)S(1)}, u32[]{:S(2)}, u32[]{:S(2)}) collective-permute-start(bf16[3,128,256]{2,1,0:T(8,128)(2,1)S(1)} %sum_over_z.3), channel_id=1, source_target_pairs={{0,1},{1,14},{2,65},{3,78},{4,5},{5,10},{6,69},{7,74},{8,7},{9,8},... | collective-permute-start | bytes 589832 | tf_op jit(solution)/shard_map/ppermute | solution.py:334
  103.6 8.9 %collective-permute-start.22 = (bf16[3,128,256]{2,1,0:T(8,128)(2,1)S(1)}, bf16[3,128,256]{2,1,0:T(8,128)(2,1)S(1)}, u32[]{:S(2)}, u32[]{:S(2)}) collective-permute-start(bf16[3,128,256]{2,1,0:T(8,128)(2,1)S(1)} %sum_over_z.3), channel_id=1, source_target_pairs={{64,1},{65,14},{66,65},{67,78},{68,5},{69,10},{70,69},{71,74},{72,... | collective-permute-start | bytes 589832 | tf_op jit(solution)/shard_map/ppermute | solution.py:334

commit v10 on v9

--- a/solution.py
+++ b/solution.py
@@ -376,8 +376,7 @@
         [x_own0, x_got0, g_other, part00[0]],
     )
     swap10 = swap_x(1, sent)
-    moved = bring_weights(kept10)
-    part01 = middle(3, swap01, kept01, moved[0])
+    part01 = middle(3, swap01, kept01, kept10)
     sent, kept11 = call(
         both_second_kernel, "fisher_of_other_grads", [sent_shape, kept_shape], [],
         [x_own1, x_got1, gt_own, gt_got, part01[0]],
@@ -386,11 +385,12 @@
 
     settled0 = settle(part00, kept11)
     own0, other0 = join(settled0, part01, kept11)
-    words0 = weigh(0, own0, other0, moved, own0)
-    part10 = middle(3, swap10, kept10, words0[3])
-    first = call(sum_kernel, "sum_over_z", words, [], [*words0, part10[0]])
-    part11 = middle(1, swap11, kept11, first)
-    own1, other1 = join(settle(part10, part11[0]), part11, first)
+    part10 = middle(3, swap10, kept10, own0)
+    part11 = middle(1, swap11, kept11, part10[0])
+    moved = bring_weights(part11[0])
+    words0 = weigh(0, own0, other0, moved, moved[0])
+    first = call(sum_kernel, "sum_over_z", words, [], [*words0, words0[3]])
+    own1, other1 = join(settle(part10, first), part11, first)
     words1 = weigh(1, own1, other1, moved, own1)
     met = call(meet_kernel, "meet_over_y", sums, [], [*results(0, first), own1])
     second = call(sum_kernel, "sum_over_z", words, [], [*words1, own1])

time: 114 us -> 126 us (1.11)
  waiting for transfers between devices: 44.8 us -> 53.6 us
  starting transfers between devices: 44.2 us -> 47.4 us
    ppermute x1, waiting for transfers between devices: 9.36 us -> 13 us  [swap_cols(): return lax.ppermute(send, 'col', [(0, 1), (1, 0)])]
    ppermute x6, waiting for transfers between devices: 7.16 us -> 10 us  [weigh(): return [lax.ppermute(v, 'member', z_pairs(d)) for d, v in send] + [own_sums]]
    ppermute x8, waiting for transfers between devices: 18 us -> 20.8 us  [swap_x(): return lax.ppermute(sent, 'tok', x_pairs(flip))]
    ppermute x8, starting transfers between devices: 8.43 us -> 10.9 us  [swap_x(): return lax.ppermute(sent, 'tok', x_pairs(flip))]
  transfers between devices with their start and end apart: 25 -> 25, of which waited for: 10 -> 10; matrix products, arithmetic and copies ran while one was open for 0% -> 0% of each run, Pallas kernels for 17% -> 16%
where the time goes in v10:
time: 126 us; the launch traced here: 125 us
  waiting for transfers between devices  53.6 us (43%)
  starting transfers between devices  47.4 us (38%)
  Pallas kernels  23.9 us (19%)
    pallas_call x23, Pallas kernels, call(): pl.pallas_call(kernel, out_shape=shapes, in_specs=[HBM] * len(hbm) + [VME...  23.1 us
    ppermute x8, waiting for transfers between devices, swap_x(): return lax.ppermute(sent, 'tok', x_pairs(flip))  20.8 us
    ppermute x1, waiting for transfers between devices, swap_cols(): return lax.ppermute(send, 'col', [(0, 1), (1, 0)])  13 us
    ppermute x4, starting transfers between devices, results(): lax.ppermute(sums, ('member', 'tok', 'col'), result_pairs(phase, y_lo))  12.2 us
    ppermute x8, starting transfers between devices, swap_x(): return lax.ppermute(sent, 'tok', x_pairs(flip))  10.9 us
    ppermute x6, waiting for transfers between devices, weigh(): return [lax.ppermute(v, 'member', z_pairs(d)) for d, v in send] + [own_sums]  10 us
    ppermute x6, starting transfers between devices, weigh(): return [lax.ppermute(v, 'member', z_pairs(d)) for d, v in send] + [own_sums]  9.85 us
    ppermute x4, waiting for transfers between devices, results(): lax.ppermute(sums, ('member', 'tok', 'col'), result_pairs(phase, y_lo))  8.04 us
  transfers between devices with their start and end apart: 25, of which 10 were waited for; matrix products, arithmetic and copies ran while one was open for 0% of the time, Pallas kernels for 16%

profile of v10, /device:TPU:1, one launch (start us, length us, event | category | flops | bytes accessed | tf_op | source)
XLA Modules:
  0.0 125.2 jit_solution(14062372996372215289)
XLA Ops:
  0.0 2.0 %load_to_swap.2.after = bf16[768,2304]{1,0:T(8,128)(2,1)S(1)} custom-call(bf16[2,768,4096]{2,1,0:T(8,128)(2,1)} %x_ref.7, bf16[2,768,256]{2,1,0:T(8,128)(2,1)} %g_ref.3), custom_call_target="tpu_custom_call" | custom-call | flops 1 | bytes 1 | tf_op jit(solution)/shard_map/load_to_swap/pallas_call | solution.py:67
  2.0 1.5 %collective-permute-start = (bf16[768,2304]{1,0:T(8,128)(2,1)S(1)}, bf16[768,2304]{1,0:T(8,128)(2,1)S(1)}, u32[]{:S(2)}, u32[]{:S(2)}) collective-permute-start(bf16[768,2304]{1,0:T(8,128)(2,1)S(1)} %load_to_swap.2.after), channel_id=1, source_target_pairs={{0,2},{2,0},{4,6},{6,4},{8,10},{10,8},{12,14},{14,12},{1,3},{3,1},... | collective-permute-start | bytes 10616840 | tf_op jit(solution)/shard_map/ppermute | solution.py:314
  3.5 1.9 %load_to_swap.3.after = bf16[4,768,512]{2,1,0:T(8,128)(2,1)S(1)} custom-call(bf16[2,768,4096]{2,1,0:T(8,128)(2,1)} %x_ref.7, bf16[768,2304]{1,0:T(8,128)(2,1)S(1)} %load_to_swap.2.after), custom_call_target="tpu_custom_call" | custom-call | flops 1 | bytes 1 | tf_op jit(solution)/shard_map/load_to_swap/pallas_call | solution.py:67
  5.6 3.2 %fisher_of_own_tokens.2 = (bf16[4,768,512]{2,1,0:T(8,128)(2,1)S(1)}, bf16[768,256]{1,0:T(8,128)(2,1)S(1)}, bf16[256,768]{1,0:T(8,128)(2,1)S(1)}, f32[4,256,512]{2,1,0:T(8,128)S(1)}) custom-call(bf16[2,768,4096]{2,1,0:T(8,128)(2,1)} %x_ref.7, bf16[2,768,256]{2,1,0:T(8,128)(2,1)} %g_ref.3, bf16[4,768,512]{2,1,0:T(8,128)(2,1)S(1)} %load_to_swap.3.after), custom_call_target="tpu_custom_call" | custom-call | flops 1 | bytes 1 | tf_op jit(solution)/shard_map/fisher_of_own_tokens/pallas_call | solution.py:67
  8.8 0.6 collective-permute-done.got.x_ref.xb_ref
  9.4 3.1 %collective-permute-start.1 = (bf16[2,768,256]{2,1,0:T(8,128)(2,1)S(1)}, bf16[2,768,256]{2,1,0:T(8,128)(2,1)S(1)}, u32[]{:S(2)}, u32[]{:S(2)}) collective-permute-start(bf16[2,768,256]{2,1,0:T(8,128)(2,1)S(1)} %pair_grads.1.after), channel_id=1, source_target_pairs={{0,1},{1,0},{2,3},{3,2},{4,5},{5,4},{6,7},{7,6},{8,9},{9,8},{10,11... | collective-permute-start | bytes 2359304 | tf_op jit(solution)/shard_map/ppermute | solution.py:317
  12.5 1.2 fisher_of_both_cores.2
  13.7 1.3 %collective-permute-start.2 = (bf16[2,256,512]{2,1,0:T(8,128)(2,1)S(1)}, bf16[2,256,512]{2,1,0:T(8,128)(2,1)S(1)}, u32[]{:S(2)}, u32[]{:S(2)}) collective-permute-start(bf16[2,256,512]{2,1,0:T(8,128)(2,1)S(1)} %get-tuple-element.49), channel_id=1, source_target_pairs={{0,4},{2,6},{4,0},{6,2},{8,12},{10,14},{12,8},{14,10},{1,5},{3,7},... | collective-permute-start | bytes 1572872 | tf_op jit(solution)/shard_map/ppermute | solution.py:320
  15.0 2.7 %fisher_of_own_tokens.3 = (bf16[4,768,512]{2,1,0:T(8,128)(2,1)S(1)}, f32[4,256,512]{2,1,0:T(8,128)S(1)}) custom-call(bf16[2,768,4096]{2,1,0:T(8,128)(2,1)} %x_ref.7, bf16[256,768]{1,0:T(8,128)(2,1)S(1)} %get-tuple-element.46.after.gt_ref, f32[2,256,512]{2,1,0:T(8,128)S(1)} %get-tuple-element.48.after.kept_ref), custom_call_target="tpu_custom_call" | custom-call | flops 1 | bytes 1 | tf_op jit(solution)/shard_map/fisher_of_own_tokens/pallas_call | solution.py:67
  17.7 1.1 fisher_of_both_cores.3
  19.1 5.5 %collective-permute-start.10 = (bf16[2,1024,256]{2,1,0:T(8,128)(2,1)S(1)}, bf16[2,1024,256]{2,1,0:T(8,128)(2,1)S(1)}, u32[]{:S(2)}, u32[]{:S(2)}) collective-permute-start(bf16[2,1024,256]{2,1,0:T(8,128)(2,1)S(1)} %copy-done), channel_id=1, source_target_pairs={{0,0},{1,2},{2,12},{3,14},{4,4},{5,6},{6,8},{7,10},{8,9},{9,11},{1... | collective-permute-start | bytes 3145736 | tf_op jit(solution)/shard_map/ppermute | solution.py:337
  24.6 1.9 %collective-permute-done.2.got_ref = bf16[2,256,512]{2,1,0:T(8,128)(2,1)S(1)} collective-permute-done((bf16[2,256,512]{2,1,0:T(8,128)(2,1)S(1)}, bf16[2,256,512]{2,1,0:T(8,128)(2,1)S(1)}, u32[]{:S(2)}, u32[]{:S(2)}) %collective-permute-start.2) | collective-permute-done | bytes 524320 | tf_op jit(solution)/shard_map/ppermute | solution.py:320
  26.6 0.7 fisher_over_first_swap.4
  27.3 13.0 %collective-permute-done.1.g_ref = bf16[2,768,256]{2,1,0:T(8,128)(2,1)S(1)} collective-permute-done((bf16[2,768,256]{2,1,0:T(8,128)(2,1)S(1)}, bf16[2,768,256]{2,1,0:T(8,128)(2,1)S(1)}, u32[]{:S(2)}, u32[]{:S(2)}) %collective-permute-start.1) | collective-permute-done | bytes 786464 | tf_op jit(solution)/shard_map/ppermute | solution.py:317
  40.3 1.9 %fisher_of_other_grads.2 = (bf16[2,256,512]{2,1,0:T(8,128)(2,1)S(1)}, f32[2,256,512]{2,1,0:T(8,128)S(1)}, bf16[256,768]{1,0:T(8,128)(2,1)S(1)}, bf16[256,768]{1,0:T(8,128)(2,1)S(1)}) custom-call(bf16[4,768,512]{2,1,0:T(8,128)(2,1)S(1)} %get-tuple-element.44.xa_ref, bf16[768,2304]{1,0:T(8,128)(2,1)S(1)} %collective-permute-done.got.x_ref.xb_ref, ...), custom_call_target="tpu_custom_call" | custom-call | flops 1 | bytes 1 | tf_op jit(solution)/shard_map/fisher_of_other_grads/pallas_call | solution.py:67
  42.2 1.3 %collective-permute-start.4 = (bf16[2,256,512]{2,1,0:T(8,128)(2,1)S(1)}, bf16[2,256,512]{2,1,0:T(8,128)(2,1)S(1)}, u32[]{:S(2)}, u32[]{:S(2)}) collective-permute-start(bf16[2,256,512]{2,1,0:T(8,128)(2,1)S(1)} %get-tuple-element.56), channel_id=1, source_target_pairs={{0,4},{2,6},{4,0},{6,2},{8,12},{10,14},{12,8},{14,10},{1,5},{3,7},... | collective-permute-start | bytes 1572872 | tf_op jit(solution)/shard_map/ppermute | solution.py:320
  43.5 0.7 fisher_over_first_swap.5
  44.3 1.9 %fisher_of_other_grads.3 = (bf16[2,256,512]{2,1,0:T(8,128)(2,1)S(1)}, f32[2,256,512]{2,1,0:T(8,128)S(1)}) custom-call(bf16[4,768,512]{2,1,0:T(8,128)(2,1)S(1)} %get-tuple-element.52.after.xa_ref, bf16[4,768,512]{2,1,0:T(8,128)(2,1)S(1)} %collective-permute-done.3.x_ref.xb_ref, bf16[256,768]{1,0:T(8,128)(2,1)S(1)} %get-tuple-element.58.gta_ref, ...), custom_call_target="tpu_custom_call" | custom-call | flops 1 | bytes 1 | tf_op jit(solution)/shard_map/fisher_of_other_grads/pallas_call | solution.py:67
  46.1 2.7 %collective-permute-start.11 = (bf16[2,256,512]{2,1,0:T(8,128)(2,1)S(1)}, bf16[2,256,512]{2,1,0:T(8,128)(2,1)S(1)}, u32[]{:S(2)}, u32[]{:S(2)}) collective-permute-start(bf16[2,256,512]{2,1,0:T(8,128)(2,1)S(1)} %get-tuple-element.68), channel_id=1, source_target_pairs={{0,12},{2,14},{4,8},{6,10},{8,4},{10,6},{12,0},{14,2},{1,13},{3,15... | collective-permute-start | bytes 1572872 | tf_op jit(solution)/shard_map/ppermute | solution.py:320
  48.9 2.6 %collective-permute-start.7 = (bf16[256,512]{1,0:T(8,128)(2,1)S(1)}, bf16[256,512]{1,0:T(8,128)(2,1)S(1)}, u32[]{:S(2)}, u32[]{:S(2)}) collective-permute-start(bf16[256,512]{1,0:T(8,128)(2,1)S(1)} %get-tuple-element.63), channel_id=1, source_target_pairs={{0,12},{2,14},{4,8},{6,10},{8,4},{10,6},{12,0},{14,2},{1,13},{3,15... | collective-permute-start | bytes 786440 | tf_op jit(solution)/shard_map/ppermute | solution.py:320
  51.5 13.5 %collective-permute-done.5.got = bf16[256,512]{1,0:T(8,128)(2,1)S(1)} collective-permute-done((bf16[256,512]{1,0:T(8,128)(2,1)S(1)}, bf16[256,512]{1,0:T(8,128)(2,1)S(1)}, u32[]{:S(2)}, u32[]{:S(2)}) %collective-permute-start.5) | collective-permute-done | bytes 262176 | tf_op jit(solution)/shard_map/ppermute | solution.py:320
  65.3 5.3 %collective-permute-done.7.got = bf16[256,512]{1,0:T(8,128)(2,1)S(1)} collective-permute-done((bf16[256,512]{1,0:T(8,128)(2,1)S(1)}, bf16[256,512]{1,0:T(8,128)(2,1)S(1)}, u32[]{:S(2)}, u32[]{:S(2)}) %collective-permute-start.7) | collective-permute-done | bytes 262176 | tf_op jit(solution)/shard_map/ppermute | solution.py:320
  70.6 0.6 fisher_over_tokens.5
  71.2 0.7 fisher_over_first_swap.6
  72.0 0.7 fisher_over_first_swap.7
  72.8 2.5 %collective-permute-start.12 = (bf16[2,512,256]{2,1,0:T(8,128)(2,1)S(1)}, bf16[2,512,256]{2,1,0:T(8,128)(2,1)S(1)}, u32[]{:S(2)}, u32[]{:S(2)}) collective-permute-start(bf16[2,512,256]{2,1,0:T(8,128)(2,1)S(1)} %get-tuple-element.71), channel_id=1, source_target_pairs={{0,2},{2,0},{4,6},{6,4},{8,10},{10,8},{12,14},{14,12},{1,3},{3,1},... | collective-permute-start | bytes 1572872 | tf_op jit(solution)/shard_map/ppermute | solution.py:314
  75.4 2.6 %collective-permute-start.8 = (bf16[256,512]{1,0:T(8,128)(2,1)S(1)}, bf16[256,512]{1,0:T(8,128)(2,1)S(1)}, u32[]{:S(2)}, u32[]{:S(2)}) collective-permute-start(bf16[256,512]{1,0:T(8,128)(2,1)S(1)} %get-tuple-element.66), channel_id=1, source_target_pairs={{0,12},{2,14},{4,8},{6,10},{8,4},{10,6},{12,0},{14,2},{1,13},{3,15... | collective-permute-start | bytes 786440 | tf_op jit(solution)/shard_map/ppermute | solution.py:320
  78.0 0.8 weigh_members.2
  78.8 1.7 %collective-permute-start.13 = (bf16[3,128,256]{2,1,0:T(8,128)(2,1)S(1)}, bf16[3,128,256]{2,1,0:T(8,128)(2,1)S(1)}, u32[]{:S(2)}, u32[]{:S(2)}) collective-permute-start(bf16[3,128,256]{2,1,0:T(8,128)(2,1)S(1)} %get-tuple-element.72), channel_id=1, source_target_pairs={{0,16},{16,32},{32,48},{48,0},{64,80},{80,96},{96,112},{112,64},{1... | collective-permute-start | bytes 589832 | tf_op jit(solution)/shard_map/ppermute | solution.py:347
  80.5 3.3 %collective-permute-start.14 = (bf16[3,128,256]{2,1,0:T(8,128)(2,1)S(1)}, bf16[3,128,256]{2,1,0:T(8,128)(2,1)S(1)}, u32[]{:S(2)}, u32[]{:S(2)}) collective-permute-start(bf16[3,128,256]{2,1,0:T(8,128)(2,1)S(1)} %get-tuple-element.73), channel_id=1, source_target_pairs={{0,32},{16,48},{32,0},{48,16},{64,96},{80,112},{96,64},{112,80},{1... | collective-permute-start | bytes 589832 | tf_op jit(solution)/shard_map/ppermute | solution.py:347
  83.8 0.7 collective-permute-start.15
  84.5 2.7 %collective-permute-done.13.one = bf16[3,128,256]{2,1,0:T(8,128)(2,1)S(1)} collective-permute-done((bf16[3,128,256]{2,1,0:T(8,128)(2,1)S(1)}, bf16[3,128,256]{2,1,0:T(8,128)(2,1)S(1)}, u32[]{:S(2)}, u32[]{:S(2)}) %collective-permute-start.13) | collective-permute-done | bytes 196640 | tf_op jit(solution)/shard_map/ppermute | solution.py:347
  87.2 5.1 %collective-permute-done.14.two = bf16[3,128,256]{2,1,0:T(8,128)(2,1)S(1)} collective-permute-done((bf16[3,128,256]{2,1,0:T(8,128)(2,1)S(1)}, bf16[3,128,256]{2,1,0:T(8,128)(2,1)S(1)}, u32[]{:S(2)}, u32[]{:S(2)}) %collective-permute-start.14) | collective-permute-done | bytes 196640 | tf_op jit(solution)/shard_map/ppermute | solution.py:347
  92.9 0.6 fisher_over_tokens.7
  93.6 1.7 %collective-permute-start.17 = (bf16[256,512]{1,0:T(8,128)(2,1)S(1)}, bf16[256,512]{1,0:T(8,128)(2,1)S(1)}, u32[]{:S(2)}, u32[]{:S(2)}) collective-permute-start(bf16[256,512]{1,0:T(8,128)(2,1)S(1)} %get-tuple-element.78), channel_id=1, source_target_pairs={{0,2},{2,0},{4,6},{6,4},{8,10},{10,8},{12,14},{14,12},{1,3},{3,1},... | collective-permute-start | bytes 786440 | tf_op jit(solution)/shard_map/ppermute | solution.py:314
  95.2 1.2 collective-permute-done.17.refs_1_
  96.4 0.7 weigh_members.3
  97.1 1.0 collective-permute-start.18
  98.1 2.1 %collective-permute-start.19 = (bf16[3,128,256]{2,1,0:T(8,128)(2,1)S(1)}, bf16[3,128,256]{2,1,0:T(8,128)(2,1)S(1)}, u32[]{:S(2)}, u32[]{:S(2)}) collective-permute-start(bf16[3,128,256]{2,1,0:T(8,128)(2,1)S(1)} %get-tuple-element.80), channel_id=1, source_target_pairs={{0,32},{16,48},{32,0},{48,16},{64,96},{80,112},{96,64},{112,80},{1... | collective-permute-start | bytes 589832 | tf_op jit(solution)/shard_map/ppermute | solution.py:347
  100.2 1.0 collective-permute-start.20
  101.2 4.3 %collective-permute-start.23 = (bf16[3,128,256]{2,1,0:T(8,128)(2,1)S(1)}, bf16[3,128,256]{2,1,0:T(8,128)(2,1)S(1)}, u32[]{:S(2)}, u32[]{:S(2)}) collective-permute-start(bf16[3,128,256]{2,1,0:T(8,128)(2,1)S(1)} %sum_over_z.2.after), channel_id=1, source_target_pairs={{0,0},{1,15},{2,64},{3,79},{4,4},{5,11},{6,68},{7,75},{8,6},{9,9},... | collective-permute-start | bytes 589832 | tf_op jit(solution)/shard_map/ppermute | solution.py:334
  105.5 1.3 %collective-permute-start.24 = (bf16[3,128,256]{2,1,0:T(8,128)(2,1)S(1)}, bf16[3,128,256]{2,1,0:T(8,128)(2,1)S(1)}, u32[]{:S(2)}, u32[]{:S(2)}) collective-permute-start(bf16[3,128,256]{2,1,0:T(8,128)(2,1)S(1)} %sum_over_z.2.after), channel_id=1, source_target_pairs={{64,0},{65,15},{66,64},{67,79},{68,4},{69,11},{70,68},{71,75},{72,... | collective-permute-start | bytes 589832 | tf_op jit(solution)/shard_map/ppermute | solution.py:334
  106.8 2.3 %collective-permute-done.19.two = bf16[3,128,256]{2,1,0:T(8,128)(2,1)S(1)} collective-permute-done((bf16[3,128,256]{2,1,0:T(8,128)(2,1)S(1)}, bf16[3,128,256]{2,1,0:T(8,128)(2,1)S(1)}, u32[]{:S(2)}, u32[]{:S(2)}) %collective-permute-start.19) | collective-permute-done | bytes 196640 | tf_op jit(solution)/shard_map/ppermute | solution.py:347
  109.1 0.3 sum_over_z.3
  109.5 5.9 %collective-permute-start.21 = (bf16[3,128,256]{2,1,0:T(8,128)(2,1)S(1)}, bf16[3,128,256]{2,1,0:T(8,128)(2,1)S(1)}, u32[]{:S(2)}, u32[]{:S(2)}) collective-permute-start(bf16[3,128,256]{2,1,0:T(8,128)(2,1)S(1)} %sum_over_z.3), channel_id=1, source_target_pairs={{0,1},{1,14},{2,65},{3,78},{4,5},{5,10},{6,69},{7,74},{8,7},{9,8},... | collective-permute-start | bytes 589832 | tf_op jit(solution)/shard_map/ppermute | solution.py:334
  115.4 0.7 collective-permute-start.22
  116.3 8.0 %collective-permute-done.21.near = bf16[3,128,256]{2,1,0:T(8,128)(2,1)S(1)} collective-permute-done((bf16[3,128,256]{2,1,0:T(8,128)(2,1)S(1)}, bf16[3,128,256]{2,1,0:T(8,128)(2,1)S(1)}, u32[]{:S(2)}, u32[]{:S(2)}) %collective-permute-start.21) | collective-permute-done | bytes 196640 | tf_op jit(solution)/shard_map/ppermute | solution.py:334
  124.3 0.8 merge_members.1
  (28 shorter events, 1.9 us)
Async XLA Ops:
  2.0 7.3 %collective-permute-start = (bf16[768,2304]{1,0:T(8,128)(2,1)S(1)}, bf16[768,2304]{1,0:T(8,128)(2,1)S(1)}, u32[]{:S(2)}, u32[]{:S(2)}) collective-permute-start(bf16[768,2304]{1,0:T(8,128)(2,1)S(1)} %load_to_swap.2.after), channel_id=1, source_target_pairs={{0,2},{2,0},{4,6},{6,4},{8,10},{10,8},{12,14},{14,12},{1,3},{3,1},... | collective-permute-start | bytes 10616840 | tf_op jit(solution)/shard_map/ppermute | solution.py:314
  5.4 12.2 %collective-permute-start.3 = (bf16[4,768,512]{2,1,0:T(8,128)(2,1)S(1)}, bf16[4,768,512]{2,1,0:T(8,128)(2,1)S(1)}, u32[]{:S(2)}, u32[]{:S(2)}) collective-permute-start(bf16[4,768,512]{2,1,0:T(8,128)(2,1)S(1)} %load_to_swap.3.after), channel_id=1, source_target_pairs={{0,2},{2,0},{4,6},{6,4},{8,10},{10,8},{12,14},{14,12},{1,3},{3,1},... | collective-permute-start | bytes 9437192 | tf_op jit(solution)/shard_map/ppermute | solution.py:314
  9.4 30.9 %collective-permute-start.1 = (bf16[2,768,256]{2,1,0:T(8,128)(2,1)S(1)}, bf16[2,768,256]{2,1,0:T(8,128)(2,1)S(1)}, u32[]{:S(2)}, u32[]{:S(2)}) collective-permute-start(bf16[2,768,256]{2,1,0:T(8,128)(2,1)S(1)} %pair_grads.1.after), channel_id=1, source_target_pairs={{0,1},{1,0},{2,3},{3,2},{4,5},{5,4},{6,7},{7,6},{8,9},{9,8},{10,11... | collective-permute-start | bytes 2359304 | tf_op jit(solution)/shard_map/ppermute | solution.py:317
  13.7 12.9 %collective-permute-start.2 = (bf16[2,256,512]{2,1,0:T(8,128)(2,1)S(1)}, bf16[2,256,512]{2,1,0:T(8,128)(2,1)S(1)}, u32[]{:S(2)}, u32[]{:S(2)}) collective-permute-start(bf16[2,256,512]{2,1,0:T(8,128)(2,1)S(1)} %get-tuple-element.49), channel_id=1, source_target_pairs={{0,4},{2,6},{4,0},{6,2},{8,12},{10,14},{12,8},{14,10},{1,5},{3,7},... | collective-permute-start | bytes 1572872 | tf_op jit(solution)/shard_map/ppermute | solution.py:320
  17.7 1.5 %copy-start = (bf16[2,1024,256]{2,1,0:T(8,128)(2,1)S(1)}, bf16[2,1024,256]{2,1,0:T(8,128)(2,1)}, u32[]{:S(2)}) copy-start(bf16[2,1024,256]{2,1,0:T(8,128)(2,1)} %param.5) | copy-start | bytes 3145732
  18.8 24.7 %collective-permute-start.6 = (bf16[2,256,512]{2,1,0:T(8,128)(2,1)S(1)}, bf16[2,256,512]{2,1,0:T(8,128)(2,1)S(1)}, u32[]{:S(2)}, u32[]{:S(2)}) collective-permute-start(bf16[2,256,512]{2,1,0:T(8,128)(2,1)S(1)} %get-tuple-element.60), channel_id=1, source_target_pairs={{0,4},{2,6},{4,0},{6,2},{8,12},{10,14},{12,8},{14,10},{1,5},{3,7},... | collective-permute-start | bytes 1572872 | tf_op jit(solution)/shard_map/ppermute | solution.py:320
  19.1 53.6 %collective-permute-start.10 = (bf16[2,1024,256]{2,1,0:T(8,128)(2,1)S(1)}, bf16[2,1024,256]{2,1,0:T(8,128)(2,1)S(1)}, u32[]{:S(2)}, u32[]{:S(2)}) collective-permute-start(bf16[2,1024,256]{2,1,0:T(8,128)(2,1)S(1)} %copy-done), channel_id=1, source_target_pairs={{0,0},{1,2},{2,12},{3,14},{4,4},{5,6},{6,8},{7,10},{8,9},{9,11},{1... | collective-permute-start | bytes 3145736 | tf_op jit(solution)/shard_map/ppermute | solution.py:337
  42.2 29.0 %collective-permute-start.4 = (bf16[2,256,512]{2,1,0:T(8,128)(2,1)S(1)}, bf16[2,256,512]{2,1,0:T(8,128)(2,1)S(1)}, u32[]{:S(2)}, u32[]{:S(2)}) collective-permute-start(bf16[2,256,512]{2,1,0:T(8,128)(2,1)S(1)} %get-tuple-element.56), channel_id=1, source_target_pairs={{0,4},{2,6},{4,0},{6,2},{8,12},{10,14},{12,8},{14,10},{1,5},{3,7},... | collective-permute-start | bytes 1572872 | tf_op jit(solution)/shard_map/ppermute | solution.py:320
  46.1 25.8 %collective-permute-start.11 = (bf16[2,256,512]{2,1,0:T(8,128)(2,1)S(1)}, bf16[2,256,512]{2,1,0:T(8,128)(2,1)S(1)}, u32[]{:S(2)}, u32[]{:S(2)}) collective-permute-start(bf16[2,256,512]{2,1,0:T(8,128)(2,1)S(1)} %get-tuple-element.68), channel_id=1, source_target_pairs={{0,12},{2,14},{4,8},{6,10},{8,4},{10,6},{12,0},{14,2},{1,13},{3,15... | collective-permute-start | bytes 1572872 | tf_op jit(solution)/shard_map/ppermute | solution.py:320
  48.8 16.2 %collective-permute-start.5 = (bf16[256,512]{1,0:T(8,128)(2,1)S(1)}, bf16[256,512]{1,0:T(8,128)(2,1)S(1)}, u32[]{:S(2)}, u32[]{:S(2)}) collective-permute-start(bf16[256,512]{1,0:T(8,128)(2,1)S(1)} %get-tuple-element.57), channel_id=1, source_target_pairs={{0,12},{2,14},{4,8},{6,10},{8,4},{10,6},{12,0},{14,2},{1,13},{3,15... | collective-permute-start | bytes 786440 | tf_op jit(solution)/shard_map/ppermute | solution.py:320
  48.9 21.7 %collective-permute-start.7 = (bf16[256,512]{1,0:T(8,128)(2,1)S(1)}, bf16[256,512]{1,0:T(8,128)(2,1)S(1)}, u32[]{:S(2)}, u32[]{:S(2)}) collective-permute-start(bf16[256,512]{1,0:T(8,128)(2,1)S(1)} %get-tuple-element.63), channel_id=1, source_target_pairs={{0,12},{2,14},{4,8},{6,10},{8,4},{10,6},{12,0},{14,2},{1,13},{3,15... | collective-permute-start | bytes 786440 | tf_op jit(solution)/shard_map/ppermute | solution.py:320
  72.8 5.2 %collective-permute-start.12 = (bf16[2,512,256]{2,1,0:T(8,128)(2,1)S(1)}, bf16[2,512,256]{2,1,0:T(8,128)(2,1)S(1)}, u32[]{:S(2)}, u32[]{:S(2)}) collective-permute-start(bf16[2,512,256]{2,1,0:T(8,128)(2,1)S(1)} %get-tuple-element.71), channel_id=1, source_target_pairs={{0,2},{2,0},{4,6},{6,4},{8,10},{10,8},{12,14},{14,12},{1,3},{3,1},... | collective-permute-start | bytes 1572872 | tf_op jit(solution)/shard_map/ppermute | solution.py:314
  75.3 2.7 %collective-permute-start.9 = (bf16[256,512]{1,0:T(8,128)(2,1)S(1)}, bf16[256,512]{1,0:T(8,128)(2,1)S(1)}, u32[]{:S(2)}, u32[]{:S(2)}) collective-permute-start(bf16[256,512]{1,0:T(8,128)(2,1)S(1)} %get-tuple-element.67), channel_id=1, source_target_pairs={{0,2},{2,0},{4,6},{6,4},{8,10},{10,8},{12,14},{14,12},{1,3},{3,1},... | collective-permute-start | bytes 786440 | tf_op jit(solution)/shard_map/ppermute | solution.py:314
  75.4 17.2 %collective-permute-start.8 = (bf16[256,512]{1,0:T(8,128)(2,1)S(1)}, bf16[256,512]{1,0:T(8,128)(2,1)S(1)}, u32[]{:S(2)}, u32[]{:S(2)}) collective-permute-start(bf16[256,512]{1,0:T(8,128)(2,1)S(1)} %get-tuple-element.66), channel_id=1, source_target_pairs={{0,12},{2,14},{4,8},{6,10},{8,4},{10,6},{12,0},{14,2},{1,13},{3,15... | collective-permute-start | bytes 786440 | tf_op jit(solution)/shard_map/ppermute | solution.py:320
  78.0 14.9 %collective-permute-start.16 = (bf16[256,512]{1,0:T(8,128)(2,1)S(1)}, bf16[256,512]{1,0:T(8,128)(2,1)S(1)}, u32[]{:S(2)}, u32[]{:S(2)}) collective-permute-start(bf16[256,512]{1,0:T(8,128)(2,1)S(1)} %get-tuple-element.76), channel_id=1, source_target_pairs={{0,4},{2,6},{4,0},{6,2},{8,12},{10,14},{12,8},{14,10},{1,5},{3,7},... | collective-permute-start | bytes 786440 | tf_op jit(solution)/shard_map/ppermute | solution.py:320
  78.8 8.4 %collective-permute-start.13 = (bf16[3,128,256]{2,1,0:T(8,128)(2,1)S(1)}, bf16[3,128,256]{2,1,0:T(8,128)(2,1)S(1)}, u32[]{:S(2)}, u32[]{:S(2)}) collective-permute-start(bf16[3,128,256]{2,1,0:T(8,128)(2,1)S(1)} %get-tuple-element.72), channel_id=1, source_target_pairs={{0,16},{16,32},{32,48},{48,0},{64,80},{80,96},{96,112},{112,64},{1... | collective-permute-start | bytes 589832 | tf_op jit(solution)/shard_map/ppermute | solution.py:347
  80.5 11.8 %collective-permute-start.14 = (bf16[3,128,256]{2,1,0:T(8,128)(2,1)S(1)}, bf16[3,128,256]{2,1,0:T(8,128)(2,1)S(1)}, u32[]{:S(2)}, u32[]{:S(2)}) collective-permute-start(bf16[3,128,256]{2,1,0:T(8,128)(2,1)S(1)} %get-tuple-element.73), channel_id=1, source_target_pairs={{0,32},{16,48},{32,0},{48,16},{64,96},{80,112},{96,64},{112,80},{1... | collective-permute-start | bytes 589832 | tf_op jit(solution)/shard_map/ppermute | solution.py:347
  83.8 8.5 %collective-permute-start.15 = (bf16[3,128,256]{2,1,0:T(8,128)(2,1)S(1)}, bf16[3,128,256]{2,1,0:T(8,128)(2,1)S(1)}, u32[]{:S(2)}, u32[]{:S(2)}) collective-permute-start(bf16[3,128,256]{2,1,0:T(8,128)(2,1)S(1)} %get-tuple-element.74), channel_id=1, source_target_pairs={{0,48},{16,0},{32,16},{48,32},{64,112},{80,64},{96,80},{112,96},{1... | collective-permute-start | bytes 589832 | tf_op jit(solution)/shard_map/ppermute | solution.py:347
  93.6 2.8 %collective-permute-start.17 = (bf16[256,512]{1,0:T(8,128)(2,1)S(1)}, bf16[256,512]{1,0:T(8,128)(2,1)S(1)}, u32[]{:S(2)}, u32[]{:S(2)}) collective-permute-start(bf16[256,512]{1,0:T(8,128)(2,1)S(1)} %get-tuple-element.78), channel_id=1, source_target_pairs={{0,2},{2,0},{4,6},{6,4},{8,10},{10,8},{12,14},{14,12},{1,3},{3,1},... | collective-permute-start | bytes 786440 | tf_op jit(solution)/shard_map/ppermute | solution.py:314
  97.1 9.7 %collective-permute-start.18 = (bf16[3,128,256]{2,1,0:T(8,128)(2,1)S(1)}, bf16[3,128,256]{2,1,0:T(8,128)(2,1)S(1)}, u32[]{:S(2)}, u32[]{:S(2)}) collective-permute-start(bf16[3,128,256]{2,1,0:T(8,128)(2,1)S(1)} %get-tuple-element.79), channel_id=1, source_target_pairs={{0,16},{16,32},{32,48},{48,0},{64,80},{80,96},{96,112},{112,64},{1... | collective-permute-start | bytes 589832 | tf_op jit(solution)/shard_map/ppermute | solution.py:347
  98.1 11.0 %collective-permute-start.19 = (bf16[3,128,256]{2,1,0:T(8,128)(2,1)S(1)}, bf16[3,128,256]{2,1,0:T(8,128)(2,1)S(1)}, u32[]{:S(2)}, u32[]{:S(2)}) collective-permute-start(bf16[3,128,256]{2,1,0:T(8,128)(2,1)S(1)} %get-tuple-element.80), channel_id=1, source_target_pairs={{0,32},{16,48},{32,0},{48,16},{64,96},{80,112},{96,64},{112,80},{1... | collective-permute-start | bytes 589832 | tf_op jit(solution)/shard_map/ppermute | solution.py:347
  100.2 8.9 %collective-permute-start.20 = (bf16[3,128,256]{2,1,0:T(8,128)(2,1)S(1)}, bf16[3,128,256]{2,1,0:T(8,128)(2,1)S(1)}, u32[]{:S(2)}, u32[]{:S(2)}) collective-permute-start(bf16[3,128,256]{2,1,0:T(8,128)(2,1)S(1)} %get-tuple-element.81), channel_id=1, source_target_pairs={{0,48},{16,0},{32,16},{48,32},{64,112},{80,64},{96,80},{112,96},{1... | collective-permute-start | bytes 589832 | tf_op jit(solution)/shard_map/ppermute | solution.py:347
  101.2 14.9 %collective-permute-start.23 = (bf16[3,128,256]{2,1,0:T(8,128)(2,1)S(1)}, bf16[3,128,256]{2,1,0:T(8,128)(2,1)S(1)}, u32[]{:S(2)}, u32[]{:S(2)}) collective-permute-start(bf16[3,128,256]{2,1,0:T(8,128)(2,1)S(1)} %sum_over_z.2.after), channel_id=1, source_target_pairs={{0,0},{1,15},{2,64},{3,79},{4,4},{5,11},{6,68},{7,75},{8,6},{9,9},... | collective-permute-start | bytes 589832 | tf_op jit(solution)/shard_map/ppermute | solution.py:334
  105.5 10.6 %collective-permute-start.24 = (bf16[3,128,256]{2,1,0:T(8,128)(2,1)S(1)}, bf16[3,128,256]{2,1,0:T(8,128)(2,1)S(1)}, u32[]{:S(2)}, u32[]{:S(2)}) collective-permute-start(bf16[3,128,256]{2,1,0:T(8,128)(2,1)S(1)} %sum_over_z.2.after), channel_id=1, source_target_pairs={{64,0},{65,15},{66,64},{67,79},{68,4},{69,11},{70,68},{71,75},{72,... | collective-permute-start | bytes 589832 | tf_op jit(solution)/shard_map/ppermute | solution.py:334
  109.5 14.9 %collective-permute-start.21 = (bf16[3,128,256]{2,1,0:T(8,128)(2,1)S(1)}, bf16[3,128,256]{2,1,0:T(8,128)(2,1)S(1)}, u32[]{:S(2)}, u32[]{:S(2)}) collective-permute-start(bf16[3,128,256]{2,1,0:T(8,128)(2,1)S(1)} %sum_over_z.3), channel_id=1, source_target_pairs={{0,1},{1,14},{2,65},{3,78},{4,5},{5,10},{6,69},{7,74},{8,7},{9,8},... | collective-permute-start | bytes 589832 | tf_op jit(solution)/shard_map/ppermute | solution.py:334
  115.4 8.9 %collective-permute-start.22 = (bf16[3,128,256]{2,1,0:T(8,128)(2,1)S(1)}, bf16[3,128,256]{2,1,0:T(8,128)(2,1)S(1)}, u32[]{:S(2)}, u32[]{:S(2)}) collective-permute-start(bf16[3,128,256]{2,1,0:T(8,128)(2,1)S(1)} %sum_over_z.3), channel_id=1, source_target_pairs={{64,1},{65,14},{66,65},{67,78},{68,5},{69,10},{70,69},{71,74},{72,... | collective-permute-start | bytes 589832 | tf_op jit(solution)/shard_map/ppermute | solution.py:334

commit v11 on v9

--- a/solution.py
+++ b/solution.py
@@ -19,8 +19,7 @@
 
 X, CORES, Z = 4, 2, 4
 
-ORDER = (1, 2, 0, 3)
-BACK = (3, 1, 2, 0)
+ORDER = ((2, 1), (3, 0))
 
 
 def code_of(values):
@@ -91,35 +90,26 @@
     return tok // 2, tok % 2, half, member // Z, member % Z
 
 
-def column_block(flip, part):
+def load_inputs(member, pair, x_ref, x_out, sem):
     x, _, half, _, _ = where_am_i()
-    owner = x ^ flip
-    local = jnp.where(owner // 2 == half, 2 * (owner % 2), 2 * ((3 - owner) % 2) + 1)
-    return 2 * local + part
-
-
-def load_inputs(member, part, x_ref, x_out, sem):
-    wide = x_out.shape[2]
+    wide = x_ref.shape[2] // 4
     copies = []
-    for s, flip in enumerate(ORDER):
-        at = pl.multiple_of(column_block(flip, part) * wide, wide)
-        copies.append(pltpu.make_async_copy(x_ref.at[member, :, pl.ds(at, wide)], x_out.at[s], sem.at[s]))
+    for s, flip in enumerate(ORDER[pair]):
+        owner = x ^ flip
+        local = jnp.where(owner // 2 == half, 2 * (owner % 2), 2 * ((3 - owner) % 2) + 1)
+        at = pl.multiple_of(local * wide, wide)
+        source = x_ref.at[member, :, pl.ds(at, wide)]
+        copies.append(pltpu.make_async_copy(source, x_out.at[:, pl.ds(s * wide, wide)], sem.at[s]))
         copies[s].start()
     return copies
 
 
 def load_first_kernel(x_ref, g_ref, out, sem, g_sem):
     core = where_am_i()[1]
-    wide = x_ref.shape[2] // 8
-    copies = [pltpu.make_async_copy(g_ref.at[1 - core], out.at[:, pl.ds(4 * wide, g_ref.shape[2])], g_sem)]
-    for s, flip in enumerate(ORDER):
-        at = pl.multiple_of(column_block(flip, 0) * wide, wide)
-        copies.append(
-            pltpu.make_async_copy(x_ref.at[1 - core, :, pl.ds(at, wide)], out.at[:, pl.ds(s * wide, wide)], sem.at[s])
-        )
-    for copy in copies:
-        copy.start()
-    for copy in copies:
+    outs = g_ref.shape[2]
+    load = pltpu.make_async_copy(g_ref.at[1 - core], out.at[:, pl.ds(out.shape[1] - outs, outs)], g_sem)
+    load.start()
+    for copy in load_inputs(1 - core, 0, x_ref, out, sem) + [load]:
         copy.wait()
 
 
@@ -133,10 +123,14 @@
     out[0], out[1] = own[...], got[:, got.shape[1] - outs :]
 
 
+def columns(s, x_ref, wide):
+    return x_ref[:, s * wide : (s + 1) * wide]
+
+
 def own_tokens(copies, x_out, gt_ref, part_out):
-    for s in range(4):
+    for s in range(2):
         copies[s].wait()
-        part_out[s] = fisher_block(x_out[s], gt_ref)
+        part_out[s] = fisher_block(columns(s, x_out, part_out.shape[2]), gt_ref)
 
 
 def own_first_kernel(x_ref, g_ref, after, x_out, g_out, gt_out, part_out, sem, g_sem):
@@ -154,38 +148,43 @@
     own_tokens(copies, x_out, gt_ref, part_out)
 
 
+def add_first_kernel(x_ref, part_ref, after, two_out, one_out, gt_out):
+    wide, outs = part_ref.shape[2], part_ref.shape[1]
+    gt_out[...] = squared_transposed(x_ref[:, 2 * wide :])
+    for s, out in enumerate((two_out, one_out)):
+        out[...] = encode(part_ref[s] + fisher_block(columns(s, x_ref, wide), gt_out))
+
+
+def add_second_kernel(x_ref, gt_ref, part_ref, after, three_out, own_out):
+    wide = part_ref.shape[2]
+    three_out[...] = encode(part_ref[0] + fisher_block(columns(0, x_ref, wide), gt_ref))
+    own_out[...] = part_ref[1] + fisher_block(columns(1, x_ref, wide), gt_ref)
+
+
+def half_block(flip, part, x_refs, gt_refs, wide):
+    pair = 0 if flip in ORDER[0] else 1
+    at = (2 * ORDER[pair].index(flip) + part) * wide
+    own, got = x_refs[2 * pair : 2 * pair + 2]
+    return fisher_block(own[:, at : at + wide], gt_refs[0]) + fisher_block(got[:, at : at + wide], gt_refs[1])
+
+
+def both_first_kernel(own_a, got_a, own_b, got_b, g_ref, after, sent_out, kept_out, gta_out, gtb_out):
+    gta_out[...] = squared_transposed(g_ref[0])
+    gtb_out[...] = squared_transposed(g_ref[1])
+    for s, flip in enumerate((1, 2, 0, 3)):
+        put(s, half_block(flip, 0, (own_a, got_a, own_b, got_b), (gta_out, gtb_out), sent_out.shape[2]), sent_out, kept_out)
+
+
+def both_second_kernel(own_a, got_a, own_b, got_b, gta_ref, gtb_ref, after, sent_out, kept_out):
+    for s, flip in enumerate((3, 2, 0, 1)):
+        put(s, half_block(flip, 1, (own_a, got_a, own_b, got_b), (gta_ref, gtb_ref), sent_out.shape[2]), sent_out, kept_out)
+
+
 def put(s, block, sent_out, kept_out):
     if s < 2:
         sent_out[s] = encode(block)
     else:
         kept_out[s - 2] = block
-
-
-def add_first_kernel(x_ref, part_ref, after, sent_out, kept_out, gt_out):
-    wide = part_ref.shape[2]
-    gt_out[...] = squared_transposed(x_ref[:, 4 * wide :])
-    for s in range(4):
-        block = fisher_block(x_ref[:, s * wide : (s + 1) * wide], gt_out)
-        put(s, part_ref[s] + block, sent_out, kept_out)
-
-
-def add_second_kernel(x_ref, gt_ref, part_ref, after, sent_out, kept_out):
-    for s in range(4):
-        put(s, part_ref[s] + fisher_block(x_ref[s], gt_ref), sent_out, kept_out)
-
-
-def both_first_kernel(xa_ref, xb_ref, g_ref, after, sent_out, kept_out, gta_out, gtb_out):
-    wide = kept_out.shape[2]
-    gta_out[...] = squared_transposed(g_ref[0])
-    gtb_out[...] = squared_transposed(g_ref[1])
-    for s in range(4):
-        block = fisher_block(xb_ref[:, s * wide : (s + 1) * wide], gtb_out)
-        put(s, fisher_block(xa_ref[s], gta_out) + block, sent_out, kept_out)
-
-
-def both_second_kernel(xa_ref, xb_ref, gta_ref, gtb_ref, after, sent_out, kept_out):
-    for s, block in enumerate(BACK):
-        put(s, fisher_block(xa_ref[block], gta_ref) + fisher_block(xb_ref[block], gtb_ref), sent_out, kept_out)
 
 
 def middle_kernel(kept_ref, got_ref, after, sent_out, own_out):
@@ -203,6 +202,17 @@
     core = where_am_i()[1]
     kept_out[...] = jnp.where(core == 0, first, second)
     sent_out[...] = encode_fine(jnp.where(core == 0, second, first))
+
+
+def join_direct_kernel(own, one, two, three, after, kept_out, sent_out):
+    wide = kept_out.shape[1]
+    halves = []
+    for s in range(2):
+        got = [decode(columns(s, ref, wide)) for ref in (one, two, three)]
+        halves.append(columns(s, own, wide) + got[0] + got[1] + got[2])
+    core = where_am_i()[1]
+    kept_out[...] = jnp.where(core == 0, halves[0], halves[1])
+    sent_out[...] = encode_fine(jnp.where(core == 0, halves[1], halves[0]))
 
 
 def split_kernel(w_ref, after, own_out, send_out):
@@ -304,9 +314,10 @@
 def shards(inputs, grads, weights):
     tokens, outs = grads.shape[1:]
     wide = inputs.shape[2] // 8
-    x_shape, g_shape, gt_shape = ((4, tokens, wide), BF16), ((tokens, outs), BF16), ((outs, tokens), BF16)
-    part_shape, sent_shape, kept_shape = ((4, outs, wide), F32), ((2, outs, wide), BF16), ((2, outs, wide), F32)
+    x_shape, g_shape, gt_shape = ((tokens, 4 * wide), BF16), ((tokens, outs), BF16), ((outs, tokens), BF16)
+    part_shape, sent_shape, sum_shape = ((2, outs, 2 * wide), F32), ((outs, 2 * wide), BF16), ((outs, 2 * wide), F32)
     code_shape, own_shape = ((outs, wide), BF16), ((outs, wide), F32)
+    pair_shape, kept_shape = ((2, outs, wide), BF16), ((2, outs, wide), F32)
     words, sums = ((3, wide // Z, outs), BF16), ((2, wide // Z, outs), F32)
     dma = pltpu.SemaphoreType.DMA
 
@@ -325,6 +336,12 @@
 
     def settle(one, after):
         return call(settle_kernel, "fisher_over_tokens", own_shape, [], [*one, after])
+
+    def join_direct(own, got, after):
+        kept_block, sent = call(
+            join_direct_kernel, "fisher_over_tokens", [own_shape, code_shape], [], [own, got[1], got[2], got[3], after]
+        )
+        return kept_block, swap_cores(sent)
 
     def join(first, two, after):
         kept_block, sent = call(join_kernel, "fisher_over_tokens", [own_shape, code_shape], [], [first, *two, after])
@@ -347,45 +364,41 @@
         return [lax.ppermute(v, "member", z_pairs(d)) for d, v in send] + [own_sums]
 
     x_send0 = call(
-        load_first_kernel, "load_to_swap", ((tokens, 4 * wide + outs), BF16), [inputs, grads], [], [dma((4,)), dma]
+        load_first_kernel, "load_to_swap", ((tokens, 4 * wide + outs), BF16), [inputs, grads], [], [dma((2,)), dma]
     )
     x_got0 = swap_cores(x_send0)
-    x_send1 = call(load_second_kernel, "load_to_swap", x_shape, [inputs], [x_send0], [dma((4,))])
+    x_send1 = call(load_second_kernel, "load_to_swap", x_shape, [inputs], [x_send0], [dma((2,))])
     x_got1 = swap_cores(x_send1)
     x_own0, g_own, gt_own, part0 = call(
         own_first_kernel, "fisher_of_own_tokens", [x_shape, g_shape, gt_shape, part_shape], [inputs, grads], [x_send1],
-        [dma((4,)), dma],
+        [dma((2,)), dma],
     )
     g_pair = call(pair_kernel, "pair_grads", ((2, tokens, outs), BF16), [], [g_own, x_got0, gt_own])
     g_other = swap_cols(g_pair)
-    sent, kept00, gt_got = call(
-        add_first_kernel, "fisher_of_both_cores", [sent_shape, kept_shape, gt_shape], [], [x_got0, part0, g_pair]
-    )
-    swap00 = swap_x(1, sent)
+    two, one, gt_got = call(
+        add_first_kernel, "fisher_of_both_cores", [sent_shape, sent_shape, gt_shape], [], [x_got0, part0, g_pair]
+    )
+    got0 = {2: swap_x(2, two), 1: swap_x(1, one)}
     x_own1, part1 = call(
-        own_second_kernel, "fisher_of_own_tokens", [x_shape, part_shape], [inputs], [gt_own, kept00], [dma((4,))]
-    )
-    sent, kept01 = call(
-        add_second_kernel, "fisher_of_both_cores", [sent_shape, kept_shape], [], [x_got1, gt_got, part1, x_own1]
-    )
-    swap01 = swap_x(1, sent)
-    part00 = middle(3, swap00, kept00, kept01)
-
+        own_second_kernel, "fisher_of_own_tokens", [x_shape, part_shape], [inputs], [gt_own, two], [dma((2,))]
+    )
+    three, sum0 = call(
+        add_second_kernel, "fisher_of_both_cores", [sent_shape, sum_shape], [], [x_got1, gt_got, part1, x_own1]
+    )
+    got0[3] = swap_x(3, three)
+
+    xs = [x_own0, x_got0, x_own1, x_got1]
     sent, kept10, gt_own, gt_got = call(
-        both_first_kernel, "fisher_of_other_grads", [sent_shape, kept_shape, gt_shape, gt_shape], [],
-        [x_own0, x_got0, g_other, part00[0]],
+        both_first_kernel, "fisher_of_other_grads", [pair_shape, kept_shape, gt_shape, gt_shape], [], [*xs, g_other, three]
     )
     swap10 = swap_x(1, sent)
     moved = bring_weights(kept10)
-    part01 = middle(3, swap01, kept01, moved[0])
     sent, kept11 = call(
-        both_second_kernel, "fisher_of_other_grads", [sent_shape, kept_shape], [],
-        [x_own1, x_got1, gt_own, gt_got, part01[0]],
+        both_second_kernel, "fisher_of_other_grads", [pair_shape, kept_shape], [], [*xs, gt_own, gt_got, moved[0]]
     )
     swap11 = swap_x(3, sent)
 
-    settled0 = settle(part00, kept11)
-    own0, other0 = join(settled0, part01, kept11)
+    own0, other0 = join_direct(sum0, got0, kept11)
     words0 = weigh(0, own0, other0, moved, own0)
     part10 = middle(3, swap10, kept10, words0[3])
     first = call(sum_kernel, "sum_over_z", words, [], [*words0, part10[0]])

time: 114 us -> 109 us (0.956)
  waiting for transfers between devices: 44.8 us -> 39.1 us
  starting transfers between devices: 44.2 us -> 46.2 us
    ppermute x8 -> x7, waiting for transfers between devices: 18 us -> 5.22 us  [swap_x(): return lax.ppermute(sent, 'tok', x_pairs(flip))]
    ppermute x1, waiting for transfers between devices: 9.36 us -> 16.8 us  [swap_cols(): return lax.ppermute(send, 'col', [(0, 1), (1, 0)])]
    ppermute x8 -> x7, starting transfers between devices: 8.43 us -> 10 us  [swap_x(): return lax.ppermute(sent, 'tok', x_pairs(flip))]
    ppermute x4, starting transfers between devices: 13.1 us -> 14.6 us  [results(): lax.ppermute(sums, ('member', 'tok', 'col'), result_pairs(phase, y_lo))]
    ppermute x4, waiting for transfers between devices: 8.04 us -> 6.85 us  [results(): lax.ppermute(sums, ('member', 'tok', 'col'), result_pairs(phase, y_lo))]
    ppermute x5, starting transfers between devices: 5.96 us -> 4.81 us  [swap_cores(): return lax.ppermute(send, 'tok', [(t, t ^ 1) for t in range(8)])]
    pallas_call x23 -> x20, Pallas kernels: 23.1 us -> 22.1 us  [call(): pl.pallas_call(kernel, out_shape=shapes, in_specs=[HBM] * len(hbm) + [VME...]
  transfers between devices with their start and end apart: 25 -> 24, of which waited for: 10 -> 8; matrix products, arithmetic and copies ran while one was open for 0% -> 0% of each run, Pallas kernels for 17% -> 17%
where the time goes in v11:
time: 109 us; the launch traced here: 108 us
  starting transfers between devices  46.2 us (42%)
  waiting for transfers between devices  39.1 us (36%)
  Pallas kernels  22.9 us (21%)
    pallas_call x20, Pallas kernels, call(): pl.pallas_call(kernel, out_shape=shapes, in_specs=[HBM] * len(hbm) + [VME...  22.1 us
    ppermute x1, waiting for transfers between devices, swap_cols(): return lax.ppermute(send, 'col', [(0, 1), (1, 0)])  16.8 us
    ppermute x4, starting transfers between devices, results(): lax.ppermute(sums, ('member', 'tok', 'col'), result_pairs(phase, y_lo))  14.6 us
    ppermute x7, starting transfers between devices, swap_x(): return lax.ppermute(sent, 'tok', x_pairs(flip))  10 us
    ppermute x6, starting transfers between devices, weigh(): return [lax.ppermute(v, 'member', z_pairs(d)) for d, v in send] + [own_sums]  9.58 us
    ppermute x6, waiting for transfers between devices, weigh(): return [lax.ppermute(v, 'member', z_pairs(d)) for d, v in send] + [own_sums]  7.96 us
    ppermute x4, waiting for transfers between devices, results(): lax.ppermute(sums, ('member', 'tok', 'col'), result_pairs(phase, y_lo))  6.85 us
    ppermute x7, waiting for transfers between devices, swap_x(): return lax.ppermute(sent, 'tok', x_pairs(flip))  5.22 us
  transfers between devices with their start and end apart: 24, of which 8 were waited for; matrix products, arithmetic and copies ran while one was open for 0% of the time, Pallas kernels for 17%

profile of v11, /device:TPU:1, one launch (start us, length us, event | category | flops | bytes accessed | tf_op | source)
XLA Modules:
  0.0 108.5 jit_solution(8209657213650277595)
XLA Ops:
  0.0 2.0 %load_to_swap.2.after = bf16[768,2304]{1,0:T(8,128)(2,1)S(1)} custom-call(bf16[2,768,4096]{2,1,0:T(8,128)(2,1)} %x_ref.7, bf16[2,768,256]{2,1,0:T(8,128)(2,1)} %g_ref.3), custom_call_target="tpu_custom_call" | custom-call | flops 1 | bytes 1 | tf_op jit(solution)/shard_map/load_to_swap/pallas_call | solution.py:66
  2.1 1.5 %collective-permute-start = (bf16[768,2304]{1,0:T(8,128)(2,1)S(1)}, bf16[768,2304]{1,0:T(8,128)(2,1)S(1)}, u32[]{:S(2)}, u32[]{:S(2)}) collective-permute-start(bf16[768,2304]{1,0:T(8,128)(2,1)S(1)} %load_to_swap.2.after), channel_id=1, source_target_pairs={{0,2},{2,0},{4,6},{6,4},{8,10},{10,8},{12,14},{14,12},{1,3},{3,1},... | collective-permute-start | bytes 10616840 | tf_op jit(solution)/shard_map/ppermute | solution.py:325
  3.6 1.9 %load_to_swap.3.after = bf16[768,2048]{1,0:T(8,128)(2,1)S(1)} custom-call(bf16[2,768,4096]{2,1,0:T(8,128)(2,1)} %x_ref.7, bf16[768,2304]{1,0:T(8,128)(2,1)S(1)} %load_to_swap.2.after), custom_call_target="tpu_custom_call" | custom-call | flops 1 | bytes 1 | tf_op jit(solution)/shard_map/load_to_swap/pallas_call | solution.py:66
  5.5 0.2 collective-permute-start.1
  5.7 4.8 %collective-permute-start.7 = (bf16[2,1024,256]{2,1,0:T(8,128)(2,1)S(1)}, bf16[2,1024,256]{2,1,0:T(8,128)(2,1)S(1)}, u32[]{:S(2)}, u32[]{:S(2)}) collective-permute-start(bf16[2,1024,256]{2,1,0:T(8,128)(2,1)S(1)} %copy-done), channel_id=1, source_target_pairs={{0,0},{1,2},{2,12},{3,14},{4,4},{5,6},{6,8},{7,10},{8,9},{9,11},{1... | collective-permute-start | bytes 3145736 | tf_op jit(solution)/shard_map/ppermute | solution.py:354
  10.4 2.9 %fisher_of_own_tokens.2 = (bf16[768,2048]{1,0:T(8,128)(2,1)S(1)}, bf16[768,256]{1,0:T(8,128)(2,1)S(1)}, bf16[256,768]{1,0:T(8,128)(2,1)S(1)}, f32[2,256,1024]{2,1,0:T(8,128)S(1)}) custom-call(bf16[2,768,4096]{2,1,0:T(8,128)(2,1)} %x_ref.7, bf16[2,768,256]{2,1,0:T(8,128)(2,1)} %g_ref.3, bf16[768,2048]{1,0:T(8,128)(2,1)S(1)} %load_to_swap.3.after), custom_call_target="tpu_custom_call" | custom-call | flops 1 | bytes 1 | tf_op jit(solution)/shard_map/fisher_of_own_tokens/pallas_call | solution.py:66
  13.4 2.5 %collective-permute-start.2 = (bf16[2,768,256]{2,1,0:T(8,128)(2,1)S(1)}, bf16[2,768,256]{2,1,0:T(8,128)(2,1)S(1)}, u32[]{:S(2)}, u32[]{:S(2)}) collective-permute-start(bf16[2,768,256]{2,1,0:T(8,128)(2,1)S(1)} %pair_grads.1.after), channel_id=1, source_target_pairs={{0,1},{1,0},{2,3},{3,2},{4,5},{5,4},{6,7},{7,6},{8,9},{9,8},{10,11... | collective-permute-start | bytes 2359304 | tf_op jit(solution)/shard_map/ppermute | solution.py:328
  15.9 1.3 %fisher_of_both_cores.2 = (bf16[256,1024]{1,0:T(8,128)(2,1)S(1)}, bf16[256,1024]{1,0:T(8,128)(2,1)S(1)}, bf16[256,768]{1,0:T(8,128)(2,1)S(1)}) custom-call(bf16[768,2304]{1,0:T(8,128)(2,1)S(1)} %collective-permute-done.got.x_ref.got_a, f32[2,256,1024]{2,1,0:T(8,128)S(1)} %get-tuple-element.42.part_ref, bf16[2,768,256]{2,1,0:T(8,128)(2,1)S(1)} %pair_grads.1.after), custom_call_target="tpu_custom_call" | custom-call | flops 1 | bytes 1 | tf_op jit(solution)/shard_map/fisher_of_both_cores/pallas_call | solution.py:66
  17.2 1.6 %collective-permute-start.5 = (bf16[256,1024]{1,0:T(8,128)(2,1)S(1)}, bf16[256,1024]{1,0:T(8,128)(2,1)S(1)}, u32[]{:S(2)}, u32[]{:S(2)}) collective-permute-start(bf16[256,1024]{1,0:T(8,128)(2,1)S(1)} %get-tuple-element.44.after), channel_id=1, source_target_pairs={{0,8},{2,10},{4,12},{6,14},{8,0},{10,2},{12,4},{14,6},{1,9},{3,11}... | collective-permute-start | bytes 1572872 | tf_op jit(solution)/shard_map/ppermute | solution.py:331
  18.8 2.6 %fisher_of_own_tokens.3 = (bf16[768,2048]{1,0:T(8,128)(2,1)S(1)}, f32[2,256,1024]{2,1,0:T(8,128)S(1)}) custom-call(bf16[2,768,4096]{2,1,0:T(8,128)(2,1)} %x_ref.7, bf16[256,768]{1,0:T(8,128)(2,1)S(1)} %get-tuple-element.41.after.gt_ref, bf16[256,1024]{1,0:T(8,128)(2,1)S(1)} %get-tuple-element.44.after), custom_call_target="tpu_custom_call" | custom-call | flops 1 | bytes 1 | tf_op jit(solution)/shard_map/fisher_of_own_tokens/pallas_call | solution.py:66
  21.4 1.1 %fisher_of_both_cores.3 = (bf16[256,1024]{1,0:T(8,128)(2,1)S(1)}, f32[256,1024]{1,0:T(8,128)S(1)}) custom-call(bf16[768,2048]{1,0:T(8,128)(2,1)S(1)} %collective-permute-done.1.x_ref.got_b, bf16[256,768]{1,0:T(8,128)(2,1)S(1)} %get-tuple-element.46.gt_ref, f32[2,256,1024]{2,1,0:T(8,128)S(1)} %get-tuple-element.47.part_ref, ...), custom_call_target="tpu_custom_call" | custom-call | flops 1 | bytes 1 | tf_op jit(solution)/shard_map/fisher_of_both_cores/pallas_call | solution.py:66
  22.6 2.3 %collective-permute-start.6 = (bf16[256,1024]{1,0:T(8,128)(2,1)S(1)}, bf16[256,1024]{1,0:T(8,128)(2,1)S(1)}, u32[]{:S(2)}, u32[]{:S(2)}) collective-permute-start(bf16[256,1024]{1,0:T(8,128)(2,1)S(1)} %get-tuple-element.48.after), channel_id=1, source_target_pairs={{0,12},{2,14},{4,8},{6,10},{8,4},{10,6},{12,0},{14,2},{1,13},{3,15... | collective-permute-start | bytes 1572872 | tf_op jit(solution)/shard_map/ppermute | solution.py:331
  24.9 16.8 %collective-permute-done.2.g_ref = bf16[2,768,256]{2,1,0:T(8,128)(2,1)S(1)} collective-permute-done((bf16[2,768,256]{2,1,0:T(8,128)(2,1)S(1)}, bf16[2,768,256]{2,1,0:T(8,128)(2,1)S(1)}, u32[]{:S(2)}, u32[]{:S(2)}) %collective-permute-start.2) | collective-permute-done | bytes 786464 | tf_op jit(solution)/shard_map/ppermute | solution.py:328
  41.6 1.9 %fisher_of_other_grads.2 = (bf16[2,256,512]{2,1,0:T(8,128)(2,1)S(1)}, f32[2,256,512]{2,1,0:T(8,128)S(1)}, bf16[256,768]{1,0:T(8,128)(2,1)S(1)}, bf16[256,768]{1,0:T(8,128)(2,1)S(1)}) custom-call(bf16[768,2048]{1,0:T(8,128)(2,1)S(1)} %get-tuple-element.40.own_a, bf16[768,2304]{1,0:T(8,128)(2,1)S(1)} %collective-permute-done.got.x_ref.got_a, ...), custom_call_target="tpu_custom_call" | custom-call | flops 1 | bytes 1 | tf_op jit(solution)/shard_map/fisher_of_other_grads/pallas_call | solution.py:66
  43.7 0.3 collective-permute-start.9
  43.9 0.3 collective-permute-start.3
  44.3 1.9 %fisher_of_other_grads.3 = (bf16[2,256,512]{2,1,0:T(8,128)(2,1)S(1)}, f32[2,256,512]{2,1,0:T(8,128)S(1)}) custom-call(bf16[768,2048]{1,0:T(8,128)(2,1)S(1)} %get-tuple-element.40.own_a, bf16[768,2304]{1,0:T(8,128)(2,1)S(1)} %collective-permute-done.got.x_ref.got_a, bf16[768,2048]{1,0:T(8,128)(2,1)S(1)} %get-tuple-element.45.after.own_b, ...), custom_call_target="tpu_custom_call" | custom-call | flops 1 | bytes 1 | tf_op jit(solution)/shard_map/fisher_of_other_grads/pallas_call | solution.py:66
  46.1 2.9 %collective-permute-start.11 = (bf16[2,256,512]{2,1,0:T(8,128)(2,1)S(1)}, bf16[2,256,512]{2,1,0:T(8,128)(2,1)S(1)}, u32[]{:S(2)}, u32[]{:S(2)}) collective-permute-start(bf16[2,256,512]{2,1,0:T(8,128)(2,1)S(1)} %get-tuple-element.63), channel_id=1, source_target_pairs={{0,12},{2,14},{4,8},{6,10},{8,4},{10,6},{12,0},{14,2},{1,13},{3,15... | collective-permute-start | bytes 1572872 | tf_op jit(solution)/shard_map/ppermute | solution.py:331
  49.0 1.6 %fisher_over_tokens.3 = (f32[256,512]{1,0:T(8,128)S(1)}, bf16[256,512]{1,0:T(8,128)(2,1)S(1)}) custom-call(f32[256,1024]{1,0:T(8,128)S(1)} %get-tuple-element.51.own, bf16[256,1024]{1,0:T(8,128)(2,1)S(1)} %collective-permute-done.4.one, bf16[256,1024]{1,0:T(8,128)(2,1)S(1)} %collective-permute-done.5.two, ...), custom_call_target="tpu_custom_call" | custom-call | flops 1 | bytes 1 | tf_op jit(solution)/shard_map/fisher_over_tokens/pallas_call | solution.py:66
  50.7 0.6 collective-permute-start.8
  51.3 1.2 %collective-permute-done.8.refs_1_ = bf16[256,512]{1,0:T(8,128)(2,1)S(1)} collective-permute-done((bf16[256,512]{1,0:T(8,128)(2,1)S(1)}, bf16[256,512]{1,0:T(8,128)(2,1)S(1)}, u32[]{:S(2)}, u32[]{:S(2)}) %collective-permute-start.8) | collective-permute-done | bytes 262176 | tf_op jit(solution)/shard_map/ppermute | solution.py:325
  52.5 0.7 weigh_members.2
  53.2 1.7 %collective-permute-start.12 = (bf16[3,128,256]{2,1,0:T(8,128)(2,1)S(1)}, bf16[3,128,256]{2,1,0:T(8,128)(2,1)S(1)}, u32[]{:S(2)}, u32[]{:S(2)}) collective-permute-start(bf16[3,128,256]{2,1,0:T(8,128)(2,1)S(1)} %get-tuple-element.64), channel_id=1, source_target_pairs={{0,16},{16,32},{32,48},{48,0},{64,80},{80,96},{96,112},{112,64},{1... | collective-permute-start | bytes 589832 | tf_op jit(solution)/shard_map/ppermute | solution.py:364
  54.9 3.3 %collective-permute-start.13 = (bf16[3,128,256]{2,1,0:T(8,128)(2,1)S(1)}, bf16[3,128,256]{2,1,0:T(8,128)(2,1)S(1)}, u32[]{:S(2)}, u32[]{:S(2)}) collective-permute-start(bf16[3,128,256]{2,1,0:T(8,128)(2,1)S(1)} %get-tuple-element.65), channel_id=1, source_target_pairs={{0,32},{16,48},{32,0},{48,16},{64,96},{80,112},{96,64},{112,80},{1... | collective-permute-start | bytes 589832 | tf_op jit(solution)/shard_map/ppermute | solution.py:364
  58.2 0.7 collective-permute-start.14
  59.0 0.7 fisher_over_first_swap.2
  59.7 1.6 %collective-permute-start.10 = (bf16[256,512]{1,0:T(8,128)(2,1)S(1)}, bf16[256,512]{1,0:T(8,128)(2,1)S(1)}, u32[]{:S(2)}, u32[]{:S(2)}) collective-permute-start(bf16[256,512]{1,0:T(8,128)(2,1)S(1)} %get-tuple-element.62), channel_id=1, source_target_pairs={{0,12},{2,14},{4,8},{6,10},{8,4},{10,6},{12,0},{14,2},{1,13},{3,15... | collective-permute-start | bytes 786440 | tf_op jit(solution)/shard_map/ppermute | solution.py:331
  61.3 0.7 collective-permute-done.12.one
  62.0 5.1 %collective-permute-done.13.two = bf16[3,128,256]{2,1,0:T(8,128)(2,1)S(1)} collective-permute-done((bf16[3,128,256]{2,1,0:T(8,128)(2,1)S(1)}, bf16[3,128,256]{2,1,0:T(8,128)(2,1)S(1)}, u32[]{:S(2)}, u32[]{:S(2)}) %collective-permute-start.13) | collective-permute-done | bytes 196640 | tf_op jit(solution)/shard_map/ppermute | solution.py:364
  67.1 0.3 sum_over_z.2.after
  67.5 0.7 fisher_over_first_swap.3
  68.2 1.2 %collective-permute-start.15 = (bf16[256,512]{1,0:T(8,128)(2,1)S(1)}, bf16[256,512]{1,0:T(8,128)(2,1)S(1)}, u32[]{:S(2)}, u32[]{:S(2)}) collective-permute-start(bf16[256,512]{1,0:T(8,128)(2,1)S(1)} %get-tuple-element.68), channel_id=1, source_target_pairs={{0,4},{2,6},{4,0},{6,2},{8,12},{10,14},{12,8},{14,10},{1,5},{3,7},... | collective-permute-start | bytes 786440 | tf_op jit(solution)/shard_map/ppermute | solution.py:331
  69.4 0.3 fisher_over_tokens.4.first_ref
  69.7 5.2 %collective-permute-done.15.got = bf16[256,512]{1,0:T(8,128)(2,1)S(1)} collective-permute-done((bf16[256,512]{1,0:T(8,128)(2,1)S(1)}, bf16[256,512]{1,0:T(8,128)(2,1)S(1)}, u32[]{:S(2)}, u32[]{:S(2)}) %collective-permute-start.15) | collective-permute-done | bytes 262176 | tf_op jit(solution)/shard_map/ppermute | solution.py:331
  74.9 0.6 fisher_over_tokens.5
  75.5 2.2 %collective-permute-start.16 = (bf16[256,512]{1,0:T(8,128)(2,1)S(1)}, bf16[256,512]{1,0:T(8,128)(2,1)S(1)}, u32[]{:S(2)}, u32[]{:S(2)}) collective-permute-start(bf16[256,512]{1,0:T(8,128)(2,1)S(1)} %get-tuple-element.70), channel_id=1, source_target_pairs={{0,2},{2,0},{4,6},{6,4},{8,10},{10,8},{12,14},{14,12},{1,3},{3,1},... | collective-permute-start | bytes 786440 | tf_op jit(solution)/shard_map/ppermute | solution.py:325
  77.7 1.2 %collective-permute-done.16.refs_1_ = bf16[256,512]{1,0:T(8,128)(2,1)S(1)} collective-permute-done((bf16[256,512]{1,0:T(8,128)(2,1)S(1)}, bf16[256,512]{1,0:T(8,128)(2,1)S(1)}, u32[]{:S(2)}, u32[]{:S(2)}) %collective-permute-start.16) | collective-permute-done | bytes 262176 | tf_op jit(solution)/shard_map/ppermute | solution.py:325
  78.9 0.7 weigh_members.3
  79.6 1.4 %collective-permute-start.17 = (bf16[3,128,256]{2,1,0:T(8,128)(2,1)S(1)}, bf16[3,128,256]{2,1,0:T(8,128)(2,1)S(1)}, u32[]{:S(2)}, u32[]{:S(2)}) collective-permute-start(bf16[3,128,256]{2,1,0:T(8,128)(2,1)S(1)} %get-tuple-element.71), channel_id=1, source_target_pairs={{0,16},{16,32},{32,48},{48,0},{64,80},{80,96},{96,112},{112,64},{1... | collective-permute-start | bytes 589832 | tf_op jit(solution)/shard_map/ppermute | solution.py:364
  81.0 2.5 %collective-permute-start.18 = (bf16[3,128,256]{2,1,0:T(8,128)(2,1)S(1)}, bf16[3,128,256]{2,1,0:T(8,128)(2,1)S(1)}, u32[]{:S(2)}, u32[]{:S(2)}) collective-permute-start(bf16[3,128,256]{2,1,0:T(8,128)(2,1)S(1)} %get-tuple-element.72), channel_id=1, source_target_pairs={{0,32},{16,48},{32,0},{48,16},{64,96},{80,112},{96,64},{112,80},{1... | collective-permute-start | bytes 589832 | tf_op jit(solution)/shard_map/ppermute | solution.py:364
  83.4 1.3 %collective-permute-start.23 = (bf16[3,128,256]{2,1,0:T(8,128)(2,1)S(1)}, bf16[3,128,256]{2,1,0:T(8,128)(2,1)S(1)}, u32[]{:S(2)}, u32[]{:S(2)}) collective-permute-start(bf16[3,128,256]{2,1,0:T(8,128)(2,1)S(1)} %sum_over_z.2.after), channel_id=1, source_target_pairs={{64,0},{65,15},{66,64},{67,79},{68,4},{69,11},{70,68},{71,75},{72,... | collective-permute-start | bytes 589832 | tf_op jit(solution)/shard_map/ppermute | solution.py:351
  84.7 5.4 %collective-permute-start.22 = (bf16[3,128,256]{2,1,0:T(8,128)(2,1)S(1)}, bf16[3,128,256]{2,1,0:T(8,128)(2,1)S(1)}, u32[]{:S(2)}, u32[]{:S(2)}) collective-permute-start(bf16[3,128,256]{2,1,0:T(8,128)(2,1)S(1)} %sum_over_z.2.after), channel_id=1, source_target_pairs={{0,0},{1,15},{2,64},{3,79},{4,4},{5,11},{6,68},{7,75},{8,6},{9,9},... | collective-permute-start | bytes 589832 | tf_op jit(solution)/shard_map/ppermute | solution.py:351
  90.1 2.2 %collective-permute-done.18.two = bf16[3,128,256]{2,1,0:T(8,128)(2,1)S(1)} collective-permute-done((bf16[3,128,256]{2,1,0:T(8,128)(2,1)S(1)}, bf16[3,128,256]{2,1,0:T(8,128)(2,1)S(1)}, u32[]{:S(2)}, u32[]{:S(2)}) %collective-permute-start.18) | collective-permute-done | bytes 196640 | tf_op jit(solution)/shard_map/ppermute | solution.py:364
  92.3 0.3 sum_over_z.3
  92.7 0.7 collective-permute-start.21
  93.3 7.3 %collective-permute-start.20 = (bf16[3,128,256]{2,1,0:T(8,128)(2,1)S(1)}, bf16[3,128,256]{2,1,0:T(8,128)(2,1)S(1)}, u32[]{:S(2)}, u32[]{:S(2)}) collective-permute-start(bf16[3,128,256]{2,1,0:T(8,128)(2,1)S(1)} %sum_over_z.3), channel_id=1, source_target_pairs={{0,1},{1,14},{2,65},{3,78},{4,5},{5,10},{6,69},{7,74},{8,7},{9,8},... | collective-permute-start | bytes 589832 | tf_op jit(solution)/shard_map/ppermute | solution.py:351
  100.8 6.8 %collective-permute-done.20.near = bf16[3,128,256]{2,1,0:T(8,128)(2,1)S(1)} collective-permute-done((bf16[3,128,256]{2,1,0:T(8,128)(2,1)S(1)}, bf16[3,128,256]{2,1,0:T(8,128)(2,1)S(1)}, u32[]{:S(2)}, u32[]{:S(2)}) %collective-permute-start.20) | collective-permute-done | bytes 196640 | tf_op jit(solution)/shard_map/ppermute | solution.py:351
  107.7 0.8 merge_members.1
  (23 shorter events, 0.4 us)
Async XLA Ops:
  2.1 3.6 %copy-start = (bf16[2,1024,256]{2,1,0:T(8,128)(2,1)S(1)}, bf16[2,1024,256]{2,1,0:T(8,128)(2,1)}, u32[]{:S(2)}) copy-start(bf16[2,1024,256]{2,1,0:T(8,128)(2,1)} %param.5) | copy-start | bytes 3145732
  2.1 11.2 %collective-permute-start = (bf16[768,2304]{1,0:T(8,128)(2,1)S(1)}, bf16[768,2304]{1,0:T(8,128)(2,1)S(1)}, u32[]{:S(2)}, u32[]{:S(2)}) collective-permute-start(bf16[768,2304]{1,0:T(8,128)(2,1)S(1)} %load_to_swap.2.after), channel_id=1, source_target_pairs={{0,2},{2,0},{4,6},{6,4},{8,10},{10,8},{12,14},{14,12},{1,3},{3,1},... | collective-permute-start | bytes 10616840 | tf_op jit(solution)/shard_map/ppermute | solution.py:325
  5.5 15.9 %collective-permute-start.1 = (bf16[768,2048]{1,0:T(8,128)(2,1)S(1)}, bf16[768,2048]{1,0:T(8,128)(2,1)S(1)}, u32[]{:S(2)}, u32[]{:S(2)}) collective-permute-start(bf16[768,2048]{1,0:T(8,128)(2,1)S(1)} %load_to_swap.3.after), channel_id=1, source_target_pairs={{0,2},{2,0},{4,6},{6,4},{8,10},{10,8},{12,14},{14,12},{1,3},{3,1},... | collective-permute-start | bytes 9437192 | tf_op jit(solution)/shard_map/ppermute | solution.py:325
  5.7 37.9 %collective-permute-start.7 = (bf16[2,1024,256]{2,1,0:T(8,128)(2,1)S(1)}, bf16[2,1024,256]{2,1,0:T(8,128)(2,1)S(1)}, u32[]{:S(2)}, u32[]{:S(2)}) collective-permute-start(bf16[2,1024,256]{2,1,0:T(8,128)(2,1)S(1)} %copy-done), channel_id=1, source_target_pairs={{0,0},{1,2},{2,12},{3,14},{4,4},{5,6},{6,8},{7,10},{8,9},{9,11},{1... | collective-permute-start | bytes 3145736 | tf_op jit(solution)/shard_map/ppermute | solution.py:354
  13.4 28.3 %collective-permute-start.2 = (bf16[2,768,256]{2,1,0:T(8,128)(2,1)S(1)}, bf16[2,768,256]{2,1,0:T(8,128)(2,1)S(1)}, u32[]{:S(2)}, u32[]{:S(2)}) collective-permute-start(bf16[2,768,256]{2,1,0:T(8,128)(2,1)S(1)} %pair_grads.1.after), channel_id=1, source_target_pairs={{0,1},{1,0},{2,3},{3,2},{4,5},{5,4},{6,7},{7,6},{8,9},{9,8},{10,11... | collective-permute-start | bytes 2359304 | tf_op jit(solution)/shard_map/ppermute | solution.py:328
  17.1 29.0 %collective-permute-start.4 = (bf16[256,1024]{1,0:T(8,128)(2,1)S(1)}, bf16[256,1024]{1,0:T(8,128)(2,1)S(1)}, u32[]{:S(2)}, u32[]{:S(2)}) collective-permute-start(bf16[256,1024]{1,0:T(8,128)(2,1)S(1)} %get-tuple-element.52), channel_id=1, source_target_pairs={{0,4},{2,6},{4,0},{6,2},{8,12},{10,14},{12,8},{14,10},{1,5},{3,7},... | collective-permute-start | bytes 1572872 | tf_op jit(solution)/shard_map/ppermute | solution.py:331
  17.2 31.8 %collective-permute-start.5 = (bf16[256,1024]{1,0:T(8,128)(2,1)S(1)}, bf16[256,1024]{1,0:T(8,128)(2,1)S(1)}, u32[]{:S(2)}, u32[]{:S(2)}) collective-permute-start(bf16[256,1024]{1,0:T(8,128)(2,1)S(1)} %get-tuple-element.44.after), channel_id=1, source_target_pairs={{0,8},{2,10},{4,12},{6,14},{8,0},{10,2},{12,4},{14,6},{1,9},{3,11}... | collective-permute-start | bytes 1572872 | tf_op jit(solution)/shard_map/ppermute | solution.py:331
  22.6 26.5 %collective-permute-start.6 = (bf16[256,1024]{1,0:T(8,128)(2,1)S(1)}, bf16[256,1024]{1,0:T(8,128)(2,1)S(1)}, u32[]{:S(2)}, u32[]{:S(2)}) collective-permute-start(bf16[256,1024]{1,0:T(8,128)(2,1)S(1)} %get-tuple-element.48.after), channel_id=1, source_target_pairs={{0,12},{2,14},{4,8},{6,10},{8,4},{10,6},{12,0},{14,2},{1,13},{3,15... | collective-permute-start | bytes 1572872 | tf_op jit(solution)/shard_map/ppermute | solution.py:331
  43.7 8.8 %collective-permute-start.9 = (bf16[2,512,256]{2,1,0:T(8,128)(2,1)S(1)}, bf16[2,512,256]{2,1,0:T(8,128)(2,1)S(1)}, u32[]{:S(2)}, u32[]{:S(2)}) collective-permute-start(bf16[2,512,256]{2,1,0:T(8,128)(2,1)S(1)} %get-tuple-element.59), channel_id=1, source_target_pairs={{0,2},{2,0},{4,6},{6,4},{8,10},{10,8},{12,14},{14,12},{1,3},{3,1},... | collective-permute-start | bytes 1572872 | tf_op jit(solution)/shard_map/ppermute | solution.py:325
  43.9 15.0 %collective-permute-start.3 = (bf16[2,256,512]{2,1,0:T(8,128)(2,1)S(1)}, bf16[2,256,512]{2,1,0:T(8,128)(2,1)S(1)}, u32[]{:S(2)}, u32[]{:S(2)}) collective-permute-start(bf16[2,256,512]{2,1,0:T(8,128)(2,1)S(1)} %get-tuple-element.50), channel_id=1, source_target_pairs={{0,4},{2,6},{4,0},{6,2},{8,12},{10,14},{12,8},{14,10},{1,5},{3,7},... | collective-permute-start | bytes 1572872 | tf_op jit(solution)/shard_map/ppermute | solution.py:331
  46.1 21.3 %collective-permute-start.11 = (bf16[2,256,512]{2,1,0:T(8,128)(2,1)S(1)}, bf16[2,256,512]{2,1,0:T(8,128)(2,1)S(1)}, u32[]{:S(2)}, u32[]{:S(2)}) collective-permute-start(bf16[2,256,512]{2,1,0:T(8,128)(2,1)S(1)} %get-tuple-element.63), channel_id=1, source_target_pairs={{0,12},{2,14},{4,8},{6,10},{8,4},{10,6},{12,0},{14,2},{1,13},{3,15... | collective-permute-start | bytes 1572872 | tf_op jit(solution)/shard_map/ppermute | solution.py:331
  50.7 1.8 %collective-permute-start.8 = (bf16[256,512]{1,0:T(8,128)(2,1)S(1)}, bf16[256,512]{1,0:T(8,128)(2,1)S(1)}, u32[]{:S(2)}, u32[]{:S(2)}) collective-permute-start(bf16[256,512]{1,0:T(8,128)(2,1)S(1)} %get-tuple-element.58), channel_id=1, source_target_pairs={{0,2},{2,0},{4,6},{6,4},{8,10},{10,8},{12,14},{14,12},{1,3},{3,1},... | collective-permute-start | bytes 786440 | tf_op jit(solution)/shard_map/ppermute | solution.py:325
  53.2 8.8 %collective-permute-start.12 = (bf16[3,128,256]{2,1,0:T(8,128)(2,1)S(1)}, bf16[3,128,256]{2,1,0:T(8,128)(2,1)S(1)}, u32[]{:S(2)}, u32[]{:S(2)}) collective-permute-start(bf16[3,128,256]{2,1,0:T(8,128)(2,1)S(1)} %get-tuple-element.64), channel_id=1, source_target_pairs={{0,16},{16,32},{32,48},{48,0},{64,80},{80,96},{96,112},{112,64},{1... | collective-permute-start | bytes 589832 | tf_op jit(solution)/shard_map/ppermute | solution.py:364
  54.9 12.2 %collective-permute-start.13 = (bf16[3,128,256]{2,1,0:T(8,128)(2,1)S(1)}, bf16[3,128,256]{2,1,0:T(8,128)(2,1)S(1)}, u32[]{:S(2)}, u32[]{:S(2)}) collective-permute-start(bf16[3,128,256]{2,1,0:T(8,128)(2,1)S(1)} %get-tuple-element.65), channel_id=1, source_target_pairs={{0,32},{16,48},{32,0},{48,16},{64,96},{80,112},{96,64},{112,80},{1... | collective-permute-start | bytes 589832 | tf_op jit(solution)/shard_map/ppermute | solution.py:364
  58.2 8.9 %collective-permute-start.14 = (bf16[3,128,256]{2,1,0:T(8,128)(2,1)S(1)}, bf16[3,128,256]{2,1,0:T(8,128)(2,1)S(1)}, u32[]{:S(2)}, u32[]{:S(2)}) collective-permute-start(bf16[3,128,256]{2,1,0:T(8,128)(2,1)S(1)} %get-tuple-element.66), channel_id=1, source_target_pairs={{0,48},{16,0},{32,16},{48,32},{64,112},{80,64},{96,80},{112,96},{1... | collective-permute-start | bytes 589832 | tf_op jit(solution)/shard_map/ppermute | solution.py:364
  59.7 9.7 %collective-permute-start.10 = (bf16[256,512]{1,0:T(8,128)(2,1)S(1)}, bf16[256,512]{1,0:T(8,128)(2,1)S(1)}, u32[]{:S(2)}, u32[]{:S(2)}) collective-permute-start(bf16[256,512]{1,0:T(8,128)(2,1)S(1)} %get-tuple-element.62), channel_id=1, source_target_pairs={{0,12},{2,14},{4,8},{6,10},{8,4},{10,6},{12,0},{14,2},{1,13},{3,15... | collective-permute-start | bytes 786440 | tf_op jit(solution)/shard_map/ppermute | solution.py:331
  68.2 6.7 %collective-permute-start.15 = (bf16[256,512]{1,0:T(8,128)(2,1)S(1)}, bf16[256,512]{1,0:T(8,128)(2,1)S(1)}, u32[]{:S(2)}, u32[]{:S(2)}) collective-permute-start(bf16[256,512]{1,0:T(8,128)(2,1)S(1)} %get-tuple-element.68), channel_id=1, source_target_pairs={{0,4},{2,6},{4,0},{6,2},{8,12},{10,14},{12,8},{14,10},{1,5},{3,7},... | collective-permute-start | bytes 786440 | tf_op jit(solution)/shard_map/ppermute | solution.py:331
  75.5 3.4 %collective-permute-start.16 = (bf16[256,512]{1,0:T(8,128)(2,1)S(1)}, bf16[256,512]{1,0:T(8,128)(2,1)S(1)}, u32[]{:S(2)}, u32[]{:S(2)}) collective-permute-start(bf16[256,512]{1,0:T(8,128)(2,1)S(1)} %get-tuple-element.70), channel_id=1, source_target_pairs={{0,2},{2,0},{4,6},{6,4},{8,10},{10,8},{12,14},{14,12},{1,3},{3,1},... | collective-permute-start | bytes 786440 | tf_op jit(solution)/shard_map/ppermute | solution.py:325
  79.6 10.5 %collective-permute-start.17 = (bf16[3,128,256]{2,1,0:T(8,128)(2,1)S(1)}, bf16[3,128,256]{2,1,0:T(8,128)(2,1)S(1)}, u32[]{:S(2)}, u32[]{:S(2)}) collective-permute-start(bf16[3,128,256]{2,1,0:T(8,128)(2,1)S(1)} %get-tuple-element.71), channel_id=1, source_target_pairs={{0,16},{16,32},{32,48},{48,0},{64,80},{80,96},{96,112},{112,64},{1... | collective-permute-start | bytes 589832 | tf_op jit(solution)/shard_map/ppermute | solution.py:364
  81.0 11.3 %collective-permute-start.18 = (bf16[3,128,256]{2,1,0:T(8,128)(2,1)S(1)}, bf16[3,128,256]{2,1,0:T(8,128)(2,1)S(1)}, u32[]{:S(2)}, u32[]{:S(2)}) collective-permute-start(bf16[3,128,256]{2,1,0:T(8,128)(2,1)S(1)} %get-tuple-element.72), channel_id=1, source_target_pairs={{0,32},{16,48},{32,0},{48,16},{64,96},{80,112},{96,64},{112,80},{1... | collective-permute-start | bytes 589832 | tf_op jit(solution)/shard_map/ppermute | solution.py:364
  83.4 8.9 %collective-permute-start.19 = (bf16[3,128,256]{2,1,0:T(8,128)(2,1)S(1)}, bf16[3,128,256]{2,1,0:T(8,128)(2,1)S(1)}, u32[]{:S(2)}, u32[]{:S(2)}) collective-permute-start(bf16[3,128,256]{2,1,0:T(8,128)(2,1)S(1)} %get-tuple-element.73), channel_id=1, source_target_pairs={{0,48},{16,0},{32,16},{48,32},{64,112},{80,64},{96,80},{112,96},{1... | collective-permute-start | bytes 589832 | tf_op jit(solution)/shard_map/ppermute | solution.py:364
  83.4 17.2 %collective-permute-start.23 = (bf16[3,128,256]{2,1,0:T(8,128)(2,1)S(1)}, bf16[3,128,256]{2,1,0:T(8,128)(2,1)S(1)}, u32[]{:S(2)}, u32[]{:S(2)}) collective-permute-start(bf16[3,128,256]{2,1,0:T(8,128)(2,1)S(1)} %sum_over_z.2.after), channel_id=1, source_target_pairs={{64,0},{65,15},{66,64},{67,79},{68,4},{69,11},{70,68},{71,75},{72,... | collective-permute-start | bytes 589832 | tf_op jit(solution)/shard_map/ppermute | solution.py:351
  84.7 15.9 %collective-permute-start.22 = (bf16[3,128,256]{2,1,0:T(8,128)(2,1)S(1)}, bf16[3,128,256]{2,1,0:T(8,128)(2,1)S(1)}, u32[]{:S(2)}, u32[]{:S(2)}) collective-permute-start(bf16[3,128,256]{2,1,0:T(8,128)(2,1)S(1)} %sum_over_z.2.after), channel_id=1, source_target_pairs={{0,0},{1,15},{2,64},{3,79},{4,4},{5,11},{6,68},{7,75},{8,6},{9,9},... | collective-permute-start | bytes 589832 | tf_op jit(solution)/shard_map/ppermute | solution.py:351
  92.7 8.1 %collective-permute-start.21 = (bf16[3,128,256]{2,1,0:T(8,128)(2,1)S(1)}, bf16[3,128,256]{2,1,0:T(8,128)(2,1)S(1)}, u32[]{:S(2)}, u32[]{:S(2)}) collective-permute-start(bf16[3,128,256]{2,1,0:T(8,128)(2,1)S(1)} %sum_over_z.3), channel_id=1, source_target_pairs={{64,1},{65,14},{66,65},{67,78},{68,5},{69,10},{70,69},{71,74},{72,... | collective-permute-start | bytes 589832 | tf_op jit(solution)/shard_map/ppermute | solution.py:351
  93.3 14.3 %collective-permute-start.20 = (bf16[3,128,256]{2,1,0:T(8,128)(2,1)S(1)}, bf16[3,128,256]{2,1,0:T(8,128)(2,1)S(1)}, u32[]{:S(2)}, u32[]{:S(2)}) collective-permute-start(bf16[3,128,256]{2,1,0:T(8,128)(2,1)S(1)} %sum_over_z.3), channel_id=1, source_target_pairs={{0,1},{1,14},{2,65},{3,78},{4,5},{5,10},{6,69},{7,74},{8,7},{9,8},... | collective-permute-start | bytes 589832 | tf_op jit(solution)/shard_map/ppermute | solution.py:351

commit v12 on v11

--- a/solution.py
+++ b/solution.py
@@ -282,12 +282,12 @@
     return 2 * (x % 2) if x // 2 == half else 2 * ((3 - x) % 2) + 1
 
 
-def weight_pairs():
+def weight_pairs(phase):
     pairs = []
     for tok in range(X * CORES):
         half, local = divmod(tok, 4)
-        for col in range(2):
-            pairs.append((tok * 2 + col, (keeper(local, half) * 2 + col) * 2 + half))
+        col = half ^ phase
+        pairs.append((tok * 2 + col, (keeper(local, half) * 2 + col) * 2 + half))
     return pairs
 
 
@@ -350,8 +350,8 @@
     def results(phase, sums):
         return [lax.ppermute(sums, ("member", "tok", "col"), result_pairs(phase, y_lo)) for y_lo in range(2)]
 
-    def bring_weights(after):
-        arrived = lax.ppermute(weights, ("tok", "col"), weight_pairs())
+    def bring_weights(phase, after):
+        arrived = lax.ppermute(weights, ("tok", "col"), weight_pairs(phase))
         half_shape = ((2, weights.shape[1] // 2, outs), BF16)
         own, send = call(split_kernel, "split_weights", [half_shape, half_shape], [], [arrived, after])
         return own, swap_cores(send)
@@ -360,7 +360,7 @@
         one, two, three, own_sums = call(
             lambda *refs: weigh_kernel(phase, *refs), "weigh_members", [words] * 3 + [sums], [], [own, other, *moved, after]
         )
-        send = ((1, one), (2, two), (3, three))
+        send = ((2, two), (1, one), (3, three))
         return [lax.ppermute(v, "member", z_pairs(d)) for d, v in send] + [own_sums]
 
     x_send0 = call(
@@ -392,19 +392,20 @@
         both_first_kernel, "fisher_of_other_grads", [pair_shape, kept_shape, gt_shape, gt_shape], [], [*xs, g_other, three]
     )
     swap10 = swap_x(1, sent)
-    moved = bring_weights(kept10)
+    w0 = bring_weights(0, kept10)
     sent, kept11 = call(
-        both_second_kernel, "fisher_of_other_grads", [pair_shape, kept_shape], [], [*xs, gt_own, gt_got, moved[0]]
+        both_second_kernel, "fisher_of_other_grads", [pair_shape, kept_shape], [], [*xs, gt_own, gt_got, w0[0]]
     )
     swap11 = swap_x(3, sent)
 
     own0, other0 = join_direct(sum0, got0, kept11)
-    words0 = weigh(0, own0, other0, moved, own0)
+    words0 = weigh(0, own0, other0, w0, own0)
     part10 = middle(3, swap10, kept10, words0[3])
     first = call(sum_kernel, "sum_over_z", words, [], [*words0, part10[0]])
     part11 = middle(1, swap11, kept11, first)
     own1, other1 = join(settle(part10, part11[0]), part11, first)
-    words1 = weigh(1, own1, other1, moved, own1)
+    w1 = bring_weights(1, own1)
+    words1 = weigh(1, own1, other1, w1, w1[0])
     met = call(meet_kernel, "meet_over_y", sums, [], [*results(0, first), own1])
     second = call(sum_kernel, "sum_over_z", words, [], [*words1, own1])
     near, far = results(1, second)

time: 109 us -> 110 us (level)
  waiting for transfers between devices: 39.1 us -> 44.2 us
  starting transfers between devices: 46.2 us -> 42.1 us
    ppermute x7, waiting for transfers between devices: 5.22 us -> 16.1 us  [swap_x(): return lax.ppermute(sent, 'tok', x_pairs(flip))]
    ppermute x1, waiting for transfers between devices: 16.8 us -> 8.51 us  [swap_cols(): return lax.ppermute(send, 'col', [(0, 1), (1, 0)])]
    ppermute x4, starting transfers between devices: 14.6 us -> 7.61 us  [results(): lax.ppermute(sums, ('member', 'tok', 'col'), result_pairs(phase, y_lo))]
    ppermute x6, starting transfers between devices: 9.58 us -> 13 us  [weigh(): return [lax.ppermute(v, 'member', z_pairs(d)) for d, v in send] + [own_sums]]
    ppermute x1, starting transfers between devices: 2.47 us -> 0.09 us  [swap_cols(): return lax.ppermute(send, 'col', [(0, 1), (1, 0)])]
    ppermute x5 -> x6, starting transfers between devices: 4.81 us -> 6.5 us  [swap_cores(): return lax.ppermute(send, 'tok', [(t, t ^ 1) for t in range(8)])]
    ppermute x1 -> x2, starting transfers between devices: 4.75 us -> 6.09 us  [bring_weights(): arrived = lax.ppermute(weights, ('tok', 'col'), weight_pairs(phase))]
    ppermute x7, starting transfers between devices: 10 us -> 8.81 us  [swap_x(): return lax.ppermute(sent, 'tok', x_pairs(flip))]
  transfers between devices with their start and end apart: 24 -> 26, of which waited for: 8 -> 14; matrix products, arithmetic and copies ran while one was open for 0% -> 0% of each run, Pallas kernels for 17% -> 18%
where the time goes in v12:
time: 110 us
  waiting for transfers between devices  44.2 us (40%)
  starting transfers between devices  42.1 us (38%)
  Pallas kernels  23 us (21%)
    pallas_call x21, Pallas kernels, call(): pl.pallas_call(kernel, out_shape=shapes, in_specs=[HBM] * len(hbm) + [VME...  22.1 us
    ppermute x7, waiting for transfers between devices, swap_x(): return lax.ppermute(sent, 'tok', x_pairs(flip))  16.1 us
    ppermute x6, starting transfers between devices, weigh(): return [lax.ppermute(v, 'member', z_pairs(d)) for d, v in send] + [own_sums]  13 us
    ppermute x6, waiting for transfers between devices, weigh(): return [lax.ppermute(v, 'member', z_pairs(d)) for d, v in send] + [own_sums]  8.89 us
    ppermute x7, starting transfers between devices, swap_x(): return lax.ppermute(sent, 'tok', x_pairs(flip))  8.81 us
    ppermute x1, waiting for transfers between devices, swap_cols(): return lax.ppermute(send, 'col', [(0, 1), (1, 0)])  8.51 us
    ppermute x4, waiting for transfers between devices, results(): lax.ppermute(sums, ('member', 'tok', 'col'), result_pairs(phase, y_lo))  7.81 us
    ppermute x4, starting transfers between devices, results(): lax.ppermute(sums, ('member', 'tok', 'col'), result_pairs(phase, y_lo))  7.61 us
  transfers between devices with their start and end apart: 26, of which 14 were waited for; matrix products, arithmetic and copies ran while one was open for 0% of the time, Pallas kernels for 18%

profile of v12, /device:TPU:1, one launch (start us, length us, event | category | flops | bytes accessed | tf_op | source)
XLA Modules:
  0.0 109.6 jit_solution(11237967581417243999)
XLA Ops:
  0.0 2.0 %load_to_swap.2.after = bf16[768,2304]{1,0:T(8,128)(2,1)S(1)} custom-call(bf16[2,768,4096]{2,1,0:T(8,128)(2,1)} %x_ref.7, bf16[2,768,256]{2,1,0:T(8,128)(2,1)} %g_ref.3), custom_call_target="tpu_custom_call" | custom-call | flops 1 | bytes 1 | tf_op jit(solution)/shard_map/load_to_swap/pallas_call | solution.py:66
  2.1 1.5 %collective-permute-start = (bf16[768,2304]{1,0:T(8,128)(2,1)S(1)}, bf16[768,2304]{1,0:T(8,128)(2,1)S(1)}, u32[]{:S(2)}, u32[]{:S(2)}) collective-permute-start(bf16[768,2304]{1,0:T(8,128)(2,1)S(1)} %load_to_swap.2.after), channel_id=1, source_target_pairs={{0,2},{2,0},{4,6},{6,4},{8,10},{10,8},{12,14},{14,12},{1,3},{3,1},... | collective-permute-start | bytes 10616840 | tf_op jit(solution)/shard_map/ppermute | solution.py:325
  3.6 1.9 %load_to_swap.3.after = bf16[768,2048]{1,0:T(8,128)(2,1)S(1)} custom-call(bf16[2,768,4096]{2,1,0:T(8,128)(2,1)} %x_ref.7, bf16[768,2304]{1,0:T(8,128)(2,1)S(1)} %load_to_swap.2.after), custom_call_target="tpu_custom_call" | custom-call | flops 1 | bytes 1 | tf_op jit(solution)/shard_map/load_to_swap/pallas_call | solution.py:66
  5.7 4.8 %collective-permute-start.7 = (bf16[2,1024,256]{2,1,0:T(8,128)(2,1)S(1)}, bf16[2,1024,256]{2,1,0:T(8,128)(2,1)S(1)}, u32[]{:S(2)}, u32[]{:S(2)}) collective-permute-start(bf16[2,1024,256]{2,1,0:T(8,128)(2,1)S(1)} %copy-done), channel_id=1, source_target_pairs={{0,0},{2,12},{4,4},{6,8},{9,11},{11,7},{13,15},{15,3},{16,16},{18,... | collective-permute-start | bytes 3145736 | tf_op jit(solution)/shard_map/ppermute | solution.py:354
  10.5 2.9 %fisher_of_own_tokens.2 = (bf16[768,2048]{1,0:T(8,128)(2,1)S(1)}, bf16[768,256]{1,0:T(8,128)(2,1)S(1)}, bf16[256,768]{1,0:T(8,128)(2,1)S(1)}, f32[2,256,1024]{2,1,0:T(8,128)S(1)}) custom-call(bf16[2,768,4096]{2,1,0:T(8,128)(2,1)} %x_ref.7, bf16[2,768,256]{2,1,0:T(8,128)(2,1)} %g_ref.3, bf16[768,2048]{1,0:T(8,128)(2,1)S(1)} %load_to_swap.3.after), custom_call_target="tpu_custom_call" | custom-call | flops 1 | bytes 1 | tf_op jit(solution)/shard_map/fisher_of_own_tokens/pallas_call | solution.py:66
  13.5 1.3 %fisher_of_both_cores.2 = (bf16[256,1024]{1,0:T(8,128)(2,1)S(1)}, bf16[256,1024]{1,0:T(8,128)(2,1)S(1)}, bf16[256,768]{1,0:T(8,128)(2,1)S(1)}) custom-call(bf16[768,2304]{1,0:T(8,128)(2,1)S(1)} %collective-permute-done.got.x_ref.got_a, f32[2,256,1024]{2,1,0:T(8,128)S(1)} %get-tuple-element.44.part_ref, bf16[2,768,256]{2,1,0:T(8,128)(2,1)S(1)} %pair_grads.1.after), custom_call_target="tpu_custom_call" | custom-call | flops 1 | bytes 1 | tf_op jit(solution)/shard_map/fisher_of_both_cores/pallas_call | solution.py:66
  14.8 0.8 collective-permute-start.4
  15.6 3.3 %collective-permute-start.5 = (bf16[256,1024]{1,0:T(8,128)(2,1)S(1)}, bf16[256,1024]{1,0:T(8,128)(2,1)S(1)}, u32[]{:S(2)}, u32[]{:S(2)}) collective-permute-start(bf16[256,1024]{1,0:T(8,128)(2,1)S(1)} %get-tuple-element.46.after), channel_id=1, source_target_pairs={{0,8},{2,10},{4,12},{6,14},{8,0},{10,2},{12,4},{14,6},{1,9},{3,11}... | collective-permute-start | bytes 1572872 | tf_op jit(solution)/shard_map/ppermute | solution.py:331
  18.8 2.6 %fisher_of_own_tokens.3 = (bf16[768,2048]{1,0:T(8,128)(2,1)S(1)}, f32[2,256,1024]{2,1,0:T(8,128)S(1)}) custom-call(bf16[2,768,4096]{2,1,0:T(8,128)(2,1)} %x_ref.7, bf16[256,768]{1,0:T(8,128)(2,1)S(1)} %get-tuple-element.43.after.gt_ref, bf16[256,1024]{1,0:T(8,128)(2,1)S(1)} %get-tuple-element.46.after), custom_call_target="tpu_custom_call" | custom-call | flops 1 | bytes 1 | tf_op jit(solution)/shard_map/fisher_of_own_tokens/pallas_call | solution.py:66
  21.4 1.1 %fisher_of_both_cores.3 = (bf16[256,1024]{1,0:T(8,128)(2,1)S(1)}, f32[256,1024]{1,0:T(8,128)S(1)}) custom-call(bf16[768,2048]{1,0:T(8,128)(2,1)S(1)} %collective-permute-done.1.x_ref.got_b, bf16[256,768]{1,0:T(8,128)(2,1)S(1)} %get-tuple-element.48.gt_ref, f32[2,256,1024]{2,1,0:T(8,128)S(1)} %get-tuple-element.49.part_ref, ...), custom_call_target="tpu_custom_call" | custom-call | flops 1 | bytes 1 | tf_op jit(solution)/shard_map/fisher_of_both_cores/pallas_call | solution.py:66
  22.6 8.5 %collective-permute-done.2.g_ref = bf16[2,768,256]{2,1,0:T(8,128)(2,1)S(1)} collective-permute-done((bf16[2,768,256]{2,1,0:T(8,128)(2,1)S(1)}, bf16[2,768,256]{2,1,0:T(8,128)(2,1)S(1)}, u32[]{:S(2)}, u32[]{:S(2)}) %collective-permute-start.2) | collective-permute-done | bytes 786464 | tf_op jit(solution)/shard_map/ppermute | solution.py:328
  31.2 1.3 %collective-permute-start.17 = (bf16[2,1024,256]{2,1,0:T(8,128)(2,1)S(1)}, bf16[2,1024,256]{2,1,0:T(8,128)(2,1)S(1)}, u32[]{:S(2)}, u32[]{:S(2)}) collective-permute-start(bf16[2,1024,256]{2,1,0:T(8,128)(2,1)S(1)} %copy-done), channel_id=1, source_target_pairs={{1,2},{3,14},{5,6},{7,10},{8,9},{10,5},{12,13},{14,1},{17,18},{19,... | collective-permute-start | bytes 3145736 | tf_op jit(solution)/shard_map/ppermute | solution.py:354
  32.4 1.9 %fisher_of_other_grads.2 = (bf16[2,256,512]{2,1,0:T(8,128)(2,1)S(1)}, f32[2,256,512]{2,1,0:T(8,128)S(1)}, bf16[256,768]{1,0:T(8,128)(2,1)S(1)}, bf16[256,768]{1,0:T(8,128)(2,1)S(1)}) custom-call(bf16[768,2048]{1,0:T(8,128)(2,1)S(1)} %get-tuple-element.42.own_a, bf16[768,2304]{1,0:T(8,128)(2,1)S(1)} %collective-permute-done.got.x_ref.got_a, ...), custom_call_target="tpu_custom_call" | custom-call | flops 1 | bytes 1 | tf_op jit(solution)/shard_map/fisher_of_other_grads/pallas_call | solution.py:66
  34.6 1.4 %collective-permute-start.3 = (bf16[2,256,512]{2,1,0:T(8,128)(2,1)S(1)}, bf16[2,256,512]{2,1,0:T(8,128)(2,1)S(1)}, u32[]{:S(2)}, u32[]{:S(2)}) collective-permute-start(bf16[2,256,512]{2,1,0:T(8,128)(2,1)S(1)} %get-tuple-element.52), channel_id=1, source_target_pairs={{0,4},{2,6},{4,0},{6,2},{8,12},{10,14},{12,8},{14,10},{1,5},{3,7},... | collective-permute-start | bytes 1572872 | tf_op jit(solution)/shard_map/ppermute | solution.py:331
  36.0 1.9 %fisher_of_other_grads.3 = (bf16[2,256,512]{2,1,0:T(8,128)(2,1)S(1)}, f32[2,256,512]{2,1,0:T(8,128)S(1)}) custom-call(bf16[768,2048]{1,0:T(8,128)(2,1)S(1)} %get-tuple-element.42.own_a, bf16[768,2304]{1,0:T(8,128)(2,1)S(1)} %collective-permute-done.got.x_ref.got_a, bf16[768,2048]{1,0:T(8,128)(2,1)S(1)} %get-tuple-element.47.after.own_b, ...), custom_call_target="tpu_custom_call" | custom-call | flops 1 | bytes 1 | tf_op jit(solution)/shard_map/fisher_of_other_grads/pallas_call | solution.py:66
  37.8 3.6 %collective-permute-done.5.two = bf16[256,1024]{1,0:T(8,128)(2,1)S(1)} collective-permute-done((bf16[256,1024]{1,0:T(8,128)(2,1)S(1)}, bf16[256,1024]{1,0:T(8,128)(2,1)S(1)}, u32[]{:S(2)}, u32[]{:S(2)}) %collective-permute-start.5) | collective-permute-done | bytes 524320 | tf_op jit(solution)/shard_map/ppermute | solution.py:331
  41.4 3.3 %collective-permute-start.11 = (bf16[2,256,512]{2,1,0:T(8,128)(2,1)S(1)}, bf16[2,256,512]{2,1,0:T(8,128)(2,1)S(1)}, u32[]{:S(2)}, u32[]{:S(2)}) collective-permute-start(bf16[2,256,512]{2,1,0:T(8,128)(2,1)S(1)} %get-tuple-element.65), channel_id=1, source_target_pairs={{0,12},{2,14},{4,8},{6,10},{8,4},{10,6},{12,0},{14,2},{1,13},{3,15... | collective-permute-start | bytes 1572872 | tf_op jit(solution)/shard_map/ppermute | solution.py:331
  44.7 2.6 %collective-permute-done.6.three = bf16[256,1024]{1,0:T(8,128)(2,1)S(1)} collective-permute-done((bf16[256,1024]{1,0:T(8,128)(2,1)S(1)}, bf16[256,1024]{1,0:T(8,128)(2,1)S(1)}, u32[]{:S(2)}, u32[]{:S(2)}) %collective-permute-start.6) | collective-permute-done | bytes 524320 | tf_op jit(solution)/shard_map/ppermute | solution.py:331
  47.3 1.6 %fisher_over_tokens.3 = (f32[256,512]{1,0:T(8,128)S(1)}, bf16[256,512]{1,0:T(8,128)(2,1)S(1)}) custom-call(f32[256,1024]{1,0:T(8,128)S(1)} %get-tuple-element.53.own, bf16[256,1024]{1,0:T(8,128)(2,1)S(1)} %collective-permute-done.4.one, bf16[256,1024]{1,0:T(8,128)(2,1)S(1)} %collective-permute-done.5.two, ...), custom_call_target="tpu_custom_call" | custom-call | flops 1 | bytes 1 | tf_op jit(solution)/shard_map/fisher_over_tokens/pallas_call | solution.py:66
  48.9 4.1 %collective-permute-start.8 = (bf16[256,512]{1,0:T(8,128)(2,1)S(1)}, bf16[256,512]{1,0:T(8,128)(2,1)S(1)}, u32[]{:S(2)}, u32[]{:S(2)}) collective-permute-start(bf16[256,512]{1,0:T(8,128)(2,1)S(1)} %get-tuple-element.60), channel_id=1, source_target_pairs={{0,2},{2,0},{4,6},{6,4},{8,10},{10,8},{12,14},{14,12},{1,3},{3,1},... | collective-permute-start | bytes 786440 | tf_op jit(solution)/shard_map/ppermute | solution.py:325
  53.1 1.2 %collective-permute-done.8.refs_1_ = bf16[256,512]{1,0:T(8,128)(2,1)S(1)} collective-permute-done((bf16[256,512]{1,0:T(8,128)(2,1)S(1)}, bf16[256,512]{1,0:T(8,128)(2,1)S(1)}, u32[]{:S(2)}, u32[]{:S(2)}) %collective-permute-start.8) | collective-permute-done | bytes 262176 | tf_op jit(solution)/shard_map/ppermute | solution.py:325
  54.2 0.7 weigh_members.2
  55.0 3.7 %collective-permute-start.12 = (bf16[3,128,256]{2,1,0:T(8,128)(2,1)S(1)}, bf16[3,128,256]{2,1,0:T(8,128)(2,1)S(1)}, u32[]{:S(2)}, u32[]{:S(2)}) collective-permute-start(bf16[3,128,256]{2,1,0:T(8,128)(2,1)S(1)} %get-tuple-element.66), channel_id=1, source_target_pairs={{0,32},{16,48},{32,0},{48,16},{64,96},{80,112},{96,64},{112,80},{1... | collective-permute-start | bytes 589832 | tf_op jit(solution)/shard_map/ppermute | solution.py:364
  58.7 0.7 collective-permute-start.13
  59.4 1.9 %collective-permute-start.14 = (bf16[3,128,256]{2,1,0:T(8,128)(2,1)S(1)}, bf16[3,128,256]{2,1,0:T(8,128)(2,1)S(1)}, u32[]{:S(2)}, u32[]{:S(2)}) collective-permute-start(bf16[3,128,256]{2,1,0:T(8,128)(2,1)S(1)} %get-tuple-element.68), channel_id=1, source_target_pairs={{0,48},{16,0},{32,16},{48,32},{64,112},{80,64},{96,80},{112,96},{1... | collective-permute-start | bytes 589832 | tf_op jit(solution)/shard_map/ppermute | solution.py:364
  61.3 0.7 fisher_over_first_swap.2
  62.1 1.6 %collective-permute-done.12.one = bf16[3,128,256]{2,1,0:T(8,128)(2,1)S(1)} collective-permute-done((bf16[3,128,256]{2,1,0:T(8,128)(2,1)S(1)}, bf16[3,128,256]{2,1,0:T(8,128)(2,1)S(1)}, u32[]{:S(2)}, u32[]{:S(2)}) %collective-permute-start.12) | collective-permute-done | bytes 196640 | tf_op jit(solution)/shard_map/ppermute | solution.py:364
  63.6 4.6 %collective-permute-done.13.two = bf16[3,128,256]{2,1,0:T(8,128)(2,1)S(1)} collective-permute-done((bf16[3,128,256]{2,1,0:T(8,128)(2,1)S(1)}, bf16[3,128,256]{2,1,0:T(8,128)(2,1)S(1)}, u32[]{:S(2)}, u32[]{:S(2)}) %collective-permute-start.13) | collective-permute-done | bytes 196640 | tf_op jit(solution)/shard_map/ppermute | solution.py:364
  68.6 4.9 %collective-permute-done.11.got_ref = bf16[2,256,512]{2,1,0:T(8,128)(2,1)S(1)} collective-permute-done((bf16[2,256,512]{2,1,0:T(8,128)(2,1)S(1)}, bf16[2,256,512]{2,1,0:T(8,128)(2,1)S(1)}, u32[]{:S(2)}, u32[]{:S(2)}) %collective-permute-start.11) | collective-permute-done | bytes 524320 | tf_op jit(solution)/shard_map/ppermute | solution.py:331
  73.5 0.7 fisher_over_first_swap.3
  74.4 2.4 %collective-permute-done.10.got = bf16[256,512]{1,0:T(8,128)(2,1)S(1)} collective-permute-done((bf16[256,512]{1,0:T(8,128)(2,1)S(1)}, bf16[256,512]{1,0:T(8,128)(2,1)S(1)}, u32[]{:S(2)}, u32[]{:S(2)}) %collective-permute-start.10) | collective-permute-done | bytes 262176 | tf_op jit(solution)/shard_map/ppermute | solution.py:331
  77.1 2.5 %collective-permute-done.15.got = bf16[256,512]{1,0:T(8,128)(2,1)S(1)} collective-permute-done((bf16[256,512]{1,0:T(8,128)(2,1)S(1)}, bf16[256,512]{1,0:T(8,128)(2,1)S(1)}, u32[]{:S(2)}, u32[]{:S(2)}) %collective-permute-start.15) | collective-permute-done | bytes 262176 | tf_op jit(solution)/shard_map/ppermute | solution.py:331
  79.6 0.6 fisher_over_tokens.5
  80.4 0.5 collective-permute-start.16
  80.9 1.8 %collective-permute-done.16.refs_1_ = bf16[256,512]{1,0:T(8,128)(2,1)S(1)} collective-permute-done((bf16[256,512]{1,0:T(8,128)(2,1)S(1)}, bf16[256,512]{1,0:T(8,128)(2,1)S(1)}, u32[]{:S(2)}, u32[]{:S(2)}) %collective-permute-start.16) | collective-permute-done | bytes 262176 | tf_op jit(solution)/shard_map/ppermute | solution.py:325
  82.7 0.7 weigh_members.3
  83.4 4.0 %collective-permute-start.19 = (bf16[3,128,256]{2,1,0:T(8,128)(2,1)S(1)}, bf16[3,128,256]{2,1,0:T(8,128)(2,1)S(1)}, u32[]{:S(2)}, u32[]{:S(2)}) collective-permute-start(bf16[3,128,256]{2,1,0:T(8,128)(2,1)S(1)} %get-tuple-element.75), channel_id=1, source_target_pairs={{0,32},{16,48},{32,0},{48,16},{64,96},{80,112},{96,64},{112,80},{1... | collective-permute-start | bytes 589832 | tf_op jit(solution)/shard_map/ppermute | solution.py:364
  87.4 0.8 collective-permute-start.20
  88.1 1.9 %collective-permute-start.21 = (bf16[3,128,256]{2,1,0:T(8,128)(2,1)S(1)}, bf16[3,128,256]{2,1,0:T(8,128)(2,1)S(1)}, u32[]{:S(2)}, u32[]{:S(2)}) collective-permute-start(bf16[3,128,256]{2,1,0:T(8,128)(2,1)S(1)} %get-tuple-element.77), channel_id=1, source_target_pairs={{0,48},{16,0},{32,16},{48,32},{64,112},{80,64},{96,80},{112,96},{1... | collective-permute-start | bytes 589832 | tf_op jit(solution)/shard_map/ppermute | solution.py:364
  90.0 3.2 %collective-permute-start.24 = (bf16[3,128,256]{2,1,0:T(8,128)(2,1)S(1)}, bf16[3,128,256]{2,1,0:T(8,128)(2,1)S(1)}, u32[]{:S(2)}, u32[]{:S(2)}) collective-permute-start(bf16[3,128,256]{2,1,0:T(8,128)(2,1)S(1)} %sum_over_z.2.after), channel_id=1, source_target_pairs={{0,0},{1,15},{2,64},{3,79},{4,4},{5,11},{6,68},{7,75},{8,6},{9,9},... | collective-permute-start | bytes 589832 | tf_op jit(solution)/shard_map/ppermute | solution.py:351
  93.2 1.3 %collective-permute-start.25 = (bf16[3,128,256]{2,1,0:T(8,128)(2,1)S(1)}, bf16[3,128,256]{2,1,0:T(8,128)(2,1)S(1)}, u32[]{:S(2)}, u32[]{:S(2)}) collective-permute-start(bf16[3,128,256]{2,1,0:T(8,128)(2,1)S(1)} %sum_over_z.2.after), channel_id=1, source_target_pairs={{64,0},{65,15},{66,64},{67,79},{68,4},{69,11},{70,68},{71,75},{72,... | collective-permute-start | bytes 589832 | tf_op jit(solution)/shard_map/ppermute | solution.py:351
  94.5 2.4 %collective-permute-done.20.two = bf16[3,128,256]{2,1,0:T(8,128)(2,1)S(1)} collective-permute-done((bf16[3,128,256]{2,1,0:T(8,128)(2,1)S(1)}, bf16[3,128,256]{2,1,0:T(8,128)(2,1)S(1)}, u32[]{:S(2)}, u32[]{:S(2)}) %collective-permute-start.20) | collective-permute-done | bytes 196640 | tf_op jit(solution)/shard_map/ppermute | solution.py:364
  97.2 0.3 sum_over_z.3
  97.6 2.5 %collective-permute-start.22 = (bf16[3,128,256]{2,1,0:T(8,128)(2,1)S(1)}, bf16[3,128,256]{2,1,0:T(8,128)(2,1)S(1)}, u32[]{:S(2)}, u32[]{:S(2)}) collective-permute-start(bf16[3,128,256]{2,1,0:T(8,128)(2,1)S(1)} %sum_over_z.3), channel_id=1, source_target_pairs={{0,1},{1,14},{2,65},{3,78},{4,5},{5,10},{6,69},{7,74},{8,7},{9,8},... | collective-permute-start | bytes 589832 | tf_op jit(solution)/shard_map/ppermute | solution.py:351
  100.1 0.7 collective-permute-start.23
  100.8 1.5 %collective-permute-done.25.far = bf16[3,128,256]{2,1,0:T(8,128)(2,1)S(1)} collective-permute-done((bf16[3,128,256]{2,1,0:T(8,128)(2,1)S(1)}, bf16[3,128,256]{2,1,0:T(8,128)(2,1)S(1)}, u32[]{:S(2)}, u32[]{:S(2)}) %collective-permute-start.25) | collective-permute-done | bytes 196640 | tf_op jit(solution)/shard_map/ppermute | solution.py:351
  102.5 6.3 %collective-permute-done.22.near = bf16[3,128,256]{2,1,0:T(8,128)(2,1)S(1)} collective-permute-done((bf16[3,128,256]{2,1,0:T(8,128)(2,1)S(1)}, bf16[3,128,256]{2,1,0:T(8,128)(2,1)S(1)}, u32[]{:S(2)}, u32[]{:S(2)}) %collective-permute-start.22) | collective-permute-done | bytes 196640 | tf_op jit(solution)/shard_map/ppermute | solution.py:351
  108.7 0.8 merge_members.1
  (28 shorter events, 2.0 us)
Async XLA Ops:
  2.1 3.6 %copy-start = (bf16[2,1024,256]{2,1,0:T(8,128)(2,1)S(1)}, bf16[2,1024,256]{2,1,0:T(8,128)(2,1)}, u32[]{:S(2)}) copy-start(bf16[2,1024,256]{2,1,0:T(8,128)(2,1)} %param.5) | copy-start | bytes 3145732
  2.1 11.3 %collective-permute-start = (bf16[768,2304]{1,0:T(8,128)(2,1)S(1)}, bf16[768,2304]{1,0:T(8,128)(2,1)S(1)}, u32[]{:S(2)}, u32[]{:S(2)}) collective-permute-start(bf16[768,2304]{1,0:T(8,128)(2,1)S(1)} %load_to_swap.2.after), channel_id=1, source_target_pairs={{0,2},{2,0},{4,6},{6,4},{8,10},{10,8},{12,14},{14,12},{1,3},{3,1},... | collective-permute-start | bytes 10616840 | tf_op jit(solution)/shard_map/ppermute | solution.py:325
  5.5 15.9 %collective-permute-start.1 = (bf16[768,2048]{1,0:T(8,128)(2,1)S(1)}, bf16[768,2048]{1,0:T(8,128)(2,1)S(1)}, u32[]{:S(2)}, u32[]{:S(2)}) collective-permute-start(bf16[768,2048]{1,0:T(8,128)(2,1)S(1)} %load_to_swap.3.after), channel_id=1, source_target_pairs={{0,2},{2,0},{4,6},{6,4},{8,10},{10,8},{12,14},{14,12},{1,3},{3,1},... | collective-permute-start | bytes 9437192 | tf_op jit(solution)/shard_map/ppermute | solution.py:325
  5.7 28.7 %collective-permute-start.7 = (bf16[2,1024,256]{2,1,0:T(8,128)(2,1)S(1)}, bf16[2,1024,256]{2,1,0:T(8,128)(2,1)S(1)}, u32[]{:S(2)}, u32[]{:S(2)}) collective-permute-start(bf16[2,1024,256]{2,1,0:T(8,128)(2,1)S(1)} %copy-done), channel_id=1, source_target_pairs={{0,0},{2,12},{4,4},{6,8},{9,11},{11,7},{13,15},{15,3},{16,16},{18,... | collective-permute-start | bytes 3145736 | tf_op jit(solution)/shard_map/ppermute | solution.py:354
  13.4 17.7 %collective-permute-start.2 = (bf16[2,768,256]{2,1,0:T(8,128)(2,1)S(1)}, bf16[2,768,256]{2,1,0:T(8,128)(2,1)S(1)}, u32[]{:S(2)}, u32[]{:S(2)}) collective-permute-start(bf16[2,768,256]{2,1,0:T(8,128)(2,1)S(1)} %pair_grads.1.after), channel_id=1, source_target_pairs={{0,1},{1,0},{2,3},{3,2},{4,5},{5,4},{6,7},{7,6},{8,9},{9,8},{10,11... | collective-permute-start | bytes 2359304 | tf_op jit(solution)/shard_map/ppermute | solution.py:328
  14.8 19.8 %collective-permute-start.4 = (bf16[256,1024]{1,0:T(8,128)(2,1)S(1)}, bf16[256,1024]{1,0:T(8,128)(2,1)S(1)}, u32[]{:S(2)}, u32[]{:S(2)}) collective-permute-start(bf16[256,1024]{1,0:T(8,128)(2,1)S(1)} %get-tuple-element.54), channel_id=1, source_target_pairs={{0,4},{2,6},{4,0},{6,2},{8,12},{10,14},{12,8},{14,10},{1,5},{3,7},... | collective-permute-start | bytes 1572872 | tf_op jit(solution)/shard_map/ppermute | solution.py:331
  15.6 25.9 %collective-permute-start.5 = (bf16[256,1024]{1,0:T(8,128)(2,1)S(1)}, bf16[256,1024]{1,0:T(8,128)(2,1)S(1)}, u32[]{:S(2)}, u32[]{:S(2)}) collective-permute-start(bf16[256,1024]{1,0:T(8,128)(2,1)S(1)} %get-tuple-element.46.after), channel_id=1, source_target_pairs={{0,8},{2,10},{4,12},{6,14},{8,0},{10,2},{12,4},{14,6},{1,9},{3,11}... | collective-permute-start | bytes 1572872 | tf_op jit(solution)/shard_map/ppermute | solution.py:331
  22.6 24.7 %collective-permute-start.6 = (bf16[256,1024]{1,0:T(8,128)(2,1)S(1)}, bf16[256,1024]{1,0:T(8,128)(2,1)S(1)}, u32[]{:S(2)}, u32[]{:S(2)}) collective-permute-start(bf16[256,1024]{1,0:T(8,128)(2,1)S(1)} %get-tuple-element.50.after), channel_id=1, source_target_pairs={{0,12},{2,14},{4,8},{6,10},{8,4},{10,6},{12,0},{14,2},{1,13},{3,15... | collective-permute-start | bytes 1572872 | tf_op jit(solution)/shard_map/ppermute | solution.py:331
  31.2 49.0 %collective-permute-start.17 = (bf16[2,1024,256]{2,1,0:T(8,128)(2,1)S(1)}, bf16[2,1024,256]{2,1,0:T(8,128)(2,1)S(1)}, u32[]{:S(2)}, u32[]{:S(2)}) collective-permute-start(bf16[2,1024,256]{2,1,0:T(8,128)(2,1)S(1)} %copy-done), channel_id=1, source_target_pairs={{1,2},{3,14},{5,6},{7,10},{8,9},{10,5},{12,13},{14,1},{17,18},{19,... | collective-permute-start | bytes 3145736 | tf_op jit(solution)/shard_map/ppermute | solution.py:354
  34.5 19.8 %collective-permute-start.9 = (bf16[2,512,256]{2,1,0:T(8,128)(2,1)S(1)}, bf16[2,512,256]{2,1,0:T(8,128)(2,1)S(1)}, u32[]{:S(2)}, u32[]{:S(2)}) collective-permute-start(bf16[2,512,256]{2,1,0:T(8,128)(2,1)S(1)} %get-tuple-element.61), channel_id=1, source_target_pairs={{0,2},{2,0},{4,6},{6,4},{8,10},{10,8},{12,14},{14,12},{1,3},{3,1},... | collective-permute-start | bytes 1572872 | tf_op jit(solution)/shard_map/ppermute | solution.py:325
  34.6 24.8 %collective-permute-start.3 = (bf16[2,256,512]{2,1,0:T(8,128)(2,1)S(1)}, bf16[2,256,512]{2,1,0:T(8,128)(2,1)S(1)}, u32[]{:S(2)}, u32[]{:S(2)}) collective-permute-start(bf16[2,256,512]{2,1,0:T(8,128)(2,1)S(1)} %get-tuple-element.52), channel_id=1, source_target_pairs={{0,4},{2,6},{4,0},{6,2},{8,12},{10,14},{12,8},{14,10},{1,5},{3,7},... | collective-permute-start | bytes 1572872 | tf_op jit(solution)/shard_map/ppermute | solution.py:331
  41.4 32.1 %collective-permute-start.11 = (bf16[2,256,512]{2,1,0:T(8,128)(2,1)S(1)}, bf16[2,256,512]{2,1,0:T(8,128)(2,1)S(1)}, u32[]{:S(2)}, u32[]{:S(2)}) collective-permute-start(bf16[2,256,512]{2,1,0:T(8,128)(2,1)S(1)} %get-tuple-element.65), channel_id=1, source_target_pairs={{0,12},{2,14},{4,8},{6,10},{8,4},{10,6},{12,0},{14,2},{1,13},{3,15... | collective-permute-start | bytes 1572872 | tf_op jit(solution)/shard_map/ppermute | solution.py:331
  48.9 5.3 %collective-permute-start.8 = (bf16[256,512]{1,0:T(8,128)(2,1)S(1)}, bf16[256,512]{1,0:T(8,128)(2,1)S(1)}, u32[]{:S(2)}, u32[]{:S(2)}) collective-permute-start(bf16[256,512]{1,0:T(8,128)(2,1)S(1)} %get-tuple-element.60), channel_id=1, source_target_pairs={{0,2},{2,0},{4,6},{6,4},{8,10},{10,8},{12,14},{14,12},{1,3},{3,1},... | collective-permute-start | bytes 786440 | tf_op jit(solution)/shard_map/ppermute | solution.py:325
  55.0 8.7 %collective-permute-start.12 = (bf16[3,128,256]{2,1,0:T(8,128)(2,1)S(1)}, bf16[3,128,256]{2,1,0:T(8,128)(2,1)S(1)}, u32[]{:S(2)}, u32[]{:S(2)}) collective-permute-start(bf16[3,128,256]{2,1,0:T(8,128)(2,1)S(1)} %get-tuple-element.66), channel_id=1, source_target_pairs={{0,32},{16,48},{32,0},{48,16},{64,96},{80,112},{96,64},{112,80},{1... | collective-permute-start | bytes 589832 | tf_op jit(solution)/shard_map/ppermute | solution.py:364
  58.7 9.6 %collective-permute-start.13 = (bf16[3,128,256]{2,1,0:T(8,128)(2,1)S(1)}, bf16[3,128,256]{2,1,0:T(8,128)(2,1)S(1)}, u32[]{:S(2)}, u32[]{:S(2)}) collective-permute-start(bf16[3,128,256]{2,1,0:T(8,128)(2,1)S(1)} %get-tuple-element.67), channel_id=1, source_target_pairs={{0,16},{16,32},{32,48},{48,0},{64,80},{80,96},{96,112},{112,64},{1... | collective-permute-start | bytes 589832 | tf_op jit(solution)/shard_map/ppermute | solution.py:364
  59.4 8.9 %collective-permute-start.14 = (bf16[3,128,256]{2,1,0:T(8,128)(2,1)S(1)}, bf16[3,128,256]{2,1,0:T(8,128)(2,1)S(1)}, u32[]{:S(2)}, u32[]{:S(2)}) collective-permute-start(bf16[3,128,256]{2,1,0:T(8,128)(2,1)S(1)} %get-tuple-element.68), channel_id=1, source_target_pairs={{0,48},{16,0},{32,16},{48,32},{64,112},{80,64},{96,80},{112,96},{1... | collective-permute-start | bytes 589832 | tf_op jit(solution)/shard_map/ppermute | solution.py:364
  63.6 13.2 %collective-permute-start.10 = (bf16[256,512]{1,0:T(8,128)(2,1)S(1)}, bf16[256,512]{1,0:T(8,128)(2,1)S(1)}, u32[]{:S(2)}, u32[]{:S(2)}) collective-permute-start(bf16[256,512]{1,0:T(8,128)(2,1)S(1)} %get-tuple-element.64), channel_id=1, source_target_pairs={{0,12},{2,14},{4,8},{6,10},{8,4},{10,6},{12,0},{14,2},{1,13},{3,15... | collective-permute-start | bytes 786440 | tf_op jit(solution)/shard_map/ppermute | solution.py:331
  74.3 5.3 %collective-permute-start.15 = (bf16[256,512]{1,0:T(8,128)(2,1)S(1)}, bf16[256,512]{1,0:T(8,128)(2,1)S(1)}, u32[]{:S(2)}, u32[]{:S(2)}) collective-permute-start(bf16[256,512]{1,0:T(8,128)(2,1)S(1)} %get-tuple-element.70), channel_id=1, source_target_pairs={{0,4},{2,6},{4,0},{6,2},{8,12},{10,14},{12,8},{14,10},{1,5},{3,7},... | collective-permute-start | bytes 786440 | tf_op jit(solution)/shard_map/ppermute | solution.py:331
  80.3 2.4 %collective-permute-start.18 = (bf16[2,512,256]{2,1,0:T(8,128)(2,1)S(1)}, bf16[2,512,256]{2,1,0:T(8,128)(2,1)S(1)}, u32[]{:S(2)}, u32[]{:S(2)}) collective-permute-start(bf16[2,512,256]{2,1,0:T(8,128)(2,1)S(1)} %get-tuple-element.74), channel_id=1, source_target_pairs={{0,2},{2,0},{4,6},{6,4},{8,10},{10,8},{12,14},{14,12},{1,3},{3,1},... | collective-permute-start | bytes 1572872 | tf_op jit(solution)/shard_map/ppermute | solution.py:325
  80.4 2.3 %collective-permute-start.16 = (bf16[256,512]{1,0:T(8,128)(2,1)S(1)}, bf16[256,512]{1,0:T(8,128)(2,1)S(1)}, u32[]{:S(2)}, u32[]{:S(2)}) collective-permute-start(bf16[256,512]{1,0:T(8,128)(2,1)S(1)} %get-tuple-element.72), channel_id=1, source_target_pairs={{0,2},{2,0},{4,6},{6,4},{8,10},{10,8},{12,14},{14,12},{1,3},{3,1},... | collective-permute-start | bytes 786440 | tf_op jit(solution)/shard_map/ppermute | solution.py:325
  83.4 11.1 %collective-permute-start.19 = (bf16[3,128,256]{2,1,0:T(8,128)(2,1)S(1)}, bf16[3,128,256]{2,1,0:T(8,128)(2,1)S(1)}, u32[]{:S(2)}, u32[]{:S(2)}) collective-permute-start(bf16[3,128,256]{2,1,0:T(8,128)(2,1)S(1)} %get-tuple-element.75), channel_id=1, source_target_pairs={{0,32},{16,48},{32,0},{48,16},{64,96},{80,112},{96,64},{112,80},{1... | collective-permute-start | bytes 589832 | tf_op jit(solution)/shard_map/ppermute | solution.py:364
  87.4 9.6 %collective-permute-start.20 = (bf16[3,128,256]{2,1,0:T(8,128)(2,1)S(1)}, bf16[3,128,256]{2,1,0:T(8,128)(2,1)S(1)}, u32[]{:S(2)}, u32[]{:S(2)}) collective-permute-start(bf16[3,128,256]{2,1,0:T(8,128)(2,1)S(1)} %get-tuple-element.76), channel_id=1, source_target_pairs={{0,16},{16,32},{32,48},{48,0},{64,80},{80,96},{96,112},{112,64},{1... | collective-permute-start | bytes 589832 | tf_op jit(solution)/shard_map/ppermute | solution.py:364
  88.1 9.1 %collective-permute-start.21 = (bf16[3,128,256]{2,1,0:T(8,128)(2,1)S(1)}, bf16[3,128,256]{2,1,0:T(8,128)(2,1)S(1)}, u32[]{:S(2)}, u32[]{:S(2)}) collective-permute-start(bf16[3,128,256]{2,1,0:T(8,128)(2,1)S(1)} %get-tuple-element.77), channel_id=1, source_target_pairs={{0,48},{16,0},{32,16},{48,32},{64,112},{80,64},{96,80},{112,96},{1... | collective-permute-start | bytes 589832 | tf_op jit(solution)/shard_map/ppermute | solution.py:364
  90.0 10.7 %collective-permute-start.24 = (bf16[3,128,256]{2,1,0:T(8,128)(2,1)S(1)}, bf16[3,128,256]{2,1,0:T(8,128)(2,1)S(1)}, u32[]{:S(2)}, u32[]{:S(2)}) collective-permute-start(bf16[3,128,256]{2,1,0:T(8,128)(2,1)S(1)} %sum_over_z.2.after), channel_id=1, source_target_pairs={{0,0},{1,15},{2,64},{3,79},{4,4},{5,11},{6,68},{7,75},{8,6},{9,9},... | collective-permute-start | bytes 589832 | tf_op jit(solution)/shard_map/ppermute | solution.py:351
  93.2 9.1 %collective-permute-start.25 = (bf16[3,128,256]{2,1,0:T(8,128)(2,1)S(1)}, bf16[3,128,256]{2,1,0:T(8,128)(2,1)S(1)}, u32[]{:S(2)}, u32[]{:S(2)}) collective-permute-start(bf16[3,128,256]{2,1,0:T(8,128)(2,1)S(1)} %sum_over_z.2.after), channel_id=1, source_target_pairs={{64,0},{65,15},{66,64},{67,79},{68,4},{69,11},{70,68},{71,75},{72,... | collective-permute-start | bytes 589832 | tf_op jit(solution)/shard_map/ppermute | solution.py:351
  97.6 11.1 %collective-permute-start.22 = (bf16[3,128,256]{2,1,0:T(8,128)(2,1)S(1)}, bf16[3,128,256]{2,1,0:T(8,128)(2,1)S(1)}, u32[]{:S(2)}, u32[]{:S(2)}) collective-permute-start(bf16[3,128,256]{2,1,0:T(8,128)(2,1)S(1)} %sum_over_z.3), channel_id=1, source_target_pairs={{0,1},{1,14},{2,65},{3,78},{4,5},{5,10},{6,69},{7,74},{8,7},{9,8},... | collective-permute-start | bytes 589832 | tf_op jit(solution)/shard_map/ppermute | solution.py:351
  100.1 8.7 %collective-permute-start.23 = (bf16[3,128,256]{2,1,0:T(8,128)(2,1)S(1)}, bf16[3,128,256]{2,1,0:T(8,128)(2,1)S(1)}, u32[]{:S(2)}, u32[]{:S(2)}) collective-permute-start(bf16[3,128,256]{2,1,0:T(8,128)(2,1)S(1)} %sum_over_z.3), channel_id=1, source_target_pairs={{64,1},{65,14},{66,65},{67,78},{68,5},{69,10},{70,69},{71,74},{72,... | collective-permute-start | bytes 589832 | tf_op jit(solution)/shard_map/ppermute | solution.py:351

commit v13 on v12

--- a/solution.py
+++ b/solution.py
@@ -176,7 +176,7 @@
 
 
 def both_second_kernel(own_a, got_a, own_b, got_b, gta_ref, gtb_ref, after, sent_out, kept_out):
-    for s, flip in enumerate((3, 2, 0, 1)):
+    for s, flip in enumerate((1, 2, 0, 3)):
         put(s, half_block(flip, 1, (own_a, got_a, own_b, got_b), (gta_ref, gtb_ref), sent_out.shape[2]), sent_out, kept_out)
 
 
@@ -396,13 +396,13 @@
     sent, kept11 = call(
         both_second_kernel, "fisher_of_other_grads", [pair_shape, kept_shape], [], [*xs, gt_own, gt_got, w0[0]]
     )
-    swap11 = swap_x(3, sent)
+    swap11 = swap_x(1, sent)
 
     own0, other0 = join_direct(sum0, got0, kept11)
     words0 = weigh(0, own0, other0, w0, own0)
     part10 = middle(3, swap10, kept10, words0[3])
     first = call(sum_kernel, "sum_over_z", words, [], [*words0, part10[0]])
-    part11 = middle(1, swap11, kept11, first)
+    part11 = middle(3, swap11, kept11, first)
     own1, other1 = join(settle(part10, part11[0]), part11, first)
     w1 = bring_weights(1, own1)
     words1 = weigh(1, own1, other1, w1, w1[0])

time: 110 us -> 109 us (level)
  starting transfers between devices: 42.1 us -> 39.2 us
    ppermute x7, starting transfers between devices: 8.81 us -> 5.64 us  [swap_x(): return lax.ppermute(sent, 'tok', x_pairs(flip))]
    ppermute x6, starting transfers between devices: 6.5 us -> 8.21 us  [swap_cores(): return lax.ppermute(send, 'tok', [(t, t ^ 1) for t in range(8)])]
    ppermute x6, starting transfers between devices: 13 us -> 11.6 us  [weigh(): return [lax.ppermute(v, 'member', z_pairs(d)) for d, v in send] + [own_sums]]
  transfers between devices with their start and end apart: 26 -> 26, of which waited for: 14 -> 12; matrix products, arithmetic and copies ran while one was open for 0% -> 0% of each run, Pallas kernels for 18% -> 18%
where the time goes in v13:
time: 109 us; the launch traced here: 108 us
  waiting for transfers between devices  45.3 us (42%)
  starting transfers between devices  39.2 us (36%)
  Pallas kernels  23 us (21%)
    pallas_call x21, Pallas kernels, call(): pl.pallas_call(kernel, out_shape=shapes, in_specs=[HBM] * len(hbm) + [VME...  22.1 us
    ppermute x7, waiting for transfers between devices, swap_x(): return lax.ppermute(sent, 'tok', x_pairs(flip))  16.9 us
    ppermute x6, starting transfers between devices, weigh(): return [lax.ppermute(v, 'member', z_pairs(d)) for d, v in send] + [own_sums]  11.6 us
    ppermute x6, waiting for transfers between devices, weigh(): return [lax.ppermute(v, 'member', z_pairs(d)) for d, v in send] + [own_sums]  8.81 us
    ppermute x1, waiting for transfers between devices, swap_cols(): return lax.ppermute(send, 'col', [(0, 1), (1, 0)])  8.51 us
    ppermute x6, starting transfers between devices, swap_cores(): return lax.ppermute(send, 'tok', [(t, t ^ 1) for t in range(8)])  8.21 us
    ppermute x4, waiting for transfers between devices, results(): lax.ppermute(sums, ('member', 'tok', 'col'), result_pairs(phase, y_lo))  8.05 us
    ppermute x4, starting transfers between devices, results(): lax.ppermute(sums, ('member', 'tok', 'col'), result_pairs(phase, y_lo))  7.56 us
  transfers between devices with their start and end apart: 26, of which 12 were waited for; matrix products, arithmetic and copies ran while one was open for 0% of the time, Pallas kernels for 18%

profile of v13, /device:TPU:1, one launch (start us, length us, event | category | flops | bytes accessed | tf_op | source)
XLA Modules:
  0.0 107.7 jit_solution(5468528147938304762)
XLA Ops:
  0.0 2.0 %load_to_swap.2.after = bf16[768,2304]{1,0:T(8,128)(2,1)S(1)} custom-call(bf16[2,768,4096]{2,1,0:T(8,128)(2,1)} %x_ref.7, bf16[2,768,256]{2,1,0:T(8,128)(2,1)} %g_ref.3), custom_call_target="tpu_custom_call" | custom-call | flops 1 | bytes 1 | tf_op jit(solution)/shard_map/load_to_swap/pallas_call | solution.py:66
  2.1 1.5 %collective-permute-start = (bf16[768,2304]{1,0:T(8,128)(2,1)S(1)}, bf16[768,2304]{1,0:T(8,128)(2,1)S(1)}, u32[]{:S(2)}, u32[]{:S(2)}) collective-permute-start(bf16[768,2304]{1,0:T(8,128)(2,1)S(1)} %load_to_swap.2.after), channel_id=1, source_target_pairs={{0,2},{2,0},{4,6},{6,4},{8,10},{10,8},{12,14},{14,12},{1,3},{3,1},... | collective-permute-start | bytes 10616840 | tf_op jit(solution)/shard_map/ppermute | solution.py:325
  3.6 1.9 %load_to_swap.3.after = bf16[768,2048]{1,0:T(8,128)(2,1)S(1)} custom-call(bf16[2,768,4096]{2,1,0:T(8,128)(2,1)} %x_ref.7, bf16[768,2304]{1,0:T(8,128)(2,1)S(1)} %load_to_swap.2.after), custom_call_target="tpu_custom_call" | custom-call | flops 1 | bytes 1 | tf_op jit(solution)/shard_map/load_to_swap/pallas_call | solution.py:66
  5.7 4.8 %collective-permute-start.7 = (bf16[2,1024,256]{2,1,0:T(8,128)(2,1)S(1)}, bf16[2,1024,256]{2,1,0:T(8,128)(2,1)S(1)}, u32[]{:S(2)}, u32[]{:S(2)}) collective-permute-start(bf16[2,1024,256]{2,1,0:T(8,128)(2,1)S(1)} %copy-done), channel_id=1, source_target_pairs={{0,0},{2,12},{4,4},{6,8},{9,11},{11,7},{13,15},{15,3},{16,16},{18,... | collective-permute-start | bytes 3145736 | tf_op jit(solution)/shard_map/ppermute | solution.py:354
  10.5 2.9 %fisher_of_own_tokens.2 = (bf16[768,2048]{1,0:T(8,128)(2,1)S(1)}, bf16[768,256]{1,0:T(8,128)(2,1)S(1)}, bf16[256,768]{1,0:T(8,128)(2,1)S(1)}, f32[2,256,1024]{2,1,0:T(8,128)S(1)}) custom-call(bf16[2,768,4096]{2,1,0:T(8,128)(2,1)} %x_ref.7, bf16[2,768,256]{2,1,0:T(8,128)(2,1)} %g_ref.3, bf16[768,2048]{1,0:T(8,128)(2,1)S(1)} %load_to_swap.3.after), custom_call_target="tpu_custom_call" | custom-call | flops 1 | bytes 1 | tf_op jit(solution)/shard_map/fisher_of_own_tokens/pallas_call | solution.py:66
  13.5 1.3 %fisher_of_both_cores.2 = (bf16[256,1024]{1,0:T(8,128)(2,1)S(1)}, bf16[256,1024]{1,0:T(8,128)(2,1)S(1)}, bf16[256,768]{1,0:T(8,128)(2,1)S(1)}) custom-call(bf16[768,2304]{1,0:T(8,128)(2,1)S(1)} %collective-permute-done.got.x_ref.got_a, f32[2,256,1024]{2,1,0:T(8,128)S(1)} %get-tuple-element.44.part_ref, bf16[2,768,256]{2,1,0:T(8,128)(2,1)S(1)} %pair_grads.1.after), custom_call_target="tpu_custom_call" | custom-call | flops 1 | bytes 1 | tf_op jit(solution)/shard_map/fisher_of_both_cores/pallas_call | solution.py:66
  14.8 0.8 collective-permute-start.4
  15.6 3.3 %collective-permute-start.5 = (bf16[256,1024]{1,0:T(8,128)(2,1)S(1)}, bf16[256,1024]{1,0:T(8,128)(2,1)S(1)}, u32[]{:S(2)}, u32[]{:S(2)}) collective-permute-start(bf16[256,1024]{1,0:T(8,128)(2,1)S(1)} %get-tuple-element.46.after), channel_id=1, source_target_pairs={{0,8},{2,10},{4,12},{6,14},{8,0},{10,2},{12,4},{14,6},{1,9},{3,11}... | collective-permute-start | bytes 1572872 | tf_op jit(solution)/shard_map/ppermute | solution.py:331
  18.8 2.6 %fisher_of_own_tokens.3 = (bf16[768,2048]{1,0:T(8,128)(2,1)S(1)}, f32[2,256,1024]{2,1,0:T(8,128)S(1)}) custom-call(bf16[2,768,4096]{2,1,0:T(8,128)(2,1)} %x_ref.7, bf16[256,768]{1,0:T(8,128)(2,1)S(1)} %get-tuple-element.43.after.gt_ref, bf16[256,1024]{1,0:T(8,128)(2,1)S(1)} %get-tuple-element.46.after), custom_call_target="tpu_custom_call" | custom-call | flops 1 | bytes 1 | tf_op jit(solution)/shard_map/fisher_of_own_tokens/pallas_call | solution.py:66
  21.4 1.1 %fisher_of_both_cores.3 = (bf16[256,1024]{1,0:T(8,128)(2,1)S(1)}, f32[256,1024]{1,0:T(8,128)S(1)}) custom-call(bf16[768,2048]{1,0:T(8,128)(2,1)S(1)} %collective-permute-done.1.x_ref.got_b, bf16[256,768]{1,0:T(8,128)(2,1)S(1)} %get-tuple-element.48.gt_ref, f32[2,256,1024]{2,1,0:T(8,128)S(1)} %get-tuple-element.49.part_ref, ...), custom_call_target="tpu_custom_call" | custom-call | flops 1 | bytes 1 | tf_op jit(solution)/shard_map/fisher_of_both_cores/pallas_call | solution.py:66
  22.6 8.5 %collective-permute-done.2.g_ref = bf16[2,768,256]{2,1,0:T(8,128)(2,1)S(1)} collective-permute-done((bf16[2,768,256]{2,1,0:T(8,128)(2,1)S(1)}, bf16[2,768,256]{2,1,0:T(8,128)(2,1)S(1)}, u32[]{:S(2)}, u32[]{:S(2)}) %collective-permute-start.2) | collective-permute-done | bytes 786464 | tf_op jit(solution)/shard_map/ppermute | solution.py:328
  31.2 1.3 %collective-permute-start.17 = (bf16[2,1024,256]{2,1,0:T(8,128)(2,1)S(1)}, bf16[2,1024,256]{2,1,0:T(8,128)(2,1)S(1)}, u32[]{:S(2)}, u32[]{:S(2)}) collective-permute-start(bf16[2,1024,256]{2,1,0:T(8,128)(2,1)S(1)} %copy-done), channel_id=1, source_target_pairs={{1,2},{3,14},{5,6},{7,10},{8,9},{10,5},{12,13},{14,1},{17,18},{19,... | collective-permute-start | bytes 3145736 | tf_op jit(solution)/shard_map/ppermute | solution.py:354
  32.4 1.9 %fisher_of_other_grads.2 = (bf16[2,256,512]{2,1,0:T(8,128)(2,1)S(1)}, f32[2,256,512]{2,1,0:T(8,128)S(1)}, bf16[256,768]{1,0:T(8,128)(2,1)S(1)}, bf16[256,768]{1,0:T(8,128)(2,1)S(1)}) custom-call(bf16[768,2048]{1,0:T(8,128)(2,1)S(1)} %get-tuple-element.42.own_a, bf16[768,2304]{1,0:T(8,128)(2,1)S(1)} %collective-permute-done.got.x_ref.got_a, ...), custom_call_target="tpu_custom_call" | custom-call | flops 1 | bytes 1 | tf_op jit(solution)/shard_map/fisher_of_other_grads/pallas_call | solution.py:66
  34.6 1.4 %collective-permute-start.3 = (bf16[2,256,512]{2,1,0:T(8,128)(2,1)S(1)}, bf16[2,256,512]{2,1,0:T(8,128)(2,1)S(1)}, u32[]{:S(2)}, u32[]{:S(2)}) collective-permute-start(bf16[2,256,512]{2,1,0:T(8,128)(2,1)S(1)} %get-tuple-element.52), channel_id=1, source_target_pairs={{0,4},{2,6},{4,0},{6,2},{8,12},{10,14},{12,8},{14,10},{1,5},{3,7},... | collective-permute-start | bytes 1572872 | tf_op jit(solution)/shard_map/ppermute | solution.py:331
  36.0 1.9 %fisher_of_other_grads.3 = (bf16[2,256,512]{2,1,0:T(8,128)(2,1)S(1)}, f32[2,256,512]{2,1,0:T(8,128)S(1)}) custom-call(bf16[768,2048]{1,0:T(8,128)(2,1)S(1)} %get-tuple-element.42.own_a, bf16[768,2304]{1,0:T(8,128)(2,1)S(1)} %collective-permute-done.got.x_ref.got_a, bf16[768,2048]{1,0:T(8,128)(2,1)S(1)} %get-tuple-element.47.after.own_b, ...), custom_call_target="tpu_custom_call" | custom-call | flops 1 | bytes 1 | tf_op jit(solution)/shard_map/fisher_of_other_grads/pallas_call | solution.py:66
  37.8 3.6 %collective-permute-done.5.two = bf16[256,1024]{1,0:T(8,128)(2,1)S(1)} collective-permute-done((bf16[256,1024]{1,0:T(8,128)(2,1)S(1)}, bf16[256,1024]{1,0:T(8,128)(2,1)S(1)}, u32[]{:S(2)}, u32[]{:S(2)}) %collective-permute-start.5) | collective-permute-done | bytes 524320 | tf_op jit(solution)/shard_map/ppermute | solution.py:331
  41.5 5.7 %collective-permute-done.6.three = bf16[256,1024]{1,0:T(8,128)(2,1)S(1)} collective-permute-done((bf16[256,1024]{1,0:T(8,128)(2,1)S(1)}, bf16[256,1024]{1,0:T(8,128)(2,1)S(1)}, u32[]{:S(2)}, u32[]{:S(2)}) %collective-permute-start.6) | collective-permute-done | bytes 524320 | tf_op jit(solution)/shard_map/ppermute | solution.py:331
  47.3 1.6 %fisher_over_tokens.3 = (f32[256,512]{1,0:T(8,128)S(1)}, bf16[256,512]{1,0:T(8,128)(2,1)S(1)}) custom-call(f32[256,1024]{1,0:T(8,128)S(1)} %get-tuple-element.53.own, bf16[256,1024]{1,0:T(8,128)(2,1)S(1)} %collective-permute-done.4.one, bf16[256,1024]{1,0:T(8,128)(2,1)S(1)} %collective-permute-done.5.two, ...), custom_call_target="tpu_custom_call" | custom-call | flops 1 | bytes 1 | tf_op jit(solution)/shard_map/fisher_over_tokens/pallas_call | solution.py:66
  48.9 4.1 %collective-permute-start.8 = (bf16[256,512]{1,0:T(8,128)(2,1)S(1)}, bf16[256,512]{1,0:T(8,128)(2,1)S(1)}, u32[]{:S(2)}, u32[]{:S(2)}) collective-permute-start(bf16[256,512]{1,0:T(8,128)(2,1)S(1)} %get-tuple-element.60), channel_id=1, source_target_pairs={{0,2},{2,0},{4,6},{6,4},{8,10},{10,8},{12,14},{14,12},{1,3},{3,1},... | collective-permute-start | bytes 786440 | tf_op jit(solution)/shard_map/ppermute | solution.py:325
  53.1 1.2 %collective-permute-done.8.refs_1_ = bf16[256,512]{1,0:T(8,128)(2,1)S(1)} collective-permute-done((bf16[256,512]{1,0:T(8,128)(2,1)S(1)}, bf16[256,512]{1,0:T(8,128)(2,1)S(1)}, u32[]{:S(2)}, u32[]{:S(2)}) %collective-permute-start.8) | collective-permute-done | bytes 262176 | tf_op jit(solution)/shard_map/ppermute | solution.py:325
  54.2 0.7 weigh_members.2
  55.0 3.7 %collective-permute-start.12 = (bf16[3,128,256]{2,1,0:T(8,128)(2,1)S(1)}, bf16[3,128,256]{2,1,0:T(8,128)(2,1)S(1)}, u32[]{:S(2)}, u32[]{:S(2)}) collective-permute-start(bf16[3,128,256]{2,1,0:T(8,128)(2,1)S(1)} %get-tuple-element.66), channel_id=1, source_target_pairs={{0,32},{16,48},{32,0},{48,16},{64,96},{80,112},{96,64},{112,80},{1... | collective-permute-start | bytes 589832 | tf_op jit(solution)/shard_map/ppermute | solution.py:364
  58.7 0.7 collective-permute-start.13
  59.4 1.9 %collective-permute-start.14 = (bf16[3,128,256]{2,1,0:T(8,128)(2,1)S(1)}, bf16[3,128,256]{2,1,0:T(8,128)(2,1)S(1)}, u32[]{:S(2)}, u32[]{:S(2)}) collective-permute-start(bf16[3,128,256]{2,1,0:T(8,128)(2,1)S(1)} %get-tuple-element.68), channel_id=1, source_target_pairs={{0,48},{16,0},{32,16},{48,32},{64,112},{80,64},{96,80},{112,96},{1... | collective-permute-start | bytes 589832 | tf_op jit(solution)/shard_map/ppermute | solution.py:364
  61.3 0.7 fisher_over_first_swap.2
  62.1 1.6 %collective-permute-done.12.one = bf16[3,128,256]{2,1,0:T(8,128)(2,1)S(1)} collective-permute-done((bf16[3,128,256]{2,1,0:T(8,128)(2,1)S(1)}, bf16[3,128,256]{2,1,0:T(8,128)(2,1)S(1)}, u32[]{:S(2)}, u32[]{:S(2)}) %collective-permute-start.12) | collective-permute-done | bytes 196640 | tf_op jit(solution)/shard_map/ppermute | solution.py:364
  63.6 4.6 %collective-permute-done.13.two = bf16[3,128,256]{2,1,0:T(8,128)(2,1)S(1)} collective-permute-done((bf16[3,128,256]{2,1,0:T(8,128)(2,1)S(1)}, bf16[3,128,256]{2,1,0:T(8,128)(2,1)S(1)}, u32[]{:S(2)}, u32[]{:S(2)}) %collective-permute-start.13) | collective-permute-done | bytes 196640 | tf_op jit(solution)/shard_map/ppermute | solution.py:364
  68.2 0.3 sum_over_z.2.after
  68.6 0.7 fisher_over_first_swap.3
  69.4 1.8 %collective-permute-done.10.got = bf16[256,512]{1,0:T(8,128)(2,1)S(1)} collective-permute-done((bf16[256,512]{1,0:T(8,128)(2,1)S(1)}, bf16[256,512]{1,0:T(8,128)(2,1)S(1)}, u32[]{:S(2)}, u32[]{:S(2)}) %collective-permute-start.10) | collective-permute-done | bytes 262176 | tf_op jit(solution)/shard_map/ppermute | solution.py:331
  71.3 0.3 fisher_over_tokens.4.first_ref
  71.6 5.7 %collective-permute-done.15.got = bf16[256,512]{1,0:T(8,128)(2,1)S(1)} collective-permute-done((bf16[256,512]{1,0:T(8,128)(2,1)S(1)}, bf16[256,512]{1,0:T(8,128)(2,1)S(1)}, u32[]{:S(2)}, u32[]{:S(2)}) %collective-permute-start.15) | collective-permute-done | bytes 262176 | tf_op jit(solution)/shard_map/ppermute | solution.py:331
  77.2 0.6 fisher_over_tokens.5
  78.0 2.2 %collective-permute-start.18 = (bf16[2,512,256]{2,1,0:T(8,128)(2,1)S(1)}, bf16[2,512,256]{2,1,0:T(8,128)(2,1)S(1)}, u32[]{:S(2)}, u32[]{:S(2)}) collective-permute-start(bf16[2,512,256]{2,1,0:T(8,128)(2,1)S(1)} %get-tuple-element.74), channel_id=1, source_target_pairs={{0,2},{2,0},{4,6},{6,4},{8,10},{10,8},{12,14},{14,12},{1,3},{3,1},... | collective-permute-start | bytes 1572872 | tf_op jit(solution)/shard_map/ppermute | solution.py:325
  80.2 1.8 %collective-permute-done.16.refs_1_ = bf16[256,512]{1,0:T(8,128)(2,1)S(1)} collective-permute-done((bf16[256,512]{1,0:T(8,128)(2,1)S(1)}, bf16[256,512]{1,0:T(8,128)(2,1)S(1)}, u32[]{:S(2)}, u32[]{:S(2)}) %collective-permute-start.16) | collective-permute-done | bytes 262176 | tf_op jit(solution)/shard_map/ppermute | solution.py:325
  82.1 0.7 weigh_members.3
  82.8 2.6 %collective-permute-start.19 = (bf16[3,128,256]{2,1,0:T(8,128)(2,1)S(1)}, bf16[3,128,256]{2,1,0:T(8,128)(2,1)S(1)}, u32[]{:S(2)}, u32[]{:S(2)}) collective-permute-start(bf16[3,128,256]{2,1,0:T(8,128)(2,1)S(1)} %get-tuple-element.75), channel_id=1, source_target_pairs={{0,32},{16,48},{32,0},{48,16},{64,96},{80,112},{96,64},{112,80},{1... | collective-permute-start | bytes 589832 | tf_op jit(solution)/shard_map/ppermute | solution.py:364
  85.4 1.2 %collective-permute-start.20 = (bf16[3,128,256]{2,1,0:T(8,128)(2,1)S(1)}, bf16[3,128,256]{2,1,0:T(8,128)(2,1)S(1)}, u32[]{:S(2)}, u32[]{:S(2)}) collective-permute-start(bf16[3,128,256]{2,1,0:T(8,128)(2,1)S(1)} %get-tuple-element.76), channel_id=1, source_target_pairs={{0,16},{16,32},{32,48},{48,0},{64,80},{80,96},{96,112},{112,64},{1... | collective-permute-start | bytes 589832 | tf_op jit(solution)/shard_map/ppermute | solution.py:364
  86.6 1.5 %collective-permute-start.21 = (bf16[3,128,256]{2,1,0:T(8,128)(2,1)S(1)}, bf16[3,128,256]{2,1,0:T(8,128)(2,1)S(1)}, u32[]{:S(2)}, u32[]{:S(2)}) collective-permute-start(bf16[3,128,256]{2,1,0:T(8,128)(2,1)S(1)} %get-tuple-element.77), channel_id=1, source_target_pairs={{0,48},{16,0},{32,16},{48,32},{64,112},{80,64},{96,80},{112,96},{1... | collective-permute-start | bytes 589832 | tf_op jit(solution)/shard_map/ppermute | solution.py:364
  88.1 3.4 %collective-permute-start.24 = (bf16[3,128,256]{2,1,0:T(8,128)(2,1)S(1)}, bf16[3,128,256]{2,1,0:T(8,128)(2,1)S(1)}, u32[]{:S(2)}, u32[]{:S(2)}) collective-permute-start(bf16[3,128,256]{2,1,0:T(8,128)(2,1)S(1)} %sum_over_z.2.after), channel_id=1, source_target_pairs={{0,0},{1,15},{2,64},{3,79},{4,4},{5,11},{6,68},{7,75},{8,6},{9,9},... | collective-permute-start | bytes 589832 | tf_op jit(solution)/shard_map/ppermute | solution.py:351
  91.5 1.3 %collective-permute-start.25 = (bf16[3,128,256]{2,1,0:T(8,128)(2,1)S(1)}, bf16[3,128,256]{2,1,0:T(8,128)(2,1)S(1)}, u32[]{:S(2)}, u32[]{:S(2)}) collective-permute-start(bf16[3,128,256]{2,1,0:T(8,128)(2,1)S(1)} %sum_over_z.2.after), channel_id=1, source_target_pairs={{64,0},{65,15},{66,64},{67,79},{68,4},{69,11},{70,68},{71,75},{72,... | collective-permute-start | bytes 589832 | tf_op jit(solution)/shard_map/ppermute | solution.py:351
  92.8 2.6 %collective-permute-done.20.two = bf16[3,128,256]{2,1,0:T(8,128)(2,1)S(1)} collective-permute-done((bf16[3,128,256]{2,1,0:T(8,128)(2,1)S(1)}, bf16[3,128,256]{2,1,0:T(8,128)(2,1)S(1)}, u32[]{:S(2)}, u32[]{:S(2)}) %collective-permute-start.20) | collective-permute-done | bytes 196640 | tf_op jit(solution)/shard_map/ppermute | solution.py:364
  95.4 0.3 sum_over_z.3
  95.8 2.2 %collective-permute-start.22 = (bf16[3,128,256]{2,1,0:T(8,128)(2,1)S(1)}, bf16[3,128,256]{2,1,0:T(8,128)(2,1)S(1)}, u32[]{:S(2)}, u32[]{:S(2)}) collective-permute-start(bf16[3,128,256]{2,1,0:T(8,128)(2,1)S(1)} %sum_over_z.3), channel_id=1, source_target_pairs={{0,1},{1,14},{2,65},{3,78},{4,5},{5,10},{6,69},{7,74},{8,7},{9,8},... | collective-permute-start | bytes 589832 | tf_op jit(solution)/shard_map/ppermute | solution.py:351
  98.0 0.7 collective-permute-start.23
  98.7 1.9 %collective-permute-done.25.far = bf16[3,128,256]{2,1,0:T(8,128)(2,1)S(1)} collective-permute-done((bf16[3,128,256]{2,1,0:T(8,128)(2,1)S(1)}, bf16[3,128,256]{2,1,0:T(8,128)(2,1)S(1)}, u32[]{:S(2)}, u32[]{:S(2)}) %collective-permute-start.25) | collective-permute-done | bytes 196640 | tf_op jit(solution)/shard_map/ppermute | solution.py:351
  100.7 6.2 %collective-permute-done.22.near = bf16[3,128,256]{2,1,0:T(8,128)(2,1)S(1)} collective-permute-done((bf16[3,128,256]{2,1,0:T(8,128)(2,1)S(1)}, bf16[3,128,256]{2,1,0:T(8,128)(2,1)S(1)}, u32[]{:S(2)}, u32[]{:S(2)}) %collective-permute-start.22) | collective-permute-done | bytes 196640 | tf_op jit(solution)/shard_map/ppermute | solution.py:351
  106.9 0.8 merge_members.1
  (28 shorter events, 1.2 us)
Async XLA Ops:
  2.1 3.6 %copy-start = (bf16[2,1024,256]{2,1,0:T(8,128)(2,1)S(1)}, bf16[2,1024,256]{2,1,0:T(8,128)(2,1)}, u32[]{:S(2)}) copy-start(bf16[2,1024,256]{2,1,0:T(8,128)(2,1)} %param.5) | copy-start | bytes 3145732
  2.1 11.3 %collective-permute-start = (bf16[768,2304]{1,0:T(8,128)(2,1)S(1)}, bf16[768,2304]{1,0:T(8,128)(2,1)S(1)}, u32[]{:S(2)}, u32[]{:S(2)}) collective-permute-start(bf16[768,2304]{1,0:T(8,128)(2,1)S(1)} %load_to_swap.2.after), channel_id=1, source_target_pairs={{0,2},{2,0},{4,6},{6,4},{8,10},{10,8},{12,14},{14,12},{1,3},{3,1},... | collective-permute-start | bytes 10616840 | tf_op jit(solution)/shard_map/ppermute | solution.py:325
  5.5 15.9 %collective-permute-start.1 = (bf16[768,2048]{1,0:T(8,128)(2,1)S(1)}, bf16[768,2048]{1,0:T(8,128)(2,1)S(1)}, u32[]{:S(2)}, u32[]{:S(2)}) collective-permute-start(bf16[768,2048]{1,0:T(8,128)(2,1)S(1)} %load_to_swap.3.after), channel_id=1, source_target_pairs={{0,2},{2,0},{4,6},{6,4},{8,10},{10,8},{12,14},{14,12},{1,3},{3,1},... | collective-permute-start | bytes 9437192 | tf_op jit(solution)/shard_map/ppermute | solution.py:325
  5.7 28.7 %collective-permute-start.7 = (bf16[2,1024,256]{2,1,0:T(8,128)(2,1)S(1)}, bf16[2,1024,256]{2,1,0:T(8,128)(2,1)S(1)}, u32[]{:S(2)}, u32[]{:S(2)}) collective-permute-start(bf16[2,1024,256]{2,1,0:T(8,128)(2,1)S(1)} %copy-done), channel_id=1, source_target_pairs={{0,0},{2,12},{4,4},{6,8},{9,11},{11,7},{13,15},{15,3},{16,16},{18,... | collective-permute-start | bytes 3145736 | tf_op jit(solution)/shard_map/ppermute | solution.py:354
  13.4 17.7 %collective-permute-start.2 = (bf16[2,768,256]{2,1,0:T(8,128)(2,1)S(1)}, bf16[2,768,256]{2,1,0:T(8,128)(2,1)S(1)}, u32[]{:S(2)}, u32[]{:S(2)}) collective-permute-start(bf16[2,768,256]{2,1,0:T(8,128)(2,1)S(1)} %pair_grads.1.after), channel_id=1, source_target_pairs={{0,1},{1,0},{2,3},{3,2},{4,5},{5,4},{6,7},{7,6},{8,9},{9,8},{10,11... | collective-permute-start | bytes 2359304 | tf_op jit(solution)/shard_map/ppermute | solution.py:328
  14.8 19.8 %collective-permute-start.4 = (bf16[256,1024]{1,0:T(8,128)(2,1)S(1)}, bf16[256,1024]{1,0:T(8,128)(2,1)S(1)}, u32[]{:S(2)}, u32[]{:S(2)}) collective-permute-start(bf16[256,1024]{1,0:T(8,128)(2,1)S(1)} %get-tuple-element.54), channel_id=1, source_target_pairs={{0,4},{2,6},{4,0},{6,2},{8,12},{10,14},{12,8},{14,10},{1,5},{3,7},... | collective-permute-start | bytes 1572872 | tf_op jit(solution)/shard_map/ppermute | solution.py:331
  15.6 25.9 %collective-permute-start.5 = (bf16[256,1024]{1,0:T(8,128)(2,1)S(1)}, bf16[256,1024]{1,0:T(8,128)(2,1)S(1)}, u32[]{:S(2)}, u32[]{:S(2)}) collective-permute-start(bf16[256,1024]{1,0:T(8,128)(2,1)S(1)} %get-tuple-element.46.after), channel_id=1, source_target_pairs={{0,8},{2,10},{4,12},{6,14},{8,0},{10,2},{12,4},{14,6},{1,9},{3,11}... | collective-permute-start | bytes 1572872 | tf_op jit(solution)/shard_map/ppermute | solution.py:331
  22.6 24.7 %collective-permute-start.6 = (bf16[256,1024]{1,0:T(8,128)(2,1)S(1)}, bf16[256,1024]{1,0:T(8,128)(2,1)S(1)}, u32[]{:S(2)}, u32[]{:S(2)}) collective-permute-start(bf16[256,1024]{1,0:T(8,128)(2,1)S(1)} %get-tuple-element.50.after), channel_id=1, source_target_pairs={{0,12},{2,14},{4,8},{6,10},{8,4},{10,6},{12,0},{14,2},{1,13},{3,15... | collective-permute-start | bytes 1572872 | tf_op jit(solution)/shard_map/ppermute | solution.py:331
  31.2 46.7 %collective-permute-start.17 = (bf16[2,1024,256]{2,1,0:T(8,128)(2,1)S(1)}, bf16[2,1024,256]{2,1,0:T(8,128)(2,1)S(1)}, u32[]{:S(2)}, u32[]{:S(2)}) collective-permute-start(bf16[2,1024,256]{2,1,0:T(8,128)(2,1)S(1)} %copy-done), channel_id=1, source_target_pairs={{1,2},{3,14},{5,6},{7,10},{8,9},{10,5},{12,13},{14,1},{17,18},{19,... | collective-permute-start | bytes 3145736 | tf_op jit(solution)/shard_map/ppermute | solution.py:354
  34.5 19.8 %collective-permute-start.9 = (bf16[2,512,256]{2,1,0:T(8,128)(2,1)S(1)}, bf16[2,512,256]{2,1,0:T(8,128)(2,1)S(1)}, u32[]{:S(2)}, u32[]{:S(2)}) collective-permute-start(bf16[2,512,256]{2,1,0:T(8,128)(2,1)S(1)} %get-tuple-element.61), channel_id=1, source_target_pairs={{0,2},{2,0},{4,6},{6,4},{8,10},{10,8},{12,14},{14,12},{1,3},{3,1},... | collective-permute-start | bytes 1572872 | tf_op jit(solution)/shard_map/ppermute | solution.py:325
  34.6 24.8 %collective-permute-start.3 = (bf16[2,256,512]{2,1,0:T(8,128)(2,1)S(1)}, bf16[2,256,512]{2,1,0:T(8,128)(2,1)S(1)}, u32[]{:S(2)}, u32[]{:S(2)}) collective-permute-start(bf16[2,256,512]{2,1,0:T(8,128)(2,1)S(1)} %get-tuple-element.52), channel_id=1, source_target_pairs={{0,4},{2,6},{4,0},{6,2},{8,12},{10,14},{12,8},{14,10},{1,5},{3,7},... | collective-permute-start | bytes 1572872 | tf_op jit(solution)/shard_map/ppermute | solution.py:331
  41.4 27.2 %collective-permute-start.11 = (bf16[2,256,512]{2,1,0:T(8,128)(2,1)S(1)}, bf16[2,256,512]{2,1,0:T(8,128)(2,1)S(1)}, u32[]{:S(2)}, u32[]{:S(2)}) collective-permute-start(bf16[2,256,512]{2,1,0:T(8,128)(2,1)S(1)} %get-tuple-element.65), channel_id=1, source_target_pairs={{0,4},{2,6},{4,0},{6,2},{8,12},{10,14},{12,8},{14,10},{1,5},{3,7},... | collective-permute-start | bytes 1572872 | tf_op jit(solution)/shard_map/ppermute | solution.py:331
  48.9 5.3 %collective-permute-start.8 = (bf16[256,512]{1,0:T(8,128)(2,1)S(1)}, bf16[256,512]{1,0:T(8,128)(2,1)S(1)}, u32[]{:S(2)}, u32[]{:S(2)}) collective-permute-start(bf16[256,512]{1,0:T(8,128)(2,1)S(1)} %get-tuple-element.60), channel_id=1, source_target_pairs={{0,2},{2,0},{4,6},{6,4},{8,10},{10,8},{12,14},{14,12},{1,3},{3,1},... | collective-permute-start | bytes 786440 | tf_op jit(solution)/shard_map/ppermute | solution.py:325
  55.0 8.7 %collective-permute-start.12 = (bf16[3,128,256]{2,1,0:T(8,128)(2,1)S(1)}, bf16[3,128,256]{2,1,0:T(8,128)(2,1)S(1)}, u32[]{:S(2)}, u32[]{:S(2)}) collective-permute-start(bf16[3,128,256]{2,1,0:T(8,128)(2,1)S(1)} %get-tuple-element.66), channel_id=1, source_target_pairs={{0,32},{16,48},{32,0},{48,16},{64,96},{80,112},{96,64},{112,80},{1... | collective-permute-start | bytes 589832 | tf_op jit(solution)/shard_map/ppermute | solution.py:364
  58.7 9.6 %collective-permute-start.13 = (bf16[3,128,256]{2,1,0:T(8,128)(2,1)S(1)}, bf16[3,128,256]{2,1,0:T(8,128)(2,1)S(1)}, u32[]{:S(2)}, u32[]{:S(2)}) collective-permute-start(bf16[3,128,256]{2,1,0:T(8,128)(2,1)S(1)} %get-tuple-element.67), channel_id=1, source_target_pairs={{0,16},{16,32},{32,48},{48,0},{64,80},{80,96},{96,112},{112,64},{1... | collective-permute-start | bytes 589832 | tf_op jit(solution)/shard_map/ppermute | solution.py:364
  59.4 8.9 %collective-permute-start.14 = (bf16[3,128,256]{2,1,0:T(8,128)(2,1)S(1)}, bf16[3,128,256]{2,1,0:T(8,128)(2,1)S(1)}, u32[]{:S(2)}, u32[]{:S(2)}) collective-permute-start(bf16[3,128,256]{2,1,0:T(8,128)(2,1)S(1)} %get-tuple-element.68), channel_id=1, source_target_pairs={{0,48},{16,0},{32,16},{48,32},{64,112},{80,64},{96,80},{112,96},{1... | collective-permute-start | bytes 589832 | tf_op jit(solution)/shard_map/ppermute | solution.py:364
  63.6 7.6 %collective-permute-start.10 = (bf16[256,512]{1,0:T(8,128)(2,1)S(1)}, bf16[256,512]{1,0:T(8,128)(2,1)S(1)}, u32[]{:S(2)}, u32[]{:S(2)}) collective-permute-start(bf16[256,512]{1,0:T(8,128)(2,1)S(1)} %get-tuple-element.64), channel_id=1, source_target_pairs={{0,12},{2,14},{4,8},{6,10},{8,4},{10,6},{12,0},{14,2},{1,13},{3,15... | collective-permute-start | bytes 786440 | tf_op jit(solution)/shard_map/ppermute | solution.py:331
  69.4 7.9 %collective-permute-start.15 = (bf16[256,512]{1,0:T(8,128)(2,1)S(1)}, bf16[256,512]{1,0:T(8,128)(2,1)S(1)}, u32[]{:S(2)}, u32[]{:S(2)}) collective-permute-start(bf16[256,512]{1,0:T(8,128)(2,1)S(1)} %get-tuple-element.70), channel_id=1, source_target_pairs={{0,12},{2,14},{4,8},{6,10},{8,4},{10,6},{12,0},{14,2},{1,13},{3,15... | collective-permute-start | bytes 786440 | tf_op jit(solution)/shard_map/ppermute | solution.py:331
  78.0 4.1 %collective-permute-start.18 = (bf16[2,512,256]{2,1,0:T(8,128)(2,1)S(1)}, bf16[2,512,256]{2,1,0:T(8,128)(2,1)S(1)}, u32[]{:S(2)}, u32[]{:S(2)}) collective-permute-start(bf16[2,512,256]{2,1,0:T(8,128)(2,1)S(1)} %get-tuple-element.74), channel_id=1, source_target_pairs={{0,2},{2,0},{4,6},{6,4},{8,10},{10,8},{12,14},{14,12},{1,3},{3,1},... | collective-permute-start | bytes 1572872 | tf_op jit(solution)/shard_map/ppermute | solution.py:325
  80.2 1.9 %collective-permute-start.16 = (bf16[256,512]{1,0:T(8,128)(2,1)S(1)}, bf16[256,512]{1,0:T(8,128)(2,1)S(1)}, u32[]{:S(2)}, u32[]{:S(2)}) collective-permute-start(bf16[256,512]{1,0:T(8,128)(2,1)S(1)} %get-tuple-element.72), channel_id=1, source_target_pairs={{0,2},{2,0},{4,6},{6,4},{8,10},{10,8},{12,14},{14,12},{1,3},{3,1},... | collective-permute-start | bytes 786440 | tf_op jit(solution)/shard_map/ppermute | solution.py:325
  82.8 10.0 %collective-permute-start.19 = (bf16[3,128,256]{2,1,0:T(8,128)(2,1)S(1)}, bf16[3,128,256]{2,1,0:T(8,128)(2,1)S(1)}, u32[]{:S(2)}, u32[]{:S(2)}) collective-permute-start(bf16[3,128,256]{2,1,0:T(8,128)(2,1)S(1)} %get-tuple-element.75), channel_id=1, source_target_pairs={{0,32},{16,48},{32,0},{48,16},{64,96},{80,112},{96,64},{112,80},{1... | collective-permute-start | bytes 589832 | tf_op jit(solution)/shard_map/ppermute | solution.py:364
  85.4 10.0 %collective-permute-start.20 = (bf16[3,128,256]{2,1,0:T(8,128)(2,1)S(1)}, bf16[3,128,256]{2,1,0:T(8,128)(2,1)S(1)}, u32[]{:S(2)}, u32[]{:S(2)}) collective-permute-start(bf16[3,128,256]{2,1,0:T(8,128)(2,1)S(1)} %get-tuple-element.76), channel_id=1, source_target_pairs={{0,16},{16,32},{32,48},{48,0},{64,80},{80,96},{96,112},{112,64},{1... | collective-permute-start | bytes 589832 | tf_op jit(solution)/shard_map/ppermute | solution.py:364
  86.6 8.9 %collective-permute-start.21 = (bf16[3,128,256]{2,1,0:T(8,128)(2,1)S(1)}, bf16[3,128,256]{2,1,0:T(8,128)(2,1)S(1)}, u32[]{:S(2)}, u32[]{:S(2)}) collective-permute-start(bf16[3,128,256]{2,1,0:T(8,128)(2,1)S(1)} %get-tuple-element.77), channel_id=1, source_target_pairs={{0,48},{16,0},{32,16},{48,32},{64,112},{80,64},{96,80},{112,96},{1... | collective-permute-start | bytes 589832 | tf_op jit(solution)/shard_map/ppermute | solution.py:364
  88.1 10.6 %collective-permute-start.24 = (bf16[3,128,256]{2,1,0:T(8,128)(2,1)S(1)}, bf16[3,128,256]{2,1,0:T(8,128)(2,1)S(1)}, u32[]{:S(2)}, u32[]{:S(2)}) collective-permute-start(bf16[3,128,256]{2,1,0:T(8,128)(2,1)S(1)} %sum_over_z.2.after), channel_id=1, source_target_pairs={{0,0},{1,15},{2,64},{3,79},{4,4},{5,11},{6,68},{7,75},{8,6},{9,9},... | collective-permute-start | bytes 589832 | tf_op jit(solution)/shard_map/ppermute | solution.py:351
  91.5 9.1 %collective-permute-start.25 = (bf16[3,128,256]{2,1,0:T(8,128)(2,1)S(1)}, bf16[3,128,256]{2,1,0:T(8,128)(2,1)S(1)}, u32[]{:S(2)}, u32[]{:S(2)}) collective-permute-start(bf16[3,128,256]{2,1,0:T(8,128)(2,1)S(1)} %sum_over_z.2.after), channel_id=1, source_target_pairs={{64,0},{65,15},{66,64},{67,79},{68,4},{69,11},{70,68},{71,75},{72,... | collective-permute-start | bytes 589832 | tf_op jit(solution)/shard_map/ppermute | solution.py:351
  95.8 11.1 %collective-permute-start.22 = (bf16[3,128,256]{2,1,0:T(8,128)(2,1)S(1)}, bf16[3,128,256]{2,1,0:T(8,128)(2,1)S(1)}, u32[]{:S(2)}, u32[]{:S(2)}) collective-permute-start(bf16[3,128,256]{2,1,0:T(8,128)(2,1)S(1)} %sum_over_z.3), channel_id=1, source_target_pairs={{0,1},{1,14},{2,65},{3,78},{4,5},{5,10},{6,69},{7,74},{8,7},{9,8},... | collective-permute-start | bytes 589832 | tf_op jit(solution)/shard_map/ppermute | solution.py:351
  98.0 8.9 %collective-permute-start.23 = (bf16[3,128,256]{2,1,0:T(8,128)(2,1)S(1)}, bf16[3,128,256]{2,1,0:T(8,128)(2,1)S(1)}, u32[]{:S(2)}, u32[]{:S(2)}) collective-permute-start(bf16[3,128,256]{2,1,0:T(8,128)(2,1)S(1)} %sum_over_z.3), channel_id=1, source_target_pairs={{64,1},{65,14},{66,65},{67,78},{68,5},{69,10},{70,69},{71,74},{72,... | collective-permute-start | bytes 589832 | tf_op jit(solution)/shard_map/ppermute | solution.py:351

commit v14 on v12

--- a/solution.py
+++ b/solution.py
@@ -213,6 +213,12 @@
     core = where_am_i()[1]
     kept_out[...] = jnp.where(core == 0, halves[0], halves[1])
     sent_out[...] = encode_fine(jnp.where(core == 0, halves[1], halves[0]))
+
+
+def load_weights_kernel(w_ref, after, out, sem):
+    copy = pltpu.make_async_copy(w_ref, out, sem)
+    copy.start()
+    copy.wait()
 
 
 def split_kernel(w_ref, after, own_out, send_out):
@@ -350,8 +356,8 @@
     def results(phase, sums):
         return [lax.ppermute(sums, ("member", "tok", "col"), result_pairs(phase, y_lo)) for y_lo in range(2)]
 
-    def bring_weights(phase, after):
-        arrived = lax.ppermute(weights, ("tok", "col"), weight_pairs(phase))
+    def bring_weights(phase, source, after):
+        arrived = lax.ppermute(source, ("tok", "col"), weight_pairs(phase))
         half_shape = ((2, weights.shape[1] // 2, outs), BF16)
         own, send = call(split_kernel, "split_weights", [half_shape, half_shape], [], [arrived, after])
         return own, swap_cores(send)
@@ -392,11 +398,12 @@
         both_first_kernel, "fisher_of_other_grads", [pair_shape, kept_shape, gt_shape, gt_shape], [], [*xs, g_other, three]
     )
     swap10 = swap_x(1, sent)
-    w0 = bring_weights(0, kept10)
+    w0 = bring_weights(0, weights, kept10)
     sent, kept11 = call(
         both_second_kernel, "fisher_of_other_grads", [pair_shape, kept_shape], [], [*xs, gt_own, gt_got, w0[0]]
     )
     swap11 = swap_x(3, sent)
+    late_weights = call(load_weights_kernel, "load_weights", (weights.shape, BF16), [weights], [kept11], [dma])
 
     own0, other0 = join_direct(sum0, got0, kept11)
     words0 = weigh(0, own0, other0, w0, own0)
@@ -404,7 +411,7 @@
     first = call(sum_kernel, "sum_over_z", words, [], [*words0, part10[0]])
     part11 = middle(1, swap11, kept11, first)
     own1, other1 = join(settle(part10, part11[0]), part11, first)
-    w1 = bring_weights(1, own1)
+    w1 = bring_weights(1, late_weights, own1)
     words1 = weigh(1, own1, other1, w1, w1[0])
     met = call(meet_kernel, "meet_over_y", sums, [], [*results(0, first), own1])
     second = call(sum_kernel, "sum_over_z", words, [], [*words1, own1])

time: 110 us -> 110 us (level)
  waiting for transfers between devices: 44.2 us -> 36.5 us
  starting transfers between devices: 42.1 us -> 49 us
  Pallas kernels: 23 us -> 24.2 us
    ppermute x4, starting transfers between devices: 7.61 us -> 13.4 us  [results(): lax.ppermute(sums, ('member', 'tok', 'col'), result_pairs(phase, y_lo))]
    ppermute x4, waiting for transfers between devices: 7.81 us -> 4.49 us  [results(): lax.ppermute(sums, ('member', 'tok', 'col'), result_pairs(phase, y_lo))]
    ppermute x7, waiting for transfers between devices: 16.1 us -> 13.6 us  [swap_x(): return lax.ppermute(sent, 'tok', x_pairs(flip))]
    ppermute x6, waiting for transfers between devices: 8.89 us -> 6.93 us  [weigh(): return [lax.ppermute(v, 'member', z_pairs(d)) for d, v in send] + [own_sums]]
    pallas_call x21 -> x22, Pallas kernels: 22.1 us -> 23.4 us  [call(): pl.pallas_call(kernel, out_shape=shapes, in_specs=[HBM] * len(hbm) + [VME...]
    ppermute x7, starting transfers between devices: 8.81 us -> 9.98 us  [swap_x(): return lax.ppermute(sent, 'tok', x_pairs(flip))]
  transfers between devices with their start and end apart: 26 -> 26, of which waited for: 14 -> 13; matrix products, arithmetic and copies ran while one was open for 0% -> 0% of each run, Pallas kernels for 18% -> 19%
where the time goes in v14:
time: 110 us
  starting transfers between devices  49 us (45%)
  waiting for transfers between devices  36.5 us (33%)
  Pallas kernels  24.2 us (22%)
    pallas_call x22, Pallas kernels, call(): pl.pallas_call(kernel, out_shape=shapes, in_specs=[HBM] * len(hbm) + [VME...  23.4 us
    ppermute x7, waiting for transfers between devices, swap_x(): return lax.ppermute(sent, 'tok', x_pairs(flip))  13.6 us
    ppermute x4, starting transfers between devices, results(): lax.ppermute(sums, ('member', 'tok', 'col'), result_pairs(phase, y_lo))  13.4 us
    ppermute x6, starting transfers between devices, weigh(): return [lax.ppermute(v, 'member', z_pairs(d)) for d, v in send] + [own_sums]  13 us
    ppermute x7, starting transfers between devices, swap_x(): return lax.ppermute(sent, 'tok', x_pairs(flip))  9.98 us
    ppermute x1, waiting for transfers between devices, swap_cols(): return lax.ppermute(send, 'col', [(0, 1), (1, 0)])  8.51 us
    ppermute x6, waiting for transfers between devices, weigh(): return [lax.ppermute(v, 'member', z_pairs(d)) for d, v in send] + [own_sums]  6.93 us
    ppermute x6, starting transfers between devices, swap_cores(): return lax.ppermute(send, 'tok', [(t, t ^ 1) for t in range(8)])  6.5 us
  transfers between devices with their start and end apart: 26, of which 13 were waited for; matrix products, arithmetic and copies ran while one was open for 0% of the time, Pallas kernels for 19%

profile of v14, /device:TPU:1, one launch (start us, length us, event | category | flops | bytes accessed | tf_op | source)
XLA Modules:
  0.0 110.1 jit_solution(17200077940140991552)
XLA Ops:
  0.0 2.0 %load_to_swap.2.after = bf16[768,2304]{1,0:T(8,128)(2,1)S(1)} custom-call(bf16[2,768,4096]{2,1,0:T(8,128)(2,1)} %x_ref.7, bf16[2,768,256]{2,1,0:T(8,128)(2,1)} %g_ref.3), custom_call_target="tpu_custom_call" | custom-call | flops 1 | bytes 1 | tf_op jit(solution)/shard_map/load_to_swap/pallas_call | solution.py:66
  2.1 1.5 %collective-permute-start = (bf16[768,2304]{1,0:T(8,128)(2,1)S(1)}, bf16[768,2304]{1,0:T(8,128)(2,1)S(1)}, u32[]{:S(2)}, u32[]{:S(2)}) collective-permute-start(bf16[768,2304]{1,0:T(8,128)(2,1)S(1)} %load_to_swap.2.after), channel_id=1, source_target_pairs={{0,2},{2,0},{4,6},{6,4},{8,10},{10,8},{12,14},{14,12},{1,3},{3,1},... | collective-permute-start | bytes 10616840 | tf_op jit(solution)/shard_map/ppermute | solution.py:331
  3.6 1.9 %load_to_swap.3.after = bf16[768,2048]{1,0:T(8,128)(2,1)S(1)} custom-call(bf16[2,768,4096]{2,1,0:T(8,128)(2,1)} %x_ref.7, bf16[768,2304]{1,0:T(8,128)(2,1)S(1)} %load_to_swap.2.after), custom_call_target="tpu_custom_call" | custom-call | flops 1 | bytes 1 | tf_op jit(solution)/shard_map/load_to_swap/pallas_call | solution.py:66
  5.7 4.8 %collective-permute-start.7 = (bf16[2,1024,256]{2,1,0:T(8,128)(2,1)S(1)}, bf16[2,1024,256]{2,1,0:T(8,128)(2,1)S(1)}, u32[]{:S(2)}, u32[]{:S(2)}) collective-permute-start(bf16[2,1024,256]{2,1,0:T(8,128)(2,1)S(1)} %copy-done), channel_id=1, source_target_pairs={{0,0},{2,12},{4,4},{6,8},{9,11},{11,7},{13,15},{15,3},{16,16},{18,... | collective-permute-start | bytes 3145736 | tf_op jit(solution)/shard_map/ppermute | solution.py:360
  10.5 2.9 %fisher_of_own_tokens.2 = (bf16[768,2048]{1,0:T(8,128)(2,1)S(1)}, bf16[768,256]{1,0:T(8,128)(2,1)S(1)}, bf16[256,768]{1,0:T(8,128)(2,1)S(1)}, f32[2,256,1024]{2,1,0:T(8,128)S(1)}) custom-call(bf16[2,768,4096]{2,1,0:T(8,128)(2,1)} %x_ref.7, bf16[2,768,256]{2,1,0:T(8,128)(2,1)} %g_ref.3, bf16[768,2048]{1,0:T(8,128)(2,1)S(1)} %load_to_swap.3.after), custom_call_target="tpu_custom_call" | custom-call | flops 1 | bytes 1 | tf_op jit(solution)/shard_map/fisher_of_own_tokens/pallas_call | solution.py:66
  13.5 1.3 %fisher_of_both_cores.2 = (bf16[256,1024]{1,0:T(8,128)(2,1)S(1)}, bf16[256,1024]{1,0:T(8,128)(2,1)S(1)}, bf16[256,768]{1,0:T(8,128)(2,1)S(1)}) custom-call(bf16[768,2304]{1,0:T(8,128)(2,1)S(1)} %collective-permute-done.got.x_ref.got_a, f32[2,256,1024]{2,1,0:T(8,128)S(1)} %get-tuple-element.44.part_ref, bf16[2,768,256]{2,1,0:T(8,128)(2,1)S(1)} %pair_grads.1.after), custom_call_target="tpu_custom_call" | custom-call | flops 1 | bytes 1 | tf_op jit(solution)/shard_map/fisher_of_both_cores/pallas_call | solution.py:66
  14.8 0.8 collective-permute-start.4
  15.6 3.3 %collective-permute-start.5 = (bf16[256,1024]{1,0:T(8,128)(2,1)S(1)}, bf16[256,1024]{1,0:T(8,128)(2,1)S(1)}, u32[]{:S(2)}, u32[]{:S(2)}) collective-permute-start(bf16[256,1024]{1,0:T(8,128)(2,1)S(1)} %get-tuple-element.46.after), channel_id=1, source_target_pairs={{0,8},{2,10},{4,12},{6,14},{8,0},{10,2},{12,4},{14,6},{1,9},{3,11}... | collective-permute-start | bytes 1572872 | tf_op jit(solution)/shard_map/ppermute | solution.py:337
  18.8 2.6 %fisher_of_own_tokens.3 = (bf16[768,2048]{1,0:T(8,128)(2,1)S(1)}, f32[2,256,1024]{2,1,0:T(8,128)S(1)}) custom-call(bf16[2,768,4096]{2,1,0:T(8,128)(2,1)} %x_ref.7, bf16[256,768]{1,0:T(8,128)(2,1)S(1)} %get-tuple-element.43.after.gt_ref, bf16[256,1024]{1,0:T(8,128)(2,1)S(1)} %get-tuple-element.46.after), custom_call_target="tpu_custom_call" | custom-call | flops 1 | bytes 1 | tf_op jit(solution)/shard_map/fisher_of_own_tokens/pallas_call | solution.py:66
  21.4 1.1 %fisher_of_both_cores.3 = (bf16[256,1024]{1,0:T(8,128)(2,1)S(1)}, f32[256,1024]{1,0:T(8,128)S(1)}) custom-call(bf16[768,2048]{1,0:T(8,128)(2,1)S(1)} %collective-permute-done.1.x_ref.got_b, bf16[256,768]{1,0:T(8,128)(2,1)S(1)} %get-tuple-element.48.gt_ref, f32[2,256,1024]{2,1,0:T(8,128)S(1)} %get-tuple-element.49.part_ref, ...), custom_call_target="tpu_custom_call" | custom-call | flops 1 | bytes 1 | tf_op jit(solution)/shard_map/fisher_of_both_cores/pallas_call | solution.py:66
  22.6 8.5 %collective-permute-done.2.g_ref = bf16[2,768,256]{2,1,0:T(8,128)(2,1)S(1)} collective-permute-done((bf16[2,768,256]{2,1,0:T(8,128)(2,1)S(1)}, bf16[2,768,256]{2,1,0:T(8,128)(2,1)S(1)}, u32[]{:S(2)}, u32[]{:S(2)}) %collective-permute-start.2) | collective-permute-done | bytes 786464 | tf_op jit(solution)/shard_map/ppermute | solution.py:334
  31.2 1.9 %fisher_of_other_grads.2 = (bf16[2,256,512]{2,1,0:T(8,128)(2,1)S(1)}, f32[2,256,512]{2,1,0:T(8,128)S(1)}, bf16[256,768]{1,0:T(8,128)(2,1)S(1)}, bf16[256,768]{1,0:T(8,128)(2,1)S(1)}) custom-call(bf16[768,2048]{1,0:T(8,128)(2,1)S(1)} %get-tuple-element.42.own_a, bf16[768,2304]{1,0:T(8,128)(2,1)S(1)} %collective-permute-done.got.x_ref.got_a, ...), custom_call_target="tpu_custom_call" | custom-call | flops 1 | bytes 1 | tf_op jit(solution)/shard_map/fisher_of_other_grads/pallas_call | solution.py:66
  33.2 1.9 %fisher_of_other_grads.3 = (bf16[2,256,512]{2,1,0:T(8,128)(2,1)S(1)}, f32[2,256,512]{2,1,0:T(8,128)S(1)}) custom-call(bf16[768,2048]{1,0:T(8,128)(2,1)S(1)} %get-tuple-element.42.own_a, bf16[768,2304]{1,0:T(8,128)(2,1)S(1)} %collective-permute-done.got.x_ref.got_a, bf16[768,2048]{1,0:T(8,128)(2,1)S(1)} %get-tuple-element.47.after.own_b, ...), custom_call_target="tpu_custom_call" | custom-call | flops 1 | bytes 1 | tf_op jit(solution)/shard_map/fisher_of_other_grads/pallas_call | solution.py:66
  35.1 1.2 %load_weights.1 = bf16[2,1024,256]{2,1,0:T(8,128)(2,1)S(1)} custom-call(bf16[2,1024,256]{2,1,0:T(8,128)(2,1)} %w_ref.1, f32[2,256,512]{2,1,0:T(8,128)S(1)} %get-tuple-element.58.after.kept_ref), custom_call_target="tpu_custom_call" | custom-call | flops 1 | bytes 1 | tf_op jit(solution)/shard_map/load_weights/pallas_call | solution.py:66
  36.3 1.3 %collective-permute-start.17 = (bf16[2,1024,256]{2,1,0:T(8,128)(2,1)S(1)}, bf16[2,1024,256]{2,1,0:T(8,128)(2,1)S(1)}, u32[]{:S(2)}, u32[]{:S(2)}) collective-permute-start(bf16[2,1024,256]{2,1,0:T(8,128)(2,1)S(1)} %load_weights.1), channel_id=1, source_target_pairs={{1,2},{3,14},{5,6},{7,10},{8,9},{10,5},{12,13},{14,1},{17,18},{19,... | collective-permute-start | bytes 3145736 | tf_op jit(solution)/shard_map/ppermute | solution.py:360
  37.7 1.4 %collective-permute-start.3 = (bf16[2,256,512]{2,1,0:T(8,128)(2,1)S(1)}, bf16[2,256,512]{2,1,0:T(8,128)(2,1)S(1)}, u32[]{:S(2)}, u32[]{:S(2)}) collective-permute-start(bf16[2,256,512]{2,1,0:T(8,128)(2,1)S(1)} %get-tuple-element.52), channel_id=1, source_target_pairs={{0,4},{2,6},{4,0},{6,2},{8,12},{10,14},{12,8},{14,10},{1,5},{3,7},... | collective-permute-start | bytes 1572872 | tf_op jit(solution)/shard_map/ppermute | solution.py:337
  39.1 2.4 %collective-permute-done.5.two = bf16[256,1024]{1,0:T(8,128)(2,1)S(1)} collective-permute-done((bf16[256,1024]{1,0:T(8,128)(2,1)S(1)}, bf16[256,1024]{1,0:T(8,128)(2,1)S(1)}, u32[]{:S(2)}, u32[]{:S(2)}) %collective-permute-start.5) | collective-permute-done | bytes 524320 | tf_op jit(solution)/shard_map/ppermute | solution.py:337
  41.4 4.4 %collective-permute-start.11 = (bf16[2,256,512]{2,1,0:T(8,128)(2,1)S(1)}, bf16[2,256,512]{2,1,0:T(8,128)(2,1)S(1)}, u32[]{:S(2)}, u32[]{:S(2)}) collective-permute-start(bf16[2,256,512]{2,1,0:T(8,128)(2,1)S(1)} %get-tuple-element.65), channel_id=1, source_target_pairs={{0,12},{2,14},{4,8},{6,10},{8,4},{10,6},{12,0},{14,2},{1,13},{3,15... | collective-permute-start | bytes 1572872 | tf_op jit(solution)/shard_map/ppermute | solution.py:337
  45.9 1.4 %collective-permute-done.6.three = bf16[256,1024]{1,0:T(8,128)(2,1)S(1)} collective-permute-done((bf16[256,1024]{1,0:T(8,128)(2,1)S(1)}, bf16[256,1024]{1,0:T(8,128)(2,1)S(1)}, u32[]{:S(2)}, u32[]{:S(2)}) %collective-permute-start.6) | collective-permute-done | bytes 524320 | tf_op jit(solution)/shard_map/ppermute | solution.py:337
  47.3 1.6 %fisher_over_tokens.3 = (f32[256,512]{1,0:T(8,128)S(1)}, bf16[256,512]{1,0:T(8,128)(2,1)S(1)}) custom-call(f32[256,1024]{1,0:T(8,128)S(1)} %get-tuple-element.53.own, bf16[256,1024]{1,0:T(8,128)(2,1)S(1)} %collective-permute-done.4.one, bf16[256,1024]{1,0:T(8,128)(2,1)S(1)} %collective-permute-done.5.two, ...), custom_call_target="tpu_custom_call" | custom-call | flops 1 | bytes 1 | tf_op jit(solution)/shard_map/fisher_over_tokens/pallas_call | solution.py:66
  48.9 4.1 %collective-permute-start.8 = (bf16[256,512]{1,0:T(8,128)(2,1)S(1)}, bf16[256,512]{1,0:T(8,128)(2,1)S(1)}, u32[]{:S(2)}, u32[]{:S(2)}) collective-permute-start(bf16[256,512]{1,0:T(8,128)(2,1)S(1)} %get-tuple-element.60), channel_id=1, source_target_pairs={{0,2},{2,0},{4,6},{6,4},{8,10},{10,8},{12,14},{14,12},{1,3},{3,1},... | collective-permute-start | bytes 786440 | tf_op jit(solution)/shard_map/ppermute | solution.py:331
  53.1 1.2 %collective-permute-done.8.refs_1_ = bf16[256,512]{1,0:T(8,128)(2,1)S(1)} collective-permute-done((bf16[256,512]{1,0:T(8,128)(2,1)S(1)}, bf16[256,512]{1,0:T(8,128)(2,1)S(1)}, u32[]{:S(2)}, u32[]{:S(2)}) %collective-permute-start.8) | collective-permute-done | bytes 262176 | tf_op jit(solution)/shard_map/ppermute | solution.py:331
  54.2 0.7 weigh_members.2
  55.0 3.7 %collective-permute-start.12 = (bf16[3,128,256]{2,1,0:T(8,128)(2,1)S(1)}, bf16[3,128,256]{2,1,0:T(8,128)(2,1)S(1)}, u32[]{:S(2)}, u32[]{:S(2)}) collective-permute-start(bf16[3,128,256]{2,1,0:T(8,128)(2,1)S(1)} %get-tuple-element.66), channel_id=1, source_target_pairs={{0,32},{16,48},{32,0},{48,16},{64,96},{80,112},{96,64},{112,80},{1... | collective-permute-start | bytes 589832 | tf_op jit(solution)/shard_map/ppermute | solution.py:370
  58.7 0.7 collective-permute-start.13
  59.4 1.9 %collective-permute-start.14 = (bf16[3,128,256]{2,1,0:T(8,128)(2,1)S(1)}, bf16[3,128,256]{2,1,0:T(8,128)(2,1)S(1)}, u32[]{:S(2)}, u32[]{:S(2)}) collective-permute-start(bf16[3,128,256]{2,1,0:T(8,128)(2,1)S(1)} %get-tuple-element.68), channel_id=1, source_target_pairs={{0,48},{16,0},{32,16},{48,32},{64,112},{80,64},{96,80},{112,96},{1... | collective-permute-start | bytes 589832 | tf_op jit(solution)/shard_map/ppermute | solution.py:370
  61.3 0.7 fisher_over_first_swap.2
  62.1 1.6 %collective-permute-done.12.one = bf16[3,128,256]{2,1,0:T(8,128)(2,1)S(1)} collective-permute-done((bf16[3,128,256]{2,1,0:T(8,128)(2,1)S(1)}, bf16[3,128,256]{2,1,0:T(8,128)(2,1)S(1)}, u32[]{:S(2)}, u32[]{:S(2)}) %collective-permute-start.12) | collective-permute-done | bytes 196640 | tf_op jit(solution)/shard_map/ppermute | solution.py:370
  63.6 4.6 %collective-permute-done.13.two = bf16[3,128,256]{2,1,0:T(8,128)(2,1)S(1)} collective-permute-done((bf16[3,128,256]{2,1,0:T(8,128)(2,1)S(1)}, bf16[3,128,256]{2,1,0:T(8,128)(2,1)S(1)}, u32[]{:S(2)}, u32[]{:S(2)}) %collective-permute-start.13) | collective-permute-done | bytes 196640 | tf_op jit(solution)/shard_map/ppermute | solution.py:370
  68.2 0.3 sum_over_z.2.after
  68.6 4.9 %collective-permute-done.11.got_ref = bf16[2,256,512]{2,1,0:T(8,128)(2,1)S(1)} collective-permute-done((bf16[2,256,512]{2,1,0:T(8,128)(2,1)S(1)}, bf16[2,256,512]{2,1,0:T(8,128)(2,1)S(1)}, u32[]{:S(2)}, u32[]{:S(2)}) %collective-permute-start.11) | collective-permute-done | bytes 524320 | tf_op jit(solution)/shard_map/ppermute | solution.py:337
  73.5 0.7 fisher_over_first_swap.3
  74.4 2.4 %collective-permute-done.10.got = bf16[256,512]{1,0:T(8,128)(2,1)S(1)} collective-permute-done((bf16[256,512]{1,0:T(8,128)(2,1)S(1)}, bf16[256,512]{1,0:T(8,128)(2,1)S(1)}, u32[]{:S(2)}, u32[]{:S(2)}) %collective-permute-start.10) | collective-permute-done | bytes 262176 | tf_op jit(solution)/shard_map/ppermute | solution.py:337
  77.1 2.5 %collective-permute-done.15.got = bf16[256,512]{1,0:T(8,128)(2,1)S(1)} collective-permute-done((bf16[256,512]{1,0:T(8,128)(2,1)S(1)}, bf16[256,512]{1,0:T(8,128)(2,1)S(1)}, u32[]{:S(2)}, u32[]{:S(2)}) %collective-permute-start.15) | collective-permute-done | bytes 262176 | tf_op jit(solution)/shard_map/ppermute | solution.py:337
  79.6 0.6 fisher_over_tokens.5
  80.4 0.5 collective-permute-start.16
  80.9 1.8 %collective-permute-done.16.refs_1_ = bf16[256,512]{1,0:T(8,128)(2,1)S(1)} collective-permute-done((bf16[256,512]{1,0:T(8,128)(2,1)S(1)}, bf16[256,512]{1,0:T(8,128)(2,1)S(1)}, u32[]{:S(2)}, u32[]{:S(2)}) %collective-permute-start.16) | collective-permute-done | bytes 262176 | tf_op jit(solution)/shard_map/ppermute | solution.py:331
  82.7 0.7 weigh_members.3
  83.4 4.0 %collective-permute-start.19 = (bf16[3,128,256]{2,1,0:T(8,128)(2,1)S(1)}, bf16[3,128,256]{2,1,0:T(8,128)(2,1)S(1)}, u32[]{:S(2)}, u32[]{:S(2)}) collective-permute-start(bf16[3,128,256]{2,1,0:T(8,128)(2,1)S(1)} %get-tuple-element.75), channel_id=1, source_target_pairs={{0,32},{16,48},{32,0},{48,16},{64,96},{80,112},{96,64},{112,80},{1... | collective-permute-start | bytes 589832 | tf_op jit(solution)/shard_map/ppermute | solution.py:370
  87.4 0.8 collective-permute-start.20
  88.1 1.9 %collective-permute-start.21 = (bf16[3,128,256]{2,1,0:T(8,128)(2,1)S(1)}, bf16[3,128,256]{2,1,0:T(8,128)(2,1)S(1)}, u32[]{:S(2)}, u32[]{:S(2)}) collective-permute-start(bf16[3,128,256]{2,1,0:T(8,128)(2,1)S(1)} %get-tuple-element.77), channel_id=1, source_target_pairs={{0,48},{16,0},{32,16},{48,32},{64,112},{80,64},{96,80},{112,96},{1... | collective-permute-start | bytes 589832 | tf_op jit(solution)/shard_map/ppermute | solution.py:370
  90.0 1.3 %collective-permute-start.25 = (bf16[3,128,256]{2,1,0:T(8,128)(2,1)S(1)}, bf16[3,128,256]{2,1,0:T(8,128)(2,1)S(1)}, u32[]{:S(2)}, u32[]{:S(2)}) collective-permute-start(bf16[3,128,256]{2,1,0:T(8,128)(2,1)S(1)} %sum_over_z.2.after), channel_id=1, source_target_pairs={{64,0},{65,15},{66,64},{67,79},{68,4},{69,11},{70,68},{71,75},{72,... | collective-permute-start | bytes 589832 | tf_op jit(solution)/shard_map/ppermute | solution.py:357
  91.3 5.1 %collective-permute-start.24 = (bf16[3,128,256]{2,1,0:T(8,128)(2,1)S(1)}, bf16[3,128,256]{2,1,0:T(8,128)(2,1)S(1)}, u32[]{:S(2)}, u32[]{:S(2)}) collective-permute-start(bf16[3,128,256]{2,1,0:T(8,128)(2,1)S(1)} %sum_over_z.2.after), channel_id=1, source_target_pairs={{0,0},{1,15},{2,64},{3,79},{4,4},{5,11},{6,68},{7,75},{8,6},{9,9},... | collective-permute-start | bytes 589832 | tf_op jit(solution)/shard_map/ppermute | solution.py:357
  96.5 0.5 collective-permute-done.20.two
  97.6 0.7 collective-permute-start.23
  98.3 6.3 %collective-permute-start.22 = (bf16[3,128,256]{2,1,0:T(8,128)(2,1)S(1)}, bf16[3,128,256]{2,1,0:T(8,128)(2,1)S(1)}, u32[]{:S(2)}, u32[]{:S(2)}) collective-permute-start(bf16[3,128,256]{2,1,0:T(8,128)(2,1)S(1)} %sum_over_z.3), channel_id=1, source_target_pairs={{0,1},{1,14},{2,65},{3,78},{4,5},{5,10},{6,69},{7,74},{8,7},{9,8},... | collective-permute-start | bytes 589832 | tf_op jit(solution)/shard_map/ppermute | solution.py:357
  104.7 4.5 %collective-permute-done.22.near = bf16[3,128,256]{2,1,0:T(8,128)(2,1)S(1)} collective-permute-done((bf16[3,128,256]{2,1,0:T(8,128)(2,1)S(1)}, bf16[3,128,256]{2,1,0:T(8,128)(2,1)S(1)}, u32[]{:S(2)}, u32[]{:S(2)}) %collective-permute-start.22) | collective-permute-done | bytes 196640 | tf_op jit(solution)/shard_map/ppermute | solution.py:357
  109.2 0.8 merge_members.1
  (29 shorter events, 2.0 us)
Async XLA Ops:
  2.1 3.6 %copy-start = (bf16[2,1024,256]{2,1,0:T(8,128)(2,1)S(1)}, bf16[2,1024,256]{2,1,0:T(8,128)(2,1)}, u32[]{:S(2)}) copy-start(bf16[2,1024,256]{2,1,0:T(8,128)(2,1)} %w_ref.1) | copy-start | bytes 3145732
  2.1 11.3 %collective-permute-start = (bf16[768,2304]{1,0:T(8,128)(2,1)S(1)}, bf16[768,2304]{1,0:T(8,128)(2,1)S(1)}, u32[]{:S(2)}, u32[]{:S(2)}) collective-permute-start(bf16[768,2304]{1,0:T(8,128)(2,1)S(1)} %load_to_swap.2.after), channel_id=1, source_target_pairs={{0,2},{2,0},{4,6},{6,4},{8,10},{10,8},{12,14},{14,12},{1,3},{3,1},... | collective-permute-start | bytes 10616840 | tf_op jit(solution)/shard_map/ppermute | solution.py:331
  5.5 15.9 %collective-permute-start.1 = (bf16[768,2048]{1,0:T(8,128)(2,1)S(1)}, bf16[768,2048]{1,0:T(8,128)(2,1)S(1)}, u32[]{:S(2)}, u32[]{:S(2)}) collective-permute-start(bf16[768,2048]{1,0:T(8,128)(2,1)S(1)} %load_to_swap.3.after), channel_id=1, source_target_pairs={{0,2},{2,0},{4,6},{6,4},{8,10},{10,8},{12,14},{14,12},{1,3},{3,1},... | collective-permute-start | bytes 9437192 | tf_op jit(solution)/shard_map/ppermute | solution.py:331
  5.7 27.4 %collective-permute-start.7 = (bf16[2,1024,256]{2,1,0:T(8,128)(2,1)S(1)}, bf16[2,1024,256]{2,1,0:T(8,128)(2,1)S(1)}, u32[]{:S(2)}, u32[]{:S(2)}) collective-permute-start(bf16[2,1024,256]{2,1,0:T(8,128)(2,1)S(1)} %copy-done), channel_id=1, source_target_pairs={{0,0},{2,12},{4,4},{6,8},{9,11},{11,7},{13,15},{15,3},{16,16},{18,... | collective-permute-start | bytes 3145736 | tf_op jit(solution)/shard_map/ppermute | solution.py:360
  13.4 17.7 %collective-permute-start.2 = (bf16[2,768,256]{2,1,0:T(8,128)(2,1)S(1)}, bf16[2,768,256]{2,1,0:T(8,128)(2,1)S(1)}, u32[]{:S(2)}, u32[]{:S(2)}) collective-permute-start(bf16[2,768,256]{2,1,0:T(8,128)(2,1)S(1)} %pair_grads.1.after), channel_id=1, source_target_pairs={{0,1},{1,0},{2,3},{3,2},{4,5},{5,4},{6,7},{7,6},{8,9},{9,8},{10,11... | collective-permute-start | bytes 2359304 | tf_op jit(solution)/shard_map/ppermute | solution.py:334
  14.8 22.9 %collective-permute-start.4 = (bf16[256,1024]{1,0:T(8,128)(2,1)S(1)}, bf16[256,1024]{1,0:T(8,128)(2,1)S(1)}, u32[]{:S(2)}, u32[]{:S(2)}) collective-permute-start(bf16[256,1024]{1,0:T(8,128)(2,1)S(1)} %get-tuple-element.54), channel_id=1, source_target_pairs={{0,4},{2,6},{4,0},{6,2},{8,12},{10,14},{12,8},{14,10},{1,5},{3,7},... | collective-permute-start | bytes 1572872 | tf_op jit(solution)/shard_map/ppermute | solution.py:337
  15.6 25.9 %collective-permute-start.5 = (bf16[256,1024]{1,0:T(8,128)(2,1)S(1)}, bf16[256,1024]{1,0:T(8,128)(2,1)S(1)}, u32[]{:S(2)}, u32[]{:S(2)}) collective-permute-start(bf16[256,1024]{1,0:T(8,128)(2,1)S(1)} %get-tuple-element.46.after), channel_id=1, source_target_pairs={{0,8},{2,10},{4,12},{6,14},{8,0},{10,2},{12,4},{14,6},{1,9},{3,11}... | collective-permute-start | bytes 1572872 | tf_op jit(solution)/shard_map/ppermute | solution.py:337
  22.6 24.7 %collective-permute-start.6 = (bf16[256,1024]{1,0:T(8,128)(2,1)S(1)}, bf16[256,1024]{1,0:T(8,128)(2,1)S(1)}, u32[]{:S(2)}, u32[]{:S(2)}) collective-permute-start(bf16[256,1024]{1,0:T(8,128)(2,1)S(1)} %get-tuple-element.50.after), channel_id=1, source_target_pairs={{0,12},{2,14},{4,8},{6,10},{8,4},{10,6},{12,0},{14,2},{1,13},{3,15... | collective-permute-start | bytes 1572872 | tf_op jit(solution)/shard_map/ppermute | solution.py:337
  36.3 43.9 %collective-permute-start.17 = (bf16[2,1024,256]{2,1,0:T(8,128)(2,1)S(1)}, bf16[2,1024,256]{2,1,0:T(8,128)(2,1)S(1)}, u32[]{:S(2)}, u32[]{:S(2)}) collective-permute-start(bf16[2,1024,256]{2,1,0:T(8,128)(2,1)S(1)} %load_weights.1), channel_id=1, source_target_pairs={{1,2},{3,14},{5,6},{7,10},{8,9},{10,5},{12,13},{14,1},{17,18},{19,... | collective-permute-start | bytes 3145736 | tf_op jit(solution)/shard_map/ppermute | solution.py:360
  37.6 16.6 %collective-permute-start.9 = (bf16[2,512,256]{2,1,0:T(8,128)(2,1)S(1)}, bf16[2,512,256]{2,1,0:T(8,128)(2,1)S(1)}, u32[]{:S(2)}, u32[]{:S(2)}) collective-permute-start(bf16[2,512,256]{2,1,0:T(8,128)(2,1)S(1)} %get-tuple-element.61), channel_id=1, source_target_pairs={{0,2},{2,0},{4,6},{6,4},{8,10},{10,8},{12,14},{14,12},{1,3},{3,1},... | collective-permute-start | bytes 1572872 | tf_op jit(solution)/shard_map/ppermute | solution.py:331
  37.7 21.7 %collective-permute-start.3 = (bf16[2,256,512]{2,1,0:T(8,128)(2,1)S(1)}, bf16[2,256,512]{2,1,0:T(8,128)(2,1)S(1)}, u32[]{:S(2)}, u32[]{:S(2)}) collective-permute-start(bf16[2,256,512]{2,1,0:T(8,128)(2,1)S(1)} %get-tuple-element.52), channel_id=1, source_target_pairs={{0,4},{2,6},{4,0},{6,2},{8,12},{10,14},{12,8},{14,10},{1,5},{3,7},... | collective-permute-start | bytes 1572872 | tf_op jit(solution)/shard_map/ppermute | solution.py:337
  41.4 32.1 %collective-permute-start.11 = (bf16[2,256,512]{2,1,0:T(8,128)(2,1)S(1)}, bf16[2,256,512]{2,1,0:T(8,128)(2,1)S(1)}, u32[]{:S(2)}, u32[]{:S(2)}) collective-permute-start(bf16[2,256,512]{2,1,0:T(8,128)(2,1)S(1)} %get-tuple-element.65), channel_id=1, source_target_pairs={{0,12},{2,14},{4,8},{6,10},{8,4},{10,6},{12,0},{14,2},{1,13},{3,15... | collective-permute-start | bytes 1572872 | tf_op jit(solution)/shard_map/ppermute | solution.py:337
  48.9 5.3 %collective-permute-start.8 = (bf16[256,512]{1,0:T(8,128)(2,1)S(1)}, bf16[256,512]{1,0:T(8,128)(2,1)S(1)}, u32[]{:S(2)}, u32[]{:S(2)}) collective-permute-start(bf16[256,512]{1,0:T(8,128)(2,1)S(1)} %get-tuple-element.60), channel_id=1, source_target_pairs={{0,2},{2,0},{4,6},{6,4},{8,10},{10,8},{12,14},{14,12},{1,3},{3,1},... | collective-permute-start | bytes 786440 | tf_op jit(solution)/shard_map/ppermute | solution.py:331
  55.0 8.7 %collective-permute-start.12 = (bf16[3,128,256]{2,1,0:T(8,128)(2,1)S(1)}, bf16[3,128,256]{2,1,0:T(8,128)(2,1)S(1)}, u32[]{:S(2)}, u32[]{:S(2)}) collective-permute-start(bf16[3,128,256]{2,1,0:T(8,128)(2,1)S(1)} %get-tuple-element.66), channel_id=1, source_target_pairs={{0,32},{16,48},{32,0},{48,16},{64,96},{80,112},{96,64},{112,80},{1... | collective-permute-start | bytes 589832 | tf_op jit(solution)/shard_map/ppermute | solution.py:370
  58.7 9.6 %collective-permute-start.13 = (bf16[3,128,256]{2,1,0:T(8,128)(2,1)S(1)}, bf16[3,128,256]{2,1,0:T(8,128)(2,1)S(1)}, u32[]{:S(2)}, u32[]{:S(2)}) collective-permute-start(bf16[3,128,256]{2,1,0:T(8,128)(2,1)S(1)} %get-tuple-element.67), channel_id=1, source_target_pairs={{0,16},{16,32},{32,48},{48,0},{64,80},{80,96},{96,112},{112,64},{1... | collective-permute-start | bytes 589832 | tf_op jit(solution)/shard_map/ppermute | solution.py:370
  59.4 8.9 %collective-permute-start.14 = (bf16[3,128,256]{2,1,0:T(8,128)(2,1)S(1)}, bf16[3,128,256]{2,1,0:T(8,128)(2,1)S(1)}, u32[]{:S(2)}, u32[]{:S(2)}) collective-permute-start(bf16[3,128,256]{2,1,0:T(8,128)(2,1)S(1)} %get-tuple-element.68), channel_id=1, source_target_pairs={{0,48},{16,0},{32,16},{48,32},{64,112},{80,64},{96,80},{112,96},{1... | collective-permute-start | bytes 589832 | tf_op jit(solution)/shard_map/ppermute | solution.py:370
  63.6 13.2 %collective-permute-start.10 = (bf16[256,512]{1,0:T(8,128)(2,1)S(1)}, bf16[256,512]{1,0:T(8,128)(2,1)S(1)}, u32[]{:S(2)}, u32[]{:S(2)}) collective-permute-start(bf16[256,512]{1,0:T(8,128)(2,1)S(1)} %get-tuple-element.64), channel_id=1, source_target_pairs={{0,12},{2,14},{4,8},{6,10},{8,4},{10,6},{12,0},{14,2},{1,13},{3,15... | collective-permute-start | bytes 786440 | tf_op jit(solution)/shard_map/ppermute | solution.py:337
  74.3 5.3 %collective-permute-start.15 = (bf16[256,512]{1,0:T(8,128)(2,1)S(1)}, bf16[256,512]{1,0:T(8,128)(2,1)S(1)}, u32[]{:S(2)}, u32[]{:S(2)}) collective-permute-start(bf16[256,512]{1,0:T(8,128)(2,1)S(1)} %get-tuple-element.70), channel_id=1, source_target_pairs={{0,4},{2,6},{4,0},{6,2},{8,12},{10,14},{12,8},{14,10},{1,5},{3,7},... | collective-permute-start | bytes 786440 | tf_op jit(solution)/shard_map/ppermute | solution.py:337
  80.3 2.4 %collective-permute-start.18 = (bf16[2,512,256]{2,1,0:T(8,128)(2,1)S(1)}, bf16[2,512,256]{2,1,0:T(8,128)(2,1)S(1)}, u32[]{:S(2)}, u32[]{:S(2)}) collective-permute-start(bf16[2,512,256]{2,1,0:T(8,128)(2,1)S(1)} %get-tuple-element.74), channel_id=1, source_target_pairs={{0,2},{2,0},{4,6},{6,4},{8,10},{10,8},{12,14},{14,12},{1,3},{3,1},... | collective-permute-start | bytes 1572872 | tf_op jit(solution)/shard_map/ppermute | solution.py:331
  80.4 2.3 %collective-permute-start.16 = (bf16[256,512]{1,0:T(8,128)(2,1)S(1)}, bf16[256,512]{1,0:T(8,128)(2,1)S(1)}, u32[]{:S(2)}, u32[]{:S(2)}) collective-permute-start(bf16[256,512]{1,0:T(8,128)(2,1)S(1)} %get-tuple-element.72), channel_id=1, source_target_pairs={{0,2},{2,0},{4,6},{6,4},{8,10},{10,8},{12,14},{14,12},{1,3},{3,1},... | collective-permute-start | bytes 786440 | tf_op jit(solution)/shard_map/ppermute | solution.py:331
  83.4 13.1 %collective-permute-start.19 = (bf16[3,128,256]{2,1,0:T(8,128)(2,1)S(1)}, bf16[3,128,256]{2,1,0:T(8,128)(2,1)S(1)}, u32[]{:S(2)}, u32[]{:S(2)}) collective-permute-start(bf16[3,128,256]{2,1,0:T(8,128)(2,1)S(1)} %get-tuple-element.75), channel_id=1, source_target_pairs={{0,32},{16,48},{32,0},{48,16},{64,96},{80,112},{96,64},{112,80},{1... | collective-permute-start | bytes 589832 | tf_op jit(solution)/shard_map/ppermute | solution.py:370
  87.4 9.6 %collective-permute-start.20 = (bf16[3,128,256]{2,1,0:T(8,128)(2,1)S(1)}, bf16[3,128,256]{2,1,0:T(8,128)(2,1)S(1)}, u32[]{:S(2)}, u32[]{:S(2)}) collective-permute-start(bf16[3,128,256]{2,1,0:T(8,128)(2,1)S(1)} %get-tuple-element.76), channel_id=1, source_target_pairs={{0,16},{16,32},{32,48},{48,0},{64,80},{80,96},{96,112},{112,64},{1... | collective-permute-start | bytes 589832 | tf_op jit(solution)/shard_map/ppermute | solution.py:370
  88.1 9.1 %collective-permute-start.21 = (bf16[3,128,256]{2,1,0:T(8,128)(2,1)S(1)}, bf16[3,128,256]{2,1,0:T(8,128)(2,1)S(1)}, u32[]{:S(2)}, u32[]{:S(2)}) collective-permute-start(bf16[3,128,256]{2,1,0:T(8,128)(2,1)S(1)} %get-tuple-element.77), channel_id=1, source_target_pairs={{0,48},{16,0},{32,16},{48,32},{64,112},{80,64},{96,80},{112,96},{1... | collective-permute-start | bytes 589832 | tf_op jit(solution)/shard_map/ppermute | solution.py:370
  90.0 14.5 %collective-permute-start.25 = (bf16[3,128,256]{2,1,0:T(8,128)(2,1)S(1)}, bf16[3,128,256]{2,1,0:T(8,128)(2,1)S(1)}, u32[]{:S(2)}, u32[]{:S(2)}) collective-permute-start(bf16[3,128,256]{2,1,0:T(8,128)(2,1)S(1)} %sum_over_z.2.after), channel_id=1, source_target_pairs={{64,0},{65,15},{66,64},{67,79},{68,4},{69,11},{70,68},{71,75},{72,... | collective-permute-start | bytes 589832 | tf_op jit(solution)/shard_map/ppermute | solution.py:357
  91.3 13.2 %collective-permute-start.24 = (bf16[3,128,256]{2,1,0:T(8,128)(2,1)S(1)}, bf16[3,128,256]{2,1,0:T(8,128)(2,1)S(1)}, u32[]{:S(2)}, u32[]{:S(2)}) collective-permute-start(bf16[3,128,256]{2,1,0:T(8,128)(2,1)S(1)} %sum_over_z.2.after), channel_id=1, source_target_pairs={{0,0},{1,15},{2,64},{3,79},{4,4},{5,11},{6,68},{7,75},{8,6},{9,9},... | collective-permute-start | bytes 589832 | tf_op jit(solution)/shard_map/ppermute | solution.py:357
  97.6 7.1 %collective-permute-start.23 = (bf16[3,128,256]{2,1,0:T(8,128)(2,1)S(1)}, bf16[3,128,256]{2,1,0:T(8,128)(2,1)S(1)}, u32[]{:S(2)}, u32[]{:S(2)}) collective-permute-start(bf16[3,128,256]{2,1,0:T(8,128)(2,1)S(1)} %sum_over_z.3), channel_id=1, source_target_pairs={{64,1},{65,14},{66,65},{67,78},{68,5},{69,10},{70,69},{71,74},{72,... | collective-permute-start | bytes 589832 | tf_op jit(solution)/shard_map/ppermute | solution.py:357
  98.3 11.0 %collective-permute-start.22 = (bf16[3,128,256]{2,1,0:T(8,128)(2,1)S(1)}, bf16[3,128,256]{2,1,0:T(8,128)(2,1)S(1)}, u32[]{:S(2)}, u32[]{:S(2)}) collective-permute-start(bf16[3,128,256]{2,1,0:T(8,128)(2,1)S(1)} %sum_over_z.3), channel_id=1, source_target_pairs={{0,1},{1,14},{2,65},{3,78},{4,5},{5,10},{6,69},{7,74},{8,7},{9,8},... | collective-permute-start | bytes 589832 | tf_op jit(solution)/shard_map/ppermute | solution.py:357

commit v15 on v11

--- a/solution.py
+++ b/solution.py
@@ -244,8 +244,8 @@
             weight = jnp.where(mine, w_own[m, cols, :].astype(F32), w_other[m, cols, :].astype(F32))
             weighted += fisher * weight
             total += fisher
-        if d == 0:
-            out[0], out[1] = weighted, total
+        if d == 0 or phase == 0:
+            out[0, :part], out[1, :part] = weighted, total
         else:
             to_words(weighted, total, out)
 
@@ -257,6 +257,15 @@
         weighted += more
         total += added
     return weighted, total
+
+
+def sum_wide_kernel(one, two, three, sums, after, out):
+    part = sums.shape[1]
+    weighted, total = sums[0], sums[1]
+    for ref in (one, two, three):
+        weighted += ref[0, :part]
+        total += ref[1, :part]
+    to_words(weighted, total, out)
 
 
 def sum_kernel(one, two, three, sums, after, out):
@@ -318,6 +327,7 @@
     part_shape, sent_shape, sum_shape = ((2, outs, 2 * wide), F32), ((outs, 2 * wide), BF16), ((outs, 2 * wide), F32)
     code_shape, own_shape = ((outs, wide), BF16), ((outs, wide), F32)
     pair_shape, kept_shape = ((2, outs, wide), BF16), ((2, outs, wide), F32)
+    wide_words = ((2, wide // Z, outs), F32)
     words, sums = ((3, wide // Z, outs), BF16), ((2, wide // Z, outs), F32)
     dma = pltpu.SemaphoreType.DMA
 
@@ -358,9 +368,9 @@
 
     def weigh(phase, own, other, moved, after):
         one, two, three, own_sums = call(
-            lambda *refs: weigh_kernel(phase, *refs), "weigh_members", [words] * 3 + [sums], [], [own, other, *moved, after]
+            lambda *refs: weigh_kernel(phase, *refs), "weigh_members", [words if phase else wide_words] * 3 + [sums], [], [own, other, *moved, after]
         )
-        send = ((1, one), (2, two), (3, three))
+        send = ((2, two), (1, one), (3, three))
         return [lax.ppermute(v, "member", z_pairs(d)) for d, v in send] + [own_sums]
 
     x_send0 = call(
@@ -401,9 +411,9 @@
     own0, other0 = join_direct(sum0, got0, kept11)
     words0 = weigh(0, own0, other0, moved, own0)
     part10 = middle(3, swap10, kept10, words0[3])
-    first = call(sum_kernel, "sum_over_z", words, [], [*words0, part10[0]])
-    part11 = middle(1, swap11, kept11, first)
-    own1, other1 = join(settle(part10, part11[0]), part11, first)
+    part11 = middle(1, swap11, kept11, part10[0])
+    first = call(sum_wide_kernel, "sum_over_z", words, [], [*words0, part11[0]])
+    own1, other1 = join(settle(part10, first), part11, first)
     words1 = weigh(1, own1, other1, moved, own1)
     met = call(meet_kernel, "meet_over_y", sums, [], [*results(0, first), own1])
     second = call(sum_kernel, "sum_over_z", words, [], [*words1, own1])

time: 109 us -> 103 us (0.945)
  waiting for transfers between devices: 39.1 us -> 31.5 us
  starting transfers between devices: 46.2 us -> 48.6 us
    ppermute x7, waiting for transfers between devices: 5.22 us -> 0.02 us  [swap_x(): return lax.ppermute(sent, 'tok', x_pairs(flip))]
    ppermute x6, starting transfers between devices: 9.58 us -> 12.5 us  [weigh(): return [lax.ppermute(v, 'member', z_pairs(d)) for d, v in send] + [own_sums]]
    ppermute x6, waiting for transfers between devices: 7.96 us -> 6.62 us  [weigh(): return [lax.ppermute(v, 'member', z_pairs(d)) for d, v in send] + [own_sums]]
    ppermute x4, waiting for transfers between devices: 6.85 us -> 5.73 us  [results(): lax.ppermute(sums, ('member', 'tok', 'col'), result_pairs(phase, y_lo))]
  transfers between devices with their start and end apart: 24 -> 24, of which waited for: 8 -> 8; matrix products, arithmetic and copies ran while one was open for 0% -> 0% of each run, Pallas kernels for 17% -> 18%
where the time goes in v15:
time: 103 us
  starting transfers between devices  48.6 us (47%)
  waiting for transfers between devices  31.5 us (31%)
  Pallas kernels  22.4 us (22%)
    pallas_call x20, Pallas kernels, call(): pl.pallas_call(kernel, out_shape=shapes, in_specs=[HBM] * len(hbm) + [VME...  21.6 us
    ppermute x1, waiting for transfers between devices, swap_cols(): return lax.ppermute(send, 'col', [(0, 1), (1, 0)])  16.8 us
    ppermute x4, starting transfers between devices, results(): lax.ppermute(sums, ('member', 'tok', 'col'), result_pairs(phase, y_lo))  15.5 us
    ppermute x6, starting transfers between devices, weigh(): return [lax.ppermute(v, 'member', z_pairs(d)) for d, v in send] + [own_sums]  12.5 us
    ppermute x7, starting transfers between devices, swap_x(): return lax.ppermute(sent, 'tok', x_pairs(flip))  9.1 us
    ppermute x6, waiting for transfers between devices, weigh(): return [lax.ppermute(v, 'member', z_pairs(d)) for d, v in send] + [own_sums]  6.62 us
    ppermute x4, waiting for transfers between devices, results(): lax.ppermute(sums, ('member', 'tok', 'col'), result_pairs(phase, y_lo))  5.73 us
    ppermute x1, starting transfers between devices, bring_weights(): arrived = lax.ppermute(weights, ('tok', 'col'), weight_pairs())  4.75 us
  transfers between devices with their start and end apart: 24, of which 8 were waited for; matrix products, arithmetic and copies ran while one was open for 0% of the time, Pallas kernels for 18%

profile of v15, /device:TPU:1, one launch (start us, length us, event | category | flops | bytes accessed | tf_op | source)
XLA Modules:
  0.0 102.8 jit_solution(11521454726358815756)
XLA Ops:
  0.0 2.0 %load_to_swap.2.after = bf16[768,2304]{1,0:T(8,128)(2,1)S(1)} custom-call(bf16[2,768,4096]{2,1,0:T(8,128)(2,1)} %x_ref.7, bf16[2,768,256]{2,1,0:T(8,128)(2,1)} %g_ref.3), custom_call_target="tpu_custom_call" | custom-call | flops 1 | bytes 1 | tf_op jit(solution)/shard_map/load_to_swap/pallas_call | solution.py:66
  2.1 1.5 %collective-permute-start = (bf16[768,2304]{1,0:T(8,128)(2,1)S(1)}, bf16[768,2304]{1,0:T(8,128)(2,1)S(1)}, u32[]{:S(2)}, u32[]{:S(2)}) collective-permute-start(bf16[768,2304]{1,0:T(8,128)(2,1)S(1)} %load_to_swap.2.after), channel_id=1, source_target_pairs={{0,2},{2,0},{4,6},{6,4},{8,10},{10,8},{12,14},{14,12},{1,3},{3,1},... | collective-permute-start | bytes 10616840 | tf_op jit(solution)/shard_map/ppermute | solution.py:335
  3.6 1.9 %load_to_swap.3.after = bf16[768,2048]{1,0:T(8,128)(2,1)S(1)} custom-call(bf16[2,768,4096]{2,1,0:T(8,128)(2,1)} %x_ref.7, bf16[768,2304]{1,0:T(8,128)(2,1)S(1)} %load_to_swap.2.after), custom_call_target="tpu_custom_call" | custom-call | flops 1 | bytes 1 | tf_op jit(solution)/shard_map/load_to_swap/pallas_call | solution.py:66
  5.5 0.2 collective-permute-start.1
  5.7 4.8 %collective-permute-start.7 = (bf16[2,1024,256]{2,1,0:T(8,128)(2,1)S(1)}, bf16[2,1024,256]{2,1,0:T(8,128)(2,1)S(1)}, u32[]{:S(2)}, u32[]{:S(2)}) collective-permute-start(bf16[2,1024,256]{2,1,0:T(8,128)(2,1)S(1)} %copy-done), channel_id=1, source_target_pairs={{0,0},{1,2},{2,12},{3,14},{4,4},{5,6},{6,8},{7,10},{8,9},{9,11},{1... | collective-permute-start | bytes 3145736 | tf_op jit(solution)/shard_map/ppermute | solution.py:364
  10.4 2.9 %fisher_of_own_tokens.2 = (bf16[768,2048]{1,0:T(8,128)(2,1)S(1)}, bf16[768,256]{1,0:T(8,128)(2,1)S(1)}, bf16[256,768]{1,0:T(8,128)(2,1)S(1)}, f32[2,256,1024]{2,1,0:T(8,128)S(1)}) custom-call(bf16[2,768,4096]{2,1,0:T(8,128)(2,1)} %x_ref.7, bf16[2,768,256]{2,1,0:T(8,128)(2,1)} %g_ref.3, bf16[768,2048]{1,0:T(8,128)(2,1)S(1)} %load_to_swap.3.after), custom_call_target="tpu_custom_call" | custom-call | flops 1 | bytes 1 | tf_op jit(solution)/shard_map/fisher_of_own_tokens/pallas_call | solution.py:66
  13.4 2.5 %collective-permute-start.2 = (bf16[2,768,256]{2,1,0:T(8,128)(2,1)S(1)}, bf16[2,768,256]{2,1,0:T(8,128)(2,1)S(1)}, u32[]{:S(2)}, u32[]{:S(2)}) collective-permute-start(bf16[2,768,256]{2,1,0:T(8,128)(2,1)S(1)} %pair_grads.1.after), channel_id=1, source_target_pairs={{0,1},{1,0},{2,3},{3,2},{4,5},{5,4},{6,7},{7,6},{8,9},{9,8},{10,11... | collective-permute-start | bytes 2359304 | tf_op jit(solution)/shard_map/ppermute | solution.py:338
  15.9 1.3 %fisher_of_both_cores.2 = (bf16[256,1024]{1,0:T(8,128)(2,1)S(1)}, bf16[256,1024]{1,0:T(8,128)(2,1)S(1)}, bf16[256,768]{1,0:T(8,128)(2,1)S(1)}) custom-call(bf16[768,2304]{1,0:T(8,128)(2,1)S(1)} %collective-permute-done.got.x_ref.got_a, f32[2,256,1024]{2,1,0:T(8,128)S(1)} %get-tuple-element.42.part_ref, bf16[2,768,256]{2,1,0:T(8,128)(2,1)S(1)} %pair_grads.1.after), custom_call_target="tpu_custom_call" | custom-call | flops 1 | bytes 1 | tf_op jit(solution)/shard_map/fisher_of_both_cores/pallas_call | solution.py:66
  17.2 1.6 %collective-permute-start.5 = (bf16[256,1024]{1,0:T(8,128)(2,1)S(1)}, bf16[256,1024]{1,0:T(8,128)(2,1)S(1)}, u32[]{:S(2)}, u32[]{:S(2)}) collective-permute-start(bf16[256,1024]{1,0:T(8,128)(2,1)S(1)} %get-tuple-element.44.after), channel_id=1, source_target_pairs={{0,8},{2,10},{4,12},{6,14},{8,0},{10,2},{12,4},{14,6},{1,9},{3,11}... | collective-permute-start | bytes 1572872 | tf_op jit(solution)/shard_map/ppermute | solution.py:341
  18.8 2.6 %fisher_of_own_tokens.3 = (bf16[768,2048]{1,0:T(8,128)(2,1)S(1)}, f32[2,256,1024]{2,1,0:T(8,128)S(1)}) custom-call(bf16[2,768,4096]{2,1,0:T(8,128)(2,1)} %x_ref.7, bf16[256,768]{1,0:T(8,128)(2,1)S(1)} %get-tuple-element.41.after.gt_ref, bf16[256,1024]{1,0:T(8,128)(2,1)S(1)} %get-tuple-element.44.after), custom_call_target="tpu_custom_call" | custom-call | flops 1 | bytes 1 | tf_op jit(solution)/shard_map/fisher_of_own_tokens/pallas_call | solution.py:66
  21.4 1.1 %fisher_of_both_cores.3 = (bf16[256,1024]{1,0:T(8,128)(2,1)S(1)}, f32[256,1024]{1,0:T(8,128)S(1)}) custom-call(bf16[768,2048]{1,0:T(8,128)(2,1)S(1)} %collective-permute-done.1.x_ref.got_b, bf16[256,768]{1,0:T(8,128)(2,1)S(1)} %get-tuple-element.46.gt_ref, f32[2,256,1024]{2,1,0:T(8,128)S(1)} %get-tuple-element.47.part_ref, ...), custom_call_target="tpu_custom_call" | custom-call | flops 1 | bytes 1 | tf_op jit(solution)/shard_map/fisher_of_both_cores/pallas_call | solution.py:66
  22.6 2.3 %collective-permute-start.6 = (bf16[256,1024]{1,0:T(8,128)(2,1)S(1)}, bf16[256,1024]{1,0:T(8,128)(2,1)S(1)}, u32[]{:S(2)}, u32[]{:S(2)}) collective-permute-start(bf16[256,1024]{1,0:T(8,128)(2,1)S(1)} %get-tuple-element.48.after), channel_id=1, source_target_pairs={{0,12},{2,14},{4,8},{6,10},{8,4},{10,6},{12,0},{14,2},{1,13},{3,15... | collective-permute-start | bytes 1572872 | tf_op jit(solution)/shard_map/ppermute | solution.py:341
  24.9 16.8 %collective-permute-done.2.g_ref = bf16[2,768,256]{2,1,0:T(8,128)(2,1)S(1)} collective-permute-done((bf16[2,768,256]{2,1,0:T(8,128)(2,1)S(1)}, bf16[2,768,256]{2,1,0:T(8,128)(2,1)S(1)}, u32[]{:S(2)}, u32[]{:S(2)}) %collective-permute-start.2) | collective-permute-done | bytes 786464 | tf_op jit(solution)/shard_map/ppermute | solution.py:338
  41.6 1.9 %fisher_of_other_grads.2 = (bf16[2,256,512]{2,1,0:T(8,128)(2,1)S(1)}, f32[2,256,512]{2,1,0:T(8,128)S(1)}, bf16[256,768]{1,0:T(8,128)(2,1)S(1)}, bf16[256,768]{1,0:T(8,128)(2,1)S(1)}) custom-call(bf16[768,2048]{1,0:T(8,128)(2,1)S(1)} %get-tuple-element.40.own_a, bf16[768,2304]{1,0:T(8,128)(2,1)S(1)} %collective-permute-done.got.x_ref.got_a, ...), custom_call_target="tpu_custom_call" | custom-call | flops 1 | bytes 1 | tf_op jit(solution)/shard_map/fisher_of_other_grads/pallas_call | solution.py:66
  43.7 0.3 collective-permute-start.9
  43.9 0.3 collective-permute-start.3
  44.3 1.9 %fisher_of_other_grads.3 = (bf16[2,256,512]{2,1,0:T(8,128)(2,1)S(1)}, f32[2,256,512]{2,1,0:T(8,128)S(1)}) custom-call(bf16[768,2048]{1,0:T(8,128)(2,1)S(1)} %get-tuple-element.40.own_a, bf16[768,2304]{1,0:T(8,128)(2,1)S(1)} %collective-permute-done.got.x_ref.got_a, bf16[768,2048]{1,0:T(8,128)(2,1)S(1)} %get-tuple-element.45.after.own_b, ...), custom_call_target="tpu_custom_call" | custom-call | flops 1 | bytes 1 | tf_op jit(solution)/shard_map/fisher_of_other_grads/pallas_call | solution.py:66
  46.1 2.9 %collective-permute-start.14 = (bf16[2,256,512]{2,1,0:T(8,128)(2,1)S(1)}, bf16[2,256,512]{2,1,0:T(8,128)(2,1)S(1)}, u32[]{:S(2)}, u32[]{:S(2)}) collective-permute-start(bf16[2,256,512]{2,1,0:T(8,128)(2,1)S(1)} %get-tuple-element.66), channel_id=1, source_target_pairs={{0,12},{2,14},{4,8},{6,10},{8,4},{10,6},{12,0},{14,2},{1,13},{3,15... | collective-permute-start | bytes 1572872 | tf_op jit(solution)/shard_map/ppermute | solution.py:341
  49.0 1.6 %fisher_over_tokens.3 = (f32[256,512]{1,0:T(8,128)S(1)}, bf16[256,512]{1,0:T(8,128)(2,1)S(1)}) custom-call(f32[256,1024]{1,0:T(8,128)S(1)} %get-tuple-element.51.own, bf16[256,1024]{1,0:T(8,128)(2,1)S(1)} %collective-permute-done.4.one, bf16[256,1024]{1,0:T(8,128)(2,1)S(1)} %collective-permute-done.5.two, ...), custom_call_target="tpu_custom_call" | custom-call | flops 1 | bytes 1 | tf_op jit(solution)/shard_map/fisher_over_tokens/pallas_call | solution.py:66
  50.7 0.6 collective-permute-start.8
  51.3 1.2 %collective-permute-done.8.refs_1_ = bf16[256,512]{1,0:T(8,128)(2,1)S(1)} collective-permute-done((bf16[256,512]{1,0:T(8,128)(2,1)S(1)}, bf16[256,512]{1,0:T(8,128)(2,1)S(1)}, u32[]{:S(2)}, u32[]{:S(2)}) %collective-permute-start.8) | collective-permute-done | bytes 262176 | tf_op jit(solution)/shard_map/ppermute | solution.py:335
  52.5 0.5 weigh_members.2
  53.0 3.7 %collective-permute-start.11 = (f32[2,128,256]{2,1,0:T(8,128)S(1)}, f32[2,128,256]{2,1,0:T(8,128)S(1)}, u32[]{:S(2)}, u32[]{:S(2)}) collective-permute-start(f32[2,128,256]{2,1,0:T(8,128)S(1)} %get-tuple-element.63), channel_id=1, source_target_pairs={{0,32},{16,48},{32,0},{48,16},{64,96},{80,112},{96,64},{112,80},{1... | collective-permute-start | bytes 786440 | tf_op jit(solution)/shard_map/ppermute | solution.py:374
  56.6 0.7 collective-permute-start.12
  57.4 1.9 %collective-permute-start.13 = (f32[2,128,256]{2,1,0:T(8,128)S(1)}, f32[2,128,256]{2,1,0:T(8,128)S(1)}, u32[]{:S(2)}, u32[]{:S(2)}) collective-permute-start(f32[2,128,256]{2,1,0:T(8,128)S(1)} %get-tuple-element.65), channel_id=1, source_target_pairs={{0,48},{16,0},{32,16},{48,32},{64,112},{80,64},{96,80},{112,96},{1... | collective-permute-start | bytes 786440 | tf_op jit(solution)/shard_map/ppermute | solution.py:374
  59.3 0.7 fisher_over_first_swap.2
  60.1 1.5 %collective-permute-start.10 = (bf16[256,512]{1,0:T(8,128)(2,1)S(1)}, bf16[256,512]{1,0:T(8,128)(2,1)S(1)}, u32[]{:S(2)}, u32[]{:S(2)}) collective-permute-start(bf16[256,512]{1,0:T(8,128)(2,1)S(1)} %get-tuple-element.62), channel_id=1, source_target_pairs={{0,12},{2,14},{4,8},{6,10},{8,4},{10,6},{12,0},{14,2},{1,13},{3,15... | collective-permute-start | bytes 786440 | tf_op jit(solution)/shard_map/ppermute | solution.py:341
  61.6 0.7 fisher_over_first_swap.3
  62.3 0.4 collective-permute-start.15
  62.7 0.4 collective-permute-done.11.one
  63.1 6.0 %collective-permute-done.12.two = f32[2,128,256]{2,1,0:T(8,128)S(1)} collective-permute-done((f32[2,128,256]{2,1,0:T(8,128)S(1)}, f32[2,128,256]{2,1,0:T(8,128)S(1)}, u32[]{:S(2)}, u32[]{:S(2)}) %collective-permute-start.12) | collective-permute-done | bytes 262176 | tf_op jit(solution)/shard_map/ppermute | solution.py:374
  69.2 0.3 fisher_over_tokens.4.first_ref
  69.5 0.6 fisher_over_tokens.5
  70.1 1.7 %collective-permute-start.16 = (bf16[256,512]{1,0:T(8,128)(2,1)S(1)}, bf16[256,512]{1,0:T(8,128)(2,1)S(1)}, u32[]{:S(2)}, u32[]{:S(2)}) collective-permute-start(bf16[256,512]{1,0:T(8,128)(2,1)S(1)} %get-tuple-element.70), channel_id=1, source_target_pairs={{0,2},{2,0},{4,6},{6,4},{8,10},{10,8},{12,14},{14,12},{1,3},{3,1},... | collective-permute-start | bytes 786440 | tf_op jit(solution)/shard_map/ppermute | solution.py:335
  71.8 1.2 %collective-permute-done.16.refs_1_ = bf16[256,512]{1,0:T(8,128)(2,1)S(1)} collective-permute-done((bf16[256,512]{1,0:T(8,128)(2,1)S(1)}, bf16[256,512]{1,0:T(8,128)(2,1)S(1)}, u32[]{:S(2)}, u32[]{:S(2)}) %collective-permute-start.16) | collective-permute-done | bytes 262176 | tf_op jit(solution)/shard_map/ppermute | solution.py:335
  73.0 0.7 weigh_members.3
  73.7 3.5 %collective-permute-start.17 = (bf16[3,128,256]{2,1,0:T(8,128)(2,1)S(1)}, bf16[3,128,256]{2,1,0:T(8,128)(2,1)S(1)}, u32[]{:S(2)}, u32[]{:S(2)}) collective-permute-start(bf16[3,128,256]{2,1,0:T(8,128)(2,1)S(1)} %get-tuple-element.71), channel_id=1, source_target_pairs={{0,32},{16,48},{32,0},{48,16},{64,96},{80,112},{96,64},{112,80},{1... | collective-permute-start | bytes 589832 | tf_op jit(solution)/shard_map/ppermute | solution.py:374
  77.2 0.7 collective-permute-start.18
  77.9 1.9 %collective-permute-start.19 = (bf16[3,128,256]{2,1,0:T(8,128)(2,1)S(1)}, bf16[3,128,256]{2,1,0:T(8,128)(2,1)S(1)}, u32[]{:S(2)}, u32[]{:S(2)}) collective-permute-start(bf16[3,128,256]{2,1,0:T(8,128)(2,1)S(1)} %get-tuple-element.73), channel_id=1, source_target_pairs={{0,48},{16,0},{32,16},{48,32},{64,112},{80,64},{96,80},{112,96},{1... | collective-permute-start | bytes 589832 | tf_op jit(solution)/shard_map/ppermute | solution.py:374
  79.8 1.3 %collective-permute-start.23 = (bf16[3,128,256]{2,1,0:T(8,128)(2,1)S(1)}, bf16[3,128,256]{2,1,0:T(8,128)(2,1)S(1)}, u32[]{:S(2)}, u32[]{:S(2)}) collective-permute-start(bf16[3,128,256]{2,1,0:T(8,128)(2,1)S(1)} %sum_over_z.2.after), channel_id=1, source_target_pairs={{64,0},{65,15},{66,64},{67,79},{68,4},{69,11},{70,68},{71,75},{72,... | collective-permute-start | bytes 589832 | tf_op jit(solution)/shard_map/ppermute | solution.py:361
  81.1 5.4 %collective-permute-start.22 = (bf16[3,128,256]{2,1,0:T(8,128)(2,1)S(1)}, bf16[3,128,256]{2,1,0:T(8,128)(2,1)S(1)}, u32[]{:S(2)}, u32[]{:S(2)}) collective-permute-start(bf16[3,128,256]{2,1,0:T(8,128)(2,1)S(1)} %sum_over_z.2.after), channel_id=1, source_target_pairs={{0,0},{1,15},{2,64},{3,79},{4,4},{5,11},{6,68},{7,75},{8,6},{9,9},... | collective-permute-start | bytes 589832 | tf_op jit(solution)/shard_map/ppermute | solution.py:361
  86.5 0.2 collective-permute-done.18.two
  86.8 0.3 sum_over_z.3
  87.1 0.7 collective-permute-start.21
  87.8 8.2 %collective-permute-start.20 = (bf16[3,128,256]{2,1,0:T(8,128)(2,1)S(1)}, bf16[3,128,256]{2,1,0:T(8,128)(2,1)S(1)}, u32[]{:S(2)}, u32[]{:S(2)}) collective-permute-start(bf16[3,128,256]{2,1,0:T(8,128)(2,1)S(1)} %sum_over_z.3), channel_id=1, source_target_pairs={{0,1},{1,14},{2,65},{3,78},{4,5},{5,10},{6,69},{7,74},{8,7},{9,8},... | collective-permute-start | bytes 589832 | tf_op jit(solution)/shard_map/ppermute | solution.py:361
  96.0 0.2 meet_over_y.1.sums
  96.2 5.7 %collective-permute-done.20.near = bf16[3,128,256]{2,1,0:T(8,128)(2,1)S(1)} collective-permute-done((bf16[3,128,256]{2,1,0:T(8,128)(2,1)S(1)}, bf16[3,128,256]{2,1,0:T(8,128)(2,1)S(1)}, u32[]{:S(2)}, u32[]{:S(2)}) %collective-permute-start.20) | collective-permute-done | bytes 196640 | tf_op jit(solution)/shard_map/ppermute | solution.py:361
  101.9 0.8 merge_members.1
  (23 shorter events, 0.5 us)
Async XLA Ops:
  2.1 3.6 %copy-start = (bf16[2,1024,256]{2,1,0:T(8,128)(2,1)S(1)}, bf16[2,1024,256]{2,1,0:T(8,128)(2,1)}, u32[]{:S(2)}) copy-start(bf16[2,1024,256]{2,1,0:T(8,128)(2,1)} %param.5) | copy-start | bytes 3145732
  2.1 11.2 %collective-permute-start = (bf16[768,2304]{1,0:T(8,128)(2,1)S(1)}, bf16[768,2304]{1,0:T(8,128)(2,1)S(1)}, u32[]{:S(2)}, u32[]{:S(2)}) collective-permute-start(bf16[768,2304]{1,0:T(8,128)(2,1)S(1)} %load_to_swap.2.after), channel_id=1, source_target_pairs={{0,2},{2,0},{4,6},{6,4},{8,10},{10,8},{12,14},{14,12},{1,3},{3,1},... | collective-permute-start | bytes 10616840 | tf_op jit(solution)/shard_map/ppermute | solution.py:335
  5.5 15.9 %collective-permute-start.1 = (bf16[768,2048]{1,0:T(8,128)(2,1)S(1)}, bf16[768,2048]{1,0:T(8,128)(2,1)S(1)}, u32[]{:S(2)}, u32[]{:S(2)}) collective-permute-start(bf16[768,2048]{1,0:T(8,128)(2,1)S(1)} %load_to_swap.3.after), channel_id=1, source_target_pairs={{0,2},{2,0},{4,6},{6,4},{8,10},{10,8},{12,14},{14,12},{1,3},{3,1},... | collective-permute-start | bytes 9437192 | tf_op jit(solution)/shard_map/ppermute | solution.py:335
  5.7 37.9 %collective-permute-start.7 = (bf16[2,1024,256]{2,1,0:T(8,128)(2,1)S(1)}, bf16[2,1024,256]{2,1,0:T(8,128)(2,1)S(1)}, u32[]{:S(2)}, u32[]{:S(2)}) collective-permute-start(bf16[2,1024,256]{2,1,0:T(8,128)(2,1)S(1)} %copy-done), channel_id=1, source_target_pairs={{0,0},{1,2},{2,12},{3,14},{4,4},{5,6},{6,8},{7,10},{8,9},{9,11},{1... | collective-permute-start | bytes 3145736 | tf_op jit(solution)/shard_map/ppermute | solution.py:364
  13.4 28.3 %collective-permute-start.2 = (bf16[2,768,256]{2,1,0:T(8,128)(2,1)S(1)}, bf16[2,768,256]{2,1,0:T(8,128)(2,1)S(1)}, u32[]{:S(2)}, u32[]{:S(2)}) collective-permute-start(bf16[2,768,256]{2,1,0:T(8,128)(2,1)S(1)} %pair_grads.1.after), channel_id=1, source_target_pairs={{0,1},{1,0},{2,3},{3,2},{4,5},{5,4},{6,7},{7,6},{8,9},{9,8},{10,11... | collective-permute-start | bytes 2359304 | tf_op jit(solution)/shard_map/ppermute | solution.py:338
  17.1 29.0 %collective-permute-start.4 = (bf16[256,1024]{1,0:T(8,128)(2,1)S(1)}, bf16[256,1024]{1,0:T(8,128)(2,1)S(1)}, u32[]{:S(2)}, u32[]{:S(2)}) collective-permute-start(bf16[256,1024]{1,0:T(8,128)(2,1)S(1)} %get-tuple-element.52), channel_id=1, source_target_pairs={{0,4},{2,6},{4,0},{6,2},{8,12},{10,14},{12,8},{14,10},{1,5},{3,7},... | collective-permute-start | bytes 1572872 | tf_op jit(solution)/shard_map/ppermute | solution.py:341
  17.2 31.8 %collective-permute-start.5 = (bf16[256,1024]{1,0:T(8,128)(2,1)S(1)}, bf16[256,1024]{1,0:T(8,128)(2,1)S(1)}, u32[]{:S(2)}, u32[]{:S(2)}) collective-permute-start(bf16[256,1024]{1,0:T(8,128)(2,1)S(1)} %get-tuple-element.44.after), channel_id=1, source_target_pairs={{0,8},{2,10},{4,12},{6,14},{8,0},{10,2},{12,4},{14,6},{1,9},{3,11}... | collective-permute-start | bytes 1572872 | tf_op jit(solution)/shard_map/ppermute | solution.py:341
  22.6 26.5 %collective-permute-start.6 = (bf16[256,1024]{1,0:T(8,128)(2,1)S(1)}, bf16[256,1024]{1,0:T(8,128)(2,1)S(1)}, u32[]{:S(2)}, u32[]{:S(2)}) collective-permute-start(bf16[256,1024]{1,0:T(8,128)(2,1)S(1)} %get-tuple-element.48.after), channel_id=1, source_target_pairs={{0,12},{2,14},{4,8},{6,10},{8,4},{10,6},{12,0},{14,2},{1,13},{3,15... | collective-permute-start | bytes 1572872 | tf_op jit(solution)/shard_map/ppermute | solution.py:341
  43.7 8.8 %collective-permute-start.9 = (bf16[2,512,256]{2,1,0:T(8,128)(2,1)S(1)}, bf16[2,512,256]{2,1,0:T(8,128)(2,1)S(1)}, u32[]{:S(2)}, u32[]{:S(2)}) collective-permute-start(bf16[2,512,256]{2,1,0:T(8,128)(2,1)S(1)} %get-tuple-element.59), channel_id=1, source_target_pairs={{0,2},{2,0},{4,6},{6,4},{8,10},{10,8},{12,14},{14,12},{1,3},{3,1},... | collective-permute-start | bytes 1572872 | tf_op jit(solution)/shard_map/ppermute | solution.py:335
  43.9 15.4 %collective-permute-start.3 = (bf16[2,256,512]{2,1,0:T(8,128)(2,1)S(1)}, bf16[2,256,512]{2,1,0:T(8,128)(2,1)S(1)}, u32[]{:S(2)}, u32[]{:S(2)}) collective-permute-start(bf16[2,256,512]{2,1,0:T(8,128)(2,1)S(1)} %get-tuple-element.50), channel_id=1, source_target_pairs={{0,4},{2,6},{4,0},{6,2},{8,12},{10,14},{12,8},{14,10},{1,5},{3,7},... | collective-permute-start | bytes 1572872 | tf_op jit(solution)/shard_map/ppermute | solution.py:341
  46.1 15.4 %collective-permute-start.14 = (bf16[2,256,512]{2,1,0:T(8,128)(2,1)S(1)}, bf16[2,256,512]{2,1,0:T(8,128)(2,1)S(1)}, u32[]{:S(2)}, u32[]{:S(2)}) collective-permute-start(bf16[2,256,512]{2,1,0:T(8,128)(2,1)S(1)} %get-tuple-element.66), channel_id=1, source_target_pairs={{0,12},{2,14},{4,8},{6,10},{8,4},{10,6},{12,0},{14,2},{1,13},{3,15... | collective-permute-start | bytes 1572872 | tf_op jit(solution)/shard_map/ppermute | solution.py:341
  50.7 1.8 %collective-permute-start.8 = (bf16[256,512]{1,0:T(8,128)(2,1)S(1)}, bf16[256,512]{1,0:T(8,128)(2,1)S(1)}, u32[]{:S(2)}, u32[]{:S(2)}) collective-permute-start(bf16[256,512]{1,0:T(8,128)(2,1)S(1)} %get-tuple-element.58), channel_id=1, source_target_pairs={{0,2},{2,0},{4,6},{6,4},{8,10},{10,8},{12,14},{14,12},{1,3},{3,1},... | collective-permute-start | bytes 786440 | tf_op jit(solution)/shard_map/ppermute | solution.py:335
  53.0 10.1 %collective-permute-start.11 = (f32[2,128,256]{2,1,0:T(8,128)S(1)}, f32[2,128,256]{2,1,0:T(8,128)S(1)}, u32[]{:S(2)}, u32[]{:S(2)}) collective-permute-start(f32[2,128,256]{2,1,0:T(8,128)S(1)} %get-tuple-element.63), channel_id=1, source_target_pairs={{0,32},{16,48},{32,0},{48,16},{64,96},{80,112},{96,64},{112,80},{1... | collective-permute-start | bytes 786440 | tf_op jit(solution)/shard_map/ppermute | solution.py:374
  56.6 12.4 %collective-permute-start.12 = (f32[2,128,256]{2,1,0:T(8,128)S(1)}, f32[2,128,256]{2,1,0:T(8,128)S(1)}, u32[]{:S(2)}, u32[]{:S(2)}) collective-permute-start(f32[2,128,256]{2,1,0:T(8,128)S(1)} %get-tuple-element.64), channel_id=1, source_target_pairs={{0,16},{16,32},{32,48},{48,0},{64,80},{80,96},{96,112},{112,64},{1... | collective-permute-start | bytes 786440 | tf_op jit(solution)/shard_map/ppermute | solution.py:374
  57.4 11.7 %collective-permute-start.13 = (f32[2,128,256]{2,1,0:T(8,128)S(1)}, f32[2,128,256]{2,1,0:T(8,128)S(1)}, u32[]{:S(2)}, u32[]{:S(2)}) collective-permute-start(f32[2,128,256]{2,1,0:T(8,128)S(1)} %get-tuple-element.65), channel_id=1, source_target_pairs={{0,48},{16,0},{32,16},{48,32},{64,112},{80,64},{96,80},{112,96},{1... | collective-permute-start | bytes 786440 | tf_op jit(solution)/shard_map/ppermute | solution.py:374
  60.1 9.2 %collective-permute-start.10 = (bf16[256,512]{1,0:T(8,128)(2,1)S(1)}, bf16[256,512]{1,0:T(8,128)(2,1)S(1)}, u32[]{:S(2)}, u32[]{:S(2)}) collective-permute-start(bf16[256,512]{1,0:T(8,128)(2,1)S(1)} %get-tuple-element.62), channel_id=1, source_target_pairs={{0,12},{2,14},{4,8},{6,10},{8,4},{10,6},{12,0},{14,2},{1,13},{3,15... | collective-permute-start | bytes 786440 | tf_op jit(solution)/shard_map/ppermute | solution.py:341
  62.3 7.2 %collective-permute-start.15 = (bf16[256,512]{1,0:T(8,128)(2,1)S(1)}, bf16[256,512]{1,0:T(8,128)(2,1)S(1)}, u32[]{:S(2)}, u32[]{:S(2)}) collective-permute-start(bf16[256,512]{1,0:T(8,128)(2,1)S(1)} %get-tuple-element.68), channel_id=1, source_target_pairs={{0,4},{2,6},{4,0},{6,2},{8,12},{10,14},{12,8},{14,10},{1,5},{3,7},... | collective-permute-start | bytes 786440 | tf_op jit(solution)/shard_map/ppermute | solution.py:341
  70.1 2.8 %collective-permute-start.16 = (bf16[256,512]{1,0:T(8,128)(2,1)S(1)}, bf16[256,512]{1,0:T(8,128)(2,1)S(1)}, u32[]{:S(2)}, u32[]{:S(2)}) collective-permute-start(bf16[256,512]{1,0:T(8,128)(2,1)S(1)} %get-tuple-element.70), channel_id=1, source_target_pairs={{0,2},{2,0},{4,6},{6,4},{8,10},{10,8},{12,14},{14,12},{1,3},{3,1},... | collective-permute-start | bytes 786440 | tf_op jit(solution)/shard_map/ppermute | solution.py:335
  73.7 12.8 %collective-permute-start.17 = (bf16[3,128,256]{2,1,0:T(8,128)(2,1)S(1)}, bf16[3,128,256]{2,1,0:T(8,128)(2,1)S(1)}, u32[]{:S(2)}, u32[]{:S(2)}) collective-permute-start(bf16[3,128,256]{2,1,0:T(8,128)(2,1)S(1)} %get-tuple-element.71), channel_id=1, source_target_pairs={{0,32},{16,48},{32,0},{48,16},{64,96},{80,112},{96,64},{112,80},{1... | collective-permute-start | bytes 589832 | tf_op jit(solution)/shard_map/ppermute | solution.py:374
  77.2 9.6 %collective-permute-start.18 = (bf16[3,128,256]{2,1,0:T(8,128)(2,1)S(1)}, bf16[3,128,256]{2,1,0:T(8,128)(2,1)S(1)}, u32[]{:S(2)}, u32[]{:S(2)}) collective-permute-start(bf16[3,128,256]{2,1,0:T(8,128)(2,1)S(1)} %get-tuple-element.72), channel_id=1, source_target_pairs={{0,16},{16,32},{32,48},{48,0},{64,80},{80,96},{96,112},{112,64},{1... | collective-permute-start | bytes 589832 | tf_op jit(solution)/shard_map/ppermute | solution.py:374
  77.9 8.9 %collective-permute-start.19 = (bf16[3,128,256]{2,1,0:T(8,128)(2,1)S(1)}, bf16[3,128,256]{2,1,0:T(8,128)(2,1)S(1)}, u32[]{:S(2)}, u32[]{:S(2)}) collective-permute-start(bf16[3,128,256]{2,1,0:T(8,128)(2,1)S(1)} %get-tuple-element.73), channel_id=1, source_target_pairs={{0,48},{16,0},{32,16},{48,32},{64,112},{80,64},{96,80},{112,96},{1... | collective-permute-start | bytes 589832 | tf_op jit(solution)/shard_map/ppermute | solution.py:374
  79.8 16.1 %collective-permute-start.23 = (bf16[3,128,256]{2,1,0:T(8,128)(2,1)S(1)}, bf16[3,128,256]{2,1,0:T(8,128)(2,1)S(1)}, u32[]{:S(2)}, u32[]{:S(2)}) collective-permute-start(bf16[3,128,256]{2,1,0:T(8,128)(2,1)S(1)} %sum_over_z.2.after), channel_id=1, source_target_pairs={{64,0},{65,15},{66,64},{67,79},{68,4},{69,11},{70,68},{71,75},{72,... | collective-permute-start | bytes 589832 | tf_op jit(solution)/shard_map/ppermute | solution.py:361
  81.1 14.9 %collective-permute-start.22 = (bf16[3,128,256]{2,1,0:T(8,128)(2,1)S(1)}, bf16[3,128,256]{2,1,0:T(8,128)(2,1)S(1)}, u32[]{:S(2)}, u32[]{:S(2)}) collective-permute-start(bf16[3,128,256]{2,1,0:T(8,128)(2,1)S(1)} %sum_over_z.2.after), channel_id=1, source_target_pairs={{0,0},{1,15},{2,64},{3,79},{4,4},{5,11},{6,68},{7,75},{8,6},{9,9},... | collective-permute-start | bytes 589832 | tf_op jit(solution)/shard_map/ppermute | solution.py:361
  87.1 9.1 %collective-permute-start.21 = (bf16[3,128,256]{2,1,0:T(8,128)(2,1)S(1)}, bf16[3,128,256]{2,1,0:T(8,128)(2,1)S(1)}, u32[]{:S(2)}, u32[]{:S(2)}) collective-permute-start(bf16[3,128,256]{2,1,0:T(8,128)(2,1)S(1)} %sum_over_z.3), channel_id=1, source_target_pairs={{64,1},{65,14},{66,65},{67,78},{68,5},{69,10},{70,69},{71,74},{72,... | collective-permute-start | bytes 589832 | tf_op jit(solution)/shard_map/ppermute | solution.py:361
  87.8 14.1 %collective-permute-start.20 = (bf16[3,128,256]{2,1,0:T(8,128)(2,1)S(1)}, bf16[3,128,256]{2,1,0:T(8,128)(2,1)S(1)}, u32[]{:S(2)}, u32[]{:S(2)}) collective-permute-start(bf16[3,128,256]{2,1,0:T(8,128)(2,1)S(1)} %sum_over_z.3), channel_id=1, source_target_pairs={{0,1},{1,14},{2,65},{3,78},{4,5},{5,10},{6,69},{7,74},{8,7},{9,8},... | collective-permute-start | bytes 589832 | tf_op jit(solution)/shard_map/ppermute | solution.py:361

commit v16 on v15

--- a/solution.py
+++ b/solution.py
@@ -113,11 +113,6 @@
         copy.wait()
 
 
-def load_second_kernel(x_ref, after, x_out, sem):
-    for copy in load_inputs(1 - where_am_i()[1], 1, x_ref, x_out, sem):
-        copy.wait()
-
-
 def pair_kernel(own, got, after, out):
     outs = own.shape[1]
     out[0], out[1] = own[...], got[:, got.shape[1] - outs :]
@@ -127,25 +122,23 @@
     return x_ref[:, s * wide : (s + 1) * wide]
 
 
-def own_tokens(copies, x_out, gt_ref, part_out):
-    for s in range(2):
-        copies[s].wait()
-        part_out[s] = fisher_block(columns(s, x_out, part_out.shape[2]), gt_ref)
-
-
-def own_first_kernel(x_ref, g_ref, after, x_out, g_out, gt_out, part_out, sem, g_sem):
+def load_rest_kernel(
+    x_ref, g_ref, after, send_out, own_a_out, own_b_out, g_out, gt_out, part_a_out, part_b_out, sem, g_sem
+):
     core = where_am_i()[1]
     load = pltpu.make_async_copy(g_ref.at[core], g_out, g_sem)
     load.start()
-    copies = load_inputs(core, 0, x_ref, x_out, sem)
+    send = load_inputs(1 - core, 1, x_ref, send_out, sem.at[0])
+    own_a = load_inputs(core, 0, x_ref, own_a_out, sem.at[1])
+    own_b = load_inputs(core, 1, x_ref, own_b_out, sem.at[2])
     load.wait()
     gt_out[...] = squared_transposed(g_out[...])
-    own_tokens(copies, x_out, gt_out, part_out)
-
-
-def own_second_kernel(x_ref, gt_ref, after, x_out, part_out, sem):
-    copies = load_inputs(where_am_i()[1], 1, x_ref, x_out, sem)
-    own_tokens(copies, x_out, gt_ref, part_out)
+    for copies, x_out, part_out in ((own_a, own_a_out, part_a_out), (own_b, own_b_out, part_b_out)):
+        for s in range(2):
+            copies[s].wait()
+            part_out[s] = fisher_block(columns(s, x_out, part_out.shape[2]), gt_out)
+    for copy in send:
+        copy.wait()
 
 
 def add_first_kernel(x_ref, part_ref, after, two_out, one_out, gt_out):
@@ -377,23 +370,20 @@
         load_first_kernel, "load_to_swap", ((tokens, 4 * wide + outs), BF16), [inputs, grads], [], [dma((2,)), dma]
     )
     x_got0 = swap_cores(x_send0)
-    x_send1 = call(load_second_kernel, "load_to_swap", x_shape, [inputs], [x_send0], [dma((2,))])
+    x_send1, x_own0, x_own1, g_own, gt_own, part0, part1 = call(
+        load_rest_kernel, "load_and_fisher_of_own_tokens",
+        [x_shape, x_shape, x_shape, g_shape, gt_shape, part_shape, part_shape], [inputs, grads], [x_send0],
+        [dma((3, 2)), dma],
+    )
     x_got1 = swap_cores(x_send1)
-    x_own0, g_own, gt_own, part0 = call(
-        own_first_kernel, "fisher_of_own_tokens", [x_shape, g_shape, gt_shape, part_shape], [inputs, grads], [x_send1],
-        [dma((2,)), dma],
-    )
     g_pair = call(pair_kernel, "pair_grads", ((2, tokens, outs), BF16), [], [g_own, x_got0, gt_own])
     g_other = swap_cols(g_pair)
     two, one, gt_got = call(
         add_first_kernel, "fisher_of_both_cores", [sent_shape, sent_shape, gt_shape], [], [x_got0, part0, g_pair]
     )
     got0 = {2: swap_x(2, two), 1: swap_x(1, one)}
-    x_own1, part1 = call(
-        own_second_kernel, "fisher_of_own_tokens", [x_shape, part_shape], [inputs], [gt_own, two], [dma((2,))]
-    )
     three, sum0 = call(
-        add_second_kernel, "fisher_of_both_cores", [sent_shape, sum_shape], [], [x_got1, gt_got, part1, x_own1]
+        add_second_kernel, "fisher_of_both_cores", [sent_shape, sum_shape], [], [x_got1, gt_got, part1, two]
     )
     got0[3] = swap_x(3, three)
 

time: 103 us -> 106 us (1.029)
  waiting for transfers between devices: 31.5 us -> 38.9 us
  starting transfers between devices: 48.6 us -> 46.2 us
  Pallas kernels: 22.4 us -> 20.2 us
    ppermute x4, starting transfers between devices: 15.5 us -> 11 us  [results(): lax.ppermute(sums, ('member', 'tok', 'col'), result_pairs(phase, y_lo))]
    ppermute x5, starting transfers between devices: 4.27 us -> 7.94 us  [swap_cores(): return lax.ppermute(send, 'tok', [(t, t ^ 1) for t in range(8)])]
    ppermute x7, waiting for transfers between devices: 0.02 us -> 2.92 us  [swap_x(): return lax.ppermute(sent, 'tok', x_pairs(flip))]
    ppermute x4, waiting for transfers between devices: 5.73 us -> 8.05 us  [results(): lax.ppermute(sums, ('member', 'tok', 'col'), result_pairs(phase, y_lo))]
    pallas_call x20 -> x18, Pallas kernels: 21.6 us -> 19.3 us  [call(): pl.pallas_call(kernel, out_shape=shapes, in_specs=[HBM] * len(hbm) + [VME...]
    ppermute x7, starting transfers between devices: 9.1 us -> 7.51 us  [swap_x(): return lax.ppermute(sent, 'tok', x_pairs(flip))]
    ppermute x1, waiting for transfers between devices: 16.8 us -> 18.1 us  [swap_cols(): return lax.ppermute(send, 'col', [(0, 1), (1, 0)])]
  transfers between devices with their start and end apart: 24 -> 24, of which waited for: 8 -> 12; matrix products, arithmetic and copies ran while one was open for 0% -> 0% of each run, Pallas kernels for 18% -> 15%
where the time goes in v16:
time: 106 us
  starting transfers between devices  46.2 us (44%)
  waiting for transfers between devices  38.9 us (37%)
  Pallas kernels  20.2 us (19%)
    pallas_call x18, Pallas kernels, call(): pl.pallas_call(kernel, out_shape=shapes, in_specs=[HBM] * len(hbm) + [VME...  19.3 us
    ppermute x1, waiting for transfers between devices, swap_cols(): return lax.ppermute(send, 'col', [(0, 1), (1, 0)])  18.1 us
    ppermute x6, starting transfers between devices, weigh(): return [lax.ppermute(v, 'member', z_pairs(d)) for d, v in send] + [own_sums]  12.6 us
    ppermute x4, starting transfers between devices, results(): lax.ppermute(sums, ('member', 'tok', 'col'), result_pairs(phase, y_lo))  11 us
    ppermute x4, waiting for transfers between devices, results(): lax.ppermute(sums, ('member', 'tok', 'col'), result_pairs(phase, y_lo))  8.05 us
    ppermute x5, starting transfers between devices, swap_cores(): return lax.ppermute(send, 'tok', [(t, t ^ 1) for t in range(8)])  7.94 us
    ppermute x7, starting transfers between devices, swap_x(): return lax.ppermute(sent, 'tok', x_pairs(flip))  7.51 us
    ppermute x6, waiting for transfers between devices, weigh(): return [lax.ppermute(v, 'member', z_pairs(d)) for d, v in send] + [own_sums]  7.44 us
  transfers between devices with their start and end apart: 24, of which 12 were waited for; matrix products, arithmetic and copies ran while one was open for 0% of the time, Pallas kernels for 15%

profile of v16, /device:TPU:1, one launch (start us, length us, event | category | flops | bytes accessed | tf_op | source)
XLA Modules:
  0.0 105.6 jit_solution(4871719981445827356)
XLA Ops:
  0.0 2.0 %load_to_swap.1.after = bf16[768,2304]{1,0:T(8,128)(2,1)S(1)} custom-call(bf16[2,768,4096]{2,1,0:T(8,128)(2,1)} %x_ref.3, bf16[2,768,256]{2,1,0:T(8,128)(2,1)} %g_ref.3), custom_call_target="tpu_custom_call" | custom-call | flops 1 | bytes 1 | tf_op jit(solution)/shard_map/load_to_swap/pallas_call | solution.py:66
  2.1 1.5 %collective-permute-start = (bf16[768,2304]{1,0:T(8,128)(2,1)S(1)}, bf16[768,2304]{1,0:T(8,128)(2,1)S(1)}, u32[]{:S(2)}, u32[]{:S(2)}) collective-permute-start(bf16[768,2304]{1,0:T(8,128)(2,1)S(1)} %load_to_swap.1.after), channel_id=1, source_target_pairs={{0,2},{2,0},{4,6},{6,4},{8,10},{10,8},{12,14},{14,12},{1,3},{3,1},... | collective-permute-start | bytes 10616840 | tf_op jit(solution)/shard_map/ppermute | solution.py:328
  3.6 5.1 %load_and_fisher_of_own_tokens.1 = (bf16[768,2048]{1,0:T(8,128)(2,1)S(1)}, bf16[768,2048]{1,0:T(8,128)(2,1)S(1)}, bf16[768,2048]{1,0:T(8,128)(2,1)S(1)}, bf16[76...) custom-call(bf16[2,768,4096]{2,1,0:T(8,128)(2,1)} %x_ref.3, ...), custom_call_target="tpu_custom_call" | custom-call | flops 1 | bytes 1 | tf_op jit(solution)/shard_map/load_and_fisher_of_own_tokens/pallas_call | solution.py:66
  8.8 4.8 %collective-permute-start.7 = (bf16[2,1024,256]{2,1,0:T(8,128)(2,1)S(1)}, bf16[2,1024,256]{2,1,0:T(8,128)(2,1)S(1)}, u32[]{:S(2)}, u32[]{:S(2)}) collective-permute-start(bf16[2,1024,256]{2,1,0:T(8,128)(2,1)S(1)} %copy-done), channel_id=1, source_target_pairs={{0,0},{1,2},{2,12},{3,14},{4,4},{5,6},{6,8},{7,10},{8,9},{9,11},{1... | collective-permute-start | bytes 3145736 | tf_op jit(solution)/shard_map/ppermute | solution.py:357
  13.7 2.4 %collective-permute-start.2 = (bf16[2,768,256]{2,1,0:T(8,128)(2,1)S(1)}, bf16[2,768,256]{2,1,0:T(8,128)(2,1)S(1)}, u32[]{:S(2)}, u32[]{:S(2)}) collective-permute-start(bf16[2,768,256]{2,1,0:T(8,128)(2,1)S(1)} %pair_grads.1.after), channel_id=1, source_target_pairs={{0,1},{1,0},{2,3},{3,2},{4,5},{5,4},{6,7},{7,6},{8,9},{9,8},{10,11... | collective-permute-start | bytes 2359304 | tf_op jit(solution)/shard_map/ppermute | solution.py:331
  16.1 1.3 %fisher_of_both_cores.2 = (bf16[256,1024]{1,0:T(8,128)(2,1)S(1)}, bf16[256,1024]{1,0:T(8,128)(2,1)S(1)}, bf16[256,768]{1,0:T(8,128)(2,1)S(1)}) custom-call(bf16[768,2304]{1,0:T(8,128)(2,1)S(1)} %collective-permute-done.got.x_ref.got_a, f32[2,256,1024]{2,1,0:T(8,128)S(1)} %get-tuple-element.46.part_ref, bf16[2,768,256]{2,1,0:T(8,128)(2,1)S(1)} %pair_grads.1.after), custom_call_target="tpu_custom_call" | custom-call | flops 1 | bytes 1 | tf_op jit(solution)/shard_map/fisher_of_both_cores/pallas_call | solution.py:66
  17.4 1.1 %fisher_of_both_cores.3 = (bf16[256,1024]{1,0:T(8,128)(2,1)S(1)}, f32[256,1024]{1,0:T(8,128)S(1)}) custom-call(bf16[768,2048]{1,0:T(8,128)(2,1)S(1)} %collective-permute-done.1.x_ref.got_b, bf16[256,768]{1,0:T(8,128)(2,1)S(1)} %get-tuple-element.47.gt_ref, f32[2,256,1024]{2,1,0:T(8,128)S(1)} %get-tuple-element.48.part_ref, ...), custom_call_target="tpu_custom_call" | custom-call | flops 1 | bytes 1 | tf_op jit(solution)/shard_map/fisher_of_both_cores/pallas_call | solution.py:66
  18.5 0.5 collective-permute-start.6
  19.0 1.3 %collective-permute-start.5 = (bf16[256,1024]{1,0:T(8,128)(2,1)S(1)}, bf16[256,1024]{1,0:T(8,128)(2,1)S(1)}, u32[]{:S(2)}, u32[]{:S(2)}) collective-permute-start(bf16[256,1024]{1,0:T(8,128)(2,1)S(1)} %get-tuple-element.49.after), channel_id=1, source_target_pairs={{0,8},{2,10},{4,12},{6,14},{8,0},{10,2},{12,4},{14,6},{1,9},{3,11}... | collective-permute-start | bytes 1572872 | tf_op jit(solution)/shard_map/ppermute | solution.py:334
  20.3 1.5 %collective-permute-start.4 = (bf16[256,1024]{1,0:T(8,128)(2,1)S(1)}, bf16[256,1024]{1,0:T(8,128)(2,1)S(1)}, u32[]{:S(2)}, u32[]{:S(2)}) collective-permute-start(bf16[256,1024]{1,0:T(8,128)(2,1)S(1)} %get-tuple-element.54), channel_id=1, source_target_pairs={{0,4},{2,6},{4,0},{6,2},{8,12},{10,14},{12,8},{14,10},{1,5},{3,7},... | collective-permute-start | bytes 1572872 | tf_op jit(solution)/shard_map/ppermute | solution.py:334
  21.9 18.1 %collective-permute-done.2.g_ref = bf16[2,768,256]{2,1,0:T(8,128)(2,1)S(1)} collective-permute-done((bf16[2,768,256]{2,1,0:T(8,128)(2,1)S(1)}, bf16[2,768,256]{2,1,0:T(8,128)(2,1)S(1)}, u32[]{:S(2)}, u32[]{:S(2)}) %collective-permute-start.2) | collective-permute-done | bytes 786464 | tf_op jit(solution)/shard_map/ppermute | solution.py:331
  40.0 1.9 %fisher_of_other_grads.2 = (bf16[2,256,512]{2,1,0:T(8,128)(2,1)S(1)}, f32[2,256,512]{2,1,0:T(8,128)S(1)}, bf16[256,768]{1,0:T(8,128)(2,1)S(1)}, bf16[256,768]{1,0:T(8,128)(2,1)S(1)}) custom-call(bf16[768,2048]{1,0:T(8,128)(2,1)S(1)} %get-tuple-element.41.own_a, bf16[768,2304]{1,0:T(8,128)(2,1)S(1)} %collective-permute-done.got.x_ref.got_a, ...), custom_call_target="tpu_custom_call" | custom-call | flops 1 | bytes 1 | tf_op jit(solution)/shard_map/fisher_of_other_grads/pallas_call | solution.py:66
  42.0 4.0 %collective-permute-start.9 = (bf16[2,512,256]{2,1,0:T(8,128)(2,1)S(1)}, bf16[2,512,256]{2,1,0:T(8,128)(2,1)S(1)}, u32[]{:S(2)}, u32[]{:S(2)}) collective-permute-start(bf16[2,512,256]{2,1,0:T(8,128)(2,1)S(1)} %get-tuple-element.61), channel_id=1, source_target_pairs={{0,2},{2,0},{4,6},{6,4},{8,10},{10,8},{12,14},{14,12},{1,3},{3,1},... | collective-permute-start | bytes 1572872 | tf_op jit(solution)/shard_map/ppermute | solution.py:328
  46.1 1.3 %collective-permute-start.3 = (bf16[2,256,512]{2,1,0:T(8,128)(2,1)S(1)}, bf16[2,256,512]{2,1,0:T(8,128)(2,1)S(1)}, u32[]{:S(2)}, u32[]{:S(2)}) collective-permute-start(bf16[2,256,512]{2,1,0:T(8,128)(2,1)S(1)} %get-tuple-element.52), channel_id=1, source_target_pairs={{0,4},{2,6},{4,0},{6,2},{8,12},{10,14},{12,8},{14,10},{1,5},{3,7},... | collective-permute-start | bytes 1572872 | tf_op jit(solution)/shard_map/ppermute | solution.py:334
  47.4 1.9 %fisher_of_other_grads.3 = (bf16[2,256,512]{2,1,0:T(8,128)(2,1)S(1)}, f32[2,256,512]{2,1,0:T(8,128)S(1)}) custom-call(bf16[768,2048]{1,0:T(8,128)(2,1)S(1)} %get-tuple-element.41.own_a, bf16[768,2304]{1,0:T(8,128)(2,1)S(1)} %collective-permute-done.got.x_ref.got_a, bf16[768,2048]{1,0:T(8,128)(2,1)S(1)} %get-tuple-element.42.own_b, ...), custom_call_target="tpu_custom_call" | custom-call | flops 1 | bytes 1 | tf_op jit(solution)/shard_map/fisher_of_other_grads/pallas_call | solution.py:66
  49.3 1.7 %collective-permute-done.6.three = bf16[256,1024]{1,0:T(8,128)(2,1)S(1)} collective-permute-done((bf16[256,1024]{1,0:T(8,128)(2,1)S(1)}, bf16[256,1024]{1,0:T(8,128)(2,1)S(1)}, u32[]{:S(2)}, u32[]{:S(2)}) %collective-permute-start.6) | collective-permute-done | bytes 524320 | tf_op jit(solution)/shard_map/ppermute | solution.py:334
  51.0 1.1 %collective-permute-start.14 = (bf16[2,256,512]{2,1,0:T(8,128)(2,1)S(1)}, bf16[2,256,512]{2,1,0:T(8,128)(2,1)S(1)}, u32[]{:S(2)}, u32[]{:S(2)}) collective-permute-start(bf16[2,256,512]{2,1,0:T(8,128)(2,1)S(1)} %get-tuple-element.68), channel_id=1, source_target_pairs={{0,12},{2,14},{4,8},{6,10},{8,4},{10,6},{12,0},{14,2},{1,13},{3,15... | collective-permute-start | bytes 1572872 | tf_op jit(solution)/shard_map/ppermute | solution.py:334
  52.2 1.6 %fisher_over_tokens.3 = (f32[256,512]{1,0:T(8,128)S(1)}, bf16[256,512]{1,0:T(8,128)(2,1)S(1)}) custom-call(f32[256,1024]{1,0:T(8,128)S(1)} %get-tuple-element.53.own, bf16[256,1024]{1,0:T(8,128)(2,1)S(1)} %collective-permute-done.4.one, bf16[256,1024]{1,0:T(8,128)(2,1)S(1)} %collective-permute-done.5.two, ...), custom_call_target="tpu_custom_call" | custom-call | flops 1 | bytes 1 | tf_op jit(solution)/shard_map/fisher_over_tokens/pallas_call | solution.py:66
  53.8 0.6 collective-permute-start.8
  54.4 1.2 %collective-permute-done.8.refs_1_ = bf16[256,512]{1,0:T(8,128)(2,1)S(1)} collective-permute-done((bf16[256,512]{1,0:T(8,128)(2,1)S(1)}, bf16[256,512]{1,0:T(8,128)(2,1)S(1)}, u32[]{:S(2)}, u32[]{:S(2)}) %collective-permute-start.8) | collective-permute-done | bytes 262176 | tf_op jit(solution)/shard_map/ppermute | solution.py:328
  55.6 0.5 weigh_members.2
  56.1 3.7 %collective-permute-start.11 = (f32[2,128,256]{2,1,0:T(8,128)S(1)}, f32[2,128,256]{2,1,0:T(8,128)S(1)}, u32[]{:S(2)}, u32[]{:S(2)}) collective-permute-start(f32[2,128,256]{2,1,0:T(8,128)S(1)} %get-tuple-element.65), channel_id=1, source_target_pairs={{0,32},{16,48},{32,0},{48,16},{64,96},{80,112},{96,64},{112,80},{1... | collective-permute-start | bytes 786440 | tf_op jit(solution)/shard_map/ppermute | solution.py:367
  59.8 0.7 collective-permute-start.12
  60.5 1.9 %collective-permute-start.13 = (f32[2,128,256]{2,1,0:T(8,128)S(1)}, f32[2,128,256]{2,1,0:T(8,128)S(1)}, u32[]{:S(2)}, u32[]{:S(2)}) collective-permute-start(f32[2,128,256]{2,1,0:T(8,128)S(1)} %get-tuple-element.67), channel_id=1, source_target_pairs={{0,48},{16,0},{32,16},{48,32},{64,112},{80,64},{96,80},{112,96},{1... | collective-permute-start | bytes 786440 | tf_op jit(solution)/shard_map/ppermute | solution.py:367
  62.4 0.7 fisher_over_first_swap.2
  63.2 1.6 %collective-permute-start.10 = (bf16[256,512]{1,0:T(8,128)(2,1)S(1)}, bf16[256,512]{1,0:T(8,128)(2,1)S(1)}, u32[]{:S(2)}, u32[]{:S(2)}) collective-permute-start(bf16[256,512]{1,0:T(8,128)(2,1)S(1)} %get-tuple-element.64), channel_id=1, source_target_pairs={{0,12},{2,14},{4,8},{6,10},{8,4},{10,6},{12,0},{14,2},{1,13},{3,15... | collective-permute-start | bytes 786440 | tf_op jit(solution)/shard_map/ppermute | solution.py:334
  64.8 0.5 collective-permute-done.14.got_ref
  65.4 0.7 fisher_over_first_swap.3
  66.2 6.0 %collective-permute-done.12.two = f32[2,128,256]{2,1,0:T(8,128)S(1)} collective-permute-done((f32[2,128,256]{2,1,0:T(8,128)S(1)}, f32[2,128,256]{2,1,0:T(8,128)S(1)}, u32[]{:S(2)}, u32[]{:S(2)}) %collective-permute-start.12) | collective-permute-done | bytes 262176 | tf_op jit(solution)/shard_map/ppermute | solution.py:367
  72.4 0.3 fisher_over_tokens.4.first_ref
  72.6 0.6 collective-permute-done.15.got
  73.3 0.6 fisher_over_tokens.5
  73.9 1.7 %collective-permute-start.16 = (bf16[256,512]{1,0:T(8,128)(2,1)S(1)}, bf16[256,512]{1,0:T(8,128)(2,1)S(1)}, u32[]{:S(2)}, u32[]{:S(2)}) collective-permute-start(bf16[256,512]{1,0:T(8,128)(2,1)S(1)} %get-tuple-element.72), channel_id=1, source_target_pairs={{0,2},{2,0},{4,6},{6,4},{8,10},{10,8},{12,14},{14,12},{1,3},{3,1},... | collective-permute-start | bytes 786440 | tf_op jit(solution)/shard_map/ppermute | solution.py:328
  75.6 1.2 %collective-permute-done.16.refs_1_ = bf16[256,512]{1,0:T(8,128)(2,1)S(1)} collective-permute-done((bf16[256,512]{1,0:T(8,128)(2,1)S(1)}, bf16[256,512]{1,0:T(8,128)(2,1)S(1)}, u32[]{:S(2)}, u32[]{:S(2)}) %collective-permute-start.16) | collective-permute-done | bytes 262176 | tf_op jit(solution)/shard_map/ppermute | solution.py:328
  76.7 0.7 weigh_members.3
  77.5 3.5 %collective-permute-start.17 = (bf16[3,128,256]{2,1,0:T(8,128)(2,1)S(1)}, bf16[3,128,256]{2,1,0:T(8,128)(2,1)S(1)}, u32[]{:S(2)}, u32[]{:S(2)}) collective-permute-start(bf16[3,128,256]{2,1,0:T(8,128)(2,1)S(1)} %get-tuple-element.73), channel_id=1, source_target_pairs={{0,32},{16,48},{32,0},{48,16},{64,96},{80,112},{96,64},{112,80},{1... | collective-permute-start | bytes 589832 | tf_op jit(solution)/shard_map/ppermute | solution.py:367
  81.0 0.9 collective-permute-start.18
  81.9 1.8 %collective-permute-start.19 = (bf16[3,128,256]{2,1,0:T(8,128)(2,1)S(1)}, bf16[3,128,256]{2,1,0:T(8,128)(2,1)S(1)}, u32[]{:S(2)}, u32[]{:S(2)}) collective-permute-start(bf16[3,128,256]{2,1,0:T(8,128)(2,1)S(1)} %get-tuple-element.75), channel_id=1, source_target_pairs={{0,48},{16,0},{32,16},{48,32},{64,112},{80,64},{96,80},{112,96},{1... | collective-permute-start | bytes 589832 | tf_op jit(solution)/shard_map/ppermute | solution.py:367
  83.7 4.4 %collective-permute-start.22 = (bf16[3,128,256]{2,1,0:T(8,128)(2,1)S(1)}, bf16[3,128,256]{2,1,0:T(8,128)(2,1)S(1)}, u32[]{:S(2)}, u32[]{:S(2)}) collective-permute-start(bf16[3,128,256]{2,1,0:T(8,128)(2,1)S(1)} %sum_over_z.2.after), channel_id=1, source_target_pairs={{0,0},{1,15},{2,64},{3,79},{4,4},{5,11},{6,68},{7,75},{8,6},{9,9},... | collective-permute-start | bytes 589832 | tf_op jit(solution)/shard_map/ppermute | solution.py:354
  88.0 1.3 %collective-permute-start.23 = (bf16[3,128,256]{2,1,0:T(8,128)(2,1)S(1)}, bf16[3,128,256]{2,1,0:T(8,128)(2,1)S(1)}, u32[]{:S(2)}, u32[]{:S(2)}) collective-permute-start(bf16[3,128,256]{2,1,0:T(8,128)(2,1)S(1)} %sum_over_z.2.after), channel_id=1, source_target_pairs={{64,0},{65,15},{66,64},{67,79},{68,4},{69,11},{70,68},{71,75},{72,... | collective-permute-start | bytes 589832 | tf_op jit(solution)/shard_map/ppermute | solution.py:354
  89.4 1.2 %collective-permute-done.18.two = bf16[3,128,256]{2,1,0:T(8,128)(2,1)S(1)} collective-permute-done((bf16[3,128,256]{2,1,0:T(8,128)(2,1)S(1)}, bf16[3,128,256]{2,1,0:T(8,128)(2,1)S(1)}, u32[]{:S(2)}, u32[]{:S(2)}) %collective-permute-start.18) | collective-permute-done | bytes 196640 | tf_op jit(solution)/shard_map/ppermute | solution.py:367
  90.6 0.2 collective-permute-done.19.three
  90.8 0.3 sum_over_z.3
  91.1 4.7 %collective-permute-start.20 = (bf16[3,128,256]{2,1,0:T(8,128)(2,1)S(1)}, bf16[3,128,256]{2,1,0:T(8,128)(2,1)S(1)}, u32[]{:S(2)}, u32[]{:S(2)}) collective-permute-start(bf16[3,128,256]{2,1,0:T(8,128)(2,1)S(1)} %sum_over_z.3), channel_id=1, source_target_pairs={{0,1},{1,14},{2,65},{3,78},{4,5},{5,10},{6,69},{7,74},{8,7},{9,8},... | collective-permute-start | bytes 589832 | tf_op jit(solution)/shard_map/ppermute | solution.py:354
  95.8 0.7 collective-permute-start.21
  96.5 0.7 collective-permute-done.23.far
  97.3 7.4 %collective-permute-done.20.near = bf16[3,128,256]{2,1,0:T(8,128)(2,1)S(1)} collective-permute-done((bf16[3,128,256]{2,1,0:T(8,128)(2,1)S(1)}, bf16[3,128,256]{2,1,0:T(8,128)(2,1)S(1)}, u32[]{:S(2)}, u32[]{:S(2)}) %collective-permute-start.20) | collective-permute-done | bytes 196640 | tf_op jit(solution)/shard_map/ppermute | solution.py:354
  104.7 0.8 merge_members.1
  (21 shorter events, 0.7 us)
Async XLA Ops:
  2.1 6.7 %copy-start = (bf16[2,1024,256]{2,1,0:T(8,128)(2,1)S(1)}, bf16[2,1024,256]{2,1,0:T(8,128)(2,1)}, u32[]{:S(2)}) copy-start(bf16[2,1024,256]{2,1,0:T(8,128)(2,1)} %param.5) | copy-start | bytes 3145732
  2.1 11.6 %collective-permute-start = (bf16[768,2304]{1,0:T(8,128)(2,1)S(1)}, bf16[768,2304]{1,0:T(8,128)(2,1)S(1)}, u32[]{:S(2)}, u32[]{:S(2)}) collective-permute-start(bf16[768,2304]{1,0:T(8,128)(2,1)S(1)} %load_to_swap.1.after), channel_id=1, source_target_pairs={{0,2},{2,0},{4,6},{6,4},{8,10},{10,8},{12,14},{14,12},{1,3},{3,1},... | collective-permute-start | bytes 10616840 | tf_op jit(solution)/shard_map/ppermute | solution.py:328
  8.7 8.7 %collective-permute-start.1 = (bf16[768,2048]{1,0:T(8,128)(2,1)S(1)}, bf16[768,2048]{1,0:T(8,128)(2,1)S(1)}, u32[]{:S(2)}, u32[]{:S(2)}) collective-permute-start(bf16[768,2048]{1,0:T(8,128)(2,1)S(1)} %get-tuple-element.43), channel_id=1, source_target_pairs={{0,2},{2,0},{4,6},{6,4},{8,10},{10,8},{12,14},{14,12},{1,3},{3,1},... | collective-permute-start | bytes 9437192 | tf_op jit(solution)/shard_map/ppermute | solution.py:328
  8.8 33.1 %collective-permute-start.7 = (bf16[2,1024,256]{2,1,0:T(8,128)(2,1)S(1)}, bf16[2,1024,256]{2,1,0:T(8,128)(2,1)S(1)}, u32[]{:S(2)}, u32[]{:S(2)}) collective-permute-start(bf16[2,1024,256]{2,1,0:T(8,128)(2,1)S(1)} %copy-done), channel_id=1, source_target_pairs={{0,0},{1,2},{2,12},{3,14},{4,4},{5,6},{6,8},{7,10},{8,9},{9,11},{1... | collective-permute-start | bytes 3145736 | tf_op jit(solution)/shard_map/ppermute | solution.py:357
  13.7 26.3 %collective-permute-start.2 = (bf16[2,768,256]{2,1,0:T(8,128)(2,1)S(1)}, bf16[2,768,256]{2,1,0:T(8,128)(2,1)S(1)}, u32[]{:S(2)}, u32[]{:S(2)}) collective-permute-start(bf16[2,768,256]{2,1,0:T(8,128)(2,1)S(1)} %pair_grads.1.after), channel_id=1, source_target_pairs={{0,1},{1,0},{2,3},{3,2},{4,5},{5,4},{6,7},{7,6},{8,9},{9,8},{10,11... | collective-permute-start | bytes 2359304 | tf_op jit(solution)/shard_map/ppermute | solution.py:331
  18.5 32.5 %collective-permute-start.6 = (bf16[256,1024]{1,0:T(8,128)(2,1)S(1)}, bf16[256,1024]{1,0:T(8,128)(2,1)S(1)}, u32[]{:S(2)}, u32[]{:S(2)}) collective-permute-start(bf16[256,1024]{1,0:T(8,128)(2,1)S(1)} %get-tuple-element.50.after), channel_id=1, source_target_pairs={{0,12},{2,14},{4,8},{6,10},{8,4},{10,6},{12,0},{14,2},{1,13},{3,15... | collective-permute-start | bytes 1572872 | tf_op jit(solution)/shard_map/ppermute | solution.py:334
  19.0 33.2 %collective-permute-start.5 = (bf16[256,1024]{1,0:T(8,128)(2,1)S(1)}, bf16[256,1024]{1,0:T(8,128)(2,1)S(1)}, u32[]{:S(2)}, u32[]{:S(2)}) collective-permute-start(bf16[256,1024]{1,0:T(8,128)(2,1)S(1)} %get-tuple-element.49.after), channel_id=1, source_target_pairs={{0,8},{2,10},{4,12},{6,14},{8,0},{10,2},{12,4},{14,6},{1,9},{3,11}... | collective-permute-start | bytes 1572872 | tf_op jit(solution)/shard_map/ppermute | solution.py:334
  20.3 31.8 %collective-permute-start.4 = (bf16[256,1024]{1,0:T(8,128)(2,1)S(1)}, bf16[256,1024]{1,0:T(8,128)(2,1)S(1)}, u32[]{:S(2)}, u32[]{:S(2)}) collective-permute-start(bf16[256,1024]{1,0:T(8,128)(2,1)S(1)} %get-tuple-element.54), channel_id=1, source_target_pairs={{0,4},{2,6},{4,0},{6,2},{8,12},{10,14},{12,8},{14,10},{1,5},{3,7},... | collective-permute-start | bytes 1572872 | tf_op jit(solution)/shard_map/ppermute | solution.py:334
  42.0 13.6 %collective-permute-start.9 = (bf16[2,512,256]{2,1,0:T(8,128)(2,1)S(1)}, bf16[2,512,256]{2,1,0:T(8,128)(2,1)S(1)}, u32[]{:S(2)}, u32[]{:S(2)}) collective-permute-start(bf16[2,512,256]{2,1,0:T(8,128)(2,1)S(1)} %get-tuple-element.61), channel_id=1, source_target_pairs={{0,2},{2,0},{4,6},{6,4},{8,10},{10,8},{12,14},{14,12},{1,3},{3,1},... | collective-permute-start | bytes 1572872 | tf_op jit(solution)/shard_map/ppermute | solution.py:328
  46.1 16.4 %collective-permute-start.3 = (bf16[2,256,512]{2,1,0:T(8,128)(2,1)S(1)}, bf16[2,256,512]{2,1,0:T(8,128)(2,1)S(1)}, u32[]{:S(2)}, u32[]{:S(2)}) collective-permute-start(bf16[2,256,512]{2,1,0:T(8,128)(2,1)S(1)} %get-tuple-element.52), channel_id=1, source_target_pairs={{0,4},{2,6},{4,0},{6,2},{8,12},{10,14},{12,8},{14,10},{1,5},{3,7},... | collective-permute-start | bytes 1572872 | tf_op jit(solution)/shard_map/ppermute | solution.py:334
  51.0 14.3 %collective-permute-start.14 = (bf16[2,256,512]{2,1,0:T(8,128)(2,1)S(1)}, bf16[2,256,512]{2,1,0:T(8,128)(2,1)S(1)}, u32[]{:S(2)}, u32[]{:S(2)}) collective-permute-start(bf16[2,256,512]{2,1,0:T(8,128)(2,1)S(1)} %get-tuple-element.68), channel_id=1, source_target_pairs={{0,12},{2,14},{4,8},{6,10},{8,4},{10,6},{12,0},{14,2},{1,13},{3,15... | collective-permute-start | bytes 1572872 | tf_op jit(solution)/shard_map/ppermute | solution.py:334
  53.8 1.8 %collective-permute-start.8 = (bf16[256,512]{1,0:T(8,128)(2,1)S(1)}, bf16[256,512]{1,0:T(8,128)(2,1)S(1)}, u32[]{:S(2)}, u32[]{:S(2)}) collective-permute-start(bf16[256,512]{1,0:T(8,128)(2,1)S(1)} %get-tuple-element.60), channel_id=1, source_target_pairs={{0,2},{2,0},{4,6},{6,4},{8,10},{10,8},{12,14},{14,12},{1,3},{3,1},... | collective-permute-start | bytes 786440 | tf_op jit(solution)/shard_map/ppermute | solution.py:328
  56.1 10.1 %collective-permute-start.11 = (f32[2,128,256]{2,1,0:T(8,128)S(1)}, f32[2,128,256]{2,1,0:T(8,128)S(1)}, u32[]{:S(2)}, u32[]{:S(2)}) collective-permute-start(f32[2,128,256]{2,1,0:T(8,128)S(1)} %get-tuple-element.65), channel_id=1, source_target_pairs={{0,32},{16,48},{32,0},{48,16},{64,96},{80,112},{96,64},{112,80},{1... | collective-permute-start | bytes 786440 | tf_op jit(solution)/shard_map/ppermute | solution.py:367
  59.8 12.4 %collective-permute-start.12 = (f32[2,128,256]{2,1,0:T(8,128)S(1)}, f32[2,128,256]{2,1,0:T(8,128)S(1)}, u32[]{:S(2)}, u32[]{:S(2)}) collective-permute-start(f32[2,128,256]{2,1,0:T(8,128)S(1)} %get-tuple-element.66), channel_id=1, source_target_pairs={{0,16},{16,32},{32,48},{48,0},{64,80},{80,96},{96,112},{112,64},{1... | collective-permute-start | bytes 786440 | tf_op jit(solution)/shard_map/ppermute | solution.py:367
  60.5 11.7 %collective-permute-start.13 = (f32[2,128,256]{2,1,0:T(8,128)S(1)}, f32[2,128,256]{2,1,0:T(8,128)S(1)}, u32[]{:S(2)}, u32[]{:S(2)}) collective-permute-start(f32[2,128,256]{2,1,0:T(8,128)S(1)} %get-tuple-element.67), channel_id=1, source_target_pairs={{0,48},{16,0},{32,16},{48,32},{64,112},{80,64},{96,80},{112,96},{1... | collective-permute-start | bytes 786440 | tf_op jit(solution)/shard_map/ppermute | solution.py:367
  63.2 9.2 %collective-permute-start.10 = (bf16[256,512]{1,0:T(8,128)(2,1)S(1)}, bf16[256,512]{1,0:T(8,128)(2,1)S(1)}, u32[]{:S(2)}, u32[]{:S(2)}) collective-permute-start(bf16[256,512]{1,0:T(8,128)(2,1)S(1)} %get-tuple-element.64), channel_id=1, source_target_pairs={{0,12},{2,14},{4,8},{6,10},{8,4},{10,6},{12,0},{14,2},{1,13},{3,15... | collective-permute-start | bytes 786440 | tf_op jit(solution)/shard_map/ppermute | solution.py:334
  66.1 7.2 %collective-permute-start.15 = (bf16[256,512]{1,0:T(8,128)(2,1)S(1)}, bf16[256,512]{1,0:T(8,128)(2,1)S(1)}, u32[]{:S(2)}, u32[]{:S(2)}) collective-permute-start(bf16[256,512]{1,0:T(8,128)(2,1)S(1)} %get-tuple-element.70), channel_id=1, source_target_pairs={{0,4},{2,6},{4,0},{6,2},{8,12},{10,14},{12,8},{14,10},{1,5},{3,7},... | collective-permute-start | bytes 786440 | tf_op jit(solution)/shard_map/ppermute | solution.py:334
  73.9 2.8 %collective-permute-start.16 = (bf16[256,512]{1,0:T(8,128)(2,1)S(1)}, bf16[256,512]{1,0:T(8,128)(2,1)S(1)}, u32[]{:S(2)}, u32[]{:S(2)}) collective-permute-start(bf16[256,512]{1,0:T(8,128)(2,1)S(1)} %get-tuple-element.72), channel_id=1, source_target_pairs={{0,2},{2,0},{4,6},{6,4},{8,10},{10,8},{12,14},{14,12},{1,3},{3,1},... | collective-permute-start | bytes 786440 | tf_op jit(solution)/shard_map/ppermute | solution.py:328
  77.5 11.9 %collective-permute-start.17 = (bf16[3,128,256]{2,1,0:T(8,128)(2,1)S(1)}, bf16[3,128,256]{2,1,0:T(8,128)(2,1)S(1)}, u32[]{:S(2)}, u32[]{:S(2)}) collective-permute-start(bf16[3,128,256]{2,1,0:T(8,128)(2,1)S(1)} %get-tuple-element.73), channel_id=1, source_target_pairs={{0,32},{16,48},{32,0},{48,16},{64,96},{80,112},{96,64},{112,80},{1... | collective-permute-start | bytes 589832 | tf_op jit(solution)/shard_map/ppermute | solution.py:367
  81.0 9.6 %collective-permute-start.18 = (bf16[3,128,256]{2,1,0:T(8,128)(2,1)S(1)}, bf16[3,128,256]{2,1,0:T(8,128)(2,1)S(1)}, u32[]{:S(2)}, u32[]{:S(2)}) collective-permute-start(bf16[3,128,256]{2,1,0:T(8,128)(2,1)S(1)} %get-tuple-element.74), channel_id=1, source_target_pairs={{0,16},{16,32},{32,48},{48,0},{64,80},{80,96},{96,112},{112,64},{1... | collective-permute-start | bytes 589832 | tf_op jit(solution)/shard_map/ppermute | solution.py:367
  81.9 8.9 %collective-permute-start.19 = (bf16[3,128,256]{2,1,0:T(8,128)(2,1)S(1)}, bf16[3,128,256]{2,1,0:T(8,128)(2,1)S(1)}, u32[]{:S(2)}, u32[]{:S(2)}) collective-permute-start(bf16[3,128,256]{2,1,0:T(8,128)(2,1)S(1)} %get-tuple-element.75), channel_id=1, source_target_pairs={{0,48},{16,0},{32,16},{48,32},{64,112},{80,64},{96,80},{112,96},{1... | collective-permute-start | bytes 589832 | tf_op jit(solution)/shard_map/ppermute | solution.py:367
  83.7 12.8 %collective-permute-start.22 = (bf16[3,128,256]{2,1,0:T(8,128)(2,1)S(1)}, bf16[3,128,256]{2,1,0:T(8,128)(2,1)S(1)}, u32[]{:S(2)}, u32[]{:S(2)}) collective-permute-start(bf16[3,128,256]{2,1,0:T(8,128)(2,1)S(1)} %sum_over_z.2.after), channel_id=1, source_target_pairs={{0,0},{1,15},{2,64},{3,79},{4,4},{5,11},{6,68},{7,75},{8,6},{9,9},... | collective-permute-start | bytes 589832 | tf_op jit(solution)/shard_map/ppermute | solution.py:354
  88.0 9.1 %collective-permute-start.23 = (bf16[3,128,256]{2,1,0:T(8,128)(2,1)S(1)}, bf16[3,128,256]{2,1,0:T(8,128)(2,1)S(1)}, u32[]{:S(2)}, u32[]{:S(2)}) collective-permute-start(bf16[3,128,256]{2,1,0:T(8,128)(2,1)S(1)} %sum_over_z.2.after), channel_id=1, source_target_pairs={{64,0},{65,15},{66,64},{67,79},{68,4},{69,11},{70,68},{71,75},{72,... | collective-permute-start | bytes 589832 | tf_op jit(solution)/shard_map/ppermute | solution.py:354
  91.1 13.6 %collective-permute-start.20 = (bf16[3,128,256]{2,1,0:T(8,128)(2,1)S(1)}, bf16[3,128,256]{2,1,0:T(8,128)(2,1)S(1)}, u32[]{:S(2)}, u32[]{:S(2)}) collective-permute-start(bf16[3,128,256]{2,1,0:T(8,128)(2,1)S(1)} %sum_over_z.3), channel_id=1, source_target_pairs={{0,1},{1,14},{2,65},{3,78},{4,5},{5,10},{6,69},{7,74},{8,7},{9,8},... | collective-permute-start | bytes 589832 | tf_op jit(solution)/shard_map/ppermute | solution.py:354
  95.8 8.9 %collective-permute-start.21 = (bf16[3,128,256]{2,1,0:T(8,128)(2,1)S(1)}, bf16[3,128,256]{2,1,0:T(8,128)(2,1)S(1)}, u32[]{:S(2)}, u32[]{:S(2)}) collective-permute-start(bf16[3,128,256]{2,1,0:T(8,128)(2,1)S(1)} %sum_over_z.3), channel_id=1, source_target_pairs={{64,1},{65,14},{66,65},{67,78},{68,5},{69,10},{70,69},{71,74},{72,... | collective-permute-start | bytes 589832 | tf_op jit(solution)/shard_map/ppermute | solution.py:354

commit v17 on v15

--- a/solution.py
+++ b/solution.py
@@ -291,12 +291,12 @@
     return 2 * (x % 2) if x // 2 == half else 2 * ((3 - x) % 2) + 1
 
 
-def weight_pairs():
+def weight_pairs(phase):
     pairs = []
     for tok in range(X * CORES):
         half, local = divmod(tok, 4)
-        for col in range(2):
-            pairs.append((tok * 2 + col, (keeper(local, half) * 2 + col) * 2 + half))
+        col = half ^ phase
+        pairs.append((tok * 2 + col, (keeper(local, half) * 2 + col) * 2 + half))
     return pairs
 
 
@@ -360,8 +360,8 @@
     def results(phase, sums):
         return [lax.ppermute(sums, ("member", "tok", "col"), result_pairs(phase, y_lo)) for y_lo in range(2)]
 
-    def bring_weights(after):
-        arrived = lax.ppermute(weights, ("tok", "col"), weight_pairs())
+    def bring_weights(phase, after):
+        arrived = lax.ppermute(weights, ("tok", "col"), weight_pairs(phase))
         half_shape = ((2, weights.shape[1] // 2, outs), BF16)
         own, send = call(split_kernel, "split_weights", [half_shape, half_shape], [], [arrived, after])
         return own, swap_cores(send)
@@ -402,19 +402,20 @@
         both_first_kernel, "fisher_of_other_grads", [pair_shape, kept_shape, gt_shape, gt_shape], [], [*xs, g_other, three]
     )
     swap10 = swap_x(1, sent)
-    moved = bring_weights(kept10)
+    w0 = bring_weights(0, kept10)
     sent, kept11 = call(
-        both_second_kernel, "fisher_of_other_grads", [pair_shape, kept_shape], [], [*xs, gt_own, gt_got, moved[0]]
+        both_second_kernel, "fisher_of_other_grads", [pair_shape, kept_shape], [], [*xs, gt_own, gt_got, w0[0]]
     )
     swap11 = swap_x(3, sent)
 
     own0, other0 = join_direct(sum0, got0, kept11)
-    words0 = weigh(0, own0, other0, moved, own0)
+    words0 = weigh(0, own0, other0, w0, own0)
     part10 = middle(3, swap10, kept10, words0[3])
     part11 = middle(1, swap11, kept11, part10[0])
-    first = call(sum_wide_kernel, "sum_over_z", words, [], [*words0, part11[0]])
+    w1 = bring_weights(1, part11[0])
+    first = call(sum_wide_kernel, "sum_over_z", words, [], [*words0, w1[0]])
     own1, other1 = join(settle(part10, first), part11, first)
-    words1 = weigh(1, own1, other1, moved, own1)
+    words1 = weigh(1, own1, other1, w1, own1)
     met = call(meet_kernel, "meet_over_y", sums, [], [*results(0, first), own1])
     second = call(sum_kernel, "sum_over_z", words, [], [*words1, own1])
     near, far = results(1, second)

time: 103 us -> 112 us (1.087); the launches traced: 103 us -> 110 us
  waiting for transfers between devices: 31.5 us -> 49.1 us
  starting transfers between devices: 48.6 us -> 38.5 us
    ppermute x7, waiting for transfers between devices: 0.02 us -> 22.6 us  [swap_x(): return lax.ppermute(sent, 'tok', x_pairs(flip))]
    ppermute x4, starting transfers between devices: 15.5 us -> 6.2 us  [results(): lax.ppermute(sums, ('member', 'tok', 'col'), result_pairs(phase, y_lo))]
    ppermute x1, waiting for transfers between devices: 16.8 us -> 8.44 us  [swap_cols(): return lax.ppermute(send, 'col', [(0, 1), (1, 0)])]
    ppermute x1, starting transfers between devices: 2.47 us -> 0.09 us  [swap_cols(): return lax.ppermute(send, 'col', [(0, 1), (1, 0)])]
    ppermute x4, waiting for transfers between devices: 5.73 us -> 8.05 us  [results(): lax.ppermute(sums, ('member', 'tok', 'col'), result_pairs(phase, y_lo))]
    ppermute x5 -> x6, starting transfers between devices: 4.27 us -> 6.1 us  [swap_cores(): return lax.ppermute(send, 'tok', [(t, t ^ 1) for t in range(8)])]
    ppermute x6, starting transfers between devices: 12.5 us -> 11.1 us  [weigh(): return [lax.ppermute(v, 'member', z_pairs(d)) for d, v in send] + [own_sums]]
    ppermute x1 -> x2, starting transfers between devices: 4.75 us -> 6.09 us  [bring_weights(): arrived = lax.ppermute(weights, ('tok', 'col'), weight_pairs(phase))]
  transfers between devices with their start and end apart: 24 -> 26, of which waited for: 8 -> 12; matrix products, arithmetic and copies ran while one was open for 0% -> 0% of each run, Pallas kernels for 18% -> 17%
where the time goes in v17:
time: 112 us; the launch traced here: 110 us
  waiting for transfers between devices  49.1 us (44%)
  starting transfers between devices  38.5 us (34%)
  Pallas kernels  22.5 us (20%)
    ppermute x7, waiting for transfers between devices, swap_x(): return lax.ppermute(sent, 'tok', x_pairs(flip))  22.6 us
    pallas_call x21, Pallas kernels, call(): pl.pallas_call(kernel, out_shape=shapes, in_specs=[HBM] * len(hbm) + [VME...  21.6 us
    ppermute x6, starting transfers between devices, weigh(): return [lax.ppermute(v, 'member', z_pairs(d)) for d, v in send] + [own_sums]  11.1 us
    ppermute x7, starting transfers between devices, swap_x(): return lax.ppermute(sent, 'tok', x_pairs(flip))  8.97 us
    ppermute x1, waiting for transfers between devices, swap_cols(): return lax.ppermute(send, 'col', [(0, 1), (1, 0)])  8.44 us
    ppermute x4, waiting for transfers between devices, results(): lax.ppermute(sums, ('member', 'tok', 'col'), result_pairs(phase, y_lo))  8.05 us
    ppermute x6, waiting for transfers between devices, weigh(): return [lax.ppermute(v, 'member', z_pairs(d)) for d, v in send] + [own_sums]  7.39 us
    ppermute x4, starting transfers between devices, results(): lax.ppermute(sums, ('member', 'tok', 'col'), result_pairs(phase, y_lo))  6.2 us
  transfers between devices with their start and end apart: 26, of which 12 were waited for; matrix products, arithmetic and copies ran while one was open for 0% of the time, Pallas kernels for 17%

profile of v17, /device:TPU:1, one launch (start us, length us, event | category | flops | bytes accessed | tf_op | source)
XLA Modules:
  0.0 110.5 jit_solution(10949372208256023916)
XLA Ops:
  0.0 2.0 %load_to_swap.2.after = bf16[768,2304]{1,0:T(8,128)(2,1)S(1)} custom-call(bf16[2,768,4096]{2,1,0:T(8,128)(2,1)} %x_ref.7, bf16[2,768,256]{2,1,0:T(8,128)(2,1)} %g_ref.3), custom_call_target="tpu_custom_call" | custom-call | flops 1 | bytes 1 | tf_op jit(solution)/shard_map/load_to_swap/pallas_call | solution.py:66
  2.1 1.5 %collective-permute-start = (bf16[768,2304]{1,0:T(8,128)(2,1)S(1)}, bf16[768,2304]{1,0:T(8,128)(2,1)S(1)}, u32[]{:S(2)}, u32[]{:S(2)}) collective-permute-start(bf16[768,2304]{1,0:T(8,128)(2,1)S(1)} %load_to_swap.2.after), channel_id=1, source_target_pairs={{0,2},{2,0},{4,6},{6,4},{8,10},{10,8},{12,14},{14,12},{1,3},{3,1},... | collective-permute-start | bytes 10616840 | tf_op jit(solution)/shard_map/ppermute | solution.py:335
  3.6 1.9 %load_to_swap.3.after = bf16[768,2048]{1,0:T(8,128)(2,1)S(1)} custom-call(bf16[2,768,4096]{2,1,0:T(8,128)(2,1)} %x_ref.7, bf16[768,2304]{1,0:T(8,128)(2,1)S(1)} %load_to_swap.2.after), custom_call_target="tpu_custom_call" | custom-call | flops 1 | bytes 1 | tf_op jit(solution)/shard_map/load_to_swap/pallas_call | solution.py:66
  5.5 0.2 collective-permute-start.1
  5.7 4.8 %collective-permute-start.7 = (bf16[2,1024,256]{2,1,0:T(8,128)(2,1)S(1)}, bf16[2,1024,256]{2,1,0:T(8,128)(2,1)S(1)}, u32[]{:S(2)}, u32[]{:S(2)}) collective-permute-start(bf16[2,1024,256]{2,1,0:T(8,128)(2,1)S(1)} %copy-done), channel_id=1, source_target_pairs={{0,0},{2,12},{4,4},{6,8},{9,11},{11,7},{13,15},{15,3},{16,16},{18,... | collective-permute-start | bytes 3145736 | tf_op jit(solution)/shard_map/ppermute | solution.py:364
  10.5 2.9 %fisher_of_own_tokens.2 = (bf16[768,2048]{1,0:T(8,128)(2,1)S(1)}, bf16[768,256]{1,0:T(8,128)(2,1)S(1)}, bf16[256,768]{1,0:T(8,128)(2,1)S(1)}, f32[2,256,1024]{2,1,0:T(8,128)S(1)}) custom-call(bf16[2,768,4096]{2,1,0:T(8,128)(2,1)} %x_ref.7, bf16[2,768,256]{2,1,0:T(8,128)(2,1)} %g_ref.3, bf16[768,2048]{1,0:T(8,128)(2,1)S(1)} %load_to_swap.3.after), custom_call_target="tpu_custom_call" | custom-call | flops 1 | bytes 1 | tf_op jit(solution)/shard_map/fisher_of_own_tokens/pallas_call | solution.py:66
  13.5 1.3 %fisher_of_both_cores.2 = (bf16[256,1024]{1,0:T(8,128)(2,1)S(1)}, bf16[256,1024]{1,0:T(8,128)(2,1)S(1)}, bf16[256,768]{1,0:T(8,128)(2,1)S(1)}) custom-call(bf16[768,2304]{1,0:T(8,128)(2,1)S(1)} %collective-permute-done.got.x_ref.got_a, f32[2,256,1024]{2,1,0:T(8,128)S(1)} %get-tuple-element.44.part_ref, bf16[2,768,256]{2,1,0:T(8,128)(2,1)S(1)} %pair_grads.1.after), custom_call_target="tpu_custom_call" | custom-call | flops 1 | bytes 1 | tf_op jit(solution)/shard_map/fisher_of_both_cores/pallas_call | solution.py:66
  14.8 0.8 collective-permute-start.4
  15.6 2.6 %fisher_of_own_tokens.3 = (bf16[768,2048]{1,0:T(8,128)(2,1)S(1)}, f32[2,256,1024]{2,1,0:T(8,128)S(1)}) custom-call(bf16[2,768,4096]{2,1,0:T(8,128)(2,1)} %x_ref.7, bf16[256,768]{1,0:T(8,128)(2,1)S(1)} %get-tuple-element.43.after.gt_ref, bf16[256,1024]{1,0:T(8,128)(2,1)S(1)} %get-tuple-element.46.after), custom_call_target="tpu_custom_call" | custom-call | flops 1 | bytes 1 | tf_op jit(solution)/shard_map/fisher_of_own_tokens/pallas_call | solution.py:66
  18.2 3.3 %collective-permute-start.5 = (bf16[256,1024]{1,0:T(8,128)(2,1)S(1)}, bf16[256,1024]{1,0:T(8,128)(2,1)S(1)}, u32[]{:S(2)}, u32[]{:S(2)}) collective-permute-start(bf16[256,1024]{1,0:T(8,128)(2,1)S(1)} %get-tuple-element.46.after), channel_id=1, source_target_pairs={{0,8},{2,10},{4,12},{6,14},{8,0},{10,2},{12,4},{14,6},{1,9},{3,11}... | collective-permute-start | bytes 1572872 | tf_op jit(solution)/shard_map/ppermute | solution.py:341
  21.5 1.1 %fisher_of_both_cores.3 = (bf16[256,1024]{1,0:T(8,128)(2,1)S(1)}, f32[256,1024]{1,0:T(8,128)S(1)}) custom-call(bf16[768,2048]{1,0:T(8,128)(2,1)S(1)} %collective-permute-done.1.x_ref.got_b, bf16[256,768]{1,0:T(8,128)(2,1)S(1)} %get-tuple-element.48.gt_ref, f32[2,256,1024]{2,1,0:T(8,128)S(1)} %get-tuple-element.49.part_ref, ...), custom_call_target="tpu_custom_call" | custom-call | flops 1 | bytes 1 | tf_op jit(solution)/shard_map/fisher_of_both_cores/pallas_call | solution.py:66
  22.7 8.4 %collective-permute-done.2.g_ref = bf16[2,768,256]{2,1,0:T(8,128)(2,1)S(1)} collective-permute-done((bf16[2,768,256]{2,1,0:T(8,128)(2,1)S(1)}, bf16[2,768,256]{2,1,0:T(8,128)(2,1)S(1)}, u32[]{:S(2)}, u32[]{:S(2)}) %collective-permute-start.2) | collective-permute-done | bytes 786464 | tf_op jit(solution)/shard_map/ppermute | solution.py:338
  31.2 1.3 %collective-permute-start.14 = (bf16[2,1024,256]{2,1,0:T(8,128)(2,1)S(1)}, bf16[2,1024,256]{2,1,0:T(8,128)(2,1)S(1)}, u32[]{:S(2)}, u32[]{:S(2)}) collective-permute-start(bf16[2,1024,256]{2,1,0:T(8,128)(2,1)S(1)} %copy-done), channel_id=1, source_target_pairs={{1,2},{3,14},{5,6},{7,10},{8,9},{10,5},{12,13},{14,1},{17,18},{19,... | collective-permute-start | bytes 3145736 | tf_op jit(solution)/shard_map/ppermute | solution.py:364
  32.4 1.9 %fisher_of_other_grads.2 = (bf16[2,256,512]{2,1,0:T(8,128)(2,1)S(1)}, f32[2,256,512]{2,1,0:T(8,128)S(1)}, bf16[256,768]{1,0:T(8,128)(2,1)S(1)}, bf16[256,768]{1,0:T(8,128)(2,1)S(1)}) custom-call(bf16[768,2048]{1,0:T(8,128)(2,1)S(1)} %get-tuple-element.42.own_a, bf16[768,2304]{1,0:T(8,128)(2,1)S(1)} %collective-permute-done.got.x_ref.got_a, ...), custom_call_target="tpu_custom_call" | custom-call | flops 1 | bytes 1 | tf_op jit(solution)/shard_map/fisher_of_other_grads/pallas_call | solution.py:66
  34.6 1.4 %collective-permute-start.3 = (bf16[2,256,512]{2,1,0:T(8,128)(2,1)S(1)}, bf16[2,256,512]{2,1,0:T(8,128)(2,1)S(1)}, u32[]{:S(2)}, u32[]{:S(2)}) collective-permute-start(bf16[2,256,512]{2,1,0:T(8,128)(2,1)S(1)} %get-tuple-element.52), channel_id=1, source_target_pairs={{0,4},{2,6},{4,0},{6,2},{8,12},{10,14},{12,8},{14,10},{1,5},{3,7},... | collective-permute-start | bytes 1572872 | tf_op jit(solution)/shard_map/ppermute | solution.py:341
  36.0 1.9 %fisher_of_other_grads.3 = (bf16[2,256,512]{2,1,0:T(8,128)(2,1)S(1)}, f32[2,256,512]{2,1,0:T(8,128)S(1)}) custom-call(bf16[768,2048]{1,0:T(8,128)(2,1)S(1)} %get-tuple-element.42.own_a, bf16[768,2304]{1,0:T(8,128)(2,1)S(1)} %collective-permute-done.got.x_ref.got_a, bf16[768,2048]{1,0:T(8,128)(2,1)S(1)} %get-tuple-element.47.after.own_b, ...), custom_call_target="tpu_custom_call" | custom-call | flops 1 | bytes 1 | tf_op jit(solution)/shard_map/fisher_of_other_grads/pallas_call | solution.py:66
  37.8 3.6 %collective-permute-done.5.two = bf16[256,1024]{1,0:T(8,128)(2,1)S(1)} collective-permute-done((bf16[256,1024]{1,0:T(8,128)(2,1)S(1)}, bf16[256,1024]{1,0:T(8,128)(2,1)S(1)}, u32[]{:S(2)}, u32[]{:S(2)}) %collective-permute-start.5) | collective-permute-done | bytes 524320 | tf_op jit(solution)/shard_map/ppermute | solution.py:341
  41.4 3.3 %collective-permute-start.15 = (bf16[2,256,512]{2,1,0:T(8,128)(2,1)S(1)}, bf16[2,256,512]{2,1,0:T(8,128)(2,1)S(1)}, u32[]{:S(2)}, u32[]{:S(2)}) collective-permute-start(bf16[2,256,512]{2,1,0:T(8,128)(2,1)S(1)} %get-tuple-element.68), channel_id=1, source_target_pairs={{0,12},{2,14},{4,8},{6,10},{8,4},{10,6},{12,0},{14,2},{1,13},{3,15... | collective-permute-start | bytes 1572872 | tf_op jit(solution)/shard_map/ppermute | solution.py:341
  44.7 2.6 %collective-permute-done.6.three = bf16[256,1024]{1,0:T(8,128)(2,1)S(1)} collective-permute-done((bf16[256,1024]{1,0:T(8,128)(2,1)S(1)}, bf16[256,1024]{1,0:T(8,128)(2,1)S(1)}, u32[]{:S(2)}, u32[]{:S(2)}) %collective-permute-start.6) | collective-permute-done | bytes 524320 | tf_op jit(solution)/shard_map/ppermute | solution.py:341
  47.3 1.6 %fisher_over_tokens.3 = (f32[256,512]{1,0:T(8,128)S(1)}, bf16[256,512]{1,0:T(8,128)(2,1)S(1)}) custom-call(f32[256,1024]{1,0:T(8,128)S(1)} %get-tuple-element.53.own, bf16[256,1024]{1,0:T(8,128)(2,1)S(1)} %collective-permute-done.4.one, bf16[256,1024]{1,0:T(8,128)(2,1)S(1)} %collective-permute-done.5.two, ...), custom_call_target="tpu_custom_call" | custom-call | flops 1 | bytes 1 | tf_op jit(solution)/shard_map/fisher_over_tokens/pallas_call | solution.py:66
  49.0 4.2 %collective-permute-start.8 = (bf16[256,512]{1,0:T(8,128)(2,1)S(1)}, bf16[256,512]{1,0:T(8,128)(2,1)S(1)}, u32[]{:S(2)}, u32[]{:S(2)}) collective-permute-start(bf16[256,512]{1,0:T(8,128)(2,1)S(1)} %get-tuple-element.60), channel_id=1, source_target_pairs={{0,2},{2,0},{4,6},{6,4},{8,10},{10,8},{12,14},{14,12},{1,3},{3,1},... | collective-permute-start | bytes 786440 | tf_op jit(solution)/shard_map/ppermute | solution.py:335
  53.1 1.2 %collective-permute-done.8.refs_1_ = bf16[256,512]{1,0:T(8,128)(2,1)S(1)} collective-permute-done((bf16[256,512]{1,0:T(8,128)(2,1)S(1)}, bf16[256,512]{1,0:T(8,128)(2,1)S(1)}, u32[]{:S(2)}, u32[]{:S(2)}) %collective-permute-start.8) | collective-permute-done | bytes 262176 | tf_op jit(solution)/shard_map/ppermute | solution.py:335
  54.3 0.5 weigh_members.2
  54.8 3.7 %collective-permute-start.11 = (f32[2,128,256]{2,1,0:T(8,128)S(1)}, f32[2,128,256]{2,1,0:T(8,128)S(1)}, u32[]{:S(2)}, u32[]{:S(2)}) collective-permute-start(f32[2,128,256]{2,1,0:T(8,128)S(1)} %get-tuple-element.65), channel_id=1, source_target_pairs={{0,32},{16,48},{32,0},{48,16},{64,96},{80,112},{96,64},{112,80},{1... | collective-permute-start | bytes 786440 | tf_op jit(solution)/shard_map/ppermute | solution.py:374
  58.5 0.7 fisher_over_first_swap.2
  59.3 0.8 collective-permute-start.12
  60.1 14.0 %collective-permute-done.15.got_ref = bf16[2,256,512]{2,1,0:T(8,128)(2,1)S(1)} collective-permute-done((bf16[2,256,512]{2,1,0:T(8,128)(2,1)S(1)}, bf16[2,256,512]{2,1,0:T(8,128)(2,1)S(1)}, u32[]{:S(2)}, u32[]{:S(2)}) %collective-permute-start.15) | collective-permute-done | bytes 524320 | tf_op jit(solution)/shard_map/ppermute | solution.py:341
  74.1 3.8 %collective-permute-start.13 = (f32[2,128,256]{2,1,0:T(8,128)S(1)}, f32[2,128,256]{2,1,0:T(8,128)S(1)}, u32[]{:S(2)}, u32[]{:S(2)}) collective-permute-start(f32[2,128,256]{2,1,0:T(8,128)S(1)} %get-tuple-element.67), channel_id=1, source_target_pairs={{0,48},{16,0},{32,16},{48,32},{64,112},{80,64},{96,80},{112,96},{1... | collective-permute-start | bytes 786440 | tf_op jit(solution)/shard_map/ppermute | solution.py:374
  77.8 0.7 fisher_over_first_swap.3
  78.9 2.3 %collective-permute-done.13.three = f32[2,128,256]{2,1,0:T(8,128)S(1)} collective-permute-done((f32[2,128,256]{2,1,0:T(8,128)S(1)}, f32[2,128,256]{2,1,0:T(8,128)S(1)}, u32[]{:S(2)}, u32[]{:S(2)}) %collective-permute-start.13) | collective-permute-done | bytes 262176 | tf_op jit(solution)/shard_map/ppermute | solution.py:374
  81.3 0.3 fisher_over_tokens.4.first_ref
  81.6 2.3 %collective-permute-done.16.got = bf16[256,512]{1,0:T(8,128)(2,1)S(1)} collective-permute-done((bf16[256,512]{1,0:T(8,128)(2,1)S(1)}, bf16[256,512]{1,0:T(8,128)(2,1)S(1)}, u32[]{:S(2)}, u32[]{:S(2)}) %collective-permute-start.16) | collective-permute-done | bytes 262176 | tf_op jit(solution)/shard_map/ppermute | solution.py:341
  83.9 0.6 fisher_over_tokens.5
  84.6 1.5 %collective-permute-done.17.refs_1_ = bf16[256,512]{1,0:T(8,128)(2,1)S(1)} collective-permute-done((bf16[256,512]{1,0:T(8,128)(2,1)S(1)}, bf16[256,512]{1,0:T(8,128)(2,1)S(1)}, u32[]{:S(2)}, u32[]{:S(2)}) %collective-permute-start.17) | collective-permute-done | bytes 262176 | tf_op jit(solution)/shard_map/ppermute | solution.py:335
  86.1 0.7 weigh_members.3
  86.9 1.4 %collective-permute-start.20 = (bf16[3,128,256]{2,1,0:T(8,128)(2,1)S(1)}, bf16[3,128,256]{2,1,0:T(8,128)(2,1)S(1)}, u32[]{:S(2)}, u32[]{:S(2)}) collective-permute-start(bf16[3,128,256]{2,1,0:T(8,128)(2,1)S(1)} %get-tuple-element.76), channel_id=1, source_target_pairs={{0,16},{16,32},{32,48},{48,0},{64,80},{80,96},{96,112},{112,64},{1... | collective-permute-start | bytes 589832 | tf_op jit(solution)/shard_map/ppermute | solution.py:374
  88.3 1.4 %collective-permute-start.21 = (bf16[3,128,256]{2,1,0:T(8,128)(2,1)S(1)}, bf16[3,128,256]{2,1,0:T(8,128)(2,1)S(1)}, u32[]{:S(2)}, u32[]{:S(2)}) collective-permute-start(bf16[3,128,256]{2,1,0:T(8,128)(2,1)S(1)} %get-tuple-element.77), channel_id=1, source_target_pairs={{0,48},{16,0},{32,16},{48,32},{64,112},{80,64},{96,80},{112,96},{1... | collective-permute-start | bytes 589832 | tf_op jit(solution)/shard_map/ppermute | solution.py:374
  89.7 2.9 %collective-permute-start.24 = (bf16[3,128,256]{2,1,0:T(8,128)(2,1)S(1)}, bf16[3,128,256]{2,1,0:T(8,128)(2,1)S(1)}, u32[]{:S(2)}, u32[]{:S(2)}) collective-permute-start(bf16[3,128,256]{2,1,0:T(8,128)(2,1)S(1)} %sum_over_z.2.after), channel_id=1, source_target_pairs={{0,0},{1,15},{2,64},{3,79},{4,4},{5,11},{6,68},{7,75},{8,6},{9,9},... | collective-permute-start | bytes 589832 | tf_op jit(solution)/shard_map/ppermute | solution.py:361
  92.6 1.3 %collective-permute-start.25 = (bf16[3,128,256]{2,1,0:T(8,128)(2,1)S(1)}, bf16[3,128,256]{2,1,0:T(8,128)(2,1)S(1)}, u32[]{:S(2)}, u32[]{:S(2)}) collective-permute-start(bf16[3,128,256]{2,1,0:T(8,128)(2,1)S(1)} %sum_over_z.2.after), channel_id=1, source_target_pairs={{64,0},{65,15},{66,64},{67,79},{68,4},{69,11},{70,68},{71,75},{72,... | collective-permute-start | bytes 589832 | tf_op jit(solution)/shard_map/ppermute | solution.py:361
  93.9 0.9 collective-permute-done.19.one
  94.8 4.2 %collective-permute-done.20.two = bf16[3,128,256]{2,1,0:T(8,128)(2,1)S(1)} collective-permute-done((bf16[3,128,256]{2,1,0:T(8,128)(2,1)S(1)}, bf16[3,128,256]{2,1,0:T(8,128)(2,1)S(1)}, u32[]{:S(2)}, u32[]{:S(2)}) %collective-permute-start.20) | collective-permute-done | bytes 196640 | tf_op jit(solution)/shard_map/ppermute | solution.py:374
  99.0 0.3 sum_over_z.3
  99.4 1.3 %collective-permute-start.22 = (bf16[3,128,256]{2,1,0:T(8,128)(2,1)S(1)}, bf16[3,128,256]{2,1,0:T(8,128)(2,1)S(1)}, u32[]{:S(2)}, u32[]{:S(2)}) collective-permute-start(bf16[3,128,256]{2,1,0:T(8,128)(2,1)S(1)} %sum_over_z.3), channel_id=1, source_target_pairs={{0,1},{1,14},{2,65},{3,78},{4,5},{5,10},{6,69},{7,74},{8,7},{9,8},... | collective-permute-start | bytes 589832 | tf_op jit(solution)/shard_map/ppermute | solution.py:361
  100.7 0.7 collective-permute-start.23
  101.4 0.3 collective-permute-done.25.far
  101.7 0.2 meet_over_y.1.sums
  101.9 7.7 %collective-permute-done.22.near = bf16[3,128,256]{2,1,0:T(8,128)(2,1)S(1)} collective-permute-done((bf16[3,128,256]{2,1,0:T(8,128)(2,1)S(1)}, bf16[3,128,256]{2,1,0:T(8,128)(2,1)S(1)}, u32[]{:S(2)}, u32[]{:S(2)}) %collective-permute-start.22) | collective-permute-done | bytes 196640 | tf_op jit(solution)/shard_map/ppermute | solution.py:361
  109.6 0.8 merge_members.1
  (28 shorter events, 1.1 us)
Async XLA Ops:
  2.1 3.6 %copy-start = (bf16[2,1024,256]{2,1,0:T(8,128)(2,1)S(1)}, bf16[2,1024,256]{2,1,0:T(8,128)(2,1)}, u32[]{:S(2)}) copy-start(bf16[2,1024,256]{2,1,0:T(8,128)(2,1)} %param.5) | copy-start | bytes 3145732
  2.1 11.3 %collective-permute-start = (bf16[768,2304]{1,0:T(8,128)(2,1)S(1)}, bf16[768,2304]{1,0:T(8,128)(2,1)S(1)}, u32[]{:S(2)}, u32[]{:S(2)}) collective-permute-start(bf16[768,2304]{1,0:T(8,128)(2,1)S(1)} %load_to_swap.2.after), channel_id=1, source_target_pairs={{0,2},{2,0},{4,6},{6,4},{8,10},{10,8},{12,14},{14,12},{1,3},{3,1},... | collective-permute-start | bytes 10616840 | tf_op jit(solution)/shard_map/ppermute | solution.py:335
  5.5 16.0 %collective-permute-start.1 = (bf16[768,2048]{1,0:T(8,128)(2,1)S(1)}, bf16[768,2048]{1,0:T(8,128)(2,1)S(1)}, u32[]{:S(2)}, u32[]{:S(2)}) collective-permute-start(bf16[768,2048]{1,0:T(8,128)(2,1)S(1)} %load_to_swap.3.after), channel_id=1, source_target_pairs={{0,2},{2,0},{4,6},{6,4},{8,10},{10,8},{12,14},{14,12},{1,3},{3,1},... | collective-permute-start | bytes 9437192 | tf_op jit(solution)/shard_map/ppermute | solution.py:335
  5.7 28.7 %collective-permute-start.7 = (bf16[2,1024,256]{2,1,0:T(8,128)(2,1)S(1)}, bf16[2,1024,256]{2,1,0:T(8,128)(2,1)S(1)}, u32[]{:S(2)}, u32[]{:S(2)}) collective-permute-start(bf16[2,1024,256]{2,1,0:T(8,128)(2,1)S(1)} %copy-done), channel_id=1, source_target_pairs={{0,0},{2,12},{4,4},{6,8},{9,11},{11,7},{13,15},{15,3},{16,16},{18,... | collective-permute-start | bytes 3145736 | tf_op jit(solution)/shard_map/ppermute | solution.py:364
  13.4 17.7 %collective-permute-start.2 = (bf16[2,768,256]{2,1,0:T(8,128)(2,1)S(1)}, bf16[2,768,256]{2,1,0:T(8,128)(2,1)S(1)}, u32[]{:S(2)}, u32[]{:S(2)}) collective-permute-start(bf16[2,768,256]{2,1,0:T(8,128)(2,1)S(1)} %pair_grads.1.after), channel_id=1, source_target_pairs={{0,1},{1,0},{2,3},{3,2},{4,5},{5,4},{6,7},{7,6},{8,9},{9,8},{10,11... | collective-permute-start | bytes 2359304 | tf_op jit(solution)/shard_map/ppermute | solution.py:338
  14.8 19.8 %collective-permute-start.4 = (bf16[256,1024]{1,0:T(8,128)(2,1)S(1)}, bf16[256,1024]{1,0:T(8,128)(2,1)S(1)}, u32[]{:S(2)}, u32[]{:S(2)}) collective-permute-start(bf16[256,1024]{1,0:T(8,128)(2,1)S(1)} %get-tuple-element.54), channel_id=1, source_target_pairs={{0,4},{2,6},{4,0},{6,2},{8,12},{10,14},{12,8},{14,10},{1,5},{3,7},... | collective-permute-start | bytes 1572872 | tf_op jit(solution)/shard_map/ppermute | solution.py:341
  18.2 23.3 %collective-permute-start.5 = (bf16[256,1024]{1,0:T(8,128)(2,1)S(1)}, bf16[256,1024]{1,0:T(8,128)(2,1)S(1)}, u32[]{:S(2)}, u32[]{:S(2)}) collective-permute-start(bf16[256,1024]{1,0:T(8,128)(2,1)S(1)} %get-tuple-element.46.after), channel_id=1, source_target_pairs={{0,8},{2,10},{4,12},{6,14},{8,0},{10,2},{12,4},{14,6},{1,9},{3,11}... | collective-permute-start | bytes 1572872 | tf_op jit(solution)/shard_map/ppermute | solution.py:341
  22.6 24.7 %collective-permute-start.6 = (bf16[256,1024]{1,0:T(8,128)(2,1)S(1)}, bf16[256,1024]{1,0:T(8,128)(2,1)S(1)}, u32[]{:S(2)}, u32[]{:S(2)}) collective-permute-start(bf16[256,1024]{1,0:T(8,128)(2,1)S(1)} %get-tuple-element.50.after), channel_id=1, source_target_pairs={{0,12},{2,14},{4,8},{6,10},{8,4},{10,6},{12,0},{14,2},{1,13},{3,15... | collective-permute-start | bytes 1572872 | tf_op jit(solution)/shard_map/ppermute | solution.py:341
  31.2 47.4 %collective-permute-start.14 = (bf16[2,1024,256]{2,1,0:T(8,128)(2,1)S(1)}, bf16[2,1024,256]{2,1,0:T(8,128)(2,1)S(1)}, u32[]{:S(2)}, u32[]{:S(2)}) collective-permute-start(bf16[2,1024,256]{2,1,0:T(8,128)(2,1)S(1)} %copy-done), channel_id=1, source_target_pairs={{1,2},{3,14},{5,6},{7,10},{8,9},{10,5},{12,13},{14,1},{17,18},{19,... | collective-permute-start | bytes 3145736 | tf_op jit(solution)/shard_map/ppermute | solution.py:364
  34.5 19.8 %collective-permute-start.9 = (bf16[2,512,256]{2,1,0:T(8,128)(2,1)S(1)}, bf16[2,512,256]{2,1,0:T(8,128)(2,1)S(1)}, u32[]{:S(2)}, u32[]{:S(2)}) collective-permute-start(bf16[2,512,256]{2,1,0:T(8,128)(2,1)S(1)} %get-tuple-element.61), channel_id=1, source_target_pairs={{0,2},{2,0},{4,6},{6,4},{8,10},{10,8},{12,14},{14,12},{1,3},{3,1},... | collective-permute-start | bytes 1572872 | tf_op jit(solution)/shard_map/ppermute | solution.py:335
  34.6 23.9 %collective-permute-start.3 = (bf16[2,256,512]{2,1,0:T(8,128)(2,1)S(1)}, bf16[2,256,512]{2,1,0:T(8,128)(2,1)S(1)}, u32[]{:S(2)}, u32[]{:S(2)}) collective-permute-start(bf16[2,256,512]{2,1,0:T(8,128)(2,1)S(1)} %get-tuple-element.52), channel_id=1, source_target_pairs={{0,4},{2,6},{4,0},{6,2},{8,12},{10,14},{12,8},{14,10},{1,5},{3,7},... | collective-permute-start | bytes 1572872 | tf_op jit(solution)/shard_map/ppermute | solution.py:341
  41.4 32.6 %collective-permute-start.15 = (bf16[2,256,512]{2,1,0:T(8,128)(2,1)S(1)}, bf16[2,256,512]{2,1,0:T(8,128)(2,1)S(1)}, u32[]{:S(2)}, u32[]{:S(2)}) collective-permute-start(bf16[2,256,512]{2,1,0:T(8,128)(2,1)S(1)} %get-tuple-element.68), channel_id=1, source_target_pairs={{0,12},{2,14},{4,8},{6,10},{8,4},{10,6},{12,0},{14,2},{1,13},{3,15... | collective-permute-start | bytes 1572872 | tf_op jit(solution)/shard_map/ppermute | solution.py:341
  49.0 5.3 %collective-permute-start.8 = (bf16[256,512]{1,0:T(8,128)(2,1)S(1)}, bf16[256,512]{1,0:T(8,128)(2,1)S(1)}, u32[]{:S(2)}, u32[]{:S(2)}) collective-permute-start(bf16[256,512]{1,0:T(8,128)(2,1)S(1)} %get-tuple-element.60), channel_id=1, source_target_pairs={{0,2},{2,0},{4,6},{6,4},{8,10},{10,8},{12,14},{14,12},{1,3},{3,1},... | collective-permute-start | bytes 786440 | tf_op jit(solution)/shard_map/ppermute | solution.py:335
  54.8 24.0 %collective-permute-start.11 = (f32[2,128,256]{2,1,0:T(8,128)S(1)}, f32[2,128,256]{2,1,0:T(8,128)S(1)}, u32[]{:S(2)}, u32[]{:S(2)}) collective-permute-start(f32[2,128,256]{2,1,0:T(8,128)S(1)} %get-tuple-element.65), channel_id=1, source_target_pairs={{0,32},{16,48},{32,0},{48,16},{64,96},{80,112},{96,64},{112,80},{1... | collective-permute-start | bytes 786440 | tf_op jit(solution)/shard_map/ppermute | solution.py:374
  59.2 22.1 %collective-permute-start.10 = (bf16[256,512]{1,0:T(8,128)(2,1)S(1)}, bf16[256,512]{1,0:T(8,128)(2,1)S(1)}, u32[]{:S(2)}, u32[]{:S(2)}) collective-permute-start(bf16[256,512]{1,0:T(8,128)(2,1)S(1)} %get-tuple-element.64), channel_id=1, source_target_pairs={{0,12},{2,14},{4,8},{6,10},{8,4},{10,6},{12,0},{14,2},{1,13},{3,15... | collective-permute-start | bytes 786440 | tf_op jit(solution)/shard_map/ppermute | solution.py:341
  59.3 19.6 %collective-permute-start.12 = (f32[2,128,256]{2,1,0:T(8,128)S(1)}, f32[2,128,256]{2,1,0:T(8,128)S(1)}, u32[]{:S(2)}, u32[]{:S(2)}) collective-permute-start(f32[2,128,256]{2,1,0:T(8,128)S(1)} %get-tuple-element.66), channel_id=1, source_target_pairs={{0,16},{16,32},{32,48},{48,0},{64,80},{80,96},{96,112},{112,64},{1... | collective-permute-start | bytes 786440 | tf_op jit(solution)/shard_map/ppermute | solution.py:374
  74.1 7.1 %collective-permute-start.13 = (f32[2,128,256]{2,1,0:T(8,128)S(1)}, f32[2,128,256]{2,1,0:T(8,128)S(1)}, u32[]{:S(2)}, u32[]{:S(2)}) collective-permute-start(f32[2,128,256]{2,1,0:T(8,128)S(1)} %get-tuple-element.67), channel_id=1, source_target_pairs={{0,48},{16,0},{32,16},{48,32},{64,112},{80,64},{96,80},{112,96},{1... | collective-permute-start | bytes 786440 | tf_op jit(solution)/shard_map/ppermute | solution.py:374
  78.6 5.3 %collective-permute-start.16 = (bf16[256,512]{1,0:T(8,128)(2,1)S(1)}, bf16[256,512]{1,0:T(8,128)(2,1)S(1)}, u32[]{:S(2)}, u32[]{:S(2)}) collective-permute-start(bf16[256,512]{1,0:T(8,128)(2,1)S(1)} %get-tuple-element.71), channel_id=1, source_target_pairs={{0,4},{2,6},{4,0},{6,2},{8,12},{10,14},{12,8},{14,10},{1,5},{3,7},... | collective-permute-start | bytes 786440 | tf_op jit(solution)/shard_map/ppermute | solution.py:341
  78.8 5.8 %collective-permute-start.18 = (bf16[2,512,256]{2,1,0:T(8,128)(2,1)S(1)}, bf16[2,512,256]{2,1,0:T(8,128)(2,1)S(1)}, u32[]{:S(2)}, u32[]{:S(2)}) collective-permute-start(bf16[2,512,256]{2,1,0:T(8,128)(2,1)S(1)} %get-tuple-element.74), channel_id=1, source_target_pairs={{0,2},{2,0},{4,6},{6,4},{8,10},{10,8},{12,14},{14,12},{1,3},{3,1},... | collective-permute-start | bytes 1572872 | tf_op jit(solution)/shard_map/ppermute | solution.py:335
  84.5 1.6 %collective-permute-start.17 = (bf16[256,512]{1,0:T(8,128)(2,1)S(1)}, bf16[256,512]{1,0:T(8,128)(2,1)S(1)}, u32[]{:S(2)}, u32[]{:S(2)}) collective-permute-start(bf16[256,512]{1,0:T(8,128)(2,1)S(1)} %get-tuple-element.73), channel_id=1, source_target_pairs={{0,2},{2,0},{4,6},{6,4},{8,10},{10,8},{12,14},{14,12},{1,3},{3,1},... | collective-permute-start | bytes 786440 | tf_op jit(solution)/shard_map/ppermute | solution.py:335
  86.8 8.0 %collective-permute-start.19 = (bf16[3,128,256]{2,1,0:T(8,128)(2,1)S(1)}, bf16[3,128,256]{2,1,0:T(8,128)(2,1)S(1)}, u32[]{:S(2)}, u32[]{:S(2)}) collective-permute-start(bf16[3,128,256]{2,1,0:T(8,128)(2,1)S(1)} %get-tuple-element.75), channel_id=1, source_target_pairs={{0,32},{16,48},{32,0},{48,16},{64,96},{80,112},{96,64},{112,80},{1... | collective-permute-start | bytes 589832 | tf_op jit(solution)/shard_map/ppermute | solution.py:374
  86.9 12.1 %collective-permute-start.20 = (bf16[3,128,256]{2,1,0:T(8,128)(2,1)S(1)}, bf16[3,128,256]{2,1,0:T(8,128)(2,1)S(1)}, u32[]{:S(2)}, u32[]{:S(2)}) collective-permute-start(bf16[3,128,256]{2,1,0:T(8,128)(2,1)S(1)} %get-tuple-element.76), channel_id=1, source_target_pairs={{0,16},{16,32},{32,48},{48,0},{64,80},{80,96},{96,112},{112,64},{1... | collective-permute-start | bytes 589832 | tf_op jit(solution)/shard_map/ppermute | solution.py:374
  88.3 10.7 %collective-permute-start.21 = (bf16[3,128,256]{2,1,0:T(8,128)(2,1)S(1)}, bf16[3,128,256]{2,1,0:T(8,128)(2,1)S(1)}, u32[]{:S(2)}, u32[]{:S(2)}) collective-permute-start(bf16[3,128,256]{2,1,0:T(8,128)(2,1)S(1)} %get-tuple-element.77), channel_id=1, source_target_pairs={{0,48},{16,0},{32,16},{48,32},{64,112},{80,64},{96,80},{112,96},{1... | collective-permute-start | bytes 589832 | tf_op jit(solution)/shard_map/ppermute | solution.py:374
  89.7 11.7 %collective-permute-start.24 = (bf16[3,128,256]{2,1,0:T(8,128)(2,1)S(1)}, bf16[3,128,256]{2,1,0:T(8,128)(2,1)S(1)}, u32[]{:S(2)}, u32[]{:S(2)}) collective-permute-start(bf16[3,128,256]{2,1,0:T(8,128)(2,1)S(1)} %sum_over_z.2.after), channel_id=1, source_target_pairs={{0,0},{1,15},{2,64},{3,79},{4,4},{5,11},{6,68},{7,75},{8,6},{9,9},... | collective-permute-start | bytes 589832 | tf_op jit(solution)/shard_map/ppermute | solution.py:361
  92.6 9.1 %collective-permute-start.25 = (bf16[3,128,256]{2,1,0:T(8,128)(2,1)S(1)}, bf16[3,128,256]{2,1,0:T(8,128)(2,1)S(1)}, u32[]{:S(2)}, u32[]{:S(2)}) collective-permute-start(bf16[3,128,256]{2,1,0:T(8,128)(2,1)S(1)} %sum_over_z.2.after), channel_id=1, source_target_pairs={{64,0},{65,15},{66,64},{67,79},{68,4},{69,11},{70,68},{71,75},{72,... | collective-permute-start | bytes 589832 | tf_op jit(solution)/shard_map/ppermute | solution.py:361
  99.4 10.2 %collective-permute-start.22 = (bf16[3,128,256]{2,1,0:T(8,128)(2,1)S(1)}, bf16[3,128,256]{2,1,0:T(8,128)(2,1)S(1)}, u32[]{:S(2)}, u32[]{:S(2)}) collective-permute-start(bf16[3,128,256]{2,1,0:T(8,128)(2,1)S(1)} %sum_over_z.3), channel_id=1, source_target_pairs={{0,1},{1,14},{2,65},{3,78},{4,5},{5,10},{6,69},{7,74},{8,7},{9,8},... | collective-permute-start | bytes 589832 | tf_op jit(solution)/shard_map/ppermute | solution.py:361
  100.7 8.9 %collective-permute-start.23 = (bf16[3,128,256]{2,1,0:T(8,128)(2,1)S(1)}, bf16[3,128,256]{2,1,0:T(8,128)(2,1)S(1)}, u32[]{:S(2)}, u32[]{:S(2)}) collective-permute-start(bf16[3,128,256]{2,1,0:T(8,128)(2,1)S(1)} %sum_over_z.3), channel_id=1, source_target_pairs={{64,1},{65,14},{66,65},{67,78},{68,5},{69,10},{70,69},{71,74},{72,... | collective-permute-start | bytes 589832 | tf_op jit(solution)/shard_map/ppermute | solution.py:361

commit v18 on v15

--- a/solution.py
+++ b/solution.py
@@ -370,7 +370,7 @@
         one, two, three, own_sums = call(
             lambda *refs: weigh_kernel(phase, *refs), "weigh_members", [words if phase else wide_words] * 3 + [sums], [], [own, other, *moved, after]
         )
-        send = ((2, two), (1, one), (3, three))
+        send = ((1, one), (2, two), (3, three))
         return [lax.ppermute(v, "member", z_pairs(d)) for d, v in send] + [own_sums]
 
     x_send0 = call(

time: 103 us -> 104 us (level)
  waiting for transfers between devices: 31.5 us -> 33.2 us
  starting transfers between devices: 48.6 us -> 47.4 us
    ppermute x6, waiting for transfers between devices: 6.62 us -> 8.39 us  [weigh(): return [lax.ppermute(v, 'member', z_pairs(d)) for d, v in send] + [own_sums]]
    ppermute x6, starting transfers between devices: 12.5 us -> 11.1 us  [weigh(): return [lax.ppermute(v, 'member', z_pairs(d)) for d, v in send] + [own_sums]]
  transfers between devices with their start and end apart: 24 -> 24, of which waited for: 8 -> 7; matrix products, arithmetic and copies ran while one was open for 0% -> 0% of each run, Pallas kernels for 18% -> 18%
where the time goes in v18:
time: 104 us; the launch traced here: 103 us
  starting transfers between devices  47.4 us (46%)
  waiting for transfers between devices  33.2 us (32%)
  Pallas kernels  22.4 us (22%)
    pallas_call x20, Pallas kernels, call(): pl.pallas_call(kernel, out_shape=shapes, in_specs=[HBM] * len(hbm) + [VME...  21.6 us
    ppermute x1, waiting for transfers between devices, swap_cols(): return lax.ppermute(send, 'col', [(0, 1), (1, 0)])  16.8 us
    ppermute x4, starting transfers between devices, results(): lax.ppermute(sums, ('member', 'tok', 'col'), result_pairs(phase, y_lo))  15.5 us
    ppermute x6, starting transfers between devices, weigh(): return [lax.ppermute(v, 'member', z_pairs(d)) for d, v in send] + [own_sums]  11.1 us
    ppermute x7, starting transfers between devices, swap_x(): return lax.ppermute(sent, 'tok', x_pairs(flip))  9.72 us
    ppermute x6, waiting for transfers between devices, weigh(): return [lax.ppermute(v, 'member', z_pairs(d)) for d, v in send] + [own_sums]  8.39 us
    ppermute x4, waiting for transfers between devices, results(): lax.ppermute(sums, ('member', 'tok', 'col'), result_pairs(phase, y_lo))  5.73 us
    ppermute x1, starting transfers between devices, bring_weights(): arrived = lax.ppermute(weights, ('tok', 'col'), weight_pairs())  4.75 us
  transfers between devices with their start and end apart: 24, of which 7 were waited for; matrix products, arithmetic and copies ran while one was open for 0% of the time, Pallas kernels for 18%

profile of v18, /device:TPU:1, one launch (start us, length us, event | category | flops | bytes accessed | tf_op | source)
XLA Modules:
  0.0 103.4 jit_solution(17944797181168038680)
XLA Ops:
  0.0 2.0 %load_to_swap.2.after = bf16[768,2304]{1,0:T(8,128)(2,1)S(1)} custom-call(bf16[2,768,4096]{2,1,0:T(8,128)(2,1)} %x_ref.7, bf16[2,768,256]{2,1,0:T(8,128)(2,1)} %g_ref.3), custom_call_target="tpu_custom_call" | custom-call | flops 1 | bytes 1 | tf_op jit(solution)/shard_map/load_to_swap/pallas_call | solution.py:66
  2.1 1.5 %collective-permute-start = (bf16[768,2304]{1,0:T(8,128)(2,1)S(1)}, bf16[768,2304]{1,0:T(8,128)(2,1)S(1)}, u32[]{:S(2)}, u32[]{:S(2)}) collective-permute-start(bf16[768,2304]{1,0:T(8,128)(2,1)S(1)} %load_to_swap.2.after), channel_id=1, source_target_pairs={{0,2},{2,0},{4,6},{6,4},{8,10},{10,8},{12,14},{14,12},{1,3},{3,1},... | collective-permute-start | bytes 10616840 | tf_op jit(solution)/shard_map/ppermute | solution.py:335
  3.6 1.9 %load_to_swap.3.after = bf16[768,2048]{1,0:T(8,128)(2,1)S(1)} custom-call(bf16[2,768,4096]{2,1,0:T(8,128)(2,1)} %x_ref.7, bf16[768,2304]{1,0:T(8,128)(2,1)S(1)} %load_to_swap.2.after), custom_call_target="tpu_custom_call" | custom-call | flops 1 | bytes 1 | tf_op jit(solution)/shard_map/load_to_swap/pallas_call | solution.py:66
  5.5 0.2 collective-permute-start.1
  5.7 4.8 %collective-permute-start.7 = (bf16[2,1024,256]{2,1,0:T(8,128)(2,1)S(1)}, bf16[2,1024,256]{2,1,0:T(8,128)(2,1)S(1)}, u32[]{:S(2)}, u32[]{:S(2)}) collective-permute-start(bf16[2,1024,256]{2,1,0:T(8,128)(2,1)S(1)} %copy-done), channel_id=1, source_target_pairs={{0,0},{1,2},{2,12},{3,14},{4,4},{5,6},{6,8},{7,10},{8,9},{9,11},{1... | collective-permute-start | bytes 3145736 | tf_op jit(solution)/shard_map/ppermute | solution.py:364
  10.4 2.9 %fisher_of_own_tokens.2 = (bf16[768,2048]{1,0:T(8,128)(2,1)S(1)}, bf16[768,256]{1,0:T(8,128)(2,1)S(1)}, bf16[256,768]{1,0:T(8,128)(2,1)S(1)}, f32[2,256,1024]{2,1,0:T(8,128)S(1)}) custom-call(bf16[2,768,4096]{2,1,0:T(8,128)(2,1)} %x_ref.7, bf16[2,768,256]{2,1,0:T(8,128)(2,1)} %g_ref.3, bf16[768,2048]{1,0:T(8,128)(2,1)S(1)} %load_to_swap.3.after), custom_call_target="tpu_custom_call" | custom-call | flops 1 | bytes 1 | tf_op jit(solution)/shard_map/fisher_of_own_tokens/pallas_call | solution.py:66
  13.4 2.5 %collective-permute-start.2 = (bf16[2,768,256]{2,1,0:T(8,128)(2,1)S(1)}, bf16[2,768,256]{2,1,0:T(8,128)(2,1)S(1)}, u32[]{:S(2)}, u32[]{:S(2)}) collective-permute-start(bf16[2,768,256]{2,1,0:T(8,128)(2,1)S(1)} %pair_grads.1.after), channel_id=1, source_target_pairs={{0,1},{1,0},{2,3},{3,2},{4,5},{5,4},{6,7},{7,6},{8,9},{9,8},{10,11... | collective-permute-start | bytes 2359304 | tf_op jit(solution)/shard_map/ppermute | solution.py:338
  15.9 1.3 %fisher_of_both_cores.2 = (bf16[256,1024]{1,0:T(8,128)(2,1)S(1)}, bf16[256,1024]{1,0:T(8,128)(2,1)S(1)}, bf16[256,768]{1,0:T(8,128)(2,1)S(1)}) custom-call(bf16[768,2304]{1,0:T(8,128)(2,1)S(1)} %collective-permute-done.got.x_ref.got_a, f32[2,256,1024]{2,1,0:T(8,128)S(1)} %get-tuple-element.42.part_ref, bf16[2,768,256]{2,1,0:T(8,128)(2,1)S(1)} %pair_grads.1.after), custom_call_target="tpu_custom_call" | custom-call | flops 1 | bytes 1 | tf_op jit(solution)/shard_map/fisher_of_both_cores/pallas_call | solution.py:66
  17.2 1.6 %collective-permute-start.5 = (bf16[256,1024]{1,0:T(8,128)(2,1)S(1)}, bf16[256,1024]{1,0:T(8,128)(2,1)S(1)}, u32[]{:S(2)}, u32[]{:S(2)}) collective-permute-start(bf16[256,1024]{1,0:T(8,128)(2,1)S(1)} %get-tuple-element.44.after), channel_id=1, source_target_pairs={{0,8},{2,10},{4,12},{6,14},{8,0},{10,2},{12,4},{14,6},{1,9},{3,11}... | collective-permute-start | bytes 1572872 | tf_op jit(solution)/shard_map/ppermute | solution.py:341
  18.8 2.6 %fisher_of_own_tokens.3 = (bf16[768,2048]{1,0:T(8,128)(2,1)S(1)}, f32[2,256,1024]{2,1,0:T(8,128)S(1)}) custom-call(bf16[2,768,4096]{2,1,0:T(8,128)(2,1)} %x_ref.7, bf16[256,768]{1,0:T(8,128)(2,1)S(1)} %get-tuple-element.41.after.gt_ref, bf16[256,1024]{1,0:T(8,128)(2,1)S(1)} %get-tuple-element.44.after), custom_call_target="tpu_custom_call" | custom-call | flops 1 | bytes 1 | tf_op jit(solution)/shard_map/fisher_of_own_tokens/pallas_call | solution.py:66
  21.4 1.1 %fisher_of_both_cores.3 = (bf16[256,1024]{1,0:T(8,128)(2,1)S(1)}, f32[256,1024]{1,0:T(8,128)S(1)}) custom-call(bf16[768,2048]{1,0:T(8,128)(2,1)S(1)} %collective-permute-done.1.x_ref.got_b, bf16[256,768]{1,0:T(8,128)(2,1)S(1)} %get-tuple-element.46.gt_ref, f32[2,256,1024]{2,1,0:T(8,128)S(1)} %get-tuple-element.47.part_ref, ...), custom_call_target="tpu_custom_call" | custom-call | flops 1 | bytes 1 | tf_op jit(solution)/shard_map/fisher_of_both_cores/pallas_call | solution.py:66
  22.6 2.3 %collective-permute-start.6 = (bf16[256,1024]{1,0:T(8,128)(2,1)S(1)}, bf16[256,1024]{1,0:T(8,128)(2,1)S(1)}, u32[]{:S(2)}, u32[]{:S(2)}) collective-permute-start(bf16[256,1024]{1,0:T(8,128)(2,1)S(1)} %get-tuple-element.48.after), channel_id=1, source_target_pairs={{0,12},{2,14},{4,8},{6,10},{8,4},{10,6},{12,0},{14,2},{1,13},{3,15... | collective-permute-start | bytes 1572872 | tf_op jit(solution)/shard_map/ppermute | solution.py:341
  24.9 16.8 %collective-permute-done.2.g_ref = bf16[2,768,256]{2,1,0:T(8,128)(2,1)S(1)} collective-permute-done((bf16[2,768,256]{2,1,0:T(8,128)(2,1)S(1)}, bf16[2,768,256]{2,1,0:T(8,128)(2,1)S(1)}, u32[]{:S(2)}, u32[]{:S(2)}) %collective-permute-start.2) | collective-permute-done | bytes 786464 | tf_op jit(solution)/shard_map/ppermute | solution.py:338
  41.6 1.9 %fisher_of_other_grads.2 = (bf16[2,256,512]{2,1,0:T(8,128)(2,1)S(1)}, f32[2,256,512]{2,1,0:T(8,128)S(1)}, bf16[256,768]{1,0:T(8,128)(2,1)S(1)}, bf16[256,768]{1,0:T(8,128)(2,1)S(1)}) custom-call(bf16[768,2048]{1,0:T(8,128)(2,1)S(1)} %get-tuple-element.40.own_a, bf16[768,2304]{1,0:T(8,128)(2,1)S(1)} %collective-permute-done.got.x_ref.got_a, ...), custom_call_target="tpu_custom_call" | custom-call | flops 1 | bytes 1 | tf_op jit(solution)/shard_map/fisher_of_other_grads/pallas_call | solution.py:66
  43.7 0.3 collective-permute-start.9
  43.9 0.3 collective-permute-start.3
  44.3 1.9 %fisher_of_other_grads.3 = (bf16[2,256,512]{2,1,0:T(8,128)(2,1)S(1)}, f32[2,256,512]{2,1,0:T(8,128)S(1)}) custom-call(bf16[768,2048]{1,0:T(8,128)(2,1)S(1)} %get-tuple-element.40.own_a, bf16[768,2304]{1,0:T(8,128)(2,1)S(1)} %collective-permute-done.got.x_ref.got_a, bf16[768,2048]{1,0:T(8,128)(2,1)S(1)} %get-tuple-element.45.after.own_b, ...), custom_call_target="tpu_custom_call" | custom-call | flops 1 | bytes 1 | tf_op jit(solution)/shard_map/fisher_of_other_grads/pallas_call | solution.py:66
  46.1 2.9 %collective-permute-start.14 = (bf16[2,256,512]{2,1,0:T(8,128)(2,1)S(1)}, bf16[2,256,512]{2,1,0:T(8,128)(2,1)S(1)}, u32[]{:S(2)}, u32[]{:S(2)}) collective-permute-start(bf16[2,256,512]{2,1,0:T(8,128)(2,1)S(1)} %get-tuple-element.66), channel_id=1, source_target_pairs={{0,12},{2,14},{4,8},{6,10},{8,4},{10,6},{12,0},{14,2},{1,13},{3,15... | collective-permute-start | bytes 1572872 | tf_op jit(solution)/shard_map/ppermute | solution.py:341
  49.0 1.6 %fisher_over_tokens.3 = (f32[256,512]{1,0:T(8,128)S(1)}, bf16[256,512]{1,0:T(8,128)(2,1)S(1)}) custom-call(f32[256,1024]{1,0:T(8,128)S(1)} %get-tuple-element.51.own, bf16[256,1024]{1,0:T(8,128)(2,1)S(1)} %collective-permute-done.4.one, bf16[256,1024]{1,0:T(8,128)(2,1)S(1)} %collective-permute-done.5.two, ...), custom_call_target="tpu_custom_call" | custom-call | flops 1 | bytes 1 | tf_op jit(solution)/shard_map/fisher_over_tokens/pallas_call | solution.py:66
  50.7 0.6 collective-permute-start.8
  51.3 1.2 %collective-permute-done.8.refs_1_ = bf16[256,512]{1,0:T(8,128)(2,1)S(1)} collective-permute-done((bf16[256,512]{1,0:T(8,128)(2,1)S(1)}, bf16[256,512]{1,0:T(8,128)(2,1)S(1)}, u32[]{:S(2)}, u32[]{:S(2)}) %collective-permute-start.8) | collective-permute-done | bytes 262176 | tf_op jit(solution)/shard_map/ppermute | solution.py:335
  52.5 0.5 weigh_members.2
  53.0 1.7 %collective-permute-start.11 = (f32[2,128,256]{2,1,0:T(8,128)S(1)}, f32[2,128,256]{2,1,0:T(8,128)S(1)}, u32[]{:S(2)}, u32[]{:S(2)}) collective-permute-start(f32[2,128,256]{2,1,0:T(8,128)S(1)} %get-tuple-element.63), channel_id=1, source_target_pairs={{0,16},{16,32},{32,48},{48,0},{64,80},{80,96},{96,112},{112,64},{1... | collective-permute-start | bytes 786440 | tf_op jit(solution)/shard_map/ppermute | solution.py:374
  54.7 3.3 %collective-permute-start.12 = (f32[2,128,256]{2,1,0:T(8,128)S(1)}, f32[2,128,256]{2,1,0:T(8,128)S(1)}, u32[]{:S(2)}, u32[]{:S(2)}) collective-permute-start(f32[2,128,256]{2,1,0:T(8,128)S(1)} %get-tuple-element.64), channel_id=1, source_target_pairs={{0,32},{16,48},{32,0},{48,16},{64,96},{80,112},{96,64},{112,80},{1... | collective-permute-start | bytes 786440 | tf_op jit(solution)/shard_map/ppermute | solution.py:374
  58.0 0.7 collective-permute-start.13
  58.7 0.7 fisher_over_first_swap.2
  59.5 1.9 %collective-permute-start.10 = (bf16[256,512]{1,0:T(8,128)(2,1)S(1)}, bf16[256,512]{1,0:T(8,128)(2,1)S(1)}, u32[]{:S(2)}, u32[]{:S(2)}) collective-permute-start(bf16[256,512]{1,0:T(8,128)(2,1)S(1)} %get-tuple-element.62), channel_id=1, source_target_pairs={{0,12},{2,14},{4,8},{6,10},{8,4},{10,6},{12,0},{14,2},{1,13},{3,15... | collective-permute-start | bytes 786440 | tf_op jit(solution)/shard_map/ppermute | solution.py:341
  61.3 0.7 fisher_over_first_swap.3
  62.1 0.6 collective-permute-start.15
  62.7 0.5 collective-permute-done.11.one
  63.2 6.5 %collective-permute-done.12.two = f32[2,128,256]{2,1,0:T(8,128)S(1)} collective-permute-done((f32[2,128,256]{2,1,0:T(8,128)S(1)}, f32[2,128,256]{2,1,0:T(8,128)S(1)}, u32[]{:S(2)}, u32[]{:S(2)}) %collective-permute-start.12) | collective-permute-done | bytes 262176 | tf_op jit(solution)/shard_map/ppermute | solution.py:374
  69.8 0.3 fisher_over_tokens.4.first_ref
  70.1 0.6 fisher_over_tokens.5
  70.7 1.3 %collective-permute-start.16 = (bf16[256,512]{1,0:T(8,128)(2,1)S(1)}, bf16[256,512]{1,0:T(8,128)(2,1)S(1)}, u32[]{:S(2)}, u32[]{:S(2)}) collective-permute-start(bf16[256,512]{1,0:T(8,128)(2,1)S(1)} %get-tuple-element.70), channel_id=1, source_target_pairs={{0,2},{2,0},{4,6},{6,4},{8,10},{10,8},{12,14},{14,12},{1,3},{3,1},... | collective-permute-start | bytes 786440 | tf_op jit(solution)/shard_map/ppermute | solution.py:335
  72.0 1.2 %collective-permute-done.16.refs_1_ = bf16[256,512]{1,0:T(8,128)(2,1)S(1)} collective-permute-done((bf16[256,512]{1,0:T(8,128)(2,1)S(1)}, bf16[256,512]{1,0:T(8,128)(2,1)S(1)}, u32[]{:S(2)}, u32[]{:S(2)}) %collective-permute-start.16) | collective-permute-done | bytes 262176 | tf_op jit(solution)/shard_map/ppermute | solution.py:335
  73.1 0.7 weigh_members.3
  73.9 1.3 %collective-permute-start.17 = (bf16[3,128,256]{2,1,0:T(8,128)(2,1)S(1)}, bf16[3,128,256]{2,1,0:T(8,128)(2,1)S(1)}, u32[]{:S(2)}, u32[]{:S(2)}) collective-permute-start(bf16[3,128,256]{2,1,0:T(8,128)(2,1)S(1)} %get-tuple-element.71), channel_id=1, source_target_pairs={{0,16},{16,32},{32,48},{48,0},{64,80},{80,96},{96,112},{112,64},{1... | collective-permute-start | bytes 589832 | tf_op jit(solution)/shard_map/ppermute | solution.py:374
  75.2 3.3 %collective-permute-start.18 = (bf16[3,128,256]{2,1,0:T(8,128)(2,1)S(1)}, bf16[3,128,256]{2,1,0:T(8,128)(2,1)S(1)}, u32[]{:S(2)}, u32[]{:S(2)}) collective-permute-start(bf16[3,128,256]{2,1,0:T(8,128)(2,1)S(1)} %get-tuple-element.72), channel_id=1, source_target_pairs={{0,32},{16,48},{32,0},{48,16},{64,96},{80,112},{96,64},{112,80},{1... | collective-permute-start | bytes 589832 | tf_op jit(solution)/shard_map/ppermute | solution.py:374
  78.5 0.7 collective-permute-start.19
  79.2 1.3 %collective-permute-start.23 = (bf16[3,128,256]{2,1,0:T(8,128)(2,1)S(1)}, bf16[3,128,256]{2,1,0:T(8,128)(2,1)S(1)}, u32[]{:S(2)}, u32[]{:S(2)}) collective-permute-start(bf16[3,128,256]{2,1,0:T(8,128)(2,1)S(1)} %sum_over_z.2.after), channel_id=1, source_target_pairs={{64,0},{65,15},{66,64},{67,79},{68,4},{69,11},{70,68},{71,75},{72,... | collective-permute-start | bytes 589832 | tf_op jit(solution)/shard_map/ppermute | solution.py:361
  80.5 5.4 %collective-permute-start.22 = (bf16[3,128,256]{2,1,0:T(8,128)(2,1)S(1)}, bf16[3,128,256]{2,1,0:T(8,128)(2,1)S(1)}, u32[]{:S(2)}, u32[]{:S(2)}) collective-permute-start(bf16[3,128,256]{2,1,0:T(8,128)(2,1)S(1)} %sum_over_z.2.after), channel_id=1, source_target_pairs={{0,0},{1,15},{2,64},{3,79},{4,4},{5,11},{6,68},{7,75},{8,6},{9,9},... | collective-permute-start | bytes 589832 | tf_op jit(solution)/shard_map/ppermute | solution.py:361
  85.9 1.5 %collective-permute-done.18.two = bf16[3,128,256]{2,1,0:T(8,128)(2,1)S(1)} collective-permute-done((bf16[3,128,256]{2,1,0:T(8,128)(2,1)S(1)}, bf16[3,128,256]{2,1,0:T(8,128)(2,1)S(1)}, u32[]{:S(2)}, u32[]{:S(2)}) %collective-permute-start.18) | collective-permute-done | bytes 196640 | tf_op jit(solution)/shard_map/ppermute | solution.py:374
  87.4 0.3 sum_over_z.3
  87.7 0.7 collective-permute-start.21
  88.4 8.2 %collective-permute-start.20 = (bf16[3,128,256]{2,1,0:T(8,128)(2,1)S(1)}, bf16[3,128,256]{2,1,0:T(8,128)(2,1)S(1)}, u32[]{:S(2)}, u32[]{:S(2)}) collective-permute-start(bf16[3,128,256]{2,1,0:T(8,128)(2,1)S(1)} %sum_over_z.3), channel_id=1, source_target_pairs={{0,1},{1,14},{2,65},{3,78},{4,5},{5,10},{6,69},{7,74},{8,7},{9,8},... | collective-permute-start | bytes 589832 | tf_op jit(solution)/shard_map/ppermute | solution.py:361
  96.6 0.2 meet_over_y.1.sums
  96.8 5.7 %collective-permute-done.20.near = bf16[3,128,256]{2,1,0:T(8,128)(2,1)S(1)} collective-permute-done((bf16[3,128,256]{2,1,0:T(8,128)(2,1)S(1)}, bf16[3,128,256]{2,1,0:T(8,128)(2,1)S(1)}, u32[]{:S(2)}, u32[]{:S(2)}) %collective-permute-start.20) | collective-permute-done | bytes 196640 | tf_op jit(solution)/shard_map/ppermute | solution.py:361
  102.5 0.8 merge_members.1
  (23 shorter events, 0.4 us)
Async XLA Ops:
  2.1 3.6 %copy-start = (bf16[2,1024,256]{2,1,0:T(8,128)(2,1)S(1)}, bf16[2,1024,256]{2,1,0:T(8,128)(2,1)}, u32[]{:S(2)}) copy-start(bf16[2,1024,256]{2,1,0:T(8,128)(2,1)} %param.5) | copy-start | bytes 3145732
  2.1 11.2 %collective-permute-start = (bf16[768,2304]{1,0:T(8,128)(2,1)S(1)}, bf16[768,2304]{1,0:T(8,128)(2,1)S(1)}, u32[]{:S(2)}, u32[]{:S(2)}) collective-permute-start(bf16[768,2304]{1,0:T(8,128)(2,1)S(1)} %load_to_swap.2.after), channel_id=1, source_target_pairs={{0,2},{2,0},{4,6},{6,4},{8,10},{10,8},{12,14},{14,12},{1,3},{3,1},... | collective-permute-start | bytes 10616840 | tf_op jit(solution)/shard_map/ppermute | solution.py:335
  5.5 15.9 %collective-permute-start.1 = (bf16[768,2048]{1,0:T(8,128)(2,1)S(1)}, bf16[768,2048]{1,0:T(8,128)(2,1)S(1)}, u32[]{:S(2)}, u32[]{:S(2)}) collective-permute-start(bf16[768,2048]{1,0:T(8,128)(2,1)S(1)} %load_to_swap.3.after), channel_id=1, source_target_pairs={{0,2},{2,0},{4,6},{6,4},{8,10},{10,8},{12,14},{14,12},{1,3},{3,1},... | collective-permute-start | bytes 9437192 | tf_op jit(solution)/shard_map/ppermute | solution.py:335
  5.7 37.9 %collective-permute-start.7 = (bf16[2,1024,256]{2,1,0:T(8,128)(2,1)S(1)}, bf16[2,1024,256]{2,1,0:T(8,128)(2,1)S(1)}, u32[]{:S(2)}, u32[]{:S(2)}) collective-permute-start(bf16[2,1024,256]{2,1,0:T(8,128)(2,1)S(1)} %copy-done), channel_id=1, source_target_pairs={{0,0},{1,2},{2,12},{3,14},{4,4},{5,6},{6,8},{7,10},{8,9},{9,11},{1... | collective-permute-start | bytes 3145736 | tf_op jit(solution)/shard_map/ppermute | solution.py:364
  13.4 28.3 %collective-permute-start.2 = (bf16[2,768,256]{2,1,0:T(8,128)(2,1)S(1)}, bf16[2,768,256]{2,1,0:T(8,128)(2,1)S(1)}, u32[]{:S(2)}, u32[]{:S(2)}) collective-permute-start(bf16[2,768,256]{2,1,0:T(8,128)(2,1)S(1)} %pair_grads.1.after), channel_id=1, source_target_pairs={{0,1},{1,0},{2,3},{3,2},{4,5},{5,4},{6,7},{7,6},{8,9},{9,8},{10,11... | collective-permute-start | bytes 2359304 | tf_op jit(solution)/shard_map/ppermute | solution.py:338
  17.1 29.0 %collective-permute-start.4 = (bf16[256,1024]{1,0:T(8,128)(2,1)S(1)}, bf16[256,1024]{1,0:T(8,128)(2,1)S(1)}, u32[]{:S(2)}, u32[]{:S(2)}) collective-permute-start(bf16[256,1024]{1,0:T(8,128)(2,1)S(1)} %get-tuple-element.52), channel_id=1, source_target_pairs={{0,4},{2,6},{4,0},{6,2},{8,12},{10,14},{12,8},{14,10},{1,5},{3,7},... | collective-permute-start | bytes 1572872 | tf_op jit(solution)/shard_map/ppermute | solution.py:341
  17.2 31.8 %collective-permute-start.5 = (bf16[256,1024]{1,0:T(8,128)(2,1)S(1)}, bf16[256,1024]{1,0:T(8,128)(2,1)S(1)}, u32[]{:S(2)}, u32[]{:S(2)}) collective-permute-start(bf16[256,1024]{1,0:T(8,128)(2,1)S(1)} %get-tuple-element.44.after), channel_id=1, source_target_pairs={{0,8},{2,10},{4,12},{6,14},{8,0},{10,2},{12,4},{14,6},{1,9},{3,11}... | collective-permute-start | bytes 1572872 | tf_op jit(solution)/shard_map/ppermute | solution.py:341
  22.6 26.5 %collective-permute-start.6 = (bf16[256,1024]{1,0:T(8,128)(2,1)S(1)}, bf16[256,1024]{1,0:T(8,128)(2,1)S(1)}, u32[]{:S(2)}, u32[]{:S(2)}) collective-permute-start(bf16[256,1024]{1,0:T(8,128)(2,1)S(1)} %get-tuple-element.48.after), channel_id=1, source_target_pairs={{0,12},{2,14},{4,8},{6,10},{8,4},{10,6},{12,0},{14,2},{1,13},{3,15... | collective-permute-start | bytes 1572872 | tf_op jit(solution)/shard_map/ppermute | solution.py:341
  43.7 8.8 %collective-permute-start.9 = (bf16[2,512,256]{2,1,0:T(8,128)(2,1)S(1)}, bf16[2,512,256]{2,1,0:T(8,128)(2,1)S(1)}, u32[]{:S(2)}, u32[]{:S(2)}) collective-permute-start(bf16[2,512,256]{2,1,0:T(8,128)(2,1)S(1)} %get-tuple-element.59), channel_id=1, source_target_pairs={{0,2},{2,0},{4,6},{6,4},{8,10},{10,8},{12,14},{14,12},{1,3},{3,1},... | collective-permute-start | bytes 1572872 | tf_op jit(solution)/shard_map/ppermute | solution.py:335
  43.9 14.8 %collective-permute-start.3 = (bf16[2,256,512]{2,1,0:T(8,128)(2,1)S(1)}, bf16[2,256,512]{2,1,0:T(8,128)(2,1)S(1)}, u32[]{:S(2)}, u32[]{:S(2)}) collective-permute-start(bf16[2,256,512]{2,1,0:T(8,128)(2,1)S(1)} %get-tuple-element.50), channel_id=1, source_target_pairs={{0,4},{2,6},{4,0},{6,2},{8,12},{10,14},{12,8},{14,10},{1,5},{3,7},... | collective-permute-start | bytes 1572872 | tf_op jit(solution)/shard_map/ppermute | solution.py:341
  46.1 15.2 %collective-permute-start.14 = (bf16[2,256,512]{2,1,0:T(8,128)(2,1)S(1)}, bf16[2,256,512]{2,1,0:T(8,128)(2,1)S(1)}, u32[]{:S(2)}, u32[]{:S(2)}) collective-permute-start(bf16[2,256,512]{2,1,0:T(8,128)(2,1)S(1)} %get-tuple-element.66), channel_id=1, source_target_pairs={{0,12},{2,14},{4,8},{6,10},{8,4},{10,6},{12,0},{14,2},{1,13},{3,15... | collective-permute-start | bytes 1572872 | tf_op jit(solution)/shard_map/ppermute | solution.py:341
  50.7 1.8 %collective-permute-start.8 = (bf16[256,512]{1,0:T(8,128)(2,1)S(1)}, bf16[256,512]{1,0:T(8,128)(2,1)S(1)}, u32[]{:S(2)}, u32[]{:S(2)}) collective-permute-start(bf16[256,512]{1,0:T(8,128)(2,1)S(1)} %get-tuple-element.58), channel_id=1, source_target_pairs={{0,2},{2,0},{4,6},{6,4},{8,10},{10,8},{12,14},{14,12},{1,3},{3,1},... | collective-permute-start | bytes 786440 | tf_op jit(solution)/shard_map/ppermute | solution.py:335
  53.0 10.2 %collective-permute-start.11 = (f32[2,128,256]{2,1,0:T(8,128)S(1)}, f32[2,128,256]{2,1,0:T(8,128)S(1)}, u32[]{:S(2)}, u32[]{:S(2)}) collective-permute-start(f32[2,128,256]{2,1,0:T(8,128)S(1)} %get-tuple-element.63), channel_id=1, source_target_pairs={{0,16},{16,32},{32,48},{48,0},{64,80},{80,96},{96,112},{112,64},{1... | collective-permute-start | bytes 786440 | tf_op jit(solution)/shard_map/ppermute | solution.py:374
  54.7 15.0 %collective-permute-start.12 = (f32[2,128,256]{2,1,0:T(8,128)S(1)}, f32[2,128,256]{2,1,0:T(8,128)S(1)}, u32[]{:S(2)}, u32[]{:S(2)}) collective-permute-start(f32[2,128,256]{2,1,0:T(8,128)S(1)} %get-tuple-element.64), channel_id=1, source_target_pairs={{0,32},{16,48},{32,0},{48,16},{64,96},{80,112},{96,64},{112,80},{1... | collective-permute-start | bytes 786440 | tf_op jit(solution)/shard_map/ppermute | solution.py:374
  58.0 11.7 %collective-permute-start.13 = (f32[2,128,256]{2,1,0:T(8,128)S(1)}, f32[2,128,256]{2,1,0:T(8,128)S(1)}, u32[]{:S(2)}, u32[]{:S(2)}) collective-permute-start(f32[2,128,256]{2,1,0:T(8,128)S(1)} %get-tuple-element.65), channel_id=1, source_target_pairs={{0,48},{16,0},{32,16},{48,32},{64,112},{80,64},{96,80},{112,96},{1... | collective-permute-start | bytes 786440 | tf_op jit(solution)/shard_map/ppermute | solution.py:374
  59.5 10.3 %collective-permute-start.10 = (bf16[256,512]{1,0:T(8,128)(2,1)S(1)}, bf16[256,512]{1,0:T(8,128)(2,1)S(1)}, u32[]{:S(2)}, u32[]{:S(2)}) collective-permute-start(bf16[256,512]{1,0:T(8,128)(2,1)S(1)} %get-tuple-element.62), channel_id=1, source_target_pairs={{0,12},{2,14},{4,8},{6,10},{8,4},{10,6},{12,0},{14,2},{1,13},{3,15... | collective-permute-start | bytes 786440 | tf_op jit(solution)/shard_map/ppermute | solution.py:341
  62.1 8.0 %collective-permute-start.15 = (bf16[256,512]{1,0:T(8,128)(2,1)S(1)}, bf16[256,512]{1,0:T(8,128)(2,1)S(1)}, u32[]{:S(2)}, u32[]{:S(2)}) collective-permute-start(bf16[256,512]{1,0:T(8,128)(2,1)S(1)} %get-tuple-element.68), channel_id=1, source_target_pairs={{0,4},{2,6},{4,0},{6,2},{8,12},{10,14},{12,8},{14,10},{1,5},{3,7},... | collective-permute-start | bytes 786440 | tf_op jit(solution)/shard_map/ppermute | solution.py:341
  70.7 2.4 %collective-permute-start.16 = (bf16[256,512]{1,0:T(8,128)(2,1)S(1)}, bf16[256,512]{1,0:T(8,128)(2,1)S(1)}, u32[]{:S(2)}, u32[]{:S(2)}) collective-permute-start(bf16[256,512]{1,0:T(8,128)(2,1)S(1)} %get-tuple-element.70), channel_id=1, source_target_pairs={{0,2},{2,0},{4,6},{6,4},{8,10},{10,8},{12,14},{14,12},{1,3},{3,1},... | collective-permute-start | bytes 786440 | tf_op jit(solution)/shard_map/ppermute | solution.py:335
  73.9 12.0 %collective-permute-start.17 = (bf16[3,128,256]{2,1,0:T(8,128)(2,1)S(1)}, bf16[3,128,256]{2,1,0:T(8,128)(2,1)S(1)}, u32[]{:S(2)}, u32[]{:S(2)}) collective-permute-start(bf16[3,128,256]{2,1,0:T(8,128)(2,1)S(1)} %get-tuple-element.71), channel_id=1, source_target_pairs={{0,16},{16,32},{32,48},{48,0},{64,80},{80,96},{96,112},{112,64},{1... | collective-permute-start | bytes 589832 | tf_op jit(solution)/shard_map/ppermute | solution.py:374
  75.2 12.2 %collective-permute-start.18 = (bf16[3,128,256]{2,1,0:T(8,128)(2,1)S(1)}, bf16[3,128,256]{2,1,0:T(8,128)(2,1)S(1)}, u32[]{:S(2)}, u32[]{:S(2)}) collective-permute-start(bf16[3,128,256]{2,1,0:T(8,128)(2,1)S(1)} %get-tuple-element.72), channel_id=1, source_target_pairs={{0,32},{16,48},{32,0},{48,16},{64,96},{80,112},{96,64},{112,80},{1... | collective-permute-start | bytes 589832 | tf_op jit(solution)/shard_map/ppermute | solution.py:374
  78.5 8.9 %collective-permute-start.19 = (bf16[3,128,256]{2,1,0:T(8,128)(2,1)S(1)}, bf16[3,128,256]{2,1,0:T(8,128)(2,1)S(1)}, u32[]{:S(2)}, u32[]{:S(2)}) collective-permute-start(bf16[3,128,256]{2,1,0:T(8,128)(2,1)S(1)} %get-tuple-element.73), channel_id=1, source_target_pairs={{0,48},{16,0},{32,16},{48,32},{64,112},{80,64},{96,80},{112,96},{1... | collective-permute-start | bytes 589832 | tf_op jit(solution)/shard_map/ppermute | solution.py:374
  79.2 17.4 %collective-permute-start.23 = (bf16[3,128,256]{2,1,0:T(8,128)(2,1)S(1)}, bf16[3,128,256]{2,1,0:T(8,128)(2,1)S(1)}, u32[]{:S(2)}, u32[]{:S(2)}) collective-permute-start(bf16[3,128,256]{2,1,0:T(8,128)(2,1)S(1)} %sum_over_z.2.after), channel_id=1, source_target_pairs={{64,0},{65,15},{66,64},{67,79},{68,4},{69,11},{70,68},{71,75},{72,... | collective-permute-start | bytes 589832 | tf_op jit(solution)/shard_map/ppermute | solution.py:361
  80.5 16.1 %collective-permute-start.22 = (bf16[3,128,256]{2,1,0:T(8,128)(2,1)S(1)}, bf16[3,128,256]{2,1,0:T(8,128)(2,1)S(1)}, u32[]{:S(2)}, u32[]{:S(2)}) collective-permute-start(bf16[3,128,256]{2,1,0:T(8,128)(2,1)S(1)} %sum_over_z.2.after), channel_id=1, source_target_pairs={{0,0},{1,15},{2,64},{3,79},{4,4},{5,11},{6,68},{7,75},{8,6},{9,9},... | collective-permute-start | bytes 589832 | tf_op jit(solution)/shard_map/ppermute | solution.py:361
  87.7 9.1 %collective-permute-start.21 = (bf16[3,128,256]{2,1,0:T(8,128)(2,1)S(1)}, bf16[3,128,256]{2,1,0:T(8,128)(2,1)S(1)}, u32[]{:S(2)}, u32[]{:S(2)}) collective-permute-start(bf16[3,128,256]{2,1,0:T(8,128)(2,1)S(1)} %sum_over_z.3), channel_id=1, source_target_pairs={{64,1},{65,14},{66,65},{67,78},{68,5},{69,10},{70,69},{71,74},{72,... | collective-permute-start | bytes 589832 | tf_op jit(solution)/shard_map/ppermute | solution.py:361
  88.4 14.1 %collective-permute-start.20 = (bf16[3,128,256]{2,1,0:T(8,128)(2,1)S(1)}, bf16[3,128,256]{2,1,0:T(8,128)(2,1)S(1)}, u32[]{:S(2)}, u32[]{:S(2)}) collective-permute-start(bf16[3,128,256]{2,1,0:T(8,128)(2,1)S(1)} %sum_over_z.3), channel_id=1, source_target_pairs={{0,1},{1,14},{2,65},{3,78},{4,5},{5,10},{6,69},{7,74},{8,7},{9,8},... | collective-permute-start | bytes 589832 | tf_op jit(solution)/shard_map/ppermute | solution.py:361

commit v19 on v18

--- a/solution.py
+++ b/solution.py
@@ -358,7 +358,7 @@
         return kept_block, swap_cores(sent)
 
     def results(phase, sums):
-        return [lax.ppermute(sums, ("member", "tok", "col"), result_pairs(phase, y_lo)) for y_lo in range(2)]
+        return [lax.ppermute(sums, ("member", "tok", "col"), result_pairs(phase, y_lo)) for y_lo in (1, 0)]
 
     def bring_weights(after):
         arrived = lax.ppermute(weights, ("tok", "col"), weight_pairs())

time: 104 us -> 104 us (level)
  starting transfers between devices: 47.4 us -> 43.8 us
  waiting for transfers between devices: 33.2 us -> 36.6 us
    ppermute x4, starting transfers between devices: 15.5 us -> 11.9 us  [results(): lax.ppermute(sums, ('member', 'tok', 'col'), result_pairs(phase, y_lo))]
    ppermute x4, waiting for transfers between devices: 5.73 us -> 8.04 us  [results(): lax.ppermute(sums, ('member', 'tok', 'col'), result_pairs(phase, y_lo))]
    ppermute x6, waiting for transfers between devices: 8.39 us -> 9.45 us  [weigh(): return [lax.ppermute(v, 'member', z_pairs(d)) for d, v in send] + [own_sums]]
where the time goes in v19:
time: 104 us; the launch traced here: 103 us
  starting transfers between devices  43.8 us (42%)
  waiting for transfers between devices  36.6 us (35%)
  Pallas kernels  22.4 us (22%)
    pallas_call x20, Pallas kernels, call(): pl.pallas_call(kernel, out_shape=shapes, in_specs=[HBM] * len(hbm) + [VME...  21.6 us
    ppermute x1, waiting for transfers between devices, swap_cols(): return lax.ppermute(send, 'col', [(0, 1), (1, 0)])  16.8 us
    ppermute x4, starting transfers between devices, results(): lax.ppermute(sums, ('member', 'tok', 'col'), result_pairs(phase, y_lo))  11.9 us
    ppermute x6, starting transfers between devices, weigh(): return [lax.ppermute(v, 'member', z_pairs(d)) for d, v in send] + [own_sums]  11.1 us
    ppermute x7, starting transfers between devices, swap_x(): return lax.ppermute(sent, 'tok', x_pairs(flip))  9.72 us
    ppermute x6, waiting for transfers between devices, weigh(): return [lax.ppermute(v, 'member', z_pairs(d)) for d, v in send] + [own_sums]  9.45 us
    ppermute x4, waiting for transfers between devices, results(): lax.ppermute(sums, ('member', 'tok', 'col'), result_pairs(phase, y_lo))  8.04 us
    ppermute x1, starting transfers between devices, bring_weights(): arrived = lax.ppermute(weights, ('tok', 'col'), weight_pairs())  4.75 us
  transfers between devices with their start and end apart: 24, of which 7 were waited for; matrix products, arithmetic and copies ran while one was open for 0% of the time, Pallas kernels for 18%

profile of v19, /device:TPU:1, one launch (start us, length us, event | category | flops | bytes accessed | tf_op | source)
XLA Modules:
  0.0 103.1 jit_solution(14802319414604583802)
XLA Ops:
  0.0 2.0 %load_to_swap.2.after = bf16[768,2304]{1,0:T(8,128)(2,1)S(1)} custom-call(bf16[2,768,4096]{2,1,0:T(8,128)(2,1)} %x_ref.7, bf16[2,768,256]{2,1,0:T(8,128)(2,1)} %g_ref.3), custom_call_target="tpu_custom_call" | custom-call | flops 1 | bytes 1 | tf_op jit(solution)/shard_map/load_to_swap/pallas_call | solution.py:66
  2.1 1.5 %collective-permute-start = (bf16[768,2304]{1,0:T(8,128)(2,1)S(1)}, bf16[768,2304]{1,0:T(8,128)(2,1)S(1)}, u32[]{:S(2)}, u32[]{:S(2)}) collective-permute-start(bf16[768,2304]{1,0:T(8,128)(2,1)S(1)} %load_to_swap.2.after), channel_id=1, source_target_pairs={{0,2},{2,0},{4,6},{6,4},{8,10},{10,8},{12,14},{14,12},{1,3},{3,1},... | collective-permute-start | bytes 10616840 | tf_op jit(solution)/shard_map/ppermute | solution.py:335
  3.6 1.9 %load_to_swap.3.after = bf16[768,2048]{1,0:T(8,128)(2,1)S(1)} custom-call(bf16[2,768,4096]{2,1,0:T(8,128)(2,1)} %x_ref.7, bf16[768,2304]{1,0:T(8,128)(2,1)S(1)} %load_to_swap.2.after), custom_call_target="tpu_custom_call" | custom-call | flops 1 | bytes 1 | tf_op jit(solution)/shard_map/load_to_swap/pallas_call | solution.py:66
  5.5 0.2 collective-permute-start.1
  5.7 4.8 %collective-permute-start.7 = (bf16[2,1024,256]{2,1,0:T(8,128)(2,1)S(1)}, bf16[2,1024,256]{2,1,0:T(8,128)(2,1)S(1)}, u32[]{:S(2)}, u32[]{:S(2)}) collective-permute-start(bf16[2,1024,256]{2,1,0:T(8,128)(2,1)S(1)} %copy-done), channel_id=1, source_target_pairs={{0,0},{1,2},{2,12},{3,14},{4,4},{5,6},{6,8},{7,10},{8,9},{9,11},{1... | collective-permute-start | bytes 3145736 | tf_op jit(solution)/shard_map/ppermute | solution.py:364
  10.4 2.9 %fisher_of_own_tokens.2 = (bf16[768,2048]{1,0:T(8,128)(2,1)S(1)}, bf16[768,256]{1,0:T(8,128)(2,1)S(1)}, bf16[256,768]{1,0:T(8,128)(2,1)S(1)}, f32[2,256,1024]{2,1,0:T(8,128)S(1)}) custom-call(bf16[2,768,4096]{2,1,0:T(8,128)(2,1)} %x_ref.7, bf16[2,768,256]{2,1,0:T(8,128)(2,1)} %g_ref.3, bf16[768,2048]{1,0:T(8,128)(2,1)S(1)} %load_to_swap.3.after), custom_call_target="tpu_custom_call" | custom-call | flops 1 | bytes 1 | tf_op jit(solution)/shard_map/fisher_of_own_tokens/pallas_call | solution.py:66
  13.4 2.5 %collective-permute-start.2 = (bf16[2,768,256]{2,1,0:T(8,128)(2,1)S(1)}, bf16[2,768,256]{2,1,0:T(8,128)(2,1)S(1)}, u32[]{:S(2)}, u32[]{:S(2)}) collective-permute-start(bf16[2,768,256]{2,1,0:T(8,128)(2,1)S(1)} %pair_grads.1.after), channel_id=1, source_target_pairs={{0,1},{1,0},{2,3},{3,2},{4,5},{5,4},{6,7},{7,6},{8,9},{9,8},{10,11... | collective-permute-start | bytes 2359304 | tf_op jit(solution)/shard_map/ppermute | solution.py:338
  15.9 1.3 %fisher_of_both_cores.2 = (bf16[256,1024]{1,0:T(8,128)(2,1)S(1)}, bf16[256,1024]{1,0:T(8,128)(2,1)S(1)}, bf16[256,768]{1,0:T(8,128)(2,1)S(1)}) custom-call(bf16[768,2304]{1,0:T(8,128)(2,1)S(1)} %collective-permute-done.got.x_ref.got_a, f32[2,256,1024]{2,1,0:T(8,128)S(1)} %get-tuple-element.42.part_ref, bf16[2,768,256]{2,1,0:T(8,128)(2,1)S(1)} %pair_grads.1.after), custom_call_target="tpu_custom_call" | custom-call | flops 1 | bytes 1 | tf_op jit(solution)/shard_map/fisher_of_both_cores/pallas_call | solution.py:66
  17.2 1.6 %collective-permute-start.5 = (bf16[256,1024]{1,0:T(8,128)(2,1)S(1)}, bf16[256,1024]{1,0:T(8,128)(2,1)S(1)}, u32[]{:S(2)}, u32[]{:S(2)}) collective-permute-start(bf16[256,1024]{1,0:T(8,128)(2,1)S(1)} %get-tuple-element.44.after), channel_id=1, source_target_pairs={{0,8},{2,10},{4,12},{6,14},{8,0},{10,2},{12,4},{14,6},{1,9},{3,11}... | collective-permute-start | bytes 1572872 | tf_op jit(solution)/shard_map/ppermute | solution.py:341
  18.8 2.6 %fisher_of_own_tokens.3 = (bf16[768,2048]{1,0:T(8,128)(2,1)S(1)}, f32[2,256,1024]{2,1,0:T(8,128)S(1)}) custom-call(bf16[2,768,4096]{2,1,0:T(8,128)(2,1)} %x_ref.7, bf16[256,768]{1,0:T(8,128)(2,1)S(1)} %get-tuple-element.41.after.gt_ref, bf16[256,1024]{1,0:T(8,128)(2,1)S(1)} %get-tuple-element.44.after), custom_call_target="tpu_custom_call" | custom-call | flops 1 | bytes 1 | tf_op jit(solution)/shard_map/fisher_of_own_tokens/pallas_call | solution.py:66
  21.4 1.1 %fisher_of_both_cores.3 = (bf16[256,1024]{1,0:T(8,128)(2,1)S(1)}, f32[256,1024]{1,0:T(8,128)S(1)}) custom-call(bf16[768,2048]{1,0:T(8,128)(2,1)S(1)} %collective-permute-done.1.x_ref.got_b, bf16[256,768]{1,0:T(8,128)(2,1)S(1)} %get-tuple-element.46.gt_ref, f32[2,256,1024]{2,1,0:T(8,128)S(1)} %get-tuple-element.47.part_ref, ...), custom_call_target="tpu_custom_call" | custom-call | flops 1 | bytes 1 | tf_op jit(solution)/shard_map/fisher_of_both_cores/pallas_call | solution.py:66
  22.6 2.3 %collective-permute-start.6 = (bf16[256,1024]{1,0:T(8,128)(2,1)S(1)}, bf16[256,1024]{1,0:T(8,128)(2,1)S(1)}, u32[]{:S(2)}, u32[]{:S(2)}) collective-permute-start(bf16[256,1024]{1,0:T(8,128)(2,1)S(1)} %get-tuple-element.48.after), channel_id=1, source_target_pairs={{0,12},{2,14},{4,8},{6,10},{8,4},{10,6},{12,0},{14,2},{1,13},{3,15... | collective-permute-start | bytes 1572872 | tf_op jit(solution)/shard_map/ppermute | solution.py:341
  24.9 16.8 %collective-permute-done.2.g_ref = bf16[2,768,256]{2,1,0:T(8,128)(2,1)S(1)} collective-permute-done((bf16[2,768,256]{2,1,0:T(8,128)(2,1)S(1)}, bf16[2,768,256]{2,1,0:T(8,128)(2,1)S(1)}, u32[]{:S(2)}, u32[]{:S(2)}) %collective-permute-start.2) | collective-permute-done | bytes 786464 | tf_op jit(solution)/shard_map/ppermute | solution.py:338
  41.6 1.9 %fisher_of_other_grads.2 = (bf16[2,256,512]{2,1,0:T(8,128)(2,1)S(1)}, f32[2,256,512]{2,1,0:T(8,128)S(1)}, bf16[256,768]{1,0:T(8,128)(2,1)S(1)}, bf16[256,768]{1,0:T(8,128)(2,1)S(1)}) custom-call(bf16[768,2048]{1,0:T(8,128)(2,1)S(1)} %get-tuple-element.40.own_a, bf16[768,2304]{1,0:T(8,128)(2,1)S(1)} %collective-permute-done.got.x_ref.got_a, ...), custom_call_target="tpu_custom_call" | custom-call | flops 1 | bytes 1 | tf_op jit(solution)/shard_map/fisher_of_other_grads/pallas_call | solution.py:66
  43.7 0.3 collective-permute-start.9
  43.9 0.3 collective-permute-start.3
  44.3 1.9 %fisher_of_other_grads.3 = (bf16[2,256,512]{2,1,0:T(8,128)(2,1)S(1)}, f32[2,256,512]{2,1,0:T(8,128)S(1)}) custom-call(bf16[768,2048]{1,0:T(8,128)(2,1)S(1)} %get-tuple-element.40.own_a, bf16[768,2304]{1,0:T(8,128)(2,1)S(1)} %collective-permute-done.got.x_ref.got_a, bf16[768,2048]{1,0:T(8,128)(2,1)S(1)} %get-tuple-element.45.after.own_b, ...), custom_call_target="tpu_custom_call" | custom-call | flops 1 | bytes 1 | tf_op jit(solution)/shard_map/fisher_of_other_grads/pallas_call | solution.py:66
  46.1 2.9 %collective-permute-start.14 = (bf16[2,256,512]{2,1,0:T(8,128)(2,1)S(1)}, bf16[2,256,512]{2,1,0:T(8,128)(2,1)S(1)}, u32[]{:S(2)}, u32[]{:S(2)}) collective-permute-start(bf16[2,256,512]{2,1,0:T(8,128)(2,1)S(1)} %get-tuple-element.66), channel_id=1, source_target_pairs={{0,12},{2,14},{4,8},{6,10},{8,4},{10,6},{12,0},{14,2},{1,13},{3,15... | collective-permute-start | bytes 1572872 | tf_op jit(solution)/shard_map/ppermute | solution.py:341
  49.0 1.6 %fisher_over_tokens.3 = (f32[256,512]{1,0:T(8,128)S(1)}, bf16[256,512]{1,0:T(8,128)(2,1)S(1)}) custom-call(f32[256,1024]{1,0:T(8,128)S(1)} %get-tuple-element.51.own, bf16[256,1024]{1,0:T(8,128)(2,1)S(1)} %collective-permute-done.4.one, bf16[256,1024]{1,0:T(8,128)(2,1)S(1)} %collective-permute-done.5.two, ...), custom_call_target="tpu_custom_call" | custom-call | flops 1 | bytes 1 | tf_op jit(solution)/shard_map/fisher_over_tokens/pallas_call | solution.py:66
  50.7 0.6 collective-permute-start.8
  51.3 1.2 %collective-permute-done.8.refs_1_ = bf16[256,512]{1,0:T(8,128)(2,1)S(1)} collective-permute-done((bf16[256,512]{1,0:T(8,128)(2,1)S(1)}, bf16[256,512]{1,0:T(8,128)(2,1)S(1)}, u32[]{:S(2)}, u32[]{:S(2)}) %collective-permute-start.8) | collective-permute-done | bytes 262176 | tf_op jit(solution)/shard_map/ppermute | solution.py:335
  52.5 0.5 weigh_members.2
  53.0 1.7 %collective-permute-start.11 = (f32[2,128,256]{2,1,0:T(8,128)S(1)}, f32[2,128,256]{2,1,0:T(8,128)S(1)}, u32[]{:S(2)}, u32[]{:S(2)}) collective-permute-start(f32[2,128,256]{2,1,0:T(8,128)S(1)} %get-tuple-element.63), channel_id=1, source_target_pairs={{0,16},{16,32},{32,48},{48,0},{64,80},{80,96},{96,112},{112,64},{1... | collective-permute-start | bytes 786440 | tf_op jit(solution)/shard_map/ppermute | solution.py:374
  54.7 3.3 %collective-permute-start.12 = (f32[2,128,256]{2,1,0:T(8,128)S(1)}, f32[2,128,256]{2,1,0:T(8,128)S(1)}, u32[]{:S(2)}, u32[]{:S(2)}) collective-permute-start(f32[2,128,256]{2,1,0:T(8,128)S(1)} %get-tuple-element.64), channel_id=1, source_target_pairs={{0,32},{16,48},{32,0},{48,16},{64,96},{80,112},{96,64},{112,80},{1... | collective-permute-start | bytes 786440 | tf_op jit(solution)/shard_map/ppermute | solution.py:374
  58.0 0.7 collective-permute-start.13
  58.7 0.7 fisher_over_first_swap.2
  59.5 1.9 %collective-permute-start.10 = (bf16[256,512]{1,0:T(8,128)(2,1)S(1)}, bf16[256,512]{1,0:T(8,128)(2,1)S(1)}, u32[]{:S(2)}, u32[]{:S(2)}) collective-permute-start(bf16[256,512]{1,0:T(8,128)(2,1)S(1)} %get-tuple-element.62), channel_id=1, source_target_pairs={{0,12},{2,14},{4,8},{6,10},{8,4},{10,6},{12,0},{14,2},{1,13},{3,15... | collective-permute-start | bytes 786440 | tf_op jit(solution)/shard_map/ppermute | solution.py:341
  61.3 0.7 fisher_over_first_swap.3
  62.1 0.6 collective-permute-start.15
  62.7 0.5 collective-permute-done.11.one
  63.2 6.5 %collective-permute-done.12.two = f32[2,128,256]{2,1,0:T(8,128)S(1)} collective-permute-done((f32[2,128,256]{2,1,0:T(8,128)S(1)}, f32[2,128,256]{2,1,0:T(8,128)S(1)}, u32[]{:S(2)}, u32[]{:S(2)}) %collective-permute-start.12) | collective-permute-done | bytes 262176 | tf_op jit(solution)/shard_map/ppermute | solution.py:374
  69.8 0.3 fisher_over_tokens.4.first_ref
  70.1 0.6 fisher_over_tokens.5
  70.7 1.3 %collective-permute-start.16 = (bf16[256,512]{1,0:T(8,128)(2,1)S(1)}, bf16[256,512]{1,0:T(8,128)(2,1)S(1)}, u32[]{:S(2)}, u32[]{:S(2)}) collective-permute-start(bf16[256,512]{1,0:T(8,128)(2,1)S(1)} %get-tuple-element.70), channel_id=1, source_target_pairs={{0,2},{2,0},{4,6},{6,4},{8,10},{10,8},{12,14},{14,12},{1,3},{3,1},... | collective-permute-start | bytes 786440 | tf_op jit(solution)/shard_map/ppermute | solution.py:335
  72.0 1.2 %collective-permute-done.16.refs_1_ = bf16[256,512]{1,0:T(8,128)(2,1)S(1)} collective-permute-done((bf16[256,512]{1,0:T(8,128)(2,1)S(1)}, bf16[256,512]{1,0:T(8,128)(2,1)S(1)}, u32[]{:S(2)}, u32[]{:S(2)}) %collective-permute-start.16) | collective-permute-done | bytes 262176 | tf_op jit(solution)/shard_map/ppermute | solution.py:335
  73.1 0.7 weigh_members.3
  73.9 1.3 %collective-permute-start.17 = (bf16[3,128,256]{2,1,0:T(8,128)(2,1)S(1)}, bf16[3,128,256]{2,1,0:T(8,128)(2,1)S(1)}, u32[]{:S(2)}, u32[]{:S(2)}) collective-permute-start(bf16[3,128,256]{2,1,0:T(8,128)(2,1)S(1)} %get-tuple-element.71), channel_id=1, source_target_pairs={{0,16},{16,32},{32,48},{48,0},{64,80},{80,96},{96,112},{112,64},{1... | collective-permute-start | bytes 589832 | tf_op jit(solution)/shard_map/ppermute | solution.py:374
  75.2 3.3 %collective-permute-start.18 = (bf16[3,128,256]{2,1,0:T(8,128)(2,1)S(1)}, bf16[3,128,256]{2,1,0:T(8,128)(2,1)S(1)}, u32[]{:S(2)}, u32[]{:S(2)}) collective-permute-start(bf16[3,128,256]{2,1,0:T(8,128)(2,1)S(1)} %get-tuple-element.72), channel_id=1, source_target_pairs={{0,32},{16,48},{32,0},{48,16},{64,96},{80,112},{96,64},{112,80},{1... | collective-permute-start | bytes 589832 | tf_op jit(solution)/shard_map/ppermute | solution.py:374
  78.5 0.7 collective-permute-start.19
  79.2 4.3 %collective-permute-start.23 = (bf16[3,128,256]{2,1,0:T(8,128)(2,1)S(1)}, bf16[3,128,256]{2,1,0:T(8,128)(2,1)S(1)}, u32[]{:S(2)}, u32[]{:S(2)}) collective-permute-start(bf16[3,128,256]{2,1,0:T(8,128)(2,1)S(1)} %sum_over_z.2.after), channel_id=1, source_target_pairs={{0,0},{1,15},{2,64},{3,79},{4,4},{5,11},{6,68},{7,75},{8,6},{9,9},... | collective-permute-start | bytes 589832 | tf_op jit(solution)/shard_map/ppermute | solution.py:361
  83.5 1.3 %collective-permute-start.22 = (bf16[3,128,256]{2,1,0:T(8,128)(2,1)S(1)}, bf16[3,128,256]{2,1,0:T(8,128)(2,1)S(1)}, u32[]{:S(2)}, u32[]{:S(2)}) collective-permute-start(bf16[3,128,256]{2,1,0:T(8,128)(2,1)S(1)} %sum_over_z.2.after), channel_id=1, source_target_pairs={{64,0},{65,15},{66,64},{67,79},{68,4},{69,11},{70,68},{71,75},{72,... | collective-permute-start | bytes 589832 | tf_op jit(solution)/shard_map/ppermute | solution.py:361
  84.8 2.5 %collective-permute-done.18.two = bf16[3,128,256]{2,1,0:T(8,128)(2,1)S(1)} collective-permute-done((bf16[3,128,256]{2,1,0:T(8,128)(2,1)S(1)}, bf16[3,128,256]{2,1,0:T(8,128)(2,1)S(1)}, u32[]{:S(2)}, u32[]{:S(2)}) %collective-permute-start.18) | collective-permute-done | bytes 196640 | tf_op jit(solution)/shard_map/ppermute | solution.py:374
  87.4 0.3 sum_over_z.3
  87.7 5.6 %collective-permute-start.21 = (bf16[3,128,256]{2,1,0:T(8,128)(2,1)S(1)}, bf16[3,128,256]{2,1,0:T(8,128)(2,1)S(1)}, u32[]{:S(2)}, u32[]{:S(2)}) collective-permute-start(bf16[3,128,256]{2,1,0:T(8,128)(2,1)S(1)} %sum_over_z.3), channel_id=1, source_target_pairs={{0,1},{1,14},{2,65},{3,78},{4,5},{5,10},{6,69},{7,74},{8,7},{9,8},... | collective-permute-start | bytes 589832 | tf_op jit(solution)/shard_map/ppermute | solution.py:361
  93.3 0.7 collective-permute-start.20
  94.0 0.2 meet_over_y.1.sums
  94.2 8.0 %collective-permute-done.21.far = bf16[3,128,256]{2,1,0:T(8,128)(2,1)S(1)} collective-permute-done((bf16[3,128,256]{2,1,0:T(8,128)(2,1)S(1)}, bf16[3,128,256]{2,1,0:T(8,128)(2,1)S(1)}, u32[]{:S(2)}, u32[]{:S(2)}) %collective-permute-start.21) | collective-permute-done | bytes 196640 | tf_op jit(solution)/shard_map/ppermute | solution.py:361
  102.2 0.8 merge_members.1
  (23 shorter events, 0.4 us)
Async XLA Ops:
  2.1 3.6 %copy-start = (bf16[2,1024,256]{2,1,0:T(8,128)(2,1)S(1)}, bf16[2,1024,256]{2,1,0:T(8,128)(2,1)}, u32[]{:S(2)}) copy-start(bf16[2,1024,256]{2,1,0:T(8,128)(2,1)} %param.5) | copy-start | bytes 3145732
  2.1 11.2 %collective-permute-start = (bf16[768,2304]{1,0:T(8,128)(2,1)S(1)}, bf16[768,2304]{1,0:T(8,128)(2,1)S(1)}, u32[]{:S(2)}, u32[]{:S(2)}) collective-permute-start(bf16[768,2304]{1,0:T(8,128)(2,1)S(1)} %load_to_swap.2.after), channel_id=1, source_target_pairs={{0,2},{2,0},{4,6},{6,4},{8,10},{10,8},{12,14},{14,12},{1,3},{3,1},... | collective-permute-start | bytes 10616840 | tf_op jit(solution)/shard_map/ppermute | solution.py:335
  5.5 15.9 %collective-permute-start.1 = (bf16[768,2048]{1,0:T(8,128)(2,1)S(1)}, bf16[768,2048]{1,0:T(8,128)(2,1)S(1)}, u32[]{:S(2)}, u32[]{:S(2)}) collective-permute-start(bf16[768,2048]{1,0:T(8,128)(2,1)S(1)} %load_to_swap.3.after), channel_id=1, source_target_pairs={{0,2},{2,0},{4,6},{6,4},{8,10},{10,8},{12,14},{14,12},{1,3},{3,1},... | collective-permute-start | bytes 9437192 | tf_op jit(solution)/shard_map/ppermute | solution.py:335
  5.7 37.9 %collective-permute-start.7 = (bf16[2,1024,256]{2,1,0:T(8,128)(2,1)S(1)}, bf16[2,1024,256]{2,1,0:T(8,128)(2,1)S(1)}, u32[]{:S(2)}, u32[]{:S(2)}) collective-permute-start(bf16[2,1024,256]{2,1,0:T(8,128)(2,1)S(1)} %copy-done), channel_id=1, source_target_pairs={{0,0},{1,2},{2,12},{3,14},{4,4},{5,6},{6,8},{7,10},{8,9},{9,11},{1... | collective-permute-start | bytes 3145736 | tf_op jit(solution)/shard_map/ppermute | solution.py:364
  13.4 28.3 %collective-permute-start.2 = (bf16[2,768,256]{2,1,0:T(8,128)(2,1)S(1)}, bf16[2,768,256]{2,1,0:T(8,128)(2,1)S(1)}, u32[]{:S(2)}, u32[]{:S(2)}) collective-permute-start(bf16[2,768,256]{2,1,0:T(8,128)(2,1)S(1)} %pair_grads.1.after), channel_id=1, source_target_pairs={{0,1},{1,0},{2,3},{3,2},{4,5},{5,4},{6,7},{7,6},{8,9},{9,8},{10,11... | collective-permute-start | bytes 2359304 | tf_op jit(solution)/shard_map/ppermute | solution.py:338
  17.1 29.0 %collective-permute-start.4 = (bf16[256,1024]{1,0:T(8,128)(2,1)S(1)}, bf16[256,1024]{1,0:T(8,128)(2,1)S(1)}, u32[]{:S(2)}, u32[]{:S(2)}) collective-permute-start(bf16[256,1024]{1,0:T(8,128)(2,1)S(1)} %get-tuple-element.52), channel_id=1, source_target_pairs={{0,4},{2,6},{4,0},{6,2},{8,12},{10,14},{12,8},{14,10},{1,5},{3,7},... | collective-permute-start | bytes 1572872 | tf_op jit(solution)/shard_map/ppermute | solution.py:341
  17.2 31.8 %collective-permute-start.5 = (bf16[256,1024]{1,0:T(8,128)(2,1)S(1)}, bf16[256,1024]{1,0:T(8,128)(2,1)S(1)}, u32[]{:S(2)}, u32[]{:S(2)}) collective-permute-start(bf16[256,1024]{1,0:T(8,128)(2,1)S(1)} %get-tuple-element.44.after), channel_id=1, source_target_pairs={{0,8},{2,10},{4,12},{6,14},{8,0},{10,2},{12,4},{14,6},{1,9},{3,11}... | collective-permute-start | bytes 1572872 | tf_op jit(solution)/shard_map/ppermute | solution.py:341
  22.6 26.5 %collective-permute-start.6 = (bf16[256,1024]{1,0:T(8,128)(2,1)S(1)}, bf16[256,1024]{1,0:T(8,128)(2,1)S(1)}, u32[]{:S(2)}, u32[]{:S(2)}) collective-permute-start(bf16[256,1024]{1,0:T(8,128)(2,1)S(1)} %get-tuple-element.48.after), channel_id=1, source_target_pairs={{0,12},{2,14},{4,8},{6,10},{8,4},{10,6},{12,0},{14,2},{1,13},{3,15... | collective-permute-start | bytes 1572872 | tf_op jit(solution)/shard_map/ppermute | solution.py:341
  43.7 8.8 %collective-permute-start.9 = (bf16[2,512,256]{2,1,0:T(8,128)(2,1)S(1)}, bf16[2,512,256]{2,1,0:T(8,128)(2,1)S(1)}, u32[]{:S(2)}, u32[]{:S(2)}) collective-permute-start(bf16[2,512,256]{2,1,0:T(8,128)(2,1)S(1)} %get-tuple-element.59), channel_id=1, source_target_pairs={{0,2},{2,0},{4,6},{6,4},{8,10},{10,8},{12,14},{14,12},{1,3},{3,1},... | collective-permute-start | bytes 1572872 | tf_op jit(solution)/shard_map/ppermute | solution.py:335
  43.9 14.8 %collective-permute-start.3 = (bf16[2,256,512]{2,1,0:T(8,128)(2,1)S(1)}, bf16[2,256,512]{2,1,0:T(8,128)(2,1)S(1)}, u32[]{:S(2)}, u32[]{:S(2)}) collective-permute-start(bf16[2,256,512]{2,1,0:T(8,128)(2,1)S(1)} %get-tuple-element.50), channel_id=1, source_target_pairs={{0,4},{2,6},{4,0},{6,2},{8,12},{10,14},{12,8},{14,10},{1,5},{3,7},... | collective-permute-start | bytes 1572872 | tf_op jit(solution)/shard_map/ppermute | solution.py:341
  46.1 15.2 %collective-permute-start.14 = (bf16[2,256,512]{2,1,0:T(8,128)(2,1)S(1)}, bf16[2,256,512]{2,1,0:T(8,128)(2,1)S(1)}, u32[]{:S(2)}, u32[]{:S(2)}) collective-permute-start(bf16[2,256,512]{2,1,0:T(8,128)(2,1)S(1)} %get-tuple-element.66), channel_id=1, source_target_pairs={{0,12},{2,14},{4,8},{6,10},{8,4},{10,6},{12,0},{14,2},{1,13},{3,15... | collective-permute-start | bytes 1572872 | tf_op jit(solution)/shard_map/ppermute | solution.py:341
  50.7 1.8 %collective-permute-start.8 = (bf16[256,512]{1,0:T(8,128)(2,1)S(1)}, bf16[256,512]{1,0:T(8,128)(2,1)S(1)}, u32[]{:S(2)}, u32[]{:S(2)}) collective-permute-start(bf16[256,512]{1,0:T(8,128)(2,1)S(1)} %get-tuple-element.58), channel_id=1, source_target_pairs={{0,2},{2,0},{4,6},{6,4},{8,10},{10,8},{12,14},{14,12},{1,3},{3,1},... | collective-permute-start | bytes 786440 | tf_op jit(solution)/shard_map/ppermute | solution.py:335
  53.0 10.2 %collective-permute-start.11 = (f32[2,128,256]{2,1,0:T(8,128)S(1)}, f32[2,128,256]{2,1,0:T(8,128)S(1)}, u32[]{:S(2)}, u32[]{:S(2)}) collective-permute-start(f32[2,128,256]{2,1,0:T(8,128)S(1)} %get-tuple-element.63), channel_id=1, source_target_pairs={{0,16},{16,32},{32,48},{48,0},{64,80},{80,96},{96,112},{112,64},{1... | collective-permute-start | bytes 786440 | tf_op jit(solution)/shard_map/ppermute | solution.py:374
  54.7 15.0 %collective-permute-start.12 = (f32[2,128,256]{2,1,0:T(8,128)S(1)}, f32[2,128,256]{2,1,0:T(8,128)S(1)}, u32[]{:S(2)}, u32[]{:S(2)}) collective-permute-start(f32[2,128,256]{2,1,0:T(8,128)S(1)} %get-tuple-element.64), channel_id=1, source_target_pairs={{0,32},{16,48},{32,0},{48,16},{64,96},{80,112},{96,64},{112,80},{1... | collective-permute-start | bytes 786440 | tf_op jit(solution)/shard_map/ppermute | solution.py:374
  58.0 11.7 %collective-permute-start.13 = (f32[2,128,256]{2,1,0:T(8,128)S(1)}, f32[2,128,256]{2,1,0:T(8,128)S(1)}, u32[]{:S(2)}, u32[]{:S(2)}) collective-permute-start(f32[2,128,256]{2,1,0:T(8,128)S(1)} %get-tuple-element.65), channel_id=1, source_target_pairs={{0,48},{16,0},{32,16},{48,32},{64,112},{80,64},{96,80},{112,96},{1... | collective-permute-start | bytes 786440 | tf_op jit(solution)/shard_map/ppermute | solution.py:374
  59.5 10.3 %collective-permute-start.10 = (bf16[256,512]{1,0:T(8,128)(2,1)S(1)}, bf16[256,512]{1,0:T(8,128)(2,1)S(1)}, u32[]{:S(2)}, u32[]{:S(2)}) collective-permute-start(bf16[256,512]{1,0:T(8,128)(2,1)S(1)} %get-tuple-element.62), channel_id=1, source_target_pairs={{0,12},{2,14},{4,8},{6,10},{8,4},{10,6},{12,0},{14,2},{1,13},{3,15... | collective-permute-start | bytes 786440 | tf_op jit(solution)/shard_map/ppermute | solution.py:341
  62.1 8.0 %collective-permute-start.15 = (bf16[256,512]{1,0:T(8,128)(2,1)S(1)}, bf16[256,512]{1,0:T(8,128)(2,1)S(1)}, u32[]{:S(2)}, u32[]{:S(2)}) collective-permute-start(bf16[256,512]{1,0:T(8,128)(2,1)S(1)} %get-tuple-element.68), channel_id=1, source_target_pairs={{0,4},{2,6},{4,0},{6,2},{8,12},{10,14},{12,8},{14,10},{1,5},{3,7},... | collective-permute-start | bytes 786440 | tf_op jit(solution)/shard_map/ppermute | solution.py:341
  70.7 2.4 %collective-permute-start.16 = (bf16[256,512]{1,0:T(8,128)(2,1)S(1)}, bf16[256,512]{1,0:T(8,128)(2,1)S(1)}, u32[]{:S(2)}, u32[]{:S(2)}) collective-permute-start(bf16[256,512]{1,0:T(8,128)(2,1)S(1)} %get-tuple-element.70), channel_id=1, source_target_pairs={{0,2},{2,0},{4,6},{6,4},{8,10},{10,8},{12,14},{14,12},{1,3},{3,1},... | collective-permute-start | bytes 786440 | tf_op jit(solution)/shard_map/ppermute | solution.py:335
  73.9 11.0 %collective-permute-start.17 = (bf16[3,128,256]{2,1,0:T(8,128)(2,1)S(1)}, bf16[3,128,256]{2,1,0:T(8,128)(2,1)S(1)}, u32[]{:S(2)}, u32[]{:S(2)}) collective-permute-start(bf16[3,128,256]{2,1,0:T(8,128)(2,1)S(1)} %get-tuple-element.71), channel_id=1, source_target_pairs={{0,16},{16,32},{32,48},{48,0},{64,80},{80,96},{96,112},{112,64},{1... | collective-permute-start | bytes 589832 | tf_op jit(solution)/shard_map/ppermute | solution.py:374
  75.2 12.2 %collective-permute-start.18 = (bf16[3,128,256]{2,1,0:T(8,128)(2,1)S(1)}, bf16[3,128,256]{2,1,0:T(8,128)(2,1)S(1)}, u32[]{:S(2)}, u32[]{:S(2)}) collective-permute-start(bf16[3,128,256]{2,1,0:T(8,128)(2,1)S(1)} %get-tuple-element.72), channel_id=1, source_target_pairs={{0,32},{16,48},{32,0},{48,16},{64,96},{80,112},{96,64},{112,80},{1... | collective-permute-start | bytes 589832 | tf_op jit(solution)/shard_map/ppermute | solution.py:374
  78.5 8.9 %collective-permute-start.19 = (bf16[3,128,256]{2,1,0:T(8,128)(2,1)S(1)}, bf16[3,128,256]{2,1,0:T(8,128)(2,1)S(1)}, u32[]{:S(2)}, u32[]{:S(2)}) collective-permute-start(bf16[3,128,256]{2,1,0:T(8,128)(2,1)S(1)} %get-tuple-element.73), channel_id=1, source_target_pairs={{0,48},{16,0},{32,16},{48,32},{64,112},{80,64},{96,80},{112,96},{1... | collective-permute-start | bytes 589832 | tf_op jit(solution)/shard_map/ppermute | solution.py:374
  79.2 14.8 %collective-permute-start.23 = (bf16[3,128,256]{2,1,0:T(8,128)(2,1)S(1)}, bf16[3,128,256]{2,1,0:T(8,128)(2,1)S(1)}, u32[]{:S(2)}, u32[]{:S(2)}) collective-permute-start(bf16[3,128,256]{2,1,0:T(8,128)(2,1)S(1)} %sum_over_z.2.after), channel_id=1, source_target_pairs={{0,0},{1,15},{2,64},{3,79},{4,4},{5,11},{6,68},{7,75},{8,6},{9,9},... | collective-permute-start | bytes 589832 | tf_op jit(solution)/shard_map/ppermute | solution.py:361
  83.5 10.5 %collective-permute-start.22 = (bf16[3,128,256]{2,1,0:T(8,128)(2,1)S(1)}, bf16[3,128,256]{2,1,0:T(8,128)(2,1)S(1)}, u32[]{:S(2)}, u32[]{:S(2)}) collective-permute-start(bf16[3,128,256]{2,1,0:T(8,128)(2,1)S(1)} %sum_over_z.2.after), channel_id=1, source_target_pairs={{64,0},{65,15},{66,64},{67,79},{68,4},{69,11},{70,68},{71,75},{72,... | collective-permute-start | bytes 589832 | tf_op jit(solution)/shard_map/ppermute | solution.py:361
  87.7 14.5 %collective-permute-start.21 = (bf16[3,128,256]{2,1,0:T(8,128)(2,1)S(1)}, bf16[3,128,256]{2,1,0:T(8,128)(2,1)S(1)}, u32[]{:S(2)}, u32[]{:S(2)}) collective-permute-start(bf16[3,128,256]{2,1,0:T(8,128)(2,1)S(1)} %sum_over_z.3), channel_id=1, source_target_pairs={{0,1},{1,14},{2,65},{3,78},{4,5},{5,10},{6,69},{7,74},{8,7},{9,8},... | collective-permute-start | bytes 589832 | tf_op jit(solution)/shard_map/ppermute | solution.py:361
  93.3 8.9 %collective-permute-start.20 = (bf16[3,128,256]{2,1,0:T(8,128)(2,1)S(1)}, bf16[3,128,256]{2,1,0:T(8,128)(2,1)S(1)}, u32[]{:S(2)}, u32[]{:S(2)}) collective-permute-start(bf16[3,128,256]{2,1,0:T(8,128)(2,1)S(1)} %sum_over_z.3), channel_id=1, source_target_pairs={{64,1},{65,14},{66,65},{67,78},{68,5},{69,10},{70,69},{71,74},{72,... | collective-permute-start | bytes 589832 | tf_op jit(solution)/shard_map/ppermute | solution.py:361
